TPU v7x, 32 devices: a whole 2x2x4 slice. The times are simulated.
32 devices in a mesh: seq: 8 (over z, x), head: 4 (over y, core).
Axes of the slice: x: 2, y: 2, z: 4, core: 2. Of those that a mesh axis runs over, the one named last changes fastest.
Arguments:
- qkv: bfloat16 [3, 8, 512, 4096], P(None, 'seq', None, 'head'), may hold values from -6 to 6
- out_weight: bfloat16 [4096, 4096], P('head', 'seq'), may hold values from -0.09375 to 0.09375
Outputs:
- layer_out: bfloat16 [512, 8, 4096], P('head', 'seq')
All inputs are finite; a program needn't handle non-finite values.
Results may differ from a plain program's by a relative error of at most 0.017.
Values may be sent and summed in bfloat16 or wider, within the bound.
No kernel may reach another device: no remote copies, remote signals or barrier semaphores. Data moves between devices by JAX's collectives and lax.ppermute only.
A program may use at most 128 MiB of HBM per device.

v0:
```python
import jax
import jax.numpy as jnp
from jax import lax
from jax.sharding import PartitionSpec as P

HEAD = 128


def shifted(shard, axis, by):
    size = lax.axis_size(axis)
    pairs = [(i, i + by) for i in range(size) if 0 <= i + by < size]
    return lax.ppermute(shard, axis, pairs)


def column_part(part):
    queries, keys_part, values = (part[0], part[1], part[2])
    rows = queries.shape[0]
    scale = queries.shape[-1] ** (-0.5)
    scores = (
        jnp.einsum("rchd,schd->chrs", queries, keys_part, preferred_element_type=jnp.float32)
        * scale
    )
    r_idx = lax.broadcasted_iota(jnp.int32, (rows, rows), 0)
    s_idx = lax.broadcasted_iota(jnp.int32, (rows, rows), 1)
    allowed = s_idx <= r_idx - 2
    masked = jnp.where(allowed, scores, jnp.float32(-1e30))
    peak = jnp.max(masked, axis=-1)
    weights = jnp.where(allowed, jnp.exp(masked - peak[..., None]), jnp.float32(0.0))
    total = jnp.maximum(jnp.sum(weights, axis=-1), jnp.float32(1.0))
    rounded = weights.astype(jnp.bfloat16)
    mixed = jnp.einsum("chrs,schd->rchd", rounded, values, preferred_element_type=jnp.float32)
    col_out = (mixed / jnp.transpose(total, (2, 0, 1))[..., None]).astype(jnp.bfloat16)
    col_lse = jnp.transpose(peak + jnp.log(total), (2, 0, 1))
    return (col_out, col_lse)


def row_part(local, previous, first_row):
    rows_dev, cols, heads_local, head_size = (
        local.shape[1],
        local.shape[2],
        local.shape[3],
        local.shape[4],
    )
    scale = head_size ** (-0.5)
    keys_ext = jnp.concatenate([previous, local[1:3]], axis=1)
    key_idx = lax.broadcasted_iota(jnp.int32, (cols, 2 * cols), 1)
    query_idx = lax.broadcasted_iota(jnp.int32, (cols, 2 * cols), 0)

    def one_row(index):
        queries = lax.dynamic_index_in_dim(local[0], index, 0, keepdims=False)
        pair = keys_ext.reshape(2, 2 * cols, heads_local, head_size)
        scores = (
            jnp.einsum("qhd,khd->hqk", queries, pair[0], preferred_element_type=jnp.float32) * scale
        )
        allowed = (key_idx < cols) & (first_row + index > 0) | (key_idx >= cols) & (
            key_idx - cols <= query_idx
        )
        masked = jnp.where(allowed[None], scores, jnp.float32(-1e30))
        peak = jnp.max(masked, axis=-1)
        weights = jnp.where(allowed[None], jnp.exp(masked - peak[..., None]), jnp.float32(0.0))
        total = jnp.sum(weights, axis=-1)
        rounded = weights.astype(jnp.bfloat16)
        mixed = jnp.einsum("hqk,khd->qhd", rounded, pair[1], preferred_element_type=jnp.float32)
        return (mixed / jnp.transpose(total)[..., None], jnp.transpose(peak + jnp.log(total)))

    return lax.map(one_row, jnp.arange(rows_dev, dtype=jnp.int32))


def body(qkv, out_weight):
    rows_dev, cols, features = (qkv.shape[1], qkv.shape[2], qkv.shape[3])
    head_size = HEAD
    heads_local = features // head_size
    local = qkv.reshape(3, rows_dev, cols, heads_local, head_size)
    previous = shifted(local[1:3, rows_dev - 1 : rows_dev], "seq", 1)
    first_row = lax.axis_index("seq") * rows_dev
    row_out, row_lse = row_part(local, previous, first_row)
    columns = lax.all_to_all(local, "seq", split_axis=2, concat_axis=1, tiled=True)
    col_part_out, col_part_lse = column_part(columns)
    col_out, col_lse = (
        lax.all_to_all(col_part_out, "seq", split_axis=0, concat_axis=1, tiled=True),
        lax.all_to_all(
            col_part_lse.astype(jnp.bfloat16), "seq", split_axis=0, concat_axis=1, tiled=True
        ).astype(col_part_lse.dtype),
    )
    top = jnp.maximum(row_lse, col_lse)
    left = jnp.exp(row_lse - top)
    right = jnp.exp(col_lse - top)
    attended = (left[..., None] * row_out + right[..., None] * col_out.astype(jnp.float32)) / (
        left + right
    )[..., None]
    attended = attended.astype(jnp.bfloat16).reshape(rows_dev, cols, features)
    terms = jnp.einsum(
        "rcf,fd->crd",
        attended,
        lax.all_gather(out_weight, "seq", axis=1, tiled=True),
        preferred_element_type=jnp.float32,
    )
    summed = lax.psum_scatter(terms.astype(jnp.bfloat16), "head", scatter_dimension=0, tiled=True)
    return summed


def solution(mesh):
    in_specs = (P(None, "seq", None, "head"), P("head", "seq"))
    out_specs = P("head", "seq", None)
    return jax.shard_map(body, mesh=mesh, in_specs=in_specs, out_specs=out_specs, check_vma=False)
```

profile of v0, /device:TPU:16, one launch (start us, length us, event | category | flops | bytes accessed | tf_op | source)
XLA Modules:
  0.0 363.7 jit_solution(16288142792757894820)
XLA Ops:
  6.5 0.7 all-gather.2.cloned.1.call-update
  7.3 3.2 copy.84
  10.5 3.3 copy.85
  13.7 6.1 %all-to-all-start = ((bf16[3,1,512,8,128]{4,3,1,0,2:T(8,128)(2,1)}), bf16[3,1,512,8,128]{4,3,1,0,2:T(8,128)(2,1)}, u32[]{:S(2)}, u32[]{:S(2)}) async-start(bf16[3,1,512,8,128]{4,3,1,0,2:T(8,128)(2,1)} %copy.85), calls=%async_computation | async-start | bytes 6291456 | tf_op jit(solution)/shard_map/all_to_all | solution.py:77
  19.9 1.7 slice-done
  21.6 0.6 copy.116
  22.2 1.7 copy.80
  23.9 3.4 collective-permute-start
  27.3 1.3 copy.110
  28.7 1.0 fusion.13
  29.7 205.6 %collective-permute-done = bf16[2,1,512,8,128]{4,2,1,3,0:T(8,128)(2,1)} collective-permute-done((bf16[2,1,512,8,128]{4,2,1,3,0:T(8,128)(2,1)}, bf16[2,1,512,8,128]{4,2,1,3,0:T(8,128)(2,1)}, u32[]{:S(2)}, u32[]{:S(2)}) %collective-permute-start) | collective-permute-done | bytes 2097184 | tf_op jit(solution)/shard_map/ppermute | solution.py:12
  235.3 1.7 constant_dynamic-update-slice_fusion.1
  237.1 0.6 constant_dynamic-update-slice_fusion
  237.6 1.7 fusion.35
  239.3 3.0 fusion.36
  242.4 2.6 fusion.17
  245.0 2.7 copy.90
  248.0 2.5 copy.100
  250.7 0.7 reshape.122
  251.4 4.2 %all-to-all-start.1 = ((bf16[8,2,256]{2,1,0:T(2,128)(2,1)}), bf16[8,2,256]{2,1,0:T(2,128)(2,1)S(1)}, u32[]{:S(2)}, u32[]{:S(2)}) async-start(bf16[8,2,256]{2,1,0:T(2,128)(2,1)} %reshape.122), calls=%async_computation.1 | async-start | bytes 16384 | tf_op jit(solution)/shard_map/all_to_all | solution.py:81
  255.6 2.5 fusion.7
  258.1 1.1 copy.103
  259.7 6.5 %all-to-all-start.2 = ((bf16[8,64,8,128]{3,2,1,0:T(8,128)(2,1)}), bf16[8,64,8,128]{3,2,1,0:T(8,128)(2,1)}, u32[]{:S(2)}, u32[]{:S(2)}) async-start(bf16[8,64,8,128]{3,2,1,0:T(8,128)(2,1)} %copy.103), calls=%async_computation.2 | async-start | bytes 2097152 | tf_op jit(solution)/shard_map/all_to_all | solution.py:80
  266.3 4.6 %fusion = (f32[8,512]{1,0:T(8,128)S(1)}, f32[8,1024,512]{2,1,0:T(8,128)S(1)}) fusion(pred[512,1024]{0,1:T(8,128)(4,1)S(1)} %fusion.13, bf16[1024,8,128]{2,0,1:T(8,128)(2,1)S(1)} %bitcast.96, bf16[512,8,128]{0,2,1:T(8,128)(2,1)} %bitcast.99), kind=kOutput, calls=%fused_computation.2 | convolution fusion | flops 1086320640 | bytes 20463616 | tf_op jit(solution)/shard_map/while/body/eval_jaxpr/qhd,khd->hqk/dot_general | solution.py:53
  270.9 5.7 %copy-done = f32[8,1024,512]{2,1,0:T(8,128)} copy-done((f32[8,1024,512]{2,1,0:T(8,128)}, f32[8,1024,512]{2,1,0:T(8,128)S(1)}, u32[]{:S(2)}) %copy-start) | copy-done | bytes 16777240
  276.6 4.0 %fusion.2 = f32[8,512]{1,0:T(8,128)S(1)} fusion(f32[8,1024,512]{2,1,0:T(8,128)S(1)} %get-tuple-element.40, f32[8,512]{1,0:T(8,128)S(1)} %get-tuple-element.39, pred[512,1024]{0,1:T(8,128)(4,1)S(1)} %fusion.13), kind=kLoop, calls=%fused_computation.4 | loop fusion | flops 20967424 | bytes 17334272 | tf_op jit(solution)/shard_map/while/body/eval_jaxpr/reduce_sum | solution.py:61
  280.8 7.2 %all-to-all-done.2 = bf16[8,64,8,128]{3,2,1,0:T(8,128)(2,1)} async-done(((bf16[8,64,8,128]{3,2,1,0:T(8,128)(2,1)}), bf16[8,64,8,128]{3,2,1,0:T(8,128)(2,1)}, u32[]{:S(2)}, u32[]{:S(2)}) %all-to-all-start.2) | async-done | bytes 1048608 | tf_op jit(solution)/shard_map/all_to_all | solution.py:80
  288.0 1.4 bitcast_convert_fusion
  289.4 1.9 copy.104
  291.2 9.6 %fusion.11 = bf16[512,8,128]{0,2,1:T(8,128)(2,1)S(1)} fusion(f32[512,8,128]{0,2,1:T(8,128)} %copy.104, bf16[1024,8,128]{2,0,1:T(8,128)(2,1)} %bitcast.102, f32[8,1024,512]{2,1,0:T(8,128)} %copy-done, f32[8,512]{1,0:T(8,128)S(1)} %get-tuple-element.39, pred[512,1024]{0,1:T(8,128)(4,1)S(1)} %fusion.13, f32[512,8]{0,1:T(8,128)S(1)} %get-tuple-element.19, ...), kind=kOutput, calls=%fused_computation.16 | convolution fusion | flops 1097859072 | bytes 22626304 | tf_op jit(solution)/shard_map/while/body/eval_jaxpr/hqk,khd->qhd/dot_general | solution.py:63
  300.9 9.5 %fusion.6 = bf16[512,1,4096]{2,0,1:T(8,128)(2,1)} fusion(bf16[512,1024]{0,1:T(8,128)(2,1)S(1)} %bitcast.106, bf16[1024,4096]{1,0:T(8,128)(2,1)} %all-gather.2.cloned.1.call-done), kind=kOutput, calls=%fused_computation.8 | convolution fusion | flops 4297064448 | bytes 13631488 | tf_op jit(solution)/shard_map/rcf,fd->crd/dot_general | solution.py:92
  310.4 46.4 %reduce-scatter.2.cloned.1.call-done = bf16[128,1,4096]{2,0,1:T(8,128)(2,1)} async-done(((bf16[512,1,4096]{2,0,1:T(8,128)(2,1)}), bf16[128,1,4096]{2,0,1:T(8,128)(2,1)}) %reduce-scatter.2.cloned.1.call-update) | async-done | bytes 1048592 | tf_op jit(solution)/shard_map/reduce_scatter | solution.py:98
  (23 shorter events, 1.4 us)
Async XLA Ops:
  6.5 294.3 %all-gather.2.cloned.1.call-start = ((), (), s32[]{:S(2)}) async-start(), calls=%async_computation.4 | async-start | bytes 9437184 | tf_op jit(solution)/shard_map/all_gather | solution.py:95
  13.7 225.6 %all-to-all-start = ((bf16[3,1,512,8,128]{4,3,1,0,2:T(8,128)(2,1)}), bf16[3,1,512,8,128]{4,3,1,0,2:T(8,128)(2,1)}, u32[]{:S(2)}, u32[]{:S(2)}) async-start(bf16[3,1,512,8,128]{4,3,1,0,2:T(8,128)(2,1)} %copy.85), calls=%async_computation | async-start | bytes 6291456 | tf_op jit(solution)/shard_map/all_to_all | solution.py:77
  19.9 1.7 slice-start
  22.2 5.1 %slice-start.1 = ((bf16[3,1,512,1024]{3,2,1,0:T(8,128)(2,1)}), bf16[1,1,512,1024]{3,2,1,0:T(8,128)(2,1)S(1)}, s32[]{:S(2)}) async-start(bf16[3,1,512,1024]{3,2,1,0:T(8,128)(2,1)} %param.2), calls=%async_computation.7 | async-start | bytes 2097152 | tf_op jit(solution)/shard_map/while/body/eval_jaxpr/slice | solution.py:50
  23.9 211.4 %collective-permute-start = (bf16[2,1,512,8,128]{4,2,1,3,0:T(8,128)(2,1)}, bf16[2,1,512,8,128]{4,2,1,3,0:T(8,128)(2,1)}, u32[]{:S(2)}, u32[]{:S(2)}) collective-permute-start(bf16[2,1,512,8,128]{4,2,1,3,0:T(8,128)(2,1)} %copy.80), channel_id=1, source_target_pairs={{0,4},{4,8},{8,12},{12,16},{16,20},{20,24},{24,28},{1,5},{5,9},{9,... | collective-permute-start | bytes 6291464 | tf_op jit(solution)/shard_map/ppermute | solution.py:12
  251.4 8.3 %all-to-all-start.1 = ((bf16[8,2,256]{2,1,0:T(2,128)(2,1)}), bf16[8,2,256]{2,1,0:T(2,128)(2,1)S(1)}, u32[]{:S(2)}, u32[]{:S(2)}) async-start(bf16[8,2,256]{2,1,0:T(2,128)(2,1)} %reshape.122), calls=%async_computation.1 | async-start | bytes 16384 | tf_op jit(solution)/shard_map/all_to_all | solution.py:81
  259.7 28.3 %all-to-all-start.2 = ((bf16[8,64,8,128]{3,2,1,0:T(8,128)(2,1)}), bf16[8,64,8,128]{3,2,1,0:T(8,128)(2,1)}, u32[]{:S(2)}, u32[]{:S(2)}) async-start(bf16[8,64,8,128]{3,2,1,0:T(8,128)(2,1)} %copy.103), calls=%async_computation.2 | async-start | bytes 2097152 | tf_op jit(solution)/shard_map/all_to_all | solution.py:80
  266.3 90.6 %reduce-scatter.2.cloned.1.call-start = ((), (), s32[]{:S(2)}) async-start(), calls=%async_computation.5 | async-start | bytes 5242880 | tf_op jit(solution)/shard_map/reduce_scatter | solution.py:98
  270.8 5.7 %copy-start = (f32[8,1024,512]{2,1,0:T(8,128)}, f32[8,1024,512]{2,1,0:T(8,128)S(1)}, u32[]{:S(2)}) copy-start(f32[8,1024,512]{2,1,0:T(8,128)S(1)} %get-tuple-element.40) | copy-start | bytes 50331652
Sparse Core Ops, SparseCore 0:
  9.4 207.5 all-gather.1
  310.5 46.2 reduce-scatter.1
where the time goes:
time: 366 us; the launch traced here: 364 us
  waiting for transfers between devices  260 us (71%)
  local copies, waits for them, and re-layouts  33.7 us (9%)
  matrix products  28.8 us (8%)
  starting transfers between devices  20.2 us (6%)
  between operations  13.6 us (4%)
  other arithmetic  6.83 us (2%)
    ppermute x1, waiting for transfers between devices, shifted(): return lax.ppermute(shard, axis, pairs)  206 us
    reduce_scatter x1, waiting for transfers between devices, body(): lax.psum_scatter(terms.astype(jnp.bfloat16), 'head', scatter_dimension=0,...  46.4 us
    unnamed x8, local copies, waits for them, and re-layouts  13.4 us
    dot_general x1, matrix products, one_row(): jnp.einsum('hqk,khd->qhd', rounded, pair[1], preferred_element_type=jnp.f...  9.63 us
    dot_general x1, matrix products, body(): jnp.einsum('rcf,fd->crd', attended, lax.all_gather(out_weight, 'seq', axi...  9.51 us
  transfers between devices with their start and end apart: 6, of which 4 were waited for; matrix products, arithmetic and copies ran while one was open for 14% of the time, Pallas kernels for 0%

commit v1 on v0

--- a/solution.py
+++ b/solution.py
@@ -1,9 +1,17 @@
+import functools
 import jax
 import jax.numpy as jnp
 from jax import lax
+from jax.experimental import pallas as pl
+from jax.experimental.pallas import tpu as pltpu
 from jax.sharding import PartitionSpec as P
 
 HEAD = 128
+LOG2E = 1.4426950408889634
+NEG = -1e30
+QB = 128
+VMEM = 48 * 1024 * 1024
+F32, BF16 = jnp.float32, jnp.bfloat16
 
 
 def shifted(shard, axis, by):
@@ -66,7 +74,7 @@
     return lax.map(one_row, jnp.arange(rows_dev, dtype=jnp.int32))
 
 
-def body(qkv, out_weight):
+def body_any(qkv, out_weight):
     rows_dev, cols, features = (qkv.shape[1], qkv.shape[2], qkv.shape[3])
     head_size = HEAD
     heads_local = features // head_size
@@ -99,7 +107,302 @@
     return summed
 
 
+def dense_scores(q, k):
+    return lax.dot_general(q, k, (((1,), (1,)), ((), ())), preferred_element_type=F32)
+
+
+def col_scores(q, k):
+    prod = q.astype(F32) * k.astype(F32)
+    high = prod.astype(BF16)
+    low = (prod - high.astype(F32)).astype(BF16)
+    ones = jnp.ones((2 * HEAD, HEAD), BF16)
+    return jnp.dot(jnp.concatenate([high, low], axis=1), ones, preferred_element_type=F32)
+
+
+def attend(q, dense, cols, coef):
+    rows = q.shape[0]
+    scores = []
+    for k, _, offset in dense:
+        s = dense_scores(q, k)
+        if offset is not None:
+            q_idx = lax.broadcasted_iota(jnp.int32, s.shape, 0) + offset
+            k_idx = lax.broadcasted_iota(jnp.int32, s.shape, 1)
+            s = jnp.where(k_idx <= q_idx, s, NEG)
+        scores.append(s)
+    singles = []
+    for k, _, allowed in cols:
+        c = col_scores(q, k)
+        singles.append(c if allowed is None else jnp.where(allowed, c, NEG))
+    peak = None
+    for s in scores:
+        m = jnp.broadcast_to(jnp.max(s, axis=1, keepdims=True), (rows, HEAD))
+        peak = m if peak is None else jnp.maximum(peak, m)
+    for c in singles:
+        peak = c if peak is None else jnp.maximum(peak, c)
+    total = jnp.zeros((rows, HEAD), F32)
+    out = jnp.zeros((rows, HEAD), F32)
+    for s, (_, v, _) in zip(scores, dense):
+        p = jnp.exp2((s - peak[:, :1]) * coef)
+        total = total + jnp.broadcast_to(jnp.sum(p, axis=1, keepdims=True), (rows, HEAD))
+        out = out + jnp.dot(p.astype(BF16), v, preferred_element_type=F32)
+    for c, (_, v, _) in zip(singles, cols):
+        w = jnp.exp2((c - peak) * coef)
+        total = total + w
+        out = out + w * v.astype(F32)
+    return out / total, peak * coef + jnp.log2(total)
+
+
+def pack_lse(even, odd):
+    lane = lax.broadcasted_iota(jnp.int32, even.shape, 1)
+    return jnp.transpose(jnp.where(lane == 0, even, odd))[:8]
+
+
+def unpack_lse(packed):
+    cols = jnp.transpose(packed)
+    rows = cols.shape[0]
+    return [jnp.broadcast_to(cols[:, i : i + 1], (rows, HEAD)) for i in range(2)]
+
+
+def own_kernel(coef, cols, at, keep, oq, okv, low_m, low_o, out, lse):
+    x, z = at[0], at[1]
+    first = x == 0
+
+    def pair(a, b):
+        return jnp.where(first, a, b), jnp.where(first, b, a)
+
+    q_e, q_o = pair(keep[0], oq[...])
+    k_e, k_o = pair(keep[1], okv[0])
+    v_e, v_o = pair(keep[2], okv[1])
+    lk_e, lk_o = pair(low_m[0], low_o[0])
+    lv_e, lv_o = pair(low_m[1], low_o[1])
+    below = z == 1
+    lses = []
+    for part in range(cols // QB):
+        a, b = part * QB, (part + 1) * QB
+        mine = slice(a, b)
+        col_e = (lk_e[mine], lv_e[mine], below)
+        col_o = (lk_o[mine], lv_o[mine], below)
+        q1, q2 = q_e[mine], q_o[mine]
+
+        def even(dense, singles):
+            return attend(q1, [(k_e[:b], v_e[:b], a)] + dense, singles, coef)
+
+        o1, l1 = even([], [])
+        o2, l2 = attend(q2, [(k_o[:b], v_o[:b], a), (k_e, v_e, None)], [col_e, col_o], coef)
+        ob, lb = attend(q1, [(lk_o, lv_o, None)], [col_e], coef)
+        lb = jnp.where(below, lb, NEG)
+        top = jnp.maximum(l1, lb)
+        w1, wb = jnp.exp2(l1 - top), jnp.exp2(lb - top)
+        out[0, mine] = (w1 * o1 + wb * ob) / (w1 + wb)
+        out[1, mine] = o2
+        lses.append(pack_lse(top + jnp.log2(w1 + wb), l2))
+    lse[0] = jnp.concatenate(lses, axis=1)
+
+
+def upper_kernel(coef, cols, at, keep, okv, low_m, low_o, qa_m, qa_o, qb_m, qb_o, out_a, lse_a, out_b, lse_b):
+    x, z = at[0], at[1]
+    first = x == 0
+
+    def pair(a, b):
+        return jnp.where(first, a, b), jnp.where(first, b, a)
+
+    k_e, k_o = pair(keep[0], okv[0])
+    v_e, v_o = pair(keep[1], okv[1])
+    lk_e, lk_o = pair(low_m[0], low_o[0])
+    lv_e, lv_o = pair(low_m[1], low_o[1])
+    below = z == 1
+    a_e, a_o = pair(qa_m[...], qa_o[...])
+    b_e, b_o = pair(qb_m[...], qb_o[...])
+    la, lb = [], []
+    for part in range(cols // QB):
+        mine = slice(part * QB, (part + 1) * QB)
+        ce, co = (k_e[mine], v_e[mine], None), (k_o[mine], v_o[mine], None)
+        le, lo = (lk_e[mine], lv_e[mine], below), (lk_o[mine], lv_o[mine], below)
+        o1, l1 = attend(a_e[mine], [(k_o, v_o, None)], [ce, le, lo], coef)
+        o2, l2 = attend(a_o[mine], [], [ce, co, le, lo], coef)
+        out_a[0, mine] = o1.astype(BF16)
+        out_a[1, mine] = o2.astype(BF16)
+        la.append(pack_lse(l1, l2))
+        o1, l1 = attend(b_e[mine], [], [ce, co, le, lo], coef)
+        o2, l2 = attend(b_o[mine], [], [ce, co, le, lo], coef)
+        out_b[0, mine] = o1.astype(BF16)
+        out_b[1, mine] = o2.astype(BF16)
+        lb.append(pack_lse(l1, l2))
+    lse_a[0] = jnp.concatenate(la, axis=1)
+    lse_b[0] = jnp.concatenate(lb, axis=1)
+
+
+def merge_kernel(at, own, own_lse, oa, la, ob, lb, out):
+    z = at[1]
+    ls, lsa, lsb = unpack_lse(own_lse[0]), unpack_lse(la[0]), unpack_lse(lb[0])
+    for row in range(2):
+        l0 = ls[row]
+        l1 = jnp.where(z >= 2, lsa[row], NEG)
+        l2 = jnp.where(z >= 3, lsb[row], NEG)
+        top = jnp.maximum(l0, jnp.maximum(l1, l2))
+        w0, w1, w2 = jnp.exp2(l0 - top), jnp.exp2(l1 - top), jnp.exp2(l2 - top)
+        mixed = w0 * own[row] + w1 * oa[row].astype(F32) + w2 * ob[row].astype(F32)
+        out[row] = (mixed / (w0 + w1 + w2)).astype(BF16)
+
+
+def head_call(kernel, at, args, outs, cols, heads, name):
+    def spec(shape, packed):
+        if packed:
+            return pl.BlockSpec((1,) + shape[1:], lambda h, at: (h, 0, 0))
+        lead = len(shape) - 1
+        return pl.BlockSpec(shape[:-1] + (HEAD,), lambda h, at: (0,) * lead + (h,))
+
+    def packed(shape):
+        return tuple(shape) == (heads, 8, cols)
+
+    return pl.pallas_call(
+        kernel,
+        out_shape=outs,
+        grid_spec=pltpu.PrefetchScalarGridSpec(
+            num_scalar_prefetch=1,
+            grid=(heads,),
+            in_specs=[spec(a.shape, packed(a.shape)) for a in args],
+            out_specs=[spec(o.shape, packed(o.shape)) for o in outs],
+        ),
+        compiler_params=pltpu.CompilerParams(vmem_limit_bytes=VMEM),
+        name=name,
+    )(at, *args)
+
+
+def project_kernel(at, a_own, a_other, *refs):
+    x, core = at[0], at[2]
+    slots = (len(refs) - 2)
+    weights, send, keep = refs[:slots], refs[slots], refs[slots + 1]
+    half = a_own.shape[-1]
+    tokens = a_own.shape[3]
+    near = pl.ds(pl.multiple_of(x * half, half), half)
+    far = pl.ds(pl.multiple_of((1 - x) * half, half), half)
+    for who, out in ((1 - core, send), (core, keep)):
+        left = jnp.concatenate([a_own[r, y, who] for r in range(2) for y in range(2)], axis=0)
+        right = jnp.concatenate([a_other[r, y, who] for r in range(2) for y in range(2)], axis=0)
+        for s, w in enumerate(weights):
+            c = jnp.dot(left, w[near], preferred_element_type=F32)
+            c = c + jnp.dot(right, w[far], preferred_element_type=F32)
+            c = c.astype(BF16).reshape(2, 2, tokens, w.shape[1])
+            for y in range(2):
+                for r in range(2):
+                    out[s, y, r] = c[r, y]
+
+
+def project(at, a_own, a_other, weights):
+    cols = a_own.shape[1]
+    shape = (2, 2, 2, cols // 4, a_own.shape[2])
+    outs = [jax.ShapeDtypeStruct((len(weights), 2, 2, cols // 4, weights[0].shape[1]), BF16)] * 2
+    return pl.pallas_call(
+        project_kernel,
+        out_shape=outs,
+        in_specs=[pl.BlockSpec(memory_space=pltpu.SMEM)]
+        + [pl.BlockSpec(memory_space=pltpu.VMEM)] * (2 + len(weights)),
+        out_specs=[pl.BlockSpec(memory_space=pltpu.VMEM)] * 2,
+        compiler_params=pltpu.CompilerParams(vmem_limit_bytes=VMEM),
+        name="project",
+    )(at, a_own.reshape(shape), a_other.reshape(shape), *weights)
+
+
+def place_kernel(order, near, out):
+    out[...] = near[0, 0]
+
+
+def place(order, blocks):
+    _, _, tokens, width = blocks.shape
+    return pl.pallas_call(
+        place_kernel,
+        out_shape=jax.ShapeDtypeStruct((tokens, 8 * width), BF16),
+        grid_spec=pltpu.PrefetchScalarGridSpec(
+            num_scalar_prefetch=1,
+            grid=(8,),
+            in_specs=[pl.BlockSpec((1, 1, tokens, width), lambda i, o: (o[i] // 2, o[i] % 2, 0, 0))],
+            out_specs=pl.BlockSpec((tokens, width), lambda i, o: (0, i)),
+        ),
+        name="place",
+    )(order, blocks)
+
+
+def added(a, b):
+    return (a.astype(F32) + b.astype(F32)).astype(BF16)
+
+
+def body_eight(qkv, out_weight):
+    _, _, cols, features = qkv.shape
+    half = features // 2
+    heads = half // HEAD
+    coef = HEAD ** (-0.5) * LOG2E
+    me = lax.axis_index("seq")
+    who = lax.axis_index("head")
+    z, x, core, y = me // 2, me % 2, who % 2, who // 2
+    at = jnp.stack([x, z, core]).astype(jnp.int32)
+    local = qkv.reshape(3, cols, features)
+    keep = lax.dynamic_slice_in_dim(local, x * half, half, axis=2)
+    give = lax.dynamic_slice_in_dim(local, (1 - x) * half, half, axis=2)
+
+    def seq_perm(array, layers, cross):
+        pairs = [(2 * a + i, 2 * b + (1 - i if cross else i)) for a, b in layers for i in range(2)]
+        return lax.ppermute(array, "seq", pairs)
+
+    def head_perm(array, flip):
+        return lax.ppermute(array, "head", [(i, i ^ flip) for i in range(4)])
+
+    here = [(i, i) for i in range(4)]
+    one_down, two_down = [(2, 1), (3, 2)], [(3, 1)]
+    one_up, two_up = [(1, 2), (2, 3)], [(1, 3)]
+
+    qa_m, qa_o = seq_perm(keep[0], one_down, False), seq_perm(give[0], one_down, True)
+    qb_m, qb_o = seq_perm(keep[0], two_down, False), seq_perm(give[0], two_down, True)
+    okv = seq_perm(give[1:], here, True)
+    low_m, low_o = seq_perm(keep[1:], [(0, 1)], False), seq_perm(give[1:], [(0, 1)], True)
+    oq = seq_perm(give[0], here, True)
+    w_up = seq_perm(out_weight, [(0, 2), (1, 3)], False)
+
+    struct = jax.ShapeDtypeStruct
+    own, own_lse = head_call(
+        functools.partial(own_kernel, coef, cols), at, [keep, oq, okv, low_m, low_o],
+        [struct((2, cols, half), F32), struct((heads, 8, cols), F32)], cols, heads, "own_rows")
+    oa, la, ob, lb = head_call(
+        functools.partial(upper_kernel, coef, cols), at,
+        [keep[1:], okv, low_m, low_o, qa_m, qa_o, qb_m, qb_o],
+        [struct((2, cols, half), BF16), struct((heads, 8, cols), F32)] * 2, cols, heads, "upper_rows")
+    la, lb = seq_perm(la, one_up, False), seq_perm(lb, two_up, False)
+    oa, ob = seq_perm(oa, one_up, False), seq_perm(ob, two_up, False)
+    weight, _ = lax.optimization_barrier((out_weight, (qa_m, qb_m)))
+    w_down = seq_perm(weight, [(2, 0), (3, 1)], False)
+    w2 = jnp.where(z >= 2, w_up, w_down)
+    w1 = seq_perm(out_weight, [(0, 1), (1, 0), (2, 3), (3, 2)], False)
+    w3 = seq_perm(w2, [(0, 1), (1, 0), (2, 3), (3, 2)], False)
+
+    (a_own,) = head_call(
+        merge_kernel, at, [own, own_lse, oa, la, ob, lb], [struct((2, cols, half), BF16)], cols, heads, "merge")
+    a_other = seq_perm(a_own, here, True)
+
+    mine, theirs = [], []
+    for weights in ([out_weight, w2], [w1, w3]):
+        send, kept = project(at, a_own, a_other, weights)
+        part = added(kept, head_perm(send, 1))
+        to_y = lax.dynamic_index_in_dim(part, 1 - y, 1, keepdims=False)
+        stay = lax.dynamic_index_in_dim(part, y, 1, keepdims=False)
+        done = added(stay, head_perm(to_y, 2))
+        to_x = lax.dynamic_index_in_dim(done, 1 - x, 1, keepdims=False)
+        mine.append(lax.dynamic_index_in_dim(done, x, 1, keepdims=False))
+        theirs.append(seq_perm(to_x, here, True))
+    blocks = jnp.stack([jnp.concatenate(mine), jnp.concatenate(theirs)], axis=1)
+    slot_of = jnp.array([0, 2, 1, 3], jnp.int32)
+    index = jnp.arange(8, dtype=jnp.int32)
+    order = slot_of[jnp.bitwise_xor(index // 2, z)] * 2 + jnp.bitwise_xor(index % 2, x)
+    return place(order.astype(jnp.int32), blocks).reshape(cols // 4, 1, 8 * out_weight.shape[1])
+
+
 def solution(mesh):
     in_specs = (P(None, "seq", None, "head"), P("head", "seq"))
     out_specs = P("head", "seq", None)
+    small = mesh.shape["seq"] == 8 and mesh.shape["head"] == 4
+
+    def body(qkv, out_weight):
+        if small and qkv.shape[1] == 1:
+            return body_eight(qkv, out_weight)
+        return body_any(qkv, out_weight)
+
     return jax.shard_map(body, mesh=mesh, in_specs=in_specs, out_specs=out_specs, check_vma=False)

time: 366 us -> 311 us (0.85)
  waiting for transfers between devices: 260 us -> 113 us
  starting transfers between devices: 20.2 us -> 125 us
  Pallas kernels: 0 us -> 52.9 us
  matrix products: 28.8 us -> 0 us
  local copies, waits for them, and re-layouts: 33.7 us -> 11.5 us
  between operations: 13.6 us -> 0.32 us
    ppermute x1 -> x23, starting transfers between devices: 3.36 us -> 125 us  [the longest x19 123 us: seq_perm(): return lax.ppermute(array, 'seq', pairs)]
    ppermute x1 -> x23, waiting for transfers between devices: 206 us -> 113 us  [the longest x19 92 us: seq_perm(): return lax.ppermute(array, 'seq', pairs)]
    pallas_call x0 -> x6, Pallas kernels: none -> 52.9 us  [the longest x3 39.2 us: head_call(): pl.pallas_call(kernel, out_shape=outs, grid_spec=pltpu.PrefetchScalarGrid...]
    reduce_scatter x1 -> x0, waiting for transfers between devices: 46.4 us -> none  [body(): lax.psum_scatter(terms.astype(jnp.bfloat16), 'head', scatter_dimension=0,...]
    dot_general x5 -> x0, matrix products: 28.8 us -> none  [the longest x1 9.63 us: one_row(): jnp.einsum('hqk,khd->qhd', rounded, pair[1], preferred_element_type=jnp.f...]
    all_to_all x3 -> x0, starting transfers between devices: 16.9 us -> none  [the longest x1 6.52 us: body(): lax.all_to_all(col_part_out, 'seq', split_axis=0, concat_axis=1, tiled=True)]
    unnamed x8 -> x22, local copies, waits for them, and re-layouts: 13.4 us -> 4.89 us
    all_to_all x3 -> x0, waiting for transfers between devices: 7.72 us -> none  [the longest x1 7.2 us: body(): lax.all_to_all(col_part_out, 'seq', split_axis=0, concat_axis=1, tiled=True)]
  transfers between devices with their start and end apart: 6 -> 23, of which waited for: 4 -> 10; matrix products, arithmetic and copies ran while one was open for 14% -> 3% of each run, Pallas kernels for 0% -> 10%
where the time goes in v1:
time: 311 us; the launch traced here: 310 us
  starting transfers between devices  125 us (40%)
  waiting for transfers between devices  113 us (36%)
  Pallas kernels  52.9 us (17%)
  local copies, waits for them, and re-layouts  11.5 us (4%)
  other arithmetic  6.47 us (2%)
    ppermute x19, starting transfers between devices, seq_perm(): return lax.ppermute(array, 'seq', pairs)  123 us
    ppermute x19, waiting for transfers between devices, seq_perm(): return lax.ppermute(array, 'seq', pairs)  92 us
    pallas_call x3, Pallas kernels, head_call(): pl.pallas_call(kernel, out_shape=outs, grid_spec=pltpu.PrefetchScalarGrid...  39.2 us
    ppermute x4, waiting for transfers between devices, head_perm(): return lax.ppermute(array, 'head', [(i, i ^ flip) for i in range(4)])  21.4 us
    pallas_call x2, Pallas kernels, project(): pl.pallas_call(project_kernel, out_shape=outs, in_specs=[pl.BlockSpec(mem...  7.79 us
  transfers between devices with their start and end apart: 23, of which 10 were waited for; matrix products, arithmetic and copies ran while one was open for 3% of the time, Pallas kernels for 10%

profile of v1, /device:TPU:16, one launch (start us, length us, event | category | flops | bytes accessed | tf_op | source)
XLA Modules:
  0.0 310.0 jit_solution(3666129633775598694)
XLA Ops:
  0.0 2.2 dynamic-slice_bitcast_fusion.3
  2.2 2.3 collective-permute-start.4
  4.6 2.2 collective-permute-start.5
  6.8 2.7 dynamic-slice_bitcast_fusion.1
  11.4 1.7 collective-permute-start.3
  13.0 6.2 %collective-permute-done.4.qa_m = bf16[512,512]{1,0:T(8,128)(2,1)} collective-permute-done((bf16[512,512]{1,0:T(8,128)(2,1)}, bf16[512,512]{1,0:T(8,128)(2,1)}, u32[]{:S(2)}, u32[]{:S(2)}) %collective-permute-start.4) | collective-permute-done | bytes 524320 | tf_op jit(solution)/shard_map/ppermute | solution.py:345
  19.2 1.5 collective-permute-start.6
  20.7 10.7 %collective-permute-done.5.qa_o = bf16[512,512]{1,0:T(8,128)(2,1)} collective-permute-done((bf16[512,512]{1,0:T(8,128)(2,1)}, bf16[512,512]{1,0:T(8,128)(2,1)}, u32[]{:S(2)}, u32[]{:S(2)}) %collective-permute-start.5) | collective-permute-done | bytes 524320 | tf_op jit(solution)/shard_map/ppermute | solution.py:345
  31.4 1.5 collective-permute-start.7
  33.0 12.5 %collective-permute-done.1.okv = bf16[2,512,512]{2,1,0:T(8,128)(2,1)S(1)} collective-permute-done((bf16[2,512,512]{2,1,0:T(8,128)(2,1)}, bf16[2,512,512]{2,1,0:T(8,128)(2,1)S(1)}, u32[]{:S(2)}, u32[]{:S(2)}) %collective-permute-start.1) | collective-permute-done | bytes 1048608 | tf_op jit(solution)/shard_map/ppermute | solution.py:345
  46.9 14.5 %upper_rows.1 = (bf16[2,512,512]{2,1,0:T(8,128)(2,1)S(1)}, f32[4,8,512]{2,1,0:T(8,128)S(1)}, bf16[2,512,512]{2,1,0:T(8,128)(2,1)S(1)}, f32[4,8,512]{2,1,0:T(8,128)S(1)}) custom-call(s32[3]{0:T(128)S(1)} %pad_add_fusion.at, bf16[2,512,512]{2,1,0:T(8,128)(2,1)S(1)} %get-tuple-element.29.keep, bf16[2,512,512]{2,1,0:T(8,128)(2,1)} %copy-done, ...), custom_call_target="tpu_custom_call" | custom-call | tf_op jit(solution)/shard_map/upper_rows/pallas_call | solution.py:258
  62.3 15.5 %collective-permute-start.8 = (bf16[2,512,512]{2,1,0:T(8,128)(2,1)S(1)}, bf16[2,512,512]{2,1,0:T(8,128)(2,1)S(1)}, u32[]{:S(2)}, u32[]{:S(2)}) collective-permute-start(bf16[2,512,512]{2,1,0:T(8,128)(2,1)S(1)} %get-tuple-element.18), channel_id=1, source_target_pairs={{8,16},{12,20},{16,24},{20,28},{9,17},{13,21},{17,25},{21,29},{10,... | collective-permute-start | bytes 3145736 | tf_op jit(solution)/shard_map/ppermute | solution.py:345
  79.1 11.0 %collective-permute-start.14 = (bf16[1024,512]{1,0:T(8,128)(2,1)}, bf16[1024,512]{1,0:T(8,128)(2,1)}, u32[]{:S(2)}, u32[]{:S(2)}) collective-permute-start(bf16[1024,512]{1,0:T(8,128)(2,1)} %refs_0_.1), channel_id=1, source_target_pairs={{16,0},{20,4},{24,8},{28,12},{17,1},{21,5},{25,9},{29,13},{18,2},{... | collective-permute-start | bytes 3145736 | tf_op jit(solution)/shard_map/ppermute | solution.py:345
  90.6 11.9 %collective-permute-done.oq = bf16[512,512]{1,0:T(8,128)(2,1)S(1)} collective-permute-done((bf16[512,512]{1,0:T(8,128)(2,1)}, bf16[512,512]{1,0:T(8,128)(2,1)S(1)}, u32[]{:S(2)}, u32[]{:S(2)}) %collective-permute-start) | collective-permute-done | bytes 524320 | tf_op jit(solution)/shard_map/ppermute | solution.py:345
  103.2 77.5 %collective-permute-start.9 = (f32[4,8,512]{2,1,0:T(8,128)S(1)}, f32[4,8,512]{2,1,0:T(8,128)S(1)}, u32[]{:S(2)}, u32[]{:S(2)}) collective-permute-start(f32[4,8,512]{2,1,0:T(8,128)S(1)} %get-tuple-element.19), channel_id=1, source_target_pairs={{8,16},{12,20},{16,24},{20,28},{9,17},{13,21},{17,25},{21,29},{10,... | collective-permute-start | bytes 196616 | tf_op jit(solution)/shard_map/ppermute | solution.py:345
  180.9 19.8 %own_rows.1 = (f32[2,512,512]{2,1,0:T(8,128)}, f32[4,8,512]{2,1,0:T(8,128)S(1)}) custom-call(s32[3]{0:T(128)S(1)} %pad_add_fusion.at, bf16[3,512,512]{2,1,0:T(8,128)(2,1)S(1)} %dynamic-slice_bitcast_fusion.keep, bf16[512,512]{1,0:T(8,128)(2,1)S(1)} %collective-permute-done.oq, bf16[2,512,512]{2,1,0:T(8,128)(2,1)S(1)} %copy-done.1, ...), custom_call_target="tpu_custom_call" | custom-call | tf_op jit(solution)/shard_map/own_rows/pallas_call | solution.py:258
  200.7 1.6 copy-done.4
  202.3 4.9 %merge.1 = bf16[2,512,512]{2,1,0:T(8,128)(2,1)S(1)} custom-call(s32[3]{0:T(128)S(1)} %pad_add_fusion.at, f32[2,512,512]{2,1,0:T(8,128)S(1)} %copy-done.4, f32[4,8,512]{2,1,0:T(8,128)S(1)} %get-tuple-element.17.own_lse, bf16[2,512,512]{2,1,0:T(8,128)(2,1)S(1)} %collective-permute-done.8.oa, f32[4,8,512]{2,1,0:T(8,128)S(1)} %collective-permute-done.9.la, ...), custom_call_target="tpu_custom_call" | custom-call | tf_op jit(solution)/shard_map/merge/pallas_call | solution.py:258
  207.9 1.3 broadcast_select_fusion.refs_1_
  209.2 2.1 collective-permute-start.18
  211.3 20.8 %collective-permute-done.12 = bf16[2,512,512]{2,1,0:T(8,128)(2,1)S(1)} collective-permute-done((bf16[2,512,512]{2,1,0:T(8,128)(2,1)S(1)}, bf16[2,512,512]{2,1,0:T(8,128)(2,1)S(1)}, u32[]{:S(2)}, u32[]{:S(2)}) %collective-permute-start.12) | collective-permute-done | bytes 1048608 | tf_op jit(solution)/shard_map/ppermute | solution.py:345
  232.1 3.9 %project.2 = (bf16[2,2,2,128,512]{4,3,2,1,0:T(8,128)(2,1)}, bf16[2,2,2,128,512]{4,3,2,1,0:T(8,128)(2,1)S(1)}) custom-call(s32[3]{0:T(128)S(1)} %pad_add_fusion.at, bf16[2,2,2,128,512]{4,3,2,1,0:T(8,128)(2,1)S(1)} %bitcast.40, bf16[2,2,2,128,512]{4,3,2,1,0:T(8,128)(2,1)S(1)} %bitcast.42, bf16[1024,512]{1,0:T(8,128)(2,1)} %refs_0_.1, bf16[1024,512]{1,0:T(8,128)(2,1)} %copy-done.9), custom_call_target="tpu_custom_call" | custom-call | tf_op jit(solution)/shard_map/project/pallas_call | solution.py:296
  236.1 18.9 %collective-permute-done.18.refs_1_ = bf16[1024,512]{1,0:T(8,128)(2,1)S(1)} collective-permute-done((bf16[1024,512]{1,0:T(8,128)(2,1)S(1)}, bf16[1024,512]{1,0:T(8,128)(2,1)S(1)}, u32[]{:S(2)}, u32[]{:S(2)}) %collective-permute-start.18) | collective-permute-done | bytes 1048608 | tf_op jit(solution)/shard_map/ppermute | solution.py:345
  256.0 3.9 %project.3 = (bf16[2,2,2,128,512]{4,3,2,1,0:T(8,128)(2,1)}, bf16[2,2,2,128,512]{4,3,2,1,0:T(8,128)(2,1)S(1)}) custom-call(s32[3]{0:T(128)S(1)} %pad_add_fusion.at, bf16[2,2,2,128,512]{4,3,2,1,0:T(8,128)(2,1)S(1)} %bitcast.41, bf16[2,2,2,128,512]{4,3,2,1,0:T(8,128)(2,1)S(1)} %bitcast.43, bf16[1024,512]{1,0:T(8,128)(2,1)} %collective-permute-done.17.refs_0_, ...), custom_call_target="tpu_custom_call" | custom-call | tf_op jit(solution)/shard_map/project/pallas_call | solution.py:296
  260.9 1.6 add_convert_fusion.1
  263.4 1.5 collective-permute-start.16
  266.5 11.8 %collective-permute-done.16 = bf16[2,2,128,512]{3,2,1,0:T(8,128)(2,1)} collective-permute-done((bf16[2,2,128,512]{3,2,1,0:T(8,128)(2,1)}, bf16[2,2,128,512]{3,2,1,0:T(8,128)(2,1)}, u32[]{:S(2)}, u32[]{:S(2)}) %collective-permute-start.16) | collective-permute-done | bytes 524320 | tf_op jit(solution)/shard_map/ppermute | solution.py:348
  279.6 9.5 %collective-permute-done.20 = bf16[2,2,128,512]{3,2,1,0:T(8,128)(2,1)S(1)} collective-permute-done((bf16[2,2,128,512]{3,2,1,0:T(8,128)(2,1)S(1)}, bf16[2,2,128,512]{3,2,1,0:T(8,128)(2,1)S(1)}, u32[]{:S(2)}, u32[]{:S(2)}) %collective-permute-start.20) | collective-permute-done | bytes 524320 | tf_op jit(solution)/shard_map/ppermute | solution.py:348
  289.3 1.6 collective-permute-start.21
  292.1 6.6 %collective-permute-done.21 = bf16[2,128,512]{2,1,0:T(8,128)(2,1)S(1)} collective-permute-done((bf16[2,128,512]{2,1,0:T(8,128)(2,1)S(1)}, bf16[2,128,512]{2,1,0:T(8,128)(2,1)S(1)}, u32[]{:S(2)}, u32[]{:S(2)}) %collective-permute-start.21) | collective-permute-done | bytes 262176 | tf_op jit(solution)/shard_map/ppermute | solution.py:345
  298.6 4.3 %collective-permute-done.22 = bf16[2,128,512]{2,1,0:T(8,128)(2,1)S(1)} collective-permute-done((bf16[2,128,512]{2,1,0:T(8,128)(2,1)S(1)}, bf16[2,128,512]{2,1,0:T(8,128)(2,1)S(1)}, u32[]{:S(2)}, u32[]{:S(2)}) %collective-permute-start.22) | collective-permute-done | bytes 262176 | tf_op jit(solution)/shard_map/ppermute | solution.py:345
  304.1 5.9 %place.1 = bf16[128,4096]{1,0:T(8,128)(2,1)} custom-call(s32[8]{0:T(128)} %fusion.5.order, bf16[4,2,128,512]{3,2,1,0:T(8,128)(2,1)} %pad_maximum_fusion.near), custom_call_target="tpu_custom_call" | custom-call | tf_op jit(solution)/shard_map/place/pallas_call | solution.py:313
  (62 shorter events, 15.6 us)
Async XLA Ops:
  2.2 17.0 %collective-permute-start.4 = (bf16[512,512]{1,0:T(8,128)(2,1)}, bf16[512,512]{1,0:T(8,128)(2,1)}, u32[]{:S(2)}, u32[]{:S(2)}) collective-permute-start(bf16[512,512]{1,0:T(8,128)(2,1)} %get-tuple-element.27), channel_id=1, source_target_pairs={{16,8},{20,12},{24,16},{28,20},{17,9},{21,13},{25,17},{29,21},{18,... | collective-permute-start | bytes 1572872 | tf_op jit(solution)/shard_map/ppermute | solution.py:345
  4.6 26.9 %collective-permute-start.5 = (bf16[512,512]{1,0:T(8,128)(2,1)}, bf16[512,512]{1,0:T(8,128)(2,1)}, u32[]{:S(2)}, u32[]{:S(2)}) collective-permute-start(bf16[512,512]{1,0:T(8,128)(2,1)} %get-tuple-element.28), channel_id=1, source_target_pairs={{16,12},{20,8},{24,20},{28,16},{17,13},{21,9},{25,21},{29,17},{18,... | collective-permute-start | bytes 1572872 | tf_op jit(solution)/shard_map/ppermute | solution.py:345
  9.5 36.1 %collective-permute-start.1 = (bf16[2,512,512]{2,1,0:T(8,128)(2,1)}, bf16[2,512,512]{2,1,0:T(8,128)(2,1)S(1)}, u32[]{:S(2)}, u32[]{:S(2)}) collective-permute-start(bf16[2,512,512]{2,1,0:T(8,128)(2,1)} %get-tuple-element.30), channel_id=1, source_target_pairs={{0,4},{4,0},{8,12},{12,8},{16,20},{20,16},{24,28},{28,24},{1,5},{5... | collective-permute-start | bytes 3145736 | tf_op jit(solution)/shard_map/ppermute | solution.py:345
  10.7 34.9 %collective-permute-start.2 = (bf16[2,512,512]{2,1,0:T(8,128)(2,1)S(1)}, bf16[2,512,512]{2,1,0:T(8,128)(2,1)S(1)}, u32[]{:S(2)}, u32[]{:S(2)}) collective-permute-start(bf16[2,512,512]{2,1,0:T(8,128)(2,1)S(1)} %get-tuple-element.29.keep), channel_id=1, source_target_pairs={{0,8},{4,12},{1,9},{5,13},{2,10},{6,14},{3,11},{7,15}} | collective-permute-start | bytes 3145736 | tf_op jit(solution)/shard_map/ppermute | solution.py:345
  11.4 34.2 %collective-permute-start.3 = (bf16[2,512,512]{2,1,0:T(8,128)(2,1)}, bf16[2,512,512]{2,1,0:T(8,128)(2,1)}, u32[]{:S(2)}, u32[]{:S(2)}) collective-permute-start(bf16[2,512,512]{2,1,0:T(8,128)(2,1)} %get-tuple-element.30), channel_id=1, source_target_pairs={{0,12},{4,8},{1,13},{5,9},{2,14},{6,10},{3,15},{7,11}} | collective-permute-start | bytes 3145736 | tf_op jit(solution)/shard_map/ppermute | solution.py:345
  19.2 13.8 %collective-permute-start.6 = (bf16[512,512]{1,0:T(8,128)(2,1)}, bf16[512,512]{1,0:T(8,128)(2,1)}, u32[]{:S(2)}, u32[]{:S(2)}) collective-permute-start(bf16[512,512]{1,0:T(8,128)(2,1)} %get-tuple-element.27), channel_id=1, source_target_pairs={{24,8},{28,12},{25,9},{29,13},{26,10},{30,14},{27,11},{31,15}} | collective-permute-start | bytes 1572872 | tf_op jit(solution)/shard_map/ppermute | solution.py:345
  31.4 1.6 collective-permute-start.7
  33.0 147.7 %copy-start.8 = (bf16[3,1,512,1024]{3,2,1,0:T(8,128)(2,1)S(1)}, bf16[3,1,512,1024]{3,2,1,0:T(8,128)(2,1)}, u32[]{:S(2)}) copy-start(bf16[3,1,512,1024]{3,2,1,0:T(8,128)(2,1)} %param.3) | copy-start | bytes 9437188
  45.5 1.0 copy-start
  45.5 1.3 copy-start.2
  61.4 119.5 %copy-start.1 = (bf16[2,512,512]{2,1,0:T(8,128)(2,1)S(1)}, bf16[2,512,512]{2,1,0:T(8,128)(2,1)}, u32[]{:S(2)}) copy-start(bf16[2,512,512]{2,1,0:T(8,128)(2,1)} %copy-done) | copy-start | bytes 3145732
  61.4 119.5 %copy-start.3 = (bf16[2,512,512]{2,1,0:T(8,128)(2,1)S(1)}, bf16[2,512,512]{2,1,0:T(8,128)(2,1)}, u32[]{:S(2)}) copy-start(bf16[2,512,512]{2,1,0:T(8,128)(2,1)} %copy-done.2) | copy-start | bytes 3145732
  61.4 139.3 %collective-permute-start.10 = (bf16[2,512,512]{2,1,0:T(8,128)(2,1)S(1)}, bf16[2,512,512]{2,1,0:T(8,128)(2,1)S(1)}, u32[]{:S(2)}, u32[]{:S(2)}) collective-permute-start(bf16[2,512,512]{2,1,0:T(8,128)(2,1)S(1)} %get-tuple-element.20), channel_id=1, source_target_pairs={{8,24},{12,28},{9,25},{13,29},{10,26},{14,30},{11,27},{15,31}} | collective-permute-start | bytes 3145736 | tf_op jit(solution)/shard_map/ppermute | solution.py:345
  62.3 138.5 %collective-permute-start.8 = (bf16[2,512,512]{2,1,0:T(8,128)(2,1)S(1)}, bf16[2,512,512]{2,1,0:T(8,128)(2,1)S(1)}, u32[]{:S(2)}, u32[]{:S(2)}) collective-permute-start(bf16[2,512,512]{2,1,0:T(8,128)(2,1)S(1)} %get-tuple-element.18), channel_id=1, source_target_pairs={{8,16},{12,20},{16,24},{20,28},{9,17},{13,21},{17,25},{21,29},{10,... | collective-permute-start | bytes 3145736 | tf_op jit(solution)/shard_map/ppermute | solution.py:345
  77.8 130.1 %collective-permute-start.13 = (bf16[1024,512]{1,0:T(8,128)(2,1)}, bf16[1024,512]{1,0:T(8,128)(2,1)}, u32[]{:S(2)}, u32[]{:S(2)}) collective-permute-start(bf16[1024,512]{1,0:T(8,128)(2,1)} %refs_0_.1), channel_id=1, source_target_pairs={{0,16},{4,20},{8,24},{12,28},{1,17},{5,21},{9,25},{13,29},{2,18},{... | collective-permute-start | bytes 3145736 | tf_op jit(solution)/shard_map/ppermute | solution.py:345
  79.1 128.8 %collective-permute-start.14 = (bf16[1024,512]{1,0:T(8,128)(2,1)}, bf16[1024,512]{1,0:T(8,128)(2,1)}, u32[]{:S(2)}, u32[]{:S(2)}) collective-permute-start(bf16[1024,512]{1,0:T(8,128)(2,1)} %refs_0_.1), channel_id=1, source_target_pairs={{16,0},{20,4},{24,8},{28,12},{17,1},{21,5},{25,9},{29,13},{18,2},{... | collective-permute-start | bytes 3145736 | tf_op jit(solution)/shard_map/ppermute | solution.py:345
  90.1 12.4 %collective-permute-start = (bf16[512,512]{1,0:T(8,128)(2,1)}, bf16[512,512]{1,0:T(8,128)(2,1)S(1)}, u32[]{:S(2)}, u32[]{:S(2)}) collective-permute-start(bf16[512,512]{1,0:T(8,128)(2,1)} %get-tuple-element.28), channel_id=1, source_target_pairs={{0,4},{4,0},{8,12},{12,8},{16,20},{20,16},{24,28},{28,24},{1,5},{5... | collective-permute-start | bytes 1572872 | tf_op jit(solution)/shard_map/ppermute | solution.py:345
  102.5 0.7 collective-permute-start.11
  103.2 97.5 %collective-permute-start.9 = (f32[4,8,512]{2,1,0:T(8,128)S(1)}, f32[4,8,512]{2,1,0:T(8,128)S(1)}, u32[]{:S(2)}, u32[]{:S(2)}) collective-permute-start(f32[4,8,512]{2,1,0:T(8,128)S(1)} %get-tuple-element.19), channel_id=1, source_target_pairs={{8,16},{12,20},{16,24},{20,28},{9,17},{13,21},{17,25},{21,29},{10,... | collective-permute-start | bytes 196616 | tf_op jit(solution)/shard_map/ppermute | solution.py:345
  200.7 1.6 copy-start.4
  207.2 24.9 %collective-permute-start.12 = (bf16[2,512,512]{2,1,0:T(8,128)(2,1)S(1)}, bf16[2,512,512]{2,1,0:T(8,128)(2,1)S(1)}, u32[]{:S(2)}, u32[]{:S(2)}) collective-permute-start(bf16[2,512,512]{2,1,0:T(8,128)(2,1)S(1)} %merge.1), channel_id=1, source_target_pairs={{0,4},{4,0},{8,12},{12,8},{16,20},{20,16},{24,28},{28,24},{1,5},{5... | collective-permute-start | bytes 3145736 | tf_op jit(solution)/shard_map/ppermute | solution.py:345
  207.8 28.3 %collective-permute-start.17 = (bf16[1024,512]{1,0:T(8,128)(2,1)}, bf16[1024,512]{1,0:T(8,128)(2,1)}, u32[]{:S(2)}, u32[]{:S(2)}) collective-permute-start(bf16[1024,512]{1,0:T(8,128)(2,1)} %refs_0_.1), channel_id=1, source_target_pairs={{0,8},{4,12},{8,0},{12,4},{16,24},{20,28},{24,16},{28,20},{1,9},{5... | collective-permute-start | bytes 3145736 | tf_op jit(solution)/shard_map/ppermute | solution.py:345
  209.2 22.9 %copy-start.9 = (bf16[1024,512]{1,0:T(8,128)(2,1)}, bf16[1024,512]{1,0:T(8,128)(2,1)S(1)}, u32[]{:S(2)}) copy-start(bf16[1024,512]{1,0:T(8,128)(2,1)S(1)} %broadcast_select_fusion.refs_1_) | copy-start | bytes 3145732
  209.2 45.8 %collective-permute-start.18 = (bf16[1024,512]{1,0:T(8,128)(2,1)S(1)}, bf16[1024,512]{1,0:T(8,128)(2,1)S(1)}, u32[]{:S(2)}, u32[]{:S(2)}) collective-permute-start(bf16[1024,512]{1,0:T(8,128)(2,1)S(1)} %broadcast_select_fusion.refs_1_), channel_id=1, source_target_pairs={{0,8},{4,12},{8,0},{12,4},{16,24},{20,28},{24,16},{28,20},{1,9},{5... | collective-permute-start | bytes 3145736 | tf_op jit(solution)/shard_map/ppermute | solution.py:345
  236.0 24.9 %collective-permute-start.15 = (bf16[2,2,2,128,512]{4,3,2,1,0:T(8,128)(2,1)}, bf16[2,2,2,128,512]{4,3,2,1,0:T(8,128)(2,1)}, u32[]{:S(2)}, u32[]{:S(2)}) collective-permute-start(bf16[2,2,2,128,512]{4,3,2,1,0:T(8,128)(2,1)} %get-tuple-element.24), channel_id=1, source_target_pairs={{0,1},{1,0},{2,3},{3,2},{4,5},{5,4},{6,7},{7,6},{8,9},{9,8},{10,11... | collective-permute-start | bytes 3145736 | tf_op jit(solution)/shard_map/ppermute | solution.py:348
  260.9 4.0 %collective-permute-start.19 = (bf16[2,2,2,128,512]{4,3,2,1,0:T(8,128)(2,1)}, bf16[2,2,2,128,512]{4,3,2,1,0:T(8,128)(2,1)S(1)}, u32[]{:S(2)}, u32[]{:S(2)}) collective-permute-start(bf16[2,2,2,128,512]{4,3,2,1,0:T(8,128)(2,1)} %get-tuple-element.26), channel_id=1, source_target_pairs={{0,1},{1,0},{2,3},{3,2},{4,5},{5,4},{6,7},{7,6},{8,9},{9,8},{10,11... | collective-permute-start | bytes 3145736 | tf_op jit(solution)/shard_map/ppermute | solution.py:348
  260.9 4.0 %copy-start.6 = (bf16[2,2,2,128,512]{4,3,2,1,0:T(8,128)(2,1)S(1)}, bf16[2,2,2,128,512]{4,3,2,1,0:T(8,128)(2,1)}, u32[]{:S(2)}) copy-start(bf16[2,2,2,128,512]{4,3,2,1,0:T(8,128)(2,1)} %copy-done.5) | copy-start | bytes 3145732
  263.4 15.0 %collective-permute-start.16 = (bf16[2,2,128,512]{3,2,1,0:T(8,128)(2,1)}, bf16[2,2,128,512]{3,2,1,0:T(8,128)(2,1)}, u32[]{:S(2)}, u32[]{:S(2)}) collective-permute-start(bf16[2,2,128,512]{3,2,1,0:T(8,128)(2,1)} %dynamic-slice_bitcast_fusion.6), channel_id=1, source_target_pairs={{0,2},{1,3},{2,0},{3,1},{4,6},{5,7},{6,4},{7,5},{8,10},{9,11},{10,... | collective-permute-start | bytes 1572872 | tf_op jit(solution)/shard_map/ppermute | solution.py:348
  264.9 1.0 copy-start.7
  265.3 23.9 %collective-permute-start.20 = (bf16[2,2,128,512]{3,2,1,0:T(8,128)(2,1)S(1)}, bf16[2,2,128,512]{3,2,1,0:T(8,128)(2,1)S(1)}, u32[]{:S(2)}, u32[]{:S(2)}) collective-permute-start(bf16[2,2,128,512]{3,2,1,0:T(8,128)(2,1)S(1)} %dynamic-slice_bitcast_fusion.5), channel_id=1, source_target_pairs={{0,2},{1,3},{2,0},{3,1},{4,6},{5,7},{6,4},{7,5},{8,10},{9,11},{10,... | collective-permute-start | bytes 1572872 | tf_op jit(solution)/shard_map/ppermute | solution.py:348
  289.3 9.3 %collective-permute-start.21 = (bf16[2,128,512]{2,1,0:T(8,128)(2,1)S(1)}, bf16[2,128,512]{2,1,0:T(8,128)(2,1)S(1)}, u32[]{:S(2)}, u32[]{:S(2)}) collective-permute-start(bf16[2,128,512]{2,1,0:T(8,128)(2,1)S(1)} %get-tuple-element.32), channel_id=1, source_target_pairs={{0,4},{4,0},{8,12},{12,8},{16,20},{20,16},{24,28},{28,24},{1,5},{5... | collective-permute-start | bytes 786440 | tf_op jit(solution)/shard_map/ppermute | solution.py:345
  290.9 12.1 %collective-permute-start.22 = (bf16[2,128,512]{2,1,0:T(8,128)(2,1)S(1)}, bf16[2,128,512]{2,1,0:T(8,128)(2,1)S(1)}, u32[]{:S(2)}, u32[]{:S(2)}) collective-permute-start(bf16[2,128,512]{2,1,0:T(8,128)(2,1)S(1)} %get-tuple-element.34), channel_id=1, source_target_pairs={{0,4},{4,0},{8,12},{12,8},{16,20},{20,16},{24,28},{28,24},{1,5},{5... | collective-permute-start | bytes 786440 | tf_op jit(solution)/shard_map/ppermute | solution.py:345
  (2 other events, 1.9 us)

commit v2 on v0

--- a/solution.py
+++ b/solution.py
@@ -1,9 +1,17 @@
+import functools
 import jax
 import jax.numpy as jnp
 from jax import lax
+from jax.experimental import pallas as pl
+from jax.experimental.pallas import tpu as pltpu
 from jax.sharding import PartitionSpec as P
 
 HEAD = 128
+LOG2E = 1.4426950408889634
+NEG = -1e30
+QB = 128
+VMEM = 48 * 1024 * 1024
+F32, BF16 = jnp.float32, jnp.bfloat16
 
 
 def shifted(shard, axis, by):
@@ -66,7 +74,7 @@
     return lax.map(one_row, jnp.arange(rows_dev, dtype=jnp.int32))
 
 
-def body(qkv, out_weight):
+def body_any(qkv, out_weight):
     rows_dev, cols, features = (qkv.shape[1], qkv.shape[2], qkv.shape[3])
     head_size = HEAD
     heads_local = features // head_size
@@ -99,7 +107,382 @@
     return summed
 
 
+def dense_scores(q, k):
+    return lax.dot_general(q, k, (((1,), (1,)), ((), ())), preferred_element_type=F32)
+
+
+def col_scores(q, k):
+    prod = q * k
+    high = prod.astype(BF16)
+    low = (prod - high.astype(F32)).astype(BF16)
+    ones = jnp.ones((2 * HEAD, HEAD), BF16)
+    return jnp.dot(jnp.concatenate([high, low], axis=1), ones, preferred_element_type=F32)
+
+
+def with_ones(v):
+    return jnp.concatenate([v, jnp.ones_like(v)], axis=1)
+
+
+def attend(q, dense, cols, coef):
+    rows = q.shape[0]
+    scores = []
+    for k, _, allowed in dense:
+        s = dense_scores(q, k)
+        scores.append(s if allowed is None else jnp.where(allowed, s, NEG))
+    singles = []
+    if cols:
+        wide = q.astype(F32)
+    for k, _, allowed in cols:
+        c = col_scores(wide, k)
+        singles.append(c if allowed is None else jnp.where(allowed, c, NEG))
+    peak = None
+    for s in scores:
+        for j in range(s.shape[1] // HEAD):
+            part = s[:, j * HEAD : (j + 1) * HEAD]
+            peak = part if peak is None else jnp.maximum(peak, part)
+    if peak is not None:
+        peak = jnp.broadcast_to(jnp.max(peak, axis=1, keepdims=True), (rows, HEAD))
+    for c in singles:
+        peak = c if peak is None else jnp.maximum(peak, c)
+    peak = peak * coef
+    both = None
+    for s, (_, v, _) in zip(scores, dense):
+        tiled = jnp.concatenate([peak] * (s.shape[1] // HEAD), axis=1)
+        p = jnp.exp2(s * coef - tiled).astype(BF16)
+        term = jnp.dot(p, v, preferred_element_type=F32)
+        both = term if both is None else both + term
+    out = None if both is None else both[:, :HEAD]
+    total = None if both is None else both[:, HEAD:]
+    for c, (_, v, _) in zip(singles, cols):
+        w = jnp.exp2(c * coef - peak)
+        total = w if total is None else total + w
+        out = w * v if out is None else out + w * v
+    return out / total, peak + jnp.log2(total)
+
+
+def lse_rows(even, odd):
+    lane = lax.broadcasted_iota(jnp.int32, (HEAD, HEAD), 1)
+    evens, odds = [], []
+    for t in range(even.shape[0] // HEAD):
+        block = slice(t * HEAD, (t + 1) * HEAD)
+        turned = jnp.transpose(jnp.where(lane == 0, even[block], odd[block]))
+        evens.append(turned[0:1])
+        odds.append(turned[1:2])
+    return evens, odds
+
+
+def put_lse(ref, base, evens, odds):
+    rows = jnp.concatenate(evens + odds, axis=0)
+    pad = (-rows.shape[0]) % 16
+    if pad:
+        rows = jnp.concatenate([rows, jnp.zeros((pad, HEAD), F32)], axis=0)
+    count = rows.shape[0]
+    for piece in range(3):
+        part = rows.astype(BF16)
+        ref[pl.ds(base + piece * count, count), :] = part
+        rows = rows - part.astype(F32)
+
+
+def get_lse(ref, base, cols):
+    blocks = cols // HEAD
+    count = -(-2 * blocks // 16) * 16
+    rows = sum(ref[pl.ds(base + piece * count, count), :].astype(F32) for piece in range(3))
+    turned = [
+        jnp.transpose(jnp.broadcast_to(rows[t : t + 1], (HEAD, HEAD))) for t in range(2 * blocks)
+    ]
+    return jnp.concatenate(turned[:blocks], axis=0), jnp.concatenate(turned[blocks:], axis=0)
+
+
+def lse_height(cols):
+    return 3 * (-(-2 * (cols // HEAD) // 16) * 16)
+
+
+def own_kernel(coef, cols, at, q, kv_m, kv_o, low_m, low_o, out):
+    x, z = at[0], at[1]
+    below = z == 1
+    block = 256
+    tri = lax.broadcasted_iota(jnp.int32, (block, block), 1) <= lax.broadcasted_iota(
+        jnp.int32, (block, block), 0
+    )
+    first = x == 0
+    k_e, k_o = jnp.where(first, kv_m[0], kv_o[0]), jnp.where(first, kv_o[0], kv_m[0])
+    v_e, v_o = jnp.where(first, kv_m[1], kv_o[1]), jnp.where(first, kv_o[1], kv_m[1])
+    v_e, v_o = with_ones(v_e), with_ones(v_o)
+    lk_e = jnp.where(first, low_m[0], low_o[0])
+    lk_o = jnp.where(first, low_o[0], low_m[0])
+    lv_e = jnp.where(first, low_m[1], low_o[1])
+    lv_o = jnp.where(first, low_o[1], low_m[1])
+    lv_o1 = with_ones(lv_o)
+    evens, odds = [], []
+    for part in range(cols // block):
+        a, b = part * block, (part + 1) * block
+        mine = slice(a, b)
+        col_e = (lk_e[mine].astype(F32), lv_e[mine].astype(F32), below)
+        col_o = (lk_o[mine].astype(F32), lv_o[mine].astype(F32), below)
+
+        def causal(k, v):
+            blocks = [(k[a:b], v[a:b], tri)]
+            return blocks if part == 0 else [(k[:a], v[:a], None)] + blocks
+
+        o1, l1 = attend(q[0, mine], causal(k_e, v_e) + [(lk_o, lv_o1, below)], [col_e], coef)
+        o2, l2 = attend(q[1, mine], causal(k_o, v_o) + [(k_e, v_e, None)], [col_e, col_o], coef)
+        out[mine] = o1.astype(BF16)
+        out[cols + a : cols + b] = o2.astype(BF16)
+        e, o = lse_rows(l1, l2)
+        evens, odds = evens + e, odds + o
+    put_lse(out, 2 * cols, evens, odds)
+
+
+def upper_kernel(coef, cols, at, qa, qb, kv_m, kv_o, low_m, low_o, out_a, out_b):
+    x, z = at[0], at[1]
+    below = z == 1
+    first = x == 0
+    block = 256
+    k_e, k_o = jnp.where(first, kv_m[0], kv_o[0]), jnp.where(first, kv_o[0], kv_m[0])
+    v_e, v_o = jnp.where(first, kv_m[1], kv_o[1]), jnp.where(first, kv_o[1], kv_m[1])
+    v_o1 = with_ones(v_o)
+    rows_a, rows_b = ([], []), ([], [])
+    for part in range(cols // block):
+        a, b = part * block, (part + 1) * block
+        mine = slice(a, b)
+        m_k, m_v = low_m[0, mine].astype(F32), low_m[1, mine].astype(F32)
+        o_k, o_v = low_o[0, mine].astype(F32), low_o[1, mine].astype(F32)
+        ce = (k_e[mine].astype(F32), v_e[mine].astype(F32), None)
+        co = (k_o[mine].astype(F32), v_o[mine].astype(F32), None)
+        low = [(m_k, m_v, below), (o_k, o_v, below)]
+        for q, out, rows, dense, singles in (
+            (qa, out_a, rows_a, [(k_o, v_o1, None)], [ce]),
+            (qb, out_b, rows_b, [], [ce, co]),
+        ):
+            o1, l1 = attend(q[0, mine], dense, singles + low, coef)
+            o2, l2 = attend(q[1, mine], [], [ce, co] + low, coef)
+            out[mine] = o1.astype(BF16)
+            out[cols + a : cols + b] = o2.astype(BF16)
+            e, o = lse_rows(l1, l2)
+            rows[0].extend(e)
+            rows[1].extend(o)
+    put_lse(out_a, 2 * cols, *rows_a)
+    put_lse(out_b, 2 * cols, *rows_b)
+
+
+def merge_kernel(cols, at, own, oa, ob, out):
+    z = at[1]
+    own_l, a_l, b_l = (get_lse(ref, 2 * cols, cols) for ref in (own, oa, ob))
+    for row in range(2):
+        tokens = slice(row * cols, (row + 1) * cols)
+        l0 = own_l[row]
+        l1 = jnp.where(z >= 2, a_l[row], NEG)
+        l2 = jnp.where(z >= 3, b_l[row], NEG)
+        top = jnp.maximum(l0, jnp.maximum(l1, l2))
+        w0, w1, w2 = jnp.exp2(l0 - top), jnp.exp2(l1 - top), jnp.exp2(l2 - top)
+        mixed = w0 * own[tokens].astype(F32) + w1 * oa[tokens].astype(F32) + w2 * ob[tokens].astype(F32)
+        out[row] = (mixed / (w0 + w1 + w2)).astype(BF16)
+
+
+def cost(us):
+    return pl.CostEstimate(flops=int(us * 1.1e9), bytes_accessed=int(us * 1e6), transcendentals=0)
+
+
+def head_call(kernel, at, args, outs, heads, name, us):
+    def spec(shape):
+        lead = len(shape) - 1
+        return pl.BlockSpec(tuple(shape[:-1]) + (HEAD,), lambda h, at: (0,) * lead + (h,))
+
+    return pl.pallas_call(
+        kernel,
+        out_shape=outs,
+        grid_spec=pltpu.PrefetchScalarGridSpec(
+            num_scalar_prefetch=1,
+            grid=(heads,),
+            in_specs=[spec(a.shape) for a in args],
+            out_specs=[spec(o.shape) for o in outs],
+        ),
+        compiler_params=pltpu.CompilerParams(vmem_limit_bytes=VMEM),
+        cost_estimate=cost(us),
+        name=name,
+    )(at, *args)
+
+
+def project_kernel(chunks, at, *refs):
+    x, core = at[0], at[2]
+    near, far = refs[:chunks], refs[chunks : 2 * chunks]
+    weights, send, keep = refs[2 * chunks : -2], refs[-2], refs[-1]
+    width = near[0].shape[-1]
+    tokens = near[0].shape[3]
+    half = width * chunks
+    for who, out in ((1 - core, send), (core, keep)):
+
+        def rows(ref):
+            return jnp.concatenate([ref[r, y, who] for y in range(2) for r in range(2)], axis=0)
+
+        left = jnp.concatenate([rows(ref) for ref in near], axis=1)
+        right = jnp.concatenate([rows(ref) for ref in far], axis=1)
+        for s, w in enumerate(weights):
+            c = jnp.dot(left, w[pl.ds(pl.multiple_of(x * half, half), half)], preferred_element_type=F32)
+            c = c + jnp.dot(right, w[pl.ds(pl.multiple_of((1 - x) * half, half), half)], preferred_element_type=F32)
+            out[s] = c.astype(BF16).reshape(2, 2, tokens, w.shape[1])
+
+
+def project(at, near, far, weights):
+    _, cols, width = near[0].shape
+    shape = (2, 2, 2, cols // 4, width)
+    outs = [jax.ShapeDtypeStruct((len(weights), 2, 2, cols // 4, weights[0].shape[1]), BF16)] * 2
+    args = [a.reshape(shape) for a in near + far] + weights
+    return pl.pallas_call(
+        functools.partial(project_kernel, len(near)),
+        out_shape=outs,
+        in_specs=[pl.BlockSpec(memory_space=pltpu.SMEM)] + [pl.BlockSpec(memory_space=pltpu.VMEM)] * len(args),
+        out_specs=[pl.BlockSpec(memory_space=pltpu.VMEM)] * 2,
+        compiler_params=pltpu.CompilerParams(vmem_limit_bytes=VMEM),
+        cost_estimate=cost(4),
+        name="project",
+    )(at, *args)
+
+
+def place_kernel(at, layer, *refs):
+    x, out = at[0], refs[-1]
+    slot = 0
+    for mine, theirs in zip(refs[:-1:2], refs[1:-1:2]):
+        width = mine.shape[-1]
+        for s in range(mine.shape[0]):
+            base = layer[slot] * 2
+            out[:, pl.ds(pl.multiple_of((base + x) * width, width), width)] = mine[s]
+            out[:, pl.ds(pl.multiple_of((base + 1 - x) * width, width), width)] = theirs[s]
+            slot += 1
+
+
+def place(at, layer, parts):
+    _, tokens, width = parts[0].shape
+    total = sum(p.shape[0] for p in parts)
+    return pl.pallas_call(
+        place_kernel,
+        out_shape=jax.ShapeDtypeStruct((tokens, total * width), BF16),
+        in_specs=[pl.BlockSpec(memory_space=pltpu.SMEM)] * 2 + [pl.BlockSpec(memory_space=pltpu.VMEM)] * len(parts),
+        out_specs=pl.BlockSpec(memory_space=pltpu.VMEM),
+        cost_estimate=cost(2),
+        name="place",
+    )(at, layer, *parts)
+
+
+def added(a, b):
+    return (a.astype(F32) + b.astype(F32)).astype(BF16)
+
+
+def after(value, *earlier):
+    return lax.optimization_barrier((value, earlier))[0]
+
+
+def body_eight(qkv, out_weight):
+    _, _, cols, features = qkv.shape
+    half = features // 2
+    chunks = 2
+    width = half // chunks
+    heads = width // HEAD
+    coef = HEAD ** (-0.5) * LOG2E
+    me = lax.axis_index("seq")
+    who = lax.axis_index("head")
+    z, x, core, y = me // 2, me % 2, who % 2, who // 2
+    at = jnp.stack([x, z, core]).astype(jnp.int32)
+    local = qkv.reshape(3, cols, features)
+    first = x == 0
+
+    def seq_perm(array, *layers, cross=False):
+        pairs = [(2 * a + i, 2 * b + (1 - i if cross else i)) for a, b in layers for i in range(2)]
+        return lax.ppermute(array, "seq", pairs)
+
+    def swap(array):
+        return seq_perm(array, (0, 0), (1, 1), (2, 2), (3, 3), cross=True)
+
+    def head_perm(array, flip):
+        return lax.ppermute(array, "head", [(i, i ^ flip) for i in range(4)])
+
+    def keep(array, lo, hi, c):
+        return lax.dynamic_slice(array, (lo, 0, x * half + c * width), (hi - lo, cols, width))
+
+    def give(array, lo, hi, c):
+        return lax.dynamic_slice(array, (lo, 0, (1 - x) * half + c * width), (hi - lo, cols, width))
+
+    q, kv, low, qa, qb = [], [], [], [], []
+    w_first = seq_perm(out_weight, (1, 2), (2, 3))
+    for c in range(chunks):
+        if c == 0:
+            for_q = for_low = local
+        else:
+            for_q = after(local, kv[0][1])
+            for_low = after(local, low[0])
+        mine, other = keep(for_q, 0, 1, c), swap(give(for_q, 0, 1, c))
+        q.append(jnp.concatenate([jnp.where(first, mine, other), jnp.where(first, other, mine)]))
+        low.append((seq_perm(keep(for_low, 1, 3, c), (0, 1)), seq_perm(give(for_low, 1, 3, c), (0, 1), cross=True)))
+        for_kv = after(local, other) if c == 0 else for_q
+        kv.append((keep(for_kv, 1, 3, c), swap(give(for_kv, 1, 3, c))))
+        going = q[c] if c == 0 else after(q[c], qa[0], qb[0])
+        qa.append(seq_perm(going, (2, 1), (3, 2)))
+        qb.append(seq_perm(going, (3, 1)))
+
+    struct = jax.ShapeDtypeStruct
+    partial = struct((2 * cols + lse_height(cols), width), BF16)
+    oa, ob, own, sent = [], [], [], []
+    for c in range(chunks):
+        at_c = at if c == 0 else after(at, own[0])
+        a, b = head_call(
+            functools.partial(upper_kernel, coef, cols), at_c, [qa[c], qb[c], *kv[c], *low[c]],
+            [partial] * 2, heads, "upper_rows", 4)
+        sent.append(a)
+        oa.append(seq_perm(a, (1, 2), (2, 3)))
+        ob.append(seq_perm(b, (1, 3)))
+        (mine,) = head_call(
+            functools.partial(own_kernel, coef, cols), after(at, a), [q[c], *kv[c], *low[c]], [partial],
+            heads, "own_rows", 4)
+        own.append(mine)
+
+    w_second = seq_perm(after(out_weight, low[1]), (0, 1), (1, 0), (3, 2))
+    w_third = seq_perm(after(out_weight, qa[1], qb[1]), (2, 1))
+    w_fourth = seq_perm(w_first, (2, 3))
+    w_fifth = seq_perm(jnp.where(z == 1, w_third, w_second), (1, 0), (2, 1))
+    w_sixth = seq_perm(w_second, (1, 2))
+    w_last = seq_perm(jnp.where(z == 1, w_fifth, w_sixth), (1, 0), (2, 3))
+    slot_a = jnp.where(z == 3, w_fourth, w_second)
+    slot_b = jnp.where(z == 0, w_fifth, jnp.where(z == 1, w_third, w_first))
+    slot_c = jnp.where(z == 1, w_fifth, jnp.where(z == 2, w_sixth, w_last))
+    layer = jnp.stack([
+        z,
+        jnp.array([1, 0, 3, 1], jnp.int32)[z],
+        jnp.array([2, 2, 1, 2], jnp.int32)[z],
+        jnp.array([3, 3, 0, 0], jnp.int32)[z],
+    ]).astype(jnp.int32)
+
+    near, far = [], []
+    for c in range(chunks):
+        (a,) = head_call(
+            functools.partial(merge_kernel, cols), after(at, sent[-1]), [own[c], oa[c], ob[c]],
+            [struct((2, cols, width), BF16)], heads, "merge", 2)
+        near.append(a)
+        far.append(swap(a))
+
+    parts = []
+    previous = None
+    for weights in ([out_weight, slot_a], [slot_b, slot_c]):
+        if previous is not None:
+            weights = [after(w, previous) for w in weights]
+        send, kept = project(at, near, far, weights)
+        part = added(kept, head_perm(send, 1))
+        previous = part
+        to_y = lax.dynamic_index_in_dim(part, 1 - y, 1, keepdims=False)
+        stay = lax.dynamic_index_in_dim(part, y, 1, keepdims=False)
+        done = added(stay, head_perm(to_y, 2))
+        theirs = swap(lax.dynamic_index_in_dim(done, 1 - x, 1, keepdims=False))
+        parts += [lax.dynamic_index_in_dim(done, x, 1, keepdims=False), theirs]
+    return place(at, layer, parts).reshape(cols // 4, 1, 8 * out_weight.shape[1])
+
+
 def solution(mesh):
     in_specs = (P(None, "seq", None, "head"), P("head", "seq"))
     out_specs = P("head", "seq", None)
+    small = mesh.shape["seq"] == 8 and mesh.shape["head"] == 4
+
+    def body(qkv, out_weight):
+        if small and qkv.shape[1] == 1:
+            return body_eight(qkv, out_weight)
+        return body_any(qkv, out_weight)
+
     return jax.shard_map(body, mesh=mesh, in_specs=in_specs, out_specs=out_specs, check_vma=False)

time: 366 us -> 244 us (0.67)
  waiting for transfers between devices: 260 us -> 102 us
  starting transfers between devices: 20.2 us -> 68.8 us
  Pallas kernels: 0 us -> 39.7 us
  matrix products: 28.8 us -> 0 us
  local copies, waits for them, and re-layouts: 33.7 us -> 15.9 us
  between operations: 13.6 us -> 0.6 us
  other arithmetic: 6.83 us -> 14.4 us
    ppermute x1 -> x31, waiting for transfers between devices: 206 us -> 102 us  [the longest x27 84.9 us: seq_perm(): return lax.ppermute(array, 'seq', pairs)]
    ppermute x1 -> x31, starting transfers between devices: 3.36 us -> 68.8 us  [the longest x27 65.5 us: seq_perm(): return lax.ppermute(array, 'seq', pairs)]
    reduce_scatter x1 -> x0, waiting for transfers between devices: 46.4 us -> none  [body(): lax.psum_scatter(terms.astype(jnp.bfloat16), 'head', scatter_dimension=0,...]
    pallas_call x0 -> x9, Pallas kernels: none -> 39.7 us  [the longest x6 30.1 us: head_call(): pl.pallas_call(kernel, out_shape=outs, grid_spec=pltpu.PrefetchScalarGrid...]
    dot_general x5 -> x0, matrix products: 28.8 us -> none  [the longest x1 9.63 us: one_row(): jnp.einsum('hqk,khd->qhd', rounded, pair[1], preferred_element_type=jnp.f...]
    all_to_all x3 -> x0, starting transfers between devices: 16.9 us -> none  [the longest x1 6.52 us: body(): lax.all_to_all(col_part_out, 'seq', split_axis=0, concat_axis=1, tiled=True)]
    dynamic_slice x0 -> x9, local copies, waits for them, and re-layouts: none -> 11.6 us  [the longest x6 9.78 us: give(): lax.dynamic_slice(array, (lo, 0, (1 - x) * half + c * width), (hi - lo, c...]
    unnamed x8 -> x42, local copies, waits for them, and re-layouts: 13.4 us -> 1.84 us
  transfers between devices with their start and end apart: 6 -> 31, of which waited for: 4 -> 12; matrix products, arithmetic and copies ran while one was open for 14% -> 10% of each run, Pallas kernels for 0% -> 14%
where the time goes in v2:
time: 244 us; the launch traced here: 242 us
  waiting for transfers between devices  102 us (42%)
  starting transfers between devices  68.8 us (28%)
  Pallas kernels  39.7 us (16%)
  local copies, waits for them, and re-layouts  15.9 us (7%)
  other arithmetic  14.4 us (6%)
    ppermute x27, waiting for transfers between devices, seq_perm(): return lax.ppermute(array, 'seq', pairs)  84.9 us
    ppermute x27, starting transfers between devices, seq_perm(): return lax.ppermute(array, 'seq', pairs)  65.5 us
    pallas_call x6, Pallas kernels, head_call(): pl.pallas_call(kernel, out_shape=outs, grid_spec=pltpu.PrefetchScalarGrid...  30.1 us
    ppermute x4, waiting for transfers between devices, head_perm(): return lax.ppermute(array, 'head', [(i, i ^ flip) for i in range(4)])  17.6 us
    dynamic_slice x6, local copies, waits for them, and re-layouts, give(): lax.dynamic_slice(array, (lo, 0, (1 - x) * half + c * width), (hi - lo, c...  9.78 us
    pallas_call x2, Pallas kernels, project(): pl.pallas_call(functools.partial(project_kernel, len(near)), out_shape=ou...  7.33 us
  transfers between devices with their start and end apart: 31, of which 12 were waited for; matrix products, arithmetic and copies ran while one was open for 10% of the time, Pallas kernels for 14%

profile of v2, /device:TPU:16, one launch (start us, length us, event | category | flops | bytes accessed | tf_op | source)
XLA Modules:
  0.0 241.8 jit_solution(15667218175064759902)
XLA Ops:
  2.6 6.6 %collective-permute-done = bf16[1,512,256]{2,1,0:T(8,128)(2,1)S(1)} collective-permute-done((bf16[1,512,256]{2,1,0:T(8,128)(2,1)S(1)}, bf16[1,512,256]{2,1,0:T(8,128)(2,1)S(1)}, u32[]{:S(2)}, u32[]{:S(2)}) %collective-permute-start) | collective-permute-done | bytes 262176 | tf_op jit(solution)/shard_map/ppermute | solution.py:391
  12.0 2.3 dynamic-slice_bitcast_fusion.2
  16.4 3.5 %collective-permute-start.18 = (bf16[1024,512]{1,0:T(8,128)(2,1)S(1)}, bf16[1024,512]{1,0:T(8,128)(2,1)}, u32[]{:S(2)}, u32[]{:S(2)}) collective-permute-start(bf16[1024,512]{1,0:T(8,128)(2,1)S(1)} %copy-done.1), channel_id=1, source_target_pairs={{8,16},{12,20},{16,24},{20,28},{9,17},{13,21},{17,25},{21,29},{10,... | collective-permute-start | bytes 3145736 | tf_op jit(solution)/shard_map/ppermute | solution.py:391
  21.0 2.3 collective-permute-done.3.kv_o
  28.0 13.4 %collective-permute-start.1 = (bf16[2,512,256]{2,1,0:T(8,128)(2,1)S(1)}, bf16[2,512,256]{2,1,0:T(8,128)(2,1)}, u32[]{:S(2)}, u32[]{:S(2)}) collective-permute-start(bf16[2,512,256]{2,1,0:T(8,128)(2,1)S(1)} %pad_maximum_fusion.q), channel_id=1, source_target_pairs={{16,8},{20,12},{24,16},{28,20},{17,9},{21,13},{25,17},{29,21},{18,... | collective-permute-start | bytes 1572872 | tf_op jit(solution)/shard_map/ppermute | solution.py:391
  41.4 2.3 constant_dynamic-slice_fusion
  47.1 15.6 %collective-permute-done.1.qa = bf16[2,512,256]{2,1,0:T(8,128)(2,1)} collective-permute-done((bf16[2,512,256]{2,1,0:T(8,128)(2,1)S(1)}, bf16[2,512,256]{2,1,0:T(8,128)(2,1)}, u32[]{:S(2)}, u32[]{:S(2)}) %collective-permute-start.1) | collective-permute-done | bytes 524320 | tf_op jit(solution)/shard_map/ppermute | solution.py:391
  63.3 3.9 %collective-permute-start.7 = (bf16[2,512,256]{2,1,0:T(8,128)(2,1)S(1)}, bf16[2,512,256]{2,1,0:T(8,128)(2,1)S(1)}, u32[]{:S(2)}, u32[]{:S(2)}) collective-permute-start(bf16[2,512,256]{2,1,0:T(8,128)(2,1)S(1)} %pad_maximum_fusion.1.q), channel_id=1, source_target_pairs={{16,8},{20,12},{24,16},{28,20},{17,9},{21,13},{25,17},{29,21},{18,... | collective-permute-start | bytes 1572872 | tf_op jit(solution)/shard_map/ppermute | solution.py:391
  69.1 6.6 %upper_rows.2 = (bf16[1072,256]{1,0:T(8,128)(2,1)S(1)}, bf16[1072,256]{1,0:T(8,128)(2,1)S(1)}) custom-call(s32[3]{0:T(128)S(1)} %pad_add_fusion.at, bf16[2,512,256]{2,1,0:T(8,128)(2,1)} %collective-permute-done.1.qa, bf16[2,512,256]{2,1,0:T(8,128)(2,1)} %collective-permute-done.2.qb, bf16[2,512,256]{2,1,0:T(8,128)(2,1)S(1)} %get-tuple-element.54.kv_m, ...), custom_call_target="tpu_custom_call" | custom-call | flops 4400000000 | bytes 4000000 | tf_op jit(solution)/shard_map/upper_rows/pallas_call | solution.py:291
  75.8 3.4 %collective-permute-start.12 = (bf16[1072,256]{1,0:T(8,128)(2,1)S(1)}, bf16[1072,256]{1,0:T(8,128)(2,1)S(1)}, u32[]{:S(2)}, u32[]{:S(2)}) collective-permute-start(bf16[1072,256]{1,0:T(8,128)(2,1)S(1)} %get-tuple-element.25), channel_id=1, source_target_pairs={{8,16},{12,20},{16,24},{20,28},{9,17},{13,21},{17,25},{21,29},{10,... | collective-permute-start | bytes 1646600 | tf_op jit(solution)/shard_map/ppermute | solution.py:391
  80.5 4.7 %collective-permute-start.19 = (bf16[1024,512]{1,0:T(8,128)(2,1)}, bf16[1024,512]{1,0:T(8,128)(2,1)S(1)}, u32[]{:S(2)}, u32[]{:S(2)}) collective-permute-start(bf16[1024,512]{1,0:T(8,128)(2,1)} %collective-permute-done.18), channel_id=1, source_target_pairs={{16,24},{20,28},{17,25},{21,29},{18,26},{22,30},{19,27},{23,31}} | collective-permute-start | bytes 3145736 | tf_op jit(solution)/shard_map/ppermute | solution.py:391
  85.2 6.2 %collective-permute-done.7.qa = bf16[2,512,256]{2,1,0:T(8,128)(2,1)S(1)} collective-permute-done((bf16[2,512,256]{2,1,0:T(8,128)(2,1)S(1)}, bf16[2,512,256]{2,1,0:T(8,128)(2,1)S(1)}, u32[]{:S(2)}, u32[]{:S(2)}) %collective-permute-start.7) | collective-permute-done | bytes 524320 | tf_op jit(solution)/shard_map/ppermute | solution.py:391
  91.4 2.4 %collective-permute-start.24 = (bf16[1024,512]{1,0:T(8,128)(2,1)S(1)}, bf16[1024,512]{1,0:T(8,128)(2,1)S(1)}, u32[]{:S(2)}, u32[]{:S(2)}) collective-permute-start(bf16[1024,512]{1,0:T(8,128)(2,1)S(1)} %copy-done.1), channel_id=1, source_target_pairs={{16,8},{20,12},{17,9},{21,13},{18,10},{22,14},{19,11},{23,15}} | collective-permute-start | bytes 3145736 | tf_op jit(solution)/shard_map/ppermute | solution.py:391
  93.9 6.0 %own_rows.2.own = bf16[1072,256]{1,0:T(8,128)(2,1)S(1)} custom-call(s32[3]{0:T(128)S(1)} %pad_add_fusion.at, bf16[2,512,256]{2,1,0:T(8,128)(2,1)S(1)} %pad_maximum_fusion.q, bf16[2,512,256]{2,1,0:T(8,128)(2,1)S(1)} %get-tuple-element.54.kv_m, bf16[2,512,256]{2,1,0:T(8,128)(2,1)S(1)} %collective-permute-done.3.kv_o, ...), custom_call_target="tpu_custom_call" | custom-call | flops 4400000000 | bytes 4000000 | tf_op jit(solution)/shard_map/own_rows/pallas_call | solution.py:291
  100.8 6.7 %upper_rows.3 = (bf16[1072,256]{1,0:T(8,128)(2,1)S(1)}, bf16[1072,256]{1,0:T(8,128)(2,1)S(1)}) custom-call(s32[3]{0:T(128)S(1)} %pad_add_fusion.at, bf16[2,512,256]{2,1,0:T(8,128)(2,1)S(1)} %collective-permute-done.7.qa, bf16[2,512,256]{2,1,0:T(8,128)(2,1)S(1)} %collective-permute-done.8.qb, bf16[2,512,256]{2,1,0:T(8,128)(2,1)S(1)} %get-tuple-element.50.kv_m, ...), custom_call_target="tpu_custom_call" | custom-call | flops 4400000000 | bytes 4000000 | tf_op jit(solution)/shard_map/upper_rows/pallas_call | solution.py:291
  107.4 6.0 %own_rows.3.own = bf16[1072,256]{1,0:T(8,128)(2,1)S(1)} custom-call(s32[3]{0:T(128)S(1)} %pad_add_fusion.at, bf16[2,512,256]{2,1,0:T(8,128)(2,1)S(1)} %pad_maximum_fusion.1.q, bf16[2,512,256]{2,1,0:T(8,128)(2,1)S(1)} %get-tuple-element.50.kv_m, bf16[2,512,256]{2,1,0:T(8,128)(2,1)S(1)} %collective-permute-done.9.kv_o, ...), custom_call_target="tpu_custom_call" | custom-call | flops 4400000000 | bytes 4000000 | tf_op jit(solution)/shard_map/own_rows/pallas_call | solution.py:291
  113.5 3.1 %collective-permute-start.14 = (bf16[1072,256]{1,0:T(8,128)(2,1)S(1)}, bf16[1072,256]{1,0:T(8,128)(2,1)S(1)}, u32[]{:S(2)}, u32[]{:S(2)}) collective-permute-start(bf16[1072,256]{1,0:T(8,128)(2,1)S(1)} %get-tuple-element.31), channel_id=1, source_target_pairs={{8,16},{12,20},{16,24},{20,28},{9,17},{13,21},{17,25},{21,29},{10,... | collective-permute-start | bytes 1646600 | tf_op jit(solution)/shard_map/ppermute | solution.py:391
  117.3 2.4 merge.2
  120.3 6.1 %collective-permute-done.19 = bf16[1024,512]{1,0:T(8,128)(2,1)S(1)} collective-permute-done((bf16[1024,512]{1,0:T(8,128)(2,1)}, bf16[1024,512]{1,0:T(8,128)(2,1)S(1)}, u32[]{:S(2)}, u32[]{:S(2)}) %collective-permute-start.19) | collective-permute-done | bytes 1048608 | tf_op jit(solution)/shard_map/ppermute | solution.py:391
  129.0 4.7 %collective-permute-start.25 = (bf16[1024,512]{1,0:T(8,128)(2,1)S(1)}, bf16[1024,512]{1,0:T(8,128)(2,1)S(1)}, u32[]{:S(2)}, u32[]{:S(2)}) collective-permute-start(bf16[1024,512]{1,0:T(8,128)(2,1)S(1)} %get-tuple-element.57), channel_id=1, source_target_pairs={{8,0},{12,4},{16,8},{20,12},{9,1},{13,5},{17,9},{21,13},{10,2},{14... | collective-permute-start | bytes 3145736 | tf_op jit(solution)/shard_map/ppermute | solution.py:391
  133.7 14.6 %collective-permute-done.14.oa = bf16[1072,256]{1,0:T(8,128)(2,1)S(1)} collective-permute-done((bf16[1072,256]{1,0:T(8,128)(2,1)S(1)}, bf16[1072,256]{1,0:T(8,128)(2,1)S(1)}, u32[]{:S(2)}, u32[]{:S(2)}) %collective-permute-start.14) | collective-permute-done | bytes 548896 | tf_op jit(solution)/shard_map/ppermute | solution.py:391
  148.3 2.4 merge.3
  152.3 10.9 %collective-permute-done.17 = bf16[2,512,256]{2,1,0:T(8,128)(2,1)S(1)} collective-permute-done((bf16[2,512,256]{2,1,0:T(8,128)(2,1)S(1)}, bf16[2,512,256]{2,1,0:T(8,128)(2,1)S(1)}, u32[]{:S(2)}, u32[]{:S(2)}) %collective-permute-start.17) | collective-permute-done | bytes 524320 | tf_op jit(solution)/shard_map/ppermute | solution.py:391
  163.2 3.8 %project.2 = (bf16[2,2,2,128,512]{4,3,2,1,0:T(8,128)(2,1)S(1)}, bf16[2,2,2,128,512]{4,3,2,1,0:T(8,128)(2,1)S(1)}) custom-call(s32[3]{0:T(128)S(1)} %pad_add_fusion.at, bf16[2,2,2,128,256]{4,3,2,1,0:T(8,128)(2,1)S(1)} %bitcast.36, bf16[2,2,2,128,256]{4,3,2,1,0:T(8,128)(2,1)S(1)} %bitcast.40, bf16[2,2,2,128,256]{4,3,2,1,0:T(8,128)(2,1)S(1)} %bitcast.38, ...), custom_call_target="tpu_custom_call" | custom-call | flops 4400000000 | bytes 4000000 | tf_op jit(solution)/shard_map/project/pallas_call | solution.py:331
  169.3 5.5 %collective-permute-start.27 = (bf16[1024,512]{1,0:T(8,128)(2,1)}, bf16[1024,512]{1,0:T(8,128)(2,1)}, u32[]{:S(2)}, u32[]{:S(2)}) collective-permute-start(bf16[1024,512]{1,0:T(8,128)(2,1)} %broadcast_select_fusion), channel_id=1, source_target_pairs={{8,0},{12,4},{16,24},{20,28},{9,1},{13,5},{17,25},{21,29},{10,2},{... | collective-permute-start | bytes 3145736 | tf_op jit(solution)/shard_map/ppermute | solution.py:391
  176.5 20.7 %collective-permute-done.27 = bf16[1024,512]{1,0:T(8,128)(2,1)} collective-permute-done((bf16[1024,512]{1,0:T(8,128)(2,1)}, bf16[1024,512]{1,0:T(8,128)(2,1)}, u32[]{:S(2)}, u32[]{:S(2)}) %collective-permute-start.27) | collective-permute-done | bytes 1048608 | tf_op jit(solution)/shard_map/ppermute | solution.py:391
  197.2 2.6 %select_select_fusion = (bf16[1024,512]{1,0:T(8,128)(2,1)}, bf16[1024,512]{1,0:T(8,128)(2,1)S(1)}) fusion(bf16[1024,512]{1,0:T(8,128)(2,1)S(1)} %copy-done.13, bf16[1024,512]{1,0:T(8,128)(2,1)S(1)} %copy-done.11, bf16[1024,512]{1,0:T(8,128)(2,1)} %collective-permute-done.27, pred[]{:T(512)S(6)} %eq.25, pred[]{:T(512)S(6)} %eq.24, ...), kind=kLoop, calls=%fused_computation.6 | loop fusion | flops 2097152 | bytes 7340035 | tf_op jit(solution)/shard_map/jit(_where)/select_n | solution.py:446
  199.8 3.6 %project.3 = (bf16[2,2,2,128,512]{4,3,2,1,0:T(8,128)(2,1)S(1)}, bf16[2,2,2,128,512]{4,3,2,1,0:T(8,128)(2,1)S(1)}) custom-call(s32[3]{0:T(128)S(1)} %pad_add_fusion.at, bf16[2,2,2,128,256]{4,3,2,1,0:T(8,128)(2,1)S(1)} %bitcast.37, bf16[2,2,2,128,256]{4,3,2,1,0:T(8,128)(2,1)S(1)} %bitcast.41, bf16[2,2,2,128,256]{4,3,2,1,0:T(8,128)(2,1)S(1)} %bitcast.39, ...), custom_call_target="tpu_custom_call" | custom-call | flops 4400000000 | bytes 4000000 | tf_op jit(solution)/shard_map/project/pallas_call | solution.py:331
  209.4 9.9 %collective-permute-done.22 = bf16[2,2,128,512]{3,2,1,0:T(8,128)(2,1)} collective-permute-done((bf16[2,2,128,512]{3,2,1,0:T(8,128)(2,1)}, bf16[2,2,128,512]{3,2,1,0:T(8,128)(2,1)}, u32[]{:S(2)}, u32[]{:S(2)}) %collective-permute-start.22) | collective-permute-done | bytes 524320 | tf_op jit(solution)/shard_map/ppermute | solution.py:397
  222.8 7.3 %collective-permute-done.29 = bf16[2,2,128,512]{3,2,1,0:T(8,128)(2,1)S(1)} collective-permute-done((bf16[2,2,128,512]{3,2,1,0:T(8,128)(2,1)S(1)}, bf16[2,2,128,512]{3,2,1,0:T(8,128)(2,1)S(1)}, u32[]{:S(2)}, u32[]{:S(2)}) %collective-permute-start.29) | collective-permute-done | bytes 524320 | tf_op jit(solution)/shard_map/ppermute | solution.py:397
  234.3 2.6 %pad_add_fusion.1.layer = s32[4]{0:T(128)} fusion(s32[1]{0:T(128)} %dynamic_slice.81, s32[1]{0:T(128)} %dynamic_slice.80, s32[1]{0:T(128)} %dynamic_slice.79, s32[1]{0:T(128)} %bitcast.1), kind=kLoop, calls=%fused_computation.34 | loop fusion | flops 12 | bytes 32 | tf_op jit(solution)/shard_map/stack | solution.py:447
  239.6 2.2 place.1
  (107 shorter events, 47.2 us)
Async XLA Ops:
  1.1 8.1 %collective-permute-start = (bf16[1,512,256]{2,1,0:T(8,128)(2,1)S(1)}, bf16[1,512,256]{2,1,0:T(8,128)(2,1)S(1)}, u32[]{:S(2)}, u32[]{:S(2)}) collective-permute-start(bf16[1,512,256]{2,1,0:T(8,128)(2,1)S(1)} %dynamic-slice_bitcast_fusion.8), channel_id=1, source_target_pairs={{0,4},{4,0},{8,12},{12,8},{16,20},{20,16},{24,28},{28,24},{1,5},{5... | collective-permute-start | bytes 786440 | tf_op jit(solution)/shard_map/ppermute | solution.py:391
  10.5 12.9 %collective-permute-start.3 = (bf16[2,512,256]{2,1,0:T(8,128)(2,1)S(1)}, bf16[2,512,256]{2,1,0:T(8,128)(2,1)S(1)}, u32[]{:S(2)}, u32[]{:S(2)}) collective-permute-start(bf16[2,512,256]{2,1,0:T(8,128)(2,1)S(1)} %get-tuple-element.53), channel_id=1, source_target_pairs={{0,4},{4,0},{8,12},{12,8},{16,20},{20,16},{24,28},{28,24},{1,5},{5... | collective-permute-start | bytes 1572872 | tf_op jit(solution)/shard_map/ppermute | solution.py:391
  14.3 13.7 %collective-permute-start.5 = (bf16[2,512,256]{2,1,0:T(8,128)(2,1)}, bf16[2,512,256]{2,1,0:T(8,128)(2,1)S(1)}, u32[]{:S(2)}, u32[]{:S(2)}) collective-permute-start(bf16[2,512,256]{2,1,0:T(8,128)(2,1)} %get-tuple-element.51), channel_id=1, source_target_pairs={{0,12},{4,8},{1,13},{5,9},{2,14},{6,10},{3,15},{7,11}} | collective-permute-start | bytes 1572872 | tf_op jit(solution)/shard_map/ppermute | solution.py:391
  15.0 26.5 %collective-permute-start.4 = (bf16[2,512,256]{2,1,0:T(8,128)(2,1)}, bf16[2,512,256]{2,1,0:T(8,128)(2,1)}, u32[]{:S(2)}, u32[]{:S(2)}) collective-permute-start(bf16[2,512,256]{2,1,0:T(8,128)(2,1)} %get-tuple-element.52), channel_id=1, source_target_pairs={{0,8},{4,12},{1,9},{5,13},{2,10},{6,14},{3,11},{7,15}} | collective-permute-start | bytes 1572872 | tf_op jit(solution)/shard_map/ppermute | solution.py:391
  16.4 62.8 %collective-permute-start.18 = (bf16[1024,512]{1,0:T(8,128)(2,1)S(1)}, bf16[1024,512]{1,0:T(8,128)(2,1)}, u32[]{:S(2)}, u32[]{:S(2)}) collective-permute-start(bf16[1024,512]{1,0:T(8,128)(2,1)S(1)} %copy-done.1), channel_id=1, source_target_pairs={{8,16},{12,20},{16,24},{20,28},{9,17},{13,21},{17,25},{21,29},{10,... | collective-permute-start | bytes 3145736 | tf_op jit(solution)/shard_map/ppermute | solution.py:391
  25.0 20.3 %collective-permute-start.6 = (bf16[1,512,256]{2,1,0:T(8,128)(2,1)}, bf16[1,512,256]{2,1,0:T(8,128)(2,1)S(1)}, u32[]{:S(2)}, u32[]{:S(2)}) collective-permute-start(bf16[1,512,256]{2,1,0:T(8,128)(2,1)} %constant_dynamic-slice_fusion.4), channel_id=1, source_target_pairs={{0,4},{4,0},{8,12},{12,8},{16,20},{20,16},{24,28},{28,24},{1,5},{5... | collective-permute-start | bytes 786440 | tf_op jit(solution)/shard_map/ppermute | solution.py:391
  26.5 20.5 %collective-permute-start.2 = (bf16[2,512,256]{2,1,0:T(8,128)(2,1)S(1)}, bf16[2,512,256]{2,1,0:T(8,128)(2,1)}, u32[]{:S(2)}, u32[]{:S(2)}) collective-permute-start(bf16[2,512,256]{2,1,0:T(8,128)(2,1)S(1)} %pad_maximum_fusion.q), channel_id=1, source_target_pairs={{24,8},{28,12},{25,9},{29,13},{26,10},{30,14},{27,11},{31,15}} | collective-permute-start | bytes 1572872 | tf_op jit(solution)/shard_map/ppermute | solution.py:391
  28.0 34.6 %collective-permute-start.1 = (bf16[2,512,256]{2,1,0:T(8,128)(2,1)S(1)}, bf16[2,512,256]{2,1,0:T(8,128)(2,1)}, u32[]{:S(2)}, u32[]{:S(2)}) collective-permute-start(bf16[2,512,256]{2,1,0:T(8,128)(2,1)S(1)} %pad_maximum_fusion.q), channel_id=1, source_target_pairs={{16,8},{20,12},{24,16},{28,20},{17,9},{21,13},{25,17},{29,21},{18,... | collective-permute-start | bytes 1572872 | tf_op jit(solution)/shard_map/ppermute | solution.py:391
  43.7 24.8 %collective-permute-start.11 = (bf16[2,512,256]{2,1,0:T(8,128)(2,1)}, bf16[2,512,256]{2,1,0:T(8,128)(2,1)}, u32[]{:S(2)}, u32[]{:S(2)}) collective-permute-start(bf16[2,512,256]{2,1,0:T(8,128)(2,1)} %get-tuple-element.47), channel_id=1, source_target_pairs={{0,12},{4,8},{1,13},{5,9},{2,14},{6,10},{3,15},{7,11}} | collective-permute-start | bytes 1572872 | tf_op jit(solution)/shard_map/ppermute | solution.py:391
  45.2 154.5 %copy-start = (s32[3]{0:T(128)}, s32[3]{0:T(128)S(1)}, u32[]{:S(2)}) copy-start(s32[3]{0:T(128)S(1)} %pad_add_fusion.at) | copy-start | bytes 40
  45.2 30.5 %collective-permute-start.10 = (bf16[2,512,256]{2,1,0:T(8,128)(2,1)}, bf16[2,512,256]{2,1,0:T(8,128)(2,1)S(1)}, u32[]{:S(2)}, u32[]{:S(2)}) collective-permute-start(bf16[2,512,256]{2,1,0:T(8,128)(2,1)} %get-tuple-element.48), channel_id=1, source_target_pairs={{0,8},{4,12},{1,9},{5,13},{2,10},{6,14},{3,11},{7,15}} | collective-permute-start | bytes 1572872 | tf_op jit(solution)/shard_map/ppermute | solution.py:391
  62.6 17.9 %collective-permute-start.8 = (bf16[2,512,256]{2,1,0:T(8,128)(2,1)S(1)}, bf16[2,512,256]{2,1,0:T(8,128)(2,1)S(1)}, u32[]{:S(2)}, u32[]{:S(2)}) collective-permute-start(bf16[2,512,256]{2,1,0:T(8,128)(2,1)S(1)} %pad_maximum_fusion.1.q), channel_id=1, source_target_pairs={{24,8},{28,12},{25,9},{29,13},{26,10},{30,14},{27,11},{31,15}} | collective-permute-start | bytes 1572872 | tf_op jit(solution)/shard_map/ppermute | solution.py:391
  63.3 28.1 %collective-permute-start.7 = (bf16[2,512,256]{2,1,0:T(8,128)(2,1)S(1)}, bf16[2,512,256]{2,1,0:T(8,128)(2,1)S(1)}, u32[]{:S(2)}, u32[]{:S(2)}) collective-permute-start(bf16[2,512,256]{2,1,0:T(8,128)(2,1)S(1)} %pad_maximum_fusion.1.q), channel_id=1, source_target_pairs={{16,8},{20,12},{24,16},{28,20},{17,9},{21,13},{25,17},{29,21},{18,... | collective-permute-start | bytes 1572872 | tf_op jit(solution)/shard_map/ppermute | solution.py:391
  68.5 31.3 %collective-permute-start.9 = (bf16[2,512,256]{2,1,0:T(8,128)(2,1)S(1)}, bf16[2,512,256]{2,1,0:T(8,128)(2,1)S(1)}, u32[]{:S(2)}, u32[]{:S(2)}) collective-permute-start(bf16[2,512,256]{2,1,0:T(8,128)(2,1)S(1)} %get-tuple-element.49), channel_id=1, source_target_pairs={{0,4},{4,0},{8,12},{12,8},{16,20},{20,16},{24,28},{28,24},{1,5},{5... | collective-permute-start | bytes 1572872 | tf_op jit(solution)/shard_map/ppermute | solution.py:391
  75.8 40.8 %collective-permute-start.12 = (bf16[1072,256]{1,0:T(8,128)(2,1)S(1)}, bf16[1072,256]{1,0:T(8,128)(2,1)S(1)}, u32[]{:S(2)}, u32[]{:S(2)}) collective-permute-start(bf16[1072,256]{1,0:T(8,128)(2,1)S(1)} %get-tuple-element.25), channel_id=1, source_target_pairs={{8,16},{12,20},{16,24},{20,28},{9,17},{13,21},{17,25},{21,29},{10,... | collective-permute-start | bytes 1646600 | tf_op jit(solution)/shard_map/ppermute | solution.py:391
  79.2 40.5 %collective-permute-start.20 = (bf16[1024,512]{1,0:T(8,128)(2,1)S(1)}, bf16[1024,512]{1,0:T(8,128)(2,1)S(1)}, u32[]{:S(2)}, u32[]{:S(2)}) collective-permute-start(bf16[1024,512]{1,0:T(8,128)(2,1)S(1)} %copy-done.1), channel_id=1, source_target_pairs={{0,8},{4,12},{8,0},{12,4},{24,16},{28,20},{1,9},{5,13},{9,1},{13,5... | collective-permute-start | bytes 3145736 | tf_op jit(solution)/shard_map/ppermute | solution.py:391
  80.5 45.9 %collective-permute-start.19 = (bf16[1024,512]{1,0:T(8,128)(2,1)}, bf16[1024,512]{1,0:T(8,128)(2,1)S(1)}, u32[]{:S(2)}, u32[]{:S(2)}) collective-permute-start(bf16[1024,512]{1,0:T(8,128)(2,1)} %collective-permute-done.18), channel_id=1, source_target_pairs={{16,24},{20,28},{17,25},{21,29},{18,26},{22,30},{19,27},{23,31}} | collective-permute-start | bytes 3145736 | tf_op jit(solution)/shard_map/ppermute | solution.py:391
  91.4 36.3 %collective-permute-start.24 = (bf16[1024,512]{1,0:T(8,128)(2,1)S(1)}, bf16[1024,512]{1,0:T(8,128)(2,1)S(1)}, u32[]{:S(2)}, u32[]{:S(2)}) collective-permute-start(bf16[1024,512]{1,0:T(8,128)(2,1)S(1)} %copy-done.1), channel_id=1, source_target_pairs={{16,8},{20,12},{17,9},{21,13},{18,10},{22,14},{19,11},{23,15}} | collective-permute-start | bytes 3145736 | tf_op jit(solution)/shard_map/ppermute | solution.py:391
  99.9 13.6 %collective-permute-start.13 = (bf16[1072,256]{1,0:T(8,128)(2,1)S(1)}, bf16[1072,256]{1,0:T(8,128)(2,1)S(1)}, u32[]{:S(2)}, u32[]{:S(2)}) collective-permute-start(bf16[1072,256]{1,0:T(8,128)(2,1)S(1)} %get-tuple-element.33), channel_id=1, source_target_pairs={{8,24},{12,28},{9,25},{13,29},{10,26},{14,30},{11,27},{15,31}} | collective-permute-start | bytes 1646600 | tf_op jit(solution)/shard_map/ppermute | solution.py:391
  113.5 34.8 %collective-permute-start.14 = (bf16[1072,256]{1,0:T(8,128)(2,1)S(1)}, bf16[1072,256]{1,0:T(8,128)(2,1)S(1)}, u32[]{:S(2)}, u32[]{:S(2)}) collective-permute-start(bf16[1072,256]{1,0:T(8,128)(2,1)S(1)} %get-tuple-element.31), channel_id=1, source_target_pairs={{8,16},{12,20},{16,24},{20,28},{9,17},{13,21},{17,25},{21,29},{10,... | collective-permute-start | bytes 1646600 | tf_op jit(solution)/shard_map/ppermute | solution.py:391
  116.6 17.1 %collective-permute-start.15 = (bf16[1072,256]{1,0:T(8,128)(2,1)S(1)}, bf16[1072,256]{1,0:T(8,128)(2,1)S(1)}, u32[]{:S(2)}, u32[]{:S(2)}) collective-permute-start(bf16[1072,256]{1,0:T(8,128)(2,1)S(1)} %get-tuple-element.34), channel_id=1, source_target_pairs={{8,24},{12,28},{9,25},{13,29},{10,26},{14,30},{11,27},{15,31}} | collective-permute-start | bytes 1646600 | tf_op jit(solution)/shard_map/ppermute | solution.py:391
  119.7 32.5 %collective-permute-start.16 = (bf16[2,512,256]{2,1,0:T(8,128)(2,1)S(1)}, bf16[2,512,256]{2,1,0:T(8,128)(2,1)S(1)}, u32[]{:S(2)}, u32[]{:S(2)}) collective-permute-start(bf16[2,512,256]{2,1,0:T(8,128)(2,1)S(1)} %merge.2), channel_id=1, source_target_pairs={{0,4},{4,0},{8,12},{12,8},{16,20},{20,16},{24,28},{28,24},{1,5},{5... | collective-permute-start | bytes 1572872 | tf_op jit(solution)/shard_map/ppermute | solution.py:391
  126.4 40.6 %collective-permute-start.26 = (bf16[1024,512]{1,0:T(8,128)(2,1)S(1)}, bf16[1024,512]{1,0:T(8,128)(2,1)S(1)}, u32[]{:S(2)}, u32[]{:S(2)}) collective-permute-start(bf16[1024,512]{1,0:T(8,128)(2,1)S(1)} %collective-permute-done.20), channel_id=1, source_target_pairs={{8,16},{12,20},{9,17},{13,21},{10,18},{14,22},{11,19},{15,23}} | collective-permute-start | bytes 3145736 | tf_op jit(solution)/shard_map/ppermute | solution.py:391
  129.0 38.0 %collective-permute-start.25 = (bf16[1024,512]{1,0:T(8,128)(2,1)S(1)}, bf16[1024,512]{1,0:T(8,128)(2,1)S(1)}, u32[]{:S(2)}, u32[]{:S(2)}) collective-permute-start(bf16[1024,512]{1,0:T(8,128)(2,1)S(1)} %get-tuple-element.57), channel_id=1, source_target_pairs={{8,0},{12,4},{16,8},{20,12},{9,1},{13,5},{17,9},{21,13},{10,2},{14... | collective-permute-start | bytes 3145736 | tf_op jit(solution)/shard_map/ppermute | solution.py:391
  150.7 12.4 %collective-permute-start.17 = (bf16[2,512,256]{2,1,0:T(8,128)(2,1)S(1)}, bf16[2,512,256]{2,1,0:T(8,128)(2,1)S(1)}, u32[]{:S(2)}, u32[]{:S(2)}) collective-permute-start(bf16[2,512,256]{2,1,0:T(8,128)(2,1)S(1)} %merge.3), channel_id=1, source_target_pairs={{0,4},{4,0},{8,12},{12,8},{16,20},{20,16},{24,28},{28,24},{1,5},{5... | collective-permute-start | bytes 1572872 | tf_op jit(solution)/shard_map/ppermute | solution.py:391
  166.9 7.9 %collective-permute-start.21 = (bf16[2,2,2,128,512]{4,3,2,1,0:T(8,128)(2,1)S(1)}, bf16[2,2,2,128,512]{4,3,2,1,0:T(8,128)(2,1)}, u32[]{:S(2)}, u32[]{:S(2)}) collective-permute-start(bf16[2,2,2,128,512]{4,3,2,1,0:T(8,128)(2,1)S(1)} %get-tuple-element.37), channel_id=1, source_target_pairs={{0,1},{1,0},{2,3},{3,2},{4,5},{5,4},{6,7},{7,6},{8,9},{9,8},{10,11... | collective-permute-start | bytes 3145736 | tf_op jit(solution)/shard_map/ppermute | solution.py:397
  169.3 27.9 %collective-permute-start.27 = (bf16[1024,512]{1,0:T(8,128)(2,1)}, bf16[1024,512]{1,0:T(8,128)(2,1)}, u32[]{:S(2)}, u32[]{:S(2)}) collective-permute-start(bf16[1024,512]{1,0:T(8,128)(2,1)} %broadcast_select_fusion), channel_id=1, source_target_pairs={{8,0},{12,4},{16,24},{20,28},{9,1},{13,5},{17,25},{21,29},{10,2},{... | collective-permute-start | bytes 3145736 | tf_op jit(solution)/shard_map/ppermute | solution.py:391
  203.4 2.9 %collective-permute-start.28 = (bf16[2,2,2,128,512]{4,3,2,1,0:T(8,128)(2,1)S(1)}, bf16[2,2,2,128,512]{4,3,2,1,0:T(8,128)(2,1)}, u32[]{:S(2)}, u32[]{:S(2)}) collective-permute-start(bf16[2,2,2,128,512]{4,3,2,1,0:T(8,128)(2,1)S(1)} %get-tuple-element.42), channel_id=1, source_target_pairs={{0,1},{1,0},{2,3},{3,2},{4,5},{5,4},{6,7},{7,6},{8,9},{9,8},{10,11... | collective-permute-start | bytes 3145736 | tf_op jit(solution)/shard_map/ppermute | solution.py:397
  204.3 15.0 %collective-permute-start.22 = (bf16[2,2,128,512]{3,2,1,0:T(8,128)(2,1)}, bf16[2,2,128,512]{3,2,1,0:T(8,128)(2,1)}, u32[]{:S(2)}, u32[]{:S(2)}) collective-permute-start(bf16[2,2,128,512]{3,2,1,0:T(8,128)(2,1)} %dynamic-slice_bitcast_fusion.1), channel_id=1, source_target_pairs={{0,2},{1,3},{2,0},{3,1},{4,6},{5,7},{6,4},{7,5},{8,10},{9,11},{10,... | collective-permute-start | bytes 1572872 | tf_op jit(solution)/shard_map/ppermute | solution.py:397
  207.8 22.2 %collective-permute-start.29 = (bf16[2,2,128,512]{3,2,1,0:T(8,128)(2,1)S(1)}, bf16[2,2,128,512]{3,2,1,0:T(8,128)(2,1)S(1)}, u32[]{:S(2)}, u32[]{:S(2)}) collective-permute-start(bf16[2,2,128,512]{3,2,1,0:T(8,128)(2,1)S(1)} %dynamic-slice_bitcast_fusion), channel_id=1, source_target_pairs={{0,2},{1,3},{2,0},{3,1},{4,6},{5,7},{6,4},{7,5},{8,10},{9,11},{10,... | collective-permute-start | bytes 1572872 | tf_op jit(solution)/shard_map/ppermute | solution.py:397
  221.3 15.6 %collective-permute-start.23 = (bf16[2,128,512]{2,1,0:T(8,128)(2,1)S(1)}, bf16[2,128,512]{2,1,0:T(8,128)(2,1)S(1)}, u32[]{:S(2)}, u32[]{:S(2)}) collective-permute-start(bf16[2,128,512]{2,1,0:T(8,128)(2,1)S(1)} %get-tuple-element.61), channel_id=1, source_target_pairs={{0,4},{4,0},{8,12},{12,8},{16,20},{20,16},{24,28},{28,24},{1,5},{5... | collective-permute-start | bytes 786440 | tf_op jit(solution)/shard_map/ppermute | solution.py:391
  231.0 7.9 %collective-permute-start.30 = (bf16[2,128,512]{2,1,0:T(8,128)(2,1)S(1)}, bf16[2,128,512]{2,1,0:T(8,128)(2,1)S(1)}, u32[]{:S(2)}, u32[]{:S(2)}) collective-permute-start(bf16[2,128,512]{2,1,0:T(8,128)(2,1)S(1)} %get-tuple-element.59), channel_id=1, source_target_pairs={{0,4},{4,0},{8,12},{12,8},{16,20},{20,16},{24,28},{28,24},{1,5},{5... | collective-permute-start | bytes 786440 | tf_op jit(solution)/shard_map/ppermute | solution.py:391
  (20 other events, 364.2 us)

commit v3 on v2

--- a/solution.py
+++ b/solution.py
@@ -306,10 +306,11 @@
 def project_kernel(chunks, at, *refs):
     x, core = at[0], at[2]
     near, far = refs[:chunks], refs[chunks : 2 * chunks]
-    weights, send, keep = refs[2 * chunks : -2], refs[-2], refs[-1]
-    width = near[0].shape[-1]
-    tokens = near[0].shape[3]
+    weight, send, keep = refs[2 * chunks :]
+    tokens, width = near[0].shape[3:]
     half = width * chunks
+    top = weight[0, pl.ds(pl.multiple_of(x * half, half), half)]
+    bottom = weight[0, pl.ds(pl.multiple_of((1 - x) * half, half), half)]
     for who, out in ((1 - core, send), (core, keep)):
 
         def rows(ref):
@@ -317,55 +318,67 @@
 
         left = jnp.concatenate([rows(ref) for ref in near], axis=1)
         right = jnp.concatenate([rows(ref) for ref in far], axis=1)
-        for s, w in enumerate(weights):
-            c = jnp.dot(left, w[pl.ds(pl.multiple_of(x * half, half), half)], preferred_element_type=F32)
-            c = c + jnp.dot(right, w[pl.ds(pl.multiple_of((1 - x) * half, half), half)], preferred_element_type=F32)
-            out[s] = c.astype(BF16).reshape(2, 2, tokens, w.shape[1])
-
-
-def project(at, near, far, weights):
+        c = jnp.dot(left, top, preferred_element_type=F32) + jnp.dot(right, bottom, preferred_element_type=F32)
+        out[0] = c.astype(BF16).reshape(2, 2, tokens, weight.shape[2])
+
+
+def project(at, near, far, weight, start, count):
     _, cols, width = near[0].shape
     shape = (2, 2, 2, cols // 4, width)
-    outs = [jax.ShapeDtypeStruct((len(weights), 2, 2, cols // 4, weights[0].shape[1]), BF16)] * 2
-    args = [a.reshape(shape) for a in near + far] + weights
+    args = [a.reshape(shape) for a in near + far]
+    _, depth, out_width = weight.shape
+    out = jax.ShapeDtypeStruct((count, 2, 2, cols // 4, out_width), BF16)
+    out_spec = pl.BlockSpec((1,) + out.shape[1:], lambda s, at: (s, 0, 0, 0, 0))
     return pl.pallas_call(
         functools.partial(project_kernel, len(near)),
+        out_shape=[out, out],
+        grid_spec=pltpu.PrefetchScalarGridSpec(
+            num_scalar_prefetch=1,
+            grid=(count,),
+            in_specs=[pl.BlockSpec(shape, lambda s, at: (0,) * 5)] * len(args)
+            + [pl.BlockSpec((1, depth, out_width), lambda s, at: (start + s, 0, 0))],
+            out_specs=[out_spec, out_spec],
+        ),
+        compiler_params=pltpu.CompilerParams(vmem_limit_bytes=VMEM),
+        cost_estimate=cost(2 * count),
+        name="project",
+    )(at, *args, weight)
+
+
+def whole_call(kernel, at, args, outs, name, us):
+    return pl.pallas_call(
+        kernel,
         out_shape=outs,
         in_specs=[pl.BlockSpec(memory_space=pltpu.SMEM)] + [pl.BlockSpec(memory_space=pltpu.VMEM)] * len(args),
-        out_specs=[pl.BlockSpec(memory_space=pltpu.VMEM)] * 2,
+        out_specs=[pl.BlockSpec(memory_space=pltpu.VMEM)] * len(outs),
         compiler_params=pltpu.CompilerParams(vmem_limit_bytes=VMEM),
-        cost_estimate=cost(4),
-        name="project",
+        cost_estimate=cost(us),
+        name=name,
     )(at, *args)
 
 
-def place_kernel(at, layer, *refs):
+def total(a, b):
+    return (a.astype(F32) + b.astype(F32)).astype(BF16)
+
+
+def split_kernel(at, kept, got, stay, to_y, to_x, to_xy):
+    x, y = at[0], at[3]
+    for s in range(kept.shape[0]):
+        for out, yy, xx in ((to_xy, 1 - y, 1 - x), (to_y, 1 - y, x), (to_x, y, 1 - x), (stay, y, x)):
+            out[s] = total(kept[s, yy, xx], got[s, yy, xx])
+
+
+def place_kernel(at, *refs):
     x, out = at[0], refs[-1]
-    slot = 0
-    for mine, theirs in zip(refs[:-1:2], refs[1:-1:2]):
-        width = mine.shape[-1]
-        for s in range(mine.shape[0]):
-            base = layer[slot] * 2
-            out[:, pl.ds(pl.multiple_of((base + x) * width, width), width)] = mine[s]
-            out[:, pl.ds(pl.multiple_of((base + 1 - x) * width, width), width)] = theirs[s]
-            slot += 1
-
-
-def place(at, layer, parts):
-    _, tokens, width = parts[0].shape
-    total = sum(p.shape[0] for p in parts)
-    return pl.pallas_call(
-        place_kernel,
-        out_shape=jax.ShapeDtypeStruct((tokens, total * width), BF16),
-        in_specs=[pl.BlockSpec(memory_space=pltpu.SMEM)] * 2 + [pl.BlockSpec(memory_space=pltpu.VMEM)] * len(parts),
-        out_specs=pl.BlockSpec(memory_space=pltpu.VMEM),
-        cost_estimate=cost(2),
-        name="place",
-    )(at, layer, *parts)
-
-
-def added(a, b):
-    return (a.astype(F32) + b.astype(F32)).astype(BF16)
+    layer = 0
+    for stay, from_y, from_x, from_xy in zip(*(refs[i:-1:4] for i in range(4))):
+        width = stay.shape[-1]
+        for s in range(stay.shape[0]):
+            mine = pl.ds(pl.multiple_of((2 * layer + x) * width, width), width)
+            theirs = pl.ds(pl.multiple_of((2 * layer + 1 - x) * width, width), width)
+            out[:, mine] = total(stay[s], from_y[s])
+            out[:, theirs] = total(from_x[s], from_xy[s])
+            layer += 1
 
 
 def after(value, *earlier):
@@ -382,7 +395,7 @@
     me = lax.axis_index("seq")
     who = lax.axis_index("head")
     z, x, core, y = me // 2, me % 2, who % 2, who // 2
-    at = jnp.stack([x, z, core]).astype(jnp.int32)
+    at = jnp.stack([x, z, core, y]).astype(jnp.int32)
     local = qkv.reshape(3, cols, features)
     first = x == 0
 
@@ -403,21 +416,17 @@
         return lax.dynamic_slice(array, (lo, 0, (1 - x) * half + c * width), (hi - lo, cols, width))
 
     q, kv, low, qa, qb = [], [], [], [], []
-    w_first = seq_perm(out_weight, (1, 2), (2, 3))
     for c in range(chunks):
-        if c == 0:
-            for_q = for_low = local
-        else:
-            for_q = after(local, kv[0][1])
-            for_low = after(local, low[0])
-        mine, other = keep(for_q, 0, 1, c), swap(give(for_q, 0, 1, c))
+        source = local if c == 0 else after(local, kv[0][1])
+        mine, other = keep(source, 0, 1, c), swap(give(source, 0, 1, c))
         q.append(jnp.concatenate([jnp.where(first, mine, other), jnp.where(first, other, mine)]))
-        low.append((seq_perm(keep(for_low, 1, 3, c), (0, 1)), seq_perm(give(for_low, 1, 3, c), (0, 1), cross=True)))
-        for_kv = after(local, other) if c == 0 else for_q
-        kv.append((keep(for_kv, 1, 3, c), swap(give(for_kv, 1, 3, c))))
         going = q[c] if c == 0 else after(q[c], qa[0], qb[0])
         qa.append(seq_perm(going, (2, 1), (3, 2)))
         qb.append(seq_perm(going, (3, 1)))
+        kv.append((keep(source, 1, 3, c), swap(give(source, 1, 3, c))))
+        low.append(tuple(seq_perm(half_kv, (0, 1)) for half_kv in kv[c]))
+    layers = [[2 * i + j for i in range(4)] for j in range(2)]
+    weight = lax.all_gather(out_weight, "seq", axis_index_groups=layers)
 
     struct = jax.ShapeDtypeStruct
     partial = struct((2 * cols + lse_height(cols), width), BF16)
@@ -435,22 +444,6 @@
             heads, "own_rows", 4)
         own.append(mine)
 
-    w_second = seq_perm(after(out_weight, low[1]), (0, 1), (1, 0), (3, 2))
-    w_third = seq_perm(after(out_weight, qa[1], qb[1]), (2, 1))
-    w_fourth = seq_perm(w_first, (2, 3))
-    w_fifth = seq_perm(jnp.where(z == 1, w_third, w_second), (1, 0), (2, 1))
-    w_sixth = seq_perm(w_second, (1, 2))
-    w_last = seq_perm(jnp.where(z == 1, w_fifth, w_sixth), (1, 0), (2, 3))
-    slot_a = jnp.where(z == 3, w_fourth, w_second)
-    slot_b = jnp.where(z == 0, w_fifth, jnp.where(z == 1, w_third, w_first))
-    slot_c = jnp.where(z == 1, w_fifth, jnp.where(z == 2, w_sixth, w_last))
-    layer = jnp.stack([
-        z,
-        jnp.array([1, 0, 3, 1], jnp.int32)[z],
-        jnp.array([2, 2, 1, 2], jnp.int32)[z],
-        jnp.array([3, 3, 0, 0], jnp.int32)[z],
-    ]).astype(jnp.int32)
-
     near, far = [], []
     for c in range(chunks):
         (a,) = head_call(
@@ -459,20 +452,19 @@
         near.append(a)
         far.append(swap(a))
 
+    count = 2
     parts = []
-    previous = None
-    for weights in ([out_weight, slot_a], [slot_b, slot_c]):
-        if previous is not None:
-            weights = [after(w, previous) for w in weights]
-        send, kept = project(at, near, far, weights)
-        part = added(kept, head_perm(send, 1))
-        previous = part
-        to_y = lax.dynamic_index_in_dim(part, 1 - y, 1, keepdims=False)
-        stay = lax.dynamic_index_in_dim(part, y, 1, keepdims=False)
-        done = added(stay, head_perm(to_y, 2))
-        theirs = swap(lax.dynamic_index_in_dim(done, 1 - x, 1, keepdims=False))
-        parts += [lax.dynamic_index_in_dim(done, x, 1, keepdims=False), theirs]
-    return place(at, layer, parts).reshape(cols // 4, 1, 8 * out_weight.shape[1])
+    for start in range(0, 4, count):
+        send, kept = project(at, near, far, weight, start, count)
+        got = head_perm(send, 1)
+        piece = struct((count,) + send.shape[3:], BF16)
+        stay, to_y, to_x, to_xy = whole_call(split_kernel, at, [kept, got], [piece] * 4, "split", 2)
+        diagonal = [((2 * i + j) * 4 + h, (2 * i + 1 - j) * 4 + (h ^ 2)) for i in range(4) for j in range(2) for h in range(4)]
+        from_xy = lax.ppermute(to_xy, ("seq", "head"), diagonal)
+        parts += [stay, head_perm(to_y, 2), swap(to_x), from_xy]
+    (out,) = whole_call(
+        place_kernel, at, parts, [struct((cols // 4, 8 * out_weight.shape[1]), BF16)], "place", 2)
+    return out.reshape(cols // 4, 1, 8 * out_weight.shape[1])
 
 
 def solution(mesh):

time: 244 us -> 224 us (0.918)
  the two profiles are of different devices: /device:TPU:16 before, /device:TPU:28 now
where the time goes in v3:
time: 224 us; the launch traced here: 223 us
  waiting for transfers between devices  130 us (58%)
  Pallas kernels  40.8 us (18%)
  starting transfers between devices  30.4 us (14%)
  between operations  13.7 us (6%)
  local copies, waits for them, and re-layouts  5.29 us (2%)
  other arithmetic  2.29 us (1%)
    ppermute x20, waiting for transfers between devices, seq_perm(): return lax.ppermute(array, 'seq', pairs)  110 us
    pallas_call x6, Pallas kernels, head_call(): pl.pallas_call(kernel, out_shape=outs, grid_spec=pltpu.PrefetchScalarGrid...  28.9 us
    ppermute x20, starting transfers between devices, seq_perm(): return lax.ppermute(array, 'seq', pairs)  26.2 us
    ppermute x2, waiting for transfers between devices, body_eight(): from_xy = lax.ppermute(to_xy, ('seq', 'head'), diagonal)  11.8 us
    pallas_call x2, Pallas kernels, project(): pl.pallas_call(functools.partial(project_kernel, len(near)), out_shape=[o...  8.61 us
    ppermute x4, waiting for transfers between devices, head_perm(): return lax.ppermute(array, 'head', [(i, i ^ flip) for i in range(4)])  8.41 us
    dynamic_slice x4, local copies, waits for them, and re-layouts, give(): lax.dynamic_slice(array, (lo, 0, (1 - x) * half + c * width), (hi - lo, c...  5.29 us
  transfers between devices with their start and end apart: 27, of which 13 were waited for; matrix products, arithmetic and copies ran while one was open for 3% of the time, Pallas kernels for 16%

profile of v3, /device:TPU:28, one launch (start us, length us, event | category | flops | bytes accessed | tf_op | source)
XLA Modules:
  0.0 223.0 jit_solution(11879857761481147365)
XLA Ops:
  8.6 1.6 collective-permute-start.3
  12.4 15.5 %collective-permute-done = bf16[1,512,256]{2,1,0:T(8,128)(2,1)S(1)} collective-permute-done((bf16[1,512,256]{2,1,0:T(8,128)(2,1)S(1)}, bf16[1,512,256]{2,1,0:T(8,128)(2,1)S(1)}, u32[]{:S(2)}, u32[]{:S(2)}) %collective-permute-start) | collective-permute-done | bytes 262176 | tf_op jit(solution)/shard_map/ppermute | solution.py:404
  30.0 1.6 collective-permute-start.6
  31.6 3.2 %collective-permute-start.1 = (bf16[2,512,256]{2,1,0:T(8,128)(2,1)S(1)}, bf16[2,512,256]{2,1,0:T(8,128)(2,1)}, u32[]{:S(2)}, u32[]{:S(2)}) collective-permute-start(bf16[2,512,256]{2,1,0:T(8,128)(2,1)S(1)} %pad_maximum_fusion.q), channel_id=1, source_target_pairs={{16,8},{20,12},{24,16},{28,20},{17,9},{21,13},{25,17},{29,21},{18,... | collective-permute-start | bytes 1572872 | tf_op jit(solution)/shard_map/ppermute | solution.py:404
  34.7 2.1 collective-permute-start.2
  36.8 2.1 constant_dynamic-slice_fusion
  39.5 1.5 collective-permute-start.5
  42.1 15.3 %collective-permute-done.1.qa = bf16[2,512,256]{2,1,0:T(8,128)(2,1)} collective-permute-done((bf16[2,512,256]{2,1,0:T(8,128)(2,1)S(1)}, bf16[2,512,256]{2,1,0:T(8,128)(2,1)}, u32[]{:S(2)}, u32[]{:S(2)}) %collective-permute-start.1) | collective-permute-done | bytes 524320 | tf_op jit(solution)/shard_map/ppermute | solution.py:404
  58.1 21.2 %collective-permute-done.2.qb = bf16[2,512,256]{2,1,0:T(8,128)(2,1)} collective-permute-done((bf16[2,512,256]{2,1,0:T(8,128)(2,1)S(1)}, bf16[2,512,256]{2,1,0:T(8,128)(2,1)}, u32[]{:S(2)}, u32[]{:S(2)}) %collective-permute-start.2) | collective-permute-done | bytes 524320 | tf_op jit(solution)/shard_map/ppermute | solution.py:404
  79.3 2.2 %collective-permute-start.7 = (bf16[2,512,256]{2,1,0:T(8,128)(2,1)S(1)}, bf16[2,512,256]{2,1,0:T(8,128)(2,1)S(1)}, u32[]{:S(2)}, u32[]{:S(2)}) collective-permute-start(bf16[2,512,256]{2,1,0:T(8,128)(2,1)S(1)} %pad_maximum_fusion.1.q), channel_id=1, source_target_pairs={{16,8},{20,12},{24,16},{28,20},{17,9},{21,13},{25,17},{29,21},{18,... | collective-permute-start | bytes 1572872 | tf_op jit(solution)/shard_map/ppermute | solution.py:404
  81.6 4.8 %collective-permute-start.8 = (bf16[2,512,256]{2,1,0:T(8,128)(2,1)S(1)}, bf16[2,512,256]{2,1,0:T(8,128)(2,1)S(1)}, u32[]{:S(2)}, u32[]{:S(2)}) collective-permute-start(bf16[2,512,256]{2,1,0:T(8,128)(2,1)S(1)} %pad_maximum_fusion.1.q), channel_id=1, source_target_pairs={{24,8},{28,12},{25,9},{29,13},{26,10},{30,14},{27,11},{31,15}} | collective-permute-start | bytes 1572872 | tf_op jit(solution)/shard_map/ppermute | solution.py:404
  87.1 6.6 %upper_rows.2 = (bf16[1072,256]{1,0:T(8,128)(2,1)S(1)}, bf16[1072,256]{1,0:T(8,128)(2,1)S(1)}) custom-call(s32[4]{0:T(128)S(1)} %pad_add_fusion.at, bf16[2,512,256]{2,1,0:T(8,128)(2,1)} %collective-permute-done.1.qa, bf16[2,512,256]{2,1,0:T(8,128)(2,1)} %collective-permute-done.2.qb, bf16[2,512,256]{2,1,0:T(8,128)(2,1)S(1)} %get-tuple-element.54.kv_m, ...), custom_call_target="tpu_custom_call" | custom-call | flops 4400000000 | bytes 4000000 | tf_op jit(solution)/shard_map/upper_rows/pallas_call | solution.py:291
  95.0 6.0 %own_rows.2.own = bf16[1072,256]{1,0:T(8,128)(2,1)S(1)} custom-call(s32[4]{0:T(128)S(1)} %pad_add_fusion.at, bf16[2,512,256]{2,1,0:T(8,128)(2,1)S(1)} %pad_maximum_fusion.q, bf16[2,512,256]{2,1,0:T(8,128)(2,1)S(1)} %get-tuple-element.54.kv_m, bf16[2,512,256]{2,1,0:T(8,128)(2,1)S(1)} %collective-permute-done.3.kv_o, ...), custom_call_target="tpu_custom_call" | custom-call | flops 4400000000 | bytes 4000000 | tf_op jit(solution)/shard_map/own_rows/pallas_call | solution.py:291
  102.4 2.6 %collective-permute-done.7.qa = bf16[2,512,256]{2,1,0:T(8,128)(2,1)S(1)} collective-permute-done((bf16[2,512,256]{2,1,0:T(8,128)(2,1)S(1)}, bf16[2,512,256]{2,1,0:T(8,128)(2,1)S(1)}, u32[]{:S(2)}, u32[]{:S(2)}) %collective-permute-start.7) | collective-permute-done | bytes 524320 | tf_op jit(solution)/shard_map/ppermute | solution.py:404
  105.0 21.3 %collective-permute-done.8.qb = bf16[2,512,256]{2,1,0:T(8,128)(2,1)S(1)} collective-permute-done((bf16[2,512,256]{2,1,0:T(8,128)(2,1)S(1)}, bf16[2,512,256]{2,1,0:T(8,128)(2,1)S(1)}, u32[]{:S(2)}, u32[]{:S(2)}) %collective-permute-start.8) | collective-permute-done | bytes 524320 | tf_op jit(solution)/shard_map/ppermute | solution.py:404
  126.3 6.1 %upper_rows.3 = (bf16[1072,256]{1,0:T(8,128)(2,1)S(1)}, bf16[1072,256]{1,0:T(8,128)(2,1)S(1)}) custom-call(s32[4]{0:T(128)S(1)} %pad_add_fusion.at, bf16[2,512,256]{2,1,0:T(8,128)(2,1)S(1)} %collective-permute-done.7.qa, bf16[2,512,256]{2,1,0:T(8,128)(2,1)S(1)} %collective-permute-done.8.qb, bf16[2,512,256]{2,1,0:T(8,128)(2,1)S(1)} %get-tuple-element.52.kv_m, ...), custom_call_target="tpu_custom_call" | custom-call | flops 4400000000 | bytes 4000000 | tf_op jit(solution)/shard_map/upper_rows/pallas_call | solution.py:291
  132.3 1.3 collective-permute-start.14
  133.6 1.5 collective-permute-start.15
  135.1 5.4 %own_rows.3.own = bf16[1072,256]{1,0:T(8,128)(2,1)S(1)} custom-call(s32[4]{0:T(128)S(1)} %pad_add_fusion.at, bf16[2,512,256]{2,1,0:T(8,128)(2,1)S(1)} %pad_maximum_fusion.1.q, bf16[2,512,256]{2,1,0:T(8,128)(2,1)S(1)} %get-tuple-element.52.kv_m, bf16[2,512,256]{2,1,0:T(8,128)(2,1)S(1)} %collective-permute-done.9.kv_o, ...), custom_call_target="tpu_custom_call" | custom-call | flops 4400000000 | bytes 4000000 | tf_op jit(solution)/shard_map/own_rows/pallas_call | solution.py:291
  140.5 2.4 %merge.2 = bf16[2,512,256]{2,1,0:T(8,128)(2,1)S(1)} custom-call(s32[4]{0:T(128)S(1)} %pad_add_fusion.at, bf16[1072,256]{1,0:T(8,128)(2,1)S(1)} %own_rows.2.own, bf16[1072,256]{1,0:T(8,128)(2,1)S(1)} %collective-permute-done.12.oa, bf16[1072,256]{1,0:T(8,128)(2,1)S(1)} %collective-permute-done.13.ob), custom_call_target="tpu_custom_call" | custom-call | flops 2200000000 | bytes 2000000 | tf_op jit(solution)/shard_map/merge/pallas_call | solution.py:291
  143.0 4.4 %collective-permute-done.14.oa = bf16[1072,256]{1,0:T(8,128)(2,1)S(1)} collective-permute-done((bf16[1072,256]{1,0:T(8,128)(2,1)S(1)}, bf16[1072,256]{1,0:T(8,128)(2,1)S(1)}, u32[]{:S(2)}, u32[]{:S(2)}) %collective-permute-start.14) | collective-permute-done | bytes 548896 | tf_op jit(solution)/shard_map/ppermute | solution.py:404
  147.4 16.6 %collective-permute-done.15.ob = bf16[1072,256]{1,0:T(8,128)(2,1)S(1)} collective-permute-done((bf16[1072,256]{1,0:T(8,128)(2,1)S(1)}, bf16[1072,256]{1,0:T(8,128)(2,1)S(1)}, u32[]{:S(2)}, u32[]{:S(2)}) %collective-permute-start.15) | collective-permute-done | bytes 548896 | tf_op jit(solution)/shard_map/ppermute | solution.py:404
  164.0 2.4 %merge.3 = bf16[2,512,256]{2,1,0:T(8,128)(2,1)S(1)} custom-call(s32[4]{0:T(128)S(1)} %pad_add_fusion.at, bf16[1072,256]{1,0:T(8,128)(2,1)S(1)} %own_rows.3.own, bf16[1072,256]{1,0:T(8,128)(2,1)S(1)} %collective-permute-done.14.oa, bf16[1072,256]{1,0:T(8,128)(2,1)S(1)} %collective-permute-done.15.ob), custom_call_target="tpu_custom_call" | custom-call | flops 2200000000 | bytes 2000000 | tf_op jit(solution)/shard_map/merge/pallas_call | solution.py:291
  166.5 11.4 %collective-permute-done.17 = bf16[2,512,256]{2,1,0:T(8,128)(2,1)S(1)} collective-permute-done((bf16[2,512,256]{2,1,0:T(8,128)(2,1)S(1)}, bf16[2,512,256]{2,1,0:T(8,128)(2,1)S(1)}, u32[]{:S(2)}, u32[]{:S(2)}) %collective-permute-start.17) | collective-permute-done | bytes 524320 | tf_op jit(solution)/shard_map/ppermute | solution.py:404
  177.9 4.3 %project.2 = (bf16[2,2,2,128,512]{4,3,2,1,0:T(8,128)(2,1)S(1)}, bf16[2,2,2,128,512]{4,3,2,1,0:T(8,128)(2,1)S(1)}) custom-call(s32[4]{0:T(128)S(1)} %pad_add_fusion.at, bf16[2,2,2,128,256]{4,3,2,1,0:T(8,128)(2,1)S(1)} %bitcast.20, bf16[2,2,2,128,256]{4,3,2,1,0:T(8,128)(2,1)S(1)} %bitcast.24, bf16[2,2,2,128,256]{4,3,2,1,0:T(8,128)(2,1)S(1)} %bitcast.22, ...), custom_call_target="tpu_custom_call" | custom-call | flops 4400000000 | bytes 4000000 | tf_op jit(solution)/shard_map/project/pallas_call | solution.py:332
  182.3 4.3 %project.3 = (bf16[2,2,2,128,512]{4,3,2,1,0:T(8,128)(2,1)S(1)}, bf16[2,2,2,128,512]{4,3,2,1,0:T(8,128)(2,1)S(1)}) custom-call(s32[4]{0:T(128)S(1)} %pad_add_fusion.at, bf16[2,2,2,128,256]{4,3,2,1,0:T(8,128)(2,1)S(1)} %bitcast.21, bf16[2,2,2,128,256]{4,3,2,1,0:T(8,128)(2,1)S(1)} %bitcast.25, bf16[2,2,2,128,256]{4,3,2,1,0:T(8,128)(2,1)S(1)} %bitcast.23, ...), custom_call_target="tpu_custom_call" | custom-call | flops 4400000000 | bytes 4000000 | tf_op jit(solution)/shard_map/project/pallas_call | solution.py:332
  188.5 3.0 %collective-permute-start.21 = (bf16[2,128,512]{2,1,0:T(8,128)(2,1)S(1)}, bf16[2,128,512]{2,1,0:T(8,128)(2,1)S(1)}, u32[]{:S(2)}, u32[]{:S(2)}) collective-permute-start(bf16[2,128,512]{2,1,0:T(8,128)(2,1)S(1)} %get-tuple-element.40), channel_id=1, source_target_pairs={{0,6},{1,7},{2,4},{3,5},{4,2},{5,3},{6,0},{7,1},{8,14},{9,15},{10,... | collective-permute-start | bytes 786440 | tf_op jit(solution)/shard_map/ppermute | solution.py:463
  193.0 5.2 %collective-permute-done.19.refs_1_ = bf16[2,128,512]{2,1,0:T(8,128)(2,1)S(1)} collective-permute-done((bf16[2,128,512]{2,1,0:T(8,128)(2,1)S(1)}, bf16[2,128,512]{2,1,0:T(8,128)(2,1)S(1)}, u32[]{:S(2)}, u32[]{:S(2)}) %collective-permute-start.19) | collective-permute-done | bytes 262176 | tf_op jit(solution)/shard_map/ppermute | solution.py:410
  198.2 6.2 %collective-permute-done.21.refs_3_ = bf16[2,128,512]{2,1,0:T(8,128)(2,1)S(1)} collective-permute-done((bf16[2,128,512]{2,1,0:T(8,128)(2,1)S(1)}, bf16[2,128,512]{2,1,0:T(8,128)(2,1)S(1)}, u32[]{:S(2)}, u32[]{:S(2)}) %collective-permute-start.21) | collective-permute-done | bytes 262176 | tf_op jit(solution)/shard_map/ppermute | solution.py:463
  204.4 3.2 %collective-permute-done.23.refs_5_ = bf16[2,128,512]{2,1,0:T(8,128)(2,1)S(1)} collective-permute-done((bf16[2,128,512]{2,1,0:T(8,128)(2,1)S(1)}, bf16[2,128,512]{2,1,0:T(8,128)(2,1)S(1)}, u32[]{:S(2)}, u32[]{:S(2)}) %collective-permute-start.23) | collective-permute-done | bytes 262176 | tf_op jit(solution)/shard_map/ppermute | solution.py:410
  208.7 5.7 %collective-permute-done.25.refs_7_ = bf16[2,128,512]{2,1,0:T(8,128)(2,1)S(1)} collective-permute-done((bf16[2,128,512]{2,1,0:T(8,128)(2,1)S(1)}, bf16[2,128,512]{2,1,0:T(8,128)(2,1)S(1)}, u32[]{:S(2)}, u32[]{:S(2)}) %collective-permute-start.25) | collective-permute-done | bytes 262176 | tf_op jit(solution)/shard_map/ppermute | solution.py:463
  214.4 1.7 place.1
  (43 shorter events, 16.8 us)
Async XLA Ops:
  6.5 171.4 %all-gather.3.cloned.1.call-start = ((), (), s32[]{:S(2)}) async-start(), calls=%async_computation | async-start | bytes 5242880 | tf_op jit(solution)/shard_map/all_gather | solution.py:429
  8.6 20.4 %collective-permute-start.3 = (bf16[2,512,256]{2,1,0:T(8,128)(2,1)S(1)}, bf16[2,512,256]{2,1,0:T(8,128)(2,1)S(1)}, u32[]{:S(2)}, u32[]{:S(2)}) collective-permute-start(bf16[2,512,256]{2,1,0:T(8,128)(2,1)S(1)} %get-tuple-element.53), channel_id=1, source_target_pairs={{0,4},{4,0},{8,12},{12,8},{16,20},{20,16},{24,28},{28,24},{1,5},{5... | collective-permute-start | bytes 1572872 | tf_op jit(solution)/shard_map/ppermute | solution.py:404
  11.1 16.8 %collective-permute-start = (bf16[1,512,256]{2,1,0:T(8,128)(2,1)S(1)}, bf16[1,512,256]{2,1,0:T(8,128)(2,1)S(1)}, u32[]{:S(2)}, u32[]{:S(2)}) collective-permute-start(bf16[1,512,256]{2,1,0:T(8,128)(2,1)S(1)} %dynamic-slice_bitcast_fusion.2), channel_id=1, source_target_pairs={{0,4},{4,0},{8,12},{12,8},{16,20},{20,16},{24,28},{28,24},{1,5},{5... | collective-permute-start | bytes 786440 | tf_op jit(solution)/shard_map/ppermute | solution.py:404
  11.7 69.9 %collective-permute-start.4 = (bf16[2,512,256]{2,1,0:T(8,128)(2,1)S(1)}, bf16[2,512,256]{2,1,0:T(8,128)(2,1)S(1)}, u32[]{:S(2)}, u32[]{:S(2)}) collective-permute-start(bf16[2,512,256]{2,1,0:T(8,128)(2,1)S(1)} %get-tuple-element.54.kv_m), channel_id=1, source_target_pairs={{0,8},{4,12},{1,9},{5,13},{2,10},{6,14},{3,11},{7,15}} | collective-permute-start | bytes 1572872 | tf_op jit(solution)/shard_map/ppermute | solution.py:404
  30.0 9.5 %collective-permute-start.6 = (bf16[1,512,256]{2,1,0:T(8,128)(2,1)S(1)}, bf16[1,512,256]{2,1,0:T(8,128)(2,1)S(1)}, u32[]{:S(2)}, u32[]{:S(2)}) collective-permute-start(bf16[1,512,256]{2,1,0:T(8,128)(2,1)S(1)} %constant_dynamic-slice_fusion.2), channel_id=1, source_target_pairs={{0,4},{4,0},{8,12},{12,8},{16,20},{20,16},{24,28},{28,24},{1,5},{5... | collective-permute-start | bytes 786440 | tf_op jit(solution)/shard_map/ppermute | solution.py:404
  31.6 25.9 %collective-permute-start.1 = (bf16[2,512,256]{2,1,0:T(8,128)(2,1)S(1)}, bf16[2,512,256]{2,1,0:T(8,128)(2,1)}, u32[]{:S(2)}, u32[]{:S(2)}) collective-permute-start(bf16[2,512,256]{2,1,0:T(8,128)(2,1)S(1)} %pad_maximum_fusion.q), channel_id=1, source_target_pairs={{16,8},{20,12},{24,16},{28,20},{17,9},{21,13},{25,17},{29,21},{18,... | collective-permute-start | bytes 1572872 | tf_op jit(solution)/shard_map/ppermute | solution.py:404
  34.7 44.6 %collective-permute-start.2 = (bf16[2,512,256]{2,1,0:T(8,128)(2,1)S(1)}, bf16[2,512,256]{2,1,0:T(8,128)(2,1)}, u32[]{:S(2)}, u32[]{:S(2)}) collective-permute-start(bf16[2,512,256]{2,1,0:T(8,128)(2,1)S(1)} %pad_maximum_fusion.q), channel_id=1, source_target_pairs={{24,8},{28,12},{25,9},{29,13},{26,10},{30,14},{27,11},{31,15}} | collective-permute-start | bytes 1572872 | tf_op jit(solution)/shard_map/ppermute | solution.py:404
  38.9 47.5 %collective-permute-start.9 = (bf16[2,512,256]{2,1,0:T(8,128)(2,1)}, bf16[2,512,256]{2,1,0:T(8,128)(2,1)S(1)}, u32[]{:S(2)}, u32[]{:S(2)}) collective-permute-start(bf16[2,512,256]{2,1,0:T(8,128)(2,1)} %get-tuple-element.51), channel_id=1, source_target_pairs={{0,4},{4,0},{8,12},{12,8},{16,20},{20,16},{24,28},{28,24},{1,5},{5... | collective-permute-start | bytes 1572872 | tf_op jit(solution)/shard_map/ppermute | solution.py:404
  39.5 47.6 %collective-permute-start.5 = (bf16[2,512,256]{2,1,0:T(8,128)(2,1)S(1)}, bf16[2,512,256]{2,1,0:T(8,128)(2,1)}, u32[]{:S(2)}, u32[]{:S(2)}) collective-permute-start(bf16[2,512,256]{2,1,0:T(8,128)(2,1)S(1)} %collective-permute-done.3.kv_o), channel_id=1, source_target_pairs={{0,8},{4,12},{1,9},{5,13},{2,10},{6,14},{3,11},{7,15}} | collective-permute-start | bytes 1572872 | tf_op jit(solution)/shard_map/ppermute | solution.py:404
  57.4 43.7 %collective-permute-start.10 = (bf16[2,512,256]{2,1,0:T(8,128)(2,1)S(1)}, bf16[2,512,256]{2,1,0:T(8,128)(2,1)S(1)}, u32[]{:S(2)}, u32[]{:S(2)}) collective-permute-start(bf16[2,512,256]{2,1,0:T(8,128)(2,1)S(1)} %get-tuple-element.52.kv_m), channel_id=1, source_target_pairs={{0,8},{4,12},{1,9},{5,13},{2,10},{6,14},{3,11},{7,15}} | collective-permute-start | bytes 1572872 | tf_op jit(solution)/shard_map/ppermute | solution.py:404
  79.3 25.7 %collective-permute-start.7 = (bf16[2,512,256]{2,1,0:T(8,128)(2,1)S(1)}, bf16[2,512,256]{2,1,0:T(8,128)(2,1)S(1)}, u32[]{:S(2)}, u32[]{:S(2)}) collective-permute-start(bf16[2,512,256]{2,1,0:T(8,128)(2,1)S(1)} %pad_maximum_fusion.1.q), channel_id=1, source_target_pairs={{16,8},{20,12},{24,16},{28,20},{17,9},{21,13},{25,17},{29,21},{18,... | collective-permute-start | bytes 1572872 | tf_op jit(solution)/shard_map/ppermute | solution.py:404
  81.6 44.7 %collective-permute-start.8 = (bf16[2,512,256]{2,1,0:T(8,128)(2,1)S(1)}, bf16[2,512,256]{2,1,0:T(8,128)(2,1)S(1)}, u32[]{:S(2)}, u32[]{:S(2)}) collective-permute-start(bf16[2,512,256]{2,1,0:T(8,128)(2,1)S(1)} %pad_maximum_fusion.1.q), channel_id=1, source_target_pairs={{24,8},{28,12},{25,9},{29,13},{26,10},{30,14},{27,11},{31,15}} | collective-permute-start | bytes 1572872 | tf_op jit(solution)/shard_map/ppermute | solution.py:404
  86.4 39.9 %collective-permute-start.11 = (bf16[2,512,256]{2,1,0:T(8,128)(2,1)S(1)}, bf16[2,512,256]{2,1,0:T(8,128)(2,1)S(1)}, u32[]{:S(2)}, u32[]{:S(2)}) collective-permute-start(bf16[2,512,256]{2,1,0:T(8,128)(2,1)S(1)} %collective-permute-done.9.kv_o), channel_id=1, source_target_pairs={{0,8},{4,12},{1,9},{5,13},{2,10},{6,14},{3,11},{7,15}} | collective-permute-start | bytes 1572872 | tf_op jit(solution)/shard_map/ppermute | solution.py:404
  93.7 46.8 %collective-permute-start.12 = (bf16[1072,256]{1,0:T(8,128)(2,1)S(1)}, bf16[1072,256]{1,0:T(8,128)(2,1)S(1)}, u32[]{:S(2)}, u32[]{:S(2)}) collective-permute-start(bf16[1072,256]{1,0:T(8,128)(2,1)S(1)} %get-tuple-element.26), channel_id=1, source_target_pairs={{8,16},{12,20},{16,24},{20,28},{9,17},{13,21},{17,25},{21,29},{10,... | collective-permute-start | bytes 1646600 | tf_op jit(solution)/shard_map/ppermute | solution.py:404
  101.1 39.4 %collective-permute-start.13 = (bf16[1072,256]{1,0:T(8,128)(2,1)S(1)}, bf16[1072,256]{1,0:T(8,128)(2,1)S(1)}, u32[]{:S(2)}, u32[]{:S(2)}) collective-permute-start(bf16[1072,256]{1,0:T(8,128)(2,1)S(1)} %get-tuple-element.33), channel_id=1, source_target_pairs={{8,24},{12,28},{9,25},{13,29},{10,26},{14,30},{11,27},{15,31}} | collective-permute-start | bytes 1646600 | tf_op jit(solution)/shard_map/ppermute | solution.py:404
  132.3 15.0 %collective-permute-start.14 = (bf16[1072,256]{1,0:T(8,128)(2,1)S(1)}, bf16[1072,256]{1,0:T(8,128)(2,1)S(1)}, u32[]{:S(2)}, u32[]{:S(2)}) collective-permute-start(bf16[1072,256]{1,0:T(8,128)(2,1)S(1)} %get-tuple-element.31), channel_id=1, source_target_pairs={{8,16},{12,20},{16,24},{20,28},{9,17},{13,21},{17,25},{21,29},{10,... | collective-permute-start | bytes 1646600 | tf_op jit(solution)/shard_map/ppermute | solution.py:404
  133.6 30.4 %collective-permute-start.15 = (bf16[1072,256]{1,0:T(8,128)(2,1)S(1)}, bf16[1072,256]{1,0:T(8,128)(2,1)S(1)}, u32[]{:S(2)}, u32[]{:S(2)}) collective-permute-start(bf16[1072,256]{1,0:T(8,128)(2,1)S(1)} %get-tuple-element.34), channel_id=1, source_target_pairs={{8,24},{12,28},{9,25},{13,29},{10,26},{14,30},{11,27},{15,31}} | collective-permute-start | bytes 1646600 | tf_op jit(solution)/shard_map/ppermute | solution.py:404
  142.9 23.6 %collective-permute-start.16 = (bf16[2,512,256]{2,1,0:T(8,128)(2,1)S(1)}, bf16[2,512,256]{2,1,0:T(8,128)(2,1)S(1)}, u32[]{:S(2)}, u32[]{:S(2)}) collective-permute-start(bf16[2,512,256]{2,1,0:T(8,128)(2,1)S(1)} %merge.2), channel_id=1, source_target_pairs={{0,4},{4,0},{8,12},{12,8},{16,20},{20,16},{24,28},{28,24},{1,5},{5... | collective-permute-start | bytes 1572872 | tf_op jit(solution)/shard_map/ppermute | solution.py:404
  166.4 11.5 %collective-permute-start.17 = (bf16[2,512,256]{2,1,0:T(8,128)(2,1)S(1)}, bf16[2,512,256]{2,1,0:T(8,128)(2,1)S(1)}, u32[]{:S(2)}, u32[]{:S(2)}) collective-permute-start(bf16[2,512,256]{2,1,0:T(8,128)(2,1)S(1)} %merge.3), channel_id=1, source_target_pairs={{0,4},{4,0},{8,12},{12,8},{16,20},{20,16},{24,28},{28,24},{1,5},{5... | collective-permute-start | bytes 1572872 | tf_op jit(solution)/shard_map/ppermute | solution.py:404
  182.2 5.0 %collective-permute-start.18 = (bf16[2,2,2,128,512]{4,3,2,1,0:T(8,128)(2,1)S(1)}, bf16[2,2,2,128,512]{4,3,2,1,0:T(8,128)(2,1)S(1)}, u32[]{:S(2)}, u32[]{:S(2)}) collective-permute-start(bf16[2,2,2,128,512]{4,3,2,1,0:T(8,128)(2,1)S(1)} %get-tuple-element.36), channel_id=1, source_target_pairs={{0,1},{1,0},{2,3},{3,2},{4,5},{5,4},{6,7},{7,6},{8,9},{9,8},{10,11... | collective-permute-start | bytes 3145736 | tf_op jit(solution)/shard_map/ppermute | solution.py:410
  186.6 4.9 %collective-permute-start.22 = (bf16[2,2,2,128,512]{4,3,2,1,0:T(8,128)(2,1)S(1)}, bf16[2,2,2,128,512]{4,3,2,1,0:T(8,128)(2,1)S(1)}, u32[]{:S(2)}, u32[]{:S(2)}) collective-permute-start(bf16[2,2,2,128,512]{4,3,2,1,0:T(8,128)(2,1)S(1)} %get-tuple-element.42), channel_id=1, source_target_pairs={{0,1},{1,0},{2,3},{3,2},{4,5},{5,4},{6,7},{7,6},{8,9},{9,8},{10,11... | collective-permute-start | bytes 3145736 | tf_op jit(solution)/shard_map/ppermute | solution.py:410
  188.0 10.2 %collective-permute-start.19 = (bf16[2,128,512]{2,1,0:T(8,128)(2,1)S(1)}, bf16[2,128,512]{2,1,0:T(8,128)(2,1)S(1)}, u32[]{:S(2)}, u32[]{:S(2)}) collective-permute-start(bf16[2,128,512]{2,1,0:T(8,128)(2,1)S(1)} %get-tuple-element.38), channel_id=1, source_target_pairs={{0,2},{1,3},{2,0},{3,1},{4,6},{5,7},{6,4},{7,5},{8,10},{9,11},{10,... | collective-permute-start | bytes 786440 | tf_op jit(solution)/shard_map/ppermute | solution.py:410
  188.3 10.0 %collective-permute-start.20 = (bf16[2,128,512]{2,1,0:T(8,128)(2,1)S(1)}, bf16[2,128,512]{2,1,0:T(8,128)(2,1)S(1)}, u32[]{:S(2)}, u32[]{:S(2)}) collective-permute-start(bf16[2,128,512]{2,1,0:T(8,128)(2,1)S(1)} %get-tuple-element.39), channel_id=1, source_target_pairs={{0,4},{4,0},{8,12},{12,8},{16,20},{20,16},{24,28},{28,24},{1,5},{5... | collective-permute-start | bytes 786440 | tf_op jit(solution)/shard_map/ppermute | solution.py:404
  188.5 15.8 %collective-permute-start.21 = (bf16[2,128,512]{2,1,0:T(8,128)(2,1)S(1)}, bf16[2,128,512]{2,1,0:T(8,128)(2,1)S(1)}, u32[]{:S(2)}, u32[]{:S(2)}) collective-permute-start(bf16[2,128,512]{2,1,0:T(8,128)(2,1)S(1)} %get-tuple-element.40), channel_id=1, source_target_pairs={{0,6},{1,7},{2,4},{3,5},{4,2},{5,3},{6,0},{7,1},{8,14},{9,15},{10,... | collective-permute-start | bytes 786440 | tf_op jit(solution)/shard_map/ppermute | solution.py:463
  192.3 15.2 %collective-permute-start.23 = (bf16[2,128,512]{2,1,0:T(8,128)(2,1)S(1)}, bf16[2,128,512]{2,1,0:T(8,128)(2,1)S(1)}, u32[]{:S(2)}, u32[]{:S(2)}) collective-permute-start(bf16[2,128,512]{2,1,0:T(8,128)(2,1)S(1)} %get-tuple-element.44), channel_id=1, source_target_pairs={{0,2},{1,3},{2,0},{3,1},{4,6},{5,7},{6,4},{7,5},{8,10},{9,11},{10,... | collective-permute-start | bytes 786440 | tf_op jit(solution)/shard_map/ppermute | solution.py:410
  192.6 16.1 %collective-permute-start.24 = (bf16[2,128,512]{2,1,0:T(8,128)(2,1)S(1)}, bf16[2,128,512]{2,1,0:T(8,128)(2,1)S(1)}, u32[]{:S(2)}, u32[]{:S(2)}) collective-permute-start(bf16[2,128,512]{2,1,0:T(8,128)(2,1)S(1)} %get-tuple-element.45), channel_id=1, source_target_pairs={{0,4},{4,0},{8,12},{12,8},{16,20},{20,16},{24,28},{28,24},{1,5},{5... | collective-permute-start | bytes 786440 | tf_op jit(solution)/shard_map/ppermute | solution.py:404
  198.2 16.1 %collective-permute-start.25 = (bf16[2,128,512]{2,1,0:T(8,128)(2,1)S(1)}, bf16[2,128,512]{2,1,0:T(8,128)(2,1)S(1)}, u32[]{:S(2)}, u32[]{:S(2)}) collective-permute-start(bf16[2,128,512]{2,1,0:T(8,128)(2,1)S(1)} %get-tuple-element.46), channel_id=1, source_target_pairs={{0,6},{1,7},{2,4},{3,5},{4,2},{5,3},{6,0},{7,1},{8,14},{9,15},{10,... | collective-permute-start | bytes 786440 | tf_op jit(solution)/shard_map/ppermute | solution.py:463
Sparse Core Ops, SparseCore 0:
  8.9 122.5 all-gather.2

commit v4 on v3

--- a/solution.py
+++ b/solution.py
@@ -197,7 +197,11 @@
     return 3 * (-(-2 * (cols // HEAD) // 16) * 16)
 
 
-def own_kernel(coef, cols, at, q, kv_m, kv_o, low_m, low_o, out):
+def stacked(refs):
+    return [ref[i] for ref in refs for i in range(ref.shape[0])]
+
+
+def own_kernel(coef, cols, at, q, kv_m, kv_o, *refs):
     x, z = at[0], at[1]
     below = z == 1
     block = 256
@@ -208,10 +212,10 @@
     k_e, k_o = jnp.where(first, kv_m[0], kv_o[0]), jnp.where(first, kv_o[0], kv_m[0])
     v_e, v_o = jnp.where(first, kv_m[1], kv_o[1]), jnp.where(first, kv_o[1], kv_m[1])
     v_e, v_o = with_ones(v_e), with_ones(v_o)
-    lk_e = jnp.where(first, low_m[0], low_o[0])
-    lk_o = jnp.where(first, low_o[0], low_m[0])
-    lv_e = jnp.where(first, low_m[1], low_o[1])
-    lv_o = jnp.where(first, low_o[1], low_m[1])
+    *low, out = refs
+    m_k, m_v, o_k, o_v = stacked(low)
+    lk_e, lk_o = jnp.where(first, m_k, o_k), jnp.where(first, o_k, m_k)
+    lv_e, lv_o = jnp.where(first, m_v, o_v), jnp.where(first, o_v, m_v)
     lv_o1 = with_ones(lv_o)
     evens, odds = [], []
     for part in range(cols // block):
@@ -233,7 +237,7 @@
     put_lse(out, 2 * cols, evens, odds)
 
 
-def upper_kernel(coef, cols, at, qa, qb, kv_m, kv_o, low_m, low_o, out_a, out_b):
+def upper_kernel(coef, cols, at, qa, qb, kv_m, kv_o, *refs):
     x, z = at[0], at[1]
     below = z == 1
     first = x == 0
@@ -241,12 +245,13 @@
     k_e, k_o = jnp.where(first, kv_m[0], kv_o[0]), jnp.where(first, kv_o[0], kv_m[0])
     v_e, v_o = jnp.where(first, kv_m[1], kv_o[1]), jnp.where(first, kv_o[1], kv_m[1])
     v_o1 = with_ones(v_o)
+    *low, out_a, out_b = refs
+    lows = stacked(low)
     rows_a, rows_b = ([], []), ([], [])
-    for part in range(cols // block):
-        a, b = part * block, (part + 1) * block
+    for index in range(cols // block):
+        a, b = index * block, (index + 1) * block
         mine = slice(a, b)
-        m_k, m_v = low_m[0, mine].astype(F32), low_m[1, mine].astype(F32)
-        o_k, o_v = low_o[0, mine].astype(F32), low_o[1, mine].astype(F32)
+        m_k, m_v, o_k, o_v = (part[mine].astype(F32) for part in lows)
         ce = (k_e[mine].astype(F32), v_e[mine].astype(F32), None)
         co = (k_o[mine].astype(F32), v_o[mine].astype(F32), None)
         low = [(m_k, m_v, below), (o_k, o_v, below)]
@@ -322,7 +327,7 @@
         out[0] = c.astype(BF16).reshape(2, 2, tokens, weight.shape[2])
 
 
-def project(at, near, far, weight, start, count):
+def project(at, near, far, weight, count, pick):
     _, cols, width = near[0].shape
     shape = (2, 2, 2, cols // 4, width)
     args = [a.reshape(shape) for a in near + far]
@@ -336,7 +341,7 @@
             num_scalar_prefetch=1,
             grid=(count,),
             in_specs=[pl.BlockSpec(shape, lambda s, at: (0,) * 5)] * len(args)
-            + [pl.BlockSpec((1, depth, out_width), lambda s, at: (start + s, 0, 0))],
+            + [pl.BlockSpec((1, depth, out_width), lambda s, at: (pick(s, at), 0, 0))],
             out_specs=[out_spec, out_spec],
         ),
         compiler_params=pltpu.CompilerParams(vmem_limit_bytes=VMEM),
@@ -369,16 +374,16 @@
 
 
 def place_kernel(at, *refs):
-    x, out = at[0], refs[-1]
-    layer = 0
+    x, z, out = at[0], at[1], refs[-1]
+    layers = [z - z % 2, z - z % 2 + 1, (z + 2) % 4, 3 - z]
     for stay, from_y, from_x, from_xy in zip(*(refs[i:-1:4] for i in range(4))):
         width = stay.shape[-1]
         for s in range(stay.shape[0]):
-            mine = pl.ds(pl.multiple_of((2 * layer + x) * width, width), width)
-            theirs = pl.ds(pl.multiple_of((2 * layer + 1 - x) * width, width), width)
+            base = 2 * layers.pop(0)
+            mine = pl.ds(pl.multiple_of((base + x) * width, width), width)
+            theirs = pl.ds(pl.multiple_of((base + 1 - x) * width, width), width)
             out[:, mine] = total(stay[s], from_y[s])
             out[:, theirs] = total(from_x[s], from_xy[s])
-            layer += 1
 
 
 def after(value, *earlier):
@@ -415,18 +420,21 @@
     def give(array, lo, hi, c):
         return lax.dynamic_slice(array, (lo, 0, (1 - x) * half + c * width), (hi - lo, cols, width))
 
+    w_up = seq_perm(out_weight, (0, 2), (1, 3))
     q, kv, low, qa, qb = [], [], [], [], []
+    q_other = swap(lax.dynamic_slice(local, (0, 0, (1 - x) * half), (1, cols, half)))
     for c in range(chunks):
-        source = local if c == 0 else after(local, kv[0][1])
-        mine, other = keep(source, 0, 1, c), swap(give(source, 0, 1, c))
+        mine, other = keep(local, 0, 1, c), q_other[:, :, c * width : (c + 1) * width]
         q.append(jnp.concatenate([jnp.where(first, mine, other), jnp.where(first, other, mine)]))
         going = q[c] if c == 0 else after(q[c], qa[0], qb[0])
         qa.append(seq_perm(going, (2, 1), (3, 2)))
         qb.append(seq_perm(going, (3, 1)))
-        kv.append((keep(source, 1, 3, c), swap(give(source, 1, 3, c))))
-        low.append(tuple(seq_perm(half_kv, (0, 1)) for half_kv in kv[c]))
-    layers = [[2 * i + j for i in range(4)] for j in range(2)]
-    weight = lax.all_gather(out_weight, "seq", axis_index_groups=layers)
+        source = after(local, q[0]) if c == 0 else after(local, kv[0][1])
+        kv.append((keep(local if c == 0 else source, 1, 3, c), swap(give(source, 1, 3, c))))
+        if c == 0:
+            low.append([seq_perm(half_kv, (0, 1)) for half_kv in kv[c]])
+        else:
+            low.append([seq_perm(after(jnp.concatenate(kv[c]), *low[0], w_up), (0, 1))])
 
     struct = jax.ShapeDtypeStruct
     partial = struct((2 * cols + lse_height(cols), width), BF16)
@@ -444,21 +452,34 @@
             heads, "own_rows", 4)
         own.append(mine)
 
-    near, far = [], []
-    for c in range(chunks):
+    pairs = [[0, 2], [1, 3], [4, 6], [5, 7]]
+    w_pair = lax.all_gather(after(out_weight, low[1][0], qa[1]), "seq", axis_index_groups=pairs)
+    w_down = seq_perm(after(out_weight, qa[1], qb[1]), (2, 0), (3, 1))
+
+    def merged(c, earlier):
         (a,) = head_call(
-            functools.partial(merge_kernel, cols), after(at, sent[-1]), [own[c], oa[c], ob[c]],
+            functools.partial(merge_kernel, cols), after(at, earlier), [own[c], oa[c], ob[c]],
             [struct((2, cols, width), BF16)], heads, "merge", 2)
-        near.append(a)
-        far.append(swap(a))
-
-    count = 2
+        return a, swap(a)
+
+    first_half = merged(0, sent[1])
+    w_far = jnp.where(z >= 2, w_up, after(w_down, first_half[0], own[1]))
+    w_far_pair = lax.all_gather(w_far, "seq", axis_index_groups=pairs)
+    near, far = map(list, zip(first_half, merged(1, w_far)))
+
     parts = []
-    for start in range(0, 4, count):
-        send, kept = project(at, near, far, weight, start, count)
+    turn = at
+    groups = [
+        (w_pair, 2, lambda s, at: s),
+        (w_far[None], 1, lambda s, at: 0),
+        (w_far_pair, 1, lambda s, at: 1 - at[1] % 2),
+    ]
+    for weight, count, pick in groups:
+        send, kept = project(turn, near, far, weight, count, pick)
         got = head_perm(send, 1)
         piece = struct((count,) + send.shape[3:], BF16)
         stay, to_y, to_x, to_xy = whole_call(split_kernel, at, [kept, got], [piece] * 4, "split", 2)
+        turn = after(at, stay, *parts)
         diagonal = [((2 * i + j) * 4 + h, (2 * i + 1 - j) * 4 + (h ^ 2)) for i in range(4) for j in range(2) for h in range(4)]
         from_xy = lax.ppermute(to_xy, ("seq", "head"), diagonal)
         parts += [stay, head_perm(to_y, 2), swap(to_x), from_xy]

time: 224 us -> 252 us (1.12)
  the two profiles are of different devices: /device:TPU:28 before, /device:TPU:16 now
where the time goes in v4:
time: 252 us; the launch traced here: 249 us
  waiting for transfers between devices  92.9 us (37%)
  starting transfers between devices  69.1 us (27%)
  Pallas kernels  44 us (17%)
  local copies, waits for them, and re-layouts  23 us (9%)
  between operations  13.7 us (5%)
  other arithmetic  6.51 us (3%)
    ppermute x21, waiting for transfers between devices, seq_perm(): return lax.ppermute(array, 'seq', pairs)  65.2 us
    ppermute x21, starting transfers between devices, seq_perm(): return lax.ppermute(array, 'seq', pairs)  61.2 us
    pallas_call x6, Pallas kernels, head_call(): pl.pallas_call(kernel, out_shape=outs, grid_spec=pltpu.PrefetchScalarGrid...  32.3 us
    unnamed x70, local copies, waits for them, and re-layouts  18.3 us
    all_gather x1, waiting for transfers between devices, body_eight(): w_far_pair = lax.all_gather(w_far, 'seq', axis_index_groups=pairs)  10.9 us
    ppermute x6, waiting for transfers between devices, head_perm(): return lax.ppermute(array, 'head', [(i, i ^ flip) for i in range(4)])  8.51 us
    ppermute x3, waiting for transfers between devices, body_eight(): from_xy = lax.ppermute(to_xy, ('seq', 'head'), diagonal)  8.33 us
    pallas_call x3, Pallas kernels, project(): pl.pallas_call(functools.partial(project_kernel, len(near)), out_shape=[o...  7.88 us
  transfers between devices with their start and end apart: 32, of which 17 were waited for; matrix products, arithmetic and copies ran while one was open for 3% of the time, Pallas kernels for 15%

profile of v4, /device:TPU:16, one launch (start us, length us, event | category | flops | bytes accessed | tf_op | source)
XLA Modules:
  0.0 249.3 jit_solution(564711059853919314)
XLA Ops:
  9.2 12.2 %collective-permute-done = bf16[1,512,512]{2,1,0:T(8,128)(2,1)S(1)} collective-permute-done((bf16[1,512,512]{2,1,0:T(8,128)(2,1)S(1)}, bf16[1,512,512]{2,1,0:T(8,128)(2,1)S(1)}, u32[]{:S(2)}, u32[]{:S(2)}) %collective-permute-start) | collective-permute-done | bytes 524320 | tf_op jit(solution)/shard_map/ppermute | solution.py:409
  21.3 1.9 bitcast_select_fusion.1
  27.3 10.0 %collective-permute-done.3.kv_o = bf16[2,512,256]{2,1,0:T(8,128)(2,1)S(1)} collective-permute-done((bf16[2,512,256]{2,1,0:T(8,128)(2,1)S(1)}, bf16[2,512,256]{2,1,0:T(8,128)(2,1)S(1)}, u32[]{:S(2)}, u32[]{:S(2)}) %collective-permute-start.3) | collective-permute-done | bytes 524320 | tf_op jit(solution)/shard_map/ppermute | solution.py:409
  42.8 3.6 %collective-permute-start.1 = (bf16[2,512,256]{2,1,0:T(8,128)(2,1)S(1)}, bf16[2,512,256]{2,1,0:T(8,128)(2,1)S(1)}, u32[]{:S(2)}, u32[]{:S(2)}) collective-permute-start(bf16[2,512,256]{2,1,0:T(8,128)(2,1)S(1)} %pad_maximum_fusion.1.q), channel_id=1, source_target_pairs={{16,8},{20,12},{24,16},{28,20},{17,9},{21,13},{25,17},{29,21},{18,... | collective-permute-start | bytes 1572872 | tf_op jit(solution)/shard_map/ppermute | solution.py:409
  46.4 4.4 %collective-permute-done.8.kv_o = bf16[2,512,256]{2,1,0:T(8,128)(2,1)S(1)} collective-permute-done((bf16[2,512,256]{2,1,0:T(8,128)(2,1)S(1)}, bf16[2,512,256]{2,1,0:T(8,128)(2,1)S(1)}, u32[]{:S(2)}, u32[]{:S(2)}) %collective-permute-start.8) | collective-permute-done | bytes 524320 | tf_op jit(solution)/shard_map/ppermute | solution.py:409
  56.0 1.6 collective-permute-start.10
  60.4 21.3 %collective-permute-start.6 = (bf16[2,512,256]{2,1,0:T(8,128)(2,1)S(1)}, bf16[2,512,256]{2,1,0:T(8,128)(2,1)S(1)}, u32[]{:S(2)}, u32[]{:S(2)}) collective-permute-start(bf16[2,512,256]{2,1,0:T(8,128)(2,1)S(1)} %pad_maximum_fusion.2.q), channel_id=1, source_target_pairs={{16,8},{20,12},{24,16},{28,20},{17,9},{21,13},{25,17},{29,21},{18,... | collective-permute-start | bytes 1572872 | tf_op jit(solution)/shard_map/ppermute | solution.py:409
  86.6 7.0 %upper_rows.2 = (bf16[1072,256]{1,0:T(8,128)(2,1)}, bf16[1072,256]{1,0:T(8,128)(2,1)S(1)}) custom-call(s32[4]{0:T(128)S(1)} %pad_add_fusion.at, bf16[2,512,256]{2,1,0:T(8,128)(2,1)S(1)} %copy-done.14, bf16[2,512,256]{2,1,0:T(8,128)(2,1)} %collective-permute-done.2.qb, bf16[2,512,256]{2,1,0:T(8,128)(2,1)S(1)} %dynamic-slice_bitcast_fusion.kv_m, ...), custom_call_target="tpu_custom_call" | custom-call | flops 4400000000 | bytes 4000000 | tf_op jit(solution)/shard_map/upper_rows/pallas_call | solution.py:296
  93.7 4.0 %collective-permute-start.11 = (bf16[1072,256]{1,0:T(8,128)(2,1)}, bf16[1072,256]{1,0:T(8,128)(2,1)}, u32[]{:S(2)}, u32[]{:S(2)}) collective-permute-start(bf16[1072,256]{1,0:T(8,128)(2,1)} %get-tuple-element.41), channel_id=1, source_target_pairs={{8,16},{12,20},{16,24},{20,28},{9,17},{13,21},{17,25},{21,29},{10,... | collective-permute-start | bytes 1646600 | tf_op jit(solution)/shard_map/ppermute | solution.py:409
  100.8 2.3 collective-permute-start.13
  106.3 5.4 %own_rows.2.own = bf16[1072,256]{1,0:T(8,128)(2,1)S(1)} custom-call(s32[4]{0:T(128)S(1)} %pad_add_fusion.at, bf16[2,512,256]{2,1,0:T(8,128)(2,1)S(1)} %pad_maximum_fusion.1.q, bf16[2,512,256]{2,1,0:T(8,128)(2,1)S(1)} %dynamic-slice_bitcast_fusion.kv_m, bf16[2,512,256]{2,1,0:T(8,128)(2,1)S(1)} %copy-done.4, bf16[2,512,256]{2,1,0:T(8,128)(2,1)S(1)} %copy-done.7, ...), custom_call_target="tpu_custom_call" | custom-call | flops 4400000000 | bytes 4000000 | tf_op jit(solution)/shard_map/own_rows/pallas_call | solution.py:296
  111.7 7.4 %upper_rows.3 = (bf16[1072,256]{1,0:T(8,128)(2,1)}, bf16[1072,256]{1,0:T(8,128)(2,1)}) custom-call(s32[4]{0:T(128)S(1)} %pad_add_fusion.at, bf16[2,512,256]{2,1,0:T(8,128)(2,1)S(1)} %copy-done.22, bf16[2,512,256]{2,1,0:T(8,128)(2,1)S(1)} %copy-done.24, bf16[2,512,256]{2,1,0:T(8,128)(2,1)S(1)} %get-tuple-element.80.kv_m, ...), custom_call_target="tpu_custom_call" | custom-call | flops 4400000000 | bytes 4000000 | tf_op jit(solution)/shard_map/upper_rows/pallas_call | solution.py:296
  119.1 11.3 %collective-permute-start.14 = (bf16[1072,256]{1,0:T(8,128)(2,1)}, bf16[1072,256]{1,0:T(8,128)(2,1)}, u32[]{:S(2)}, u32[]{:S(2)}) collective-permute-start(bf16[1072,256]{1,0:T(8,128)(2,1)} %get-tuple-element.47), channel_id=1, source_target_pairs={{8,16},{12,20},{16,24},{20,28},{9,17},{13,21},{17,25},{21,29},{10,... | collective-permute-start | bytes 1646600 | tf_op jit(solution)/shard_map/ppermute | solution.py:409
  131.9 3.2 %merge.2 = bf16[2,512,256]{2,1,0:T(8,128)(2,1)S(1)} custom-call(s32[4]{0:T(128)S(1)} %pad_add_fusion.at, bf16[1072,256]{1,0:T(8,128)(2,1)S(1)} %own_rows.2.own, bf16[1072,256]{1,0:T(8,128)(2,1)} %collective-permute-done.11.oa, bf16[1072,256]{1,0:T(8,128)(2,1)} %collective-permute-done.12.ob), custom_call_target="tpu_custom_call" | custom-call | flops 2200000000 | bytes 2000000 | tf_op jit(solution)/shard_map/merge/pallas_call | solution.py:296
  135.6 6.1 %own_rows.3.own = bf16[1072,256]{1,0:T(8,128)(2,1)S(1)} custom-call(s32[4]{0:T(128)S(1)} %pad_add_fusion.at, bf16[2,512,256]{2,1,0:T(8,128)(2,1)S(1)} %pad_maximum_fusion.2.q, bf16[2,512,256]{2,1,0:T(8,128)(2,1)S(1)} %get-tuple-element.80.kv_m, bf16[2,512,256]{2,1,0:T(8,128)(2,1)S(1)} %collective-permute-done.8.kv_o, ...), custom_call_target="tpu_custom_call" | custom-call | flops 4400000000 | bytes 4000000 | tf_op jit(solution)/shard_map/own_rows/pallas_call | solution.py:296
  142.5 7.2 %collective-permute-done.13 = bf16[1024,512]{1,0:T(8,128)(2,1)} collective-permute-done((bf16[1024,512]{1,0:T(8,128)(2,1)}, bf16[1024,512]{1,0:T(8,128)(2,1)}, u32[]{:S(2)}, u32[]{:S(2)}) %collective-permute-start.13) | collective-permute-done | bytes 1048608 | tf_op jit(solution)/shard_map/ppermute | solution.py:409
  149.7 2.4 broadcast_select_fusion
  152.1 14.3 %collective-permute-done.14.oa = bf16[1072,256]{1,0:T(8,128)(2,1)} collective-permute-done((bf16[1072,256]{1,0:T(8,128)(2,1)}, bf16[1072,256]{1,0:T(8,128)(2,1)}, u32[]{:S(2)}, u32[]{:S(2)}) %collective-permute-start.14) | collective-permute-done | bytes 548896 | tf_op jit(solution)/shard_map/ppermute | solution.py:409
  166.4 3.2 %merge.3 = bf16[2,512,256]{2,1,0:T(8,128)(2,1)S(1)} custom-call(s32[4]{0:T(128)S(1)} %pad_add_fusion.at, bf16[1072,256]{1,0:T(8,128)(2,1)S(1)} %copy-done.32, bf16[1072,256]{1,0:T(8,128)(2,1)} %collective-permute-done.14.oa, bf16[1072,256]{1,0:T(8,128)(2,1)} %collective-permute-done.15.ob), custom_call_target="tpu_custom_call" | custom-call | flops 2200000000 | bytes 2000000 | tf_op jit(solution)/shard_map/merge/pallas_call | solution.py:296
  170.2 11.6 %collective-permute-done.17 = bf16[2,512,256]{2,1,0:T(8,128)(2,1)S(1)} collective-permute-done((bf16[2,512,256]{2,1,0:T(8,128)(2,1)S(1)}, bf16[2,512,256]{2,1,0:T(8,128)(2,1)S(1)}, u32[]{:S(2)}, u32[]{:S(2)}) %collective-permute-start.17) | collective-permute-done | bytes 524320 | tf_op jit(solution)/shard_map/ppermute | solution.py:409
  181.8 4.3 %project.3 = (bf16[2,2,2,128,512]{4,3,2,1,0:T(8,128)(2,1)S(1)}, bf16[2,2,2,128,512]{4,3,2,1,0:T(8,128)(2,1)S(1)}) custom-call(s32[4]{0:T(128)S(1)} %pad_add_fusion.at, bf16[2,2,2,128,256]{4,3,2,1,0:T(8,128)(2,1)S(1)} %bitcast.25, bf16[2,2,2,128,256]{4,3,2,1,0:T(8,128)(2,1)S(1)} %bitcast.31, bf16[2,2,2,128,256]{4,3,2,1,0:T(8,128)(2,1)S(1)} %bitcast.28, ...), custom_call_target="tpu_custom_call" | custom-call | flops 4400000000 | bytes 4000000 | tf_op jit(solution)/shard_map/project/pallas_call | solution.py:337
  187.2 2.6 %collective-permute-done.18.got = bf16[2,2,2,128,512]{4,3,2,1,0:T(8,128)(2,1)S(1)} collective-permute-done((bf16[2,2,2,128,512]{4,3,2,1,0:T(8,128)(2,1)S(1)}, bf16[2,2,2,128,512]{4,3,2,1,0:T(8,128)(2,1)S(1)}, u32[]{:S(2)}, u32[]{:S(2)}) %collective-permute-start.18) | collective-permute-done | bytes 1048608 | tf_op jit(solution)/shard_map/ppermute | solution.py:415
  192.7 1.8 project.4
  198.9 4.4 %collective-permute-done.19.refs_1_ = bf16[2,128,512]{2,1,0:T(8,128)(2,1)S(1)} collective-permute-done((bf16[2,128,512]{2,1,0:T(8,128)(2,1)S(1)}, bf16[2,128,512]{2,1,0:T(8,128)(2,1)S(1)}, u32[]{:S(2)}, u32[]{:S(2)}) %collective-permute-start.19) | collective-permute-done | bytes 262176 | tf_op jit(solution)/shard_map/ppermute | solution.py:415
  203.3 2.1 collective-permute-done.20.refs_2_
  206.1 4.0 %collective-permute-done.21.refs_3_ = bf16[2,128,512]{2,1,0:T(8,128)(2,1)S(1)} collective-permute-done((bf16[2,128,512]{2,1,0:T(8,128)(2,1)S(1)}, bf16[2,128,512]{2,1,0:T(8,128)(2,1)S(1)}, u32[]{:S(2)}, u32[]{:S(2)}) %collective-permute-start.21) | collective-permute-done | bytes 262176 | tf_op jit(solution)/shard_map/ppermute | solution.py:484
  210.8 10.9 %all-gather.7.cloned.1.call-done = bf16[2048,512]{1,0:T(8,128)(2,1)} async-done(((bf16[1024,512]{1,0:T(8,128)(2,1)}), bf16[2048,512]{1,0:T(8,128)(2,1)}) %all-gather.7.cloned.1.call-update) | async-done | bytes 2097168 | tf_op jit(solution)/shard_map/all_gather | solution.py:467
  221.7 1.6 copy-done.1
  223.3 1.8 project.5
  233.5 2.3 collective-permute-done.25.refs_7_
  238.7 2.0 collective-permute-done.29.refs_11_
  240.7 1.8 place.1
  (127 shorter events, 55.7 us)
Async XLA Ops:
  6.5 175.3 %all-gather.5.cloned.1.call-start = ((), (), s32[]{:S(2)}) async-start(), calls=%async_computation | async-start | bytes 3145728 | tf_op jit(solution)/shard_map/all_gather | solution.py:456
  7.6 13.7 %collective-permute-start = (bf16[1,512,512]{2,1,0:T(8,128)(2,1)S(1)}, bf16[1,512,512]{2,1,0:T(8,128)(2,1)S(1)}, u32[]{:S(2)}, u32[]{:S(2)}) collective-permute-start(bf16[1,512,512]{2,1,0:T(8,128)(2,1)S(1)} %dynamic-slice_bitcast_fusion.1), channel_id=1, source_target_pairs={{0,4},{4,0},{8,12},{12,8},{16,20},{20,16},{24,28},{28,24},{1,5},{5... | collective-permute-start | bytes 1572872 | tf_op jit(solution)/shard_map/ppermute | solution.py:409
  24.4 12.9 %collective-permute-start.3 = (bf16[2,512,256]{2,1,0:T(8,128)(2,1)S(1)}, bf16[2,512,256]{2,1,0:T(8,128)(2,1)S(1)}, u32[]{:S(2)}, u32[]{:S(2)}) collective-permute-start(bf16[2,512,256]{2,1,0:T(8,128)(2,1)S(1)} %constant_dynamic-slice_fusion.2), channel_id=1, source_target_pairs={{0,4},{4,0},{8,12},{12,8},{16,20},{20,16},{24,28},{28,24},{1,5},{5... | collective-permute-start | bytes 1572872 | tf_op jit(solution)/shard_map/ppermute | solution.py:409
  26.0 29.2 %collective-permute-start.9 = (bf16[1024,512]{1,0:T(8,128)(2,1)}, bf16[1024,512]{1,0:T(8,128)(2,1)}, u32[]{:S(2)}, u32[]{:S(2)}) collective-permute-start(bf16[1024,512]{1,0:T(8,128)(2,1)} %param.3), channel_id=1, source_target_pairs={{0,16},{4,20},{8,24},{12,28},{1,17},{5,21},{9,25},{13,29},{2,18},{... | collective-permute-start | bytes 3145736 | tf_op jit(solution)/shard_map/ppermute | solution.py:409
  38.8 12.0 %collective-permute-start.8 = (bf16[2,512,256]{2,1,0:T(8,128)(2,1)S(1)}, bf16[2,512,256]{2,1,0:T(8,128)(2,1)S(1)}, u32[]{:S(2)}, u32[]{:S(2)}) collective-permute-start(bf16[2,512,256]{2,1,0:T(8,128)(2,1)S(1)} %get-tuple-element.79), channel_id=1, source_target_pairs={{0,4},{4,0},{8,12},{12,8},{16,20},{20,16},{24,28},{28,24},{1,5},{5... | collective-permute-start | bytes 1572872 | tf_op jit(solution)/shard_map/ppermute | solution.py:409
  41.4 12.0 %collective-permute-start.4 = (bf16[2,512,256]{2,1,0:T(8,128)(2,1)S(1)}, bf16[2,512,256]{2,1,0:T(8,128)(2,1)S(1)}, u32[]{:S(2)}, u32[]{:S(2)}) collective-permute-start(bf16[2,512,256]{2,1,0:T(8,128)(2,1)S(1)} %dynamic-slice_bitcast_fusion.kv_m), channel_id=1, source_target_pairs={{0,8},{4,12},{1,9},{5,13},{2,10},{6,14},{3,11},{7,15}} | collective-permute-start | bytes 1572872 | tf_op jit(solution)/shard_map/ppermute | solution.py:409
  42.1 13.1 %collective-permute-start.5 = (bf16[2,512,256]{2,1,0:T(8,128)(2,1)S(1)}, bf16[2,512,256]{2,1,0:T(8,128)(2,1)S(1)}, u32[]{:S(2)}, u32[]{:S(2)}) collective-permute-start(bf16[2,512,256]{2,1,0:T(8,128)(2,1)S(1)} %collective-permute-done.3.kv_o), channel_id=1, source_target_pairs={{0,8},{4,12},{1,9},{5,13},{2,10},{6,14},{3,11},{7,15}} | collective-permute-start | bytes 1572872 | tf_op jit(solution)/shard_map/ppermute | solution.py:409
  42.8 16.8 %collective-permute-start.1 = (bf16[2,512,256]{2,1,0:T(8,128)(2,1)S(1)}, bf16[2,512,256]{2,1,0:T(8,128)(2,1)S(1)}, u32[]{:S(2)}, u32[]{:S(2)}) collective-permute-start(bf16[2,512,256]{2,1,0:T(8,128)(2,1)S(1)} %pad_maximum_fusion.1.q), channel_id=1, source_target_pairs={{16,8},{20,12},{24,16},{28,20},{17,9},{21,13},{25,17},{29,21},{18,... | collective-permute-start | bytes 1572872 | tf_op jit(solution)/shard_map/ppermute | solution.py:409
  50.8 9.6 %collective-permute-start.2 = (bf16[2,512,256]{2,1,0:T(8,128)(2,1)S(1)}, bf16[2,512,256]{2,1,0:T(8,128)(2,1)}, u32[]{:S(2)}, u32[]{:S(2)}) collective-permute-start(bf16[2,512,256]{2,1,0:T(8,128)(2,1)S(1)} %pad_maximum_fusion.1.q), channel_id=1, source_target_pairs={{24,8},{28,12},{25,9},{29,13},{26,10},{30,14},{27,11},{31,15}} | collective-permute-start | bytes 1572872 | tf_op jit(solution)/shard_map/ppermute | solution.py:409
  56.0 47.1 %collective-permute-start.10 = (bf16[4,512,256]{2,1,0:T(8,128)(2,1)}, bf16[4,512,256]{2,1,0:T(8,128)(2,1)}, u32[]{:S(2)}, u32[]{:S(2)}) collective-permute-start(bf16[4,512,256]{2,1,0:T(8,128)(2,1)} %pad_maximum_fusion), channel_id=1, source_target_pairs={{0,8},{4,12},{1,9},{5,13},{2,10},{6,14},{3,11},{7,15}} | collective-permute-start | bytes 3145736 | tf_op jit(solution)/shard_map/ppermute | solution.py:409
  60.4 38.8 %collective-permute-start.6 = (bf16[2,512,256]{2,1,0:T(8,128)(2,1)S(1)}, bf16[2,512,256]{2,1,0:T(8,128)(2,1)S(1)}, u32[]{:S(2)}, u32[]{:S(2)}) collective-permute-start(bf16[2,512,256]{2,1,0:T(8,128)(2,1)S(1)} %pad_maximum_fusion.2.q), channel_id=1, source_target_pairs={{16,8},{20,12},{24,16},{28,20},{17,9},{21,13},{25,17},{29,21},{18,... | collective-permute-start | bytes 1572872 | tf_op jit(solution)/shard_map/ppermute | solution.py:409
  81.7 18.3 %collective-permute-start.7 = (bf16[2,512,256]{2,1,0:T(8,128)(2,1)S(1)}, bf16[2,512,256]{2,1,0:T(8,128)(2,1)S(1)}, u32[]{:S(2)}, u32[]{:S(2)}) collective-permute-start(bf16[2,512,256]{2,1,0:T(8,128)(2,1)S(1)} %pad_maximum_fusion.2.q), channel_id=1, source_target_pairs={{24,8},{28,12},{25,9},{29,13},{26,10},{30,14},{27,11},{31,15}} | collective-permute-start | bytes 1572872 | tf_op jit(solution)/shard_map/ppermute | solution.py:409
  93.7 38.2 %collective-permute-start.11 = (bf16[1072,256]{1,0:T(8,128)(2,1)}, bf16[1072,256]{1,0:T(8,128)(2,1)}, u32[]{:S(2)}, u32[]{:S(2)}) collective-permute-start(bf16[1072,256]{1,0:T(8,128)(2,1)} %get-tuple-element.41), channel_id=1, source_target_pairs={{8,16},{12,20},{16,24},{20,28},{9,17},{13,21},{17,25},{21,29},{10,... | collective-permute-start | bytes 1646600 | tf_op jit(solution)/shard_map/ppermute | solution.py:409
  97.7 34.2 %collective-permute-start.12 = (bf16[1072,256]{1,0:T(8,128)(2,1)S(1)}, bf16[1072,256]{1,0:T(8,128)(2,1)}, u32[]{:S(2)}, u32[]{:S(2)}) collective-permute-start(bf16[1072,256]{1,0:T(8,128)(2,1)S(1)} %get-tuple-element.49), channel_id=1, source_target_pairs={{8,24},{12,28},{9,25},{13,29},{10,26},{14,30},{11,27},{15,31}} | collective-permute-start | bytes 1646600 | tf_op jit(solution)/shard_map/ppermute | solution.py:409
  100.8 48.9 %collective-permute-start.13 = (bf16[1024,512]{1,0:T(8,128)(2,1)}, bf16[1024,512]{1,0:T(8,128)(2,1)}, u32[]{:S(2)}, u32[]{:S(2)}) collective-permute-start(bf16[1024,512]{1,0:T(8,128)(2,1)} %param.3), channel_id=1, source_target_pairs={{16,0},{20,4},{24,8},{28,12},{17,1},{21,5},{25,9},{29,13},{18,2},{... | collective-permute-start | bytes 3145736 | tf_op jit(solution)/shard_map/ppermute | solution.py:409
  103.1 118.5 %all-gather.7.cloned.1.call-start = ((), (), s32[]{:S(2)}) async-start(), calls=%async_computation.1 | async-start | bytes 3145728 | tf_op jit(solution)/shard_map/all_gather | solution.py:467
  119.1 47.3 %collective-permute-start.14 = (bf16[1072,256]{1,0:T(8,128)(2,1)}, bf16[1072,256]{1,0:T(8,128)(2,1)}, u32[]{:S(2)}, u32[]{:S(2)}) collective-permute-start(bf16[1072,256]{1,0:T(8,128)(2,1)} %get-tuple-element.47), channel_id=1, source_target_pairs={{8,16},{12,20},{16,24},{20,28},{9,17},{13,21},{17,25},{21,29},{10,... | collective-permute-start | bytes 1646600 | tf_op jit(solution)/shard_map/ppermute | solution.py:409
  130.4 36.0 %collective-permute-start.15 = (bf16[1072,256]{1,0:T(8,128)(2,1)}, bf16[1072,256]{1,0:T(8,128)(2,1)}, u32[]{:S(2)}, u32[]{:S(2)}) collective-permute-start(bf16[1072,256]{1,0:T(8,128)(2,1)} %get-tuple-element.53), channel_id=1, source_target_pairs={{8,24},{12,28},{9,25},{13,29},{10,26},{14,30},{11,27},{15,31}} | collective-permute-start | bytes 1646600 | tf_op jit(solution)/shard_map/ppermute | solution.py:409
  135.1 35.1 %collective-permute-start.16 = (bf16[2,512,256]{2,1,0:T(8,128)(2,1)S(1)}, bf16[2,512,256]{2,1,0:T(8,128)(2,1)S(1)}, u32[]{:S(2)}, u32[]{:S(2)}) collective-permute-start(bf16[2,512,256]{2,1,0:T(8,128)(2,1)S(1)} %merge.2), channel_id=1, source_target_pairs={{0,4},{4,0},{8,12},{12,8},{16,20},{20,16},{24,28},{28,24},{1,5},{5... | collective-permute-start | bytes 1572872 | tf_op jit(solution)/shard_map/ppermute | solution.py:409
  169.6 12.2 %collective-permute-start.17 = (bf16[2,512,256]{2,1,0:T(8,128)(2,1)S(1)}, bf16[2,512,256]{2,1,0:T(8,128)(2,1)S(1)}, u32[]{:S(2)}, u32[]{:S(2)}) collective-permute-start(bf16[2,512,256]{2,1,0:T(8,128)(2,1)S(1)} %merge.3), channel_id=1, source_target_pairs={{0,4},{4,0},{8,12},{12,8},{16,20},{20,16},{24,28},{28,24},{1,5},{5... | collective-permute-start | bytes 1572872 | tf_op jit(solution)/shard_map/ppermute | solution.py:409
  187.1 2.7 %collective-permute-start.18 = (bf16[2,2,2,128,512]{4,3,2,1,0:T(8,128)(2,1)S(1)}, bf16[2,2,2,128,512]{4,3,2,1,0:T(8,128)(2,1)S(1)}, u32[]{:S(2)}, u32[]{:S(2)}) collective-permute-start(bf16[2,2,2,128,512]{4,3,2,1,0:T(8,128)(2,1)S(1)} %get-tuple-element.56), channel_id=1, source_target_pairs={{0,1},{1,0},{2,3},{3,2},{4,5},{5,4},{6,7},{7,6},{8,9},{9,8},{10,11... | collective-permute-start | bytes 3145736 | tf_op jit(solution)/shard_map/ppermute | solution.py:415
  194.5 3.7 %collective-permute-start.22 = (bf16[1,2,2,128,512]{4,3,2,1,0:T(8,128)(2,1)S(1)}, bf16[1,2,2,128,512]{4,3,2,1,0:T(8,128)(2,1)S(1)}, u32[]{:S(2)}, u32[]{:S(2)}) collective-permute-start(bf16[1,2,2,128,512]{4,3,2,1,0:T(8,128)(2,1)S(1)} %get-tuple-element.63), channel_id=1, source_target_pairs={{0,1},{1,0},{2,3},{3,2},{4,5},{5,4},{6,7},{7,6},{8,9},{9,8},{10,11... | collective-permute-start | bytes 1572872 | tf_op jit(solution)/shard_map/ppermute | solution.py:415
  194.7 8.6 %collective-permute-start.19 = (bf16[2,128,512]{2,1,0:T(8,128)(2,1)S(1)}, bf16[2,128,512]{2,1,0:T(8,128)(2,1)S(1)}, u32[]{:S(2)}, u32[]{:S(2)}) collective-permute-start(bf16[2,128,512]{2,1,0:T(8,128)(2,1)S(1)} %get-tuple-element.58), channel_id=1, source_target_pairs={{0,2},{1,3},{2,0},{3,1},{4,6},{5,7},{6,4},{7,5},{8,10},{9,11},{10,... | collective-permute-start | bytes 786440 | tf_op jit(solution)/shard_map/ppermute | solution.py:415
  196.2 9.2 %collective-permute-start.20 = (bf16[2,128,512]{2,1,0:T(8,128)(2,1)S(1)}, bf16[2,128,512]{2,1,0:T(8,128)(2,1)S(1)}, u32[]{:S(2)}, u32[]{:S(2)}) collective-permute-start(bf16[2,128,512]{2,1,0:T(8,128)(2,1)S(1)} %get-tuple-element.59), channel_id=1, source_target_pairs={{0,4},{4,0},{8,12},{12,8},{16,20},{20,16},{24,28},{28,24},{1,5},{5... | collective-permute-start | bytes 786440 | tf_op jit(solution)/shard_map/ppermute | solution.py:409
  196.8 13.2 %collective-permute-start.21 = (bf16[2,128,512]{2,1,0:T(8,128)(2,1)S(1)}, bf16[2,128,512]{2,1,0:T(8,128)(2,1)S(1)}, u32[]{:S(2)}, u32[]{:S(2)}) collective-permute-start(bf16[2,128,512]{2,1,0:T(8,128)(2,1)S(1)} %get-tuple-element.60), channel_id=1, source_target_pairs={{0,6},{1,7},{2,4},{3,5},{4,2},{5,3},{6,0},{7,1},{8,14},{9,15},{10,... | collective-permute-start | bytes 786440 | tf_op jit(solution)/shard_map/ppermute | solution.py:484
  225.1 3.6 %collective-permute-start.26 = (bf16[1,2,2,128,512]{4,3,2,1,0:T(8,128)(2,1)S(1)}, bf16[1,2,2,128,512]{4,3,2,1,0:T(8,128)(2,1)S(1)}, u32[]{:S(2)}, u32[]{:S(2)}) collective-permute-start(bf16[1,2,2,128,512]{4,3,2,1,0:T(8,128)(2,1)S(1)} %get-tuple-element.70), channel_id=1, source_target_pairs={{0,1},{1,0},{2,3},{3,2},{4,5},{5,4},{6,7},{7,6},{8,9},{9,8},{10,11... | collective-permute-start | bytes 1572872 | tf_op jit(solution)/shard_map/ppermute | solution.py:415
  225.2 7.3 %collective-permute-start.23 = (bf16[1,128,512]{2,1,0:T(8,128)(2,1)S(1)}, bf16[1,128,512]{2,1,0:T(8,128)(2,1)S(1)}, u32[]{:S(2)}, u32[]{:S(2)}) collective-permute-start(bf16[1,128,512]{2,1,0:T(8,128)(2,1)S(1)} %get-tuple-element.65), channel_id=1, source_target_pairs={{0,2},{1,3},{2,0},{3,1},{4,6},{5,7},{6,4},{7,5},{8,10},{9,11},{10,... | collective-permute-start | bytes 393224 | tf_op jit(solution)/shard_map/ppermute | solution.py:415
  226.7 6.8 %collective-permute-start.24 = (bf16[1,128,512]{2,1,0:T(8,128)(2,1)S(1)}, bf16[1,128,512]{2,1,0:T(8,128)(2,1)S(1)}, u32[]{:S(2)}, u32[]{:S(2)}) collective-permute-start(bf16[1,128,512]{2,1,0:T(8,128)(2,1)S(1)} %get-tuple-element.66), channel_id=1, source_target_pairs={{0,4},{4,0},{8,12},{12,8},{16,20},{20,16},{24,28},{28,24},{1,5},{5... | collective-permute-start | bytes 393224 | tf_op jit(solution)/shard_map/ppermute | solution.py:409
  228.2 7.6 %collective-permute-start.25 = (bf16[1,128,512]{2,1,0:T(8,128)(2,1)S(1)}, bf16[1,128,512]{2,1,0:T(8,128)(2,1)S(1)}, u32[]{:S(2)}, u32[]{:S(2)}) collective-permute-start(bf16[1,128,512]{2,1,0:T(8,128)(2,1)S(1)} %get-tuple-element.67), channel_id=1, source_target_pairs={{0,6},{1,7},{2,4},{3,5},{4,2},{5,3},{6,0},{7,1},{8,14},{9,15},{10,... | collective-permute-start | bytes 393224 | tf_op jit(solution)/shard_map/ppermute | solution.py:484
  229.4 7.8 %collective-permute-start.27 = (bf16[1,128,512]{2,1,0:T(8,128)(2,1)S(1)}, bf16[1,128,512]{2,1,0:T(8,128)(2,1)S(1)}, u32[]{:S(2)}, u32[]{:S(2)}) collective-permute-start(bf16[1,128,512]{2,1,0:T(8,128)(2,1)S(1)} %get-tuple-element.72), channel_id=1, source_target_pairs={{0,2},{1,3},{2,0},{3,1},{4,6},{5,7},{6,4},{7,5},{8,10},{9,11},{10,... | collective-permute-start | bytes 393224 | tf_op jit(solution)/shard_map/ppermute | solution.py:415
  231.0 7.7 %collective-permute-start.28 = (bf16[1,128,512]{2,1,0:T(8,128)(2,1)S(1)}, bf16[1,128,512]{2,1,0:T(8,128)(2,1)S(1)}, u32[]{:S(2)}, u32[]{:S(2)}) collective-permute-start(bf16[1,128,512]{2,1,0:T(8,128)(2,1)S(1)} %get-tuple-element.73), channel_id=1, source_target_pairs={{0,4},{4,0},{8,12},{12,8},{16,20},{20,16},{24,28},{28,24},{1,5},{5... | collective-permute-start | bytes 393224 | tf_op jit(solution)/shard_map/ppermute | solution.py:409
  232.4 8.3 %collective-permute-start.29 = (bf16[1,128,512]{2,1,0:T(8,128)(2,1)S(1)}, bf16[1,128,512]{2,1,0:T(8,128)(2,1)S(1)}, u32[]{:S(2)}, u32[]{:S(2)}) collective-permute-start(bf16[1,128,512]{2,1,0:T(8,128)(2,1)S(1)} %get-tuple-element.74), channel_id=1, source_target_pairs={{0,6},{1,7},{2,4},{3,5},{4,2},{5,3},{6,0},{7,1},{8,14},{9,15},{10,... | collective-permute-start | bytes 393224 | tf_op jit(solution)/shard_map/ppermute | solution.py:484
  (35 other events, 193.5 us)
Sparse Core Ops, SparseCore 0:
  103.3 63.5 all-gather.4
  187.3 34.3 all-gather.6

commit v5 on v4

--- a/solution.py
+++ b/solution.py
@@ -10,7 +10,7 @@
 LOG2E = 1.4426950408889634
 NEG = -1e30
 QB = 128
-VMEM = 48 * 1024 * 1024
+VMEM = 20 * 1024 * 1024
 F32, BF16 = jnp.float32, jnp.bfloat16
 
 
@@ -285,13 +285,13 @@
 
 
 def cost(us):
-    return pl.CostEstimate(flops=int(us * 1.1e9), bytes_accessed=int(us * 1e6), transcendentals=0)
+    return pl.CostEstimate(flops=int(us * 0.1e9), bytes_accessed=1024, transcendentals=0)
 
 
 def head_call(kernel, at, args, outs, heads, name, us):
-    def spec(shape):
+    def spec(shape, start=0):
         lead = len(shape) - 1
-        return pl.BlockSpec(tuple(shape[:-1]) + (HEAD,), lambda h, at: (0,) * lead + (h,))
+        return pl.BlockSpec(tuple(shape[:-1]) + (HEAD,), lambda h, at: (0,) * lead + (start + h,))
 
     return pl.pallas_call(
         kernel,
@@ -299,13 +299,13 @@
         grid_spec=pltpu.PrefetchScalarGridSpec(
             num_scalar_prefetch=1,
             grid=(heads,),
-            in_specs=[spec(a.shape) for a in args],
+            in_specs=[spec(a.shape, start) for a, start in args],
             out_specs=[spec(o.shape) for o in outs],
         ),
         compiler_params=pltpu.CompilerParams(vmem_limit_bytes=VMEM),
         cost_estimate=cost(us),
         name=name,
-    )(at, *args)
+    )(at, *(a for a, _ in args))
 
 
 def project_kernel(chunks, at, *refs):
@@ -414,65 +414,57 @@
     def head_perm(array, flip):
         return lax.ppermute(array, "head", [(i, i ^ flip) for i in range(4)])
 
-    def keep(array, lo, hi, c):
-        return lax.dynamic_slice(array, (lo, 0, x * half + c * width), (hi - lo, cols, width))
-
-    def give(array, lo, hi, c):
-        return lax.dynamic_slice(array, (lo, 0, (1 - x) * half + c * width), (hi - lo, cols, width))
-
-    w_up = seq_perm(out_weight, (0, 2), (1, 3))
-    q, kv, low, qa, qb = [], [], [], [], []
-    q_other = swap(lax.dynamic_slice(local, (0, 0, (1 - x) * half), (1, cols, half)))
-    for c in range(chunks):
-        mine, other = keep(local, 0, 1, c), q_other[:, :, c * width : (c + 1) * width]
-        q.append(jnp.concatenate([jnp.where(first, mine, other), jnp.where(first, other, mine)]))
-        going = q[c] if c == 0 else after(q[c], qa[0], qb[0])
-        qa.append(seq_perm(going, (2, 1), (3, 2)))
-        qb.append(seq_perm(going, (3, 1)))
-        source = after(local, q[0]) if c == 0 else after(local, kv[0][1])
-        kv.append((keep(local if c == 0 else source, 1, 3, c), swap(give(source, 1, 3, c))))
-        if c == 0:
-            low.append([seq_perm(half_kv, (0, 1)) for half_kv in kv[c]])
-        else:
-            low.append([seq_perm(after(jnp.concatenate(kv[c]), *low[0], w_up), (0, 1))])
+    def lanes(lo, hi, part):
+        return lax.dynamic_slice(local, (lo, 0, part * half), (hi - lo, cols, half))
+
+    mine, other = lanes(0, 1, x), swap(lanes(0, 1, 1 - x))
+    q = jnp.concatenate([jnp.where(first, mine, other), jnp.where(first, other, mine)])
+    kv_m, kv_give = lanes(1, 3, x), lanes(1, 3, 1 - x)
+    low_m = seq_perm(kv_m, (0, 1))
+    low_o = seq_perm(kv_give, (0, 1), cross=True)
+    kv_o = swap(kv_give)
+    qa = seq_perm(q, (2, 1), (3, 2))
+    qb = seq_perm(q, (3, 1))
 
     struct = jax.ShapeDtypeStruct
     partial = struct((2 * cols + lse_height(cols), width), BF16)
-    oa, ob, own, sent = [], [], [], []
+    oa, ob = [], []
+    previous = at
     for c in range(chunks):
-        at_c = at if c == 0 else after(at, own[0])
         a, b = head_call(
-            functools.partial(upper_kernel, coef, cols), at_c, [qa[c], qb[c], *kv[c], *low[c]],
+            functools.partial(upper_kernel, coef, cols), previous,
+            [(array, c * heads) for array in (qa, qb, kv_m, kv_o, low_m, low_o)],
             [partial] * 2, heads, "upper_rows", 4)
-        sent.append(a)
+        previous = after(at, a)
         oa.append(seq_perm(a, (1, 2), (2, 3)))
         ob.append(seq_perm(b, (1, 3)))
-        (mine,) = head_call(
-            functools.partial(own_kernel, coef, cols), after(at, a), [q[c], *kv[c], *low[c]], [partial],
-            heads, "own_rows", 4)
-        own.append(mine)
+    (own,) = head_call(
+        functools.partial(own_kernel, coef, cols), previous,
+        [(array, 0) for array in (q, kv_m, kv_o, low_m, low_o)],
+        [struct((partial.shape[0], half), BF16)], chunks * heads, "own_rows", 8)
 
     pairs = [[0, 2], [1, 3], [4, 6], [5, 7]]
-    w_pair = lax.all_gather(after(out_weight, low[1][0], qa[1]), "seq", axis_index_groups=pairs)
-    w_down = seq_perm(after(out_weight, qa[1], qb[1]), (2, 0), (3, 1))
+    w_pair = lax.all_gather(after(out_weight, low_m, low_o), "seq", axis_index_groups=pairs)
+    w_up = seq_perm(after(out_weight, low_m, low_o), (0, 2), (1, 3))
+    w_down = seq_perm(after(out_weight, qa, qb), (2, 0), (3, 1))
 
     def merged(c, earlier):
         (a,) = head_call(
-            functools.partial(merge_kernel, cols), after(at, earlier), [own[c], oa[c], ob[c]],
+            functools.partial(merge_kernel, cols), after(at, earlier), [(own, c * heads), (oa[c], 0), (ob[c], 0)],
             [struct((2, cols, width), BF16)], heads, "merge", 2)
         return a, swap(a)
 
-    first_half = merged(0, sent[1])
-    w_far = jnp.where(z >= 2, w_up, after(w_down, first_half[0], own[1]))
-    w_far_pair = lax.all_gather(w_far, "seq", axis_index_groups=pairs)
+    first_half = merged(0, previous)
+    w_far = jnp.where(z >= 2, w_up, after(w_down, first_half[0], own))
     near, far = map(list, zip(first_half, merged(1, w_far)))
+    w_other = seq_perm(w_far, (0, 1), (1, 0), (2, 3), (3, 2))
 
     parts = []
     turn = at
     groups = [
         (w_pair, 2, lambda s, at: s),
         (w_far[None], 1, lambda s, at: 0),
-        (w_far_pair, 1, lambda s, at: 1 - at[1] % 2),
+        (w_other[None], 1, lambda s, at: 0),
     ]
     for weight, count, pick in groups:
         send, kept = project(turn, near, far, weight, count, pick)

time: 252 us -> 237 us (0.940)
  local copies, waits for them, and re-layouts: 23 us -> 7.02 us
  waiting for transfers between devices: 92.9 us -> 99.7 us
  other arithmetic: 6.51 us -> 3.87 us
    ppermute x21 -> x18, waiting for transfers between devices: 65.2 us -> 84.1 us  [seq_perm(): return lax.ppermute(array, 'seq', pairs)]
    unnamed x70 -> x6, local copies, waits for them, and re-layouts: 18.3 us -> 2.39 us
    all_gather x2 -> x1, waiting for transfers between devices: 10.9 us -> 0.01 us  [body_eight(): lax.all_gather(after(out_weight, low_m, low_o), 'seq', axis_index_groups=...]
    ppermute x6, waiting for transfers between devices: 8.51 us -> 5.74 us  [head_perm(): return lax.ppermute(array, 'head', [(i, i ^ flip) for i in range(4)])]
    ppermute x21 -> x18, starting transfers between devices: 61.2 us -> 59.8 us  [seq_perm(): return lax.ppermute(array, 'seq', pairs)]
    pallas_call x6 -> x5, Pallas kernels: 32.3 us -> 31.6 us  [head_call(): pl.pallas_call(kernel, out_shape=outs, grid_spec=pltpu.PrefetchScalarGrid...]
  transfers between devices with their start and end apart: 32 -> 28, of which waited for: 17 -> 14; matrix products, arithmetic and copies ran while one was open for 3% -> 3% of each run, Pallas kernels for 15% -> 15%
where the time goes in v5:
time: 237 us; the launch traced here: 235 us
  waiting for transfers between devices  99.7 us (42%)
  starting transfers between devices  69.1 us (29%)
  Pallas kernels  42.1 us (18%)
  between operations  13.6 us (6%)
  local copies, waits for them, and re-layouts  7.02 us (3%)
  other arithmetic  3.87 us (2%)
    ppermute x18, waiting for transfers between devices, seq_perm(): return lax.ppermute(array, 'seq', pairs)  84.1 us
    ppermute x18, starting transfers between devices, seq_perm(): return lax.ppermute(array, 'seq', pairs)  59.8 us
    pallas_call x5, Pallas kernels, head_call(): pl.pallas_call(kernel, out_shape=outs, grid_spec=pltpu.PrefetchScalarGrid...  31.6 us
    ppermute x3, waiting for transfers between devices, body_eight(): from_xy = lax.ppermute(to_xy, ('seq', 'head'), diagonal)  9.83 us
    pallas_call x3, Pallas kernels, project(): pl.pallas_call(functools.partial(project_kernel, len(near)), out_shape=[o...  6.66 us
    ppermute x6, waiting for transfers between devices, head_perm(): return lax.ppermute(array, 'head', [(i, i ^ flip) for i in range(4)])  5.74 us
  transfers between devices with their start and end apart: 28, of which 14 were waited for; matrix products, arithmetic and copies ran while one was open for 3% of the time, Pallas kernels for 15%

profile of v5, /device:TPU:16, one launch (start us, length us, event | category | flops | bytes accessed | tf_op | source)
XLA Modules:
  0.0 235.3 jit_solution(9235322110904507957)
XLA Ops:
  6.5 1.9 dynamic-slice_bitcast_fusion.2
  9.9 2.8 %dynamic-slice_bitcast_fusion = (bf16[2,512,512]{2,1,0:T(8,128)(2,1)}, bf16[2,512,512]{2,1,0:T(8,128)(2,1)S(1)}) fusion(bf16[3,1,512,1024]{3,2,1,0:T(8,128)(2,1)} %param.2, s32[]{:T(128)S(6)} %select_n.52, s32[]{:T(128)S(6)} %select_n.51), kind=kLoop, calls=%fused_computation.1 | loop fusion | bytes 4194312 | tf_op jit(solution)/shard_map/dynamic_slice | solution.py:418
  14.1 8.3 %collective-permute-done = bf16[1,512,512]{2,1,0:T(8,128)(2,1)} collective-permute-done((bf16[1,512,512]{2,1,0:T(8,128)(2,1)}, bf16[1,512,512]{2,1,0:T(8,128)(2,1)}, u32[]{:S(2)}, u32[]{:S(2)}) %collective-permute-start) | collective-permute-done | bytes 524320 | tf_op jit(solution)/shard_map/ppermute | solution.py:409
  24.8 2.3 collective-permute-start.1
  27.2 1.7 collective-permute-start.2
  30.4 22.8 %collective-permute-done.1.qa = bf16[2,512,512]{2,1,0:T(8,128)(2,1)} collective-permute-done((bf16[2,512,512]{2,1,0:T(8,128)(2,1)}, bf16[2,512,512]{2,1,0:T(8,128)(2,1)}, u32[]{:S(2)}, u32[]{:S(2)}) %collective-permute-start.1) | collective-permute-done | bytes 1048608 | tf_op jit(solution)/shard_map/ppermute | solution.py:409
  53.1 11.0 %collective-permute-start.9 = (bf16[1024,512]{1,0:T(8,128)(2,1)}, bf16[1024,512]{1,0:T(8,128)(2,1)}, u32[]{:S(2)}, u32[]{:S(2)}) collective-permute-start(bf16[1024,512]{1,0:T(8,128)(2,1)} %param.3), channel_id=1, source_target_pairs={{16,0},{20,4},{24,8},{28,12},{17,1},{21,5},{25,9},{29,13},{18,2},{... | collective-permute-start | bytes 3145736 | tf_op jit(solution)/shard_map/ppermute | solution.py:409
  65.6 7.3 %upper_rows.2 = (bf16[1072,256]{1,0:T(8,128)(2,1)S(1)}, bf16[1072,256]{1,0:T(8,128)(2,1)}) custom-call(s32[4]{0:T(128)S(1)} %pad_add_fusion.at, bf16[2,512,512]{2,1,0:T(8,128)(2,1)} %collective-permute-done.1.qa, bf16[2,512,512]{2,1,0:T(8,128)(2,1)} %collective-permute-done.2.qb, bf16[2,512,512]{2,1,0:T(8,128)(2,1)S(1)} %get-tuple-element.70.kv_m, ...), custom_call_target="tpu_custom_call" | custom-call | flops 400000000 | bytes 1024 | tf_op jit(solution)/shard_map/upper_rows/pallas_call | solution.py:296
  72.9 21.3 %collective-permute-start.6 = (bf16[1072,256]{1,0:T(8,128)(2,1)S(1)}, bf16[1072,256]{1,0:T(8,128)(2,1)S(1)}, u32[]{:S(2)}, u32[]{:S(2)}) collective-permute-start(bf16[1072,256]{1,0:T(8,128)(2,1)S(1)} %get-tuple-element.36), channel_id=1, source_target_pairs={{8,16},{12,20},{16,24},{20,28},{9,17},{13,21},{17,25},{21,29},{10,... | collective-permute-start | bytes 1646600 | tf_op jit(solution)/shard_map/ppermute | solution.py:409
  95.7 7.3 %upper_rows.3 = (bf16[1072,256]{1,0:T(8,128)(2,1)}, bf16[1072,256]{1,0:T(8,128)(2,1)}) custom-call(s32[4]{0:T(128)S(1)} %pad_add_fusion.at, bf16[2,512,512]{2,1,0:T(8,128)(2,1)} %collective-permute-done.1.qa, bf16[2,512,512]{2,1,0:T(8,128)(2,1)} %collective-permute-done.2.qb, bf16[2,512,512]{2,1,0:T(8,128)(2,1)S(1)} %get-tuple-element.70.kv_m, ...), custom_call_target="tpu_custom_call" | custom-call | flops 400000000 | bytes 1024 | tf_op jit(solution)/shard_map/upper_rows/pallas_call | solution.py:296
  103.0 1.9 collective-permute-start.10
  104.9 29.2 %collective-permute-done.6.oa = bf16[1072,256]{1,0:T(8,128)(2,1)S(1)} collective-permute-done((bf16[1072,256]{1,0:T(8,128)(2,1)S(1)}, bf16[1072,256]{1,0:T(8,128)(2,1)S(1)}, u32[]{:S(2)}, u32[]{:S(2)}) %collective-permute-start.6) | collective-permute-done | bytes 548896 | tf_op jit(solution)/shard_map/ppermute | solution.py:409
  136.4 10.6 %own_rows.1.own = bf16[1072,512]{1,0:T(8,128)(2,1)S(1)} custom-call(s32[4]{0:T(128)S(1)} %pad_add_fusion.at, bf16[2,512,512]{2,1,0:T(8,128)(2,1)} %pad_maximum_fusion.q, bf16[2,512,512]{2,1,0:T(8,128)(2,1)S(1)} %get-tuple-element.70.kv_m, bf16[2,512,512]{2,1,0:T(8,128)(2,1)} %collective-permute-done.3.kv_o, ...), custom_call_target="tpu_custom_call" | custom-call | flops 800000000 | bytes 1024 | tf_op jit(solution)/shard_map/own_rows/pallas_call | solution.py:296
  147.0 3.1 %merge.2 = bf16[2,512,256]{2,1,0:T(8,128)(2,1)S(1)} custom-call(s32[4]{0:T(128)S(1)} %pad_add_fusion.at, bf16[1072,512]{1,0:T(8,128)(2,1)S(1)} %own_rows.1.own, bf16[1072,256]{1,0:T(8,128)(2,1)S(1)} %copy-done.2, bf16[1072,256]{1,0:T(8,128)(2,1)} %collective-permute-done.7.ob), custom_call_target="tpu_custom_call" | custom-call | flops 200000000 | bytes 1024 | tf_op jit(solution)/shard_map/merge/pallas_call | solution.py:296
  152.1 5.8 %collective-permute-done.10.oa = bf16[1072,256]{1,0:T(8,128)(2,1)} collective-permute-done((bf16[1072,256]{1,0:T(8,128)(2,1)}, bf16[1072,256]{1,0:T(8,128)(2,1)}, u32[]{:S(2)}, u32[]{:S(2)}) %collective-permute-start.10) | collective-permute-done | bytes 548896 | tf_op jit(solution)/shard_map/ppermute | solution.py:409
  157.8 3.2 %merge.3 = bf16[2,512,256]{2,1,0:T(8,128)(2,1)S(1)} custom-call(s32[4]{0:T(128)S(1)} %pad_add_fusion.at, bf16[1072,512]{1,0:T(8,128)(2,1)S(1)} %own_rows.1.own, bf16[1072,256]{1,0:T(8,128)(2,1)} %collective-permute-done.10.oa, bf16[1072,256]{1,0:T(8,128)(2,1)} %collective-permute-done.11.ob), custom_call_target="tpu_custom_call" | custom-call | flops 200000000 | bytes 1024 | tf_op jit(solution)/shard_map/merge/pallas_call | solution.py:296
  162.5 8.2 %collective-permute-done.13 = bf16[2,512,256]{2,1,0:T(8,128)(2,1)S(1)} collective-permute-done((bf16[2,512,256]{2,1,0:T(8,128)(2,1)S(1)}, bf16[2,512,256]{2,1,0:T(8,128)(2,1)S(1)}, u32[]{:S(2)}, u32[]{:S(2)}) %collective-permute-start.13) | collective-permute-done | bytes 524320 | tf_op jit(solution)/shard_map/ppermute | solution.py:409
  170.6 1.6 copy-done
  172.2 3.1 %project.3 = (bf16[2,2,2,128,512]{4,3,2,1,0:T(8,128)(2,1)S(1)}, bf16[2,2,2,128,512]{4,3,2,1,0:T(8,128)(2,1)S(1)}) custom-call(s32[4]{0:T(128)S(1)} %pad_add_fusion.at, bf16[2,2,2,128,256]{4,3,2,1,0:T(8,128)(2,1)S(1)} %bitcast.21, bf16[2,2,2,128,256]{4,3,2,1,0:T(8,128)(2,1)S(1)} %bitcast.24, bf16[2,2,2,128,256]{4,3,2,1,0:T(8,128)(2,1)S(1)} %bitcast.27, ...), custom_call_target="tpu_custom_call" | custom-call | flops 400000000 | bytes 1024 | tf_op jit(solution)/shard_map/project/pallas_call | solution.py:337
  175.4 10.1 %collective-permute-start.22 = (bf16[1024,512]{1,0:T(8,128)(2,1)S(1)}, bf16[1024,512]{1,0:T(8,128)(2,1)S(1)}, u32[]{:S(2)}, u32[]{:S(2)}) collective-permute-start(bf16[1024,512]{1,0:T(8,128)(2,1)S(1)} %broadcast_select_fusion), channel_id=1, source_target_pairs={{0,8},{4,12},{8,0},{12,4},{16,24},{20,28},{24,16},{28,20},{1,9},{5... | collective-permute-start | bytes 3145736 | tf_op jit(solution)/shard_map/ppermute | solution.py:409
  186.3 1.8 project.4
  190.3 1.5 collective-permute-start.17
  192.5 4.4 %collective-permute-done.15.refs_1_ = bf16[2,128,512]{2,1,0:T(8,128)(2,1)S(1)} collective-permute-done((bf16[2,128,512]{2,1,0:T(8,128)(2,1)S(1)}, bf16[2,128,512]{2,1,0:T(8,128)(2,1)S(1)}, u32[]{:S(2)}, u32[]{:S(2)}) %collective-permute-start.15) | collective-permute-done | bytes 262176 | tf_op jit(solution)/shard_map/ppermute | solution.py:415
  196.9 2.0 collective-permute-done.16.refs_2_
  198.9 4.8 %collective-permute-done.17.refs_3_ = bf16[2,128,512]{2,1,0:T(8,128)(2,1)S(1)} collective-permute-done((bf16[2,128,512]{2,1,0:T(8,128)(2,1)S(1)}, bf16[2,128,512]{2,1,0:T(8,128)(2,1)S(1)}, u32[]{:S(2)}, u32[]{:S(2)}) %collective-permute-start.17) | collective-permute-done | bytes 262176 | tf_op jit(solution)/shard_map/ppermute | solution.py:476
  203.7 5.6 %collective-permute-done.22 = bf16[1024,512]{1,0:T(8,128)(2,1)S(1)} collective-permute-done((bf16[1024,512]{1,0:T(8,128)(2,1)S(1)}, bf16[1024,512]{1,0:T(8,128)(2,1)S(1)}, u32[]{:S(2)}, u32[]{:S(2)}) %collective-permute-start.22) | collective-permute-done | bytes 1048608 | tf_op jit(solution)/shard_map/ppermute | solution.py:409
  209.3 1.8 project.5
  213.2 1.5 collective-permute-start.21
  217.4 1.5 collective-permute-start.26
  219.0 2.9 %collective-permute-done.21.refs_7_ = bf16[1,128,512]{2,1,0:T(8,128)(2,1)S(1)} collective-permute-done((bf16[1,128,512]{2,1,0:T(8,128)(2,1)S(1)}, bf16[1,128,512]{2,1,0:T(8,128)(2,1)S(1)}, u32[]{:S(2)}, u32[]{:S(2)}) %collective-permute-start.21) | collective-permute-done | bytes 131104 | tf_op jit(solution)/shard_map/ppermute | solution.py:476
  224.6 2.1 collective-permute-done.26.refs_11_
  226.7 1.7 place.1
  (49 shorter events, 26.6 us)
Async XLA Ops:
  6.5 156.0 %all-gather.3.cloned.1.call-start = ((), (), s32[]{:S(2)}) async-start(), calls=%async_computation | async-start | bytes 3145728 | tf_op jit(solution)/shard_map/all_gather | solution.py:447
  8.4 14.0 %collective-permute-start = (bf16[1,512,512]{2,1,0:T(8,128)(2,1)}, bf16[1,512,512]{2,1,0:T(8,128)(2,1)}, u32[]{:S(2)}, u32[]{:S(2)}) collective-permute-start(bf16[1,512,512]{2,1,0:T(8,128)(2,1)} %dynamic-slice_bitcast_fusion.2), channel_id=1, source_target_pairs={{0,4},{4,0},{8,12},{12,8},{16,20},{20,16},{24,28},{28,24},{1,5},{5... | collective-permute-start | bytes 1572872 | tf_op jit(solution)/shard_map/ppermute | solution.py:409
  12.7 17.7 %collective-permute-start.4 = (bf16[2,512,512]{2,1,0:T(8,128)(2,1)S(1)}, bf16[2,512,512]{2,1,0:T(8,128)(2,1)S(1)}, u32[]{:S(2)}, u32[]{:S(2)}) collective-permute-start(bf16[2,512,512]{2,1,0:T(8,128)(2,1)S(1)} %get-tuple-element.70.kv_m), channel_id=1, source_target_pairs={{0,8},{4,12},{1,9},{5,13},{2,10},{6,14},{3,11},{7,15}} | collective-permute-start | bytes 3145736 | tf_op jit(solution)/shard_map/ppermute | solution.py:409
  13.4 17.0 %collective-permute-start.5 = (bf16[2,512,512]{2,1,0:T(8,128)(2,1)}, bf16[2,512,512]{2,1,0:T(8,128)(2,1)S(1)}, u32[]{:S(2)}, u32[]{:S(2)}) collective-permute-start(bf16[2,512,512]{2,1,0:T(8,128)(2,1)} %get-tuple-element.69), channel_id=1, source_target_pairs={{0,12},{4,8},{1,13},{5,9},{2,14},{6,10},{3,15},{7,11}} | collective-permute-start | bytes 3145736 | tf_op jit(solution)/shard_map/ppermute | solution.py:409
  24.8 28.3 %collective-permute-start.1 = (bf16[2,512,512]{2,1,0:T(8,128)(2,1)}, bf16[2,512,512]{2,1,0:T(8,128)(2,1)}, u32[]{:S(2)}, u32[]{:S(2)}) collective-permute-start(bf16[2,512,512]{2,1,0:T(8,128)(2,1)} %pad_maximum_fusion.q), channel_id=1, source_target_pairs={{16,8},{20,12},{24,16},{28,20},{17,9},{21,13},{25,17},{29,21},{18,... | collective-permute-start | bytes 3145736 | tf_op jit(solution)/shard_map/ppermute | solution.py:409
  27.2 25.9 %collective-permute-start.2 = (bf16[2,512,512]{2,1,0:T(8,128)(2,1)}, bf16[2,512,512]{2,1,0:T(8,128)(2,1)}, u32[]{:S(2)}, u32[]{:S(2)}) collective-permute-start(bf16[2,512,512]{2,1,0:T(8,128)(2,1)} %pad_maximum_fusion.q), channel_id=1, source_target_pairs={{24,8},{28,12},{25,9},{29,13},{26,10},{30,14},{27,11},{31,15}} | collective-permute-start | bytes 3145736 | tf_op jit(solution)/shard_map/ppermute | solution.py:409
  28.8 36.7 %collective-permute-start.3 = (bf16[2,512,512]{2,1,0:T(8,128)(2,1)}, bf16[2,512,512]{2,1,0:T(8,128)(2,1)}, u32[]{:S(2)}, u32[]{:S(2)}) collective-permute-start(bf16[2,512,512]{2,1,0:T(8,128)(2,1)} %get-tuple-element.69), channel_id=1, source_target_pairs={{0,4},{4,0},{8,12},{12,8},{16,20},{20,16},{24,28},{28,24},{1,5},{5... | collective-permute-start | bytes 3145736 | tf_op jit(solution)/shard_map/ppermute | solution.py:409
  53.1 97.6 %collective-permute-start.9 = (bf16[1024,512]{1,0:T(8,128)(2,1)}, bf16[1024,512]{1,0:T(8,128)(2,1)}, u32[]{:S(2)}, u32[]{:S(2)}) collective-permute-start(bf16[1024,512]{1,0:T(8,128)(2,1)} %param.3), channel_id=1, source_target_pairs={{16,0},{20,4},{24,8},{28,12},{17,1},{21,5},{25,9},{29,13},{18,2},{... | collective-permute-start | bytes 3145736 | tf_op jit(solution)/shard_map/ppermute | solution.py:409
  64.2 86.5 %collective-permute-start.8 = (bf16[1024,512]{1,0:T(8,128)(2,1)}, bf16[1024,512]{1,0:T(8,128)(2,1)}, u32[]{:S(2)}, u32[]{:S(2)}) collective-permute-start(bf16[1024,512]{1,0:T(8,128)(2,1)} %param.3), channel_id=1, source_target_pairs={{0,16},{4,20},{8,24},{12,28},{1,17},{5,21},{9,25},{13,29},{2,18},{... | collective-permute-start | bytes 3145736 | tf_op jit(solution)/shard_map/ppermute | solution.py:409
  72.9 61.3 %collective-permute-start.6 = (bf16[1072,256]{1,0:T(8,128)(2,1)S(1)}, bf16[1072,256]{1,0:T(8,128)(2,1)S(1)}, u32[]{:S(2)}, u32[]{:S(2)}) collective-permute-start(bf16[1072,256]{1,0:T(8,128)(2,1)S(1)} %get-tuple-element.36), channel_id=1, source_target_pairs={{8,16},{12,20},{16,24},{20,28},{9,17},{13,21},{17,25},{21,29},{10,... | collective-permute-start | bytes 1646600 | tf_op jit(solution)/shard_map/ppermute | solution.py:409
  94.2 52.8 %collective-permute-start.7 = (bf16[1072,256]{1,0:T(8,128)(2,1)}, bf16[1072,256]{1,0:T(8,128)(2,1)}, u32[]{:S(2)}, u32[]{:S(2)}) collective-permute-start(bf16[1072,256]{1,0:T(8,128)(2,1)} %get-tuple-element.41), channel_id=1, source_target_pairs={{8,24},{12,28},{9,25},{13,29},{10,26},{14,30},{11,27},{15,31}} | collective-permute-start | bytes 1646600 | tf_op jit(solution)/shard_map/ppermute | solution.py:409
  103.0 54.8 %collective-permute-start.10 = (bf16[1072,256]{1,0:T(8,128)(2,1)}, bf16[1072,256]{1,0:T(8,128)(2,1)}, u32[]{:S(2)}, u32[]{:S(2)}) collective-permute-start(bf16[1072,256]{1,0:T(8,128)(2,1)} %get-tuple-element.38), channel_id=1, source_target_pairs={{8,16},{12,20},{16,24},{20,28},{9,17},{13,21},{17,25},{21,29},{10,... | collective-permute-start | bytes 1646600 | tf_op jit(solution)/shard_map/ppermute | solution.py:409
  134.1 0.8 copy-start.1
  134.9 22.9 %collective-permute-start.11 = (bf16[1072,256]{1,0:T(8,128)(2,1)}, bf16[1072,256]{1,0:T(8,128)(2,1)}, u32[]{:S(2)}, u32[]{:S(2)}) collective-permute-start(bf16[1072,256]{1,0:T(8,128)(2,1)} %get-tuple-element.46), channel_id=1, source_target_pairs={{8,24},{12,28},{9,25},{13,29},{10,26},{14,30},{11,27},{15,31}} | collective-permute-start | bytes 1646600 | tf_op jit(solution)/shard_map/ppermute | solution.py:409
  136.4 10.6 %copy-start.2 = (bf16[1072,256]{1,0:T(8,128)(2,1)S(1)}, bf16[1072,256]{1,0:T(8,128)(2,1)}, u32[]{:S(2)}) copy-start(bf16[1072,256]{1,0:T(8,128)(2,1)} %copy-done.1) | copy-start | bytes 1646596
  150.2 12.3 %collective-permute-start.12 = (bf16[2,512,256]{2,1,0:T(8,128)(2,1)S(1)}, bf16[2,512,256]{2,1,0:T(8,128)(2,1)S(1)}, u32[]{:S(2)}, u32[]{:S(2)}) collective-permute-start(bf16[2,512,256]{2,1,0:T(8,128)(2,1)S(1)} %merge.2), channel_id=1, source_target_pairs={{0,4},{4,0},{8,12},{12,8},{16,20},{20,16},{24,28},{28,24},{1,5},{5... | collective-permute-start | bytes 1572872 | tf_op jit(solution)/shard_map/ppermute | solution.py:409
  161.0 9.6 %collective-permute-start.13 = (bf16[2,512,256]{2,1,0:T(8,128)(2,1)S(1)}, bf16[2,512,256]{2,1,0:T(8,128)(2,1)S(1)}, u32[]{:S(2)}, u32[]{:S(2)}) collective-permute-start(bf16[2,512,256]{2,1,0:T(8,128)(2,1)S(1)} %merge.3), channel_id=1, source_target_pairs={{0,4},{4,0},{8,12},{12,8},{16,20},{20,16},{24,28},{28,24},{1,5},{5... | collective-permute-start | bytes 1572872 | tf_op jit(solution)/shard_map/ppermute | solution.py:409
  170.6 1.6 copy-start
  175.3 10.2 %collective-permute-start.14 = (bf16[2,2,2,128,512]{4,3,2,1,0:T(8,128)(2,1)S(1)}, bf16[2,2,2,128,512]{4,3,2,1,0:T(8,128)(2,1)S(1)}, u32[]{:S(2)}, u32[]{:S(2)}) collective-permute-start(bf16[2,2,2,128,512]{4,3,2,1,0:T(8,128)(2,1)S(1)} %get-tuple-element.48), channel_id=1, source_target_pairs={{0,1},{1,0},{2,3},{3,2},{4,5},{5,4},{6,7},{7,6},{8,9},{9,8},{10,11... | collective-permute-start | bytes 3145736 | tf_op jit(solution)/shard_map/ppermute | solution.py:415
  175.4 33.9 %collective-permute-start.22 = (bf16[1024,512]{1,0:T(8,128)(2,1)S(1)}, bf16[1024,512]{1,0:T(8,128)(2,1)S(1)}, u32[]{:S(2)}, u32[]{:S(2)}) collective-permute-start(bf16[1024,512]{1,0:T(8,128)(2,1)S(1)} %broadcast_select_fusion), channel_id=1, source_target_pairs={{0,8},{4,12},{8,0},{12,4},{16,24},{20,28},{24,16},{28,20},{1,9},{5... | collective-permute-start | bytes 3145736 | tf_op jit(solution)/shard_map/ppermute | solution.py:409
  188.1 3.7 %collective-permute-start.18 = (bf16[1,2,2,128,512]{4,3,2,1,0:T(8,128)(2,1)S(1)}, bf16[1,2,2,128,512]{4,3,2,1,0:T(8,128)(2,1)S(1)}, u32[]{:S(2)}, u32[]{:S(2)}) collective-permute-start(bf16[1,2,2,128,512]{4,3,2,1,0:T(8,128)(2,1)S(1)} %get-tuple-element.55), channel_id=1, source_target_pairs={{0,1},{1,0},{2,3},{3,2},{4,5},{5,4},{6,7},{7,6},{8,9},{9,8},{10,11... | collective-permute-start | bytes 1572872 | tf_op jit(solution)/shard_map/ppermute | solution.py:415
  188.4 8.6 %collective-permute-start.15 = (bf16[2,128,512]{2,1,0:T(8,128)(2,1)S(1)}, bf16[2,128,512]{2,1,0:T(8,128)(2,1)S(1)}, u32[]{:S(2)}, u32[]{:S(2)}) collective-permute-start(bf16[2,128,512]{2,1,0:T(8,128)(2,1)S(1)} %get-tuple-element.50), channel_id=1, source_target_pairs={{0,2},{1,3},{2,0},{3,1},{4,6},{5,7},{6,4},{7,5},{8,10},{9,11},{10,... | collective-permute-start | bytes 786440 | tf_op jit(solution)/shard_map/ppermute | solution.py:415
  189.8 9.2 %collective-permute-start.16 = (bf16[2,128,512]{2,1,0:T(8,128)(2,1)S(1)}, bf16[2,128,512]{2,1,0:T(8,128)(2,1)S(1)}, u32[]{:S(2)}, u32[]{:S(2)}) collective-permute-start(bf16[2,128,512]{2,1,0:T(8,128)(2,1)S(1)} %get-tuple-element.51), channel_id=1, source_target_pairs={{0,4},{4,0},{8,12},{12,8},{16,20},{20,16},{24,28},{28,24},{1,5},{5... | collective-permute-start | bytes 786440 | tf_op jit(solution)/shard_map/ppermute | solution.py:409
  190.3 13.4 %collective-permute-start.17 = (bf16[2,128,512]{2,1,0:T(8,128)(2,1)S(1)}, bf16[2,128,512]{2,1,0:T(8,128)(2,1)S(1)}, u32[]{:S(2)}, u32[]{:S(2)}) collective-permute-start(bf16[2,128,512]{2,1,0:T(8,128)(2,1)S(1)} %get-tuple-element.52), channel_id=1, source_target_pairs={{0,6},{1,7},{2,4},{3,5},{4,2},{5,3},{6,0},{7,1},{8,14},{9,15},{10,... | collective-permute-start | bytes 786440 | tf_op jit(solution)/shard_map/ppermute | solution.py:476
  211.1 3.6 %collective-permute-start.23 = (bf16[1,2,2,128,512]{4,3,2,1,0:T(8,128)(2,1)S(1)}, bf16[1,2,2,128,512]{4,3,2,1,0:T(8,128)(2,1)S(1)}, u32[]{:S(2)}, u32[]{:S(2)}) collective-permute-start(bf16[1,2,2,128,512]{4,3,2,1,0:T(8,128)(2,1)S(1)} %get-tuple-element.62), channel_id=1, source_target_pairs={{0,1},{1,0},{2,3},{3,2},{4,5},{5,4},{6,7},{7,6},{8,9},{9,8},{10,11... | collective-permute-start | bytes 1572872 | tf_op jit(solution)/shard_map/ppermute | solution.py:415
  211.2 6.3 %collective-permute-start.19 = (bf16[1,128,512]{2,1,0:T(8,128)(2,1)S(1)}, bf16[1,128,512]{2,1,0:T(8,128)(2,1)S(1)}, u32[]{:S(2)}, u32[]{:S(2)}) collective-permute-start(bf16[1,128,512]{2,1,0:T(8,128)(2,1)S(1)} %get-tuple-element.57), channel_id=1, source_target_pairs={{0,2},{1,3},{2,0},{3,1},{4,6},{5,7},{6,4},{7,5},{8,10},{9,11},{10,... | collective-permute-start | bytes 393224 | tf_op jit(solution)/shard_map/ppermute | solution.py:415
  212.6 6.3 %collective-permute-start.20 = (bf16[1,128,512]{2,1,0:T(8,128)(2,1)S(1)}, bf16[1,128,512]{2,1,0:T(8,128)(2,1)S(1)}, u32[]{:S(2)}, u32[]{:S(2)}) collective-permute-start(bf16[1,128,512]{2,1,0:T(8,128)(2,1)S(1)} %get-tuple-element.58), channel_id=1, source_target_pairs={{0,4},{4,0},{8,12},{12,8},{16,20},{20,16},{24,28},{28,24},{1,5},{5... | collective-permute-start | bytes 393224 | tf_op jit(solution)/shard_map/ppermute | solution.py:409
  213.2 8.7 %collective-permute-start.21 = (bf16[1,128,512]{2,1,0:T(8,128)(2,1)S(1)}, bf16[1,128,512]{2,1,0:T(8,128)(2,1)S(1)}, u32[]{:S(2)}, u32[]{:S(2)}) collective-permute-start(bf16[1,128,512]{2,1,0:T(8,128)(2,1)S(1)} %get-tuple-element.59), channel_id=1, source_target_pairs={{0,6},{1,7},{2,4},{3,5},{4,2},{5,3},{6,0},{7,1},{8,14},{9,15},{10,... | collective-permute-start | bytes 393224 | tf_op jit(solution)/shard_map/ppermute | solution.py:476
  215.4 7.8 %collective-permute-start.24 = (bf16[1,128,512]{2,1,0:T(8,128)(2,1)S(1)}, bf16[1,128,512]{2,1,0:T(8,128)(2,1)S(1)}, u32[]{:S(2)}, u32[]{:S(2)}) collective-permute-start(bf16[1,128,512]{2,1,0:T(8,128)(2,1)S(1)} %get-tuple-element.64), channel_id=1, source_target_pairs={{0,2},{1,3},{2,0},{3,1},{4,6},{5,7},{6,4},{7,5},{8,10},{9,11},{10,... | collective-permute-start | bytes 393224 | tf_op jit(solution)/shard_map/ppermute | solution.py:415
  216.9 7.8 %collective-permute-start.25 = (bf16[1,128,512]{2,1,0:T(8,128)(2,1)S(1)}, bf16[1,128,512]{2,1,0:T(8,128)(2,1)S(1)}, u32[]{:S(2)}, u32[]{:S(2)}) collective-permute-start(bf16[1,128,512]{2,1,0:T(8,128)(2,1)S(1)} %get-tuple-element.65), channel_id=1, source_target_pairs={{0,4},{4,0},{8,12},{12,8},{16,20},{20,16},{24,28},{28,24},{1,5},{5... | collective-permute-start | bytes 393224 | tf_op jit(solution)/shard_map/ppermute | solution.py:409
  217.4 9.3 %collective-permute-start.26 = (bf16[1,128,512]{2,1,0:T(8,128)(2,1)S(1)}, bf16[1,128,512]{2,1,0:T(8,128)(2,1)S(1)}, u32[]{:S(2)}, u32[]{:S(2)}) collective-permute-start(bf16[1,128,512]{2,1,0:T(8,128)(2,1)S(1)} %get-tuple-element.66), channel_id=1, source_target_pairs={{0,6},{1,7},{2,4},{3,5},{4,2},{5,3},{6,0},{7,1},{8,14},{9,15},{10,... | collective-permute-start | bytes 393224 | tf_op jit(solution)/shard_map/ppermute | solution.py:476
Sparse Core Ops, SparseCore 0:
  30.5 89.7 all-gather.2

commit v6 on v5

--- a/solution.py
+++ b/solution.py
@@ -10,7 +10,7 @@
 LOG2E = 1.4426950408889634
 NEG = -1e30
 QB = 128
-VMEM = 20 * 1024 * 1024
+VMEM = 24 * 1024 * 1024
 F32, BF16 = jnp.float32, jnp.bfloat16
 
 
@@ -201,7 +201,7 @@
     return [ref[i] for ref in refs for i in range(ref.shape[0])]
 
 
-def own_kernel(coef, cols, at, q, kv_m, kv_o, *refs):
+def own_kernel(coef, cols, at, q_m, q_o, kv_m, kv_o, *refs):
     x, z = at[0], at[1]
     below = z == 1
     block = 256
@@ -217,6 +217,7 @@
     lk_e, lk_o = jnp.where(first, m_k, o_k), jnp.where(first, o_k, m_k)
     lv_e, lv_o = jnp.where(first, m_v, o_v), jnp.where(first, o_v, m_v)
     lv_o1 = with_ones(lv_o)
+    q_e, q_o = jnp.where(first, q_m[0], q_o[0]), jnp.where(first, q_o[0], q_m[0])
     evens, odds = [], []
     for part in range(cols // block):
         a, b = part * block, (part + 1) * block
@@ -228,8 +229,8 @@
             blocks = [(k[a:b], v[a:b], tri)]
             return blocks if part == 0 else [(k[:a], v[:a], None)] + blocks
 
-        o1, l1 = attend(q[0, mine], causal(k_e, v_e) + [(lk_o, lv_o1, below)], [col_e], coef)
-        o2, l2 = attend(q[1, mine], causal(k_o, v_o) + [(k_e, v_e, None)], [col_e, col_o], coef)
+        o1, l1 = attend(q_e[mine], causal(k_e, v_e) + [(lk_o, lv_o1, below)], [col_e], coef)
+        o2, l2 = attend(q_o[mine], causal(k_o, v_o) + [(k_e, v_e, None)], [col_e, col_o], coef)
         out[mine] = o1.astype(BF16)
         out[cols + a : cols + b] = o2.astype(BF16)
         e, o = lse_rows(l1, l2)
@@ -237,7 +238,7 @@
     put_lse(out, 2 * cols, evens, odds)
 
 
-def upper_kernel(coef, cols, at, qa, qb, kv_m, kv_o, *refs):
+def upper_kernel(coef, cols, at, qa_m, qa_o, qb_m, qb_o, kv_m, kv_o, *refs):
     x, z = at[0], at[1]
     below = z == 1
     first = x == 0
@@ -247,6 +248,8 @@
     v_o1 = with_ones(v_o)
     *low, out_a, out_b = refs
     lows = stacked(low)
+    qa = jnp.where(first, qa_m[0], qa_o[0]), jnp.where(first, qa_o[0], qa_m[0])
+    qb = jnp.where(first, qb_m[0], qb_o[0]), jnp.where(first, qb_o[0], qb_m[0])
     rows_a, rows_b = ([], []), ([], [])
     for index in range(cols // block):
         a, b = index * block, (index + 1) * block
@@ -259,8 +262,8 @@
             (qa, out_a, rows_a, [(k_o, v_o1, None)], [ce]),
             (qb, out_b, rows_b, [], [ce, co]),
         ):
-            o1, l1 = attend(q[0, mine], dense, singles + low, coef)
-            o2, l2 = attend(q[1, mine], [], [ce, co] + low, coef)
+            o1, l1 = attend(q[0][mine], dense, singles + low, coef)
+            o2, l2 = attend(q[1][mine], [], [ce, co] + low, coef)
             out[mine] = o1.astype(BF16)
             out[cols + a : cols + b] = o2.astype(BF16)
             e, o = lse_rows(l1, l2)
@@ -285,7 +288,7 @@
 
 
 def cost(us):
-    return pl.CostEstimate(flops=int(us * 0.1e9), bytes_accessed=1024, transcendentals=0)
+    return pl.CostEstimate(flops=int(us * 1e8), bytes_accessed=1024, transcendentals=0)
 
 
 def head_call(kernel, at, args, outs, heads, name, us):
@@ -311,11 +314,9 @@
 def project_kernel(chunks, at, *refs):
     x, core = at[0], at[2]
     near, far = refs[:chunks], refs[chunks : 2 * chunks]
-    weight, send, keep = refs[2 * chunks :]
-    tokens, width = near[0].shape[3:]
-    half = width * chunks
-    top = weight[0, pl.ds(pl.multiple_of(x * half, half), half)]
-    bottom = weight[0, pl.ds(pl.multiple_of((1 - x) * half, half), half)]
+    weights, send, keep = refs[2 * chunks : -2], refs[-2], refs[-1]
+    tokens = near[0].shape[3]
+    half = sum(ref.shape[4] for ref in near)
     for who, out in ((1 - core, send), (core, keep)):
 
         def rows(ref):
@@ -323,31 +324,38 @@
 
         left = jnp.concatenate([rows(ref) for ref in near], axis=1)
         right = jnp.concatenate([rows(ref) for ref in far], axis=1)
-        c = jnp.dot(left, top, preferred_element_type=F32) + jnp.dot(right, bottom, preferred_element_type=F32)
-        out[0] = c.astype(BF16).reshape(2, 2, tokens, weight.shape[2])
-
-
-def project(at, near, far, weight, count, pick):
-    _, cols, width = near[0].shape
-    shape = (2, 2, 2, cols // 4, width)
-    args = [a.reshape(shape) for a in near + far]
-    _, depth, out_width = weight.shape
-    out = jax.ShapeDtypeStruct((count, 2, 2, cols // 4, out_width), BF16)
-    out_spec = pl.BlockSpec((1,) + out.shape[1:], lambda s, at: (s, 0, 0, 0, 0))
+        for s, weight in enumerate(weights):
+            top = weight[0, pl.ds(pl.multiple_of(x * half, half), half)]
+            bottom = weight[0, pl.ds(pl.multiple_of((1 - x) * half, half), half)]
+            c = jnp.dot(left, top, preferred_element_type=F32) + jnp.dot(right, bottom, preferred_element_type=F32)
+            out[s] = c.astype(BF16).reshape(2, 2, tokens, weight.shape[2])
+
+
+def project(at, near, far, weights):
+    cols = near[0].shape[1]
+    args = [a.reshape(2, 2, 2, cols // 4, a.shape[2]) for a in near + far]
+    _, depth, out_width = weights[0][0].shape
+    out = jax.ShapeDtypeStruct((len(weights), 2, 2, cols // 4, out_width), BF16)
+
+    def weight_spec(pick):
+        return pl.BlockSpec((1, depth, out_width), lambda s, at: (pick(at), 0, 0))
+
+    def whole(shape):
+        return pl.BlockSpec(shape, lambda s, at: (0,) * len(shape))
+
     return pl.pallas_call(
         functools.partial(project_kernel, len(near)),
         out_shape=[out, out],
         grid_spec=pltpu.PrefetchScalarGridSpec(
             num_scalar_prefetch=1,
-            grid=(count,),
-            in_specs=[pl.BlockSpec(shape, lambda s, at: (0,) * 5)] * len(args)
-            + [pl.BlockSpec((1, depth, out_width), lambda s, at: (pick(s, at), 0, 0))],
-            out_specs=[out_spec, out_spec],
+            grid=(1,),
+            in_specs=[whole(a.shape) for a in args] + [weight_spec(pick) for _, pick in weights],
+            out_specs=[whole(out.shape)] * 2,
         ),
         compiler_params=pltpu.CompilerParams(vmem_limit_bytes=VMEM),
-        cost_estimate=cost(2 * count),
+        cost_estimate=cost(2 * len(weights)),
         name="project",
-    )(at, *args, weight)
+    )(at, *args, *(w for w, _ in weights))
 
 
 def whole_call(kernel, at, args, outs, name, us):
@@ -375,7 +383,7 @@
 
 def place_kernel(at, *refs):
     x, z, out = at[0], at[1], refs[-1]
-    layers = [z - z % 2, z - z % 2 + 1, (z + 2) % 4, 3 - z]
+    layers = [z, z + 1 - 2 * (z % 2), (z + 2) % 4, 3 - z]
     for stay, from_y, from_x, from_xy in zip(*(refs[i:-1:4] for i in range(4))):
         width = stay.shape[-1]
         for s in range(stay.shape[0]):
@@ -414,64 +422,69 @@
     def head_perm(array, flip):
         return lax.ppermute(array, "head", [(i, i ^ flip) for i in range(4)])
 
-    def lanes(lo, hi, part):
-        return lax.dynamic_slice(local, (lo, 0, part * half), (hi - lo, cols, half))
-
-    mine, other = lanes(0, 1, x), swap(lanes(0, 1, 1 - x))
-    q = jnp.concatenate([jnp.where(first, mine, other), jnp.where(first, other, mine)])
+    def lanes(lo, hi, part, source=local):
+        return lax.dynamic_slice(source, (lo, 0, part * half), (hi - lo, cols, half))
+
+    down, two_down = [(2, 1), (3, 2)], [(3, 1)]
+    q_m = lanes(0, 1, x)
+    q_o = swap(lanes(0, 1, 1 - x))
+    qs = [seq_perm(q_m, *down), None, seq_perm(q_m, *two_down), None]
     kv_m, kv_give = lanes(1, 3, x), lanes(1, 3, 1 - x)
-    low_m = seq_perm(kv_m, (0, 1))
-    low_o = seq_perm(kv_give, (0, 1), cross=True)
-    kv_o = swap(kv_give)
-    qa = seq_perm(q, (2, 1), (3, 2))
-    qb = seq_perm(q, (3, 1))
+    block = out_weight.reshape(kv_m.shape)
+    low_m = seq_perm(jnp.where(z == 0, kv_m, block), (0, 1), (1, 3))
+    pairs = [(i, 2 + 1 - i) for i in range(2)] + [(2 + i, i) for i in range(2)] + [(4 + i, 6 + i) for i in range(2)]
+    low_o = lax.ppermute(jnp.where(z == 0, kv_give, block), "seq", pairs)
+    low = [low_m, low_o]
+    kv_o = swap(after(kv_give, q_o))
+    qs[1], qs[3] = seq_perm(q_o, *down), seq_perm(q_o, *two_down)
+    w_second = seq_perm(after(out_weight, *qs), (0, 2))
 
     struct = jax.ShapeDtypeStruct
     partial = struct((2 * cols + lse_height(cols), width), BF16)
-    oa, ob = [], []
-    previous = at
+    oa, ob, own = [], [], []
+    turn = at
+    kvs = [kv_m, kv_o, low_m, low_o]
     for c in range(chunks):
         a, b = head_call(
-            functools.partial(upper_kernel, coef, cols), previous,
-            [(array, c * heads) for array in (qa, qb, kv_m, kv_o, low_m, low_o)],
+            functools.partial(upper_kernel, coef, cols), turn, [(a, c * heads) for a in qs + kvs],
             [partial] * 2, heads, "upper_rows", 4)
-        previous = after(at, a)
+        turn = after(at, a)
         oa.append(seq_perm(a, (1, 2), (2, 3)))
         ob.append(seq_perm(b, (1, 3)))
-    (own,) = head_call(
-        functools.partial(own_kernel, coef, cols), previous,
-        [(array, 0) for array in (q, kv_m, kv_o, low_m, low_o)],
-        [struct((partial.shape[0], half), BF16)], chunks * heads, "own_rows", 8)
-
-    pairs = [[0, 2], [1, 3], [4, 6], [5, 7]]
-    w_pair = lax.all_gather(after(out_weight, low_m, low_o), "seq", axis_index_groups=pairs)
-    w_up = seq_perm(after(out_weight, low_m, low_o), (0, 2), (1, 3))
-    w_down = seq_perm(after(out_weight, qa, qb), (2, 0), (3, 1))
+    for c in range(chunks):
+        (mine,) = head_call(
+            functools.partial(own_kernel, coef, cols), turn, [(a, c * heads) for a in [q_m, q_o] + kvs],
+            [partial], heads, "own_rows", 4)
+        own.append(mine)
+        turn = after(at, mine, w_second)
+
+    w_down = seq_perm(after(out_weight, *qs), (2, 0), (3, 1))
+    w_near = seq_perm(after(out_weight, own[0]), (0, 1), (3, 2))
+    w_near = jnp.where((z == 0) | (z == 3), low_o.reshape(out_weight.shape), w_near)
 
     def merged(c, earlier):
         (a,) = head_call(
-            functools.partial(merge_kernel, cols), after(at, earlier), [(own, c * heads), (oa[c], 0), (ob[c], 0)],
+            functools.partial(merge_kernel, cols), after(at, earlier), [(a[c], 0) for a in (own, oa, ob)],
             [struct((2, cols, width), BF16)], heads, "merge", 2)
         return a, swap(a)
 
-    first_half = merged(0, previous)
-    w_far = jnp.where(z >= 2, w_up, after(w_down, first_half[0], own))
-    near, far = map(list, zip(first_half, merged(1, w_far)))
+    first_half = merged(0, own[1])
+    w_far = jnp.where(
+        z >= 2, jnp.where(z == 2, w_second, low_m.reshape(out_weight.shape)), after(w_down, first_half[0], own[1]))
+    near, far = map(list, zip(first_half, merged(1, (w_far, first_half[1]))))
     w_other = seq_perm(w_far, (0, 1), (1, 0), (2, 3), (3, 2))
 
     parts = []
-    turn = at
-    groups = [
-        (w_pair, 2, lambda s, at: s),
-        (w_far[None], 1, lambda s, at: 0),
-        (w_other[None], 1, lambda s, at: 0),
-    ]
-    for weight, count, pick in groups:
-        send, kept = project(turn, near, far, weight, count, pick)
+    turn = after(at, w_other)
+    for weights in (
+        [out_weight, w_near],
+        [w_far, w_other],
+    ):
+        send, kept = project(turn, near, far, [(w[None], lambda at: 0) for w in weights])
         got = head_perm(send, 1)
-        piece = struct((count,) + send.shape[3:], BF16)
+        piece = struct(send.shape[:1] + send.shape[3:], BF16)
         stay, to_y, to_x, to_xy = whole_call(split_kernel, at, [kept, got], [piece] * 4, "split", 2)
-        turn = after(at, stay, *parts)
+        turn = after(at, stay)
         diagonal = [((2 * i + j) * 4 + h, (2 * i + 1 - j) * 4 + (h ^ 2)) for i in range(4) for j in range(2) for h in range(4)]
         from_xy = lax.ppermute(to_xy, ("seq", "head"), diagonal)
         parts += [stay, head_perm(to_y, 2), swap(to_x), from_xy]

time: 237 us -> 194 us (0.82)
  starting transfers between devices: 69.1 us -> 45.7 us
  waiting for transfers between devices: 99.7 us -> 85.7 us
  between operations: 13.6 us -> 0.23 us
  other arithmetic: 3.87 us -> 7.82 us
    ppermute x18 -> x19, waiting for transfers between devices: 84.1 us -> 58.1 us  [seq_perm(): return lax.ppermute(array, 'seq', pairs)]
    ppermute x18 -> x19, starting transfers between devices: 59.8 us -> 33.8 us  [seq_perm(): return lax.ppermute(array, 'seq', pairs)]
    ppermute x0 -> x1, waiting for transfers between devices: none -> 8.38 us  [body_eight(): low_o = lax.ppermute(jnp.where(z == 0, kv_give, block), 'seq', pairs)]
    ppermute x0 -> x1, starting transfers between devices: none -> 5.52 us  [body_eight(): low_o = lax.ppermute(jnp.where(z == 0, kv_give, block), 'seq', pairs)]
    select_n x2 -> x3, other arithmetic: 2.73 us -> 7.74 us  [the longest x1 4.07 us: body_eight(): low_o = lax.ppermute(jnp.where(z == 0, kv_give, block), 'seq', pairs)]
    unnamed x6 -> x12, local copies, waits for them, and re-layouts: 2.39 us -> 5.84 us
    ppermute x6 -> x4, waiting for transfers between devices: 5.74 us -> 9.12 us  [head_perm(): return lax.ppermute(array, 'head', [(i, i ^ flip) for i in range(4)])]
    pallas_call x3 -> x2, Pallas kernels: 6.66 us -> 8.51 us  [project(): pl.pallas_call(functools.partial(project_kernel, len(near)), out_shape=[o...]
  transfers between devices with their start and end apart: 28 -> 26, of which waited for: 14 -> 12; matrix products, arithmetic and copies ran while one was open for 3% -> 4% of each run, Pallas kernels for 15% -> 17%
where the time goes in v6:
time: 194 us; the launch traced here: 191 us
  waiting for transfers between devices  85.7 us (44%)
  starting transfers between devices  45.7 us (24%)
  Pallas kernels  43.5 us (22%)
  local copies, waits for them, and re-layouts  8.11 us (4%)
  other arithmetic  7.82 us (4%)
    ppermute x19, waiting for transfers between devices, seq_perm(): return lax.ppermute(array, 'seq', pairs)  58.1 us
    ppermute x19, starting transfers between devices, seq_perm(): return lax.ppermute(array, 'seq', pairs)  33.8 us
    pallas_call x6, Pallas kernels, head_call(): pl.pallas_call(kernel, out_shape=outs, grid_spec=pltpu.PrefetchScalarGrid...  31.7 us
    ppermute x2, waiting for transfers between devices, body_eight(): from_xy = lax.ppermute(to_xy, ('seq', 'head'), diagonal)  10.1 us
    ppermute x4, waiting for transfers between devices, head_perm(): return lax.ppermute(array, 'head', [(i, i ^ flip) for i in range(4)])  9.12 us
    pallas_call x2, Pallas kernels, project(): pl.pallas_call(functools.partial(project_kernel, len(near)), out_shape=[o...  8.51 us
    ppermute x1, waiting for transfers between devices, body_eight(): low_o = lax.ppermute(jnp.where(z == 0, kv_give, block), 'seq', pairs)  8.38 us
    unnamed x12, local copies, waits for them, and re-layouts  5.84 us
  transfers between devices with their start and end apart: 26, of which 12 were waited for; matrix products, arithmetic and copies ran while one was open for 4% of the time, Pallas kernels for 17%

profile of v6, /device:TPU:16, one launch (start us, length us, event | category | flops | bytes accessed | tf_op | source)
XLA Modules:
  0.0 191.1 jit_solution(7596330643169173488)
XLA Ops:
  0.0 2.3 %dynamic-slice_bitcast_fusion.2 = (bf16[1,512,512]{2,1,0:T(8,128)(2,1)}, bf16[1,512,512]{2,1,0:T(8,128)(2,1)}) fusion(bf16[3,1,512,1024]{3,2,1,0:T(8,128)(2,1)} %param.2, s32[]{:T(128)S(6)} %select_n.65, s32[]{:T(128)S(6)} %select_n.64), kind=kLoop, calls=%fused_computation.7 | loop fusion | bytes 2097160 | tf_op jit(solution)/shard_map/dynamic_slice | solution.py:426
  3.8 2.3 %collective-permute-start = (bf16[1,512,512]{2,1,0:T(8,128)(2,1)}, bf16[1,512,512]{2,1,0:T(8,128)(2,1)}, u32[]{:S(2)}, u32[]{:S(2)}) collective-permute-start(bf16[1,512,512]{2,1,0:T(8,128)(2,1)} %get-tuple-element.66.q_m), channel_id=1, source_target_pairs={{16,8},{20,12},{24,16},{28,20},{17,9},{21,13},{25,17},{29,21},{18,... | collective-permute-start | bytes 1572872 | tf_op jit(solution)/shard_map/ppermute | solution.py:417
  7.6 4.1 %broadcast_select_fusion = (bf16[2,512,512]{2,1,0:T(8,128)(2,1)}, bf16[2,512,512]{2,1,0:T(8,128)(2,1)}, bf16[2,512,512]{2,1,0:T(8,128)(2,1)}, bf16[2,512,512]{2,1,0:T(8,128)(2,1)S(1)}) fusion(bf16[2,512,512]{2,1,0:T(8,128)(2,1)} %bitcast.7, pred[]{:T(512)S(6)} %eq.15, bf16[3,1,512,1024]{3,2,1,0:T(8,128)(2,1)} %param.2, s32[]{:T(128)S(6)} %select_n.65, ...), kind=kLoop, calls=%fused_computation.5 | loop fusion | flops 1048576 | bytes 7340041 | tf_op jit(solution)/shard_map/jit(_where)/select_n | solution.py:436
  12.4 5.5 %collective-permute-start.9 = (bf16[2,512,512]{2,1,0:T(8,128)(2,1)}, bf16[2,512,512]{2,1,0:T(8,128)(2,1)S(1)}, u32[]{:S(2)}, u32[]{:S(2)}) collective-permute-start(bf16[2,512,512]{2,1,0:T(8,128)(2,1)} %get-tuple-element.59), channel_id=1, source_target_pairs={{0,12},{4,8},{8,0},{12,4},{16,24},{20,28},{1,13},{5,9},{9,1},{13,5... | collective-permute-start | bytes 3145736 | tf_op jit(solution)/shard_map/ppermute | solution.py:436
  18.5 2.3 %collective-permute-done.qa_m = bf16[1,512,512]{2,1,0:T(8,128)(2,1)} collective-permute-done((bf16[1,512,512]{2,1,0:T(8,128)(2,1)}, bf16[1,512,512]{2,1,0:T(8,128)(2,1)}, u32[]{:S(2)}, u32[]{:S(2)}) %collective-permute-start) | collective-permute-done | bytes 524320 | tf_op jit(solution)/shard_map/ppermute | solution.py:417
  20.8 1.9 collective-permute-start.2
  23.4 19.8 %collective-permute-done.2.qa_o = bf16[1,512,512]{2,1,0:T(8,128)(2,1)S(1)} collective-permute-done((bf16[1,512,512]{2,1,0:T(8,128)(2,1)}, bf16[1,512,512]{2,1,0:T(8,128)(2,1)S(1)}, u32[]{:S(2)}, u32[]{:S(2)}) %collective-permute-start.2) | collective-permute-done | bytes 524320 | tf_op jit(solution)/shard_map/ppermute | solution.py:417
  46.2 7.4 %collective-permute-start.7 = (bf16[1024,512]{1,0:T(8,128)(2,1)}, bf16[1024,512]{1,0:T(8,128)(2,1)}, u32[]{:S(2)}, u32[]{:S(2)}) collective-permute-start(bf16[1024,512]{1,0:T(8,128)(2,1)} %param.3), channel_id=1, source_target_pairs={{16,0},{20,4},{24,8},{28,12},{17,1},{21,5},{25,9},{29,13},{18,2},{... | collective-permute-start | bytes 3145736 | tf_op jit(solution)/shard_map/ppermute | solution.py:417
  53.7 8.4 %collective-permute-done.9.refs_1_ = bf16[2,512,512]{2,1,0:T(8,128)(2,1)S(1)} collective-permute-done((bf16[2,512,512]{2,1,0:T(8,128)(2,1)}, bf16[2,512,512]{2,1,0:T(8,128)(2,1)S(1)}, u32[]{:S(2)}, u32[]{:S(2)}) %collective-permute-start.9) | collective-permute-done | bytes 1048608 | tf_op jit(solution)/shard_map/ppermute | solution.py:436
  64.1 7.3 %upper_rows.2 = (bf16[1072,256]{1,0:T(8,128)(2,1)}, bf16[1072,256]{1,0:T(8,128)(2,1)}) custom-call(s32[4]{0:T(128)S(1)} %pad_add_fusion.at, bf16[1,512,512]{2,1,0:T(8,128)(2,1)} %collective-permute-done.qa_m, bf16[1,512,512]{2,1,0:T(8,128)(2,1)S(1)} %copy-done.1, bf16[1,512,512]{2,1,0:T(8,128)(2,1)} %collective-permute-done.3.qb_m, ...), custom_call_target="tpu_custom_call" | custom-call | flops 400000000 | bytes 1024 | tf_op jit(solution)/shard_map/upper_rows/pallas_call | solution.py:299
  71.5 4.3 %collective-permute-start.10 = (bf16[1072,256]{1,0:T(8,128)(2,1)}, bf16[1072,256]{1,0:T(8,128)(2,1)}, u32[]{:S(2)}, u32[]{:S(2)}) collective-permute-start(bf16[1072,256]{1,0:T(8,128)(2,1)} %get-tuple-element.34), channel_id=1, source_target_pairs={{8,16},{12,20},{16,24},{20,28},{9,17},{13,21},{17,25},{21,29},{10,... | collective-permute-start | bytes 1646600 | tf_op jit(solution)/shard_map/ppermute | solution.py:417
  79.3 6.7 %upper_rows.3 = (bf16[1072,256]{1,0:T(8,128)(2,1)S(1)}, bf16[1072,256]{1,0:T(8,128)(2,1)S(1)}) custom-call(s32[4]{0:T(128)S(1)} %pad_add_fusion.at, bf16[1,512,512]{2,1,0:T(8,128)(2,1)} %collective-permute-done.qa_m, bf16[1,512,512]{2,1,0:T(8,128)(2,1)S(1)} %copy-done.2, bf16[1,512,512]{2,1,0:T(8,128)(2,1)} %collective-permute-done.3.qb_m, ...), custom_call_target="tpu_custom_call" | custom-call | flops 400000000 | bytes 1024 | tf_op jit(solution)/shard_map/upper_rows/pallas_call | solution.py:299
  86.1 1.9 %collective-permute-start.14 = (bf16[1072,256]{1,0:T(8,128)(2,1)S(1)}, bf16[1072,256]{1,0:T(8,128)(2,1)S(1)}, u32[]{:S(2)}, u32[]{:S(2)}) collective-permute-start(bf16[1072,256]{1,0:T(8,128)(2,1)S(1)} %get-tuple-element.36), channel_id=1, source_target_pairs={{8,16},{12,20},{16,24},{20,28},{9,17},{13,21},{17,25},{21,29},{10,... | collective-permute-start | bytes 1646600 | tf_op jit(solution)/shard_map/ppermute | solution.py:417
  88.0 6.0 %own_rows.2.own = bf16[1072,256]{1,0:T(8,128)(2,1)S(1)} custom-call(s32[4]{0:T(128)S(1)} %pad_add_fusion.at, bf16[1,512,512]{2,1,0:T(8,128)(2,1)} %get-tuple-element.66.q_m, bf16[1,512,512]{2,1,0:T(8,128)(2,1)} %collective-permute-done.1.q_o, bf16[2,512,512]{2,1,0:T(8,128)(2,1)S(1)} %get-tuple-element.64.kv_m, ...), custom_call_target="tpu_custom_call" | custom-call | flops 400000000 | bytes 1024 | tf_op jit(solution)/shard_map/own_rows/pallas_call | solution.py:299
  94.9 6.0 %own_rows.3.own = bf16[1072,256]{1,0:T(8,128)(2,1)S(1)} custom-call(s32[4]{0:T(128)S(1)} %pad_add_fusion.at, bf16[1,512,512]{2,1,0:T(8,128)(2,1)} %get-tuple-element.66.q_m, bf16[1,512,512]{2,1,0:T(8,128)(2,1)} %collective-permute-done.1.q_o, bf16[2,512,512]{2,1,0:T(8,128)(2,1)S(1)} %get-tuple-element.64.kv_m, ...), custom_call_target="tpu_custom_call" | custom-call | flops 400000000 | bytes 1024 | tf_op jit(solution)/shard_map/own_rows/pallas_call | solution.py:299
  102.3 3.2 %merge.2 = bf16[2,512,256]{2,1,0:T(8,128)(2,1)S(1)} custom-call(s32[4]{0:T(128)S(1)} %pad_add_fusion.at, bf16[1072,256]{1,0:T(8,128)(2,1)S(1)} %own_rows.2.own, bf16[1072,256]{1,0:T(8,128)(2,1)} %collective-permute-done.10.oa, bf16[1072,256]{1,0:T(8,128)(2,1)} %collective-permute-done.11.ob), custom_call_target="tpu_custom_call" | custom-call | flops 200000000 | bytes 1024 | tf_op jit(solution)/shard_map/merge/pallas_call | solution.py:299
  106.1 2.3 %fusion = bf16[1024,512]{1,0:T(8,128)(2,1)} fusion(bf16[1024,512]{1,0:T(8,128)(2,1)} %collective-permute-done.7, bf16[1024,512]{1,0:T(8,128)(2,1)} %collective-permute-done.5, bf16[2,512,512]{2,1,0:T(8,128)(2,1)S(1)} %collective-permute-done.6.refs_0_, pred[]{:T(512)S(6)} %eq.14, pred[]{:T(512)S(6)} %ge.3), kind=kLoop, calls=%fused_computation.2 | loop fusion | flops 1048576 | bytes 4194306 | tf_op jit(solution)/shard_map/jit(_where)/select_n | solution.py:472
  108.4 3.9 %collective-permute-start.12 = (bf16[1024,512]{1,0:T(8,128)(2,1)}, bf16[1024,512]{1,0:T(8,128)(2,1)}, u32[]{:S(2)}, u32[]{:S(2)}) collective-permute-start(bf16[1024,512]{1,0:T(8,128)(2,1)} %fusion), channel_id=1, source_target_pairs={{0,8},{4,12},{8,0},{12,4},{16,24},{20,28},{24,16},{28,20},{1,9},{5... | collective-permute-start | bytes 3145736 | tf_op jit(solution)/shard_map/ppermute | solution.py:417
  112.2 6.8 %collective-permute-done.13 = bf16[2,512,256]{2,1,0:T(8,128)(2,1)S(1)} collective-permute-done((bf16[2,512,256]{2,1,0:T(8,128)(2,1)S(1)}, bf16[2,512,256]{2,1,0:T(8,128)(2,1)S(1)}, u32[]{:S(2)}, u32[]{:S(2)}) %collective-permute-start.13) | collective-permute-done | bytes 524320 | tf_op jit(solution)/shard_map/ppermute | solution.py:417
  119.1 2.4 %merge.3 = bf16[2,512,256]{2,1,0:T(8,128)(2,1)S(1)} custom-call(s32[4]{0:T(128)S(1)} %pad_add_fusion.at, bf16[1072,256]{1,0:T(8,128)(2,1)S(1)} %own_rows.3.own, bf16[1072,256]{1,0:T(8,128)(2,1)S(1)} %collective-permute-done.14.oa, bf16[1072,256]{1,0:T(8,128)(2,1)S(1)} %collective-permute-done.15.ob), custom_call_target="tpu_custom_call" | custom-call | flops 200000000 | bytes 1024 | tf_op jit(solution)/shard_map/merge/pallas_call | solution.py:299
  122.1 7.1 %collective-permute-done.17 = bf16[1024,512]{1,0:T(8,128)(2,1)} collective-permute-done((bf16[1024,512]{1,0:T(8,128)(2,1)}, bf16[1024,512]{1,0:T(8,128)(2,1)}, u32[]{:S(2)}, u32[]{:S(2)}) %collective-permute-start.17) | collective-permute-done | bytes 1048608 | tf_op jit(solution)/shard_map/ppermute | solution.py:417
  130.6 19.9 %collective-permute-done.12 = bf16[1024,512]{1,0:T(8,128)(2,1)} collective-permute-done((bf16[1024,512]{1,0:T(8,128)(2,1)}, bf16[1024,512]{1,0:T(8,128)(2,1)}, u32[]{:S(2)}, u32[]{:S(2)}) %collective-permute-start.12) | collective-permute-done | bytes 1048608 | tf_op jit(solution)/shard_map/ppermute | solution.py:417
  150.4 4.1 %project.2 = (bf16[2,2,2,128,512]{4,3,2,1,0:T(8,128)(2,1)S(1)}, bf16[2,2,2,128,512]{4,3,2,1,0:T(8,128)(2,1)S(1)}) custom-call(s32[4]{0:T(128)S(1)} %pad_add_fusion.at, bf16[2,2,2,128,256]{4,3,2,1,0:T(8,128)(2,1)S(1)} %bitcast.30, bf16[2,2,2,128,256]{4,3,2,1,0:T(8,128)(2,1)S(1)} %bitcast.32, bf16[2,2,2,128,256]{4,3,2,1,0:T(8,128)(2,1)S(1)} %bitcast.35, ...), custom_call_target="tpu_custom_call" | custom-call | flops 400000000 | bytes 1024 | tf_op jit(solution)/shard_map/project/pallas_call | solution.py:346
  154.6 2.6 %collective-permute-done.18.got = bf16[2,2,2,128,512]{4,3,2,1,0:T(8,128)(2,1)S(1)} collective-permute-done((bf16[2,2,2,128,512]{4,3,2,1,0:T(8,128)(2,1)S(1)}, bf16[2,2,2,128,512]{4,3,2,1,0:T(8,128)(2,1)S(1)}, u32[]{:S(2)}, u32[]{:S(2)}) %collective-permute-start.18) | collective-permute-done | bytes 1048608 | tf_op jit(solution)/shard_map/ppermute | solution.py:423
  158.1 4.4 %project.3 = (bf16[2,2,2,128,512]{4,3,2,1,0:T(8,128)(2,1)S(1)}, bf16[2,2,2,128,512]{4,3,2,1,0:T(8,128)(2,1)S(1)}) custom-call(s32[4]{0:T(128)S(1)} %pad_add_fusion.at, bf16[2,2,2,128,256]{4,3,2,1,0:T(8,128)(2,1)S(1)} %bitcast.31, bf16[2,2,2,128,256]{4,3,2,1,0:T(8,128)(2,1)S(1)} %bitcast.33, bf16[2,2,2,128,256]{4,3,2,1,0:T(8,128)(2,1)S(1)} %bitcast.36, ...), custom_call_target="tpu_custom_call" | custom-call | flops 400000000 | bytes 1024 | tf_op jit(solution)/shard_map/project/pallas_call | solution.py:346
  167.0 1.6 collective-permute-start.23
  169.1 3.0 %collective-permute-done.19.refs_1_ = bf16[2,128,512]{2,1,0:T(8,128)(2,1)S(1)} collective-permute-done((bf16[2,128,512]{2,1,0:T(8,128)(2,1)S(1)}, bf16[2,128,512]{2,1,0:T(8,128)(2,1)S(1)}, u32[]{:S(2)}, u32[]{:S(2)}) %collective-permute-start.19) | collective-permute-done | bytes 262176 | tf_op jit(solution)/shard_map/ppermute | solution.py:423
  173.6 5.4 %collective-permute-done.21.refs_3_ = bf16[2,128,512]{2,1,0:T(8,128)(2,1)S(1)} collective-permute-done((bf16[2,128,512]{2,1,0:T(8,128)(2,1)S(1)}, bf16[2,128,512]{2,1,0:T(8,128)(2,1)S(1)}, u32[]{:S(2)}, u32[]{:S(2)}) %collective-permute-start.21) | collective-permute-done | bytes 262176 | tf_op jit(solution)/shard_map/ppermute | solution.py:489
  179.0 3.5 %collective-permute-done.23.refs_5_ = bf16[2,128,512]{2,1,0:T(8,128)(2,1)S(1)} collective-permute-done((bf16[2,128,512]{2,1,0:T(8,128)(2,1)S(1)}, bf16[2,128,512]{2,1,0:T(8,128)(2,1)S(1)}, u32[]{:S(2)}, u32[]{:S(2)}) %collective-permute-start.23) | collective-permute-done | bytes 262176 | tf_op jit(solution)/shard_map/ppermute | solution.py:423
  182.5 2.2 %collective-permute-done.24.refs_6_ = bf16[2,128,512]{2,1,0:T(8,128)(2,1)S(1)} collective-permute-done((bf16[2,128,512]{2,1,0:T(8,128)(2,1)S(1)}, bf16[2,128,512]{2,1,0:T(8,128)(2,1)S(1)}, u32[]{:S(2)}, u32[]{:S(2)}) %collective-permute-start.24) | collective-permute-done | bytes 262176 | tf_op jit(solution)/shard_map/ppermute | solution.py:417
  184.7 4.7 %collective-permute-done.25.refs_7_ = bf16[2,128,512]{2,1,0:T(8,128)(2,1)S(1)} collective-permute-done((bf16[2,128,512]{2,1,0:T(8,128)(2,1)S(1)}, bf16[2,128,512]{2,1,0:T(8,128)(2,1)S(1)}, u32[]{:S(2)}, u32[]{:S(2)}) %collective-permute-start.25) | collective-permute-done | bytes 262176 | tf_op jit(solution)/shard_map/ppermute | solution.py:489
  189.3 1.7 place.1
  (48 shorter events, 25.7 us)
Async XLA Ops:
  2.3 15.6 %collective-permute-start.1 = (bf16[1,512,512]{2,1,0:T(8,128)(2,1)}, bf16[1,512,512]{2,1,0:T(8,128)(2,1)}, u32[]{:S(2)}, u32[]{:S(2)}) collective-permute-start(bf16[1,512,512]{2,1,0:T(8,128)(2,1)} %get-tuple-element.65), channel_id=1, source_target_pairs={{0,4},{4,0},{8,12},{12,8},{16,20},{20,16},{24,28},{28,24},{1,5},{5... | collective-permute-start | bytes 1572872 | tf_op jit(solution)/shard_map/ppermute | solution.py:417
  3.8 17.0 %collective-permute-start = (bf16[1,512,512]{2,1,0:T(8,128)(2,1)}, bf16[1,512,512]{2,1,0:T(8,128)(2,1)}, u32[]{:S(2)}, u32[]{:S(2)}) collective-permute-start(bf16[1,512,512]{2,1,0:T(8,128)(2,1)} %get-tuple-element.66.q_m), channel_id=1, source_target_pairs={{16,8},{20,12},{24,16},{28,20},{17,9},{21,13},{25,17},{29,21},{18,... | collective-permute-start | bytes 1572872 | tf_op jit(solution)/shard_map/ppermute | solution.py:417
  6.1 16.6 %collective-permute-start.3 = (bf16[1,512,512]{2,1,0:T(8,128)(2,1)}, bf16[1,512,512]{2,1,0:T(8,128)(2,1)}, u32[]{:S(2)}, u32[]{:S(2)}) collective-permute-start(bf16[1,512,512]{2,1,0:T(8,128)(2,1)} %get-tuple-element.66.q_m), channel_id=1, source_target_pairs={{24,8},{28,12},{25,9},{29,13},{26,10},{30,14},{27,11},{31,15}} | collective-permute-start | bytes 1572872 | tf_op jit(solution)/shard_map/ppermute | solution.py:417
  11.6 42.0 %collective-permute-start.6 = (bf16[2,512,512]{2,1,0:T(8,128)(2,1)}, bf16[2,512,512]{2,1,0:T(8,128)(2,1)S(1)}, u32[]{:S(2)}, u32[]{:S(2)}) collective-permute-start(bf16[2,512,512]{2,1,0:T(8,128)(2,1)} %get-tuple-element.63), channel_id=1, source_target_pairs={{0,8},{4,12},{8,24},{12,28},{1,9},{5,13},{9,25},{13,29},{2,10},{6,... | collective-permute-start | bytes 3145736 | tf_op jit(solution)/shard_map/ppermute | solution.py:417
  12.4 49.7 %collective-permute-start.9 = (bf16[2,512,512]{2,1,0:T(8,128)(2,1)}, bf16[2,512,512]{2,1,0:T(8,128)(2,1)S(1)}, u32[]{:S(2)}, u32[]{:S(2)}) collective-permute-start(bf16[2,512,512]{2,1,0:T(8,128)(2,1)} %get-tuple-element.59), channel_id=1, source_target_pairs={{0,12},{4,8},{8,0},{12,4},{16,24},{20,28},{1,13},{5,9},{9,1},{13,5... | collective-permute-start | bytes 3145736 | tf_op jit(solution)/shard_map/ppermute | solution.py:436
  17.9 44.2 %collective-permute-start.8 = (bf16[2,512,512]{2,1,0:T(8,128)(2,1)}, bf16[2,512,512]{2,1,0:T(8,128)(2,1)}, u32[]{:S(2)}, u32[]{:S(2)}) collective-permute-start(bf16[2,512,512]{2,1,0:T(8,128)(2,1)} %get-tuple-element.33), channel_id=1, source_target_pairs={{0,4},{4,0},{8,12},{12,8},{16,20},{20,16},{24,28},{28,24},{1,5},{5... | collective-permute-start | bytes 3145736 | tf_op jit(solution)/shard_map/ppermute | solution.py:417
  20.8 22.4 %collective-permute-start.2 = (bf16[1,512,512]{2,1,0:T(8,128)(2,1)}, bf16[1,512,512]{2,1,0:T(8,128)(2,1)S(1)}, u32[]{:S(2)}, u32[]{:S(2)}) collective-permute-start(bf16[1,512,512]{2,1,0:T(8,128)(2,1)} %collective-permute-done.1.q_o), channel_id=1, source_target_pairs={{16,8},{20,12},{24,16},{28,20},{17,9},{21,13},{25,17},{29,21},{18,... | collective-permute-start | bytes 1572872 | tf_op jit(solution)/shard_map/ppermute | solution.py:417
  22.7 21.3 %collective-permute-start.4 = (bf16[1,512,512]{2,1,0:T(8,128)(2,1)}, bf16[1,512,512]{2,1,0:T(8,128)(2,1)S(1)}, u32[]{:S(2)}, u32[]{:S(2)}) collective-permute-start(bf16[1,512,512]{2,1,0:T(8,128)(2,1)} %collective-permute-done.1.q_o), channel_id=1, source_target_pairs={{24,8},{28,12},{25,9},{29,13},{26,10},{30,14},{27,11},{31,15}} | collective-permute-start | bytes 1572872 | tf_op jit(solution)/shard_map/ppermute | solution.py:417
  43.2 0.8 copy-start
  44.1 0.8 copy-start.3
  44.9 49.1 %collective-permute-start.5 = (bf16[1024,512]{1,0:T(8,128)(2,1)}, bf16[1024,512]{1,0:T(8,128)(2,1)}, u32[]{:S(2)}, u32[]{:S(2)}) collective-permute-start(bf16[1024,512]{1,0:T(8,128)(2,1)} %param.3), channel_id=1, source_target_pairs={{0,16},{4,20},{1,17},{5,21},{2,18},{6,22},{3,19},{7,23}} | collective-permute-start | bytes 3145736 | tf_op jit(solution)/shard_map/ppermute | solution.py:417
  46.2 59.9 %collective-permute-start.7 = (bf16[1024,512]{1,0:T(8,128)(2,1)}, bf16[1024,512]{1,0:T(8,128)(2,1)}, u32[]{:S(2)}, u32[]{:S(2)}) collective-permute-start(bf16[1024,512]{1,0:T(8,128)(2,1)} %param.3), channel_id=1, source_target_pairs={{16,0},{20,4},{24,8},{28,12},{17,1},{21,5},{25,9},{29,13},{18,2},{... | collective-permute-start | bytes 3145736 | tf_op jit(solution)/shard_map/ppermute | solution.py:417
  62.1 1.0 copy-start.1
  63.1 1.0 copy-start.4
  71.5 29.4 %collective-permute-start.10 = (bf16[1072,256]{1,0:T(8,128)(2,1)}, bf16[1072,256]{1,0:T(8,128)(2,1)}, u32[]{:S(2)}, u32[]{:S(2)}) collective-permute-start(bf16[1072,256]{1,0:T(8,128)(2,1)} %get-tuple-element.34), channel_id=1, source_target_pairs={{8,16},{12,20},{16,24},{20,28},{9,17},{13,21},{17,25},{21,29},{10,... | collective-permute-start | bytes 1646600 | tf_op jit(solution)/shard_map/ppermute | solution.py:417
  75.8 26.5 %collective-permute-start.11 = (bf16[1072,256]{1,0:T(8,128)(2,1)}, bf16[1072,256]{1,0:T(8,128)(2,1)}, u32[]{:S(2)}, u32[]{:S(2)}) collective-permute-start(bf16[1072,256]{1,0:T(8,128)(2,1)} %get-tuple-element.40), channel_id=1, source_target_pairs={{8,24},{12,28},{9,25},{13,29},{10,26},{14,30},{11,27},{15,31}} | collective-permute-start | bytes 1646600 | tf_op jit(solution)/shard_map/ppermute | solution.py:417
  77.2 1.0 copy-start.2
  78.3 1.0 copy-start.5
  86.1 33.0 %collective-permute-start.14 = (bf16[1072,256]{1,0:T(8,128)(2,1)S(1)}, bf16[1072,256]{1,0:T(8,128)(2,1)S(1)}, u32[]{:S(2)}, u32[]{:S(2)}) collective-permute-start(bf16[1072,256]{1,0:T(8,128)(2,1)S(1)} %get-tuple-element.36), channel_id=1, source_target_pairs={{8,16},{12,20},{16,24},{20,28},{9,17},{13,21},{17,25},{21,29},{10,... | collective-permute-start | bytes 1646600 | tf_op jit(solution)/shard_map/ppermute | solution.py:417
  94.0 25.1 %collective-permute-start.15 = (bf16[1072,256]{1,0:T(8,128)(2,1)S(1)}, bf16[1072,256]{1,0:T(8,128)(2,1)S(1)}, u32[]{:S(2)}, u32[]{:S(2)}) collective-permute-start(bf16[1072,256]{1,0:T(8,128)(2,1)S(1)} %get-tuple-element.44), channel_id=1, source_target_pairs={{8,24},{12,28},{9,25},{13,29},{10,26},{14,30},{11,27},{15,31}} | collective-permute-start | bytes 1646600 | tf_op jit(solution)/shard_map/ppermute | solution.py:417
  100.9 28.3 %collective-permute-start.17 = (bf16[1024,512]{1,0:T(8,128)(2,1)}, bf16[1024,512]{1,0:T(8,128)(2,1)}, u32[]{:S(2)}, u32[]{:S(2)}) collective-permute-start(bf16[1024,512]{1,0:T(8,128)(2,1)} %param.3), channel_id=1, source_target_pairs={{0,8},{4,12},{24,16},{28,20},{1,9},{5,13},{25,17},{29,21},{2,10},{... | collective-permute-start | bytes 3145736 | tf_op jit(solution)/shard_map/ppermute | solution.py:417
  105.5 13.6 %collective-permute-start.13 = (bf16[2,512,256]{2,1,0:T(8,128)(2,1)S(1)}, bf16[2,512,256]{2,1,0:T(8,128)(2,1)S(1)}, u32[]{:S(2)}, u32[]{:S(2)}) collective-permute-start(bf16[2,512,256]{2,1,0:T(8,128)(2,1)S(1)} %merge.2), channel_id=1, source_target_pairs={{0,4},{4,0},{8,12},{12,8},{16,20},{20,16},{24,28},{28,24},{1,5},{5... | collective-permute-start | bytes 1572872 | tf_op jit(solution)/shard_map/ppermute | solution.py:417
  108.4 42.0 %collective-permute-start.12 = (bf16[1024,512]{1,0:T(8,128)(2,1)}, bf16[1024,512]{1,0:T(8,128)(2,1)}, u32[]{:S(2)}, u32[]{:S(2)}) collective-permute-start(bf16[1024,512]{1,0:T(8,128)(2,1)} %fusion), channel_id=1, source_target_pairs={{0,8},{4,12},{8,0},{12,4},{16,24},{20,28},{24,16},{28,20},{1,9},{5... | collective-permute-start | bytes 3145736 | tf_op jit(solution)/shard_map/ppermute | solution.py:417
  121.5 28.9 %collective-permute-start.16 = (bf16[2,512,256]{2,1,0:T(8,128)(2,1)S(1)}, bf16[2,512,256]{2,1,0:T(8,128)(2,1)S(1)}, u32[]{:S(2)}, u32[]{:S(2)}) collective-permute-start(bf16[2,512,256]{2,1,0:T(8,128)(2,1)S(1)} %merge.3), channel_id=1, source_target_pairs={{0,4},{4,0},{8,12},{12,8},{16,20},{20,16},{24,28},{28,24},{1,5},{5... | collective-permute-start | bytes 1572872 | tf_op jit(solution)/shard_map/ppermute | solution.py:417
  154.5 2.7 %collective-permute-start.18 = (bf16[2,2,2,128,512]{4,3,2,1,0:T(8,128)(2,1)S(1)}, bf16[2,2,2,128,512]{4,3,2,1,0:T(8,128)(2,1)S(1)}, u32[]{:S(2)}, u32[]{:S(2)}) collective-permute-start(bf16[2,2,2,128,512]{4,3,2,1,0:T(8,128)(2,1)S(1)} %get-tuple-element.47), channel_id=1, source_target_pairs={{0,1},{1,0},{2,3},{3,2},{4,5},{5,4},{6,7},{7,6},{8,9},{9,8},{10,11... | collective-permute-start | bytes 3145736 | tf_op jit(solution)/shard_map/ppermute | solution.py:423
  162.5 3.7 %collective-permute-start.22 = (bf16[2,2,2,128,512]{4,3,2,1,0:T(8,128)(2,1)S(1)}, bf16[2,2,2,128,512]{4,3,2,1,0:T(8,128)(2,1)S(1)}, u32[]{:S(2)}, u32[]{:S(2)}) collective-permute-start(bf16[2,2,2,128,512]{4,3,2,1,0:T(8,128)(2,1)S(1)} %get-tuple-element.54), channel_id=1, source_target_pairs={{0,1},{1,0},{2,3},{3,2},{4,5},{5,4},{6,7},{7,6},{8,9},{9,8},{10,11... | collective-permute-start | bytes 3145736 | tf_op jit(solution)/shard_map/ppermute | solution.py:423
  162.7 9.4 %collective-permute-start.19 = (bf16[2,128,512]{2,1,0:T(8,128)(2,1)S(1)}, bf16[2,128,512]{2,1,0:T(8,128)(2,1)S(1)}, u32[]{:S(2)}, u32[]{:S(2)}) collective-permute-start(bf16[2,128,512]{2,1,0:T(8,128)(2,1)S(1)} %get-tuple-element.49), channel_id=1, source_target_pairs={{0,2},{1,3},{2,0},{3,1},{4,6},{5,7},{6,4},{7,5},{8,10},{9,11},{10,... | collective-permute-start | bytes 786440 | tf_op jit(solution)/shard_map/ppermute | solution.py:423
  164.2 9.3 %collective-permute-start.20 = (bf16[2,128,512]{2,1,0:T(8,128)(2,1)S(1)}, bf16[2,128,512]{2,1,0:T(8,128)(2,1)S(1)}, u32[]{:S(2)}, u32[]{:S(2)}) collective-permute-start(bf16[2,128,512]{2,1,0:T(8,128)(2,1)S(1)} %get-tuple-element.50), channel_id=1, source_target_pairs={{0,4},{4,0},{8,12},{12,8},{16,20},{20,16},{24,28},{28,24},{1,5},{5... | collective-permute-start | bytes 786440 | tf_op jit(solution)/shard_map/ppermute | solution.py:417
  164.7 14.2 %collective-permute-start.21 = (bf16[2,128,512]{2,1,0:T(8,128)(2,1)S(1)}, bf16[2,128,512]{2,1,0:T(8,128)(2,1)S(1)}, u32[]{:S(2)}, u32[]{:S(2)}) collective-permute-start(bf16[2,128,512]{2,1,0:T(8,128)(2,1)S(1)} %get-tuple-element.51), channel_id=1, source_target_pairs={{0,6},{1,7},{2,4},{3,5},{4,2},{5,3},{6,0},{7,1},{8,14},{9,15},{10,... | collective-permute-start | bytes 786440 | tf_op jit(solution)/shard_map/ppermute | solution.py:489
  167.0 15.5 %collective-permute-start.23 = (bf16[2,128,512]{2,1,0:T(8,128)(2,1)S(1)}, bf16[2,128,512]{2,1,0:T(8,128)(2,1)S(1)}, u32[]{:S(2)}, u32[]{:S(2)}) collective-permute-start(bf16[2,128,512]{2,1,0:T(8,128)(2,1)S(1)} %get-tuple-element.56), channel_id=1, source_target_pairs={{0,2},{1,3},{2,0},{3,1},{4,6},{5,7},{6,4},{7,5},{8,10},{9,11},{10,... | collective-permute-start | bytes 786440 | tf_op jit(solution)/shard_map/ppermute | solution.py:423
  168.6 16.1 %collective-permute-start.24 = (bf16[2,128,512]{2,1,0:T(8,128)(2,1)S(1)}, bf16[2,128,512]{2,1,0:T(8,128)(2,1)S(1)}, u32[]{:S(2)}, u32[]{:S(2)}) collective-permute-start(bf16[2,128,512]{2,1,0:T(8,128)(2,1)S(1)} %get-tuple-element.57), channel_id=1, source_target_pairs={{0,4},{4,0},{8,12},{12,8},{16,20},{20,16},{24,28},{28,24},{1,5},{5... | collective-permute-start | bytes 786440 | tf_op jit(solution)/shard_map/ppermute | solution.py:417
  172.1 17.3 %collective-permute-start.25 = (bf16[2,128,512]{2,1,0:T(8,128)(2,1)S(1)}, bf16[2,128,512]{2,1,0:T(8,128)(2,1)S(1)}, u32[]{:S(2)}, u32[]{:S(2)}) collective-permute-start(bf16[2,128,512]{2,1,0:T(8,128)(2,1)S(1)} %get-tuple-element.58), channel_id=1, source_target_pairs={{0,6},{1,7},{2,4},{3,5},{4,2},{5,3},{6,0},{7,1},{8,14},{9,15},{10,... | collective-permute-start | bytes 786440 | tf_op jit(solution)/shard_map/ppermute | solution.py:489

commit v7 on v6

--- a/solution.py
+++ b/solution.py
@@ -201,7 +201,7 @@
     return [ref[i] for ref in refs for i in range(ref.shape[0])]
 
 
-def own_kernel(coef, cols, at, q_m, q_o, kv_m, kv_o, *refs):
+def own_kernel(coef, cols, at, q, kv_m, kv_o, *refs):
     x, z = at[0], at[1]
     below = z == 1
     block = 256
@@ -217,7 +217,6 @@
     lk_e, lk_o = jnp.where(first, m_k, o_k), jnp.where(first, o_k, m_k)
     lv_e, lv_o = jnp.where(first, m_v, o_v), jnp.where(first, o_v, m_v)
     lv_o1 = with_ones(lv_o)
-    q_e, q_o = jnp.where(first, q_m[0], q_o[0]), jnp.where(first, q_o[0], q_m[0])
     evens, odds = [], []
     for part in range(cols // block):
         a, b = part * block, (part + 1) * block
@@ -229,8 +228,8 @@
             blocks = [(k[a:b], v[a:b], tri)]
             return blocks if part == 0 else [(k[:a], v[:a], None)] + blocks
 
-        o1, l1 = attend(q_e[mine], causal(k_e, v_e) + [(lk_o, lv_o1, below)], [col_e], coef)
-        o2, l2 = attend(q_o[mine], causal(k_o, v_o) + [(k_e, v_e, None)], [col_e, col_o], coef)
+        o1, l1 = attend(q[0, mine], causal(k_e, v_e) + [(lk_o, lv_o1, below)], [col_e], coef)
+        o2, l2 = attend(q[1, mine], causal(k_o, v_o) + [(k_e, v_e, None)], [col_e, col_o], coef)
         out[mine] = o1.astype(BF16)
         out[cols + a : cols + b] = o2.astype(BF16)
         e, o = lse_rows(l1, l2)
@@ -238,7 +237,7 @@
     put_lse(out, 2 * cols, evens, odds)
 
 
-def upper_kernel(coef, cols, at, qa_m, qa_o, qb_m, qb_o, kv_m, kv_o, *refs):
+def upper_kernel(coef, cols, at, qa, qb, kv_m, kv_o, *refs):
     x, z = at[0], at[1]
     below = z == 1
     first = x == 0
@@ -246,10 +245,8 @@
     k_e, k_o = jnp.where(first, kv_m[0], kv_o[0]), jnp.where(first, kv_o[0], kv_m[0])
     v_e, v_o = jnp.where(first, kv_m[1], kv_o[1]), jnp.where(first, kv_o[1], kv_m[1])
     v_o1 = with_ones(v_o)
-    *low, out_a, out_b = refs
+    *low, weight, out_a, out_b = refs
     lows = stacked(low)
-    qa = jnp.where(first, qa_m[0], qa_o[0]), jnp.where(first, qa_o[0], qa_m[0])
-    qb = jnp.where(first, qb_m[0], qb_o[0]), jnp.where(first, qb_o[0], qb_m[0])
     rows_a, rows_b = ([], []), ([], [])
     for index in range(cols // block):
         a, b = index * block, (index + 1) * block
@@ -262,10 +259,14 @@
             (qa, out_a, rows_a, [(k_o, v_o1, None)], [ce]),
             (qb, out_b, rows_b, [], [ce, co]),
         ):
-            o1, l1 = attend(q[0][mine], dense, singles + low, coef)
-            o2, l2 = attend(q[1][mine], [], [ce, co] + low, coef)
-            out[mine] = o1.astype(BF16)
-            out[cols + a : cols + b] = o2.astype(BF16)
+            o1, l1 = attend(q[0, mine], dense, singles + low, coef)
+            o2, l2 = attend(q[1, mine], [], [ce, co] + low, coef)
+            o1, o2 = o1.astype(BF16), o2.astype(BF16)
+            other = slice(cols + a, cols + b)
+            if out is out_b:
+                o1, o2 = jnp.where(below, o1, weight[mine]), jnp.where(below, o2, weight[other])
+            out[mine] = o1
+            out[other] = o2
             e, o = lse_rows(l1, l2)
             rows[0].extend(e)
             rows[1].extend(o)
@@ -288,7 +289,7 @@
 
 
 def cost(us):
-    return pl.CostEstimate(flops=int(us * 1e8), bytes_accessed=1024, transcendentals=0)
+    return pl.CostEstimate(flops=int(us * 1e9), bytes_accessed=1024, transcendentals=0)
 
 
 def head_call(kernel, at, args, outs, heads, name, us):
@@ -324,38 +325,24 @@
 
         left = jnp.concatenate([rows(ref) for ref in near], axis=1)
         right = jnp.concatenate([rows(ref) for ref in far], axis=1)
-        for s, weight in enumerate(weights):
-            top = weight[0, pl.ds(pl.multiple_of(x * half, half), half)]
-            bottom = weight[0, pl.ds(pl.multiple_of((1 - x) * half, half), half)]
+        base = 0
+        for weight in weights:
+            top = weight[pl.ds(pl.multiple_of(x * half, half), half)]
+            bottom = weight[pl.ds(pl.multiple_of((1 - x) * half, half), half)]
             c = jnp.dot(left, top, preferred_element_type=F32) + jnp.dot(right, bottom, preferred_element_type=F32)
-            out[s] = c.astype(BF16).reshape(2, 2, tokens, weight.shape[2])
-
-
-def project(at, near, far, weights):
+            width = weight.shape[1]
+            s, lane = base // out.shape[4], base % out.shape[4]
+            out[s, :, :, :, lane : lane + width] = c.astype(BF16).reshape(2, 2, tokens, width)
+            base += width
+
+
+def project(at, near, far, weights, out_width):
     cols = near[0].shape[1]
-    args = [a.reshape(2, 2, 2, cols // 4, a.shape[2]) for a in near + far]
-    _, depth, out_width = weights[0][0].shape
-    out = jax.ShapeDtypeStruct((len(weights), 2, 2, cols // 4, out_width), BF16)
-
-    def weight_spec(pick):
-        return pl.BlockSpec((1, depth, out_width), lambda s, at: (pick(at), 0, 0))
-
-    def whole(shape):
-        return pl.BlockSpec(shape, lambda s, at: (0,) * len(shape))
-
-    return pl.pallas_call(
-        functools.partial(project_kernel, len(near)),
-        out_shape=[out, out],
-        grid_spec=pltpu.PrefetchScalarGridSpec(
-            num_scalar_prefetch=1,
-            grid=(1,),
-            in_specs=[whole(a.shape) for a in args] + [weight_spec(pick) for _, pick in weights],
-            out_specs=[whole(out.shape)] * 2,
-        ),
-        compiler_params=pltpu.CompilerParams(vmem_limit_bytes=VMEM),
-        cost_estimate=cost(2 * len(weights)),
-        name="project",
-    )(at, *args, *(w for w, _ in weights))
+    args = [a.reshape(2, 2, 2, cols // 4, a.shape[2]) for a in near + far] + weights
+    layers = sum(w.shape[1] for w in weights) // out_width
+    out = jax.ShapeDtypeStruct((layers, 2, 2, cols // 4, out_width), BF16)
+    return whole_call(
+        functools.partial(project_kernel, len(near)), at, args, [out, out], "project", 2 * layers)
 
 
 def whole_call(kernel, at, args, outs, name, us):
@@ -425,42 +412,55 @@
     def lanes(lo, hi, part, source=local):
         return lax.dynamic_slice(source, (lo, 0, part * half), (hi - lo, cols, half))
 
-    down, two_down = [(2, 1), (3, 2)], [(3, 1)]
-    q_m = lanes(0, 1, x)
-    q_o = swap(lanes(0, 1, 1 - x))
-    qs = [seq_perm(q_m, *down), None, seq_perm(q_m, *two_down), None]
+    def lanes(lo, hi, half_of):
+        return lax.dynamic_slice(local, (lo, 0, half_of * half), (hi - lo, cols, half))
+
+    def pieces(array, c):
+        return array[..., c * width : (c + 1) * width]
+
+    q_m, q_o = lanes(0, 1, x), swap(lanes(0, 1, 1 - x))
     kv_m, kv_give = lanes(1, 3, x), lanes(1, 3, 1 - x)
-    block = out_weight.reshape(kv_m.shape)
-    low_m = seq_perm(jnp.where(z == 0, kv_m, block), (0, 1), (1, 3))
-    pairs = [(i, 2 + 1 - i) for i in range(2)] + [(2 + i, i) for i in range(2)] + [(4 + i, 6 + i) for i in range(2)]
-    low_o = lax.ppermute(jnp.where(z == 0, kv_give, block), "seq", pairs)
-    low = [low_m, low_o]
-    kv_o = swap(after(kv_give, q_o))
-    qs[1], qs[3] = seq_perm(q_o, *down), seq_perm(q_o, *two_down)
-    w_second = seq_perm(after(out_weight, *qs), (0, 2))
+    q, qs, low = [], [], []
+    for c in range(chunks):
+        a, b = pieces(q_m, c), pieces(q_o, c)
+        q.append(jnp.concatenate([jnp.where(first, a, b), jnp.where(first, b, a)]))
+        block = pieces(out_weight, c).reshape(q[c].shape)
+        going = [q[c], jnp.where(z == 3, q[c], block)]
+        if c:
+            going = after(going, *qs[0])
+        else:
+            kv_o = swap(after(kv_give, q[0]))
+        qs.append([seq_perm(going[0], (2, 1), (3, 2)), seq_perm(going[1], (3, 1), (1, 0), (2, 3))])
+        mine = jnp.where(z == 0, pieces(kv_m, c), block)
+        if c:
+            low.append([seq_perm(after(jnp.concatenate([mine, pieces(kv_o, c)]), *low[0]), (0, 1), (1, 3))])
+        else:
+            low.append([seq_perm(mine, (0, 1), (1, 3)), seq_perm(pieces(kv_give, c), (0, 1), cross=True)])
 
     struct = jax.ShapeDtypeStruct
     partial = struct((2 * cols + lse_height(cols), width), BF16)
-    oa, ob, own = [], [], []
+    oa, ob, own, sent = [], [], [], []
     turn = at
-    kvs = [kv_m, kv_o, low_m, low_o]
     for c in range(chunks):
+        kvs = [(a, c * heads) for a in (kv_m, kv_o)]
         a, b = head_call(
-            functools.partial(upper_kernel, coef, cols), turn, [(a, c * heads) for a in qs + kvs],
-            [partial] * 2, heads, "upper_rows", 4)
-        turn = after(at, a)
+            functools.partial(upper_kernel, coef, cols), turn,
+            [(a, 0) for a in qs[c]] + kvs + [(a, 0) for a in low[c]] + [(out_weight, c * heads)], [partial] * 2, heads, "upper_rows", 7)
+        sent.append(a)
         oa.append(seq_perm(a, (1, 2), (2, 3)))
-        ob.append(seq_perm(b, (1, 3)))
-    for c in range(chunks):
+        ob.append(seq_perm(b, (1, 3), (0, 1), (3, 2)))
         (mine,) = head_call(
-            functools.partial(own_kernel, coef, cols), turn, [(a, c * heads) for a in [q_m, q_o] + kvs],
-            [partial], heads, "own_rows", 4)
+            functools.partial(own_kernel, coef, cols), after(at, a), [(q[c], 0)] + kvs + [(a, 0) for a in low[c]],
+            [partial], heads, "own_rows", 6)
         own.append(mine)
-        turn = after(at, mine, w_second)
-
-    w_down = seq_perm(after(out_weight, *qs), (2, 0), (3, 1))
-    w_near = seq_perm(after(out_weight, own[0]), (0, 1), (3, 2))
-    w_near = jnp.where((z == 0) | (z == 3), low_o.reshape(out_weight.shape), w_near)
+        turn = after(at, mine, oa[c], ob[c])
+
+    w_second = seq_perm(after(out_weight, own[0], *qs[1]), (0, 2))
+    depth = out_weight.shape[0]
+    w_down = seq_perm(after(out_weight, own[0], *qs[1]), (2, 0), (3, 1))
+    w_near = [
+        jnp.where((z == 0) | (z == 3), qs[c][1].reshape(depth, width), ob[c][:depth]) for c in range(chunks)
+    ]
 
     def merged(c, earlier):
         (a,) = head_call(
@@ -469,18 +469,19 @@
         return a, swap(a)
 
     first_half = merged(0, own[1])
+    w_ridden = jnp.concatenate([low[c][0][:2].reshape(depth, width) for c in range(chunks)], axis=1)
     w_far = jnp.where(
-        z >= 2, jnp.where(z == 2, w_second, low_m.reshape(out_weight.shape)), after(w_down, first_half[0], own[1]))
+        z >= 2, jnp.where(z == 2, w_second, w_ridden), after(w_down, first_half[0], own[1]))
     near, far = map(list, zip(first_half, merged(1, (w_far, first_half[1]))))
     w_other = seq_perm(w_far, (0, 1), (1, 0), (2, 3), (3, 2))
 
     parts = []
     turn = after(at, w_other)
     for weights in (
-        [out_weight, w_near],
+        [out_weight] + w_near,
         [w_far, w_other],
     ):
-        send, kept = project(turn, near, far, [(w[None], lambda at: 0) for w in weights])
+        send, kept = project(turn, near, far, weights, out_weight.shape[1])
         got = head_perm(send, 1)
         piece = struct(send.shape[:1] + send.shape[3:], BF16)
         stay, to_y, to_x, to_xy = whole_call(split_kernel, at, [kept, got], [piece] * 4, "split", 2)

time: 194 us -> 221 us (1.14)
  waiting for transfers between devices: 85.7 us -> 107 us
  starting transfers between devices: 45.7 us -> 55.5 us
  other arithmetic: 7.82 us -> 4.56 us
    ppermute x19 -> x20, waiting for transfers between devices: 58.1 us -> 90.9 us  [seq_perm(): return lax.ppermute(array, 'seq', pairs)]
    ppermute x19 -> x20, starting transfers between devices: 33.8 us -> 48.7 us  [seq_perm(): return lax.ppermute(array, 'seq', pairs)]
    pallas_call x2 -> x0, Pallas kernels: 8.51 us -> none  [project(): pl.pallas_call(functools.partial(project_kernel, len(near)), out_shape=[o...]
    ppermute x1 -> x0, waiting for transfers between devices: 8.38 us -> none  [body_eight(): low_o = lax.ppermute(jnp.where(z == 0, kv_give, block), 'seq', pairs)]
    pallas_call x3 -> x5, Pallas kernels: 3.32 us -> 10.8 us  [whole_call(): pl.pallas_call(kernel, out_shape=outs, in_specs=[pl.BlockSpec(memory_spac...]
    ppermute x1 -> x0, starting transfers between devices: 5.52 us -> none  [body_eight(): low_o = lax.ppermute(jnp.where(z == 0, kv_give, block), 'seq', pairs)]
    unnamed x12 -> x16, local copies, waits for them, and re-layouts: 5.84 us -> 1.08 us
    select_n x3 -> x5, other arithmetic: 7.74 us -> 3.35 us  [the longest x1 1.68 us: body_eight(): mine = jnp.where(z == 0, pieces(kv_m, c), block)]
  transfers between devices with their start and end apart: 26 -> 26, of which waited for: 12 -> 14; matrix products, arithmetic and copies ran while one was open for 4% -> 4% of each run, Pallas kernels for 17% -> 15%
where the time goes in v7:
time: 221 us; the launch traced here: 219 us
  waiting for transfers between devices  107 us (48%)
  starting transfers between devices  55.5 us (25%)
  Pallas kernels  43 us (19%)
  local copies, waits for them, and re-layouts  8.94 us (4%)
  other arithmetic  4.56 us (2%)
    ppermute x20, waiting for transfers between devices, seq_perm(): return lax.ppermute(array, 'seq', pairs)  90.9 us
    ppermute x20, starting transfers between devices, seq_perm(): return lax.ppermute(array, 'seq', pairs)  48.7 us
    pallas_call x6, Pallas kernels, head_call(): pl.pallas_call(kernel, out_shape=outs, grid_spec=pltpu.PrefetchScalarGrid...  32.3 us
    pallas_call x5, Pallas kernels, whole_call(): pl.pallas_call(kernel, out_shape=outs, in_specs=[pl.BlockSpec(memory_spac...  10.8 us
    ppermute x2, waiting for transfers between devices, body_eight(): from_xy = lax.ppermute(to_xy, ('seq', 'head'), diagonal)  8.89 us
    ppermute x4, waiting for transfers between devices, head_perm(): return lax.ppermute(array, 'head', [(i, i ^ flip) for i in range(4)])  7 us
    dynamic_slice x2, local copies, waits for them, and re-layouts, lanes(): lax.dynamic_slice(local, (lo, 0, half_of * half), (hi - lo, cols, half))  4.8 us
  transfers between devices with their start and end apart: 26, of which 14 were waited for; matrix products, arithmetic and copies ran while one was open for 4% of the time, Pallas kernels for 15%

profile of v7, /device:TPU:16, one launch (start us, length us, event | category | flops | bytes accessed | tf_op | source)
XLA Modules:
  0.0 219.1 jit_solution(14984659347297749528)
XLA Ops:
  0.0 2.2 dynamic-slice_bitcast_fusion.3
  3.6 2.6 %dynamic-slice_bitcast_fusion = (bf16[2,512,512]{2,1,0:T(8,128)(2,1)}, bf16[2,512,512]{2,1,0:T(8,128)(2,1)S(1)}) fusion(bf16[3,1,512,1024]{3,2,1,0:T(8,128)(2,1)} %param.2, s32[]{:T(128)S(6)} %select_n.102, s32[]{:T(128)S(6)} %select_n.101), kind=kLoop, calls=%fused_computation.3 | loop fusion | bytes 4194312 | tf_op jit(solution)/shard_map/dynamic_slice | solution.py:416
  6.4 9.7 %collective-permute-done = bf16[1,512,512]{2,1,0:T(8,128)(2,1)S(1)} collective-permute-done((bf16[1,512,512]{2,1,0:T(8,128)(2,1)}, bf16[1,512,512]{2,1,0:T(8,128)(2,1)S(1)}, u32[]{:S(2)}, u32[]{:S(2)}) %collective-permute-start) | collective-permute-done | bytes 524320 | tf_op jit(solution)/shard_map/ppermute | solution.py:404
  19.3 2.3 %collective-permute-start.1 = (bf16[2,512,256]{2,1,0:T(8,128)(2,1)}, bf16[2,512,256]{2,1,0:T(8,128)(2,1)}, u32[]{:S(2)}, u32[]{:S(2)}) collective-permute-start(bf16[2,512,256]{2,1,0:T(8,128)(2,1)} %get-tuple-element.76.q), channel_id=1, source_target_pairs={{16,8},{20,12},{24,16},{28,20},{17,9},{21,13},{25,17},{29,21},{18,... | collective-permute-start | bytes 1572872 | tf_op jit(solution)/shard_map/ppermute | solution.py:404
  21.6 4.3 %collective-permute-start.2 = (bf16[2,512,256]{2,1,0:T(8,128)(2,1)}, bf16[2,512,256]{2,1,0:T(8,128)(2,1)S(1)}, u32[]{:S(2)}, u32[]{:S(2)}) collective-permute-start(bf16[2,512,256]{2,1,0:T(8,128)(2,1)} %get-tuple-element.75), channel_id=1, source_target_pairs={{24,8},{28,12},{8,0},{12,4},{16,24},{20,28},{25,9},{29,13},{9,1},{... | collective-permute-start | bytes 1572872 | tf_op jit(solution)/shard_map/ppermute | solution.py:404
  30.1 6.2 %collective-permute-done.1.qa = bf16[2,512,256]{2,1,0:T(8,128)(2,1)} collective-permute-done((bf16[2,512,256]{2,1,0:T(8,128)(2,1)}, bf16[2,512,256]{2,1,0:T(8,128)(2,1)}, u32[]{:S(2)}, u32[]{:S(2)}) %collective-permute-start.1) | collective-permute-done | bytes 524320 | tf_op jit(solution)/shard_map/ppermute | solution.py:404
  36.3 10.9 %collective-permute-done.2.qb = bf16[2,512,256]{2,1,0:T(8,128)(2,1)S(1)} collective-permute-done((bf16[2,512,256]{2,1,0:T(8,128)(2,1)}, bf16[2,512,256]{2,1,0:T(8,128)(2,1)S(1)}, u32[]{:S(2)}, u32[]{:S(2)}) %collective-permute-start.2) | collective-permute-done | bytes 524320 | tf_op jit(solution)/shard_map/ppermute | solution.py:404
  49.1 4.0 %collective-permute-start.7 = (bf16[2,512,256]{2,1,0:T(8,128)(2,1)}, bf16[2,512,256]{2,1,0:T(8,128)(2,1)S(1)}, u32[]{:S(2)}, u32[]{:S(2)}) collective-permute-start(bf16[2,512,256]{2,1,0:T(8,128)(2,1)} %get-tuple-element.38), channel_id=1, source_target_pairs={{24,8},{28,12},{8,0},{12,4},{16,24},{20,28},{25,9},{29,13},{9,1},{... | collective-permute-start | bytes 1572872 | tf_op jit(solution)/shard_map/ppermute | solution.py:404
  56.1 6.7 %upper_rows.2 = (bf16[1072,256]{1,0:T(8,128)(2,1)S(1)}, bf16[1072,256]{1,0:T(8,128)(2,1)S(1)}) custom-call(s32[4]{0:T(128)S(1)} %pad_add_fusion.at, bf16[2,512,256]{2,1,0:T(8,128)(2,1)} %collective-permute-done.1.qa, bf16[2,512,256]{2,1,0:T(8,128)(2,1)S(1)} %collective-permute-done.2.qb, bf16[2,512,512]{2,1,0:T(8,128)(2,1)S(1)} %get-tuple-element.64.kv_m, ...), custom_call_target="tpu_custom_call" | custom-call | flops 7000000000 | bytes 1024 | tf_op jit(solution)/shard_map/upper_rows/pallas_call | solution.py:300
  62.8 2.5 %collective-permute-start.11 = (bf16[1072,256]{1,0:T(8,128)(2,1)S(1)}, bf16[1072,256]{1,0:T(8,128)(2,1)S(1)}, u32[]{:S(2)}, u32[]{:S(2)}) collective-permute-start(bf16[1072,256]{1,0:T(8,128)(2,1)S(1)} %get-tuple-element.35), channel_id=1, source_target_pairs={{8,16},{12,20},{16,24},{20,28},{9,17},{13,21},{17,25},{21,29},{10,... | collective-permute-start | bytes 1646600 | tf_op jit(solution)/shard_map/ppermute | solution.py:404
  66.6 6.0 %own_rows.2.own = bf16[1072,256]{1,0:T(8,128)(2,1)S(1)} custom-call(s32[4]{0:T(128)S(1)} %pad_add_fusion.at, bf16[2,512,256]{2,1,0:T(8,128)(2,1)} %get-tuple-element.76.q, bf16[2,512,512]{2,1,0:T(8,128)(2,1)S(1)} %get-tuple-element.64.kv_m, bf16[2,512,512]{2,1,0:T(8,128)(2,1)} %collective-permute-done.3.kv_o, ...), custom_call_target="tpu_custom_call" | custom-call | flops 6000000000 | bytes 1024 | tf_op jit(solution)/shard_map/own_rows/pallas_call | solution.py:300
  72.7 16.3 %collective-permute-done.7.qb = bf16[2,512,256]{2,1,0:T(8,128)(2,1)S(1)} collective-permute-done((bf16[2,512,256]{2,1,0:T(8,128)(2,1)}, bf16[2,512,256]{2,1,0:T(8,128)(2,1)S(1)}, u32[]{:S(2)}, u32[]{:S(2)}) %collective-permute-start.7) | collective-permute-done | bytes 524320 | tf_op jit(solution)/shard_map/ppermute | solution.py:404
  91.6 25.4 %collective-permute-done.11.oa = bf16[1072,256]{1,0:T(8,128)(2,1)S(1)} collective-permute-done((bf16[1072,256]{1,0:T(8,128)(2,1)S(1)}, bf16[1072,256]{1,0:T(8,128)(2,1)S(1)}, u32[]{:S(2)}, u32[]{:S(2)}) %collective-permute-start.11) | collective-permute-done | bytes 548896 | tf_op jit(solution)/shard_map/ppermute | solution.py:404
  117.0 7.3 %upper_rows.3 = (bf16[1072,256]{1,0:T(8,128)(2,1)}, bf16[1072,256]{1,0:T(8,128)(2,1)}) custom-call(s32[4]{0:T(128)S(1)} %pad_add_fusion.at, bf16[2,512,256]{2,1,0:T(8,128)(2,1)S(1)} %collective-permute-done.6.qa, bf16[2,512,256]{2,1,0:T(8,128)(2,1)S(1)} %collective-permute-done.7.qb, bf16[2,512,512]{2,1,0:T(8,128)(2,1)S(1)} %get-tuple-element.64.kv_m, ...), custom_call_target="tpu_custom_call" | custom-call | flops 7000000000 | bytes 1024 | tf_op jit(solution)/shard_map/upper_rows/pallas_call | solution.py:300
  124.4 11.7 %collective-permute-start.15 = (bf16[1072,256]{1,0:T(8,128)(2,1)}, bf16[1072,256]{1,0:T(8,128)(2,1)}, u32[]{:S(2)}, u32[]{:S(2)}) collective-permute-start(bf16[1072,256]{1,0:T(8,128)(2,1)} %get-tuple-element.43), channel_id=1, source_target_pairs={{8,16},{12,20},{16,24},{20,28},{9,17},{13,21},{17,25},{21,29},{10,... | collective-permute-start | bytes 1646600 | tf_op jit(solution)/shard_map/ppermute | solution.py:404
  137.6 6.0 %own_rows.3.own = bf16[1072,256]{1,0:T(8,128)(2,1)S(1)} custom-call(s32[4]{0:T(128)S(1)} %pad_add_fusion.at, bf16[2,512,256]{2,1,0:T(8,128)(2,1)S(1)} %copy-done.3, bf16[2,512,512]{2,1,0:T(8,128)(2,1)S(1)} %get-tuple-element.64.kv_m, bf16[2,512,512]{2,1,0:T(8,128)(2,1)} %collective-permute-done.3.kv_o, bf16[4,512,256]{2,1,0:T(8,128)(2,1)S(1)} %collective-permute-done.9.refs_0_), custom_call_target="tpu_custom_call" | custom-call | flops 6000000000 | bytes 1024 | tf_op jit(solution)/shard_map/own_rows/pallas_call | solution.py:300
  143.5 3.1 %merge.2 = bf16[2,512,256]{2,1,0:T(8,128)(2,1)} custom-call(s32[4]{0:T(128)S(1)} %pad_add_fusion.at, bf16[1072,256]{1,0:T(8,128)(2,1)S(1)} %own_rows.2.own, bf16[1072,256]{1,0:T(8,128)(2,1)S(1)} %collective-permute-done.11.oa, bf16[1072,256]{1,0:T(8,128)(2,1)S(1)} %collective-permute-done.12.ob), custom_call_target="tpu_custom_call" | custom-call | flops 2000000000 | bytes 1024 | tf_op jit(solution)/shard_map/merge/pallas_call | solution.py:300
  148.6 2.7 %collective-permute-start.13 = (bf16[1024,512]{1,0:T(8,128)(2,1)S(1)}, bf16[1024,512]{1,0:T(8,128)(2,1)}, u32[]{:S(2)}, u32[]{:S(2)}) collective-permute-start(bf16[1024,512]{1,0:T(8,128)(2,1)S(1)} %fusion.refs_4_), channel_id=1, source_target_pairs={{0,8},{4,12},{8,0},{12,4},{16,24},{20,28},{24,16},{28,20},{1,9},{5... | collective-permute-start | bytes 3145736 | tf_op jit(solution)/shard_map/ppermute | solution.py:404
  151.3 6.4 %collective-permute-done.14 = bf16[2,512,256]{2,1,0:T(8,128)(2,1)} collective-permute-done((bf16[2,512,256]{2,1,0:T(8,128)(2,1)}, bf16[2,512,256]{2,1,0:T(8,128)(2,1)}, u32[]{:S(2)}, u32[]{:S(2)}) %collective-permute-start.14) | collective-permute-done | bytes 524320 | tf_op jit(solution)/shard_map/ppermute | solution.py:404
  160.4 3.2 %merge.3 = bf16[2,512,256]{2,1,0:T(8,128)(2,1)S(1)} custom-call(s32[4]{0:T(128)S(1)} %pad_add_fusion.at, bf16[1072,256]{1,0:T(8,128)(2,1)S(1)} %copy-done.7, bf16[1072,256]{1,0:T(8,128)(2,1)} %collective-permute-done.15.oa, bf16[1072,256]{1,0:T(8,128)(2,1)} %collective-permute-done.16.ob), custom_call_target="tpu_custom_call" | custom-call | flops 2000000000 | bytes 1024 | tf_op jit(solution)/shard_map/merge/pallas_call | solution.py:300
  163.6 2.3 %collective-permute-start.17 = (bf16[2,512,256]{2,1,0:T(8,128)(2,1)S(1)}, bf16[2,512,256]{2,1,0:T(8,128)(2,1)S(1)}, u32[]{:S(2)}, u32[]{:S(2)}) collective-permute-start(bf16[2,512,256]{2,1,0:T(8,128)(2,1)S(1)} %merge.3), channel_id=1, source_target_pairs={{0,4},{4,0},{8,12},{12,8},{16,20},{20,16},{24,28},{28,24},{1,5},{5... | collective-permute-start | bytes 1572872 | tf_op jit(solution)/shard_map/ppermute | solution.py:404
  167.1 12.0 %collective-permute-done.13.refs_5_ = bf16[1024,512]{1,0:T(8,128)(2,1)} collective-permute-done((bf16[1024,512]{1,0:T(8,128)(2,1)S(1)}, bf16[1024,512]{1,0:T(8,128)(2,1)}, u32[]{:S(2)}, u32[]{:S(2)}) %collective-permute-start.13) | collective-permute-done | bytes 1048608 | tf_op jit(solution)/shard_map/ppermute | solution.py:404
  179.0 3.5 %project.2 = (bf16[2,2,2,128,512]{4,3,2,1,0:T(8,128)(2,1)S(1)}, bf16[2,2,2,128,512]{4,3,2,1,0:T(8,128)(2,1)S(1)}) custom-call(s32[4]{0:T(128)S(1)} %pad_add_fusion.at, bf16[2,2,2,128,256]{4,3,2,1,0:T(8,128)(2,1)} %bitcast.12.refs_0_, bf16[2,2,2,128,256]{4,3,2,1,0:T(8,128)(2,1)S(1)} %bitcast.26, bf16[2,2,2,128,256]{4,3,2,1,0:T(8,128)(2,1)} %bitcast.14.refs_2_, ...), custom_call_target="tpu_custom_call" | custom-call | flops 4000000000 | bytes 1024 | tf_op jit(solution)/shard_map/project/pallas_call | solution.py:349
  182.7 2.6 %collective-permute-done.18.got = bf16[2,2,2,128,512]{4,3,2,1,0:T(8,128)(2,1)S(1)} collective-permute-done((bf16[2,2,2,128,512]{4,3,2,1,0:T(8,128)(2,1)S(1)}, bf16[2,2,2,128,512]{4,3,2,1,0:T(8,128)(2,1)S(1)}, u32[]{:S(2)}, u32[]{:S(2)}) %collective-permute-start.18) | collective-permute-done | bytes 1048608 | tf_op jit(solution)/shard_map/ppermute | solution.py:410
  186.1 3.9 %project.3 = (bf16[2,2,2,128,512]{4,3,2,1,0:T(8,128)(2,1)S(1)}, bf16[2,2,2,128,512]{4,3,2,1,0:T(8,128)(2,1)S(1)}) custom-call(s32[4]{0:T(128)S(1)} %pad_add_fusion.at, bf16[2,2,2,128,256]{4,3,2,1,0:T(8,128)(2,1)} %bitcast.12.refs_0_, bf16[2,2,2,128,256]{4,3,2,1,0:T(8,128)(2,1)S(1)} %bitcast.27, bf16[2,2,2,128,256]{4,3,2,1,0:T(8,128)(2,1)} %bitcast.14.refs_2_, ...), custom_call_target="tpu_custom_call" | custom-call | flops 4000000000 | bytes 1024 | tf_op jit(solution)/shard_map/project/pallas_call | solution.py:349
  191.8 2.2 %collective-permute-start.20 = (bf16[2,128,512]{2,1,0:T(8,128)(2,1)S(1)}, bf16[2,128,512]{2,1,0:T(8,128)(2,1)S(1)}, u32[]{:S(2)}, u32[]{:S(2)}) collective-permute-start(bf16[2,128,512]{2,1,0:T(8,128)(2,1)S(1)} %get-tuple-element.54), channel_id=1, source_target_pairs={{0,4},{4,0},{8,12},{12,8},{16,20},{20,16},{24,28},{28,24},{1,5},{5... | collective-permute-start | bytes 786440 | tf_op jit(solution)/shard_map/ppermute | solution.py:404
  196.3 2.0 collective-permute-start.24
  199.4 3.4 %collective-permute-start.25 = (bf16[2,128,512]{2,1,0:T(8,128)(2,1)S(1)}, bf16[2,128,512]{2,1,0:T(8,128)(2,1)S(1)}, u32[]{:S(2)}, u32[]{:S(2)}) collective-permute-start(bf16[2,128,512]{2,1,0:T(8,128)(2,1)S(1)} %get-tuple-element.62), channel_id=1, source_target_pairs={{0,6},{1,7},{2,4},{3,5},{4,2},{5,3},{6,0},{7,1},{8,14},{9,15},{10,... | collective-permute-start | bytes 786440 | tf_op jit(solution)/shard_map/ppermute | solution.py:490
  202.8 3.9 %collective-permute-done.21.refs_3_ = bf16[2,128,512]{2,1,0:T(8,128)(2,1)S(1)} collective-permute-done((bf16[2,128,512]{2,1,0:T(8,128)(2,1)S(1)}, bf16[2,128,512]{2,1,0:T(8,128)(2,1)S(1)}, u32[]{:S(2)}, u32[]{:S(2)}) %collective-permute-start.21) | collective-permute-done | bytes 262176 | tf_op jit(solution)/shard_map/ppermute | solution.py:490
  206.7 3.3 %collective-permute-done.23.refs_5_ = bf16[2,128,512]{2,1,0:T(8,128)(2,1)S(1)} collective-permute-done((bf16[2,128,512]{2,1,0:T(8,128)(2,1)S(1)}, bf16[2,128,512]{2,1,0:T(8,128)(2,1)S(1)}, u32[]{:S(2)}, u32[]{:S(2)}) %collective-permute-start.23) | collective-permute-done | bytes 262176 | tf_op jit(solution)/shard_map/ppermute | solution.py:410
  210.0 2.3 %collective-permute-done.24.refs_6_ = bf16[2,128,512]{2,1,0:T(8,128)(2,1)S(1)} collective-permute-done((bf16[2,128,512]{2,1,0:T(8,128)(2,1)S(1)}, bf16[2,128,512]{2,1,0:T(8,128)(2,1)S(1)}, u32[]{:S(2)}, u32[]{:S(2)}) %collective-permute-start.24) | collective-permute-done | bytes 262176 | tf_op jit(solution)/shard_map/ppermute | solution.py:404
  212.4 5.0 %collective-permute-done.25.refs_7_ = bf16[2,128,512]{2,1,0:T(8,128)(2,1)S(1)} collective-permute-done((bf16[2,128,512]{2,1,0:T(8,128)(2,1)S(1)}, bf16[2,128,512]{2,1,0:T(8,128)(2,1)S(1)}, u32[]{:S(2)}, u32[]{:S(2)}) %collective-permute-start.25) | collective-permute-done | bytes 262176 | tf_op jit(solution)/shard_map/ppermute | solution.py:490
  (60 shorter events, 32.7 us)
Async XLA Ops:
  0.0 6.3 %copy-start = (bf16[1024,512]{1,0:T(8,128)(2,1)S(1)}, bf16[1024,512]{1,0:T(8,128)(2,1)}, u32[]{:S(2)}) copy-start(bf16[1024,512]{1,0:T(8,128)(2,1)} %refs_4_.1) | copy-start | bytes 3145732
  2.2 13.9 %collective-permute-start = (bf16[1,512,512]{2,1,0:T(8,128)(2,1)}, bf16[1,512,512]{2,1,0:T(8,128)(2,1)S(1)}, u32[]{:S(2)}, u32[]{:S(2)}) collective-permute-start(bf16[1,512,512]{2,1,0:T(8,128)(2,1)} %get-tuple-element.66), channel_id=1, source_target_pairs={{0,4},{4,0},{8,12},{12,8},{16,20},{20,16},{24,28},{28,24},{1,5},{5... | collective-permute-start | bytes 1572872 | tf_op jit(solution)/shard_map/ppermute | solution.py:404
  17.8 35.3 %collective-permute-start.3 = (bf16[2,512,512]{2,1,0:T(8,128)(2,1)}, bf16[2,512,512]{2,1,0:T(8,128)(2,1)}, u32[]{:S(2)}, u32[]{:S(2)}) collective-permute-start(bf16[2,512,512]{2,1,0:T(8,128)(2,1)} %get-tuple-element.34), channel_id=1, source_target_pairs={{0,4},{4,0},{8,12},{12,8},{16,20},{20,16},{24,28},{28,24},{1,5},{5... | collective-permute-start | bytes 3145736 | tf_op jit(solution)/shard_map/ppermute | solution.py:404
  19.3 17.1 %collective-permute-start.1 = (bf16[2,512,256]{2,1,0:T(8,128)(2,1)}, bf16[2,512,256]{2,1,0:T(8,128)(2,1)}, u32[]{:S(2)}, u32[]{:S(2)}) collective-permute-start(bf16[2,512,256]{2,1,0:T(8,128)(2,1)} %get-tuple-element.76.q), channel_id=1, source_target_pairs={{16,8},{20,12},{24,16},{28,20},{17,9},{21,13},{25,17},{29,21},{18,... | collective-permute-start | bytes 1572872 | tf_op jit(solution)/shard_map/ppermute | solution.py:404
  21.6 25.6 %collective-permute-start.2 = (bf16[2,512,256]{2,1,0:T(8,128)(2,1)}, bf16[2,512,256]{2,1,0:T(8,128)(2,1)S(1)}, u32[]{:S(2)}, u32[]{:S(2)}) collective-permute-start(bf16[2,512,256]{2,1,0:T(8,128)(2,1)} %get-tuple-element.75), channel_id=1, source_target_pairs={{24,8},{28,12},{8,0},{12,4},{16,24},{20,28},{25,9},{29,13},{9,1},{... | collective-permute-start | bytes 1572872 | tf_op jit(solution)/shard_map/ppermute | solution.py:404
  27.9 27.5 %collective-permute-start.5 = (bf16[2,512,256]{2,1,0:T(8,128)(2,1)}, bf16[2,512,256]{2,1,0:T(8,128)(2,1)}, u32[]{:S(2)}, u32[]{:S(2)}) collective-permute-start(bf16[2,512,256]{2,1,0:T(8,128)(2,1)} %slice.55), channel_id=1, source_target_pairs={{0,12},{4,8},{1,13},{5,9},{2,14},{6,10},{3,15},{7,11}} | collective-permute-start | bytes 1572872 | tf_op jit(solution)/shard_map/ppermute | solution.py:404
  29.3 26.1 %collective-permute-start.4 = (bf16[2,512,256]{2,1,0:T(8,128)(2,1)}, bf16[2,512,256]{2,1,0:T(8,128)(2,1)S(1)}, u32[]{:S(2)}, u32[]{:S(2)}) collective-permute-start(bf16[2,512,256]{2,1,0:T(8,128)(2,1)} %get-tuple-element.68), channel_id=1, source_target_pairs={{0,8},{4,12},{8,24},{12,28},{1,9},{5,13},{9,25},{13,29},{2,10},{6,... | collective-permute-start | bytes 1572872 | tf_op jit(solution)/shard_map/ppermute | solution.py:404
  47.2 25.4 %collective-permute-start.6 = (bf16[2,512,256]{2,1,0:T(8,128)(2,1)}, bf16[2,512,256]{2,1,0:T(8,128)(2,1)S(1)}, u32[]{:S(2)}, u32[]{:S(2)}) collective-permute-start(bf16[2,512,256]{2,1,0:T(8,128)(2,1)} %get-tuple-element.37.q), channel_id=1, source_target_pairs={{16,8},{20,12},{24,16},{28,20},{17,9},{21,13},{25,17},{29,21},{18,... | collective-permute-start | bytes 1572872 | tf_op jit(solution)/shard_map/ppermute | solution.py:404
  49.1 39.8 %collective-permute-start.7 = (bf16[2,512,256]{2,1,0:T(8,128)(2,1)}, bf16[2,512,256]{2,1,0:T(8,128)(2,1)S(1)}, u32[]{:S(2)}, u32[]{:S(2)}) collective-permute-start(bf16[2,512,256]{2,1,0:T(8,128)(2,1)} %get-tuple-element.38), channel_id=1, source_target_pairs={{24,8},{28,12},{8,0},{12,4},{16,24},{20,28},{25,9},{29,13},{9,1},{... | collective-permute-start | bytes 1572872 | tf_op jit(solution)/shard_map/ppermute | solution.py:404
  55.4 61.7 %collective-permute-start.9 = (bf16[4,512,256]{2,1,0:T(8,128)(2,1)S(1)}, bf16[4,512,256]{2,1,0:T(8,128)(2,1)S(1)}, u32[]{:S(2)}, u32[]{:S(2)}) collective-permute-start(bf16[4,512,256]{2,1,0:T(8,128)(2,1)S(1)} %pad_maximum_fusion), channel_id=1, source_target_pairs={{0,8},{4,12},{8,24},{12,28},{1,9},{5,13},{9,25},{13,29},{2,10},{6,... | collective-permute-start | bytes 3145736 | tf_op jit(solution)/shard_map/ppermute | solution.py:404
  62.8 54.2 %collective-permute-start.11 = (bf16[1072,256]{1,0:T(8,128)(2,1)S(1)}, bf16[1072,256]{1,0:T(8,128)(2,1)S(1)}, u32[]{:S(2)}, u32[]{:S(2)}) collective-permute-start(bf16[1072,256]{1,0:T(8,128)(2,1)S(1)} %get-tuple-element.35), channel_id=1, source_target_pairs={{8,16},{12,20},{16,24},{20,28},{9,17},{13,21},{17,25},{21,29},{10,... | collective-permute-start | bytes 1646600 | tf_op jit(solution)/shard_map/ppermute | solution.py:404
  65.3 51.7 %collective-permute-start.12 = (bf16[1072,256]{1,0:T(8,128)(2,1)S(1)}, bf16[1072,256]{1,0:T(8,128)(2,1)S(1)}, u32[]{:S(2)}, u32[]{:S(2)}) collective-permute-start(bf16[1072,256]{1,0:T(8,128)(2,1)S(1)} %get-tuple-element.41), channel_id=1, source_target_pairs={{8,24},{12,28},{0,8},{4,12},{24,16},{28,20},{9,25},{13,29},{1,9},{... | collective-permute-start | bytes 1646600 | tf_op jit(solution)/shard_map/ppermute | solution.py:404
  72.6 64.9 %copy-start.3 = (bf16[2,512,256]{2,1,0:T(8,128)(2,1)S(1)}, bf16[2,512,256]{2,1,0:T(8,128)(2,1)}, u32[]{:S(2)}) copy-start(bf16[2,512,256]{2,1,0:T(8,128)(2,1)} %get-tuple-element.37.q) | copy-start | bytes 1572868
  89.0 35.4 %copy-start.1 = (bf16[2,512,256]{2,1,0:T(8,128)(2,1)}, bf16[2,512,256]{2,1,0:T(8,128)(2,1)S(1)}, u32[]{:S(2)}) copy-start(bf16[2,512,256]{2,1,0:T(8,128)(2,1)S(1)} %collective-permute-done.7.qb) | copy-start | bytes 1572868
  89.0 59.1 %collective-permute-start.10 = (bf16[1024,512]{1,0:T(8,128)(2,1)S(1)}, bf16[1024,512]{1,0:T(8,128)(2,1)S(1)}, u32[]{:S(2)}, u32[]{:S(2)}) collective-permute-start(bf16[1024,512]{1,0:T(8,128)(2,1)S(1)} %copy-done), channel_id=1, source_target_pairs={{16,0},{20,4},{24,8},{28,12},{17,1},{21,5},{25,9},{29,13},{18,2},{... | collective-permute-start | bytes 3145736 | tf_op jit(solution)/shard_map/ppermute | solution.py:404
  90.3 57.8 %collective-permute-start.8 = (bf16[1024,512]{1,0:T(8,128)(2,1)S(1)}, bf16[1024,512]{1,0:T(8,128)(2,1)S(1)}, u32[]{:S(2)}, u32[]{:S(2)}) collective-permute-start(bf16[1024,512]{1,0:T(8,128)(2,1)S(1)} %copy-done), channel_id=1, source_target_pairs={{0,16},{4,20},{1,17},{5,21},{2,18},{6,22},{3,19},{7,23}} | collective-permute-start | bytes 3145736 | tf_op jit(solution)/shard_map/ppermute | solution.py:404
  117.0 26.5 %copy-start.4 = (bf16[1072,256]{1,0:T(8,128)(2,1)}, bf16[1072,256]{1,0:T(8,128)(2,1)S(1)}, u32[]{:S(2)}) copy-start(bf16[1072,256]{1,0:T(8,128)(2,1)S(1)} %collective-permute-done.12.ob) | copy-start | bytes 1646596
  124.4 35.0 %collective-permute-start.15 = (bf16[1072,256]{1,0:T(8,128)(2,1)}, bf16[1072,256]{1,0:T(8,128)(2,1)}, u32[]{:S(2)}, u32[]{:S(2)}) collective-permute-start(bf16[1072,256]{1,0:T(8,128)(2,1)} %get-tuple-element.43), channel_id=1, source_target_pairs={{8,16},{12,20},{16,24},{20,28},{9,17},{13,21},{17,25},{21,29},{10,... | collective-permute-start | bytes 1646600 | tf_op jit(solution)/shard_map/ppermute | solution.py:404
  136.1 21.6 %collective-permute-start.16 = (bf16[1072,256]{1,0:T(8,128)(2,1)}, bf16[1072,256]{1,0:T(8,128)(2,1)}, u32[]{:S(2)}, u32[]{:S(2)}) collective-permute-start(bf16[1072,256]{1,0:T(8,128)(2,1)} %get-tuple-element.49), channel_id=1, source_target_pairs={{8,24},{12,28},{0,8},{4,12},{24,16},{28,20},{9,25},{13,29},{1,9},{... | collective-permute-start | bytes 1646600 | tf_op jit(solution)/shard_map/ppermute | solution.py:404
  146.6 11.0 %collective-permute-start.14 = (bf16[2,512,256]{2,1,0:T(8,128)(2,1)}, bf16[2,512,256]{2,1,0:T(8,128)(2,1)}, u32[]{:S(2)}, u32[]{:S(2)}) collective-permute-start(bf16[2,512,256]{2,1,0:T(8,128)(2,1)} %merge.2), channel_id=1, source_target_pairs={{0,4},{4,0},{8,12},{12,8},{16,20},{20,16},{24,28},{28,24},{1,5},{5... | collective-permute-start | bytes 1572872 | tf_op jit(solution)/shard_map/ppermute | solution.py:404
  148.6 30.5 %collective-permute-start.13 = (bf16[1024,512]{1,0:T(8,128)(2,1)S(1)}, bf16[1024,512]{1,0:T(8,128)(2,1)}, u32[]{:S(2)}, u32[]{:S(2)}) collective-permute-start(bf16[1024,512]{1,0:T(8,128)(2,1)S(1)} %fusion.refs_4_), channel_id=1, source_target_pairs={{0,8},{4,12},{8,0},{12,4},{16,24},{20,28},{24,16},{28,20},{1,9},{5... | collective-permute-start | bytes 3145736 | tf_op jit(solution)/shard_map/ppermute | solution.py:404
  151.3 14.6 %copy-start.5 = (bf16[1072,256]{1,0:T(8,128)(2,1)S(1)}, bf16[1072,256]{1,0:T(8,128)(2,1)}, u32[]{:S(2)}) copy-start(bf16[1072,256]{1,0:T(8,128)(2,1)} %copy-done.4) | copy-start | bytes 1646596
  151.3 14.7 %copy-start.2 = (bf16[2,512,256]{2,1,0:T(8,128)(2,1)S(1)}, bf16[2,512,256]{2,1,0:T(8,128)(2,1)}, u32[]{:S(2)}) copy-start(bf16[2,512,256]{2,1,0:T(8,128)(2,1)} %copy-done.1) | copy-start | bytes 1572868
  163.6 15.5 %collective-permute-start.17 = (bf16[2,512,256]{2,1,0:T(8,128)(2,1)S(1)}, bf16[2,512,256]{2,1,0:T(8,128)(2,1)S(1)}, u32[]{:S(2)}, u32[]{:S(2)}) collective-permute-start(bf16[2,512,256]{2,1,0:T(8,128)(2,1)S(1)} %merge.3), channel_id=1, source_target_pairs={{0,4},{4,0},{8,12},{12,8},{16,20},{20,16},{24,28},{28,24},{1,5},{5... | collective-permute-start | bytes 1572872 | tf_op jit(solution)/shard_map/ppermute | solution.py:404
  182.6 2.7 %collective-permute-start.18 = (bf16[2,2,2,128,512]{4,3,2,1,0:T(8,128)(2,1)S(1)}, bf16[2,2,2,128,512]{4,3,2,1,0:T(8,128)(2,1)S(1)}, u32[]{:S(2)}, u32[]{:S(2)}) collective-permute-start(bf16[2,2,2,128,512]{4,3,2,1,0:T(8,128)(2,1)S(1)} %get-tuple-element.51), channel_id=1, source_target_pairs={{0,1},{1,0},{2,3},{3,2},{4,5},{5,4},{6,7},{7,6},{8,9},{9,8},{10,11... | collective-permute-start | bytes 3145736 | tf_op jit(solution)/shard_map/ppermute | solution.py:410
  190.0 4.0 %collective-permute-start.22 = (bf16[2,2,2,128,512]{4,3,2,1,0:T(8,128)(2,1)S(1)}, bf16[2,2,2,128,512]{4,3,2,1,0:T(8,128)(2,1)S(1)}, u32[]{:S(2)}, u32[]{:S(2)}) collective-permute-start(bf16[2,2,2,128,512]{4,3,2,1,0:T(8,128)(2,1)S(1)} %get-tuple-element.58), channel_id=1, source_target_pairs={{0,1},{1,0},{2,3},{3,2},{4,5},{5,4},{6,7},{7,6},{8,9},{9,8},{10,11... | collective-permute-start | bytes 3145736 | tf_op jit(solution)/shard_map/ppermute | solution.py:410
  190.2 9.1 %collective-permute-start.19 = (bf16[2,128,512]{2,1,0:T(8,128)(2,1)S(1)}, bf16[2,128,512]{2,1,0:T(8,128)(2,1)S(1)}, u32[]{:S(2)}, u32[]{:S(2)}) collective-permute-start(bf16[2,128,512]{2,1,0:T(8,128)(2,1)S(1)} %get-tuple-element.53), channel_id=1, source_target_pairs={{0,2},{1,3},{2,0},{3,1},{4,6},{5,7},{6,4},{7,5},{8,10},{9,11},{10,... | collective-permute-start | bytes 786440 | tf_op jit(solution)/shard_map/ppermute | solution.py:410
  191.8 11.1 %collective-permute-start.20 = (bf16[2,128,512]{2,1,0:T(8,128)(2,1)S(1)}, bf16[2,128,512]{2,1,0:T(8,128)(2,1)S(1)}, u32[]{:S(2)}, u32[]{:S(2)}) collective-permute-start(bf16[2,128,512]{2,1,0:T(8,128)(2,1)S(1)} %get-tuple-element.54), channel_id=1, source_target_pairs={{0,4},{4,0},{8,12},{12,8},{16,20},{20,16},{24,28},{28,24},{1,5},{5... | collective-permute-start | bytes 786440 | tf_op jit(solution)/shard_map/ppermute | solution.py:404
  194.0 12.7 %collective-permute-start.21 = (bf16[2,128,512]{2,1,0:T(8,128)(2,1)S(1)}, bf16[2,128,512]{2,1,0:T(8,128)(2,1)S(1)}, u32[]{:S(2)}, u32[]{:S(2)}) collective-permute-start(bf16[2,128,512]{2,1,0:T(8,128)(2,1)S(1)} %get-tuple-element.55), channel_id=1, source_target_pairs={{0,6},{1,7},{2,4},{3,5},{4,2},{5,3},{6,0},{7,1},{8,14},{9,15},{10,... | collective-permute-start | bytes 786440 | tf_op jit(solution)/shard_map/ppermute | solution.py:490
  194.8 15.2 %collective-permute-start.23 = (bf16[2,128,512]{2,1,0:T(8,128)(2,1)S(1)}, bf16[2,128,512]{2,1,0:T(8,128)(2,1)S(1)}, u32[]{:S(2)}, u32[]{:S(2)}) collective-permute-start(bf16[2,128,512]{2,1,0:T(8,128)(2,1)S(1)} %get-tuple-element.60), channel_id=1, source_target_pairs={{0,2},{1,3},{2,0},{3,1},{4,6},{5,7},{6,4},{7,5},{8,10},{9,11},{10,... | collective-permute-start | bytes 786440 | tf_op jit(solution)/shard_map/ppermute | solution.py:410
  196.3 16.1 %collective-permute-start.24 = (bf16[2,128,512]{2,1,0:T(8,128)(2,1)S(1)}, bf16[2,128,512]{2,1,0:T(8,128)(2,1)S(1)}, u32[]{:S(2)}, u32[]{:S(2)}) collective-permute-start(bf16[2,128,512]{2,1,0:T(8,128)(2,1)S(1)} %get-tuple-element.61), channel_id=1, source_target_pairs={{0,4},{4,0},{8,12},{12,8},{16,20},{20,16},{24,28},{28,24},{1,5},{5... | collective-permute-start | bytes 786440 | tf_op jit(solution)/shard_map/ppermute | solution.py:404
  199.4 18.0 %collective-permute-start.25 = (bf16[2,128,512]{2,1,0:T(8,128)(2,1)S(1)}, bf16[2,128,512]{2,1,0:T(8,128)(2,1)S(1)}, u32[]{:S(2)}, u32[]{:S(2)}) collective-permute-start(bf16[2,128,512]{2,1,0:T(8,128)(2,1)S(1)} %get-tuple-element.62), channel_id=1, source_target_pairs={{0,6},{1,7},{2,4},{3,5},{4,2},{5,3},{6,0},{7,1},{8,14},{9,15},{10,... | collective-permute-start | bytes 786440 | tf_op jit(solution)/shard_map/ppermute | solution.py:490
  (2 other events, 4.1 us)

commit v8 on v7

--- a/solution.py
+++ b/solution.py
@@ -419,43 +419,43 @@
         return array[..., c * width : (c + 1) * width]
 
     q_m, q_o = lanes(0, 1, x), swap(lanes(0, 1, 1 - x))
+    w_second = seq_perm(out_weight, (0, 2))
     kv_m, kv_give = lanes(1, 3, x), lanes(1, 3, 1 - x)
     q, qs, low = [], [], []
     for c in range(chunks):
         a, b = pieces(q_m, c), pieces(q_o, c)
         q.append(jnp.concatenate([jnp.where(first, a, b), jnp.where(first, b, a)]))
         block = pieces(out_weight, c).reshape(q[c].shape)
-        going = [q[c], jnp.where(z == 3, q[c], block)]
+        going = [jnp.where(z == 1, block, q[c]), jnp.where(z == 3, q[c], block)]
         if c:
             going = after(going, *qs[0])
+        qs.append([seq_perm(going[0], (2, 1), (3, 2), (1, 3)), seq_perm(going[1], (3, 1), (1, 0), (2, 3))])
+        if c == 0:
+            kv_o = swap(after(kv_give, q[0]))
+            ups = after([pieces(kv_m, c), pieces(kv_give, c)], w_second)
+            low.append([seq_perm(ups[0], (0, 1)), seq_perm(ups[1], (0, 1), cross=True)])
         else:
-            kv_o = swap(after(kv_give, q[0]))
-        qs.append([seq_perm(going[0], (2, 1), (3, 2)), seq_perm(going[1], (3, 1), (1, 0), (2, 3))])
-        mine = jnp.where(z == 0, pieces(kv_m, c), block)
-        if c:
-            low.append([seq_perm(after(jnp.concatenate([mine, pieces(kv_o, c)]), *low[0]), (0, 1), (1, 3))])
-        else:
-            low.append([seq_perm(mine, (0, 1), (1, 3)), seq_perm(pieces(kv_give, c), (0, 1), cross=True)])
+            up = jnp.concatenate([pieces(kv_m, c), pieces(kv_o, c)])
+            low.append([seq_perm(after(up, *low[0]), (0, 1))])
 
     struct = jax.ShapeDtypeStruct
     partial = struct((2 * cols + lse_height(cols), width), BF16)
     oa, ob, own, sent = [], [], [], []
     turn = at
     for c in range(chunks):
-        kvs = [(a, c * heads) for a in (kv_m, kv_o)]
+        pair = [(kv_m, c * heads), (kv_o, c * heads)]
         a, b = head_call(
             functools.partial(upper_kernel, coef, cols), turn,
-            [(a, 0) for a in qs[c]] + kvs + [(a, 0) for a in low[c]] + [(out_weight, c * heads)], [partial] * 2, heads, "upper_rows", 7)
+            [(a, 0) for a in qs[c]] + pair + [(a, 0) for a in low[c]] + [(out_weight, c * heads)], [partial] * 2, heads, "upper_rows", 7)
         sent.append(a)
         oa.append(seq_perm(a, (1, 2), (2, 3)))
         ob.append(seq_perm(b, (1, 3), (0, 1), (3, 2)))
         (mine,) = head_call(
-            functools.partial(own_kernel, coef, cols), after(at, a), [(q[c], 0)] + kvs + [(a, 0) for a in low[c]],
+            functools.partial(own_kernel, coef, cols), after(at, a), [(q[c], 0)] + pair + [(a, 0) for a in low[c]],
             [partial], heads, "own_rows", 6)
         own.append(mine)
-        turn = after(at, mine, oa[c], ob[c])
-
-    w_second = seq_perm(after(out_weight, own[0], *qs[1]), (0, 2))
+        turn = after(at, mine)
+
     depth = out_weight.shape[0]
     w_down = seq_perm(after(out_weight, own[0], *qs[1]), (2, 0), (3, 1))
     w_near = [
@@ -469,7 +469,7 @@
         return a, swap(a)
 
     first_half = merged(0, own[1])
-    w_ridden = jnp.concatenate([low[c][0][:2].reshape(depth, width) for c in range(chunks)], axis=1)
+    w_ridden = jnp.concatenate([qs[c][0].reshape(depth, width) for c in range(chunks)], axis=1)
     w_far = jnp.where(
         z >= 2, jnp.where(z == 2, w_second, w_ridden), after(w_down, first_half[0], own[1]))
     near, far = map(list, zip(first_half, merged(1, (w_far, first_half[1]))))
@@ -484,7 +484,8 @@
         send, kept = project(turn, near, far, weights, out_weight.shape[1])
         got = head_perm(send, 1)
         piece = struct(send.shape[:1] + send.shape[3:], BF16)
-        stay, to_y, to_x, to_xy = whole_call(split_kernel, at, [kept, got], [piece] * 4, "split", 2)
+        stay, to_y, to_x, to_xy = whole_call(
+            split_kernel, after(at, parts[1:2]), [kept, got], [piece] * 4, "split", 2)
         turn = after(at, stay)
         diagonal = [((2 * i + j) * 4 + h, (2 * i + 1 - j) * 4 + (h ^ 2)) for i in range(4) for j in range(2) for h in range(4)]
         from_xy = lax.ppermute(to_xy, ("seq", "head"), diagonal)

time: 221 us -> 189 us (0.86)
  the two profiles are of different devices: /device:TPU:16 before, /device:TPU:0 now
where the time goes in v8:
time: 189 us; the launch traced here: 188 us
  waiting for transfers between devices  83.4 us (44%)
  starting transfers between devices  45.6 us (24%)
  Pallas kernels  42.9 us (23%)
  local copies, waits for them, and re-layouts  9.9 us (5%)
  other arithmetic  5.9 us (3%)
    ppermute x20, waiting for transfers between devices, seq_perm(): return lax.ppermute(array, 'seq', pairs)  62.1 us
    ppermute x20, starting transfers between devices, seq_perm(): return lax.ppermute(array, 'seq', pairs)  39.3 us
    pallas_call x6, Pallas kernels, head_call(): pl.pallas_call(kernel, out_shape=outs, grid_spec=pltpu.PrefetchScalarGrid...  32.1 us
    ppermute x4, waiting for transfers between devices, head_perm(): return lax.ppermute(array, 'head', [(i, i ^ flip) for i in range(4)])  13.3 us
    pallas_call x5, Pallas kernels, whole_call(): pl.pallas_call(kernel, out_shape=outs, in_specs=[pl.BlockSpec(memory_spac...  10.8 us
    ppermute x2, waiting for transfers between devices, body_eight(): from_xy = lax.ppermute(to_xy, ('seq', 'head'), diagonal)  8.06 us
    dynamic_slice x2, local copies, waits for them, and re-layouts, lanes(): lax.dynamic_slice(local, (lo, 0, half_of * half), (hi - lo, cols, half))  4.8 us
    slice x4, local copies, waits for them, and re-layouts, pieces(): return array[..., c * width:(c + 1) * width]  3.95 us
  transfers between devices with their start and end apart: 26, of which 15 were waited for; matrix products, arithmetic and copies ran while one was open for 7% of the time, Pallas kernels for 17%

profile of v8, /device:TPU:0, one launch (start us, length us, event | category | flops | bytes accessed | tf_op | source)
XLA Modules:
  0.0 188.0 jit_solution(3825866473162803512)
XLA Ops:
  0.0 2.2 %dynamic-slice_bitcast_fusion.3 = (bf16[1,512,512]{2,1,0:T(8,128)(2,1)S(1)}, bf16[1,512,512]{2,1,0:T(8,128)(2,1)}) fusion(bf16[3,1,512,1024]{3,2,1,0:T(8,128)(2,1)} %param.2, s32[]{:T(128)S(6)} %select_n.102, s32[]{:T(128)S(6)} %select_n.103), kind=kLoop, calls=%fused_computation.10 | loop fusion | bytes 2097160 | tf_op jit(solution)/shard_map/dynamic_slice | solution.py:416
  2.2 2.9 %collective-permute-start.1 = (bf16[1,512,512]{2,1,0:T(8,128)(2,1)}, bf16[1,512,512]{2,1,0:T(8,128)(2,1)}, u32[]{:S(2)}, u32[]{:S(2)}) collective-permute-start(bf16[1,512,512]{2,1,0:T(8,128)(2,1)} %get-tuple-element.72), channel_id=1, source_target_pairs={{0,4},{4,0},{8,12},{12,8},{16,20},{20,16},{24,28},{28,24},{1,5},{5... | collective-permute-start | bytes 1572872 | tf_op jit(solution)/shard_map/ppermute | solution.py:404
  5.1 5.5 %collective-permute-start = (bf16[1024,512]{1,0:T(8,128)(2,1)}, bf16[1024,512]{1,0:T(8,128)(2,1)}, u32[]{:S(2)}, u32[]{:S(2)}) collective-permute-start(bf16[1024,512]{1,0:T(8,128)(2,1)} %refs_4_.1), channel_id=1, source_target_pairs={{0,16},{4,20},{1,17},{5,21},{2,18},{6,22},{3,19},{7,23}} | collective-permute-start | bytes 3145736 | tf_op jit(solution)/shard_map/ppermute | solution.py:404
  10.6 2.6 %dynamic-slice_bitcast_fusion = (bf16[2,512,512]{2,1,0:T(8,128)(2,1)}, bf16[2,512,512]{2,1,0:T(8,128)(2,1)S(1)}) fusion(bf16[3,1,512,1024]{3,2,1,0:T(8,128)(2,1)} %param.2, s32[]{:T(128)S(6)} %select_n.103, s32[]{:T(128)S(6)} %select_n.102), kind=kLoop, calls=%fused_computation.3 | loop fusion | bytes 4194312 | tf_op jit(solution)/shard_map/dynamic_slice | solution.py:416
  14.1 3.2 %collective-permute-done.1 = bf16[1,512,512]{2,1,0:T(8,128)(2,1)} collective-permute-done((bf16[1,512,512]{2,1,0:T(8,128)(2,1)}, bf16[1,512,512]{2,1,0:T(8,128)(2,1)}, u32[]{:S(2)}, u32[]{:S(2)}) %collective-permute-start.1) | collective-permute-done | bytes 524320 | tf_op jit(solution)/shard_map/ppermute | solution.py:404
  17.3 1.8 broadcast_select_fusion.5
  20.3 1.7 collective-permute-start.5
  22.0 1.9 %slice.53 = bf16[2,512,256]{2,1,0:T(8,128)(2,1)} slice(bf16[2,512,512]{2,1,0:T(8,128)(2,1)} %get-tuple-element.38), slice={[0:2], [0:512], [0:256]} | slice | bytes 1048576 | tf_op jit(solution)/shard_map/slice | solution.py:419
  26.0 6.1 %collective-permute-done = bf16[1024,512]{1,0:T(8,128)(2,1)} collective-permute-done((bf16[1024,512]{1,0:T(8,128)(2,1)}, bf16[1024,512]{1,0:T(8,128)(2,1)}, u32[]{:S(2)}, u32[]{:S(2)}) %collective-permute-start) | collective-permute-done | bytes 1048608 | tf_op jit(solution)/shard_map/ppermute | solution.py:404
  32.1 1.9 %collective-permute-start.6 = (bf16[2,512,256]{2,1,0:T(8,128)(2,1)S(1)}, bf16[2,512,256]{2,1,0:T(8,128)(2,1)S(1)}, u32[]{:S(2)}, u32[]{:S(2)}) collective-permute-start(bf16[2,512,256]{2,1,0:T(8,128)(2,1)S(1)} %get-tuple-element.39), channel_id=1, source_target_pairs={{0,8},{4,12},{1,9},{5,13},{2,10},{6,14},{3,11},{7,15}} | collective-permute-start | bytes 1572872 | tf_op jit(solution)/shard_map/ppermute | solution.py:404
  36.6 6.0 %collective-permute-done.3.qb = bf16[2,512,256]{2,1,0:T(8,128)(2,1)S(1)} collective-permute-done((bf16[2,512,256]{2,1,0:T(8,128)(2,1)}, bf16[2,512,256]{2,1,0:T(8,128)(2,1)S(1)}, u32[]{:S(2)}, u32[]{:S(2)}) %collective-permute-start.3) | collective-permute-done | bytes 524320 | tf_op jit(solution)/shard_map/ppermute | solution.py:404
  46.3 8.8 %collective-permute-done.7.refs_1_ = bf16[2,512,256]{2,1,0:T(8,128)(2,1)S(1)} collective-permute-done((bf16[2,512,256]{2,1,0:T(8,128)(2,1)}, bf16[2,512,256]{2,1,0:T(8,128)(2,1)S(1)}, u32[]{:S(2)}, u32[]{:S(2)}) %collective-permute-start.7) | collective-permute-done | bytes 524320 | tf_op jit(solution)/shard_map/ppermute | solution.py:404
  55.0 7.9 %collective-permute-start.10 = (bf16[4,512,256]{2,1,0:T(8,128)(2,1)S(1)}, bf16[4,512,256]{2,1,0:T(8,128)(2,1)S(1)}, u32[]{:S(2)}, u32[]{:S(2)}) collective-permute-start(bf16[4,512,256]{2,1,0:T(8,128)(2,1)S(1)} %pad_maximum_fusion), channel_id=1, source_target_pairs={{0,8},{4,12},{1,9},{5,13},{2,10},{6,14},{3,11},{7,15}} | collective-permute-start | bytes 3145736 | tf_op jit(solution)/shard_map/ppermute | solution.py:404
  62.9 6.6 %upper_rows.2 = (bf16[1072,256]{1,0:T(8,128)(2,1)S(1)}, bf16[1072,256]{1,0:T(8,128)(2,1)S(1)}) custom-call(s32[4]{0:T(128)S(1)} %pad_add_fusion.at, bf16[2,512,256]{2,1,0:T(8,128)(2,1)S(1)} %collective-permute-done.2.qa, bf16[2,512,256]{2,1,0:T(8,128)(2,1)S(1)} %collective-permute-done.3.qb, bf16[2,512,512]{2,1,0:T(8,128)(2,1)S(1)} %get-tuple-element.70.kv_m, ...), custom_call_target="tpu_custom_call" | custom-call | flops 7000000000 | bytes 1024 | tf_op jit(solution)/shard_map/upper_rows/pallas_call | solution.py:300
  70.3 5.9 %own_rows.2.own = bf16[1072,256]{1,0:T(8,128)(2,1)S(1)} custom-call(s32[4]{0:T(128)S(1)} %pad_add_fusion.at, bf16[2,512,256]{2,1,0:T(8,128)(2,1)S(1)} %get-tuple-element.86.q, bf16[2,512,512]{2,1,0:T(8,128)(2,1)S(1)} %get-tuple-element.70.kv_m, bf16[2,512,512]{2,1,0:T(8,128)(2,1)} %collective-permute-done.5.kv_o, ...), custom_call_target="tpu_custom_call" | custom-call | flops 6000000000 | bytes 1024 | tf_op jit(solution)/shard_map/own_rows/pallas_call | solution.py:300
  76.2 2.5 %collective-permute-start.12 = (bf16[1072,256]{1,0:T(8,128)(2,1)S(1)}, bf16[1072,256]{1,0:T(8,128)(2,1)S(1)}, u32[]{:S(2)}, u32[]{:S(2)}) collective-permute-start(bf16[1072,256]{1,0:T(8,128)(2,1)S(1)} %get-tuple-element.50), channel_id=1, source_target_pairs={{8,24},{12,28},{0,8},{4,12},{24,16},{28,20},{9,25},{13,29},{1,9},{... | collective-permute-start | bytes 1646600 | tf_op jit(solution)/shard_map/ppermute | solution.py:404
  80.1 6.4 %collective-permute-done.10.refs_0_ = bf16[4,512,256]{2,1,0:T(8,128)(2,1)S(1)} collective-permute-done((bf16[4,512,256]{2,1,0:T(8,128)(2,1)S(1)}, bf16[4,512,256]{2,1,0:T(8,128)(2,1)S(1)}, u32[]{:S(2)}, u32[]{:S(2)}) %collective-permute-start.10) | collective-permute-done | bytes 1048608 | tf_op jit(solution)/shard_map/ppermute | solution.py:404
  86.5 7.3 %upper_rows.3 = (bf16[1072,256]{1,0:T(8,128)(2,1)}, bf16[1072,256]{1,0:T(8,128)(2,1)}) custom-call(s32[4]{0:T(128)S(1)} %pad_add_fusion.at, bf16[2,512,256]{2,1,0:T(8,128)(2,1)S(1)} %collective-permute-done.4.qa, bf16[2,512,256]{2,1,0:T(8,128)(2,1)S(1)} %collective-permute-done.8.qb, bf16[2,512,512]{2,1,0:T(8,128)(2,1)S(1)} %get-tuple-element.70.kv_m, ...), custom_call_target="tpu_custom_call" | custom-call | flops 7000000000 | bytes 1024 | tf_op jit(solution)/shard_map/upper_rows/pallas_call | solution.py:300
  95.3 5.8 %collective-permute-start.16 = (bf16[1072,256]{1,0:T(8,128)(2,1)}, bf16[1072,256]{1,0:T(8,128)(2,1)}, u32[]{:S(2)}, u32[]{:S(2)}) collective-permute-start(bf16[1072,256]{1,0:T(8,128)(2,1)} %get-tuple-element.54), channel_id=1, source_target_pairs={{8,24},{12,28},{0,8},{4,12},{24,16},{28,20},{9,25},{13,29},{1,9},{... | collective-permute-start | bytes 1646600 | tf_op jit(solution)/shard_map/ppermute | solution.py:404
  101.1 6.0 %own_rows.3.own = bf16[1072,256]{1,0:T(8,128)(2,1)S(1)} custom-call(s32[4]{0:T(128)S(1)} %pad_add_fusion.at, bf16[2,512,256]{2,1,0:T(8,128)(2,1)S(1)} %get-tuple-element.85.q, bf16[2,512,512]{2,1,0:T(8,128)(2,1)S(1)} %get-tuple-element.70.kv_m, bf16[2,512,512]{2,1,0:T(8,128)(2,1)} %collective-permute-done.5.kv_o, ...), custom_call_target="tpu_custom_call" | custom-call | flops 6000000000 | bytes 1024 | tf_op jit(solution)/shard_map/own_rows/pallas_call | solution.py:300
  107.1 3.1 %merge.2 = bf16[2,512,256]{2,1,0:T(8,128)(2,1)} custom-call(s32[4]{0:T(128)S(1)} %pad_add_fusion.at, bf16[1072,256]{1,0:T(8,128)(2,1)S(1)} %own_rows.2.own, bf16[1072,256]{1,0:T(8,128)(2,1)S(1)} %collective-permute-done.11.oa, bf16[1072,256]{1,0:T(8,128)(2,1)S(1)} %collective-permute-done.12.ob), custom_call_target="tpu_custom_call" | custom-call | flops 2000000000 | bytes 1024 | tf_op jit(solution)/shard_map/merge/pallas_call | solution.py:300
  110.7 15.2 %collective-permute-done.9 = bf16[1024,512]{1,0:T(8,128)(2,1)S(1)} collective-permute-done((bf16[1024,512]{1,0:T(8,128)(2,1)S(1)}, bf16[1024,512]{1,0:T(8,128)(2,1)S(1)}, u32[]{:S(2)}, u32[]{:S(2)}) %collective-permute-start.9) | collective-permute-done | bytes 1048608 | tf_op jit(solution)/shard_map/ppermute | solution.py:404
  127.6 3.2 %merge.3 = bf16[2,512,256]{2,1,0:T(8,128)(2,1)S(1)} custom-call(s32[4]{0:T(128)S(1)} %pad_add_fusion.at, bf16[1072,256]{1,0:T(8,128)(2,1)S(1)} %copy-done.6, bf16[1072,256]{1,0:T(8,128)(2,1)} %collective-permute-done.15.oa, bf16[1072,256]{1,0:T(8,128)(2,1)} %collective-permute-done.16.ob), custom_call_target="tpu_custom_call" | custom-call | flops 2000000000 | bytes 1024 | tf_op jit(solution)/shard_map/merge/pallas_call | solution.py:300
  132.6 15.8 %collective-permute-done.13.refs_5_ = bf16[1024,512]{1,0:T(8,128)(2,1)} collective-permute-done((bf16[1024,512]{1,0:T(8,128)(2,1)S(1)}, bf16[1024,512]{1,0:T(8,128)(2,1)}, u32[]{:S(2)}, u32[]{:S(2)}) %collective-permute-start.13) | collective-permute-done | bytes 1048608 | tf_op jit(solution)/shard_map/ppermute | solution.py:404
  148.4 3.5 %project.2 = (bf16[2,2,2,128,512]{4,3,2,1,0:T(8,128)(2,1)S(1)}, bf16[2,2,2,128,512]{4,3,2,1,0:T(8,128)(2,1)S(1)}) custom-call(s32[4]{0:T(128)S(1)} %pad_add_fusion.at, bf16[2,2,2,128,256]{4,3,2,1,0:T(8,128)(2,1)} %bitcast.12.refs_0_, bf16[2,2,2,128,256]{4,3,2,1,0:T(8,128)(2,1)S(1)} %bitcast.27, bf16[2,2,2,128,256]{4,3,2,1,0:T(8,128)(2,1)} %bitcast.14.refs_2_, ...), custom_call_target="tpu_custom_call" | custom-call | flops 4000000000 | bytes 1024 | tf_op jit(solution)/shard_map/project/pallas_call | solution.py:349
  152.0 2.6 %collective-permute-done.18.got = bf16[2,2,2,128,512]{4,3,2,1,0:T(8,128)(2,1)S(1)} collective-permute-done((bf16[2,2,2,128,512]{4,3,2,1,0:T(8,128)(2,1)S(1)}, bf16[2,2,2,128,512]{4,3,2,1,0:T(8,128)(2,1)S(1)}, u32[]{:S(2)}, u32[]{:S(2)}) %collective-permute-start.18) | collective-permute-done | bytes 1048608 | tf_op jit(solution)/shard_map/ppermute | solution.py:410
  155.4 3.9 %project.3 = (bf16[2,2,2,128,512]{4,3,2,1,0:T(8,128)(2,1)S(1)}, bf16[2,2,2,128,512]{4,3,2,1,0:T(8,128)(2,1)S(1)}) custom-call(s32[4]{0:T(128)S(1)} %pad_add_fusion.at, bf16[2,2,2,128,256]{4,3,2,1,0:T(8,128)(2,1)} %bitcast.12.refs_0_, bf16[2,2,2,128,256]{4,3,2,1,0:T(8,128)(2,1)S(1)} %bitcast.28, bf16[2,2,2,128,256]{4,3,2,1,0:T(8,128)(2,1)} %bitcast.14.refs_2_, ...), custom_call_target="tpu_custom_call" | custom-call | flops 4000000000 | bytes 1024 | tf_op jit(solution)/shard_map/project/pallas_call | solution.py:349
  163.1 5.1 %collective-permute-done.19.refs_1_ = bf16[2,128,512]{2,1,0:T(8,128)(2,1)S(1)} collective-permute-done((bf16[2,128,512]{2,1,0:T(8,128)(2,1)S(1)}, bf16[2,128,512]{2,1,0:T(8,128)(2,1)S(1)}, u32[]{:S(2)}, u32[]{:S(2)}) %collective-permute-start.19) | collective-permute-done | bytes 262176 | tf_op jit(solution)/shard_map/ppermute | solution.py:410
  172.5 3.4 %collective-permute-done.21.refs_3_ = bf16[2,128,512]{2,1,0:T(8,128)(2,1)S(1)} collective-permute-done((bf16[2,128,512]{2,1,0:T(8,128)(2,1)S(1)}, bf16[2,128,512]{2,1,0:T(8,128)(2,1)S(1)}, u32[]{:S(2)}, u32[]{:S(2)}) %collective-permute-start.21) | collective-permute-done | bytes 262176 | tf_op jit(solution)/shard_map/ppermute | solution.py:491
  175.8 5.5 %collective-permute-done.23.refs_5_ = bf16[2,128,512]{2,1,0:T(8,128)(2,1)S(1)} collective-permute-done((bf16[2,128,512]{2,1,0:T(8,128)(2,1)S(1)}, bf16[2,128,512]{2,1,0:T(8,128)(2,1)S(1)}, u32[]{:S(2)}, u32[]{:S(2)}) %collective-permute-start.23) | collective-permute-done | bytes 262176 | tf_op jit(solution)/shard_map/ppermute | solution.py:410
  181.5 4.7 %collective-permute-done.25.refs_7_ = bf16[2,128,512]{2,1,0:T(8,128)(2,1)S(1)} collective-permute-done((bf16[2,128,512]{2,1,0:T(8,128)(2,1)S(1)}, bf16[2,128,512]{2,1,0:T(8,128)(2,1)S(1)}, u32[]{:S(2)}, u32[]{:S(2)}) %collective-permute-start.25) | collective-permute-done | bytes 262176 | tf_op jit(solution)/shard_map/ppermute | solution.py:491
  186.2 1.7 place.1
  (59 shorter events, 26.7 us)
Async XLA Ops:
  0.0 13.2 %copy-start = (bf16[1024,512]{1,0:T(8,128)(2,1)S(1)}, bf16[1024,512]{1,0:T(8,128)(2,1)}, u32[]{:S(2)}) copy-start(bf16[1024,512]{1,0:T(8,128)(2,1)} %refs_4_.1) | copy-start | bytes 3145732
  2.2 15.2 %collective-permute-start.1 = (bf16[1,512,512]{2,1,0:T(8,128)(2,1)}, bf16[1,512,512]{2,1,0:T(8,128)(2,1)}, u32[]{:S(2)}, u32[]{:S(2)}) collective-permute-start(bf16[1,512,512]{2,1,0:T(8,128)(2,1)} %get-tuple-element.72), channel_id=1, source_target_pairs={{0,4},{4,0},{8,12},{12,8},{16,20},{20,16},{24,28},{28,24},{1,5},{5... | collective-permute-start | bytes 1572872 | tf_op jit(solution)/shard_map/ppermute | solution.py:404
  5.1 27.0 %collective-permute-start = (bf16[1024,512]{1,0:T(8,128)(2,1)}, bf16[1024,512]{1,0:T(8,128)(2,1)}, u32[]{:S(2)}, u32[]{:S(2)}) collective-permute-start(bf16[1024,512]{1,0:T(8,128)(2,1)} %refs_4_.1), channel_id=1, source_target_pairs={{0,16},{4,20},{1,17},{5,21},{2,18},{6,22},{3,19},{7,23}} | collective-permute-start | bytes 3145736 | tf_op jit(solution)/shard_map/ppermute | solution.py:404
  20.3 24.7 %collective-permute-start.5 = (bf16[2,512,512]{2,1,0:T(8,128)(2,1)}, bf16[2,512,512]{2,1,0:T(8,128)(2,1)}, u32[]{:S(2)}, u32[]{:S(2)}) collective-permute-start(bf16[2,512,512]{2,1,0:T(8,128)(2,1)} %get-tuple-element.38), channel_id=1, source_target_pairs={{0,4},{4,0},{8,12},{12,8},{16,20},{20,16},{24,28},{28,24},{1,5},{5... | collective-permute-start | bytes 3145736 | tf_op jit(solution)/shard_map/ppermute | solution.py:404
  23.9 12.7 %collective-permute-start.2 = (bf16[2,512,256]{2,1,0:T(8,128)(2,1)}, bf16[2,512,256]{2,1,0:T(8,128)(2,1)S(1)}, u32[]{:S(2)}, u32[]{:S(2)}) collective-permute-start(bf16[2,512,256]{2,1,0:T(8,128)(2,1)} %get-tuple-element.84), channel_id=1, source_target_pairs={{16,8},{20,12},{24,16},{28,20},{8,24},{12,28},{17,9},{21,13},{25,1... | collective-permute-start | bytes 1572872 | tf_op jit(solution)/shard_map/ppermute | solution.py:404
  24.6 18.0 %collective-permute-start.3 = (bf16[2,512,256]{2,1,0:T(8,128)(2,1)}, bf16[2,512,256]{2,1,0:T(8,128)(2,1)S(1)}, u32[]{:S(2)}, u32[]{:S(2)}) collective-permute-start(bf16[2,512,256]{2,1,0:T(8,128)(2,1)} %get-tuple-element.83), channel_id=1, source_target_pairs={{24,8},{28,12},{8,0},{12,4},{16,24},{20,28},{25,9},{29,13},{9,1},{... | collective-permute-start | bytes 1572872 | tf_op jit(solution)/shard_map/ppermute | solution.py:404
  32.1 14.2 %collective-permute-start.6 = (bf16[2,512,256]{2,1,0:T(8,128)(2,1)S(1)}, bf16[2,512,256]{2,1,0:T(8,128)(2,1)S(1)}, u32[]{:S(2)}, u32[]{:S(2)}) collective-permute-start(bf16[2,512,256]{2,1,0:T(8,128)(2,1)S(1)} %get-tuple-element.39), channel_id=1, source_target_pairs={{0,8},{4,12},{1,9},{5,13},{2,10},{6,14},{3,11},{7,15}} | collective-permute-start | bytes 1572872 | tf_op jit(solution)/shard_map/ppermute | solution.py:404
  34.0 21.1 %collective-permute-start.7 = (bf16[2,512,256]{2,1,0:T(8,128)(2,1)}, bf16[2,512,256]{2,1,0:T(8,128)(2,1)S(1)}, u32[]{:S(2)}, u32[]{:S(2)}) collective-permute-start(bf16[2,512,256]{2,1,0:T(8,128)(2,1)} %slice.53), channel_id=1, source_target_pairs={{0,12},{4,8},{1,13},{5,9},{2,14},{6,10},{3,15},{7,11}} | collective-permute-start | bytes 1572872 | tf_op jit(solution)/shard_map/ppermute | solution.py:404
  42.6 36.2 %collective-permute-start.4 = (bf16[2,512,256]{2,1,0:T(8,128)(2,1)S(1)}, bf16[2,512,256]{2,1,0:T(8,128)(2,1)S(1)}, u32[]{:S(2)}, u32[]{:S(2)}) collective-permute-start(bf16[2,512,256]{2,1,0:T(8,128)(2,1)S(1)} %get-tuple-element.37), channel_id=1, source_target_pairs={{16,8},{20,12},{24,16},{28,20},{8,24},{12,28},{17,9},{21,13},{25,1... | collective-permute-start | bytes 1572872 | tf_op jit(solution)/shard_map/ppermute | solution.py:404
  43.3 35.5 %collective-permute-start.8 = (bf16[2,512,256]{2,1,0:T(8,128)(2,1)S(1)}, bf16[2,512,256]{2,1,0:T(8,128)(2,1)S(1)}, u32[]{:S(2)}, u32[]{:S(2)}) collective-permute-start(bf16[2,512,256]{2,1,0:T(8,128)(2,1)S(1)} %get-tuple-element.43), channel_id=1, source_target_pairs={{24,8},{28,12},{8,0},{12,4},{16,24},{20,28},{25,9},{29,13},{9,1},{... | collective-permute-start | bytes 1572872 | tf_op jit(solution)/shard_map/ppermute | solution.py:404
  55.0 31.4 %collective-permute-start.10 = (bf16[4,512,256]{2,1,0:T(8,128)(2,1)S(1)}, bf16[4,512,256]{2,1,0:T(8,128)(2,1)S(1)}, u32[]{:S(2)}, u32[]{:S(2)}) collective-permute-start(bf16[4,512,256]{2,1,0:T(8,128)(2,1)S(1)} %pad_maximum_fusion), channel_id=1, source_target_pairs={{0,8},{4,12},{1,9},{5,13},{2,10},{6,14},{3,11},{7,15}} | collective-permute-start | bytes 3145736 | tf_op jit(solution)/shard_map/ppermute | solution.py:404
  69.6 37.5 %collective-permute-start.11 = (bf16[1072,256]{1,0:T(8,128)(2,1)S(1)}, bf16[1072,256]{1,0:T(8,128)(2,1)S(1)}, u32[]{:S(2)}, u32[]{:S(2)}) collective-permute-start(bf16[1072,256]{1,0:T(8,128)(2,1)S(1)} %get-tuple-element.41), channel_id=1, source_target_pairs={{8,16},{12,20},{16,24},{20,28},{9,17},{13,21},{17,25},{21,29},{10,... | collective-permute-start | bytes 1646600 | tf_op jit(solution)/shard_map/ppermute | solution.py:404
  76.2 30.8 %collective-permute-start.12 = (bf16[1072,256]{1,0:T(8,128)(2,1)S(1)}, bf16[1072,256]{1,0:T(8,128)(2,1)S(1)}, u32[]{:S(2)}, u32[]{:S(2)}) collective-permute-start(bf16[1072,256]{1,0:T(8,128)(2,1)S(1)} %get-tuple-element.50), channel_id=1, source_target_pairs={{8,24},{12,28},{0,8},{4,12},{24,16},{28,20},{9,25},{13,29},{1,9},{... | collective-permute-start | bytes 1646600 | tf_op jit(solution)/shard_map/ppermute | solution.py:404
  78.8 15.0 %copy-start.1 = (bf16[2,512,256]{2,1,0:T(8,128)(2,1)}, bf16[2,512,256]{2,1,0:T(8,128)(2,1)S(1)}, u32[]{:S(2)}) copy-start(bf16[2,512,256]{2,1,0:T(8,128)(2,1)S(1)} %collective-permute-done.8.qb) | copy-start | bytes 1572868
  78.8 47.1 %collective-permute-start.9 = (bf16[1024,512]{1,0:T(8,128)(2,1)S(1)}, bf16[1024,512]{1,0:T(8,128)(2,1)S(1)}, u32[]{:S(2)}, u32[]{:S(2)}) collective-permute-start(bf16[1024,512]{1,0:T(8,128)(2,1)S(1)} %copy-done), channel_id=1, source_target_pairs={{16,0},{20,4},{24,8},{28,12},{17,1},{21,5},{25,9},{29,13},{18,2},{... | collective-permute-start | bytes 3145736 | tf_op jit(solution)/shard_map/ppermute | solution.py:404
  93.8 32.6 %collective-permute-start.15 = (bf16[1072,256]{1,0:T(8,128)(2,1)}, bf16[1072,256]{1,0:T(8,128)(2,1)}, u32[]{:S(2)}, u32[]{:S(2)}) collective-permute-start(bf16[1072,256]{1,0:T(8,128)(2,1)} %get-tuple-element.47), channel_id=1, source_target_pairs={{8,16},{12,20},{16,24},{20,28},{9,17},{13,21},{17,25},{21,29},{10,... | collective-permute-start | bytes 1646600 | tf_op jit(solution)/shard_map/ppermute | solution.py:404
  95.3 31.2 %collective-permute-start.16 = (bf16[1072,256]{1,0:T(8,128)(2,1)}, bf16[1072,256]{1,0:T(8,128)(2,1)}, u32[]{:S(2)}, u32[]{:S(2)}) collective-permute-start(bf16[1072,256]{1,0:T(8,128)(2,1)} %get-tuple-element.54), channel_id=1, source_target_pairs={{8,24},{12,28},{0,8},{4,12},{24,16},{28,20},{9,25},{13,29},{1,9},{... | collective-permute-start | bytes 1646600 | tf_op jit(solution)/shard_map/ppermute | solution.py:404
  107.0 3.1 %copy-start.5 = (bf16[1072,256]{1,0:T(8,128)(2,1)}, bf16[1072,256]{1,0:T(8,128)(2,1)S(1)}, u32[]{:S(2)}) copy-start(bf16[1072,256]{1,0:T(8,128)(2,1)S(1)} %own_rows.3.own) | copy-start | bytes 1646596
  107.1 3.1 %copy-start.3 = (bf16[1072,256]{1,0:T(8,128)(2,1)}, bf16[1072,256]{1,0:T(8,128)(2,1)S(1)}, u32[]{:S(2)}) copy-start(bf16[1072,256]{1,0:T(8,128)(2,1)S(1)} %collective-permute-done.12.ob) | copy-start | bytes 1646596
  110.1 16.3 %collective-permute-start.14 = (bf16[2,512,256]{2,1,0:T(8,128)(2,1)}, bf16[2,512,256]{2,1,0:T(8,128)(2,1)}, u32[]{:S(2)}, u32[]{:S(2)}) collective-permute-start(bf16[2,512,256]{2,1,0:T(8,128)(2,1)} %merge.2), channel_id=1, source_target_pairs={{0,4},{4,0},{8,12},{12,8},{16,20},{20,16},{24,28},{28,24},{1,5},{5... | collective-permute-start | bytes 1572872 | tf_op jit(solution)/shard_map/ppermute | solution.py:404
  126.3 22.1 %collective-permute-start.13 = (bf16[1024,512]{1,0:T(8,128)(2,1)S(1)}, bf16[1024,512]{1,0:T(8,128)(2,1)}, u32[]{:S(2)}, u32[]{:S(2)}) collective-permute-start(bf16[1024,512]{1,0:T(8,128)(2,1)S(1)} %fusion.refs_4_), channel_id=1, source_target_pairs={{0,8},{4,12},{8,0},{12,4},{16,24},{20,28},{24,16},{28,20},{1,9},{5... | collective-permute-start | bytes 3145736 | tf_op jit(solution)/shard_map/ppermute | solution.py:404
  126.4 5.0 %copy-start.4 = (bf16[1072,256]{1,0:T(8,128)(2,1)S(1)}, bf16[1072,256]{1,0:T(8,128)(2,1)}, u32[]{:S(2)}) copy-start(bf16[1072,256]{1,0:T(8,128)(2,1)} %copy-done.3) | copy-start | bytes 1646596
  126.4 5.1 %copy-start.2 = (bf16[2,512,256]{2,1,0:T(8,128)(2,1)S(1)}, bf16[2,512,256]{2,1,0:T(8,128)(2,1)}, u32[]{:S(2)}) copy-start(bf16[2,512,256]{2,1,0:T(8,128)(2,1)} %copy-done.1) | copy-start | bytes 1572868
  130.8 17.6 %collective-permute-start.17 = (bf16[2,512,256]{2,1,0:T(8,128)(2,1)S(1)}, bf16[2,512,256]{2,1,0:T(8,128)(2,1)S(1)}, u32[]{:S(2)}, u32[]{:S(2)}) collective-permute-start(bf16[2,512,256]{2,1,0:T(8,128)(2,1)S(1)} %merge.3), channel_id=1, source_target_pairs={{0,4},{4,0},{8,12},{12,8},{16,20},{20,16},{24,28},{28,24},{1,5},{5... | collective-permute-start | bytes 1572872 | tf_op jit(solution)/shard_map/ppermute | solution.py:404
  151.9 2.7 %collective-permute-start.18 = (bf16[2,2,2,128,512]{4,3,2,1,0:T(8,128)(2,1)S(1)}, bf16[2,2,2,128,512]{4,3,2,1,0:T(8,128)(2,1)S(1)}, u32[]{:S(2)}, u32[]{:S(2)}) collective-permute-start(bf16[2,2,2,128,512]{4,3,2,1,0:T(8,128)(2,1)S(1)} %get-tuple-element.56), channel_id=1, source_target_pairs={{0,1},{1,0},{2,3},{3,2},{4,5},{5,4},{6,7},{7,6},{8,9},{9,8},{10,11... | collective-permute-start | bytes 3145736 | tf_op jit(solution)/shard_map/ppermute | solution.py:410
  159.3 8.8 %collective-permute-start.22 = (bf16[2,2,2,128,512]{4,3,2,1,0:T(8,128)(2,1)S(1)}, bf16[2,2,2,128,512]{4,3,2,1,0:T(8,128)(2,1)S(1)}, u32[]{:S(2)}, u32[]{:S(2)}) collective-permute-start(bf16[2,2,2,128,512]{4,3,2,1,0:T(8,128)(2,1)S(1)} %get-tuple-element.64), channel_id=1, source_target_pairs={{0,1},{1,0},{2,3},{3,2},{4,5},{5,4},{6,7},{7,6},{8,9},{9,8},{10,11... | collective-permute-start | bytes 3145736 | tf_op jit(solution)/shard_map/ppermute | solution.py:410
  159.5 8.6 %collective-permute-start.19 = (bf16[2,128,512]{2,1,0:T(8,128)(2,1)S(1)}, bf16[2,128,512]{2,1,0:T(8,128)(2,1)S(1)}, u32[]{:S(2)}, u32[]{:S(2)}) collective-permute-start(bf16[2,128,512]{2,1,0:T(8,128)(2,1)S(1)} %get-tuple-element.58), channel_id=1, source_target_pairs={{0,2},{1,3},{2,0},{3,1},{4,6},{5,7},{6,4},{7,5},{8,10},{9,11},{10,... | collective-permute-start | bytes 786440 | tf_op jit(solution)/shard_map/ppermute | solution.py:410
  161.1 11.4 %collective-permute-start.20 = (bf16[2,128,512]{2,1,0:T(8,128)(2,1)S(1)}, bf16[2,128,512]{2,1,0:T(8,128)(2,1)S(1)}, u32[]{:S(2)}, u32[]{:S(2)}) collective-permute-start(bf16[2,128,512]{2,1,0:T(8,128)(2,1)S(1)} %get-tuple-element.59), channel_id=1, source_target_pairs={{0,4},{4,0},{8,12},{12,8},{16,20},{20,16},{24,28},{28,24},{1,5},{5... | collective-permute-start | bytes 786440 | tf_op jit(solution)/shard_map/ppermute | solution.py:404
  161.6 14.2 %collective-permute-start.21 = (bf16[2,128,512]{2,1,0:T(8,128)(2,1)S(1)}, bf16[2,128,512]{2,1,0:T(8,128)(2,1)S(1)}, u32[]{:S(2)}, u32[]{:S(2)}) collective-permute-start(bf16[2,128,512]{2,1,0:T(8,128)(2,1)S(1)} %get-tuple-element.60), channel_id=1, source_target_pairs={{0,6},{1,7},{2,4},{3,5},{4,2},{5,3},{6,0},{7,1},{8,14},{9,15},{10,... | collective-permute-start | bytes 786440 | tf_op jit(solution)/shard_map/ppermute | solution.py:491
  168.9 12.4 %collective-permute-start.23 = (bf16[2,128,512]{2,1,0:T(8,128)(2,1)S(1)}, bf16[2,128,512]{2,1,0:T(8,128)(2,1)S(1)}, u32[]{:S(2)}, u32[]{:S(2)}) collective-permute-start(bf16[2,128,512]{2,1,0:T(8,128)(2,1)S(1)} %get-tuple-element.66), channel_id=1, source_target_pairs={{0,2},{1,3},{2,0},{3,1},{4,6},{5,7},{6,4},{7,5},{8,10},{9,11},{10,... | collective-permute-start | bytes 786440 | tf_op jit(solution)/shard_map/ppermute | solution.py:410
  170.5 11.0 %collective-permute-start.24 = (bf16[2,128,512]{2,1,0:T(8,128)(2,1)S(1)}, bf16[2,128,512]{2,1,0:T(8,128)(2,1)S(1)}, u32[]{:S(2)}, u32[]{:S(2)}) collective-permute-start(bf16[2,128,512]{2,1,0:T(8,128)(2,1)S(1)} %get-tuple-element.67), channel_id=1, source_target_pairs={{0,4},{4,0},{8,12},{12,8},{16,20},{20,16},{24,28},{28,24},{1,5},{5... | collective-permute-start | bytes 786440 | tf_op jit(solution)/shard_map/ppermute | solution.py:404
  171.0 15.2 %collective-permute-start.25 = (bf16[2,128,512]{2,1,0:T(8,128)(2,1)S(1)}, bf16[2,128,512]{2,1,0:T(8,128)(2,1)S(1)}, u32[]{:S(2)}, u32[]{:S(2)}) collective-permute-start(bf16[2,128,512]{2,1,0:T(8,128)(2,1)S(1)} %get-tuple-element.68), channel_id=1, source_target_pairs={{0,6},{1,7},{2,4},{3,5},{4,2},{5,3},{6,0},{7,1},{8,14},{9,15},{10,... | collective-permute-start | bytes 786440 | tf_op jit(solution)/shard_map/ppermute | solution.py:491
  (1 other events, 1.1 us)

commit v9 on v8

--- a/solution.py
+++ b/solution.py
@@ -418,22 +418,26 @@
     def pieces(array, c):
         return array[..., c * width : (c + 1) * width]
 
+    w_halves = [pieces(out_weight, c) for c in range(chunks)]
+    w_first = seq_perm(w_halves[0], (0, 2), (1, 3), (2, 0), (3, 1))
     q_m, q_o = lanes(0, 1, x), swap(lanes(0, 1, 1 - x))
-    w_second = seq_perm(out_weight, (0, 2))
     kv_m, kv_give = lanes(1, 3, x), lanes(1, 3, 1 - x)
     q, qs, low = [], [], []
     for c in range(chunks):
         a, b = pieces(q_m, c), pieces(q_o, c)
         q.append(jnp.concatenate([jnp.where(first, a, b), jnp.where(first, b, a)]))
-        block = pieces(out_weight, c).reshape(q[c].shape)
-        going = [jnp.where(z == 1, block, q[c]), jnp.where(z == 3, q[c], block)]
-        if c:
-            going = after(going, *qs[0])
-        qs.append([seq_perm(going[0], (2, 1), (3, 2), (1, 3)), seq_perm(going[1], (3, 1), (1, 0), (2, 3))])
+        block, last = (w.reshape(q[c].shape) for w in (w_halves[c], w_halves[1]))
         if c == 0:
-            kv_o = swap(after(kv_give, q[0]))
-            ups = after([pieces(kv_m, c), pieces(kv_give, c)], w_second)
-            low.append([seq_perm(ups[0], (0, 1)), seq_perm(ups[1], (0, 1), cross=True)])
+            going = [jnp.where(z == 1, last, q[c]), jnp.where(z == 3, q[c], jnp.where(z == 0, last, block))]
+        else:
+            going = after([q[c], jnp.where(z == 3, q[c], block)], *qs[0])
+        qs.append([
+            seq_perm(going[0], (2, 1), (3, 2), *([(1, 3)] if c == 0 else [])),
+            seq_perm(going[1], (3, 1), (1, 0), (2, 3), *([(0, 2)] if c == 0 else [])),
+        ])
+        if c == 0:
+            kv_o = swap(after(kv_give, q[0], w_first))
+            low.append([seq_perm(pieces(kv_m, c), (0, 1)), seq_perm(pieces(kv_give, c), (0, 1), cross=True)])
         else:
             up = jnp.concatenate([pieces(kv_m, c), pieces(kv_o, c)])
             low.append([seq_perm(after(up, *low[0]), (0, 1))])
@@ -457,10 +461,16 @@
         turn = after(at, mine)
 
     depth = out_weight.shape[0]
-    w_down = seq_perm(after(out_weight, own[0], *qs[1]), (2, 0), (3, 1))
-    w_near = [
-        jnp.where((z == 0) | (z == 3), qs[c][1].reshape(depth, width), ob[c][:depth]) for c in range(chunks)
-    ]
+
+    def block(array):
+        return array.reshape(depth, width)
+
+    def pair_swap(half):
+        return seq_perm(half, (0, 1), (1, 0), (2, 3), (3, 2))
+
+    w_near = [jnp.where((z == 0) | (z == 3), block(qs[c][1]), ob[c][:depth]) for c in range(chunks)]
+    w_last = seq_perm(after(w_halves[1], own[0], *qs[1]), (2, 0), (3, 1))
+    w_other = [pair_swap(after(w_first, oa[0], ob[0]))]
 
     def merged(c, earlier):
         (a,) = head_call(
@@ -468,25 +478,22 @@
             [struct((2, cols, width), BF16)], heads, "merge", 2)
         return a, swap(a)
 
-    first_half = merged(0, own[1])
-    w_ridden = jnp.concatenate([qs[c][0].reshape(depth, width) for c in range(chunks)], axis=1)
-    w_far = jnp.where(
-        z >= 2, jnp.where(z == 2, w_second, w_ridden), after(w_down, first_half[0], own[1]))
-    near, far = map(list, zip(first_half, merged(1, (w_far, first_half[1]))))
-    w_other = seq_perm(w_far, (0, 1), (1, 0), (2, 3), (3, 2))
+    first_half = merged(0, (own[1], w_last))
+    up_last = jnp.where(z == 2, block(qs[0][1]), block(qs[0][0]))
+    w_far = [w_first, jnp.where(z >= 2, up_last, after(w_last, own[1]))]
+    w_other.append(pair_swap(w_far[1]))
+    near, far = map(list, zip(first_half, merged(1, (first_half[1], w_other))))
 
     parts = []
-    turn = after(at, w_other)
     for weights in (
         [out_weight] + w_near,
-        [w_far, w_other],
+        w_far + w_other,
     ):
-        send, kept = project(turn, near, far, weights, out_weight.shape[1])
+        send, kept = project(at, near, far, weights, out_weight.shape[1])
         got = head_perm(send, 1)
         piece = struct(send.shape[:1] + send.shape[3:], BF16)
         stay, to_y, to_x, to_xy = whole_call(
-            split_kernel, after(at, parts[1:2]), [kept, got], [piece] * 4, "split", 2)
-        turn = after(at, stay)
+            split_kernel, at, [kept, got], [piece] * 4, "split", 2)
         diagonal = [((2 * i + j) * 4 + h, (2 * i + 1 - j) * 4 + (h ^ 2)) for i in range(4) for j in range(2) for h in range(4)]
         from_xy = lax.ppermute(to_xy, ("seq", "head"), diagonal)
         parts += [stay, head_perm(to_y, 2), swap(to_x), from_xy]

time: 189 us -> 203 us (1.074)
  the two profiles are of different devices: /device:TPU:0 before, /device:TPU:16 now
where the time goes in v9:
time: 203 us; the launch traced here: 201 us
  waiting for transfers between devices  95.4 us (47%)
  starting transfers between devices  50.4 us (25%)
  Pallas kernels  39.5 us (19%)
  local copies, waits for them, and re-layouts  10.9 us (5%)
  other arithmetic  4.25 us (2%)
    ppermute x21, waiting for transfers between devices, seq_perm(): return lax.ppermute(array, 'seq', pairs)  81.9 us
    ppermute x21, starting transfers between devices, seq_perm(): return lax.ppermute(array, 'seq', pairs)  43.7 us
    pallas_call x6, Pallas kernels, head_call(): pl.pallas_call(kernel, out_shape=outs, grid_spec=pltpu.PrefetchScalarGrid...  30.4 us
    pallas_call x5, Pallas kernels, whole_call(): pl.pallas_call(kernel, out_shape=outs, in_specs=[pl.BlockSpec(memory_spac...  9.1 us
    ppermute x2, waiting for transfers between devices, body_eight(): from_xy = lax.ppermute(to_xy, ('seq', 'head'), diagonal)  7.79 us
    ppermute x4, waiting for transfers between devices, head_perm(): return lax.ppermute(array, 'head', [(i, i ^ flip) for i in range(4)])  5.74 us
    slice x4, local copies, waits for them, and re-layouts, pieces(): return array[..., c * width:(c + 1) * width]  5.28 us
    dynamic_slice x2, local copies, waits for them, and re-layouts, lanes(): lax.dynamic_slice(local, (lo, 0, half_of * half), (hi - lo, cols, half))  4.78 us
  transfers between devices with their start and end apart: 27, of which 13 were waited for; matrix products, arithmetic and copies ran while one was open for 6% of the time, Pallas kernels for 16%

profile of v9, /device:TPU:16, one launch (start us, length us, event | category | flops | bytes accessed | tf_op | source)
XLA Modules:
  0.0 200.8 jit_solution(4545142576645959645)
XLA Ops:
  5.2 2.7 %dynamic-slice_bitcast_fusion = (bf16[2,512,512]{2,1,0:T(8,128)(2,1)}, bf16[2,512,512]{2,1,0:T(8,128)(2,1)S(1)}) fusion(bf16[3,1,512,1024]{3,2,1,0:T(8,128)(2,1)} %param.2, s32[]{:T(128)S(6)} %select_n.101, s32[]{:T(128)S(6)} %select_n.100), kind=kLoop, calls=%fused_computation.1 | loop fusion | bytes 4194312 | tf_op jit(solution)/shard_map/dynamic_slice | solution.py:416
  8.0 8.1 %collective-permute-done = bf16[1,512,512]{2,1,0:T(8,128)(2,1)} collective-permute-done((bf16[1,512,512]{2,1,0:T(8,128)(2,1)}, bf16[1,512,512]{2,1,0:T(8,128)(2,1)}, u32[]{:S(2)}, u32[]{:S(2)}) %collective-permute-start) | collective-permute-done | bytes 524320 | tf_op jit(solution)/shard_map/ppermute | solution.py:404
  18.8 8.6 %collective-permute-done.3.refs_4_ = bf16[1024,256]{1,0:T(8,128)(2,1)S(1)} collective-permute-done((bf16[1024,256]{1,0:T(8,128)(2,1)S(1)}, bf16[1024,256]{1,0:T(8,128)(2,1)S(1)}, u32[]{:S(2)}, u32[]{:S(2)}) %collective-permute-start.3) | collective-permute-done | bytes 524320 | tf_op jit(solution)/shard_map/ppermute | solution.py:404
  32.1 4.3 %collective-permute-start.1 = (bf16[2,512,256]{2,1,0:T(8,128)(2,1)}, bf16[2,512,256]{2,1,0:T(8,128)(2,1)S(1)}, u32[]{:S(2)}, u32[]{:S(2)}) collective-permute-start(bf16[2,512,256]{2,1,0:T(8,128)(2,1)} %get-tuple-element.79), channel_id=1, source_target_pairs={{16,8},{20,12},{24,16},{28,20},{8,24},{12,28},{17,9},{21,13},{25,1... | collective-permute-start | bytes 1572872 | tf_op jit(solution)/shard_map/ppermute | solution.py:404
  36.4 2.2 %collective-permute-start.2 = (bf16[2,512,256]{2,1,0:T(8,128)(2,1)}, bf16[2,512,256]{2,1,0:T(8,128)(2,1)S(1)}, u32[]{:S(2)}, u32[]{:S(2)}) collective-permute-start(bf16[2,512,256]{2,1,0:T(8,128)(2,1)} %get-tuple-element.80), channel_id=1, source_target_pairs={{24,8},{28,12},{8,0},{12,4},{16,24},{20,28},{0,16},{4,20},{25,9},{... | collective-permute-start | bytes 1572872 | tf_op jit(solution)/shard_map/ppermute | solution.py:404
  41.2 10.3 %collective-permute-done.1.qa = bf16[2,512,256]{2,1,0:T(8,128)(2,1)S(1)} collective-permute-done((bf16[2,512,256]{2,1,0:T(8,128)(2,1)}, bf16[2,512,256]{2,1,0:T(8,128)(2,1)S(1)}, u32[]{:S(2)}, u32[]{:S(2)}) %collective-permute-start.1) | collective-permute-done | bytes 524320 | tf_op jit(solution)/shard_map/ppermute | solution.py:404
  51.5 10.3 %collective-permute-done.2.qb = bf16[2,512,256]{2,1,0:T(8,128)(2,1)S(1)} collective-permute-done((bf16[2,512,256]{2,1,0:T(8,128)(2,1)}, bf16[2,512,256]{2,1,0:T(8,128)(2,1)S(1)}, u32[]{:S(2)}, u32[]{:S(2)}) %collective-permute-start.2) | collective-permute-done | bytes 524320 | tf_op jit(solution)/shard_map/ppermute | solution.py:404
  61.8 3.4 %collective-permute-start.7 = (bf16[2,512,256]{2,1,0:T(8,128)(2,1)}, bf16[2,512,256]{2,1,0:T(8,128)(2,1)S(1)}, u32[]{:S(2)}, u32[]{:S(2)}) collective-permute-start(bf16[2,512,256]{2,1,0:T(8,128)(2,1)} %get-tuple-element.37.q), channel_id=1, source_target_pairs={{16,8},{20,12},{24,16},{28,20},{17,9},{21,13},{25,17},{29,21},{18,... | collective-permute-start | bytes 1572872 | tf_op jit(solution)/shard_map/ppermute | solution.py:404
  65.2 2.6 %collective-permute-start.8 = (bf16[2,512,256]{2,1,0:T(8,128)(2,1)}, bf16[2,512,256]{2,1,0:T(8,128)(2,1)S(1)}, u32[]{:S(2)}, u32[]{:S(2)}) collective-permute-start(bf16[2,512,256]{2,1,0:T(8,128)(2,1)} %get-tuple-element.38), channel_id=1, source_target_pairs={{24,8},{28,12},{8,0},{12,4},{16,24},{20,28},{25,9},{29,13},{9,1},{... | collective-permute-start | bytes 1572872 | tf_op jit(solution)/shard_map/ppermute | solution.py:404
  70.9 6.8 %upper_rows.2 = (bf16[1072,256]{1,0:T(8,128)(2,1)S(1)}, bf16[1072,256]{1,0:T(8,128)(2,1)S(1)}) custom-call(s32[4]{0:T(128)S(1)} %pad_add_fusion.at, bf16[2,512,256]{2,1,0:T(8,128)(2,1)S(1)} %collective-permute-done.1.qa, bf16[2,512,256]{2,1,0:T(8,128)(2,1)S(1)} %collective-permute-done.2.qb, bf16[2,512,512]{2,1,0:T(8,128)(2,1)S(1)} %get-tuple-element.62.kv_m, ...), custom_call_target="tpu_custom_call" | custom-call | flops 7000000000 | bytes 1024 | tf_op jit(solution)/shard_map/upper_rows/pallas_call | solution.py:300
  77.8 2.1 %collective-permute-start.11 = (bf16[1072,256]{1,0:T(8,128)(2,1)S(1)}, bf16[1072,256]{1,0:T(8,128)(2,1)S(1)}, u32[]{:S(2)}, u32[]{:S(2)}) collective-permute-start(bf16[1072,256]{1,0:T(8,128)(2,1)S(1)} %get-tuple-element.34), channel_id=1, source_target_pairs={{8,16},{12,20},{16,24},{20,28},{9,17},{13,21},{17,25},{21,29},{10,... | collective-permute-start | bytes 1646600 | tf_op jit(solution)/shard_map/ppermute | solution.py:404
  81.3 6.1 %own_rows.2.own = bf16[1072,256]{1,0:T(8,128)(2,1)S(1)} custom-call(s32[4]{0:T(128)S(1)} %pad_add_fusion.at, bf16[2,512,256]{2,1,0:T(8,128)(2,1)S(1)} %copy-done.2, bf16[2,512,512]{2,1,0:T(8,128)(2,1)S(1)} %get-tuple-element.62.kv_m, bf16[2,512,512]{2,1,0:T(8,128)(2,1)} %collective-permute-done.4.kv_o, bf16[2,512,256]{2,1,0:T(8,128)(2,1)} %collective-permute-done.5.refs_0_, ...), custom_call_target="tpu_custom_call" | custom-call | flops 6000000000 | bytes 1024 | tf_op jit(solution)/shard_map/own_rows/pallas_call | solution.py:300
  87.5 6.3 %collective-permute-start.10 = (bf16[1024,256]{1,0:T(8,128)(2,1)S(1)}, bf16[1024,256]{1,0:T(8,128)(2,1)S(1)}, u32[]{:S(2)}, u32[]{:S(2)}) collective-permute-start(bf16[1024,256]{1,0:T(8,128)(2,1)S(1)} %copy-done.6), channel_id=1, source_target_pairs={{16,0},{20,4},{24,8},{28,12},{17,1},{21,5},{25,9},{29,13},{18,2},{... | collective-permute-start | bytes 1572872 | tf_op jit(solution)/shard_map/ppermute | solution.py:404
  93.8 8.1 %collective-permute-done.12.ob = bf16[1072,256]{1,0:T(8,128)(2,1)S(1)} collective-permute-done((bf16[1072,256]{1,0:T(8,128)(2,1)S(1)}, bf16[1072,256]{1,0:T(8,128)(2,1)S(1)}, u32[]{:S(2)}, u32[]{:S(2)}) %collective-permute-start.12) | collective-permute-done | bytes 548896 | tf_op jit(solution)/shard_map/ppermute | solution.py:404
  101.8 4.8 %collective-permute-start.14 = (bf16[1024,256]{1,0:T(8,128)(2,1)S(1)}, bf16[1024,256]{1,0:T(8,128)(2,1)S(1)}, u32[]{:S(2)}, u32[]{:S(2)}) collective-permute-start(bf16[1024,256]{1,0:T(8,128)(2,1)S(1)} %copy-done.4), channel_id=1, source_target_pairs={{0,8},{4,12},{8,0},{12,4},{16,24},{20,28},{24,16},{28,20},{1,9},{5... | collective-permute-start | bytes 1572872 | tf_op jit(solution)/shard_map/ppermute | solution.py:404
  106.6 6.7 %upper_rows.3 = (bf16[1072,256]{1,0:T(8,128)(2,1)S(1)}, bf16[1072,256]{1,0:T(8,128)(2,1)S(1)}) custom-call(s32[4]{0:T(128)S(1)} %pad_add_fusion.at, bf16[2,512,256]{2,1,0:T(8,128)(2,1)S(1)} %collective-permute-done.7.qa, bf16[2,512,256]{2,1,0:T(8,128)(2,1)S(1)} %collective-permute-done.8.qb, bf16[2,512,512]{2,1,0:T(8,128)(2,1)S(1)} %get-tuple-element.62.kv_m, ...), custom_call_target="tpu_custom_call" | custom-call | flops 7000000000 | bytes 1024 | tf_op jit(solution)/shard_map/upper_rows/pallas_call | solution.py:300
  113.3 2.1 %collective-permute-start.16 = (bf16[1072,256]{1,0:T(8,128)(2,1)S(1)}, bf16[1072,256]{1,0:T(8,128)(2,1)S(1)}, u32[]{:S(2)}, u32[]{:S(2)}) collective-permute-start(bf16[1072,256]{1,0:T(8,128)(2,1)S(1)} %get-tuple-element.40), channel_id=1, source_target_pairs={{8,16},{12,20},{16,24},{20,28},{9,17},{13,21},{17,25},{21,29},{10,... | collective-permute-start | bytes 1646600 | tf_op jit(solution)/shard_map/ppermute | solution.py:404
  115.4 6.0 %own_rows.3.own = bf16[1072,256]{1,0:T(8,128)(2,1)S(1)} custom-call(s32[4]{0:T(128)S(1)} %pad_add_fusion.at, bf16[2,512,256]{2,1,0:T(8,128)(2,1)S(1)} %copy-done.1, bf16[2,512,512]{2,1,0:T(8,128)(2,1)S(1)} %get-tuple-element.62.kv_m, bf16[2,512,512]{2,1,0:T(8,128)(2,1)} %collective-permute-done.4.kv_o, bf16[4,512,256]{2,1,0:T(8,128)(2,1)S(1)} %collective-permute-done.9.refs_0_), custom_call_target="tpu_custom_call" | custom-call | flops 6000000000 | bytes 1024 | tf_op jit(solution)/shard_map/own_rows/pallas_call | solution.py:300
  121.4 2.4 %merge.2 = bf16[2,512,256]{2,1,0:T(8,128)(2,1)S(1)} custom-call(s32[4]{0:T(128)S(1)} %pad_add_fusion.at, bf16[1072,256]{1,0:T(8,128)(2,1)S(1)} %own_rows.2.own, bf16[1072,256]{1,0:T(8,128)(2,1)S(1)} %collective-permute-done.11.oa, bf16[1072,256]{1,0:T(8,128)(2,1)S(1)} %collective-permute-done.12.ob), custom_call_target="tpu_custom_call" | custom-call | flops 2000000000 | bytes 1024 | tf_op jit(solution)/shard_map/merge/pallas_call | solution.py:300
  126.1 2.7 %collective-permute-start.15 = (bf16[1024,256]{1,0:T(8,128)(2,1)S(1)}, bf16[1024,256]{1,0:T(8,128)(2,1)S(1)}, u32[]{:S(2)}, u32[]{:S(2)}) collective-permute-start(bf16[1024,256]{1,0:T(8,128)(2,1)S(1)} %get-tuple-element.76.refs_5_), channel_id=1, source_target_pairs={{0,8},{4,12},{8,0},{12,4},{16,24},{20,28},{24,16},{28,20},{1,9},{5... | collective-permute-start | bytes 1572872 | tf_op jit(solution)/shard_map/ppermute | solution.py:404
  128.8 6.9 %collective-permute-done.13 = bf16[2,512,256]{2,1,0:T(8,128)(2,1)S(1)} collective-permute-done((bf16[2,512,256]{2,1,0:T(8,128)(2,1)S(1)}, bf16[2,512,256]{2,1,0:T(8,128)(2,1)S(1)}, u32[]{:S(2)}, u32[]{:S(2)}) %collective-permute-start.13) | collective-permute-done | bytes 524320 | tf_op jit(solution)/shard_map/ppermute | solution.py:404
  135.7 15.3 %collective-permute-done.15.refs_7_ = bf16[1024,256]{1,0:T(8,128)(2,1)S(1)} collective-permute-done((bf16[1024,256]{1,0:T(8,128)(2,1)S(1)}, bf16[1024,256]{1,0:T(8,128)(2,1)S(1)}, u32[]{:S(2)}, u32[]{:S(2)}) %collective-permute-start.15) | collective-permute-done | bytes 524320 | tf_op jit(solution)/shard_map/ppermute | solution.py:404
  151.0 2.4 %merge.3 = bf16[2,512,256]{2,1,0:T(8,128)(2,1)S(1)} custom-call(s32[4]{0:T(128)S(1)} %pad_add_fusion.at, bf16[1072,256]{1,0:T(8,128)(2,1)S(1)} %own_rows.3.own, bf16[1072,256]{1,0:T(8,128)(2,1)S(1)} %collective-permute-done.16.oa, bf16[1072,256]{1,0:T(8,128)(2,1)S(1)} %collective-permute-done.17.ob), custom_call_target="tpu_custom_call" | custom-call | flops 2000000000 | bytes 1024 | tf_op jit(solution)/shard_map/merge/pallas_call | solution.py:300
  153.7 11.8 %collective-permute-done.18 = bf16[2,512,256]{2,1,0:T(8,128)(2,1)S(1)} collective-permute-done((bf16[2,512,256]{2,1,0:T(8,128)(2,1)S(1)}, bf16[2,512,256]{2,1,0:T(8,128)(2,1)S(1)}, u32[]{:S(2)}, u32[]{:S(2)}) %collective-permute-start.18) | collective-permute-done | bytes 524320 | tf_op jit(solution)/shard_map/ppermute | solution.py:404
  165.4 2.9 %project.3 = (bf16[2,2,2,128,512]{4,3,2,1,0:T(8,128)(2,1)S(1)}, bf16[2,2,2,128,512]{4,3,2,1,0:T(8,128)(2,1)S(1)}) custom-call(s32[4]{0:T(128)S(1)} %pad_add_fusion.at, bf16[2,2,2,128,256]{4,3,2,1,0:T(8,128)(2,1)S(1)} %bitcast.28, bf16[2,2,2,128,256]{4,3,2,1,0:T(8,128)(2,1)S(1)} %bitcast.32, bf16[2,2,2,128,256]{4,3,2,1,0:T(8,128)(2,1)S(1)} %bitcast.30, ...), custom_call_target="tpu_custom_call" | custom-call | flops 4000000000 | bytes 1024 | tf_op jit(solution)/shard_map/project/pallas_call | solution.py:349
  168.4 2.9 %project.2 = (bf16[2,2,2,128,512]{4,3,2,1,0:T(8,128)(2,1)S(1)}, bf16[2,2,2,128,512]{4,3,2,1,0:T(8,128)(2,1)S(1)}) custom-call(s32[4]{0:T(128)S(1)} %pad_add_fusion.at, bf16[2,2,2,128,256]{4,3,2,1,0:T(8,128)(2,1)S(1)} %bitcast.29, bf16[2,2,2,128,256]{4,3,2,1,0:T(8,128)(2,1)S(1)} %bitcast.33, bf16[2,2,2,128,256]{4,3,2,1,0:T(8,128)(2,1)S(1)} %bitcast.31, ...), custom_call_target="tpu_custom_call" | custom-call | flops 4000000000 | bytes 1024 | tf_op jit(solution)/shard_map/project/pallas_call | solution.py:349
  180.3 2.6 %collective-permute-done.24.refs_5_ = bf16[2,128,512]{2,1,0:T(8,128)(2,1)S(1)} collective-permute-done((bf16[2,128,512]{2,1,0:T(8,128)(2,1)S(1)}, bf16[2,128,512]{2,1,0:T(8,128)(2,1)S(1)}, u32[]{:S(2)}, u32[]{:S(2)}) %collective-permute-start.24) | collective-permute-done | bytes 262176 | tf_op jit(solution)/shard_map/ppermute | solution.py:410
  182.9 2.7 %collective-permute-start.22 = (bf16[2,128,512]{2,1,0:T(8,128)(2,1)S(1)}, bf16[2,128,512]{2,1,0:T(8,128)(2,1)S(1)}, u32[]{:S(2)}, u32[]{:S(2)}) collective-permute-start(bf16[2,128,512]{2,1,0:T(8,128)(2,1)S(1)} %get-tuple-element.54), channel_id=1, source_target_pairs={{0,6},{1,7},{2,4},{3,5},{4,2},{5,3},{6,0},{7,1},{8,14},{9,15},{10,... | collective-permute-start | bytes 786440 | tf_op jit(solution)/shard_map/ppermute | solution.py:498
  185.6 3.5 %collective-permute-done.26.refs_7_ = bf16[2,128,512]{2,1,0:T(8,128)(2,1)S(1)} collective-permute-done((bf16[2,128,512]{2,1,0:T(8,128)(2,1)S(1)}, bf16[2,128,512]{2,1,0:T(8,128)(2,1)S(1)}, u32[]{:S(2)}, u32[]{:S(2)}) %collective-permute-start.26) | collective-permute-done | bytes 262176 | tf_op jit(solution)/shard_map/ppermute | solution.py:498
  189.1 3.2 %collective-permute-done.20.refs_1_ = bf16[2,128,512]{2,1,0:T(8,128)(2,1)S(1)} collective-permute-done((bf16[2,128,512]{2,1,0:T(8,128)(2,1)S(1)}, bf16[2,128,512]{2,1,0:T(8,128)(2,1)S(1)}, u32[]{:S(2)}, u32[]{:S(2)}) %collective-permute-start.20) | collective-permute-done | bytes 262176 | tf_op jit(solution)/shard_map/ppermute | solution.py:410
  192.2 2.5 %collective-permute-done.21.refs_2_ = bf16[2,128,512]{2,1,0:T(8,128)(2,1)S(1)} collective-permute-done((bf16[2,128,512]{2,1,0:T(8,128)(2,1)S(1)}, bf16[2,128,512]{2,1,0:T(8,128)(2,1)S(1)}, u32[]{:S(2)}, u32[]{:S(2)}) %collective-permute-start.21) | collective-permute-done | bytes 262176 | tf_op jit(solution)/shard_map/ppermute | solution.py:404
  194.7 4.3 %collective-permute-done.22.refs_3_ = bf16[2,128,512]{2,1,0:T(8,128)(2,1)S(1)} collective-permute-done((bf16[2,128,512]{2,1,0:T(8,128)(2,1)S(1)}, bf16[2,128,512]{2,1,0:T(8,128)(2,1)S(1)}, u32[]{:S(2)}, u32[]{:S(2)}) %collective-permute-start.22) | collective-permute-done | bytes 262176 | tf_op jit(solution)/shard_map/ppermute | solution.py:498
  (59 shorter events, 33.1 us)
Async XLA Ops:
  2.1 14.0 %collective-permute-start = (bf16[1,512,512]{2,1,0:T(8,128)(2,1)}, bf16[1,512,512]{2,1,0:T(8,128)(2,1)}, u32[]{:S(2)}, u32[]{:S(2)}) collective-permute-start(bf16[1,512,512]{2,1,0:T(8,128)(2,1)} %get-tuple-element.64), channel_id=1, source_target_pairs={{0,4},{4,0},{8,12},{12,8},{16,20},{20,16},{24,28},{28,24},{1,5},{5... | collective-permute-start | bytes 1572872 | tf_op jit(solution)/shard_map/ppermute | solution.py:404
  4.8 12.3 %copy-start.5 = (bf16[1024,256]{1,0:T(8,128)(2,1)}, bf16[1024,256]{1,0:T(8,128)(2,1)S(1)}, u32[]{:S(2)}) copy-start(bf16[1024,256]{1,0:T(8,128)(2,1)S(1)} %get-tuple-element.42) | copy-start | bytes 1572868
  4.8 22.5 %collective-permute-start.3 = (bf16[1024,256]{1,0:T(8,128)(2,1)S(1)}, bf16[1024,256]{1,0:T(8,128)(2,1)S(1)}, u32[]{:S(2)}, u32[]{:S(2)}) collective-permute-start(bf16[1024,256]{1,0:T(8,128)(2,1)S(1)} %get-tuple-element.73), channel_id=1, source_target_pairs={{0,16},{4,20},{8,24},{12,28},{16,0},{20,4},{24,8},{28,12},{1,17},{... | collective-permute-start | bytes 1572872 | tf_op jit(solution)/shard_map/ppermute | solution.py:404
  28.2 42.7 %copy-start = (bf16[1024,512]{1,0:T(8,128)(2,1)S(1)}, bf16[1024,512]{1,0:T(8,128)(2,1)}, u32[]{:S(2)}) copy-start(bf16[1024,512]{1,0:T(8,128)(2,1)} %refs_4_.1) | copy-start | bytes 3145732
  28.2 39.6 %collective-permute-start.4 = (bf16[2,512,512]{2,1,0:T(8,128)(2,1)}, bf16[2,512,512]{2,1,0:T(8,128)(2,1)}, u32[]{:S(2)}, u32[]{:S(2)}) collective-permute-start(bf16[2,512,512]{2,1,0:T(8,128)(2,1)} %get-tuple-element.33), channel_id=1, source_target_pairs={{0,4},{4,0},{8,12},{12,8},{16,20},{20,16},{24,28},{28,24},{1,5},{5... | collective-permute-start | bytes 3145736 | tf_op jit(solution)/shard_map/ppermute | solution.py:404
  30.6 39.4 %collective-permute-start.6 = (bf16[2,512,256]{2,1,0:T(8,128)(2,1)}, bf16[2,512,256]{2,1,0:T(8,128)(2,1)}, u32[]{:S(2)}, u32[]{:S(2)}) collective-permute-start(bf16[2,512,256]{2,1,0:T(8,128)(2,1)} %slice.51), channel_id=1, source_target_pairs={{0,12},{4,8},{1,13},{5,9},{2,14},{6,10},{3,15},{7,11}} | collective-permute-start | bytes 1572872 | tf_op jit(solution)/shard_map/ppermute | solution.py:404
  32.1 19.4 %collective-permute-start.1 = (bf16[2,512,256]{2,1,0:T(8,128)(2,1)}, bf16[2,512,256]{2,1,0:T(8,128)(2,1)S(1)}, u32[]{:S(2)}, u32[]{:S(2)}) collective-permute-start(bf16[2,512,256]{2,1,0:T(8,128)(2,1)} %get-tuple-element.79), channel_id=1, source_target_pairs={{16,8},{20,12},{24,16},{28,20},{8,24},{12,28},{17,9},{21,13},{25,1... | collective-permute-start | bytes 1572872 | tf_op jit(solution)/shard_map/ppermute | solution.py:404
  36.4 25.4 %collective-permute-start.2 = (bf16[2,512,256]{2,1,0:T(8,128)(2,1)}, bf16[2,512,256]{2,1,0:T(8,128)(2,1)S(1)}, u32[]{:S(2)}, u32[]{:S(2)}) collective-permute-start(bf16[2,512,256]{2,1,0:T(8,128)(2,1)} %get-tuple-element.80), channel_id=1, source_target_pairs={{24,8},{28,12},{8,0},{12,4},{16,24},{20,28},{0,16},{4,20},{25,9},{... | collective-permute-start | bytes 1572872 | tf_op jit(solution)/shard_map/ppermute | solution.py:404
  39.6 30.4 %collective-permute-start.5 = (bf16[2,512,256]{2,1,0:T(8,128)(2,1)}, bf16[2,512,256]{2,1,0:T(8,128)(2,1)}, u32[]{:S(2)}, u32[]{:S(2)}) collective-permute-start(bf16[2,512,256]{2,1,0:T(8,128)(2,1)} %get-tuple-element.66), channel_id=1, source_target_pairs={{0,8},{4,12},{1,9},{5,13},{2,10},{6,14},{3,11},{7,15}} | collective-permute-start | bytes 1572872 | tf_op jit(solution)/shard_map/ppermute | solution.py:404
  61.8 25.7 %collective-permute-start.7 = (bf16[2,512,256]{2,1,0:T(8,128)(2,1)}, bf16[2,512,256]{2,1,0:T(8,128)(2,1)S(1)}, u32[]{:S(2)}, u32[]{:S(2)}) collective-permute-start(bf16[2,512,256]{2,1,0:T(8,128)(2,1)} %get-tuple-element.37.q), channel_id=1, source_target_pairs={{16,8},{20,12},{24,16},{28,20},{17,9},{21,13},{25,17},{29,21},{18,... | collective-permute-start | bytes 1572872 | tf_op jit(solution)/shard_map/ppermute | solution.py:404
  65.2 22.3 %collective-permute-start.8 = (bf16[2,512,256]{2,1,0:T(8,128)(2,1)}, bf16[2,512,256]{2,1,0:T(8,128)(2,1)S(1)}, u32[]{:S(2)}, u32[]{:S(2)}) collective-permute-start(bf16[2,512,256]{2,1,0:T(8,128)(2,1)} %get-tuple-element.38), channel_id=1, source_target_pairs={{24,8},{28,12},{8,0},{12,4},{16,24},{20,28},{25,9},{29,13},{9,1},{... | collective-permute-start | bytes 1572872 | tf_op jit(solution)/shard_map/ppermute | solution.py:404
  70.0 11.3 %copy-start.2 = (bf16[2,512,256]{2,1,0:T(8,128)(2,1)S(1)}, bf16[2,512,256]{2,1,0:T(8,128)(2,1)}, u32[]{:S(2)}) copy-start(bf16[2,512,256]{2,1,0:T(8,128)(2,1)} %get-tuple-element.81.q) | copy-start | bytes 1572868
  70.0 36.6 %collective-permute-start.9 = (bf16[4,512,256]{2,1,0:T(8,128)(2,1)S(1)}, bf16[4,512,256]{2,1,0:T(8,128)(2,1)S(1)}, u32[]{:S(2)}, u32[]{:S(2)}) collective-permute-start(bf16[4,512,256]{2,1,0:T(8,128)(2,1)S(1)} %pad_maximum_fusion), channel_id=1, source_target_pairs={{0,8},{4,12},{1,9},{5,13},{2,10},{6,14},{3,11},{7,15}} | collective-permute-start | bytes 3145736 | tf_op jit(solution)/shard_map/ppermute | solution.py:404
  77.8 24.1 %collective-permute-start.11 = (bf16[1072,256]{1,0:T(8,128)(2,1)S(1)}, bf16[1072,256]{1,0:T(8,128)(2,1)S(1)}, u32[]{:S(2)}, u32[]{:S(2)}) collective-permute-start(bf16[1072,256]{1,0:T(8,128)(2,1)S(1)} %get-tuple-element.34), channel_id=1, source_target_pairs={{8,16},{12,20},{16,24},{20,28},{9,17},{13,21},{17,25},{21,29},{10,... | collective-permute-start | bytes 1646600 | tf_op jit(solution)/shard_map/ppermute | solution.py:404
  79.9 22.0 %copy-start.4 = (bf16[1024,256]{1,0:T(8,128)(2,1)S(1)}, bf16[1024,256]{1,0:T(8,128)(2,1)}, u32[]{:S(2)}) copy-start(bf16[1024,256]{1,0:T(8,128)(2,1)} %copy-done.3) | copy-start | bytes 1572868
  79.9 22.0 %collective-permute-start.12 = (bf16[1072,256]{1,0:T(8,128)(2,1)S(1)}, bf16[1072,256]{1,0:T(8,128)(2,1)S(1)}, u32[]{:S(2)}, u32[]{:S(2)}) collective-permute-start(bf16[1072,256]{1,0:T(8,128)(2,1)S(1)} %get-tuple-element.44), channel_id=1, source_target_pairs={{8,24},{12,28},{0,8},{4,12},{24,16},{28,20},{9,25},{13,29},{1,9},{... | collective-permute-start | bytes 1646600 | tf_op jit(solution)/shard_map/ppermute | solution.py:404
  87.4 28.0 %copy-start.1 = (bf16[2,512,256]{2,1,0:T(8,128)(2,1)S(1)}, bf16[2,512,256]{2,1,0:T(8,128)(2,1)}, u32[]{:S(2)}) copy-start(bf16[2,512,256]{2,1,0:T(8,128)(2,1)} %get-tuple-element.37.q) | copy-start | bytes 1572868
  87.5 33.9 %collective-permute-start.10 = (bf16[1024,256]{1,0:T(8,128)(2,1)S(1)}, bf16[1024,256]{1,0:T(8,128)(2,1)S(1)}, u32[]{:S(2)}, u32[]{:S(2)}) collective-permute-start(bf16[1024,256]{1,0:T(8,128)(2,1)S(1)} %copy-done.6), channel_id=1, source_target_pairs={{16,0},{20,4},{24,8},{28,12},{17,1},{21,5},{25,9},{29,13},{18,2},{... | collective-permute-start | bytes 1572872 | tf_op jit(solution)/shard_map/ppermute | solution.py:404
  101.8 27.0 %collective-permute-start.14 = (bf16[1024,256]{1,0:T(8,128)(2,1)S(1)}, bf16[1024,256]{1,0:T(8,128)(2,1)S(1)}, u32[]{:S(2)}, u32[]{:S(2)}) collective-permute-start(bf16[1024,256]{1,0:T(8,128)(2,1)S(1)} %copy-done.4), channel_id=1, source_target_pairs={{0,8},{4,12},{8,0},{12,4},{16,24},{20,28},{24,16},{28,20},{1,9},{5... | collective-permute-start | bytes 1572872 | tf_op jit(solution)/shard_map/ppermute | solution.py:404
  113.3 37.7 %collective-permute-start.16 = (bf16[1072,256]{1,0:T(8,128)(2,1)S(1)}, bf16[1072,256]{1,0:T(8,128)(2,1)S(1)}, u32[]{:S(2)}, u32[]{:S(2)}) collective-permute-start(bf16[1072,256]{1,0:T(8,128)(2,1)S(1)} %get-tuple-element.40), channel_id=1, source_target_pairs={{8,16},{12,20},{16,24},{20,28},{9,17},{13,21},{17,25},{21,29},{10,... | collective-permute-start | bytes 1646600 | tf_op jit(solution)/shard_map/ppermute | solution.py:404
  123.8 11.9 %collective-permute-start.13 = (bf16[2,512,256]{2,1,0:T(8,128)(2,1)S(1)}, bf16[2,512,256]{2,1,0:T(8,128)(2,1)S(1)}, u32[]{:S(2)}, u32[]{:S(2)}) collective-permute-start(bf16[2,512,256]{2,1,0:T(8,128)(2,1)S(1)} %merge.2), channel_id=1, source_target_pairs={{0,4},{4,0},{8,12},{12,8},{16,20},{20,16},{24,28},{28,24},{1,5},{5... | collective-permute-start | bytes 1572872 | tf_op jit(solution)/shard_map/ppermute | solution.py:404
  124.5 26.4 %collective-permute-start.17 = (bf16[1072,256]{1,0:T(8,128)(2,1)S(1)}, bf16[1072,256]{1,0:T(8,128)(2,1)S(1)}, u32[]{:S(2)}, u32[]{:S(2)}) collective-permute-start(bf16[1072,256]{1,0:T(8,128)(2,1)S(1)} %get-tuple-element.48), channel_id=1, source_target_pairs={{8,24},{12,28},{0,8},{4,12},{24,16},{28,20},{9,25},{13,29},{1,9},{... | collective-permute-start | bytes 1646600 | tf_op jit(solution)/shard_map/ppermute | solution.py:404
  126.1 24.9 %collective-permute-start.15 = (bf16[1024,256]{1,0:T(8,128)(2,1)S(1)}, bf16[1024,256]{1,0:T(8,128)(2,1)S(1)}, u32[]{:S(2)}, u32[]{:S(2)}) collective-permute-start(bf16[1024,256]{1,0:T(8,128)(2,1)S(1)} %get-tuple-element.76.refs_5_), channel_id=1, source_target_pairs={{0,8},{4,12},{8,0},{12,4},{16,24},{20,28},{24,16},{28,20},{1,9},{5... | collective-permute-start | bytes 1572872 | tf_op jit(solution)/shard_map/ppermute | solution.py:404
  153.4 12.0 %collective-permute-start.18 = (bf16[2,512,256]{2,1,0:T(8,128)(2,1)S(1)}, bf16[2,512,256]{2,1,0:T(8,128)(2,1)S(1)}, u32[]{:S(2)}, u32[]{:S(2)}) collective-permute-start(bf16[2,512,256]{2,1,0:T(8,128)(2,1)S(1)} %merge.3), channel_id=1, source_target_pairs={{0,4},{4,0},{8,12},{12,8},{16,20},{20,16},{24,28},{28,24},{1,5},{5... | collective-permute-start | bytes 1572872 | tf_op jit(solution)/shard_map/ppermute | solution.py:404
  168.3 3.5 %collective-permute-start.23 = (bf16[2,2,2,128,512]{4,3,2,1,0:T(8,128)(2,1)S(1)}, bf16[2,2,2,128,512]{4,3,2,1,0:T(8,128)(2,1)S(1)}, u32[]{:S(2)}, u32[]{:S(2)}) collective-permute-start(bf16[2,2,2,128,512]{4,3,2,1,0:T(8,128)(2,1)S(1)} %get-tuple-element.56), channel_id=1, source_target_pairs={{0,1},{1,0},{2,3},{3,2},{4,5},{5,4},{6,7},{7,6},{8,9},{9,8},{10,11... | collective-permute-start | bytes 3145736 | tf_op jit(solution)/shard_map/ppermute | solution.py:410
  171.3 4.9 %collective-permute-start.19 = (bf16[2,2,2,128,512]{4,3,2,1,0:T(8,128)(2,1)S(1)}, bf16[2,2,2,128,512]{4,3,2,1,0:T(8,128)(2,1)S(1)}, u32[]{:S(2)}, u32[]{:S(2)}) collective-permute-start(bf16[2,2,2,128,512]{4,3,2,1,0:T(8,128)(2,1)S(1)} %get-tuple-element.50), channel_id=1, source_target_pairs={{0,1},{1,0},{2,3},{3,2},{4,5},{5,4},{6,7},{7,6},{8,9},{9,8},{10,11... | collective-permute-start | bytes 3145736 | tf_op jit(solution)/shard_map/ppermute | solution.py:410
  172.7 10.2 %collective-permute-start.24 = (bf16[2,128,512]{2,1,0:T(8,128)(2,1)S(1)}, bf16[2,128,512]{2,1,0:T(8,128)(2,1)S(1)}, u32[]{:S(2)}, u32[]{:S(2)}) collective-permute-start(bf16[2,128,512]{2,1,0:T(8,128)(2,1)S(1)} %get-tuple-element.58), channel_id=1, source_target_pairs={{0,2},{1,3},{2,0},{3,1},{4,6},{5,7},{6,4},{7,5},{8,10},{9,11},{10,... | collective-permute-start | bytes 786440 | tf_op jit(solution)/shard_map/ppermute | solution.py:410
  174.3 11.3 %collective-permute-start.25 = (bf16[2,128,512]{2,1,0:T(8,128)(2,1)S(1)}, bf16[2,128,512]{2,1,0:T(8,128)(2,1)S(1)}, u32[]{:S(2)}, u32[]{:S(2)}) collective-permute-start(bf16[2,128,512]{2,1,0:T(8,128)(2,1)S(1)} %get-tuple-element.59), channel_id=1, source_target_pairs={{0,4},{4,0},{8,12},{12,8},{16,20},{20,16},{24,28},{28,24},{1,5},{5... | collective-permute-start | bytes 786440 | tf_op jit(solution)/shard_map/ppermute | solution.py:404
  176.0 13.1 %collective-permute-start.26 = (bf16[2,128,512]{2,1,0:T(8,128)(2,1)S(1)}, bf16[2,128,512]{2,1,0:T(8,128)(2,1)S(1)}, u32[]{:S(2)}, u32[]{:S(2)}) collective-permute-start(bf16[2,128,512]{2,1,0:T(8,128)(2,1)S(1)} %get-tuple-element.60), channel_id=1, source_target_pairs={{0,6},{1,7},{2,4},{3,5},{4,2},{5,3},{6,0},{7,1},{8,14},{9,15},{10,... | collective-permute-start | bytes 786440 | tf_op jit(solution)/shard_map/ppermute | solution.py:498
  177.0 15.2 %collective-permute-start.20 = (bf16[2,128,512]{2,1,0:T(8,128)(2,1)S(1)}, bf16[2,128,512]{2,1,0:T(8,128)(2,1)S(1)}, u32[]{:S(2)}, u32[]{:S(2)}) collective-permute-start(bf16[2,128,512]{2,1,0:T(8,128)(2,1)S(1)} %get-tuple-element.52), channel_id=1, source_target_pairs={{0,2},{1,3},{2,0},{3,1},{4,6},{5,7},{6,4},{7,5},{8,10},{9,11},{10,... | collective-permute-start | bytes 786440 | tf_op jit(solution)/shard_map/ppermute | solution.py:410
  178.6 16.1 %collective-permute-start.21 = (bf16[2,128,512]{2,1,0:T(8,128)(2,1)S(1)}, bf16[2,128,512]{2,1,0:T(8,128)(2,1)S(1)}, u32[]{:S(2)}, u32[]{:S(2)}) collective-permute-start(bf16[2,128,512]{2,1,0:T(8,128)(2,1)S(1)} %get-tuple-element.53), channel_id=1, source_target_pairs={{0,4},{4,0},{8,12},{12,8},{16,20},{20,16},{24,28},{28,24},{1,5},{5... | collective-permute-start | bytes 786440 | tf_op jit(solution)/shard_map/ppermute | solution.py:404
  182.9 16.1 %collective-permute-start.22 = (bf16[2,128,512]{2,1,0:T(8,128)(2,1)S(1)}, bf16[2,128,512]{2,1,0:T(8,128)(2,1)S(1)}, u32[]{:S(2)}, u32[]{:S(2)}) collective-permute-start(bf16[2,128,512]{2,1,0:T(8,128)(2,1)S(1)} %get-tuple-element.54), channel_id=1, source_target_pairs={{0,6},{1,7},{2,4},{3,5},{4,2},{5,3},{6,0},{7,1},{8,14},{9,15},{10,... | collective-permute-start | bytes 786440 | tf_op jit(solution)/shard_map/ppermute | solution.py:498
  (2 other events, 8.4 us)

commit v10 on v8

--- a/solution.py
+++ b/solution.py
@@ -420,15 +420,16 @@
 
     q_m, q_o = lanes(0, 1, x), swap(lanes(0, 1, 1 - x))
     w_second = seq_perm(out_weight, (0, 2))
+    w_halves = [pieces(out_weight, c) for c in range(chunks)]
     kv_m, kv_give = lanes(1, 3, x), lanes(1, 3, 1 - x)
     q, qs, low = [], [], []
     for c in range(chunks):
         a, b = pieces(q_m, c), pieces(q_o, c)
         q.append(jnp.concatenate([jnp.where(first, a, b), jnp.where(first, b, a)]))
-        block = pieces(out_weight, c).reshape(q[c].shape)
+        block = w_halves[c].reshape(q[c].shape)
         going = [jnp.where(z == 1, block, q[c]), jnp.where(z == 3, q[c], block)]
         if c:
-            going = after(going, *qs[0])
+            going = [after(a, b) for a, b in zip(going, qs[0])]
         qs.append([seq_perm(going[0], (2, 1), (3, 2), (1, 3)), seq_perm(going[1], (3, 1), (1, 0), (2, 3))])
         if c == 0:
             kv_o = swap(after(kv_give, q[0]))
@@ -457,10 +458,16 @@
         turn = after(at, mine)
 
     depth = out_weight.shape[0]
-    w_down = seq_perm(after(out_weight, own[0], *qs[1]), (2, 0), (3, 1))
     w_near = [
         jnp.where((z == 0) | (z == 3), qs[c][1].reshape(depth, width), ob[c][:depth]) for c in range(chunks)
     ]
+    w_down = [seq_perm(after(w_halves[0], own[0], *qs[1]), (2, 0), (3, 1))]
+    w_down.append(seq_perm(after(w_halves[1], w_down[0], sent[1]), (2, 0), (3, 1)))
+
+    def far_half(c, earlier):
+        up = jnp.where(z == 2, pieces(w_second, c), qs[c][0].reshape(depth, width))
+        half = jnp.where(z >= 2, up, after(w_down[c], earlier))
+        return half, seq_perm(half, (0, 1), (1, 0), (2, 3), (3, 2))
 
     def merged(c, earlier):
         (a,) = head_call(
@@ -468,25 +475,23 @@
             [struct((2, cols, width), BF16)], heads, "merge", 2)
         return a, swap(a)
 
+    far_0 = far_half(0, own[1])
     first_half = merged(0, own[1])
-    w_ridden = jnp.concatenate([qs[c][0].reshape(depth, width) for c in range(chunks)], axis=1)
-    w_far = jnp.where(
-        z >= 2, jnp.where(z == 2, w_second, w_ridden), after(w_down, first_half[0], own[1]))
-    near, far = map(list, zip(first_half, merged(1, (w_far, first_half[1]))))
-    w_other = seq_perm(w_far, (0, 1), (1, 0), (2, 3), (3, 2))
+    near, far = map(list, zip(first_half, merged(1, (first_half[1], far_0[1]))))
+    w_far, w_other = map(list, zip(far_0, far_half(1, near[1])))
 
     parts = []
-    turn = after(at, w_other)
+    turn = at
     for weights in (
         [out_weight] + w_near,
-        [w_far, w_other],
+        w_far + w_other,
     ):
         send, kept = project(turn, near, far, weights, out_weight.shape[1])
+        turn = after(at, send)
         got = head_perm(send, 1)
         piece = struct(send.shape[:1] + send.shape[3:], BF16)
         stay, to_y, to_x, to_xy = whole_call(
-            split_kernel, after(at, parts[1:2]), [kept, got], [piece] * 4, "split", 2)
-        turn = after(at, stay)
+            split_kernel, at, [kept, got], [piece] * 4, "split", 2)
         diagonal = [((2 * i + j) * 4 + h, (2 * i + 1 - j) * 4 + (h ^ 2)) for i in range(4) for j in range(2) for h in range(4)]
         from_xy = lax.ppermute(to_xy, ("seq", "head"), diagonal)
         parts += [stay, head_perm(to_y, 2), swap(to_x), from_xy]

time: 189 us -> 195 us (1.032)
  starting transfers between devices: 45.6 us -> 62.2 us
  waiting for transfers between devices: 83.4 us -> 70.2 us
  other arithmetic: 5.9 us -> 8.97 us
    ppermute x20 -> x22, starting transfers between devices: 39.3 us -> 55.5 us  [seq_perm(): return lax.ppermute(array, 'seq', pairs)]
    ppermute x20 -> x22, waiting for transfers between devices: 62.1 us -> 53.9 us  [seq_perm(): return lax.ppermute(array, 'seq', pairs)]
    ppermute x4, waiting for transfers between devices: 13.3 us -> 7.94 us  [head_perm(): return lax.ppermute(array, 'head', [(i, i ^ flip) for i in range(4)])]
    select_n x1 -> x2, other arithmetic: 0.39 us -> 2.45 us  [far_half(): half = jnp.where(z >= 2, up, after(w_down[c], earlier))]
  transfers between devices with their start and end apart: 26 -> 28, of which waited for: 15 -> 16; matrix products, arithmetic and copies ran while one was open for 7% -> 8% of each run, Pallas kernels for 17% -> 19%
where the time goes in v10:
time: 195 us; the launch traced here: 194 us
  waiting for transfers between devices  70.2 us (36%)
  starting transfers between devices  62.2 us (32%)
  Pallas kernels  41.7 us (21%)
  local copies, waits for them, and re-layouts  10.6 us (5%)
  other arithmetic  8.97 us (5%)
    ppermute x22, starting transfers between devices, seq_perm(): return lax.ppermute(array, 'seq', pairs)  55.5 us
    ppermute x22, waiting for transfers between devices, seq_perm(): return lax.ppermute(array, 'seq', pairs)  53.9 us
    pallas_call x6, Pallas kernels, head_call(): pl.pallas_call(kernel, out_shape=outs, grid_spec=pltpu.PrefetchScalarGrid...  31.5 us
    pallas_call x5, Pallas kernels, whole_call(): pl.pallas_call(kernel, out_shape=outs, in_specs=[pl.BlockSpec(memory_spac...  10.3 us
    ppermute x2, waiting for transfers between devices, body_eight(): from_xy = lax.ppermute(to_xy, ('seq', 'head'), diagonal)  8.41 us
    ppermute x4, waiting for transfers between devices, head_perm(): return lax.ppermute(array, 'head', [(i, i ^ flip) for i in range(4)])  7.94 us
    dynamic_slice x2, local copies, waits for them, and re-layouts, lanes(): lax.dynamic_slice(local, (lo, 0, half_of * half), (hi - lo, cols, half))  4.8 us
    slice x4, local copies, waits for them, and re-layouts, pieces(): return array[..., c * width:(c + 1) * width]  3.93 us
  transfers between devices with their start and end apart: 28, of which 16 were waited for; matrix products, arithmetic and copies ran while one was open for 8% of the time, Pallas kernels for 19%

profile of v10, /device:TPU:0, one launch (start us, length us, event | category | flops | bytes accessed | tf_op | source)
XLA Modules:
  0.0 194.1 jit_solution(3621102939598081287)
XLA Ops:
  0.0 2.2 %dynamic-slice_bitcast_fusion.3 = (bf16[1,512,512]{2,1,0:T(8,128)(2,1)S(1)}, bf16[1,512,512]{2,1,0:T(8,128)(2,1)}) fusion(bf16[3,1,512,1024]{3,2,1,0:T(8,128)(2,1)} %param.2, s32[]{:T(128)S(6)} %select_n.106, s32[]{:T(128)S(6)} %select_n.107), kind=kLoop, calls=%fused_computation.12 | loop fusion | bytes 2097160 | tf_op jit(solution)/shard_map/dynamic_slice | solution.py:416
  2.2 2.9 %collective-permute-start = (bf16[1,512,512]{2,1,0:T(8,128)(2,1)}, bf16[1,512,512]{2,1,0:T(8,128)(2,1)S(1)}, u32[]{:S(2)}, u32[]{:S(2)}) collective-permute-start(bf16[1,512,512]{2,1,0:T(8,128)(2,1)} %get-tuple-element.72), channel_id=1, source_target_pairs={{0,4},{4,0},{8,12},{12,8},{16,20},{20,16},{24,28},{28,24},{1,5},{5... | collective-permute-start | bytes 1572872 | tf_op jit(solution)/shard_map/ppermute | solution.py:404
  5.1 5.5 %collective-permute-start.4 = (bf16[1024,512]{1,0:T(8,128)(2,1)}, bf16[1024,512]{1,0:T(8,128)(2,1)}, u32[]{:S(2)}, u32[]{:S(2)}) collective-permute-start(bf16[1024,512]{1,0:T(8,128)(2,1)} %refs_4_.1), channel_id=1, source_target_pairs={{0,16},{4,20},{1,17},{5,21},{2,18},{6,22},{3,19},{7,23}} | collective-permute-start | bytes 3145736 | tf_op jit(solution)/shard_map/ppermute | solution.py:404
  10.6 2.6 %dynamic-slice_bitcast_fusion = (bf16[2,512,512]{2,1,0:T(8,128)(2,1)}, bf16[2,512,512]{2,1,0:T(8,128)(2,1)S(1)}) fusion(bf16[3,1,512,1024]{3,2,1,0:T(8,128)(2,1)} %param.2, s32[]{:T(128)S(6)} %select_n.107, s32[]{:T(128)S(6)} %select_n.106), kind=kLoop, calls=%fused_computation.1 | loop fusion | bytes 4194312 | tf_op jit(solution)/shard_map/dynamic_slice | solution.py:416
  14.1 3.1 %collective-permute-done = bf16[1,512,512]{2,1,0:T(8,128)(2,1)S(1)} collective-permute-done((bf16[1,512,512]{2,1,0:T(8,128)(2,1)}, bf16[1,512,512]{2,1,0:T(8,128)(2,1)S(1)}, u32[]{:S(2)}, u32[]{:S(2)}) %collective-permute-start) | collective-permute-done | bytes 524320 | tf_op jit(solution)/shard_map/ppermute | solution.py:404
  26.7 5.4 %collective-permute-done.4 = bf16[1024,512]{1,0:T(8,128)(2,1)} collective-permute-done((bf16[1024,512]{1,0:T(8,128)(2,1)}, bf16[1024,512]{1,0:T(8,128)(2,1)}, u32[]{:S(2)}, u32[]{:S(2)}) %collective-permute-start.4) | collective-permute-done | bytes 1048608 | tf_op jit(solution)/shard_map/ppermute | solution.py:404
  32.1 2.9 %collective-permute-start.5 = (bf16[2,512,256]{2,1,0:T(8,128)(2,1)S(1)}, bf16[2,512,256]{2,1,0:T(8,128)(2,1)S(1)}, u32[]{:S(2)}, u32[]{:S(2)}) collective-permute-start(bf16[2,512,256]{2,1,0:T(8,128)(2,1)S(1)} %get-tuple-element.38), channel_id=1, source_target_pairs={{0,8},{4,12},{1,9},{5,13},{2,10},{6,14},{3,11},{7,15}} | collective-permute-start | bytes 1572872 | tf_op jit(solution)/shard_map/ppermute | solution.py:404
  41.2 4.4 %collective-permute-done.3.kv_o = bf16[2,512,512]{2,1,0:T(8,128)(2,1)} collective-permute-done((bf16[2,512,512]{2,1,0:T(8,128)(2,1)}, bf16[2,512,512]{2,1,0:T(8,128)(2,1)}, u32[]{:S(2)}, u32[]{:S(2)}) %collective-permute-start.3) | collective-permute-done | bytes 1048608 | tf_op jit(solution)/shard_map/ppermute | solution.py:404
  47.3 8.5 %collective-permute-done.6.refs_1_ = bf16[2,512,256]{2,1,0:T(8,128)(2,1)S(1)} collective-permute-done((bf16[2,512,256]{2,1,0:T(8,128)(2,1)}, bf16[2,512,256]{2,1,0:T(8,128)(2,1)S(1)}, u32[]{:S(2)}, u32[]{:S(2)}) %collective-permute-start.6) | collective-permute-done | bytes 524320 | tf_op jit(solution)/shard_map/ppermute | solution.py:404
  55.8 5.9 %collective-permute-start.9 = (bf16[4,512,256]{2,1,0:T(8,128)(2,1)S(1)}, bf16[4,512,256]{2,1,0:T(8,128)(2,1)S(1)}, u32[]{:S(2)}, u32[]{:S(2)}) collective-permute-start(bf16[4,512,256]{2,1,0:T(8,128)(2,1)S(1)} %pad_maximum_fusion), channel_id=1, source_target_pairs={{0,8},{4,12},{1,9},{5,13},{2,10},{6,14},{3,11},{7,15}} | collective-permute-start | bytes 3145736 | tf_op jit(solution)/shard_map/ppermute | solution.py:404
  61.6 6.6 %upper_rows.2 = (bf16[1072,256]{1,0:T(8,128)(2,1)S(1)}, bf16[1072,256]{1,0:T(8,128)(2,1)S(1)}) custom-call(s32[4]{0:T(128)S(1)} %pad_add_fusion.at, bf16[2,512,256]{2,1,0:T(8,128)(2,1)S(1)} %collective-permute-done.1.qa, bf16[2,512,256]{2,1,0:T(8,128)(2,1)S(1)} %collective-permute-done.2.qb, bf16[2,512,512]{2,1,0:T(8,128)(2,1)S(1)} %get-tuple-element.70.kv_m, ...), custom_call_target="tpu_custom_call" | custom-call | flops 7000000000 | bytes 1024 | tf_op jit(solution)/shard_map/upper_rows/pallas_call | solution.py:300
  69.1 5.9 %own_rows.2.own = bf16[1072,256]{1,0:T(8,128)(2,1)S(1)} custom-call(s32[4]{0:T(128)S(1)} %pad_add_fusion.at, bf16[2,512,256]{2,1,0:T(8,128)(2,1)S(1)} %get-tuple-element.86.q, bf16[2,512,512]{2,1,0:T(8,128)(2,1)S(1)} %get-tuple-element.70.kv_m, bf16[2,512,512]{2,1,0:T(8,128)(2,1)} %collective-permute-done.3.kv_o, ...), custom_call_target="tpu_custom_call" | custom-call | flops 6000000000 | bytes 1024 | tf_op jit(solution)/shard_map/own_rows/pallas_call | solution.py:300
  76.4 6.8 %collective-permute-start.11 = (bf16[1072,256]{1,0:T(8,128)(2,1)S(1)}, bf16[1072,256]{1,0:T(8,128)(2,1)S(1)}, u32[]{:S(2)}, u32[]{:S(2)}) collective-permute-start(bf16[1072,256]{1,0:T(8,128)(2,1)S(1)} %get-tuple-element.49), channel_id=1, source_target_pairs={{8,24},{12,28},{0,8},{4,12},{24,16},{28,20},{9,25},{13,29},{1,9},{... | collective-permute-start | bytes 1646600 | tf_op jit(solution)/shard_map/ppermute | solution.py:404
  83.3 7.3 %upper_rows.3 = (bf16[1072,256]{1,0:T(8,128)(2,1)}, bf16[1072,256]{1,0:T(8,128)(2,1)}) custom-call(s32[4]{0:T(128)S(1)} %pad_add_fusion.at, bf16[2,512,256]{2,1,0:T(8,128)(2,1)S(1)} %collective-permute-done.7.qa, bf16[2,512,256]{2,1,0:T(8,128)(2,1)S(1)} %collective-permute-done.8.qb, bf16[2,512,512]{2,1,0:T(8,128)(2,1)S(1)} %get-tuple-element.70.kv_m, ...), custom_call_target="tpu_custom_call" | custom-call | flops 7000000000 | bytes 1024 | tf_op jit(solution)/shard_map/upper_rows/pallas_call | solution.py:300
  92.1 6.0 %own_rows.3.own = bf16[1072,256]{1,0:T(8,128)(2,1)S(1)} custom-call(s32[4]{0:T(128)S(1)} %pad_add_fusion.at, bf16[2,512,256]{2,1,0:T(8,128)(2,1)S(1)} %get-tuple-element.85.q, bf16[2,512,512]{2,1,0:T(8,128)(2,1)S(1)} %get-tuple-element.70.kv_m, bf16[2,512,512]{2,1,0:T(8,128)(2,1)} %collective-permute-done.3.kv_o, ...), custom_call_target="tpu_custom_call" | custom-call | flops 6000000000 | bytes 1024 | tf_op jit(solution)/shard_map/own_rows/pallas_call | solution.py:300
  98.1 5.2 %collective-permute-done.13 = bf16[1024,256]{1,0:T(8,128)(2,1)S(1)} collective-permute-done((bf16[1024,256]{1,0:T(8,128)(2,1)S(1)}, bf16[1024,256]{1,0:T(8,128)(2,1)S(1)}, u32[]{:S(2)}, u32[]{:S(2)}) %collective-permute-start.13) | collective-permute-done | bytes 524320 | tf_op jit(solution)/shard_map/ppermute | solution.py:404
  103.3 2.4 %merge.2 = bf16[2,512,256]{2,1,0:T(8,128)(2,1)S(1)} custom-call(s32[4]{0:T(128)S(1)} %pad_add_fusion.at, bf16[1072,256]{1,0:T(8,128)(2,1)S(1)} %own_rows.2.own, bf16[1072,256]{1,0:T(8,128)(2,1)S(1)} %collective-permute-done.10.oa, bf16[1072,256]{1,0:T(8,128)(2,1)S(1)} %collective-permute-done.11.ob), custom_call_target="tpu_custom_call" | custom-call | flops 2000000000 | bytes 1024 | tf_op jit(solution)/shard_map/merge/pallas_call | solution.py:300
  109.6 3.8 %collective-permute-start.14 = (bf16[1024,256]{1,0:T(8,128)(2,1)S(1)}, bf16[1024,256]{1,0:T(8,128)(2,1)}, u32[]{:S(2)}, u32[]{:S(2)}) collective-permute-start(bf16[1024,256]{1,0:T(8,128)(2,1)S(1)} %fusion.1.refs_4_), channel_id=1, source_target_pairs={{0,8},{4,12},{8,0},{12,4},{16,24},{20,28},{24,16},{28,20},{1,9},{5... | collective-permute-start | bytes 1572872 | tf_op jit(solution)/shard_map/ppermute | solution.py:404
  115.8 3.1 %collective-permute-done.12 = bf16[2,512,256]{2,1,0:T(8,128)(2,1)} collective-permute-done((bf16[2,512,256]{2,1,0:T(8,128)(2,1)S(1)}, bf16[2,512,256]{2,1,0:T(8,128)(2,1)}, u32[]{:S(2)}, u32[]{:S(2)}) %collective-permute-start.12) | collective-permute-done | bytes 524320 | tf_op jit(solution)/shard_map/ppermute | solution.py:404
  118.9 15.8 %collective-permute-done.14.refs_6_ = bf16[1024,256]{1,0:T(8,128)(2,1)} collective-permute-done((bf16[1024,256]{1,0:T(8,128)(2,1)S(1)}, bf16[1024,256]{1,0:T(8,128)(2,1)}, u32[]{:S(2)}, u32[]{:S(2)}) %collective-permute-start.14) | collective-permute-done | bytes 524320 | tf_op jit(solution)/shard_map/ppermute | solution.py:404
  135.8 3.2 %merge.3 = bf16[2,512,256]{2,1,0:T(8,128)(2,1)S(1)} custom-call(s32[4]{0:T(128)S(1)} %pad_add_fusion.at, bf16[1072,256]{1,0:T(8,128)(2,1)S(1)} %copy-done.9, bf16[1072,256]{1,0:T(8,128)(2,1)} %collective-permute-done.15.oa, bf16[1072,256]{1,0:T(8,128)(2,1)} %collective-permute-done.16.ob), custom_call_target="tpu_custom_call" | custom-call | flops 2000000000 | bytes 1024 | tf_op jit(solution)/shard_map/merge/pallas_call | solution.py:300
  141.9 8.6 %collective-permute-start.23 = (bf16[1024,256]{1,0:T(8,128)(2,1)S(1)}, bf16[1024,256]{1,0:T(8,128)(2,1)S(1)}, u32[]{:S(2)}, u32[]{:S(2)}) collective-permute-start(bf16[1024,256]{1,0:T(8,128)(2,1)S(1)} %fusion.refs_5_), channel_id=1, source_target_pairs={{0,8},{4,12},{8,0},{12,4},{16,24},{20,28},{24,16},{28,20},{1,9},{5... | collective-permute-start | bytes 1572872 | tf_op jit(solution)/shard_map/ppermute | solution.py:404
  151.5 3.4 %project.2 = (bf16[2,2,2,128,512]{4,3,2,1,0:T(8,128)(2,1)S(1)}, bf16[2,2,2,128,512]{4,3,2,1,0:T(8,128)(2,1)S(1)}) custom-call(s32[4]{0:T(128)S(1)} %pad_add_fusion.at, bf16[2,2,2,128,256]{4,3,2,1,0:T(8,128)(2,1)S(1)} %bitcast.27, bf16[2,2,2,128,256]{4,3,2,1,0:T(8,128)(2,1)S(1)} %bitcast.29, bf16[2,2,2,128,256]{4,3,2,1,0:T(8,128)(2,1)} %bitcast.13.refs_2_, ...), custom_call_target="tpu_custom_call" | custom-call | flops 4000000000 | bytes 1024 | tf_op jit(solution)/shard_map/project/pallas_call | solution.py:349
  154.9 3.8 %collective-permute-done.23.refs_7_ = bf16[1024,256]{1,0:T(8,128)(2,1)S(1)} collective-permute-done((bf16[1024,256]{1,0:T(8,128)(2,1)S(1)}, bf16[1024,256]{1,0:T(8,128)(2,1)S(1)}, u32[]{:S(2)}, u32[]{:S(2)}) %collective-permute-start.23) | collective-permute-done | bytes 524320 | tf_op jit(solution)/shard_map/ppermute | solution.py:404
  158.8 3.6 %project.3 = (bf16[2,2,2,128,512]{4,3,2,1,0:T(8,128)(2,1)S(1)}, bf16[2,2,2,128,512]{4,3,2,1,0:T(8,128)(2,1)S(1)}) custom-call(s32[4]{0:T(128)S(1)} %pad_add_fusion.at, bf16[2,2,2,128,256]{4,3,2,1,0:T(8,128)(2,1)S(1)} %bitcast.28, bf16[2,2,2,128,256]{4,3,2,1,0:T(8,128)(2,1)S(1)} %bitcast.30, bf16[2,2,2,128,256]{4,3,2,1,0:T(8,128)(2,1)} %bitcast.13.refs_2_, ...), custom_call_target="tpu_custom_call" | custom-call | flops 4000000000 | bytes 1024 | tf_op jit(solution)/shard_map/project/pallas_call | solution.py:349
  162.9 2.1 %collective-permute-done.24.got = bf16[2,2,2,128,512]{4,3,2,1,0:T(8,128)(2,1)S(1)} collective-permute-done((bf16[2,2,2,128,512]{4,3,2,1,0:T(8,128)(2,1)S(1)}, bf16[2,2,2,128,512]{4,3,2,1,0:T(8,128)(2,1)S(1)}, u32[]{:S(2)}, u32[]{:S(2)}) %collective-permute-start.24) | collective-permute-done | bytes 1048608 | tf_op jit(solution)/shard_map/ppermute | solution.py:410
  173.3 2.5 %collective-permute-done.25.refs_5_ = bf16[2,128,512]{2,1,0:T(8,128)(2,1)S(1)} collective-permute-done((bf16[2,128,512]{2,1,0:T(8,128)(2,1)S(1)}, bf16[2,128,512]{2,1,0:T(8,128)(2,1)S(1)}, u32[]{:S(2)}, u32[]{:S(2)}) %collective-permute-start.25) | collective-permute-done | bytes 262176 | tf_op jit(solution)/shard_map/ppermute | solution.py:410
  175.8 2.4 %collective-permute-start.21 = (bf16[2,128,512]{2,1,0:T(8,128)(2,1)S(1)}, bf16[2,128,512]{2,1,0:T(8,128)(2,1)S(1)}, u32[]{:S(2)}, u32[]{:S(2)}) collective-permute-start(bf16[2,128,512]{2,1,0:T(8,128)(2,1)S(1)} %get-tuple-element.59), channel_id=1, source_target_pairs={{0,6},{1,7},{2,4},{3,5},{4,2},{5,3},{6,0},{7,1},{8,14},{9,15},{10,... | collective-permute-start | bytes 786440 | tf_op jit(solution)/shard_map/ppermute | solution.py:496
  178.3 4.0 %collective-permute-done.27.refs_7_ = bf16[2,128,512]{2,1,0:T(8,128)(2,1)S(1)} collective-permute-done((bf16[2,128,512]{2,1,0:T(8,128)(2,1)S(1)}, bf16[2,128,512]{2,1,0:T(8,128)(2,1)S(1)}, u32[]{:S(2)}, u32[]{:S(2)}) %collective-permute-start.27) | collective-permute-done | bytes 262176 | tf_op jit(solution)/shard_map/ppermute | solution.py:496
  182.2 3.3 %collective-permute-done.19.refs_1_ = bf16[2,128,512]{2,1,0:T(8,128)(2,1)S(1)} collective-permute-done((bf16[2,128,512]{2,1,0:T(8,128)(2,1)S(1)}, bf16[2,128,512]{2,1,0:T(8,128)(2,1)S(1)}, u32[]{:S(2)}, u32[]{:S(2)}) %collective-permute-start.19) | collective-permute-done | bytes 262176 | tf_op jit(solution)/shard_map/ppermute | solution.py:410
  185.5 2.4 %collective-permute-done.20.refs_2_ = bf16[2,128,512]{2,1,0:T(8,128)(2,1)S(1)} collective-permute-done((bf16[2,128,512]{2,1,0:T(8,128)(2,1)S(1)}, bf16[2,128,512]{2,1,0:T(8,128)(2,1)S(1)}, u32[]{:S(2)}, u32[]{:S(2)}) %collective-permute-start.20) | collective-permute-done | bytes 262176 | tf_op jit(solution)/shard_map/ppermute | solution.py:404
  187.9 4.4 %collective-permute-done.21.refs_3_ = bf16[2,128,512]{2,1,0:T(8,128)(2,1)S(1)} collective-permute-done((bf16[2,128,512]{2,1,0:T(8,128)(2,1)S(1)}, bf16[2,128,512]{2,1,0:T(8,128)(2,1)S(1)}, u32[]{:S(2)}, u32[]{:S(2)}) %collective-permute-start.21) | collective-permute-done | bytes 262176 | tf_op jit(solution)/shard_map/ppermute | solution.py:496
  (78 shorter events, 43.6 us)
Async XLA Ops:
  2.2 15.1 %collective-permute-start = (bf16[1,512,512]{2,1,0:T(8,128)(2,1)}, bf16[1,512,512]{2,1,0:T(8,128)(2,1)S(1)}, u32[]{:S(2)}, u32[]{:S(2)}) collective-permute-start(bf16[1,512,512]{2,1,0:T(8,128)(2,1)} %get-tuple-element.72), channel_id=1, source_target_pairs={{0,4},{4,0},{8,12},{12,8},{16,20},{20,16},{24,28},{28,24},{1,5},{5... | collective-permute-start | bytes 1572872 | tf_op jit(solution)/shard_map/ppermute | solution.py:404
  5.1 27.0 %collective-permute-start.4 = (bf16[1024,512]{1,0:T(8,128)(2,1)}, bf16[1024,512]{1,0:T(8,128)(2,1)}, u32[]{:S(2)}, u32[]{:S(2)}) collective-permute-start(bf16[1024,512]{1,0:T(8,128)(2,1)} %refs_4_.1), channel_id=1, source_target_pairs={{0,16},{4,20},{1,17},{5,21},{2,18},{6,22},{3,19},{7,23}} | collective-permute-start | bytes 3145736 | tf_op jit(solution)/shard_map/ppermute | solution.py:404
  21.0 24.7 %collective-permute-start.3 = (bf16[2,512,512]{2,1,0:T(8,128)(2,1)}, bf16[2,512,512]{2,1,0:T(8,128)(2,1)}, u32[]{:S(2)}, u32[]{:S(2)}) collective-permute-start(bf16[2,512,512]{2,1,0:T(8,128)(2,1)} %get-tuple-element.37), channel_id=1, source_target_pairs={{0,4},{4,0},{8,12},{12,8},{16,20},{20,16},{24,28},{28,24},{1,5},{5... | collective-permute-start | bytes 3145736 | tf_op jit(solution)/shard_map/ppermute | solution.py:404
  24.6 14.6 %collective-permute-start.2 = (bf16[2,512,256]{2,1,0:T(8,128)(2,1)}, bf16[2,512,256]{2,1,0:T(8,128)(2,1)S(1)}, u32[]{:S(2)}, u32[]{:S(2)}) collective-permute-start(bf16[2,512,256]{2,1,0:T(8,128)(2,1)} %get-tuple-element.83), channel_id=1, source_target_pairs={{24,8},{28,12},{8,0},{12,4},{16,24},{20,28},{25,9},{29,13},{9,1},{... | collective-permute-start | bytes 1572872 | tf_op jit(solution)/shard_map/ppermute | solution.py:404
  25.9 13.3 %collective-permute-start.1 = (bf16[2,512,256]{2,1,0:T(8,128)(2,1)}, bf16[2,512,256]{2,1,0:T(8,128)(2,1)S(1)}, u32[]{:S(2)}, u32[]{:S(2)}) collective-permute-start(bf16[2,512,256]{2,1,0:T(8,128)(2,1)} %get-tuple-element.84), channel_id=1, source_target_pairs={{16,8},{20,12},{24,16},{28,20},{8,24},{12,28},{17,9},{21,13},{25,1... | collective-permute-start | bytes 1572872 | tf_op jit(solution)/shard_map/ppermute | solution.py:404
  32.1 15.2 %collective-permute-start.5 = (bf16[2,512,256]{2,1,0:T(8,128)(2,1)S(1)}, bf16[2,512,256]{2,1,0:T(8,128)(2,1)S(1)}, u32[]{:S(2)}, u32[]{:S(2)}) collective-permute-start(bf16[2,512,256]{2,1,0:T(8,128)(2,1)S(1)} %get-tuple-element.38), channel_id=1, source_target_pairs={{0,8},{4,12},{1,9},{5,13},{2,10},{6,14},{3,11},{7,15}} | collective-permute-start | bytes 1572872 | tf_op jit(solution)/shard_map/ppermute | solution.py:404
  35.0 20.8 %collective-permute-start.6 = (bf16[2,512,256]{2,1,0:T(8,128)(2,1)}, bf16[2,512,256]{2,1,0:T(8,128)(2,1)S(1)}, u32[]{:S(2)}, u32[]{:S(2)}) collective-permute-start(bf16[2,512,256]{2,1,0:T(8,128)(2,1)} %slice.59), channel_id=1, source_target_pairs={{0,12},{4,8},{1,13},{5,9},{2,14},{6,10},{3,15},{7,11}} | collective-permute-start | bytes 1572872 | tf_op jit(solution)/shard_map/ppermute | solution.py:404
  39.2 35.9 %collective-permute-start.7 = (bf16[2,512,256]{2,1,0:T(8,128)(2,1)S(1)}, bf16[2,512,256]{2,1,0:T(8,128)(2,1)S(1)}, u32[]{:S(2)}, u32[]{:S(2)}) collective-permute-start(bf16[2,512,256]{2,1,0:T(8,128)(2,1)S(1)} %get-tuple-element.43), channel_id=1, source_target_pairs={{16,8},{20,12},{24,16},{28,20},{8,24},{12,28},{17,9},{21,13},{25,1... | collective-permute-start | bytes 1572872 | tf_op jit(solution)/shard_map/ppermute | solution.py:404
  39.9 35.2 %collective-permute-start.8 = (bf16[2,512,256]{2,1,0:T(8,128)(2,1)S(1)}, bf16[2,512,256]{2,1,0:T(8,128)(2,1)S(1)}, u32[]{:S(2)}, u32[]{:S(2)}) collective-permute-start(bf16[2,512,256]{2,1,0:T(8,128)(2,1)S(1)} %get-tuple-element.44), channel_id=1, source_target_pairs={{24,8},{28,12},{8,0},{12,4},{16,24},{20,28},{25,9},{29,13},{9,1},{... | collective-permute-start | bytes 1572872 | tf_op jit(solution)/shard_map/ppermute | solution.py:404
  55.8 27.5 %collective-permute-start.9 = (bf16[4,512,256]{2,1,0:T(8,128)(2,1)S(1)}, bf16[4,512,256]{2,1,0:T(8,128)(2,1)S(1)}, u32[]{:S(2)}, u32[]{:S(2)}) collective-permute-start(bf16[4,512,256]{2,1,0:T(8,128)(2,1)S(1)} %pad_maximum_fusion), channel_id=1, source_target_pairs={{0,8},{4,12},{1,9},{5,13},{2,10},{6,14},{3,11},{7,15}} | collective-permute-start | bytes 3145736 | tf_op jit(solution)/shard_map/ppermute | solution.py:404
  68.3 35.0 %collective-permute-start.10 = (bf16[1072,256]{1,0:T(8,128)(2,1)S(1)}, bf16[1072,256]{1,0:T(8,128)(2,1)S(1)}, u32[]{:S(2)}, u32[]{:S(2)}) collective-permute-start(bf16[1072,256]{1,0:T(8,128)(2,1)S(1)} %get-tuple-element.40), channel_id=1, source_target_pairs={{8,16},{12,20},{16,24},{20,28},{9,17},{13,21},{17,25},{21,29},{10,... | collective-permute-start | bytes 1646600 | tf_op jit(solution)/shard_map/ppermute | solution.py:404
  75.1 15.5 %copy-start.3 = (bf16[2,512,256]{2,1,0:T(8,128)(2,1)}, bf16[2,512,256]{2,1,0:T(8,128)(2,1)S(1)}, u32[]{:S(2)}) copy-start(bf16[2,512,256]{2,1,0:T(8,128)(2,1)S(1)} %collective-permute-done.7.qa) | copy-start | bytes 1572868
  75.1 28.2 %collective-permute-start.13 = (bf16[1024,256]{1,0:T(8,128)(2,1)S(1)}, bf16[1024,256]{1,0:T(8,128)(2,1)S(1)}, u32[]{:S(2)}, u32[]{:S(2)}) collective-permute-start(bf16[1024,256]{1,0:T(8,128)(2,1)S(1)} %copy-done.12), channel_id=1, source_target_pairs={{16,0},{20,4},{24,8},{28,12},{17,1},{21,5},{25,9},{29,13},{18,2},{... | collective-permute-start | bytes 1572872 | tf_op jit(solution)/shard_map/ppermute | solution.py:404
  76.4 26.9 %collective-permute-start.11 = (bf16[1072,256]{1,0:T(8,128)(2,1)S(1)}, bf16[1072,256]{1,0:T(8,128)(2,1)S(1)}, u32[]{:S(2)}, u32[]{:S(2)}) collective-permute-start(bf16[1072,256]{1,0:T(8,128)(2,1)S(1)} %get-tuple-element.49), channel_id=1, source_target_pairs={{8,24},{12,28},{0,8},{4,12},{24,16},{28,20},{9,25},{13,29},{1,9},{... | collective-permute-start | bytes 1646600 | tf_op jit(solution)/shard_map/ppermute | solution.py:404
  90.6 44.1 %collective-permute-start.15 = (bf16[1072,256]{1,0:T(8,128)(2,1)}, bf16[1072,256]{1,0:T(8,128)(2,1)}, u32[]{:S(2)}, u32[]{:S(2)}) collective-permute-start(bf16[1072,256]{1,0:T(8,128)(2,1)} %get-tuple-element.46), channel_id=1, source_target_pairs={{8,16},{12,20},{16,24},{20,28},{9,17},{13,21},{17,25},{21,29},{10,... | collective-permute-start | bytes 1646600 | tf_op jit(solution)/shard_map/ppermute | solution.py:404
  105.8 33.2 %copy-start.6 = (bf16[2,512,256]{2,1,0:T(8,128)(2,1)}, bf16[2,512,256]{2,1,0:T(8,128)(2,1)S(1)}, u32[]{:S(2)}) copy-start(bf16[2,512,256]{2,1,0:T(8,128)(2,1)S(1)} %merge.2) | copy-start | bytes 1572868
  105.8 13.2 %collective-permute-start.12 = (bf16[2,512,256]{2,1,0:T(8,128)(2,1)S(1)}, bf16[2,512,256]{2,1,0:T(8,128)(2,1)}, u32[]{:S(2)}, u32[]{:S(2)}) collective-permute-start(bf16[2,512,256]{2,1,0:T(8,128)(2,1)S(1)} %merge.2), channel_id=1, source_target_pairs={{0,4},{4,0},{8,12},{12,8},{16,20},{20,16},{24,28},{28,24},{1,5},{5... | collective-permute-start | bytes 1572872 | tf_op jit(solution)/shard_map/ppermute | solution.py:404
  106.4 28.3 %collective-permute-start.16 = (bf16[1072,256]{1,0:T(8,128)(2,1)}, bf16[1072,256]{1,0:T(8,128)(2,1)}, u32[]{:S(2)}, u32[]{:S(2)}) collective-permute-start(bf16[1072,256]{1,0:T(8,128)(2,1)} %get-tuple-element.53), channel_id=1, source_target_pairs={{8,24},{12,28},{0,8},{4,12},{24,16},{28,20},{9,25},{13,29},{1,9},{... | collective-permute-start | bytes 1646600 | tf_op jit(solution)/shard_map/ppermute | solution.py:404
  109.6 25.1 %collective-permute-start.14 = (bf16[1024,256]{1,0:T(8,128)(2,1)S(1)}, bf16[1024,256]{1,0:T(8,128)(2,1)}, u32[]{:S(2)}, u32[]{:S(2)}) collective-permute-start(bf16[1024,256]{1,0:T(8,128)(2,1)S(1)} %fusion.1.refs_4_), channel_id=1, source_target_pairs={{0,8},{4,12},{8,0},{12,4},{16,24},{20,28},{24,16},{28,20},{1,9},{5... | collective-permute-start | bytes 1572872 | tf_op jit(solution)/shard_map/ppermute | solution.py:404
  113.4 27.1 %collective-permute-start.22 = (bf16[1024,256]{1,0:T(8,128)(2,1)S(1)}, bf16[1024,256]{1,0:T(8,128)(2,1)}, u32[]{:S(2)}, u32[]{:S(2)}) collective-permute-start(bf16[1024,256]{1,0:T(8,128)(2,1)S(1)} %copy-done.10), channel_id=1, source_target_pairs={{16,0},{20,4},{24,8},{28,12},{17,1},{21,5},{25,9},{29,13},{18,2},{... | collective-permute-start | bytes 1572872 | tf_op jit(solution)/shard_map/ppermute | solution.py:404
  115.8 24.7 %copy-start.4 = (bf16[2,512,256]{2,1,0:T(8,128)(2,1)S(1)}, bf16[2,512,256]{2,1,0:T(8,128)(2,1)}, u32[]{:S(2)}) copy-start(bf16[2,512,256]{2,1,0:T(8,128)(2,1)} %copy-done.3) | copy-start | bytes 1572868
  115.8 34.6 %copy-start.2 = (bf16[2,512,256]{2,1,0:T(8,128)(2,1)S(1)}, bf16[2,512,256]{2,1,0:T(8,128)(2,1)}, u32[]{:S(2)}) copy-start(bf16[2,512,256]{2,1,0:T(8,128)(2,1)} %copy-done.1) | copy-start | bytes 1572868
  139.0 12.6 %collective-permute-start.17 = (bf16[2,512,256]{2,1,0:T(8,128)(2,1)S(1)}, bf16[2,512,256]{2,1,0:T(8,128)(2,1)S(1)}, u32[]{:S(2)}, u32[]{:S(2)}) collective-permute-start(bf16[2,512,256]{2,1,0:T(8,128)(2,1)S(1)} %merge.3), channel_id=1, source_target_pairs={{0,4},{4,0},{8,12},{12,8},{16,20},{20,16},{24,28},{28,24},{1,5},{5... | collective-permute-start | bytes 1572872 | tf_op jit(solution)/shard_map/ppermute | solution.py:404
  141.9 16.9 %collective-permute-start.23 = (bf16[1024,256]{1,0:T(8,128)(2,1)S(1)}, bf16[1024,256]{1,0:T(8,128)(2,1)S(1)}, u32[]{:S(2)}, u32[]{:S(2)}) collective-permute-start(bf16[1024,256]{1,0:T(8,128)(2,1)S(1)} %fusion.refs_5_), channel_id=1, source_target_pairs={{0,8},{4,12},{8,0},{12,4},{16,24},{20,28},{24,16},{28,20},{1,9},{5... | collective-permute-start | bytes 1572872 | tf_op jit(solution)/shard_map/ppermute | solution.py:404
  162.3 2.7 %collective-permute-start.24 = (bf16[2,2,2,128,512]{4,3,2,1,0:T(8,128)(2,1)S(1)}, bf16[2,2,2,128,512]{4,3,2,1,0:T(8,128)(2,1)S(1)}, u32[]{:S(2)}, u32[]{:S(2)}) collective-permute-start(bf16[2,2,2,128,512]{4,3,2,1,0:T(8,128)(2,1)S(1)} %get-tuple-element.64), channel_id=1, source_target_pairs={{0,1},{1,0},{2,3},{3,2},{4,5},{5,4},{6,7},{7,6},{8,9},{9,8},{10,11... | collective-permute-start | bytes 3145736 | tf_op jit(solution)/shard_map/ppermute | solution.py:410
  162.4 7.0 %collective-permute-start.18 = (bf16[2,2,2,128,512]{4,3,2,1,0:T(8,128)(2,1)S(1)}, bf16[2,2,2,128,512]{4,3,2,1,0:T(8,128)(2,1)S(1)}, u32[]{:S(2)}, u32[]{:S(2)}) collective-permute-start(bf16[2,2,2,128,512]{4,3,2,1,0:T(8,128)(2,1)S(1)} %get-tuple-element.55), channel_id=1, source_target_pairs={{0,1},{1,0},{2,3},{3,2},{4,5},{5,4},{6,7},{7,6},{8,9},{9,8},{10,11... | collective-permute-start | bytes 3145736 | tf_op jit(solution)/shard_map/ppermute | solution.py:410
  165.9 10.0 %collective-permute-start.25 = (bf16[2,128,512]{2,1,0:T(8,128)(2,1)S(1)}, bf16[2,128,512]{2,1,0:T(8,128)(2,1)S(1)}, u32[]{:S(2)}, u32[]{:S(2)}) collective-permute-start(bf16[2,128,512]{2,1,0:T(8,128)(2,1)S(1)} %get-tuple-element.66), channel_id=1, source_target_pairs={{0,2},{1,3},{2,0},{3,1},{4,6},{5,7},{6,4},{7,5},{8,10},{9,11},{10,... | collective-permute-start | bytes 786440 | tf_op jit(solution)/shard_map/ppermute | solution.py:410
  167.5 10.8 %collective-permute-start.26 = (bf16[2,128,512]{2,1,0:T(8,128)(2,1)S(1)}, bf16[2,128,512]{2,1,0:T(8,128)(2,1)S(1)}, u32[]{:S(2)}, u32[]{:S(2)}) collective-permute-start(bf16[2,128,512]{2,1,0:T(8,128)(2,1)S(1)} %get-tuple-element.67), channel_id=1, source_target_pairs={{0,4},{4,0},{8,12},{12,8},{16,20},{20,16},{24,28},{28,24},{1,5},{5... | collective-permute-start | bytes 786440 | tf_op jit(solution)/shard_map/ppermute | solution.py:404
  168.9 13.3 %collective-permute-start.27 = (bf16[2,128,512]{2,1,0:T(8,128)(2,1)S(1)}, bf16[2,128,512]{2,1,0:T(8,128)(2,1)S(1)}, u32[]{:S(2)}, u32[]{:S(2)}) collective-permute-start(bf16[2,128,512]{2,1,0:T(8,128)(2,1)S(1)} %get-tuple-element.68), channel_id=1, source_target_pairs={{0,6},{1,7},{2,4},{3,5},{4,2},{5,3},{6,0},{7,1},{8,14},{9,15},{10,... | collective-permute-start | bytes 786440 | tf_op jit(solution)/shard_map/ppermute | solution.py:496
  170.2 15.3 %collective-permute-start.19 = (bf16[2,128,512]{2,1,0:T(8,128)(2,1)S(1)}, bf16[2,128,512]{2,1,0:T(8,128)(2,1)S(1)}, u32[]{:S(2)}, u32[]{:S(2)}) collective-permute-start(bf16[2,128,512]{2,1,0:T(8,128)(2,1)S(1)} %get-tuple-element.57), channel_id=1, source_target_pairs={{0,2},{1,3},{2,0},{3,1},{4,6},{5,7},{6,4},{7,5},{8,10},{9,11},{10,... | collective-permute-start | bytes 786440 | tf_op jit(solution)/shard_map/ppermute | solution.py:410
  171.8 16.1 %collective-permute-start.20 = (bf16[2,128,512]{2,1,0:T(8,128)(2,1)S(1)}, bf16[2,128,512]{2,1,0:T(8,128)(2,1)S(1)}, u32[]{:S(2)}, u32[]{:S(2)}) collective-permute-start(bf16[2,128,512]{2,1,0:T(8,128)(2,1)S(1)} %get-tuple-element.58), channel_id=1, source_target_pairs={{0,4},{4,0},{8,12},{12,8},{16,20},{20,16},{24,28},{28,24},{1,5},{5... | collective-permute-start | bytes 786440 | tf_op jit(solution)/shard_map/ppermute | solution.py:404
  175.8 16.5 %collective-permute-start.21 = (bf16[2,128,512]{2,1,0:T(8,128)(2,1)S(1)}, bf16[2,128,512]{2,1,0:T(8,128)(2,1)S(1)}, u32[]{:S(2)}, u32[]{:S(2)}) collective-permute-start(bf16[2,128,512]{2,1,0:T(8,128)(2,1)S(1)} %get-tuple-element.59), channel_id=1, source_target_pairs={{0,6},{1,7},{2,4},{3,5},{4,2},{5,3},{6,0},{7,1},{8,14},{9,15},{10,... | collective-permute-start | bytes 786440 | tf_op jit(solution)/shard_map/ppermute | solution.py:496
  (10 other events, 79.6 us)

commit v11 on v10

--- a/solution.py
+++ b/solution.py
@@ -263,8 +263,8 @@
             o2, l2 = attend(q[1, mine], [], [ce, co] + low, coef)
             o1, o2 = o1.astype(BF16), o2.astype(BF16)
             other = slice(cols + a, cols + b)
-            if out is out_b:
-                o1, o2 = jnp.where(below, o1, weight[mine]), jnp.where(below, o2, weight[other])
+            useful = below if out is out_b else z < 3
+            o1, o2 = jnp.where(useful, o1, weight[mine]), jnp.where(useful, o2, weight[other])
             out[mine] = o1
             out[other] = o2
             e, o = lse_rows(l1, l2)
@@ -429,7 +429,7 @@
         block = w_halves[c].reshape(q[c].shape)
         going = [jnp.where(z == 1, block, q[c]), jnp.where(z == 3, q[c], block)]
         if c:
-            going = [after(a, b) for a, b in zip(going, qs[0])]
+            going = after(going, *qs[0])
         qs.append([seq_perm(going[0], (2, 1), (3, 2), (1, 3)), seq_perm(going[1], (3, 1), (1, 0), (2, 3))])
         if c == 0:
             kv_o = swap(after(kv_give, q[0]))
@@ -449,8 +449,8 @@
             functools.partial(upper_kernel, coef, cols), turn,
             [(a, 0) for a in qs[c]] + pair + [(a, 0) for a in low[c]] + [(out_weight, c * heads)], [partial] * 2, heads, "upper_rows", 7)
         sent.append(a)
-        oa.append(seq_perm(a, (1, 2), (2, 3)))
-        ob.append(seq_perm(b, (1, 3), (0, 1), (3, 2)))
+        oa.append(seq_perm(a, (1, 2), (2, 3), (3, 1)))
+        ob.append(seq_perm(b, (1, 3), (0, 1), (3, 2), (2, 0)))
         (mine,) = head_call(
             functools.partial(own_kernel, coef, cols), after(at, a), [(q[c], 0)] + pair + [(a, 0) for a in low[c]],
             [partial], heads, "own_rows", 6)
@@ -458,16 +458,16 @@
         turn = after(at, mine)
 
     depth = out_weight.shape[0]
-    w_near = [
-        jnp.where((z == 0) | (z == 3), qs[c][1].reshape(depth, width), ob[c][:depth]) for c in range(chunks)
-    ]
-    w_down = [seq_perm(after(w_halves[0], own[0], *qs[1]), (2, 0), (3, 1))]
-    w_down.append(seq_perm(after(w_halves[1], w_down[0], sent[1]), (2, 0), (3, 1)))
+
+    def block(array):
+        return array[:depth] if array.ndim == 2 else array.reshape(depth, width)
 
     def far_half(c, earlier):
-        up = jnp.where(z == 2, pieces(w_second, c), qs[c][0].reshape(depth, width))
-        half = jnp.where(z >= 2, up, after(w_down[c], earlier))
+        down = jnp.where(z == 0, block(ob[c]), after(block(oa[c]), earlier))
+        half = jnp.where(z >= 2, jnp.where(z == 2, pieces(w_second, c), block(qs[c][0])), down)
         return half, seq_perm(half, (0, 1), (1, 0), (2, 3), (3, 2))
+
+    w_near = [jnp.where((z == 0) | (z == 3), block(qs[c][1]), block(ob[c])) for c in range(chunks)]
 
     def merged(c, earlier):
         (a,) = head_call(
@@ -475,8 +475,8 @@
             [struct((2, cols, width), BF16)], heads, "merge", 2)
         return a, swap(a)
 
-    far_0 = far_half(0, own[1])
     first_half = merged(0, own[1])
+    far_0 = far_half(0, first_half[0])
     near, far = map(list, zip(first_half, merged(1, (first_half[1], far_0[1]))))
     w_far, w_other = map(list, zip(far_0, far_half(1, near[1])))
 
@@ -487,11 +487,11 @@
         w_far + w_other,
     ):
         send, kept = project(turn, near, far, weights, out_weight.shape[1])
-        turn = after(at, send)
         got = head_perm(send, 1)
         piece = struct(send.shape[:1] + send.shape[3:], BF16)
         stay, to_y, to_x, to_xy = whole_call(
             split_kernel, at, [kept, got], [piece] * 4, "split", 2)
+        turn = after(at, send)
         diagonal = [((2 * i + j) * 4 + h, (2 * i + 1 - j) * 4 + (h ^ 2)) for i in range(4) for j in range(2) for h in range(4)]
         from_xy = lax.ppermute(to_xy, ("seq", "head"), diagonal)
         parts += [stay, head_perm(to_y, 2), swap(to_x), from_xy]

time: 195 us -> 201 us (1.031)
  the two profiles are of different devices: /device:TPU:0 before, /device:TPU:16 now
where the time goes in v11:
time: 201 us; the launch traced here: 198 us
  waiting for transfers between devices  103 us (51%)
  starting transfers between devices  40.7 us (20%)
  Pallas kernels  39.2 us (20%)
  local copies, waits for them, and re-layouts  8.06 us (4%)
  other arithmetic  6.67 us (3%)
    ppermute x20, waiting for transfers between devices, seq_perm(): return lax.ppermute(array, 'seq', pairs)  85.2 us
    ppermute x20, starting transfers between devices, seq_perm(): return lax.ppermute(array, 'seq', pairs)  34 us
    pallas_call x6, Pallas kernels, head_call(): pl.pallas_call(kernel, out_shape=outs, grid_spec=pltpu.PrefetchScalarGrid...  30.1 us
    ppermute x2, waiting for transfers between devices, body_eight(): from_xy = lax.ppermute(to_xy, ('seq', 'head'), diagonal)  9.37 us
    pallas_call x5, Pallas kernels, whole_call(): pl.pallas_call(kernel, out_shape=outs, in_specs=[pl.BlockSpec(memory_spac...  9.08 us
    ppermute x4, waiting for transfers between devices, head_perm(): return lax.ppermute(array, 'head', [(i, i ^ flip) for i in range(4)])  8.9 us
    dynamic_slice x2, local copies, waits for them, and re-layouts, lanes(): lax.dynamic_slice(local, (lo, 0, half_of * half), (hi - lo, cols, half))  4.88 us
  transfers between devices with their start and end apart: 26, of which 13 were waited for; matrix products, arithmetic and copies ran while one was open for 6% of the time, Pallas kernels for 16%

profile of v11, /device:TPU:16, one launch (start us, length us, event | category | flops | bytes accessed | tf_op | source)
XLA Modules:
  0.0 198.4 jit_solution(17678681706689207379)
XLA Ops:
  0.0 2.2 %dynamic-slice_bitcast_fusion.3 = (bf16[1,512,512]{2,1,0:T(8,128)(2,1)S(1)}, bf16[1,512,512]{2,1,0:T(8,128)(2,1)}) fusion(bf16[3,1,512,1024]{3,2,1,0:T(8,128)(2,1)} %param.2, s32[]{:T(128)S(6)} %select_n.116, s32[]{:T(128)S(6)} %select_n.117), kind=kLoop, calls=%fused_computation.12 | loop fusion | bytes 2097160 | tf_op jit(solution)/shard_map/dynamic_slice | solution.py:416
  5.0 2.7 %dynamic-slice_bitcast_fusion = (bf16[2,512,512]{2,1,0:T(8,128)(2,1)}, bf16[2,512,512]{2,1,0:T(8,128)(2,1)S(1)}) fusion(bf16[3,1,512,1024]{3,2,1,0:T(8,128)(2,1)} %param.2, s32[]{:T(128)S(6)} %select_n.117, s32[]{:T(128)S(6)} %select_n.116), kind=kLoop, calls=%fused_computation.1 | loop fusion | bytes 4194312 | tf_op jit(solution)/shard_map/dynamic_slice | solution.py:416
  7.8 8.4 %collective-permute-done = bf16[1,512,512]{2,1,0:T(8,128)(2,1)} collective-permute-done((bf16[1,512,512]{2,1,0:T(8,128)(2,1)}, bf16[1,512,512]{2,1,0:T(8,128)(2,1)}, u32[]{:S(2)}, u32[]{:S(2)}) %collective-permute-start) | collective-permute-done | bytes 524320 | tf_op jit(solution)/shard_map/ppermute | solution.py:404
  16.1 1.8 broadcast_select_fusion.5
  20.5 1.9 slice.69
  22.4 2.3 %collective-permute-start.1 = (bf16[2,512,256]{2,1,0:T(8,128)(2,1)}, bf16[2,512,256]{2,1,0:T(8,128)(2,1)S(1)}, u32[]{:S(2)}, u32[]{:S(2)}) collective-permute-start(bf16[2,512,256]{2,1,0:T(8,128)(2,1)} %get-tuple-element.80), channel_id=1, source_target_pairs={{16,8},{20,12},{24,16},{28,20},{8,24},{12,28},{17,9},{21,13},{25,1... | collective-permute-start | bytes 1572872 | tf_op jit(solution)/shard_map/ppermute | solution.py:404
  24.8 3.5 %collective-permute-start.2 = (bf16[2,512,256]{2,1,0:T(8,128)(2,1)}, bf16[2,512,256]{2,1,0:T(8,128)(2,1)S(1)}, u32[]{:S(2)}, u32[]{:S(2)}) collective-permute-start(bf16[2,512,256]{2,1,0:T(8,128)(2,1)} %get-tuple-element.79), channel_id=1, source_target_pairs={{24,8},{28,12},{8,0},{12,4},{16,24},{20,28},{25,9},{29,13},{9,1},{... | collective-permute-start | bytes 1572872 | tf_op jit(solution)/shard_map/ppermute | solution.py:404
  28.4 3.1 %collective-permute-done.4 = bf16[1024,512]{1,0:T(8,128)(2,1)} collective-permute-done((bf16[1024,512]{1,0:T(8,128)(2,1)}, bf16[1024,512]{1,0:T(8,128)(2,1)}, u32[]{:S(2)}, u32[]{:S(2)}) %collective-permute-start.4) | collective-permute-done | bytes 1048608 | tf_op jit(solution)/shard_map/ppermute | solution.py:404
  34.0 5.4 %collective-permute-done.1.qa = bf16[2,512,256]{2,1,0:T(8,128)(2,1)S(1)} collective-permute-done((bf16[2,512,256]{2,1,0:T(8,128)(2,1)}, bf16[2,512,256]{2,1,0:T(8,128)(2,1)S(1)}, u32[]{:S(2)}, u32[]{:S(2)}) %collective-permute-start.1) | collective-permute-done | bytes 524320 | tf_op jit(solution)/shard_map/ppermute | solution.py:404
  39.4 10.1 %collective-permute-done.2.qb = bf16[2,512,256]{2,1,0:T(8,128)(2,1)S(1)} collective-permute-done((bf16[2,512,256]{2,1,0:T(8,128)(2,1)}, bf16[2,512,256]{2,1,0:T(8,128)(2,1)S(1)}, u32[]{:S(2)}, u32[]{:S(2)}) %collective-permute-start.2) | collective-permute-done | bytes 524320 | tf_op jit(solution)/shard_map/ppermute | solution.py:404
  49.4 2.2 %collective-permute-start.7 = (bf16[2,512,256]{2,1,0:T(8,128)(2,1)S(1)}, bf16[2,512,256]{2,1,0:T(8,128)(2,1)S(1)}, u32[]{:S(2)}, u32[]{:S(2)}) collective-permute-start(bf16[2,512,256]{2,1,0:T(8,128)(2,1)S(1)} %get-tuple-element.41), channel_id=1, source_target_pairs={{16,8},{20,12},{24,16},{28,20},{8,24},{12,28},{17,9},{21,13},{25,1... | collective-permute-start | bytes 1572872 | tf_op jit(solution)/shard_map/ppermute | solution.py:404
  51.6 4.0 %collective-permute-start.8 = (bf16[2,512,256]{2,1,0:T(8,128)(2,1)S(1)}, bf16[2,512,256]{2,1,0:T(8,128)(2,1)S(1)}, u32[]{:S(2)}, u32[]{:S(2)}) collective-permute-start(bf16[2,512,256]{2,1,0:T(8,128)(2,1)S(1)} %get-tuple-element.42), channel_id=1, source_target_pairs={{24,8},{28,12},{8,0},{12,4},{16,24},{20,28},{25,9},{29,13},{9,1},{... | collective-permute-start | bytes 1572872 | tf_op jit(solution)/shard_map/ppermute | solution.py:404
  57.6 6.7 %upper_rows.2 = (bf16[1072,256]{1,0:T(8,128)(2,1)S(1)}, bf16[1072,256]{1,0:T(8,128)(2,1)S(1)}) custom-call(s32[4]{0:T(128)S(1)} %pad_add_fusion.at, bf16[2,512,256]{2,1,0:T(8,128)(2,1)S(1)} %collective-permute-done.1.qa, bf16[2,512,256]{2,1,0:T(8,128)(2,1)S(1)} %collective-permute-done.2.qb, bf16[2,512,512]{2,1,0:T(8,128)(2,1)S(1)} %get-tuple-element.66.kv_m, ...), custom_call_target="tpu_custom_call" | custom-call | flops 7000000000 | bytes 1024 | tf_op jit(solution)/shard_map/upper_rows/pallas_call | solution.py:300
  64.3 4.8 %collective-permute-start.10 = (bf16[1072,256]{1,0:T(8,128)(2,1)S(1)}, bf16[1072,256]{1,0:T(8,128)(2,1)S(1)}, u32[]{:S(2)}, u32[]{:S(2)}) collective-permute-start(bf16[1072,256]{1,0:T(8,128)(2,1)S(1)} %get-tuple-element.38), channel_id=1, source_target_pairs={{8,16},{12,20},{16,24},{20,28},{24,8},{28,12},{9,17},{13,21},{17,2... | collective-permute-start | bytes 1646600 | tf_op jit(solution)/shard_map/ppermute | solution.py:404
  69.1 5.9 %own_rows.2.own = bf16[1072,256]{1,0:T(8,128)(2,1)S(1)} custom-call(s32[4]{0:T(128)S(1)} %pad_add_fusion.at, bf16[2,512,256]{2,1,0:T(8,128)(2,1)S(1)} %get-tuple-element.86.q, bf16[2,512,512]{2,1,0:T(8,128)(2,1)S(1)} %get-tuple-element.66.kv_m, bf16[2,512,512]{2,1,0:T(8,128)(2,1)} %collective-permute-done.3.kv_o, ...), custom_call_target="tpu_custom_call" | custom-call | flops 6000000000 | bytes 1024 | tf_op jit(solution)/shard_map/own_rows/pallas_call | solution.py:300
  75.2 23.0 %collective-permute-done.10.oa = bf16[1072,256]{1,0:T(8,128)(2,1)S(1)} collective-permute-done((bf16[1072,256]{1,0:T(8,128)(2,1)S(1)}, bf16[1072,256]{1,0:T(8,128)(2,1)S(1)}, u32[]{:S(2)}, u32[]{:S(2)}) %collective-permute-start.10) | collective-permute-done | bytes 548896 | tf_op jit(solution)/shard_map/ppermute | solution.py:404
  98.3 6.7 %upper_rows.3 = (bf16[1072,256]{1,0:T(8,128)(2,1)S(1)}, bf16[1072,256]{1,0:T(8,128)(2,1)S(1)}) custom-call(s32[4]{0:T(128)S(1)} %pad_add_fusion.at, bf16[2,512,256]{2,1,0:T(8,128)(2,1)S(1)} %collective-permute-done.7.qa, bf16[2,512,256]{2,1,0:T(8,128)(2,1)S(1)} %collective-permute-done.8.qb, bf16[2,512,512]{2,1,0:T(8,128)(2,1)S(1)} %get-tuple-element.66.kv_m, ...), custom_call_target="tpu_custom_call" | custom-call | flops 7000000000 | bytes 1024 | tf_op jit(solution)/shard_map/upper_rows/pallas_call | solution.py:300
  105.0 4.6 %collective-permute-start.14 = (bf16[1072,256]{1,0:T(8,128)(2,1)S(1)}, bf16[1072,256]{1,0:T(8,128)(2,1)S(1)}, u32[]{:S(2)}, u32[]{:S(2)}) collective-permute-start(bf16[1072,256]{1,0:T(8,128)(2,1)S(1)} %get-tuple-element.44), channel_id=1, source_target_pairs={{8,16},{12,20},{16,24},{20,28},{24,8},{28,12},{9,17},{13,21},{17,2... | collective-permute-start | bytes 1646600 | tf_op jit(solution)/shard_map/ppermute | solution.py:404
  109.6 6.0 %own_rows.3.own = bf16[1072,256]{1,0:T(8,128)(2,1)S(1)} custom-call(s32[4]{0:T(128)S(1)} %pad_add_fusion.at, bf16[2,512,256]{2,1,0:T(8,128)(2,1)S(1)} %get-tuple-element.85.q, bf16[2,512,512]{2,1,0:T(8,128)(2,1)S(1)} %get-tuple-element.66.kv_m, bf16[2,512,512]{2,1,0:T(8,128)(2,1)} %collective-permute-done.3.kv_o, ...), custom_call_target="tpu_custom_call" | custom-call | flops 6000000000 | bytes 1024 | tf_op jit(solution)/shard_map/own_rows/pallas_call | solution.py:300
  115.5 2.4 %merge.2 = bf16[2,512,256]{2,1,0:T(8,128)(2,1)S(1)} custom-call(s32[4]{0:T(128)S(1)} %pad_add_fusion.at, bf16[1072,256]{1,0:T(8,128)(2,1)S(1)} %own_rows.2.own, bf16[1072,256]{1,0:T(8,128)(2,1)S(1)} %collective-permute-done.10.oa, bf16[1072,256]{1,0:T(8,128)(2,1)S(1)} %collective-permute-done.11.ob), custom_call_target="tpu_custom_call" | custom-call | flops 2000000000 | bytes 1024 | tf_op jit(solution)/shard_map/merge/pallas_call | solution.py:300
  119.3 2.1 %collective-permute-start.13 = (bf16[1024,256]{1,0:T(8,128)(2,1)S(1)}, bf16[1024,256]{1,0:T(8,128)(2,1)S(1)}, u32[]{:S(2)}, u32[]{:S(2)}) collective-permute-start(bf16[1024,256]{1,0:T(8,128)(2,1)S(1)} %get-tuple-element.84.refs_4_), channel_id=1, source_target_pairs={{0,8},{4,12},{8,0},{12,4},{16,24},{20,28},{24,16},{28,20},{1,9},{5... | collective-permute-start | bytes 1572872 | tf_op jit(solution)/shard_map/ppermute | solution.py:404
  121.9 23.1 %collective-permute-done.13.refs_6_ = bf16[1024,256]{1,0:T(8,128)(2,1)S(1)} collective-permute-done((bf16[1024,256]{1,0:T(8,128)(2,1)S(1)}, bf16[1024,256]{1,0:T(8,128)(2,1)S(1)}, u32[]{:S(2)}, u32[]{:S(2)}) %collective-permute-start.13) | collective-permute-done | bytes 524320 | tf_op jit(solution)/shard_map/ppermute | solution.py:404
  145.0 2.4 %merge.3 = bf16[2,512,256]{2,1,0:T(8,128)(2,1)S(1)} custom-call(s32[4]{0:T(128)S(1)} %pad_add_fusion.at, bf16[1072,256]{1,0:T(8,128)(2,1)S(1)} %own_rows.3.own, bf16[1072,256]{1,0:T(8,128)(2,1)S(1)} %collective-permute-done.14.oa, bf16[1072,256]{1,0:T(8,128)(2,1)S(1)} %collective-permute-done.15.ob), custom_call_target="tpu_custom_call" | custom-call | flops 2000000000 | bytes 1024 | tf_op jit(solution)/shard_map/merge/pallas_call | solution.py:300
  151.1 9.7 %collective-permute-done.16 = bf16[2,512,256]{2,1,0:T(8,128)(2,1)S(1)} collective-permute-done((bf16[2,512,256]{2,1,0:T(8,128)(2,1)S(1)}, bf16[2,512,256]{2,1,0:T(8,128)(2,1)S(1)}, u32[]{:S(2)}, u32[]{:S(2)}) %collective-permute-start.16) | collective-permute-done | bytes 524320 | tf_op jit(solution)/shard_map/ppermute | solution.py:404
  160.8 2.9 %project.2 = (bf16[2,2,2,128,512]{4,3,2,1,0:T(8,128)(2,1)S(1)}, bf16[2,2,2,128,512]{4,3,2,1,0:T(8,128)(2,1)S(1)}) custom-call(s32[4]{0:T(128)S(1)} %pad_add_fusion.at, bf16[2,2,2,128,256]{4,3,2,1,0:T(8,128)(2,1)S(1)} %bitcast.27, bf16[2,2,2,128,256]{4,3,2,1,0:T(8,128)(2,1)S(1)} %bitcast.31, bf16[2,2,2,128,256]{4,3,2,1,0:T(8,128)(2,1)S(1)} %bitcast.29, ...), custom_call_target="tpu_custom_call" | custom-call | flops 4000000000 | bytes 1024 | tf_op jit(solution)/shard_map/project/pallas_call | solution.py:349
  163.7 2.9 %project.3 = (bf16[2,2,2,128,512]{4,3,2,1,0:T(8,128)(2,1)S(1)}, bf16[2,2,2,128,512]{4,3,2,1,0:T(8,128)(2,1)S(1)}) custom-call(s32[4]{0:T(128)S(1)} %pad_add_fusion.at, bf16[2,2,2,128,256]{4,3,2,1,0:T(8,128)(2,1)S(1)} %bitcast.28, bf16[2,2,2,128,256]{4,3,2,1,0:T(8,128)(2,1)S(1)} %bitcast.32, bf16[2,2,2,128,256]{4,3,2,1,0:T(8,128)(2,1)S(1)} %bitcast.30, ...), custom_call_target="tpu_custom_call" | custom-call | flops 4000000000 | bytes 1024 | tf_op jit(solution)/shard_map/project/pallas_call | solution.py:349
  167.2 2.1 %collective-permute-done.22.got = bf16[2,2,2,128,512]{4,3,2,1,0:T(8,128)(2,1)S(1)} collective-permute-done((bf16[2,2,2,128,512]{4,3,2,1,0:T(8,128)(2,1)S(1)}, bf16[2,2,2,128,512]{4,3,2,1,0:T(8,128)(2,1)S(1)}, u32[]{:S(2)}, u32[]{:S(2)}) %collective-permute-start.22) | collective-permute-done | bytes 1048608 | tf_op jit(solution)/shard_map/ppermute | solution.py:410
  176.6 3.5 %collective-permute-done.23.refs_5_ = bf16[2,128,512]{2,1,0:T(8,128)(2,1)S(1)} collective-permute-done((bf16[2,128,512]{2,1,0:T(8,128)(2,1)S(1)}, bf16[2,128,512]{2,1,0:T(8,128)(2,1)S(1)}, u32[]{:S(2)}, u32[]{:S(2)}) %collective-permute-start.23) | collective-permute-done | bytes 262176 | tf_op jit(solution)/shard_map/ppermute | solution.py:410
  181.6 4.9 %collective-permute-done.25.refs_7_ = bf16[2,128,512]{2,1,0:T(8,128)(2,1)S(1)} collective-permute-done((bf16[2,128,512]{2,1,0:T(8,128)(2,1)S(1)}, bf16[2,128,512]{2,1,0:T(8,128)(2,1)S(1)}, u32[]{:S(2)}, u32[]{:S(2)}) %collective-permute-start.25) | collective-permute-done | bytes 262176 | tf_op jit(solution)/shard_map/ppermute | solution.py:496
  186.5 3.3 %collective-permute-done.18.refs_1_ = bf16[2,128,512]{2,1,0:T(8,128)(2,1)S(1)} collective-permute-done((bf16[2,128,512]{2,1,0:T(8,128)(2,1)S(1)}, bf16[2,128,512]{2,1,0:T(8,128)(2,1)S(1)}, u32[]{:S(2)}, u32[]{:S(2)}) %collective-permute-start.18) | collective-permute-done | bytes 262176 | tf_op jit(solution)/shard_map/ppermute | solution.py:410
  189.8 2.4 %collective-permute-done.19.refs_2_ = bf16[2,128,512]{2,1,0:T(8,128)(2,1)S(1)} collective-permute-done((bf16[2,128,512]{2,1,0:T(8,128)(2,1)S(1)}, bf16[2,128,512]{2,1,0:T(8,128)(2,1)S(1)}, u32[]{:S(2)}, u32[]{:S(2)}) %collective-permute-start.19) | collective-permute-done | bytes 262176 | tf_op jit(solution)/shard_map/ppermute | solution.py:404
  192.2 4.4 %collective-permute-done.20.refs_3_ = bf16[2,128,512]{2,1,0:T(8,128)(2,1)S(1)} collective-permute-done((bf16[2,128,512]{2,1,0:T(8,128)(2,1)S(1)}, bf16[2,128,512]{2,1,0:T(8,128)(2,1)S(1)}, u32[]{:S(2)}, u32[]{:S(2)}) %collective-permute-start.20) | collective-permute-done | bytes 262176 | tf_op jit(solution)/shard_map/ppermute | solution.py:496
  (48 shorter events, 26.7 us)
Async XLA Ops:
  0.0 7.7 %copy-start = (bf16[1024,512]{1,0:T(8,128)(2,1)S(1)}, bf16[1024,512]{1,0:T(8,128)(2,1)}, u32[]{:S(2)}) copy-start(bf16[1024,512]{1,0:T(8,128)(2,1)} %refs_4_.1) | copy-start | bytes 3145732
  2.2 14.0 %collective-permute-start = (bf16[1,512,512]{2,1,0:T(8,128)(2,1)}, bf16[1,512,512]{2,1,0:T(8,128)(2,1)}, u32[]{:S(2)}, u32[]{:S(2)}) collective-permute-start(bf16[1,512,512]{2,1,0:T(8,128)(2,1)} %get-tuple-element.68), channel_id=1, source_target_pairs={{0,4},{4,0},{8,12},{12,8},{16,20},{20,16},{24,28},{28,24},{1,5},{5... | collective-permute-start | bytes 1572872 | tf_op jit(solution)/shard_map/ppermute | solution.py:404
  3.7 27.8 %collective-permute-start.4 = (bf16[1024,512]{1,0:T(8,128)(2,1)}, bf16[1024,512]{1,0:T(8,128)(2,1)}, u32[]{:S(2)}, u32[]{:S(2)}) collective-permute-start(bf16[1024,512]{1,0:T(8,128)(2,1)} %refs_4_.1), channel_id=1, source_target_pairs={{0,16},{4,20},{1,17},{5,21},{2,18},{6,22},{3,19},{7,23}} | collective-permute-start | bytes 3145736 | tf_op jit(solution)/shard_map/ppermute | solution.py:404
  19.0 36.7 %collective-permute-start.3 = (bf16[2,512,512]{2,1,0:T(8,128)(2,1)}, bf16[2,512,512]{2,1,0:T(8,128)(2,1)}, u32[]{:S(2)}, u32[]{:S(2)}) collective-permute-start(bf16[2,512,512]{2,1,0:T(8,128)(2,1)} %get-tuple-element.35), channel_id=1, source_target_pairs={{0,4},{4,0},{8,12},{12,8},{16,20},{20,16},{24,28},{28,24},{1,5},{5... | collective-permute-start | bytes 3145736 | tf_op jit(solution)/shard_map/ppermute | solution.py:404
  22.4 17.0 %collective-permute-start.1 = (bf16[2,512,256]{2,1,0:T(8,128)(2,1)}, bf16[2,512,256]{2,1,0:T(8,128)(2,1)S(1)}, u32[]{:S(2)}, u32[]{:S(2)}) collective-permute-start(bf16[2,512,256]{2,1,0:T(8,128)(2,1)} %get-tuple-element.80), channel_id=1, source_target_pairs={{16,8},{20,12},{24,16},{28,20},{8,24},{12,28},{17,9},{21,13},{25,1... | collective-permute-start | bytes 1572872 | tf_op jit(solution)/shard_map/ppermute | solution.py:404
  24.8 24.7 %collective-permute-start.2 = (bf16[2,512,256]{2,1,0:T(8,128)(2,1)}, bf16[2,512,256]{2,1,0:T(8,128)(2,1)S(1)}, u32[]{:S(2)}, u32[]{:S(2)}) collective-permute-start(bf16[2,512,256]{2,1,0:T(8,128)(2,1)} %get-tuple-element.79), channel_id=1, source_target_pairs={{24,8},{28,12},{8,0},{12,4},{16,24},{20,28},{25,9},{29,13},{9,1},{... | collective-permute-start | bytes 1572872 | tf_op jit(solution)/shard_map/ppermute | solution.py:404
  31.5 25.4 %collective-permute-start.5 = (bf16[2,512,256]{2,1,0:T(8,128)(2,1)S(1)}, bf16[2,512,256]{2,1,0:T(8,128)(2,1)S(1)}, u32[]{:S(2)}, u32[]{:S(2)}) collective-permute-start(bf16[2,512,256]{2,1,0:T(8,128)(2,1)S(1)} %get-tuple-element.36), channel_id=1, source_target_pairs={{0,8},{4,12},{1,9},{5,13},{2,10},{6,14},{3,11},{7,15}} | collective-permute-start | bytes 1572872 | tf_op jit(solution)/shard_map/ppermute | solution.py:404
  32.2 24.7 %collective-permute-start.6 = (bf16[2,512,256]{2,1,0:T(8,128)(2,1)}, bf16[2,512,256]{2,1,0:T(8,128)(2,1)S(1)}, u32[]{:S(2)}, u32[]{:S(2)}) collective-permute-start(bf16[2,512,256]{2,1,0:T(8,128)(2,1)} %slice.69), channel_id=1, source_target_pairs={{0,12},{4,8},{1,13},{5,9},{2,14},{6,10},{3,15},{7,11}} | collective-permute-start | bytes 1572872 | tf_op jit(solution)/shard_map/ppermute | solution.py:404
  49.4 48.8 %collective-permute-start.7 = (bf16[2,512,256]{2,1,0:T(8,128)(2,1)S(1)}, bf16[2,512,256]{2,1,0:T(8,128)(2,1)S(1)}, u32[]{:S(2)}, u32[]{:S(2)}) collective-permute-start(bf16[2,512,256]{2,1,0:T(8,128)(2,1)S(1)} %get-tuple-element.41), channel_id=1, source_target_pairs={{16,8},{20,12},{24,16},{28,20},{8,24},{12,28},{17,9},{21,13},{25,1... | collective-permute-start | bytes 1572872 | tf_op jit(solution)/shard_map/ppermute | solution.py:404
  51.6 46.6 %collective-permute-start.8 = (bf16[2,512,256]{2,1,0:T(8,128)(2,1)S(1)}, bf16[2,512,256]{2,1,0:T(8,128)(2,1)S(1)}, u32[]{:S(2)}, u32[]{:S(2)}) collective-permute-start(bf16[2,512,256]{2,1,0:T(8,128)(2,1)S(1)} %get-tuple-element.42), channel_id=1, source_target_pairs={{24,8},{28,12},{8,0},{12,4},{16,24},{20,28},{25,9},{29,13},{9,1},{... | collective-permute-start | bytes 1572872 | tf_op jit(solution)/shard_map/ppermute | solution.py:404
  56.9 41.4 %collective-permute-start.9 = (bf16[4,512,256]{2,1,0:T(8,128)(2,1)S(1)}, bf16[4,512,256]{2,1,0:T(8,128)(2,1)S(1)}, u32[]{:S(2)}, u32[]{:S(2)}) collective-permute-start(bf16[4,512,256]{2,1,0:T(8,128)(2,1)S(1)} %pad_maximum_fusion), channel_id=1, source_target_pairs={{0,8},{4,12},{1,9},{5,13},{2,10},{6,14},{3,11},{7,15}} | collective-permute-start | bytes 3145736 | tf_op jit(solution)/shard_map/ppermute | solution.py:404
  64.3 33.9 %collective-permute-start.10 = (bf16[1072,256]{1,0:T(8,128)(2,1)S(1)}, bf16[1072,256]{1,0:T(8,128)(2,1)S(1)}, u32[]{:S(2)}, u32[]{:S(2)}) collective-permute-start(bf16[1072,256]{1,0:T(8,128)(2,1)S(1)} %get-tuple-element.38), channel_id=1, source_target_pairs={{8,16},{12,20},{16,24},{20,28},{24,8},{28,12},{9,17},{13,21},{17,2... | collective-permute-start | bytes 1646600 | tf_op jit(solution)/shard_map/ppermute | solution.py:404
  75.1 40.5 %collective-permute-start.11 = (bf16[1072,256]{1,0:T(8,128)(2,1)S(1)}, bf16[1072,256]{1,0:T(8,128)(2,1)S(1)}, u32[]{:S(2)}, u32[]{:S(2)}) collective-permute-start(bf16[1072,256]{1,0:T(8,128)(2,1)S(1)} %get-tuple-element.47), channel_id=1, source_target_pairs={{8,24},{12,28},{0,8},{4,12},{24,16},{28,20},{16,0},{20,4},{9,25},{... | collective-permute-start | bytes 1646600 | tf_op jit(solution)/shard_map/ppermute | solution.py:404
  105.0 40.1 %collective-permute-start.14 = (bf16[1072,256]{1,0:T(8,128)(2,1)S(1)}, bf16[1072,256]{1,0:T(8,128)(2,1)S(1)}, u32[]{:S(2)}, u32[]{:S(2)}) collective-permute-start(bf16[1072,256]{1,0:T(8,128)(2,1)S(1)} %get-tuple-element.44), channel_id=1, source_target_pairs={{8,16},{12,20},{16,24},{20,28},{24,8},{28,12},{9,17},{13,21},{17,2... | collective-permute-start | bytes 1646600 | tf_op jit(solution)/shard_map/ppermute | solution.py:404
  118.0 27.1 %collective-permute-start.15 = (bf16[1072,256]{1,0:T(8,128)(2,1)S(1)}, bf16[1072,256]{1,0:T(8,128)(2,1)S(1)}, u32[]{:S(2)}, u32[]{:S(2)}) collective-permute-start(bf16[1072,256]{1,0:T(8,128)(2,1)S(1)} %get-tuple-element.50), channel_id=1, source_target_pairs={{8,24},{12,28},{0,8},{4,12},{24,16},{28,20},{16,0},{20,4},{9,25},{... | collective-permute-start | bytes 1646600 | tf_op jit(solution)/shard_map/ppermute | solution.py:404
  119.3 25.7 %collective-permute-start.13 = (bf16[1024,256]{1,0:T(8,128)(2,1)S(1)}, bf16[1024,256]{1,0:T(8,128)(2,1)S(1)}, u32[]{:S(2)}, u32[]{:S(2)}) collective-permute-start(bf16[1024,256]{1,0:T(8,128)(2,1)S(1)} %get-tuple-element.84.refs_4_), channel_id=1, source_target_pairs={{0,8},{4,12},{8,0},{12,4},{16,24},{20,28},{24,16},{28,20},{1,9},{5... | collective-permute-start | bytes 1572872 | tf_op jit(solution)/shard_map/ppermute | solution.py:404
  121.4 23.7 %collective-permute-start.12 = (bf16[2,512,256]{2,1,0:T(8,128)(2,1)S(1)}, bf16[2,512,256]{2,1,0:T(8,128)(2,1)S(1)}, u32[]{:S(2)}, u32[]{:S(2)}) collective-permute-start(bf16[2,512,256]{2,1,0:T(8,128)(2,1)S(1)} %merge.2), channel_id=1, source_target_pairs={{0,4},{4,0},{8,12},{12,8},{16,20},{20,16},{24,28},{28,24},{1,5},{5... | collective-permute-start | bytes 1572872 | tf_op jit(solution)/shard_map/ppermute | solution.py:404
  147.5 13.4 %collective-permute-start.16 = (bf16[2,512,256]{2,1,0:T(8,128)(2,1)S(1)}, bf16[2,512,256]{2,1,0:T(8,128)(2,1)S(1)}, u32[]{:S(2)}, u32[]{:S(2)}) collective-permute-start(bf16[2,512,256]{2,1,0:T(8,128)(2,1)S(1)} %merge.3), channel_id=1, source_target_pairs={{0,4},{4,0},{8,12},{12,8},{16,20},{20,16},{24,28},{28,24},{1,5},{5... | collective-permute-start | bytes 1572872 | tf_op jit(solution)/shard_map/ppermute | solution.py:404
  149.4 14.4 %collective-permute-start.21 = (bf16[1024,256]{1,0:T(8,128)(2,1)S(1)}, bf16[1024,256]{1,0:T(8,128)(2,1)S(1)}, u32[]{:S(2)}, u32[]{:S(2)}) collective-permute-start(bf16[1024,256]{1,0:T(8,128)(2,1)S(1)} %get-tuple-element.81.refs_5_), channel_id=1, source_target_pairs={{0,8},{4,12},{8,0},{12,4},{16,24},{20,28},{24,16},{28,20},{1,9},{5... | collective-permute-start | bytes 1572872 | tf_op jit(solution)/shard_map/ppermute | solution.py:404
  166.6 2.7 %collective-permute-start.22 = (bf16[2,2,2,128,512]{4,3,2,1,0:T(8,128)(2,1)S(1)}, bf16[2,2,2,128,512]{4,3,2,1,0:T(8,128)(2,1)S(1)}, u32[]{:S(2)}, u32[]{:S(2)}) collective-permute-start(bf16[2,2,2,128,512]{4,3,2,1,0:T(8,128)(2,1)S(1)} %get-tuple-element.60), channel_id=1, source_target_pairs={{0,1},{1,0},{2,3},{3,2},{4,5},{5,4},{6,7},{7,6},{8,9},{9,8},{10,11... | collective-permute-start | bytes 3145736 | tf_op jit(solution)/shard_map/ppermute | solution.py:410
  166.7 7.0 %collective-permute-start.17 = (bf16[2,2,2,128,512]{4,3,2,1,0:T(8,128)(2,1)S(1)}, bf16[2,2,2,128,512]{4,3,2,1,0:T(8,128)(2,1)S(1)}, u32[]{:S(2)}, u32[]{:S(2)}) collective-permute-start(bf16[2,2,2,128,512]{4,3,2,1,0:T(8,128)(2,1)S(1)} %get-tuple-element.52), channel_id=1, source_target_pairs={{0,1},{1,0},{2,3},{3,2},{4,5},{5,4},{6,7},{7,6},{8,9},{9,8},{10,11... | collective-permute-start | bytes 3145736 | tf_op jit(solution)/shard_map/ppermute | solution.py:410
  170.1 10.0 %collective-permute-start.23 = (bf16[2,128,512]{2,1,0:T(8,128)(2,1)S(1)}, bf16[2,128,512]{2,1,0:T(8,128)(2,1)S(1)}, u32[]{:S(2)}, u32[]{:S(2)}) collective-permute-start(bf16[2,128,512]{2,1,0:T(8,128)(2,1)S(1)} %get-tuple-element.62), channel_id=1, source_target_pairs={{0,2},{1,3},{2,0},{3,1},{4,6},{5,7},{6,4},{7,5},{8,10},{9,11},{10,... | collective-permute-start | bytes 786440 | tf_op jit(solution)/shard_map/ppermute | solution.py:410
  171.7 9.9 %collective-permute-start.24 = (bf16[2,128,512]{2,1,0:T(8,128)(2,1)S(1)}, bf16[2,128,512]{2,1,0:T(8,128)(2,1)S(1)}, u32[]{:S(2)}, u32[]{:S(2)}) collective-permute-start(bf16[2,128,512]{2,1,0:T(8,128)(2,1)S(1)} %get-tuple-element.63), channel_id=1, source_target_pairs={{0,4},{4,0},{8,12},{12,8},{16,20},{20,16},{24,28},{28,24},{1,5},{5... | collective-permute-start | bytes 786440 | tf_op jit(solution)/shard_map/ppermute | solution.py:404
  172.3 14.3 %collective-permute-start.25 = (bf16[2,128,512]{2,1,0:T(8,128)(2,1)S(1)}, bf16[2,128,512]{2,1,0:T(8,128)(2,1)S(1)}, u32[]{:S(2)}, u32[]{:S(2)}) collective-permute-start(bf16[2,128,512]{2,1,0:T(8,128)(2,1)S(1)} %get-tuple-element.64), channel_id=1, source_target_pairs={{0,6},{1,7},{2,4},{3,5},{4,2},{5,3},{6,0},{7,1},{8,14},{9,15},{10,... | collective-permute-start | bytes 786440 | tf_op jit(solution)/shard_map/ppermute | solution.py:496
  174.5 15.3 %collective-permute-start.18 = (bf16[2,128,512]{2,1,0:T(8,128)(2,1)S(1)}, bf16[2,128,512]{2,1,0:T(8,128)(2,1)S(1)}, u32[]{:S(2)}, u32[]{:S(2)}) collective-permute-start(bf16[2,128,512]{2,1,0:T(8,128)(2,1)S(1)} %get-tuple-element.54), channel_id=1, source_target_pairs={{0,2},{1,3},{2,0},{3,1},{4,6},{5,7},{6,4},{7,5},{8,10},{9,11},{10,... | collective-permute-start | bytes 786440 | tf_op jit(solution)/shard_map/ppermute | solution.py:410
  176.1 16.1 %collective-permute-start.19 = (bf16[2,128,512]{2,1,0:T(8,128)(2,1)S(1)}, bf16[2,128,512]{2,1,0:T(8,128)(2,1)S(1)}, u32[]{:S(2)}, u32[]{:S(2)}) collective-permute-start(bf16[2,128,512]{2,1,0:T(8,128)(2,1)S(1)} %get-tuple-element.55), channel_id=1, source_target_pairs={{0,4},{4,0},{8,12},{12,8},{16,20},{20,16},{24,28},{28,24},{1,5},{5... | collective-permute-start | bytes 786440 | tf_op jit(solution)/shard_map/ppermute | solution.py:404
  180.1 16.5 %collective-permute-start.20 = (bf16[2,128,512]{2,1,0:T(8,128)(2,1)S(1)}, bf16[2,128,512]{2,1,0:T(8,128)(2,1)S(1)}, u32[]{:S(2)}, u32[]{:S(2)}) collective-permute-start(bf16[2,128,512]{2,1,0:T(8,128)(2,1)S(1)} %get-tuple-element.56), channel_id=1, source_target_pairs={{0,6},{1,7},{2,4},{3,5},{4,2},{5,3},{6,0},{7,1},{8,14},{9,15},{10,... | collective-permute-start | bytes 786440 | tf_op jit(solution)/shard_map/ppermute | solution.py:496

commit v12 on v9

--- a/solution.py
+++ b/solution.py
@@ -436,8 +436,9 @@
             seq_perm(going[1], (3, 1), (1, 0), (2, 3), *([(0, 2)] if c == 0 else [])),
         ])
         if c == 0:
-            kv_o = swap(after(kv_give, q[0], w_first))
-            low.append([seq_perm(pieces(kv_m, c), (0, 1)), seq_perm(pieces(kv_give, c), (0, 1), cross=True)])
+            kv_o = swap(after(kv_give, q[0]))
+            low_m = seq_perm(after(pieces(kv_m, c), w_first), (0, 1))
+            low.append([low_m, seq_perm(after(pieces(kv_give, c), low_m), (0, 1), cross=True)])
         else:
             up = jnp.concatenate([pieces(kv_m, c), pieces(kv_o, c)])
             low.append([seq_perm(after(up, *low[0]), (0, 1))])
@@ -465,12 +466,8 @@
     def block(array):
         return array.reshape(depth, width)
 
-    def pair_swap(half):
-        return seq_perm(half, (0, 1), (1, 0), (2, 3), (3, 2))
-
     w_near = [jnp.where((z == 0) | (z == 3), block(qs[c][1]), ob[c][:depth]) for c in range(chunks)]
-    w_last = seq_perm(after(w_halves[1], own[0], *qs[1]), (2, 0), (3, 1))
-    w_other = [pair_swap(after(w_first, oa[0], ob[0]))]
+    w_down = seq_perm(after(w_halves[1], own[0], *qs[1]), (2, 0), (3, 1))
 
     def merged(c, earlier):
         (a,) = head_call(
@@ -478,22 +475,24 @@
             [struct((2, cols, width), BF16)], heads, "merge", 2)
         return a, swap(a)
 
-    first_half = merged(0, (own[1], w_last))
-    up_last = jnp.where(z == 2, block(qs[0][1]), block(qs[0][0]))
-    w_far = [w_first, jnp.where(z >= 2, up_last, after(w_last, own[1]))]
-    w_other.append(pair_swap(w_far[1]))
-    near, far = map(list, zip(first_half, merged(1, (first_half[1], w_other))))
+    first_half = merged(0, own[1])
+    up = jnp.where(z == 2, block(qs[0][1]), block(qs[0][0]))
+    w_far = [w_first, jnp.where(z >= 2, up, after(w_down, first_half[0], own[1]))]
+    near, far = map(list, zip(first_half, merged(1, (w_far, first_half[1]))))
+    w_other = seq_perm(jnp.concatenate(w_far, axis=1), (0, 1), (1, 0), (2, 3), (3, 2))
 
     parts = []
+    turn = after(at, w_other)
     for weights in (
         [out_weight] + w_near,
-        w_far + w_other,
+        w_far + [w_other],
     ):
-        send, kept = project(at, near, far, weights, out_weight.shape[1])
+        send, kept = project(turn, near, far, weights, out_weight.shape[1])
         got = head_perm(send, 1)
         piece = struct(send.shape[:1] + send.shape[3:], BF16)
         stay, to_y, to_x, to_xy = whole_call(
             split_kernel, at, [kept, got], [piece] * 4, "split", 2)
+        turn = after(at, send)
         diagonal = [((2 * i + j) * 4 + h, (2 * i + 1 - j) * 4 + (h ^ 2)) for i in range(4) for j in range(2) for h in range(4)]
         from_xy = lax.ppermute(to_xy, ("seq", "head"), diagonal)
         parts += [stay, head_perm(to_y, 2), swap(to_x), from_xy]

time: 203 us -> 189 us (0.931)
  waiting for transfers between devices: 95.4 us -> 84.4 us
    ppermute x21 -> x20, waiting for transfers between devices: 81.9 us -> 68.1 us  [seq_perm(): return lax.ppermute(array, 'seq', pairs)]
    ppermute x4, waiting for transfers between devices: 5.74 us -> 7.94 us  [head_perm(): return lax.ppermute(array, 'head', [(i, i ^ flip) for i in range(4)])]
    ppermute x21 -> x20, starting transfers between devices: 43.7 us -> 42.5 us  [seq_perm(): return lax.ppermute(array, 'seq', pairs)]
  transfers between devices with their start and end apart: 27 -> 26, of which waited for: 13 -> 14; matrix products, arithmetic and copies ran while one was open for 6% -> 6% of each run, Pallas kernels for 16% -> 17%
where the time goes in v12:
time: 189 us; the launch traced here: 188 us
  waiting for transfers between devices  84.4 us (45%)
  starting transfers between devices  49.2 us (26%)
  Pallas kernels  39.3 us (21%)
  local copies, waits for them, and re-layouts  10.8 us (6%)
  other arithmetic  4.34 us (2%)
    ppermute x20, waiting for transfers between devices, seq_perm(): return lax.ppermute(array, 'seq', pairs)  68.1 us
    ppermute x20, starting transfers between devices, seq_perm(): return lax.ppermute(array, 'seq', pairs)  42.5 us
    pallas_call x6, Pallas kernels, head_call(): pl.pallas_call(kernel, out_shape=outs, grid_spec=pltpu.PrefetchScalarGrid...  30.2 us
    pallas_call x5, Pallas kernels, whole_call(): pl.pallas_call(kernel, out_shape=outs, in_specs=[pl.BlockSpec(memory_spac...  9.08 us
    ppermute x2, waiting for transfers between devices, body_eight(): from_xy = lax.ppermute(to_xy, ('seq', 'head'), diagonal)  8.42 us
    ppermute x4, waiting for transfers between devices, head_perm(): return lax.ppermute(array, 'head', [(i, i ^ flip) for i in range(4)])  7.94 us
    slice x4, local copies, waits for them, and re-layouts, pieces(): return array[..., c * width:(c + 1) * width]  5.11 us
    dynamic_slice x2, local copies, waits for them, and re-layouts, lanes(): lax.dynamic_slice(local, (lo, 0, half_of * half), (hi - lo, cols, half))  4.77 us
  transfers between devices with their start and end apart: 26, of which 14 were waited for; matrix products, arithmetic and copies ran while one was open for 6% of the time, Pallas kernels for 17%

profile of v12, /device:TPU:16, one launch (start us, length us, event | category | flops | bytes accessed | tf_op | source)
XLA Modules:
  0.0 188.4 jit_solution(8756600603149887890)
XLA Ops:
  0.0 2.1 %dynamic-slice_bitcast_fusion.3 = (bf16[1,512,512]{2,1,0:T(8,128)(2,1)S(1)}, bf16[1,512,512]{2,1,0:T(8,128)(2,1)}) fusion(bf16[3,1,512,1024]{3,2,1,0:T(8,128)(2,1)} %param.2, s32[]{:T(128)S(6)} %select_n.102, s32[]{:T(128)S(6)} %select_n.103), kind=kLoop, calls=%fused_computation.12 | loop fusion | bytes 2097160 | tf_op jit(solution)/shard_map/dynamic_slice | solution.py:416
  5.2 2.7 %dynamic-slice_bitcast_fusion = (bf16[2,512,512]{2,1,0:T(8,128)(2,1)}, bf16[2,512,512]{2,1,0:T(8,128)(2,1)S(1)}) fusion(bf16[3,1,512,1024]{3,2,1,0:T(8,128)(2,1)} %param.2, s32[]{:T(128)S(6)} %select_n.103, s32[]{:T(128)S(6)} %select_n.102), kind=kLoop, calls=%fused_computation.2 | loop fusion | bytes 4194312 | tf_op jit(solution)/shard_map/dynamic_slice | solution.py:416
  7.9 8.1 %collective-permute-done.1 = bf16[1,512,512]{2,1,0:T(8,128)(2,1)} collective-permute-done((bf16[1,512,512]{2,1,0:T(8,128)(2,1)}, bf16[1,512,512]{2,1,0:T(8,128)(2,1)}, u32[]{:S(2)}, u32[]{:S(2)}) %collective-permute-start.1) | collective-permute-done | bytes 524320 | tf_op jit(solution)/shard_map/ppermute | solution.py:404
  21.2 6.2 %collective-permute-done.refs_4_ = bf16[1024,256]{1,0:T(8,128)(2,1)S(1)} collective-permute-done((bf16[1024,256]{1,0:T(8,128)(2,1)S(1)}, bf16[1024,256]{1,0:T(8,128)(2,1)S(1)}, u32[]{:S(2)}, u32[]{:S(2)}) %collective-permute-start) | collective-permute-done | bytes 524320 | tf_op jit(solution)/shard_map/ppermute | solution.py:404
  28.2 5.0 %collective-permute-start.3 = (bf16[2,512,256]{2,1,0:T(8,128)(2,1)}, bf16[2,512,256]{2,1,0:T(8,128)(2,1)S(1)}, u32[]{:S(2)}, u32[]{:S(2)}) collective-permute-start(bf16[2,512,256]{2,1,0:T(8,128)(2,1)} %get-tuple-element.85), channel_id=1, source_target_pairs={{16,8},{20,12},{24,16},{28,20},{8,24},{12,28},{17,9},{21,13},{25,1... | collective-permute-start | bytes 1572872 | tf_op jit(solution)/shard_map/ppermute | solution.py:404
  38.9 8.6 %collective-permute-done.3.qa = bf16[2,512,256]{2,1,0:T(8,128)(2,1)S(1)} collective-permute-done((bf16[2,512,256]{2,1,0:T(8,128)(2,1)}, bf16[2,512,256]{2,1,0:T(8,128)(2,1)S(1)}, u32[]{:S(2)}, u32[]{:S(2)}) %collective-permute-start.3) | collective-permute-done | bytes 524320 | tf_op jit(solution)/shard_map/ppermute | solution.py:404
  47.5 9.8 %collective-permute-done.2.qb = bf16[2,512,256]{2,1,0:T(8,128)(2,1)S(1)} collective-permute-done((bf16[2,512,256]{2,1,0:T(8,128)(2,1)}, bf16[2,512,256]{2,1,0:T(8,128)(2,1)S(1)}, u32[]{:S(2)}, u32[]{:S(2)}) %collective-permute-start.2) | collective-permute-done | bytes 524320 | tf_op jit(solution)/shard_map/ppermute | solution.py:404
  57.4 4.1 %collective-permute-start.7 = (bf16[2,512,256]{2,1,0:T(8,128)(2,1)}, bf16[2,512,256]{2,1,0:T(8,128)(2,1)S(1)}, u32[]{:S(2)}, u32[]{:S(2)}) collective-permute-start(bf16[2,512,256]{2,1,0:T(8,128)(2,1)} %get-tuple-element.41.q), channel_id=1, source_target_pairs={{16,8},{20,12},{24,16},{28,20},{17,9},{21,13},{25,17},{29,21},{18,... | collective-permute-start | bytes 1572872 | tf_op jit(solution)/shard_map/ppermute | solution.py:404
  61.5 2.6 %collective-permute-start.8 = (bf16[2,512,256]{2,1,0:T(8,128)(2,1)}, bf16[2,512,256]{2,1,0:T(8,128)(2,1)S(1)}, u32[]{:S(2)}, u32[]{:S(2)}) collective-permute-start(bf16[2,512,256]{2,1,0:T(8,128)(2,1)} %get-tuple-element.42), channel_id=1, source_target_pairs={{24,8},{28,12},{8,0},{12,4},{16,24},{20,28},{25,9},{29,13},{9,1},{... | collective-permute-start | bytes 1572872 | tf_op jit(solution)/shard_map/ppermute | solution.py:404
  67.2 6.7 %upper_rows.2 = (bf16[1072,256]{1,0:T(8,128)(2,1)S(1)}, bf16[1072,256]{1,0:T(8,128)(2,1)S(1)}) custom-call(s32[4]{0:T(128)S(1)} %pad_add_fusion.at, bf16[2,512,256]{2,1,0:T(8,128)(2,1)S(1)} %collective-permute-done.3.qa, bf16[2,512,256]{2,1,0:T(8,128)(2,1)S(1)} %collective-permute-done.2.qb, bf16[2,512,512]{2,1,0:T(8,128)(2,1)S(1)} %get-tuple-element.68.kv_m, ...), custom_call_target="tpu_custom_call" | custom-call | flops 7000000000 | bytes 1024 | tf_op jit(solution)/shard_map/upper_rows/pallas_call | solution.py:300
  74.0 2.2 %collective-permute-start.11 = (bf16[1072,256]{1,0:T(8,128)(2,1)S(1)}, bf16[1072,256]{1,0:T(8,128)(2,1)S(1)}, u32[]{:S(2)}, u32[]{:S(2)}) collective-permute-start(bf16[1072,256]{1,0:T(8,128)(2,1)S(1)} %get-tuple-element.39), channel_id=1, source_target_pairs={{8,16},{12,20},{16,24},{20,28},{9,17},{13,21},{17,25},{21,29},{10,... | collective-permute-start | bytes 1646600 | tf_op jit(solution)/shard_map/ppermute | solution.py:404
  76.2 6.0 %own_rows.2.own = bf16[1072,256]{1,0:T(8,128)(2,1)S(1)} custom-call(s32[4]{0:T(128)S(1)} %pad_add_fusion.at, bf16[2,512,256]{2,1,0:T(8,128)(2,1)S(1)} %copy-done.4, bf16[2,512,512]{2,1,0:T(8,128)(2,1)S(1)} %get-tuple-element.68.kv_m, bf16[2,512,512]{2,1,0:T(8,128)(2,1)} %collective-permute-done.4.kv_o, bf16[2,512,256]{2,1,0:T(8,128)(2,1)S(1)} %copy-done.6, ...), custom_call_target="tpu_custom_call" | custom-call | flops 6000000000 | bytes 1024 | tf_op jit(solution)/shard_map/own_rows/pallas_call | solution.py:300
  82.3 5.1 %collective-permute-start.9 = (bf16[1024,256]{1,0:T(8,128)(2,1)S(1)}, bf16[1024,256]{1,0:T(8,128)(2,1)S(1)}, u32[]{:S(2)}, u32[]{:S(2)}) collective-permute-start(bf16[1024,256]{1,0:T(8,128)(2,1)S(1)} %copy-done.8), channel_id=1, source_target_pairs={{16,0},{20,4},{24,8},{28,12},{17,1},{21,5},{25,9},{29,13},{18,2},{... | collective-permute-start | bytes 1572872 | tf_op jit(solution)/shard_map/ppermute | solution.py:404
  88.8 6.7 %upper_rows.3 = (bf16[1072,256]{1,0:T(8,128)(2,1)S(1)}, bf16[1072,256]{1,0:T(8,128)(2,1)S(1)}) custom-call(s32[4]{0:T(128)S(1)} %pad_add_fusion.at, bf16[2,512,256]{2,1,0:T(8,128)(2,1)S(1)} %collective-permute-done.7.qa, bf16[2,512,256]{2,1,0:T(8,128)(2,1)S(1)} %collective-permute-done.8.qb, bf16[2,512,512]{2,1,0:T(8,128)(2,1)S(1)} %get-tuple-element.68.kv_m, ...), custom_call_target="tpu_custom_call" | custom-call | flops 7000000000 | bytes 1024 | tf_op jit(solution)/shard_map/upper_rows/pallas_call | solution.py:300
  95.5 5.1 %collective-permute-start.15 = (bf16[1072,256]{1,0:T(8,128)(2,1)S(1)}, bf16[1072,256]{1,0:T(8,128)(2,1)S(1)}, u32[]{:S(2)}, u32[]{:S(2)}) collective-permute-start(bf16[1072,256]{1,0:T(8,128)(2,1)S(1)} %get-tuple-element.46), channel_id=1, source_target_pairs={{8,16},{12,20},{16,24},{20,28},{9,17},{13,21},{17,25},{21,29},{10,... | collective-permute-start | bytes 1646600 | tf_op jit(solution)/shard_map/ppermute | solution.py:404
  100.6 6.0 %own_rows.3.own = bf16[1072,256]{1,0:T(8,128)(2,1)S(1)} custom-call(s32[4]{0:T(128)S(1)} %pad_add_fusion.at, bf16[2,512,256]{2,1,0:T(8,128)(2,1)S(1)} %copy-done.3, bf16[2,512,512]{2,1,0:T(8,128)(2,1)S(1)} %get-tuple-element.68.kv_m, bf16[2,512,512]{2,1,0:T(8,128)(2,1)} %collective-permute-done.4.kv_o, bf16[4,512,256]{2,1,0:T(8,128)(2,1)S(1)} %collective-permute-done.10.refs_0_), custom_call_target="tpu_custom_call" | custom-call | flops 6000000000 | bytes 1024 | tf_op jit(solution)/shard_map/own_rows/pallas_call | solution.py:300
  106.6 5.2 %collective-permute-done.12.ob = bf16[1072,256]{1,0:T(8,128)(2,1)S(1)} collective-permute-done((bf16[1072,256]{1,0:T(8,128)(2,1)S(1)}, bf16[1072,256]{1,0:T(8,128)(2,1)S(1)}, u32[]{:S(2)}, u32[]{:S(2)}) %collective-permute-start.12) | collective-permute-done | bytes 548896 | tf_op jit(solution)/shard_map/ppermute | solution.py:404
  111.8 2.4 %merge.2 = bf16[2,512,256]{2,1,0:T(8,128)(2,1)S(1)} custom-call(s32[4]{0:T(128)S(1)} %pad_add_fusion.at, bf16[1072,256]{1,0:T(8,128)(2,1)S(1)} %own_rows.2.own, bf16[1072,256]{1,0:T(8,128)(2,1)S(1)} %collective-permute-done.11.oa, bf16[1072,256]{1,0:T(8,128)(2,1)S(1)} %collective-permute-done.12.ob), custom_call_target="tpu_custom_call" | custom-call | flops 2000000000 | bytes 1024 | tf_op jit(solution)/shard_map/merge/pallas_call | solution.py:300
  116.4 2.7 %collective-permute-start.13 = (bf16[1024,512]{1,0:T(8,128)(2,1)S(1)}, bf16[1024,512]{1,0:T(8,128)(2,1)S(1)}, u32[]{:S(2)}, u32[]{:S(2)}) collective-permute-start(bf16[1024,512]{1,0:T(8,128)(2,1)S(1)} %pad_maximum_fusion.1), channel_id=1, source_target_pairs={{0,8},{4,12},{8,0},{12,4},{16,24},{20,28},{24,16},{28,20},{1,9},{5... | collective-permute-start | bytes 3145736 | tf_op jit(solution)/shard_map/ppermute | solution.py:404
  119.1 6.6 %collective-permute-done.14 = bf16[2,512,256]{2,1,0:T(8,128)(2,1)S(1)} collective-permute-done((bf16[2,512,256]{2,1,0:T(8,128)(2,1)S(1)}, bf16[2,512,256]{2,1,0:T(8,128)(2,1)S(1)}, u32[]{:S(2)}, u32[]{:S(2)}) %collective-permute-start.14) | collective-permute-done | bytes 524320 | tf_op jit(solution)/shard_map/ppermute | solution.py:404
  125.7 6.4 %collective-permute-done.16.ob = bf16[1072,256]{1,0:T(8,128)(2,1)S(1)} collective-permute-done((bf16[1072,256]{1,0:T(8,128)(2,1)S(1)}, bf16[1072,256]{1,0:T(8,128)(2,1)S(1)}, u32[]{:S(2)}, u32[]{:S(2)}) %collective-permute-start.16) | collective-permute-done | bytes 548896 | tf_op jit(solution)/shard_map/ppermute | solution.py:404
  132.1 2.4 %merge.3 = bf16[2,512,256]{2,1,0:T(8,128)(2,1)S(1)} custom-call(s32[4]{0:T(128)S(1)} %pad_add_fusion.at, bf16[1072,256]{1,0:T(8,128)(2,1)S(1)} %own_rows.3.own, bf16[1072,256]{1,0:T(8,128)(2,1)S(1)} %collective-permute-done.15.oa, bf16[1072,256]{1,0:T(8,128)(2,1)S(1)} %collective-permute-done.16.ob), custom_call_target="tpu_custom_call" | custom-call | flops 2000000000 | bytes 1024 | tf_op jit(solution)/shard_map/merge/pallas_call | solution.py:300
  136.1 14.7 %collective-permute-done.13.refs_6_ = bf16[1024,512]{1,0:T(8,128)(2,1)S(1)} collective-permute-done((bf16[1024,512]{1,0:T(8,128)(2,1)S(1)}, bf16[1024,512]{1,0:T(8,128)(2,1)S(1)}, u32[]{:S(2)}, u32[]{:S(2)}) %collective-permute-start.13) | collective-permute-done | bytes 1048608 | tf_op jit(solution)/shard_map/ppermute | solution.py:404
  150.8 2.9 %project.2 = (bf16[2,2,2,128,512]{4,3,2,1,0:T(8,128)(2,1)S(1)}, bf16[2,2,2,128,512]{4,3,2,1,0:T(8,128)(2,1)S(1)}) custom-call(s32[4]{0:T(128)S(1)} %pad_add_fusion.at, bf16[2,2,2,128,256]{4,3,2,1,0:T(8,128)(2,1)S(1)} %bitcast.28, bf16[2,2,2,128,256]{4,3,2,1,0:T(8,128)(2,1)S(1)} %bitcast.32, bf16[2,2,2,128,256]{4,3,2,1,0:T(8,128)(2,1)S(1)} %bitcast.30, ...), custom_call_target="tpu_custom_call" | custom-call | flops 4000000000 | bytes 1024 | tf_op jit(solution)/shard_map/project/pallas_call | solution.py:349
  153.7 2.9 %project.3 = (bf16[2,2,2,128,512]{4,3,2,1,0:T(8,128)(2,1)S(1)}, bf16[2,2,2,128,512]{4,3,2,1,0:T(8,128)(2,1)S(1)}) custom-call(s32[4]{0:T(128)S(1)} %pad_add_fusion.at, bf16[2,2,2,128,256]{4,3,2,1,0:T(8,128)(2,1)S(1)} %bitcast.29, bf16[2,2,2,128,256]{4,3,2,1,0:T(8,128)(2,1)S(1)} %bitcast.33, bf16[2,2,2,128,256]{4,3,2,1,0:T(8,128)(2,1)S(1)} %bitcast.31, ...), custom_call_target="tpu_custom_call" | custom-call | flops 4000000000 | bytes 1024 | tf_op jit(solution)/shard_map/project/pallas_call | solution.py:349
  157.2 2.1 %collective-permute-done.22.got = bf16[2,2,2,128,512]{4,3,2,1,0:T(8,128)(2,1)S(1)} collective-permute-done((bf16[2,2,2,128,512]{4,3,2,1,0:T(8,128)(2,1)S(1)}, bf16[2,2,2,128,512]{4,3,2,1,0:T(8,128)(2,1)S(1)}, u32[]{:S(2)}, u32[]{:S(2)}) %collective-permute-start.22) | collective-permute-done | bytes 1048608 | tf_op jit(solution)/shard_map/ppermute | solution.py:410
  167.6 2.5 %collective-permute-done.23.refs_5_ = bf16[2,128,512]{2,1,0:T(8,128)(2,1)S(1)} collective-permute-done((bf16[2,128,512]{2,1,0:T(8,128)(2,1)S(1)}, bf16[2,128,512]{2,1,0:T(8,128)(2,1)S(1)}, u32[]{:S(2)}, u32[]{:S(2)}) %collective-permute-start.23) | collective-permute-done | bytes 262176 | tf_op jit(solution)/shard_map/ppermute | solution.py:410
  170.1 2.4 %collective-permute-start.21 = (bf16[2,128,512]{2,1,0:T(8,128)(2,1)S(1)}, bf16[2,128,512]{2,1,0:T(8,128)(2,1)S(1)}, u32[]{:S(2)}, u32[]{:S(2)}) collective-permute-start(bf16[2,128,512]{2,1,0:T(8,128)(2,1)S(1)} %get-tuple-element.59), channel_id=1, source_target_pairs={{0,6},{1,7},{2,4},{3,5},{4,2},{5,3},{6,0},{7,1},{8,14},{9,15},{10,... | collective-permute-start | bytes 786440 | tf_op jit(solution)/shard_map/ppermute | solution.py:497
  172.5 4.0 %collective-permute-done.25.refs_7_ = bf16[2,128,512]{2,1,0:T(8,128)(2,1)S(1)} collective-permute-done((bf16[2,128,512]{2,1,0:T(8,128)(2,1)S(1)}, bf16[2,128,512]{2,1,0:T(8,128)(2,1)S(1)}, u32[]{:S(2)}, u32[]{:S(2)}) %collective-permute-start.25) | collective-permute-done | bytes 262176 | tf_op jit(solution)/shard_map/ppermute | solution.py:497
  176.5 3.3 %collective-permute-done.19.refs_1_ = bf16[2,128,512]{2,1,0:T(8,128)(2,1)S(1)} collective-permute-done((bf16[2,128,512]{2,1,0:T(8,128)(2,1)S(1)}, bf16[2,128,512]{2,1,0:T(8,128)(2,1)S(1)}, u32[]{:S(2)}, u32[]{:S(2)}) %collective-permute-start.19) | collective-permute-done | bytes 262176 | tf_op jit(solution)/shard_map/ppermute | solution.py:410
  179.8 2.4 %collective-permute-done.20.refs_2_ = bf16[2,128,512]{2,1,0:T(8,128)(2,1)S(1)} collective-permute-done((bf16[2,128,512]{2,1,0:T(8,128)(2,1)S(1)}, bf16[2,128,512]{2,1,0:T(8,128)(2,1)S(1)}, u32[]{:S(2)}, u32[]{:S(2)}) %collective-permute-start.20) | collective-permute-done | bytes 262176 | tf_op jit(solution)/shard_map/ppermute | solution.py:404
  182.2 4.4 %collective-permute-done.21.refs_3_ = bf16[2,128,512]{2,1,0:T(8,128)(2,1)S(1)} collective-permute-done((bf16[2,128,512]{2,1,0:T(8,128)(2,1)S(1)}, bf16[2,128,512]{2,1,0:T(8,128)(2,1)S(1)}, u32[]{:S(2)}, u32[]{:S(2)}) %collective-permute-start.21) | collective-permute-done | bytes 262176 | tf_op jit(solution)/shard_map/ppermute | solution.py:497
  (62 shorter events, 33.7 us)
Async XLA Ops:
  2.1 14.0 %collective-permute-start.1 = (bf16[1,512,512]{2,1,0:T(8,128)(2,1)}, bf16[1,512,512]{2,1,0:T(8,128)(2,1)}, u32[]{:S(2)}, u32[]{:S(2)}) collective-permute-start(bf16[1,512,512]{2,1,0:T(8,128)(2,1)} %get-tuple-element.70), channel_id=1, source_target_pairs={{0,4},{4,0},{8,12},{12,8},{16,20},{20,16},{24,28},{28,24},{1,5},{5... | collective-permute-start | bytes 1572872 | tf_op jit(solution)/shard_map/ppermute | solution.py:404
  4.8 12.3 %copy-start.7 = (bf16[1024,256]{1,0:T(8,128)(2,1)}, bf16[1024,256]{1,0:T(8,128)(2,1)S(1)}, u32[]{:S(2)}) copy-start(bf16[1024,256]{1,0:T(8,128)(2,1)S(1)} %get-tuple-element.43) | copy-start | bytes 1572868
  4.8 22.5 %collective-permute-start = (bf16[1024,256]{1,0:T(8,128)(2,1)S(1)}, bf16[1024,256]{1,0:T(8,128)(2,1)S(1)}, u32[]{:S(2)}, u32[]{:S(2)}) collective-permute-start(bf16[1024,256]{1,0:T(8,128)(2,1)S(1)} %get-tuple-element.79), channel_id=1, source_target_pairs={{0,16},{4,20},{8,24},{12,28},{16,0},{20,4},{24,8},{28,12},{1,17},{... | collective-permute-start | bytes 1572872 | tf_op jit(solution)/shard_map/ppermute | solution.py:404
  18.8 45.3 %collective-permute-start.4 = (bf16[2,512,512]{2,1,0:T(8,128)(2,1)}, bf16[2,512,512]{2,1,0:T(8,128)(2,1)}, u32[]{:S(2)}, u32[]{:S(2)}) collective-permute-start(bf16[2,512,512]{2,1,0:T(8,128)(2,1)} %get-tuple-element.36), channel_id=1, source_target_pairs={{0,4},{4,0},{8,12},{12,8},{16,20},{20,16},{24,28},{28,24},{1,5},{5... | collective-permute-start | bytes 3145736 | tf_op jit(solution)/shard_map/ppermute | solution.py:404
  20.3 46.9 %copy-start = (bf16[1024,512]{1,0:T(8,128)(2,1)S(1)}, bf16[1024,512]{1,0:T(8,128)(2,1)}, u32[]{:S(2)}) copy-start(bf16[1024,512]{1,0:T(8,128)(2,1)} %refs_4_.1) | copy-start | bytes 3145732
  27.4 9.1 %collective-permute-start.5 = (bf16[2,512,256]{2,1,0:T(8,128)(2,1)S(1)}, bf16[2,512,256]{2,1,0:T(8,128)(2,1)S(1)}, u32[]{:S(2)}, u32[]{:S(2)}) collective-permute-start(bf16[2,512,256]{2,1,0:T(8,128)(2,1)S(1)} %get-tuple-element.37), channel_id=1, source_target_pairs={{0,8},{4,12},{1,9},{5,13},{2,10},{6,14},{3,11},{7,15}} | collective-permute-start | bytes 1572872 | tf_op jit(solution)/shard_map/ppermute | solution.py:404
  28.2 19.3 %collective-permute-start.3 = (bf16[2,512,256]{2,1,0:T(8,128)(2,1)}, bf16[2,512,256]{2,1,0:T(8,128)(2,1)S(1)}, u32[]{:S(2)}, u32[]{:S(2)}) collective-permute-start(bf16[2,512,256]{2,1,0:T(8,128)(2,1)} %get-tuple-element.85), channel_id=1, source_target_pairs={{16,8},{20,12},{24,16},{28,20},{8,24},{12,28},{17,9},{21,13},{25,1... | collective-permute-start | bytes 1572872 | tf_op jit(solution)/shard_map/ppermute | solution.py:404
  33.2 24.2 %collective-permute-start.2 = (bf16[2,512,256]{2,1,0:T(8,128)(2,1)}, bf16[2,512,256]{2,1,0:T(8,128)(2,1)S(1)}, u32[]{:S(2)}, u32[]{:S(2)}) collective-permute-start(bf16[2,512,256]{2,1,0:T(8,128)(2,1)} %get-tuple-element.86), channel_id=1, source_target_pairs={{24,8},{28,12},{8,0},{12,4},{16,24},{20,28},{0,16},{4,20},{25,9},{... | collective-permute-start | bytes 1572872 | tf_op jit(solution)/shard_map/ppermute | solution.py:404
  37.3 29.0 %collective-permute-start.6 = (bf16[2,512,256]{2,1,0:T(8,128)(2,1)}, bf16[2,512,256]{2,1,0:T(8,128)(2,1)}, u32[]{:S(2)}, u32[]{:S(2)}) collective-permute-start(bf16[2,512,256]{2,1,0:T(8,128)(2,1)} %slice.51), channel_id=1, source_target_pairs={{0,12},{4,8},{1,13},{5,9},{2,14},{6,10},{3,15},{7,11}} | collective-permute-start | bytes 1572872 | tf_op jit(solution)/shard_map/ppermute | solution.py:404
  38.8 28.4 %copy-start.6 = (bf16[2,512,256]{2,1,0:T(8,128)(2,1)S(1)}, bf16[2,512,256]{2,1,0:T(8,128)(2,1)}, u32[]{:S(2)}) copy-start(bf16[2,512,256]{2,1,0:T(8,128)(2,1)} %copy-done.5) | copy-start | bytes 1572868
  57.4 24.9 %collective-permute-start.7 = (bf16[2,512,256]{2,1,0:T(8,128)(2,1)}, bf16[2,512,256]{2,1,0:T(8,128)(2,1)S(1)}, u32[]{:S(2)}, u32[]{:S(2)}) collective-permute-start(bf16[2,512,256]{2,1,0:T(8,128)(2,1)} %get-tuple-element.41.q), channel_id=1, source_target_pairs={{16,8},{20,12},{24,16},{28,20},{17,9},{21,13},{25,17},{29,21},{18,... | collective-permute-start | bytes 1572872 | tf_op jit(solution)/shard_map/ppermute | solution.py:404
  61.5 20.8 %collective-permute-start.8 = (bf16[2,512,256]{2,1,0:T(8,128)(2,1)}, bf16[2,512,256]{2,1,0:T(8,128)(2,1)S(1)}, u32[]{:S(2)}, u32[]{:S(2)}) collective-permute-start(bf16[2,512,256]{2,1,0:T(8,128)(2,1)} %get-tuple-element.42), channel_id=1, source_target_pairs={{24,8},{28,12},{8,0},{12,4},{16,24},{20,28},{25,9},{29,13},{9,1},{... | collective-permute-start | bytes 1572872 | tf_op jit(solution)/shard_map/ppermute | solution.py:404
  66.3 9.9 %copy-start.4 = (bf16[2,512,256]{2,1,0:T(8,128)(2,1)S(1)}, bf16[2,512,256]{2,1,0:T(8,128)(2,1)}, u32[]{:S(2)}) copy-start(bf16[2,512,256]{2,1,0:T(8,128)(2,1)} %get-tuple-element.87.q) | copy-start | bytes 1572868
  66.3 22.5 %collective-permute-start.10 = (bf16[4,512,256]{2,1,0:T(8,128)(2,1)S(1)}, bf16[4,512,256]{2,1,0:T(8,128)(2,1)S(1)}, u32[]{:S(2)}, u32[]{:S(2)}) collective-permute-start(bf16[4,512,256]{2,1,0:T(8,128)(2,1)S(1)} %pad_maximum_fusion), channel_id=1, source_target_pairs={{0,8},{4,12},{1,9},{5,13},{2,10},{6,14},{3,11},{7,15}} | collective-permute-start | bytes 3145736 | tf_op jit(solution)/shard_map/ppermute | solution.py:404
  74.0 8.3 %copy-start.8 = (bf16[1024,256]{1,0:T(8,128)(2,1)S(1)}, bf16[1024,256]{1,0:T(8,128)(2,1)}, u32[]{:S(2)}) copy-start(bf16[1024,256]{1,0:T(8,128)(2,1)} %copy-done.7) | copy-start | bytes 1572868
  74.0 37.8 %collective-permute-start.11 = (bf16[1072,256]{1,0:T(8,128)(2,1)S(1)}, bf16[1072,256]{1,0:T(8,128)(2,1)S(1)}, u32[]{:S(2)}, u32[]{:S(2)}) collective-permute-start(bf16[1072,256]{1,0:T(8,128)(2,1)S(1)} %get-tuple-element.39), channel_id=1, source_target_pairs={{8,16},{12,20},{16,24},{20,28},{9,17},{13,21},{17,25},{21,29},{10,... | collective-permute-start | bytes 1646600 | tf_op jit(solution)/shard_map/ppermute | solution.py:404
  82.3 32.5 %collective-permute-start.9 = (bf16[1024,256]{1,0:T(8,128)(2,1)S(1)}, bf16[1024,256]{1,0:T(8,128)(2,1)S(1)}, u32[]{:S(2)}, u32[]{:S(2)}) collective-permute-start(bf16[1024,256]{1,0:T(8,128)(2,1)S(1)} %copy-done.8), channel_id=1, source_target_pairs={{16,0},{20,4},{24,8},{28,12},{17,1},{21,5},{25,9},{29,13},{18,2},{... | collective-permute-start | bytes 1572872 | tf_op jit(solution)/shard_map/ppermute | solution.py:404
  87.4 13.2 %copy-start.3 = (bf16[2,512,256]{2,1,0:T(8,128)(2,1)S(1)}, bf16[2,512,256]{2,1,0:T(8,128)(2,1)}, u32[]{:S(2)}) copy-start(bf16[2,512,256]{2,1,0:T(8,128)(2,1)} %get-tuple-element.41.q) | copy-start | bytes 1572868
  87.4 24.4 %collective-permute-start.12 = (bf16[1072,256]{1,0:T(8,128)(2,1)S(1)}, bf16[1072,256]{1,0:T(8,128)(2,1)S(1)}, u32[]{:S(2)}, u32[]{:S(2)}) collective-permute-start(bf16[1072,256]{1,0:T(8,128)(2,1)S(1)} %get-tuple-element.49), channel_id=1, source_target_pairs={{8,24},{12,28},{0,8},{4,12},{24,16},{28,20},{9,25},{13,29},{1,9},{... | collective-permute-start | bytes 1646600 | tf_op jit(solution)/shard_map/ppermute | solution.py:404
  95.5 36.6 %collective-permute-start.15 = (bf16[1072,256]{1,0:T(8,128)(2,1)S(1)}, bf16[1072,256]{1,0:T(8,128)(2,1)S(1)}, u32[]{:S(2)}, u32[]{:S(2)}) collective-permute-start(bf16[1072,256]{1,0:T(8,128)(2,1)S(1)} %get-tuple-element.46), channel_id=1, source_target_pairs={{8,16},{12,20},{16,24},{20,28},{9,17},{13,21},{17,25},{21,29},{10,... | collective-permute-start | bytes 1646600 | tf_op jit(solution)/shard_map/ppermute | solution.py:404
  114.2 11.5 %collective-permute-start.14 = (bf16[2,512,256]{2,1,0:T(8,128)(2,1)S(1)}, bf16[2,512,256]{2,1,0:T(8,128)(2,1)S(1)}, u32[]{:S(2)}, u32[]{:S(2)}) collective-permute-start(bf16[2,512,256]{2,1,0:T(8,128)(2,1)S(1)} %merge.2), channel_id=1, source_target_pairs={{0,4},{4,0},{8,12},{12,8},{16,20},{20,16},{24,28},{28,24},{1,5},{5... | collective-permute-start | bytes 1572872 | tf_op jit(solution)/shard_map/ppermute | solution.py:404
  114.8 17.3 %collective-permute-start.16 = (bf16[1072,256]{1,0:T(8,128)(2,1)S(1)}, bf16[1072,256]{1,0:T(8,128)(2,1)S(1)}, u32[]{:S(2)}, u32[]{:S(2)}) collective-permute-start(bf16[1072,256]{1,0:T(8,128)(2,1)S(1)} %get-tuple-element.53), channel_id=1, source_target_pairs={{8,24},{12,28},{0,8},{4,12},{24,16},{28,20},{9,25},{13,29},{1,9},{... | collective-permute-start | bytes 1646600 | tf_op jit(solution)/shard_map/ppermute | solution.py:404
  116.4 34.4 %collective-permute-start.13 = (bf16[1024,512]{1,0:T(8,128)(2,1)S(1)}, bf16[1024,512]{1,0:T(8,128)(2,1)S(1)}, u32[]{:S(2)}, u32[]{:S(2)}) collective-permute-start(bf16[1024,512]{1,0:T(8,128)(2,1)S(1)} %pad_maximum_fusion.1), channel_id=1, source_target_pairs={{0,8},{4,12},{8,0},{12,4},{16,24},{20,28},{24,16},{28,20},{1,9},{5... | collective-permute-start | bytes 3145736 | tf_op jit(solution)/shard_map/ppermute | solution.py:404
  134.5 16.3 %collective-permute-start.17 = (bf16[2,512,256]{2,1,0:T(8,128)(2,1)S(1)}, bf16[2,512,256]{2,1,0:T(8,128)(2,1)S(1)}, u32[]{:S(2)}, u32[]{:S(2)}) collective-permute-start(bf16[2,512,256]{2,1,0:T(8,128)(2,1)S(1)} %merge.3), channel_id=1, source_target_pairs={{0,4},{4,0},{8,12},{12,8},{16,20},{20,16},{24,28},{28,24},{1,5},{5... | collective-permute-start | bytes 1572872 | tf_op jit(solution)/shard_map/ppermute | solution.py:404
  156.6 2.7 %collective-permute-start.22 = (bf16[2,2,2,128,512]{4,3,2,1,0:T(8,128)(2,1)S(1)}, bf16[2,2,2,128,512]{4,3,2,1,0:T(8,128)(2,1)S(1)}, u32[]{:S(2)}, u32[]{:S(2)}) collective-permute-start(bf16[2,2,2,128,512]{4,3,2,1,0:T(8,128)(2,1)S(1)} %get-tuple-element.62), channel_id=1, source_target_pairs={{0,1},{1,0},{2,3},{3,2},{4,5},{5,4},{6,7},{7,6},{8,9},{9,8},{10,11... | collective-permute-start | bytes 3145736 | tf_op jit(solution)/shard_map/ppermute | solution.py:410
  156.7 7.0 %collective-permute-start.18 = (bf16[2,2,2,128,512]{4,3,2,1,0:T(8,128)(2,1)S(1)}, bf16[2,2,2,128,512]{4,3,2,1,0:T(8,128)(2,1)S(1)}, u32[]{:S(2)}, u32[]{:S(2)}) collective-permute-start(bf16[2,2,2,128,512]{4,3,2,1,0:T(8,128)(2,1)S(1)} %get-tuple-element.55), channel_id=1, source_target_pairs={{0,1},{1,0},{2,3},{3,2},{4,5},{5,4},{6,7},{7,6},{8,9},{9,8},{10,11... | collective-permute-start | bytes 3145736 | tf_op jit(solution)/shard_map/ppermute | solution.py:410
  160.1 10.0 %collective-permute-start.23 = (bf16[2,128,512]{2,1,0:T(8,128)(2,1)S(1)}, bf16[2,128,512]{2,1,0:T(8,128)(2,1)S(1)}, u32[]{:S(2)}, u32[]{:S(2)}) collective-permute-start(bf16[2,128,512]{2,1,0:T(8,128)(2,1)S(1)} %get-tuple-element.64), channel_id=1, source_target_pairs={{0,2},{1,3},{2,0},{3,1},{4,6},{5,7},{6,4},{7,5},{8,10},{9,11},{10,... | collective-permute-start | bytes 786440 | tf_op jit(solution)/shard_map/ppermute | solution.py:410
  161.7 10.8 %collective-permute-start.24 = (bf16[2,128,512]{2,1,0:T(8,128)(2,1)S(1)}, bf16[2,128,512]{2,1,0:T(8,128)(2,1)S(1)}, u32[]{:S(2)}, u32[]{:S(2)}) collective-permute-start(bf16[2,128,512]{2,1,0:T(8,128)(2,1)S(1)} %get-tuple-element.65), channel_id=1, source_target_pairs={{0,4},{4,0},{8,12},{12,8},{16,20},{20,16},{24,28},{28,24},{1,5},{5... | collective-permute-start | bytes 786440 | tf_op jit(solution)/shard_map/ppermute | solution.py:404
  163.2 13.3 %collective-permute-start.25 = (bf16[2,128,512]{2,1,0:T(8,128)(2,1)S(1)}, bf16[2,128,512]{2,1,0:T(8,128)(2,1)S(1)}, u32[]{:S(2)}, u32[]{:S(2)}) collective-permute-start(bf16[2,128,512]{2,1,0:T(8,128)(2,1)S(1)} %get-tuple-element.66), channel_id=1, source_target_pairs={{0,6},{1,7},{2,4},{3,5},{4,2},{5,3},{6,0},{7,1},{8,14},{9,15},{10,... | collective-permute-start | bytes 786440 | tf_op jit(solution)/shard_map/ppermute | solution.py:497
  164.5 15.3 %collective-permute-start.19 = (bf16[2,128,512]{2,1,0:T(8,128)(2,1)S(1)}, bf16[2,128,512]{2,1,0:T(8,128)(2,1)S(1)}, u32[]{:S(2)}, u32[]{:S(2)}) collective-permute-start(bf16[2,128,512]{2,1,0:T(8,128)(2,1)S(1)} %get-tuple-element.57), channel_id=1, source_target_pairs={{0,2},{1,3},{2,0},{3,1},{4,6},{5,7},{6,4},{7,5},{8,10},{9,11},{10,... | collective-permute-start | bytes 786440 | tf_op jit(solution)/shard_map/ppermute | solution.py:410
  166.1 16.1 %collective-permute-start.20 = (bf16[2,128,512]{2,1,0:T(8,128)(2,1)S(1)}, bf16[2,128,512]{2,1,0:T(8,128)(2,1)S(1)}, u32[]{:S(2)}, u32[]{:S(2)}) collective-permute-start(bf16[2,128,512]{2,1,0:T(8,128)(2,1)S(1)} %get-tuple-element.58), channel_id=1, source_target_pairs={{0,4},{4,0},{8,12},{12,8},{16,20},{20,16},{24,28},{28,24},{1,5},{5... | collective-permute-start | bytes 786440 | tf_op jit(solution)/shard_map/ppermute | solution.py:404
  170.1 16.5 %collective-permute-start.21 = (bf16[2,128,512]{2,1,0:T(8,128)(2,1)S(1)}, bf16[2,128,512]{2,1,0:T(8,128)(2,1)S(1)}, u32[]{:S(2)}, u32[]{:S(2)}) collective-permute-start(bf16[2,128,512]{2,1,0:T(8,128)(2,1)S(1)} %get-tuple-element.59), channel_id=1, source_target_pairs={{0,6},{1,7},{2,4},{3,5},{4,2},{5,3},{6,0},{7,1},{8,14},{9,15},{10,... | collective-permute-start | bytes 786440 | tf_op jit(solution)/shard_map/ppermute | solution.py:497
  (3 other events, 3.8 us)

commit v13 on v7

--- a/solution.py
+++ b/solution.py
@@ -201,7 +201,7 @@
     return [ref[i] for ref in refs for i in range(ref.shape[0])]
 
 
-def own_kernel(coef, cols, at, q, kv_m, kv_o, *refs):
+def own_kernel(coef, cols, at, q_m, q_o, kv_m, kv_o, *refs):
     x, z = at[0], at[1]
     below = z == 1
     block = 256
@@ -217,6 +217,7 @@
     lk_e, lk_o = jnp.where(first, m_k, o_k), jnp.where(first, o_k, m_k)
     lv_e, lv_o = jnp.where(first, m_v, o_v), jnp.where(first, o_v, m_v)
     lv_o1 = with_ones(lv_o)
+    q_e, q_o = jnp.where(first, q_m[0], q_o[0]), jnp.where(first, q_o[0], q_m[0])
     evens, odds = [], []
     for part in range(cols // block):
         a, b = part * block, (part + 1) * block
@@ -228,8 +229,8 @@
             blocks = [(k[a:b], v[a:b], tri)]
             return blocks if part == 0 else [(k[:a], v[:a], None)] + blocks
 
-        o1, l1 = attend(q[0, mine], causal(k_e, v_e) + [(lk_o, lv_o1, below)], [col_e], coef)
-        o2, l2 = attend(q[1, mine], causal(k_o, v_o) + [(k_e, v_e, None)], [col_e, col_o], coef)
+        o1, l1 = attend(q_e[mine], causal(k_e, v_e) + [(lk_o, lv_o1, below)], [col_e], coef)
+        o2, l2 = attend(q_o[mine], causal(k_o, v_o) + [(k_e, v_e, None)], [col_e, col_o], coef)
         out[mine] = o1.astype(BF16)
         out[cols + a : cols + b] = o2.astype(BF16)
         e, o = lse_rows(l1, l2)
@@ -237,7 +238,7 @@
     put_lse(out, 2 * cols, evens, odds)
 
 
-def upper_kernel(coef, cols, at, qa, qb, kv_m, kv_o, *refs):
+def upper_kernel(coef, cols, at, qa_m, qa_o, qb_m, qb_o, kv_m, kv_o, *refs):
     x, z = at[0], at[1]
     below = z == 1
     first = x == 0
@@ -247,6 +248,8 @@
     v_o1 = with_ones(v_o)
     *low, weight, out_a, out_b = refs
     lows = stacked(low)
+    qa = jnp.where(first, qa_m[0], qa_o[0]), jnp.where(first, qa_o[0], qa_m[0])
+    qb = jnp.where(first, qb_m[0], qb_o[0]), jnp.where(first, qb_o[0], qb_m[0])
     rows_a, rows_b = ([], []), ([], [])
     for index in range(cols // block):
         a, b = index * block, (index + 1) * block
@@ -259,8 +262,8 @@
             (qa, out_a, rows_a, [(k_o, v_o1, None)], [ce]),
             (qb, out_b, rows_b, [], [ce, co]),
         ):
-            o1, l1 = attend(q[0, mine], dense, singles + low, coef)
-            o2, l2 = attend(q[1, mine], [], [ce, co] + low, coef)
+            o1, l1 = attend(q[0][mine], dense, singles + low, coef)
+            o2, l2 = attend(q[1][mine], [], [ce, co] + low, coef)
             o1, o2 = o1.astype(BF16), o2.astype(BF16)
             other = slice(cols + a, cols + b)
             if out is out_b:
@@ -289,7 +292,7 @@
 
 
 def cost(us):
-    return pl.CostEstimate(flops=int(us * 1e9), bytes_accessed=1024, transcendentals=0)
+    return pl.CostEstimate(flops=int(us * 1e8), bytes_accessed=1024, transcendentals=0)
 
 
 def head_call(kernel, at, args, outs, heads, name, us):
@@ -412,55 +415,42 @@
     def lanes(lo, hi, part, source=local):
         return lax.dynamic_slice(source, (lo, 0, part * half), (hi - lo, cols, half))
 
-    def lanes(lo, hi, half_of):
-        return lax.dynamic_slice(local, (lo, 0, half_of * half), (hi - lo, cols, half))
-
-    def pieces(array, c):
-        return array[..., c * width : (c + 1) * width]
-
-    q_m, q_o = lanes(0, 1, x), swap(lanes(0, 1, 1 - x))
+    def with_weight(array, part):
+        return jnp.where(z == 3, array, out_weight[part * cols : (part + 1) * cols].reshape(array.shape))
+
+    down, two_down = [(2, 1), (3, 2)], [(3, 1), (0, 2), (1, 0), (2, 3)]
+    q_m = lanes(0, 1, x)
+    q_o = swap(lanes(0, 1, 1 - x))
+    qs = [seq_perm(q_m, *down), None, seq_perm(with_weight(q_m, 0), *two_down), None]
     kv_m, kv_give = lanes(1, 3, x), lanes(1, 3, 1 - x)
-    q, qs, low = [], [], []
-    for c in range(chunks):
-        a, b = pieces(q_m, c), pieces(q_o, c)
-        q.append(jnp.concatenate([jnp.where(first, a, b), jnp.where(first, b, a)]))
-        block = pieces(out_weight, c).reshape(q[c].shape)
-        going = [q[c], jnp.where(z == 3, q[c], block)]
-        if c:
-            going = after(going, *qs[0])
-        else:
-            kv_o = swap(after(kv_give, q[0]))
-        qs.append([seq_perm(going[0], (2, 1), (3, 2)), seq_perm(going[1], (3, 1), (1, 0), (2, 3))])
-        mine = jnp.where(z == 0, pieces(kv_m, c), block)
-        if c:
-            low.append([seq_perm(after(jnp.concatenate([mine, pieces(kv_o, c)]), *low[0]), (0, 1), (1, 3))])
-        else:
-            low.append([seq_perm(mine, (0, 1), (1, 3)), seq_perm(pieces(kv_give, c), (0, 1), cross=True)])
+    low_m = seq_perm(jnp.where(z == 0, kv_m, out_weight.reshape(kv_m.shape)), (0, 1), (1, 3))
+    low_o = seq_perm(kv_give, (0, 1), cross=True)
+    kv_o = swap(after(kv_give, q_o, qs[0]))
+    qs[1], qs[3] = seq_perm(q_o, *down), seq_perm(with_weight(q_o, 1), *two_down)
 
     struct = jax.ShapeDtypeStruct
     partial = struct((2 * cols + lse_height(cols), width), BF16)
-    oa, ob, own, sent = [], [], [], []
+    oa, ob, own = [], [], []
     turn = at
+    kvs = [kv_m, kv_o, low_m, low_o]
     for c in range(chunks):
-        kvs = [(a, c * heads) for a in (kv_m, kv_o)]
         a, b = head_call(
-            functools.partial(upper_kernel, coef, cols), turn,
-            [(a, 0) for a in qs[c]] + kvs + [(a, 0) for a in low[c]] + [(out_weight, c * heads)], [partial] * 2, heads, "upper_rows", 7)
-        sent.append(a)
+            functools.partial(upper_kernel, coef, cols), turn, [(a, c * heads) for a in qs + kvs + [out_weight]],
+            [partial] * 2, heads, "upper_rows", 7)
+        turn = after(at, a)
         oa.append(seq_perm(a, (1, 2), (2, 3)))
         ob.append(seq_perm(b, (1, 3), (0, 1), (3, 2)))
+    for c in range(chunks):
         (mine,) = head_call(
-            functools.partial(own_kernel, coef, cols), after(at, a), [(q[c], 0)] + kvs + [(a, 0) for a in low[c]],
+            functools.partial(own_kernel, coef, cols), turn, [(a, c * heads) for a in [q_m, q_o] + kvs],
             [partial], heads, "own_rows", 6)
         own.append(mine)
-        turn = after(at, mine, oa[c], ob[c])
-
-    w_second = seq_perm(after(out_weight, own[0], *qs[1]), (0, 2))
+        turn = after(at, mine)
+
+    w_down = seq_perm(after(out_weight, *qs), (2, 0), (3, 1))
     depth = out_weight.shape[0]
-    w_down = seq_perm(after(out_weight, own[0], *qs[1]), (2, 0), (3, 1))
-    w_near = [
-        jnp.where((z == 0) | (z == 3), qs[c][1].reshape(depth, width), ob[c][:depth]) for c in range(chunks)
-    ]
+    ridden = jnp.concatenate([qs[2], qs[3]], axis=1).reshape(out_weight.shape)
+    w_near = jnp.where((z == 0) | (z == 3), ridden, jnp.concatenate([o[:depth] for o in ob], axis=1))
 
     def merged(c, earlier):
         (a,) = head_call(
@@ -469,23 +459,22 @@
         return a, swap(a)
 
     first_half = merged(0, own[1])
-    w_ridden = jnp.concatenate([low[c][0][:2].reshape(depth, width) for c in range(chunks)], axis=1)
     w_far = jnp.where(
-        z >= 2, jnp.where(z == 2, w_second, w_ridden), after(w_down, first_half[0], own[1]))
+        z >= 2, jnp.where(z == 2, ridden, low_m.reshape(out_weight.shape)), after(w_down, first_half[0], own[1]))
     near, far = map(list, zip(first_half, merged(1, (w_far, first_half[1]))))
     w_other = seq_perm(w_far, (0, 1), (1, 0), (2, 3), (3, 2))
 
     parts = []
     turn = after(at, w_other)
     for weights in (
-        [out_weight] + w_near,
+        [out_weight, w_near],
         [w_far, w_other],
     ):
         send, kept = project(turn, near, far, weights, out_weight.shape[1])
         got = head_perm(send, 1)
         piece = struct(send.shape[:1] + send.shape[3:], BF16)
         stay, to_y, to_x, to_xy = whole_call(split_kernel, at, [kept, got], [piece] * 4, "split", 2)
-        turn = after(at, stay)
+        turn = after(at, send)
         diagonal = [((2 * i + j) * 4 + h, (2 * i + 1 - j) * 4 + (h ^ 2)) for i in range(4) for j in range(2) for h in range(4)]
         from_xy = lax.ppermute(to_xy, ("seq", "head"), diagonal)
         parts += [stay, head_perm(to_y, 2), swap(to_x), from_xy]

time: 221 us -> 203 us (0.919)
  starting transfers between devices: 55.5 us -> 40 us
  waiting for transfers between devices: 107 us -> 101 us
  local copies, waits for them, and re-layouts: 8.94 us -> 11.2 us
    ppermute x20 -> x18, starting transfers between devices: 48.7 us -> 33.4 us  [seq_perm(): return lax.ppermute(array, 'seq', pairs)]
    ppermute x20 -> x18, waiting for transfers between devices: 90.9 us -> 82.3 us  [seq_perm(): return lax.ppermute(array, 'seq', pairs)]
    unnamed x16 -> x14, local copies, waits for them, and re-layouts: 1.08 us -> 4.46 us
    select_n x5 -> x4, other arithmetic: 3.35 us -> 6.19 us  [the longest x1 2.51 us: body_eight(): jnp.where(z == 0, kv_m, out_weight.reshape(kv_m.shape))]
  transfers between devices with their start and end apart: 26 -> 24, of which waited for: 14 -> 11; matrix products, arithmetic and copies ran while one was open for 4% -> 5% of each run, Pallas kernels for 15% -> 18%
where the time goes in v13:
time: 203 us; the launch traced here: 201 us
  waiting for transfers between devices  101 us (50%)
  Pallas kernels  42.8 us (21%)
  starting transfers between devices  40 us (20%)
  local copies, waits for them, and re-layouts  11.2 us (6%)
  other arithmetic  6.26 us (3%)
    ppermute x18, waiting for transfers between devices, seq_perm(): return lax.ppermute(array, 'seq', pairs)  82.3 us
    pallas_call x6, Pallas kernels, head_call(): pl.pallas_call(kernel, out_shape=outs, grid_spec=pltpu.PrefetchScalarGrid...  33.7 us
    ppermute x18, starting transfers between devices, seq_perm(): return lax.ppermute(array, 'seq', pairs)  33.4 us
    ppermute x2, waiting for transfers between devices, body_eight(): from_xy = lax.ppermute(to_xy, ('seq', 'head'), diagonal)  9.37 us
    pallas_call x5, Pallas kernels, whole_call(): pl.pallas_call(kernel, out_shape=outs, in_specs=[pl.BlockSpec(memory_spac...  9.07 us
    ppermute x4, waiting for transfers between devices, head_perm(): return lax.ppermute(array, 'head', [(i, i ^ flip) for i in range(4)])  8.9 us
    dynamic_slice x2, local copies, waits for them, and re-layouts, lanes(): lax.dynamic_slice(source, (lo, 0, part * half), (hi - lo, cols, half))  4.63 us
    unnamed x14, local copies, waits for them, and re-layouts  4.46 us
  transfers between devices with their start and end apart: 24, of which 11 were waited for; matrix products, arithmetic and copies ran while one was open for 5% of the time, Pallas kernels for 18%

profile of v13, /device:TPU:16, one launch (start us, length us, event | category | flops | bytes accessed | tf_op | source)
XLA Modules:
  0.0 201.2 jit_solution(9694698223485866075)
XLA Ops:
  0.0 2.3 %dynamic-slice_bitcast_fusion.2 = (bf16[1,512,512]{2,1,0:T(8,128)(2,1)}, bf16[1,512,512]{2,1,0:T(8,128)(2,1)}) fusion(bf16[3,1,512,1024]{3,2,1,0:T(8,128)(2,1)} %param.2, s32[]{:T(128)S(6)} %select_n.82, s32[]{:T(128)S(6)} %select_n.78), kind=kLoop, calls=%fused_computation.10 | loop fusion | bytes 2097160 | tf_op jit(solution)/shard_map/dynamic_slice | solution.py:416
  3.8 2.3 %collective-permute-start.4 = (bf16[1,512,512]{2,1,0:T(8,128)(2,1)}, bf16[1,512,512]{2,1,0:T(8,128)(2,1)}, u32[]{:S(2)}, u32[]{:S(2)}) collective-permute-start(bf16[1,512,512]{2,1,0:T(8,128)(2,1)} %get-tuple-element.60.q_m), channel_id=1, source_target_pairs={{16,8},{20,12},{24,16},{28,20},{17,9},{21,13},{25,17},{29,21},{18,... | collective-permute-start | bytes 1572872 | tf_op jit(solution)/shard_map/ppermute | solution.py:407
  6.2 2.0 fusion.1
  8.2 2.3 %collective-permute-start = (bf16[1,512,512]{2,1,0:T(8,128)(2,1)}, bf16[1,512,512]{2,1,0:T(8,128)(2,1)}, u32[]{:S(2)}, u32[]{:S(2)}) collective-permute-start(bf16[1,512,512]{2,1,0:T(8,128)(2,1)} %fusion.1), channel_id=1, source_target_pairs={{24,8},{28,12},{0,16},{4,20},{8,0},{12,4},{16,24},{20,28},{25,9},{... | collective-permute-start | bytes 1572872 | tf_op jit(solution)/shard_map/ppermute | solution.py:407
  10.5 2.3 %dynamic-slice_bitcast_fusion = bf16[2,512,512]{2,1,0:T(8,128)(2,1)} fusion(bf16[3,1,512,1024]{3,2,1,0:T(8,128)(2,1)} %param.2, s32[]{:T(128)S(6)} %select_n.82), kind=kLoop, calls=%fused_computation.4 | loop fusion | bytes 2097156 | tf_op jit(solution)/shard_map/dynamic_slice | solution.py:416
  12.8 1.7 collective-permute-start.8
  14.5 2.5 %broadcast_select_fusion = (bf16[2,512,512]{2,1,0:T(8,128)(2,1)}, bf16[2,512,512]{2,1,0:T(8,128)(2,1)S(1)}) fusion(bf16[2,512,512]{2,1,0:T(8,128)(2,1)S(1)} %bitcast.37, pred[]{:T(512)S(6)} %eq.17, bf16[3,1,512,1024]{3,2,1,0:T(8,128)(2,1)} %param.2, s32[]{:T(128)S(6)} %select_n.78), kind=kLoop, calls=%fused_computation.6 | loop fusion | flops 524288 | bytes 4194309 | tf_op jit(solution)/shard_map/jit(_where)/select_n | solution.py:426
  17.7 3.2 %collective-permute-done.4.qa_m = bf16[1,512,512]{2,1,0:T(8,128)(2,1)} collective-permute-done((bf16[1,512,512]{2,1,0:T(8,128)(2,1)}, bf16[1,512,512]{2,1,0:T(8,128)(2,1)}, u32[]{:S(2)}, u32[]{:S(2)}) %collective-permute-start.4) | collective-permute-done | bytes 524320 | tf_op jit(solution)/shard_map/ppermute | solution.py:407
  22.1 23.6 %collective-permute-done.qb_m = bf16[1,512,512]{2,1,0:T(8,128)(2,1)} collective-permute-done((bf16[1,512,512]{2,1,0:T(8,128)(2,1)}, bf16[1,512,512]{2,1,0:T(8,128)(2,1)}, u32[]{:S(2)}, u32[]{:S(2)}) %collective-permute-start) | collective-permute-done | bytes 524320 | tf_op jit(solution)/shard_map/ppermute | solution.py:407
  45.7 1.9 collective-permute-start.5
  47.6 31.0 %collective-permute-done.2.qb_o = bf16[1,512,512]{2,1,0:T(8,128)(2,1)S(1)} collective-permute-done((bf16[1,512,512]{2,1,0:T(8,128)(2,1)S(1)}, bf16[1,512,512]{2,1,0:T(8,128)(2,1)S(1)}, u32[]{:S(2)}, u32[]{:S(2)}) %collective-permute-start.2) | collective-permute-done | bytes 524320 | tf_op jit(solution)/shard_map/ppermute | solution.py:407
  80.2 2.4 %collective-permute-start.6 = (bf16[1024,512]{1,0:T(8,128)(2,1)S(1)}, bf16[1024,512]{1,0:T(8,128)(2,1)}, u32[]{:S(2)}, u32[]{:S(2)}) collective-permute-start(bf16[1024,512]{1,0:T(8,128)(2,1)S(1)} %copy-done), channel_id=1, source_target_pairs={{16,0},{20,4},{24,8},{28,12},{17,1},{21,5},{25,9},{29,13},{18,2},{... | collective-permute-start | bytes 3145736 | tf_op jit(solution)/shard_map/ppermute | solution.py:407
  84.8 7.5 %upper_rows.2 = (bf16[1072,256]{1,0:T(8,128)(2,1)}, bf16[1072,256]{1,0:T(8,128)(2,1)}) custom-call(s32[4]{0:T(128)S(1)} %pad_add_fusion.at, bf16[1,512,512]{2,1,0:T(8,128)(2,1)} %collective-permute-done.4.qa_m, bf16[1,512,512]{2,1,0:T(8,128)(2,1)S(1)} %copy-done.5, bf16[1,512,512]{2,1,0:T(8,128)(2,1)} %collective-permute-done.qb_m, ...), custom_call_target="tpu_custom_call" | custom-call | flops 700000000 | bytes 1024 | tf_op jit(solution)/shard_map/upper_rows/pallas_call | solution.py:303
  92.4 1.9 collective-permute-start.9
  95.6 7.6 %upper_rows.3 = (bf16[1072,256]{1,0:T(8,128)(2,1)S(1)}, bf16[1072,256]{1,0:T(8,128)(2,1)}) custom-call(s32[4]{0:T(128)S(1)} %pad_add_fusion.at, bf16[1,512,512]{2,1,0:T(8,128)(2,1)} %collective-permute-done.4.qa_m, bf16[1,512,512]{2,1,0:T(8,128)(2,1)S(1)} %copy-done.5, bf16[1,512,512]{2,1,0:T(8,128)(2,1)} %collective-permute-done.qb_m, ...), custom_call_target="tpu_custom_call" | custom-call | flops 700000000 | bytes 1024 | tf_op jit(solution)/shard_map/upper_rows/pallas_call | solution.py:303
  105.3 5.4 %collective-permute-start.13 = (bf16[1072,256]{1,0:T(8,128)(2,1)}, bf16[1072,256]{1,0:T(8,128)(2,1)S(1)}, u32[]{:S(2)}, u32[]{:S(2)}) collective-permute-start(bf16[1072,256]{1,0:T(8,128)(2,1)} %copy-done.6), channel_id=1, source_target_pairs={{8,16},{12,20},{16,24},{20,28},{9,17},{13,21},{17,25},{21,29},{10,... | collective-permute-start | bytes 1646600 | tf_op jit(solution)/shard_map/ppermute | solution.py:407
  110.6 6.1 %own_rows.2.own = bf16[1072,256]{1,0:T(8,128)(2,1)S(1)} custom-call(s32[4]{0:T(128)S(1)} %pad_add_fusion.at, bf16[1,512,512]{2,1,0:T(8,128)(2,1)} %get-tuple-element.60.q_m, bf16[1,512,512]{2,1,0:T(8,128)(2,1)} %collective-permute-done.1.q_o, bf16[2,512,512]{2,1,0:T(8,128)(2,1)S(1)} %get-tuple-element.58.kv_m, ...), custom_call_target="tpu_custom_call" | custom-call | flops 600000000 | bytes 1024 | tf_op jit(solution)/shard_map/own_rows/pallas_call | solution.py:303
  116.8 6.1 %own_rows.3.own = bf16[1072,256]{1,0:T(8,128)(2,1)S(1)} custom-call(s32[4]{0:T(128)S(1)} %pad_add_fusion.at, bf16[1,512,512]{2,1,0:T(8,128)(2,1)} %get-tuple-element.60.q_m, bf16[1,512,512]{2,1,0:T(8,128)(2,1)} %collective-permute-done.1.q_o, bf16[2,512,512]{2,1,0:T(8,128)(2,1)S(1)} %get-tuple-element.58.kv_m, ...), custom_call_target="tpu_custom_call" | custom-call | flops 600000000 | bytes 1024 | tf_op jit(solution)/shard_map/own_rows/pallas_call | solution.py:303
  122.9 3.2 %merge.2 = bf16[2,512,256]{2,1,0:T(8,128)(2,1)S(1)} custom-call(s32[4]{0:T(128)S(1)} %pad_add_fusion.at, bf16[1072,256]{1,0:T(8,128)(2,1)S(1)} %own_rows.2.own, bf16[1072,256]{1,0:T(8,128)(2,1)} %collective-permute-done.9.oa, bf16[1072,256]{1,0:T(8,128)(2,1)} %collective-permute-done.10.ob), custom_call_target="tpu_custom_call" | custom-call | flops 200000000 | bytes 1024 | tf_op jit(solution)/shard_map/merge/pallas_call | solution.py:303
  130.6 7.2 %collective-permute-start.11 = (bf16[1024,512]{1,0:T(8,128)(2,1)S(1)}, bf16[1024,512]{1,0:T(8,128)(2,1)S(1)}, u32[]{:S(2)}, u32[]{:S(2)}) collective-permute-start(bf16[1024,512]{1,0:T(8,128)(2,1)S(1)} %get-tuple-element.62.refs_4_), channel_id=1, source_target_pairs={{0,8},{4,12},{8,0},{12,4},{16,24},{20,28},{24,16},{28,20},{1,9},{5... | collective-permute-start | bytes 3145736 | tf_op jit(solution)/shard_map/ppermute | solution.py:407
  137.8 4.6 %collective-permute-done.13.oa = bf16[1072,256]{1,0:T(8,128)(2,1)S(1)} collective-permute-done((bf16[1072,256]{1,0:T(8,128)(2,1)}, bf16[1072,256]{1,0:T(8,128)(2,1)S(1)}, u32[]{:S(2)}, u32[]{:S(2)}) %collective-permute-start.13) | collective-permute-done | bytes 548896 | tf_op jit(solution)/shard_map/ppermute | solution.py:407
  142.3 3.1 %merge.3 = bf16[2,512,256]{2,1,0:T(8,128)(2,1)S(1)} custom-call(s32[4]{0:T(128)S(1)} %pad_add_fusion.at, bf16[1072,256]{1,0:T(8,128)(2,1)S(1)} %own_rows.3.own, bf16[1072,256]{1,0:T(8,128)(2,1)S(1)} %collective-permute-done.13.oa, bf16[1072,256]{1,0:T(8,128)(2,1)} %collective-permute-done.14.ob), custom_call_target="tpu_custom_call" | custom-call | flops 200000000 | bytes 1024 | tf_op jit(solution)/shard_map/merge/pallas_call | solution.py:303
  146.1 17.6 %collective-permute-done.11.refs_5_ = bf16[1024,512]{1,0:T(8,128)(2,1)S(1)} collective-permute-done((bf16[1024,512]{1,0:T(8,128)(2,1)S(1)}, bf16[1024,512]{1,0:T(8,128)(2,1)S(1)}, u32[]{:S(2)}, u32[]{:S(2)}) %collective-permute-start.11) | collective-permute-done | bytes 1048608 | tf_op jit(solution)/shard_map/ppermute | solution.py:407
  163.7 2.9 %project.2 = (bf16[2,2,2,128,512]{4,3,2,1,0:T(8,128)(2,1)S(1)}, bf16[2,2,2,128,512]{4,3,2,1,0:T(8,128)(2,1)S(1)}) custom-call(s32[4]{0:T(128)S(1)} %pad_add_fusion.at, bf16[2,2,2,128,256]{4,3,2,1,0:T(8,128)(2,1)S(1)} %bitcast.38, bf16[2,2,2,128,256]{4,3,2,1,0:T(8,128)(2,1)S(1)} %bitcast.40, bf16[2,2,2,128,256]{4,3,2,1,0:T(8,128)(2,1)S(1)} %bitcast.42, ...), custom_call_target="tpu_custom_call" | custom-call | flops 400000000 | bytes 1024 | tf_op jit(solution)/shard_map/project/pallas_call | solution.py:352
  166.5 2.9 %project.3 = (bf16[2,2,2,128,512]{4,3,2,1,0:T(8,128)(2,1)S(1)}, bf16[2,2,2,128,512]{4,3,2,1,0:T(8,128)(2,1)S(1)}) custom-call(s32[4]{0:T(128)S(1)} %pad_add_fusion.at, bf16[2,2,2,128,256]{4,3,2,1,0:T(8,128)(2,1)S(1)} %bitcast.39, bf16[2,2,2,128,256]{4,3,2,1,0:T(8,128)(2,1)S(1)} %bitcast.41, bf16[2,2,2,128,256]{4,3,2,1,0:T(8,128)(2,1)S(1)} %bitcast.43, ...), custom_call_target="tpu_custom_call" | custom-call | flops 400000000 | bytes 1024 | tf_op jit(solution)/shard_map/project/pallas_call | solution.py:352
  170.0 2.1 %collective-permute-done.20.got = bf16[2,2,2,128,512]{4,3,2,1,0:T(8,128)(2,1)S(1)} collective-permute-done((bf16[2,2,2,128,512]{4,3,2,1,0:T(8,128)(2,1)S(1)}, bf16[2,2,2,128,512]{4,3,2,1,0:T(8,128)(2,1)S(1)}, u32[]{:S(2)}, u32[]{:S(2)}) %collective-permute-start.20) | collective-permute-done | bytes 1048608 | tf_op jit(solution)/shard_map/ppermute | solution.py:413
  179.4 3.5 %collective-permute-done.21.refs_5_ = bf16[2,128,512]{2,1,0:T(8,128)(2,1)S(1)} collective-permute-done((bf16[2,128,512]{2,1,0:T(8,128)(2,1)S(1)}, bf16[2,128,512]{2,1,0:T(8,128)(2,1)S(1)}, u32[]{:S(2)}, u32[]{:S(2)}) %collective-permute-start.21) | collective-permute-done | bytes 262176 | tf_op jit(solution)/shard_map/ppermute | solution.py:413
  184.4 4.9 %collective-permute-done.23.refs_7_ = bf16[2,128,512]{2,1,0:T(8,128)(2,1)S(1)} collective-permute-done((bf16[2,128,512]{2,1,0:T(8,128)(2,1)S(1)}, bf16[2,128,512]{2,1,0:T(8,128)(2,1)S(1)}, u32[]{:S(2)}, u32[]{:S(2)}) %collective-permute-start.23) | collective-permute-done | bytes 262176 | tf_op jit(solution)/shard_map/ppermute | solution.py:479
  189.3 3.3 %collective-permute-done.17.refs_1_ = bf16[2,128,512]{2,1,0:T(8,128)(2,1)S(1)} collective-permute-done((bf16[2,128,512]{2,1,0:T(8,128)(2,1)S(1)}, bf16[2,128,512]{2,1,0:T(8,128)(2,1)S(1)}, u32[]{:S(2)}, u32[]{:S(2)}) %collective-permute-start.17) | collective-permute-done | bytes 262176 | tf_op jit(solution)/shard_map/ppermute | solution.py:413
  192.6 2.4 %collective-permute-done.18.refs_2_ = bf16[2,128,512]{2,1,0:T(8,128)(2,1)S(1)} collective-permute-done((bf16[2,128,512]{2,1,0:T(8,128)(2,1)S(1)}, bf16[2,128,512]{2,1,0:T(8,128)(2,1)S(1)}, u32[]{:S(2)}, u32[]{:S(2)}) %collective-permute-start.18) | collective-permute-done | bytes 262176 | tf_op jit(solution)/shard_map/ppermute | solution.py:407
  195.0 4.4 %collective-permute-done.19.refs_3_ = bf16[2,128,512]{2,1,0:T(8,128)(2,1)S(1)} collective-permute-done((bf16[2,128,512]{2,1,0:T(8,128)(2,1)S(1)}, bf16[2,128,512]{2,1,0:T(8,128)(2,1)S(1)}, u32[]{:S(2)}, u32[]{:S(2)}) %collective-permute-start.19) | collective-permute-done | bytes 262176 | tf_op jit(solution)/shard_map/ppermute | solution.py:479
  199.4 1.7 place.1
  (50 shorter events, 24.9 us)
Async XLA Ops:
  0.0 6.2 %copy-start = (bf16[1024,512]{1,0:T(8,128)(2,1)S(1)}, bf16[1024,512]{1,0:T(8,128)(2,1)}, u32[]{:S(2)}) copy-start(bf16[1024,512]{1,0:T(8,128)(2,1)} %refs_4_.1) | copy-start | bytes 3145732
  2.3 15.4 %collective-permute-start.1 = (bf16[1,512,512]{2,1,0:T(8,128)(2,1)}, bf16[1,512,512]{2,1,0:T(8,128)(2,1)}, u32[]{:S(2)}, u32[]{:S(2)}) collective-permute-start(bf16[1,512,512]{2,1,0:T(8,128)(2,1)} %get-tuple-element.59), channel_id=1, source_target_pairs={{0,4},{4,0},{8,12},{12,8},{16,20},{20,16},{24,28},{28,24},{1,5},{5... | collective-permute-start | bytes 1572872 | tf_op jit(solution)/shard_map/ppermute | solution.py:407
  3.8 17.0 %collective-permute-start.4 = (bf16[1,512,512]{2,1,0:T(8,128)(2,1)}, bf16[1,512,512]{2,1,0:T(8,128)(2,1)}, u32[]{:S(2)}, u32[]{:S(2)}) collective-permute-start(bf16[1,512,512]{2,1,0:T(8,128)(2,1)} %get-tuple-element.60.q_m), channel_id=1, source_target_pairs={{16,8},{20,12},{24,16},{28,20},{17,9},{21,13},{25,17},{29,21},{18,... | collective-permute-start | bytes 1572872 | tf_op jit(solution)/shard_map/ppermute | solution.py:407
  8.2 37.5 %collective-permute-start = (bf16[1,512,512]{2,1,0:T(8,128)(2,1)}, bf16[1,512,512]{2,1,0:T(8,128)(2,1)}, u32[]{:S(2)}, u32[]{:S(2)}) collective-permute-start(bf16[1,512,512]{2,1,0:T(8,128)(2,1)} %fusion.1), channel_id=1, source_target_pairs={{24,8},{28,12},{0,16},{4,20},{8,0},{12,4},{16,24},{20,28},{25,9},{... | collective-permute-start | bytes 1572872 | tf_op jit(solution)/shard_map/ppermute | solution.py:407
  12.8 69.9 %collective-permute-start.8 = (bf16[2,512,512]{2,1,0:T(8,128)(2,1)}, bf16[2,512,512]{2,1,0:T(8,128)(2,1)}, u32[]{:S(2)}, u32[]{:S(2)}) collective-permute-start(bf16[2,512,512]{2,1,0:T(8,128)(2,1)} %dynamic-slice_bitcast_fusion), channel_id=1, source_target_pairs={{0,12},{4,8},{1,13},{5,9},{2,14},{6,10},{3,15},{7,11}} | collective-permute-start | bytes 3145736 | tf_op jit(solution)/shard_map/ppermute | solution.py:407
  17.0 65.7 %collective-permute-start.3 = (bf16[2,512,512]{2,1,0:T(8,128)(2,1)}, bf16[2,512,512]{2,1,0:T(8,128)(2,1)S(1)}, u32[]{:S(2)}, u32[]{:S(2)}) collective-permute-start(bf16[2,512,512]{2,1,0:T(8,128)(2,1)} %get-tuple-element.57), channel_id=1, source_target_pairs={{0,8},{4,12},{8,24},{12,28},{1,9},{5,13},{9,25},{13,29},{2,10},{6,... | collective-permute-start | bytes 3145736 | tf_op jit(solution)/shard_map/ppermute | solution.py:407
  20.9 61.8 %collective-permute-start.7 = (bf16[2,512,512]{2,1,0:T(8,128)(2,1)}, bf16[2,512,512]{2,1,0:T(8,128)(2,1)}, u32[]{:S(2)}, u32[]{:S(2)}) collective-permute-start(bf16[2,512,512]{2,1,0:T(8,128)(2,1)} %dynamic-slice_bitcast_fusion), channel_id=1, source_target_pairs={{0,4},{4,0},{8,12},{12,8},{16,20},{20,16},{24,28},{28,24},{1,5},{5... | collective-permute-start | bytes 3145736 | tf_op jit(solution)/shard_map/ppermute | solution.py:407
  21.5 57.2 %collective-permute-start.2 = (bf16[1,512,512]{2,1,0:T(8,128)(2,1)S(1)}, bf16[1,512,512]{2,1,0:T(8,128)(2,1)S(1)}, u32[]{:S(2)}, u32[]{:S(2)}) collective-permute-start(bf16[1,512,512]{2,1,0:T(8,128)(2,1)S(1)} %bitcast_select_fusion.1), channel_id=1, source_target_pairs={{24,8},{28,12},{0,16},{4,20},{8,0},{12,4},{16,24},{20,28},{25,9},{... | collective-permute-start | bytes 1572872 | tf_op jit(solution)/shard_map/ppermute | solution.py:407
  45.7 33.7 %collective-permute-start.5 = (bf16[1,512,512]{2,1,0:T(8,128)(2,1)}, bf16[1,512,512]{2,1,0:T(8,128)(2,1)S(1)}, u32[]{:S(2)}, u32[]{:S(2)}) collective-permute-start(bf16[1,512,512]{2,1,0:T(8,128)(2,1)} %collective-permute-done.1.q_o), channel_id=1, source_target_pairs={{16,8},{20,12},{24,16},{28,20},{17,9},{21,13},{25,17},{29,21},{18,... | collective-permute-start | bytes 1572872 | tf_op jit(solution)/shard_map/ppermute | solution.py:407
  78.6 0.8 copy-start.1
  79.4 0.8 copy-start.4
  80.2 46.5 %collective-permute-start.6 = (bf16[1024,512]{1,0:T(8,128)(2,1)S(1)}, bf16[1024,512]{1,0:T(8,128)(2,1)}, u32[]{:S(2)}, u32[]{:S(2)}) collective-permute-start(bf16[1024,512]{1,0:T(8,128)(2,1)S(1)} %copy-done), channel_id=1, source_target_pairs={{16,0},{20,4},{24,8},{28,12},{17,1},{21,5},{25,9},{29,13},{18,2},{... | collective-permute-start | bytes 3145736 | tf_op jit(solution)/shard_map/ppermute | solution.py:407
  82.7 1.0 copy-start.2
  83.8 1.0 copy-start.5
  92.4 30.6 %collective-permute-start.9 = (bf16[1072,256]{1,0:T(8,128)(2,1)}, bf16[1072,256]{1,0:T(8,128)(2,1)}, u32[]{:S(2)}, u32[]{:S(2)}) collective-permute-start(bf16[1072,256]{1,0:T(8,128)(2,1)} %get-tuple-element.33), channel_id=1, source_target_pairs={{8,16},{12,20},{16,24},{20,28},{9,17},{13,21},{17,25},{21,29},{10,... | collective-permute-start | bytes 1646600 | tf_op jit(solution)/shard_map/ppermute | solution.py:407
  94.3 28.7 %collective-permute-start.10 = (bf16[1072,256]{1,0:T(8,128)(2,1)}, bf16[1072,256]{1,0:T(8,128)(2,1)}, u32[]{:S(2)}, u32[]{:S(2)}) collective-permute-start(bf16[1072,256]{1,0:T(8,128)(2,1)} %get-tuple-element.39), channel_id=1, source_target_pairs={{8,24},{12,28},{0,8},{4,12},{24,16},{28,20},{9,25},{13,29},{1,9},{... | collective-permute-start | bytes 1646600 | tf_op jit(solution)/shard_map/ppermute | solution.py:407
  103.2 0.8 copy-start.6
  104.0 23.9 %collective-permute-start.14 = (bf16[1072,256]{1,0:T(8,128)(2,1)}, bf16[1072,256]{1,0:T(8,128)(2,1)}, u32[]{:S(2)}, u32[]{:S(2)}) collective-permute-start(bf16[1072,256]{1,0:T(8,128)(2,1)} %get-tuple-element.43), channel_id=1, source_target_pairs={{8,24},{12,28},{0,8},{4,12},{24,16},{28,20},{9,25},{13,29},{1,9},{... | collective-permute-start | bytes 1646600 | tf_op jit(solution)/shard_map/ppermute | solution.py:407
  105.3 37.1 %collective-permute-start.13 = (bf16[1072,256]{1,0:T(8,128)(2,1)}, bf16[1072,256]{1,0:T(8,128)(2,1)S(1)}, u32[]{:S(2)}, u32[]{:S(2)}) collective-permute-start(bf16[1072,256]{1,0:T(8,128)(2,1)} %copy-done.6), channel_id=1, source_target_pairs={{8,16},{12,20},{16,24},{20,28},{9,17},{13,21},{17,25},{21,29},{10,... | collective-permute-start | bytes 1646600 | tf_op jit(solution)/shard_map/ppermute | solution.py:407
  122.9 6.0 %copy-start.3 = (bf16[1,512,512]{2,1,0:T(8,128)(2,1)S(1)}, bf16[1,512,512]{2,1,0:T(8,128)(2,1)}, u32[]{:S(2)}) copy-start(bf16[1,512,512]{2,1,0:T(8,128)(2,1)} %copy-done.1) | copy-start | bytes 1572868
  126.1 11.6 %collective-permute-start.12 = (bf16[2,512,256]{2,1,0:T(8,128)(2,1)S(1)}, bf16[2,512,256]{2,1,0:T(8,128)(2,1)S(1)}, u32[]{:S(2)}, u32[]{:S(2)}) collective-permute-start(bf16[2,512,256]{2,1,0:T(8,128)(2,1)S(1)} %merge.2), channel_id=1, source_target_pairs={{0,4},{4,0},{8,12},{12,8},{16,20},{20,16},{24,28},{28,24},{1,5},{5... | collective-permute-start | bytes 1572872 | tf_op jit(solution)/shard_map/ppermute | solution.py:407
  130.6 33.1 %collective-permute-start.11 = (bf16[1024,512]{1,0:T(8,128)(2,1)S(1)}, bf16[1024,512]{1,0:T(8,128)(2,1)S(1)}, u32[]{:S(2)}, u32[]{:S(2)}) collective-permute-start(bf16[1024,512]{1,0:T(8,128)(2,1)S(1)} %get-tuple-element.62.refs_4_), channel_id=1, source_target_pairs={{0,8},{4,12},{8,0},{12,4},{16,24},{20,28},{24,16},{28,20},{1,9},{5... | collective-permute-start | bytes 3145736 | tf_op jit(solution)/shard_map/ppermute | solution.py:407
  145.5 18.2 %collective-permute-start.15 = (bf16[2,512,256]{2,1,0:T(8,128)(2,1)S(1)}, bf16[2,512,256]{2,1,0:T(8,128)(2,1)S(1)}, u32[]{:S(2)}, u32[]{:S(2)}) collective-permute-start(bf16[2,512,256]{2,1,0:T(8,128)(2,1)S(1)} %merge.3), channel_id=1, source_target_pairs={{0,4},{4,0},{8,12},{12,8},{16,20},{20,16},{24,28},{28,24},{1,5},{5... | collective-permute-start | bytes 1572872 | tf_op jit(solution)/shard_map/ppermute | solution.py:407
  169.4 2.7 %collective-permute-start.20 = (bf16[2,2,2,128,512]{4,3,2,1,0:T(8,128)(2,1)S(1)}, bf16[2,2,2,128,512]{4,3,2,1,0:T(8,128)(2,1)S(1)}, u32[]{:S(2)}, u32[]{:S(2)}) collective-permute-start(bf16[2,2,2,128,512]{4,3,2,1,0:T(8,128)(2,1)S(1)} %get-tuple-element.52), channel_id=1, source_target_pairs={{0,1},{1,0},{2,3},{3,2},{4,5},{5,4},{6,7},{7,6},{8,9},{9,8},{10,11... | collective-permute-start | bytes 3145736 | tf_op jit(solution)/shard_map/ppermute | solution.py:413
  169.5 7.0 %collective-permute-start.16 = (bf16[2,2,2,128,512]{4,3,2,1,0:T(8,128)(2,1)S(1)}, bf16[2,2,2,128,512]{4,3,2,1,0:T(8,128)(2,1)S(1)}, u32[]{:S(2)}, u32[]{:S(2)}) collective-permute-start(bf16[2,2,2,128,512]{4,3,2,1,0:T(8,128)(2,1)S(1)} %get-tuple-element.45), channel_id=1, source_target_pairs={{0,1},{1,0},{2,3},{3,2},{4,5},{5,4},{6,7},{7,6},{8,9},{9,8},{10,11... | collective-permute-start | bytes 3145736 | tf_op jit(solution)/shard_map/ppermute | solution.py:413
  172.9 10.0 %collective-permute-start.21 = (bf16[2,128,512]{2,1,0:T(8,128)(2,1)S(1)}, bf16[2,128,512]{2,1,0:T(8,128)(2,1)S(1)}, u32[]{:S(2)}, u32[]{:S(2)}) collective-permute-start(bf16[2,128,512]{2,1,0:T(8,128)(2,1)S(1)} %get-tuple-element.54), channel_id=1, source_target_pairs={{0,2},{1,3},{2,0},{3,1},{4,6},{5,7},{6,4},{7,5},{8,10},{9,11},{10,... | collective-permute-start | bytes 786440 | tf_op jit(solution)/shard_map/ppermute | solution.py:413
  174.5 9.9 %collective-permute-start.22 = (bf16[2,128,512]{2,1,0:T(8,128)(2,1)S(1)}, bf16[2,128,512]{2,1,0:T(8,128)(2,1)S(1)}, u32[]{:S(2)}, u32[]{:S(2)}) collective-permute-start(bf16[2,128,512]{2,1,0:T(8,128)(2,1)S(1)} %get-tuple-element.55), channel_id=1, source_target_pairs={{0,4},{4,0},{8,12},{12,8},{16,20},{20,16},{24,28},{28,24},{1,5},{5... | collective-permute-start | bytes 786440 | tf_op jit(solution)/shard_map/ppermute | solution.py:407
  175.1 14.3 %collective-permute-start.23 = (bf16[2,128,512]{2,1,0:T(8,128)(2,1)S(1)}, bf16[2,128,512]{2,1,0:T(8,128)(2,1)S(1)}, u32[]{:S(2)}, u32[]{:S(2)}) collective-permute-start(bf16[2,128,512]{2,1,0:T(8,128)(2,1)S(1)} %get-tuple-element.56), channel_id=1, source_target_pairs={{0,6},{1,7},{2,4},{3,5},{4,2},{5,3},{6,0},{7,1},{8,14},{9,15},{10,... | collective-permute-start | bytes 786440 | tf_op jit(solution)/shard_map/ppermute | solution.py:479
  177.3 15.3 %collective-permute-start.17 = (bf16[2,128,512]{2,1,0:T(8,128)(2,1)S(1)}, bf16[2,128,512]{2,1,0:T(8,128)(2,1)S(1)}, u32[]{:S(2)}, u32[]{:S(2)}) collective-permute-start(bf16[2,128,512]{2,1,0:T(8,128)(2,1)S(1)} %get-tuple-element.47), channel_id=1, source_target_pairs={{0,2},{1,3},{2,0},{3,1},{4,6},{5,7},{6,4},{7,5},{8,10},{9,11},{10,... | collective-permute-start | bytes 786440 | tf_op jit(solution)/shard_map/ppermute | solution.py:413
  178.9 16.1 %collective-permute-start.18 = (bf16[2,128,512]{2,1,0:T(8,128)(2,1)S(1)}, bf16[2,128,512]{2,1,0:T(8,128)(2,1)S(1)}, u32[]{:S(2)}, u32[]{:S(2)}) collective-permute-start(bf16[2,128,512]{2,1,0:T(8,128)(2,1)S(1)} %get-tuple-element.48), channel_id=1, source_target_pairs={{0,4},{4,0},{8,12},{12,8},{16,20},{20,16},{24,28},{28,24},{1,5},{5... | collective-permute-start | bytes 786440 | tf_op jit(solution)/shard_map/ppermute | solution.py:407
  182.9 16.5 %collective-permute-start.19 = (bf16[2,128,512]{2,1,0:T(8,128)(2,1)S(1)}, bf16[2,128,512]{2,1,0:T(8,128)(2,1)S(1)}, u32[]{:S(2)}, u32[]{:S(2)}) collective-permute-start(bf16[2,128,512]{2,1,0:T(8,128)(2,1)S(1)} %get-tuple-element.49), channel_id=1, source_target_pairs={{0,6},{1,7},{2,4},{3,5},{4,2},{5,3},{6,0},{7,1},{8,14},{9,15},{10,... | collective-permute-start | bytes 786440 | tf_op jit(solution)/shard_map/ppermute | solution.py:479

commit v14 on v13

--- a/solution.py
+++ b/solution.py
@@ -418,7 +418,7 @@
     def with_weight(array, part):
         return jnp.where(z == 3, array, out_weight[part * cols : (part + 1) * cols].reshape(array.shape))
 
-    down, two_down = [(2, 1), (3, 2)], [(3, 1), (0, 2), (1, 0), (2, 3)]
+    down, two_down = [(2, 1), (3, 2)], [(3, 1), (1, 0), (2, 3)]
     q_m = lanes(0, 1, x)
     q_o = swap(lanes(0, 1, 1 - x))
     qs = [seq_perm(q_m, *down), None, seq_perm(with_weight(q_m, 0), *two_down), None]
@@ -427,6 +427,8 @@
     low_o = seq_perm(kv_give, (0, 1), cross=True)
     kv_o = swap(after(kv_give, q_o, qs[0]))
     qs[1], qs[3] = seq_perm(q_o, *down), seq_perm(with_weight(q_o, 1), *two_down)
+
+    w_second = seq_perm(after(out_weight, *qs), (0, 2))
 
     struct = jax.ShapeDtypeStruct
     partial = struct((2 * cols + lse_height(cols), width), BF16)
@@ -445,7 +447,7 @@
             functools.partial(own_kernel, coef, cols), turn, [(a, c * heads) for a in [q_m, q_o] + kvs],
             [partial], heads, "own_rows", 6)
         own.append(mine)
-        turn = after(at, mine)
+        turn = after(at, mine, w_second)
 
     w_down = seq_perm(after(out_weight, *qs), (2, 0), (3, 1))
     depth = out_weight.shape[0]
@@ -460,7 +462,7 @@
 
     first_half = merged(0, own[1])
     w_far = jnp.where(
-        z >= 2, jnp.where(z == 2, ridden, low_m.reshape(out_weight.shape)), after(w_down, first_half[0], own[1]))
+        z >= 2, jnp.where(z == 2, w_second, low_m.reshape(out_weight.shape)), after(w_down, first_half[0], own[1]))
     near, far = map(list, zip(first_half, merged(1, (w_far, first_half[1]))))
     w_other = seq_perm(w_far, (0, 1), (1, 0), (2, 3), (3, 2))
 

time: 203 us -> 191 us (0.941)
  waiting for transfers between devices: 101 us -> 78.8 us
  starting transfers between devices: 40 us -> 46.3 us
    ppermute x18 -> x19, waiting for transfers between devices: 82.3 us -> 60.5 us  [seq_perm(): return lax.ppermute(array, 'seq', pairs)]
    ppermute x18 -> x19, starting transfers between devices: 33.4 us -> 39.6 us  [seq_perm(): return lax.ppermute(array, 'seq', pairs)]
    select_n x0 -> x1, other arithmetic: none -> 2.34 us  [body_eight(): jnp.where(z >= 2, jnp.where(z == 2, w_second, low_m.reshape(out_weight.sh...]
    unnamed x14 -> x22, local copies, waits for them, and re-layouts: 4.46 us -> 6.6 us
  transfers between devices with their start and end apart: 24 -> 25, of which waited for: 11 -> 11; matrix products, arithmetic and copies ran while one was open for 5% -> 6% of each run, Pallas kernels for 18% -> 18%
where the time goes in v14:
time: 191 us; the launch traced here: 189 us
  waiting for transfers between devices  78.8 us (41%)
  starting transfers between devices  46.3 us (24%)
  Pallas kernels  43.1 us (23%)
  local copies, waits for them, and re-layouts  12.4 us (6%)
  other arithmetic  8.29 us (4%)
    ppermute x19, waiting for transfers between devices, seq_perm(): return lax.ppermute(array, 'seq', pairs)  60.5 us
    ppermute x19, starting transfers between devices, seq_perm(): return lax.ppermute(array, 'seq', pairs)  39.6 us
    pallas_call x6, Pallas kernels, head_call(): pl.pallas_call(kernel, out_shape=outs, grid_spec=pltpu.PrefetchScalarGrid...  32.3 us
    pallas_call x5, Pallas kernels, whole_call(): pl.pallas_call(kernel, out_shape=outs, in_specs=[pl.BlockSpec(memory_spac...  10.7 us
    ppermute x2, waiting for transfers between devices, body_eight(): from_xy = lax.ppermute(to_xy, ('seq', 'head'), diagonal)  9.37 us
    ppermute x4, waiting for transfers between devices, head_perm(): return lax.ppermute(array, 'head', [(i, i ^ flip) for i in range(4)])  8.9 us
    unnamed x22, local copies, waits for them, and re-layouts  6.6 us
    dynamic_slice x2, local copies, waits for them, and re-layouts, lanes(): lax.dynamic_slice(source, (lo, 0, part * half), (hi - lo, cols, half))  4.63 us
  transfers between devices with their start and end apart: 25, of which 11 were waited for; matrix products, arithmetic and copies ran while one was open for 6% of the time, Pallas kernels for 18%

profile of v14, /device:TPU:16, one launch (start us, length us, event | category | flops | bytes accessed | tf_op | source)
XLA Modules:
  0.0 189.1 jit_solution(14449627571676855124)
XLA Ops:
  0.0 2.3 %dynamic-slice_bitcast_fusion.2 = (bf16[1,512,512]{2,1,0:T(8,128)(2,1)}, bf16[1,512,512]{2,1,0:T(8,128)(2,1)}) fusion(bf16[3,1,512,1024]{3,2,1,0:T(8,128)(2,1)} %param.2, s32[]{:T(128)S(6)} %select_n.78, s32[]{:T(128)S(6)} %select_n.77), kind=kLoop, calls=%fused_computation.10 | loop fusion | bytes 2097160 | tf_op jit(solution)/shard_map/dynamic_slice | solution.py:416
  2.3 2.3 %collective-permute-start = (bf16[1,512,512]{2,1,0:T(8,128)(2,1)}, bf16[1,512,512]{2,1,0:T(8,128)(2,1)}, u32[]{:S(2)}, u32[]{:S(2)}) collective-permute-start(bf16[1,512,512]{2,1,0:T(8,128)(2,1)} %get-tuple-element.60.q_m), channel_id=1, source_target_pairs={{16,8},{20,12},{24,16},{28,20},{17,9},{21,13},{25,17},{29,21},{18,... | collective-permute-start | bytes 1572872 | tf_op jit(solution)/shard_map/ppermute | solution.py:407
  6.3 2.0 %fusion.2 = bf16[1,512,512]{2,1,0:T(8,128)(2,1)} fusion(bf16[1024,512]{1,0:T(8,128)(2,1)S(1)} %copy-done, pred[]{:T(512)S(6)} %eq.16, bf16[3,1,512,1024]{3,2,1,0:T(8,128)(2,1)} %param.2, s32[]{:T(128)S(6)} %select_n.77), kind=kLoop, calls=%fused_computation.9 | loop fusion | flops 262144 | bytes 1572869 | tf_op jit(solution)/shard_map/jit(_where)/select_n | solution.py:419
  8.2 5.0 %collective-permute-start.3 = (bf16[1,512,512]{2,1,0:T(8,128)(2,1)}, bf16[1,512,512]{2,1,0:T(8,128)(2,1)}, u32[]{:S(2)}, u32[]{:S(2)}) collective-permute-start(bf16[1,512,512]{2,1,0:T(8,128)(2,1)} %fusion.2), channel_id=1, source_target_pairs={{24,8},{28,12},{8,0},{12,4},{16,24},{20,28},{25,9},{29,13},{9,1},{... | collective-permute-start | bytes 1572872 | tf_op jit(solution)/shard_map/ppermute | solution.py:407
  13.3 2.6 %broadcast_select_fusion = (bf16[2,512,512]{2,1,0:T(8,128)(2,1)}, bf16[2,512,512]{2,1,0:T(8,128)(2,1)S(1)}) fusion(bf16[2,512,512]{2,1,0:T(8,128)(2,1)S(1)} %bitcast.35, pred[]{:T(512)S(6)} %eq.17, bf16[3,1,512,1024]{3,2,1,0:T(8,128)(2,1)} %param.2, s32[]{:T(128)S(6)} %select_n.77), kind=kLoop, calls=%fused_computation.6 | loop fusion | flops 524288 | bytes 4194309 | tf_op jit(solution)/shard_map/jit(_where)/select_n | solution.py:426
  16.6 2.3 %dynamic-slice_bitcast_fusion = bf16[2,512,512]{2,1,0:T(8,128)(2,1)} fusion(bf16[3,1,512,1024]{3,2,1,0:T(8,128)(2,1)} %param.2, s32[]{:T(128)S(6)} %select_n.78), kind=kLoop, calls=%fused_computation.4 | loop fusion | bytes 2097156 | tf_op jit(solution)/shard_map/dynamic_slice | solution.py:416
  21.1 4.2 %collective-permute-start.4 = (bf16[1,512,512]{2,1,0:T(8,128)(2,1)S(1)}, bf16[1,512,512]{2,1,0:T(8,128)(2,1)S(1)}, u32[]{:S(2)}, u32[]{:S(2)}) collective-permute-start(bf16[1,512,512]{2,1,0:T(8,128)(2,1)S(1)} %bitcast_select_fusion.1), channel_id=1, source_target_pairs={{24,8},{28,12},{8,0},{12,4},{16,24},{20,28},{25,9},{29,13},{9,1},{... | collective-permute-start | bytes 1572872 | tf_op jit(solution)/shard_map/ppermute | solution.py:407
  25.3 22.3 %collective-permute-done.3.qb_m = bf16[1,512,512]{2,1,0:T(8,128)(2,1)} collective-permute-done((bf16[1,512,512]{2,1,0:T(8,128)(2,1)}, bf16[1,512,512]{2,1,0:T(8,128)(2,1)}, u32[]{:S(2)}, u32[]{:S(2)}) %collective-permute-start.3) | collective-permute-done | bytes 524320 | tf_op jit(solution)/shard_map/ppermute | solution.py:407
  47.6 1.9 %collective-permute-start.2 = (bf16[1,512,512]{2,1,0:T(8,128)(2,1)}, bf16[1,512,512]{2,1,0:T(8,128)(2,1)S(1)}, u32[]{:S(2)}, u32[]{:S(2)}) collective-permute-start(bf16[1,512,512]{2,1,0:T(8,128)(2,1)} %collective-permute-done.1.q_o), channel_id=1, source_target_pairs={{16,8},{20,12},{24,16},{28,20},{17,9},{21,13},{25,17},{29,21},{18,... | collective-permute-start | bytes 1572872 | tf_op jit(solution)/shard_map/ppermute | solution.py:407
  49.5 7.5 %collective-permute-done.4.qb_o = bf16[1,512,512]{2,1,0:T(8,128)(2,1)S(1)} collective-permute-done((bf16[1,512,512]{2,1,0:T(8,128)(2,1)S(1)}, bf16[1,512,512]{2,1,0:T(8,128)(2,1)S(1)}, u32[]{:S(2)}, u32[]{:S(2)}) %collective-permute-start.4) | collective-permute-done | bytes 524320 | tf_op jit(solution)/shard_map/ppermute | solution.py:407
  57.8 2.5 %collective-permute-done.2.qa_o = bf16[1,512,512]{2,1,0:T(8,128)(2,1)S(1)} collective-permute-done((bf16[1,512,512]{2,1,0:T(8,128)(2,1)}, bf16[1,512,512]{2,1,0:T(8,128)(2,1)S(1)}, u32[]{:S(2)}, u32[]{:S(2)}) %collective-permute-start.2) | collective-permute-done | bytes 524320 | tf_op jit(solution)/shard_map/ppermute | solution.py:407
  62.4 7.4 %collective-permute-start.7 = (bf16[1024,512]{1,0:T(8,128)(2,1)S(1)}, bf16[1024,512]{1,0:T(8,128)(2,1)}, u32[]{:S(2)}, u32[]{:S(2)}) collective-permute-start(bf16[1024,512]{1,0:T(8,128)(2,1)S(1)} %copy-done), channel_id=1, source_target_pairs={{16,0},{20,4},{24,8},{28,12},{17,1},{21,5},{25,9},{29,13},{18,2},{... | collective-permute-start | bytes 3145736 | tf_op jit(solution)/shard_map/ppermute | solution.py:407
  71.9 7.6 %upper_rows.2 = (bf16[1072,256]{1,0:T(8,128)(2,1)}, bf16[1072,256]{1,0:T(8,128)(2,1)}) custom-call(s32[4]{0:T(128)S(1)} %pad_add_fusion.at, bf16[1,512,512]{2,1,0:T(8,128)(2,1)} %collective-permute-done.qa_m, bf16[1,512,512]{2,1,0:T(8,128)(2,1)S(1)} %copy-done.9, bf16[1,512,512]{2,1,0:T(8,128)(2,1)} %collective-permute-done.3.qb_m, ...), custom_call_target="tpu_custom_call" | custom-call | flops 700000000 | bytes 1024 | tf_op jit(solution)/shard_map/upper_rows/pallas_call | solution.py:303
  80.8 4.6 %collective-permute-start.10 = (bf16[1072,256]{1,0:T(8,128)(2,1)}, bf16[1072,256]{1,0:T(8,128)(2,1)}, u32[]{:S(2)}, u32[]{:S(2)}) collective-permute-start(bf16[1072,256]{1,0:T(8,128)(2,1)} %get-tuple-element.33), channel_id=1, source_target_pairs={{8,16},{12,20},{16,24},{20,28},{9,17},{13,21},{17,25},{21,29},{10,... | collective-permute-start | bytes 1646600 | tf_op jit(solution)/shard_map/ppermute | solution.py:407
  87.5 6.9 %upper_rows.3 = (bf16[1072,256]{1,0:T(8,128)(2,1)S(1)}, bf16[1072,256]{1,0:T(8,128)(2,1)S(1)}) custom-call(s32[4]{0:T(128)S(1)} %pad_add_fusion.at, bf16[1,512,512]{2,1,0:T(8,128)(2,1)} %collective-permute-done.qa_m, bf16[1,512,512]{2,1,0:T(8,128)(2,1)S(1)} %copy-done.10, bf16[1,512,512]{2,1,0:T(8,128)(2,1)} %collective-permute-done.3.qb_m, ...), custom_call_target="tpu_custom_call" | custom-call | flops 700000000 | bytes 1024 | tf_op jit(solution)/shard_map/upper_rows/pallas_call | solution.py:303
  94.4 1.9 %collective-permute-start.14 = (bf16[1072,256]{1,0:T(8,128)(2,1)S(1)}, bf16[1072,256]{1,0:T(8,128)(2,1)S(1)}, u32[]{:S(2)}, u32[]{:S(2)}) collective-permute-start(bf16[1072,256]{1,0:T(8,128)(2,1)S(1)} %get-tuple-element.35), channel_id=1, source_target_pairs={{8,16},{12,20},{16,24},{20,28},{9,17},{13,21},{17,25},{21,29},{10,... | collective-permute-start | bytes 1646600 | tf_op jit(solution)/shard_map/ppermute | solution.py:407
  96.3 6.1 %own_rows.2.own = bf16[1072,256]{1,0:T(8,128)(2,1)S(1)} custom-call(s32[4]{0:T(128)S(1)} %pad_add_fusion.at, bf16[1,512,512]{2,1,0:T(8,128)(2,1)} %get-tuple-element.60.q_m, bf16[1,512,512]{2,1,0:T(8,128)(2,1)} %collective-permute-done.1.q_o, bf16[2,512,512]{2,1,0:T(8,128)(2,1)S(1)} %get-tuple-element.58.kv_m, ...), custom_call_target="tpu_custom_call" | custom-call | flops 600000000 | bytes 1024 | tf_op jit(solution)/shard_map/own_rows/pallas_call | solution.py:303
  103.9 6.1 %own_rows.3.own = bf16[1072,256]{1,0:T(8,128)(2,1)S(1)} custom-call(s32[4]{0:T(128)S(1)} %pad_add_fusion.at, bf16[1,512,512]{2,1,0:T(8,128)(2,1)} %get-tuple-element.60.q_m, bf16[1,512,512]{2,1,0:T(8,128)(2,1)} %collective-permute-done.1.q_o, bf16[2,512,512]{2,1,0:T(8,128)(2,1)S(1)} %get-tuple-element.58.kv_m, ...), custom_call_target="tpu_custom_call" | custom-call | flops 600000000 | bytes 1024 | tf_op jit(solution)/shard_map/own_rows/pallas_call | solution.py:303
  110.1 3.2 %merge.2 = bf16[2,512,256]{2,1,0:T(8,128)(2,1)S(1)} custom-call(s32[4]{0:T(128)S(1)} %pad_add_fusion.at, bf16[1072,256]{1,0:T(8,128)(2,1)S(1)} %own_rows.2.own, bf16[1072,256]{1,0:T(8,128)(2,1)} %collective-permute-done.10.oa, bf16[1072,256]{1,0:T(8,128)(2,1)} %collective-permute-done.11.ob), custom_call_target="tpu_custom_call" | custom-call | flops 200000000 | bytes 1024 | tf_op jit(solution)/shard_map/merge/pallas_call | solution.py:303
  113.9 2.3 %fusion.1.refs_4_ = bf16[1024,512]{1,0:T(8,128)(2,1)} fusion(bf16[1024,512]{1,0:T(8,128)(2,1)} %collective-permute-done.7, bf16[1024,512]{1,0:T(8,128)(2,1)} %collective-permute-done.5, bf16[2,512,512]{2,1,0:T(8,128)(2,1)S(1)} %collective-permute-done.6.refs_0_, pred[]{:T(512)S(6)} %eq.15, pred[]{:T(512)S(6)} %ge.3), kind=kLoop, calls=%fused_computation.3 | loop fusion | flops 1048576 | bytes 4194306 | tf_op jit(solution)/shard_map/jit(_where)/select_n | solution.py:464
  117.7 7.2 %collective-permute-done.13 = bf16[2,512,256]{2,1,0:T(8,128)(2,1)S(1)} collective-permute-done((bf16[2,512,256]{2,1,0:T(8,128)(2,1)S(1)}, bf16[2,512,256]{2,1,0:T(8,128)(2,1)S(1)}, u32[]{:S(2)}, u32[]{:S(2)}) %collective-permute-start.13) | collective-permute-done | bytes 524320 | tf_op jit(solution)/shard_map/ppermute | solution.py:407
  125.8 2.4 %merge.3 = bf16[2,512,256]{2,1,0:T(8,128)(2,1)S(1)} custom-call(s32[4]{0:T(128)S(1)} %pad_add_fusion.at, bf16[1072,256]{1,0:T(8,128)(2,1)S(1)} %own_rows.3.own, bf16[1072,256]{1,0:T(8,128)(2,1)S(1)} %collective-permute-done.14.oa, bf16[1072,256]{1,0:T(8,128)(2,1)S(1)} %collective-permute-done.15.ob), custom_call_target="tpu_custom_call" | custom-call | flops 200000000 | bytes 1024 | tf_op jit(solution)/shard_map/merge/pallas_call | solution.py:303
  131.3 18.6 %collective-permute-done.12.refs_5_ = bf16[1024,512]{1,0:T(8,128)(2,1)} collective-permute-done((bf16[1024,512]{1,0:T(8,128)(2,1)}, bf16[1024,512]{1,0:T(8,128)(2,1)}, u32[]{:S(2)}, u32[]{:S(2)}) %collective-permute-start.12) | collective-permute-done | bytes 1048608 | tf_op jit(solution)/shard_map/ppermute | solution.py:407
  149.9 3.4 %project.2 = (bf16[2,2,2,128,512]{4,3,2,1,0:T(8,128)(2,1)S(1)}, bf16[2,2,2,128,512]{4,3,2,1,0:T(8,128)(2,1)S(1)}) custom-call(s32[4]{0:T(128)S(1)} %pad_add_fusion.at, bf16[2,2,2,128,256]{4,3,2,1,0:T(8,128)(2,1)S(1)} %bitcast.36, bf16[2,2,2,128,256]{4,3,2,1,0:T(8,128)(2,1)S(1)} %bitcast.38, bf16[2,2,2,128,256]{4,3,2,1,0:T(8,128)(2,1)S(1)} %bitcast.40, ...), custom_call_target="tpu_custom_call" | custom-call | flops 400000000 | bytes 1024 | tf_op jit(solution)/shard_map/project/pallas_call | solution.py:352
  153.3 4.0 %project.3 = (bf16[2,2,2,128,512]{4,3,2,1,0:T(8,128)(2,1)S(1)}, bf16[2,2,2,128,512]{4,3,2,1,0:T(8,128)(2,1)S(1)}) custom-call(s32[4]{0:T(128)S(1)} %pad_add_fusion.at, bf16[2,2,2,128,256]{4,3,2,1,0:T(8,128)(2,1)S(1)} %bitcast.37, bf16[2,2,2,128,256]{4,3,2,1,0:T(8,128)(2,1)S(1)} %bitcast.39, bf16[2,2,2,128,256]{4,3,2,1,0:T(8,128)(2,1)S(1)} %bitcast.41, ...), custom_call_target="tpu_custom_call" | custom-call | flops 400000000 | bytes 1024 | tf_op jit(solution)/shard_map/project/pallas_call | solution.py:352
  157.9 2.1 %collective-permute-done.21.got = bf16[2,2,2,128,512]{4,3,2,1,0:T(8,128)(2,1)S(1)} collective-permute-done((bf16[2,2,2,128,512]{4,3,2,1,0:T(8,128)(2,1)S(1)}, bf16[2,2,2,128,512]{4,3,2,1,0:T(8,128)(2,1)S(1)}, u32[]{:S(2)}, u32[]{:S(2)}) %collective-permute-start.21) | collective-permute-done | bytes 1048608 | tf_op jit(solution)/shard_map/ppermute | solution.py:413
  167.3 3.5 %collective-permute-done.22.refs_5_ = bf16[2,128,512]{2,1,0:T(8,128)(2,1)S(1)} collective-permute-done((bf16[2,128,512]{2,1,0:T(8,128)(2,1)S(1)}, bf16[2,128,512]{2,1,0:T(8,128)(2,1)S(1)}, u32[]{:S(2)}, u32[]{:S(2)}) %collective-permute-start.22) | collective-permute-done | bytes 262176 | tf_op jit(solution)/shard_map/ppermute | solution.py:413
  172.3 4.9 %collective-permute-done.24.refs_7_ = bf16[2,128,512]{2,1,0:T(8,128)(2,1)S(1)} collective-permute-done((bf16[2,128,512]{2,1,0:T(8,128)(2,1)S(1)}, bf16[2,128,512]{2,1,0:T(8,128)(2,1)S(1)}, u32[]{:S(2)}, u32[]{:S(2)}) %collective-permute-start.24) | collective-permute-done | bytes 262176 | tf_op jit(solution)/shard_map/ppermute | solution.py:481
  177.2 3.3 %collective-permute-done.18.refs_1_ = bf16[2,128,512]{2,1,0:T(8,128)(2,1)S(1)} collective-permute-done((bf16[2,128,512]{2,1,0:T(8,128)(2,1)S(1)}, bf16[2,128,512]{2,1,0:T(8,128)(2,1)S(1)}, u32[]{:S(2)}, u32[]{:S(2)}) %collective-permute-start.18) | collective-permute-done | bytes 262176 | tf_op jit(solution)/shard_map/ppermute | solution.py:413
  180.5 2.4 %collective-permute-done.19.refs_2_ = bf16[2,128,512]{2,1,0:T(8,128)(2,1)S(1)} collective-permute-done((bf16[2,128,512]{2,1,0:T(8,128)(2,1)S(1)}, bf16[2,128,512]{2,1,0:T(8,128)(2,1)S(1)}, u32[]{:S(2)}, u32[]{:S(2)}) %collective-permute-start.19) | collective-permute-done | bytes 262176 | tf_op jit(solution)/shard_map/ppermute | solution.py:407
  182.9 4.4 %collective-permute-done.20.refs_3_ = bf16[2,128,512]{2,1,0:T(8,128)(2,1)S(1)} collective-permute-done((bf16[2,128,512]{2,1,0:T(8,128)(2,1)S(1)}, bf16[2,128,512]{2,1,0:T(8,128)(2,1)S(1)}, u32[]{:S(2)}, u32[]{:S(2)}) %collective-permute-start.20) | collective-permute-done | bytes 262176 | tf_op jit(solution)/shard_map/ppermute | solution.py:481
  187.4 1.7 place.1
  (62 shorter events, 29.7 us)
Async XLA Ops:
  0.0 6.3 %copy-start = (bf16[1024,512]{1,0:T(8,128)(2,1)S(1)}, bf16[1024,512]{1,0:T(8,128)(2,1)}, u32[]{:S(2)}) copy-start(bf16[1024,512]{1,0:T(8,128)(2,1)} %refs_4_.1) | copy-start | bytes 3145732
  2.3 18.2 %collective-permute-start = (bf16[1,512,512]{2,1,0:T(8,128)(2,1)}, bf16[1,512,512]{2,1,0:T(8,128)(2,1)}, u32[]{:S(2)}, u32[]{:S(2)}) collective-permute-start(bf16[1,512,512]{2,1,0:T(8,128)(2,1)} %get-tuple-element.60.q_m), channel_id=1, source_target_pairs={{16,8},{20,12},{24,16},{28,20},{17,9},{21,13},{25,17},{29,21},{18,... | collective-permute-start | bytes 1572872 | tf_op jit(solution)/shard_map/ppermute | solution.py:407
  4.7 15.8 %collective-permute-start.1 = (bf16[1,512,512]{2,1,0:T(8,128)(2,1)}, bf16[1,512,512]{2,1,0:T(8,128)(2,1)}, u32[]{:S(2)}, u32[]{:S(2)}) collective-permute-start(bf16[1,512,512]{2,1,0:T(8,128)(2,1)} %get-tuple-element.59), channel_id=1, source_target_pairs={{0,4},{4,0},{8,12},{12,8},{16,20},{20,16},{24,28},{28,24},{1,5},{5... | collective-permute-start | bytes 1572872 | tf_op jit(solution)/shard_map/ppermute | solution.py:407
  8.2 39.4 %collective-permute-start.3 = (bf16[1,512,512]{2,1,0:T(8,128)(2,1)}, bf16[1,512,512]{2,1,0:T(8,128)(2,1)}, u32[]{:S(2)}, u32[]{:S(2)}) collective-permute-start(bf16[1,512,512]{2,1,0:T(8,128)(2,1)} %fusion.2), channel_id=1, source_target_pairs={{24,8},{28,12},{8,0},{12,4},{16,24},{20,28},{25,9},{29,13},{9,1},{... | collective-permute-start | bytes 1572872 | tf_op jit(solution)/shard_map/ppermute | solution.py:407
  15.8 54.0 %collective-permute-start.6 = (bf16[2,512,512]{2,1,0:T(8,128)(2,1)}, bf16[2,512,512]{2,1,0:T(8,128)(2,1)S(1)}, u32[]{:S(2)}, u32[]{:S(2)}) collective-permute-start(bf16[2,512,512]{2,1,0:T(8,128)(2,1)} %get-tuple-element.57), channel_id=1, source_target_pairs={{0,8},{4,12},{8,24},{12,28},{1,9},{5,13},{9,25},{13,29},{2,10},{6,... | collective-permute-start | bytes 3145736 | tf_op jit(solution)/shard_map/ppermute | solution.py:407
  18.9 51.0 %collective-permute-start.9 = (bf16[2,512,512]{2,1,0:T(8,128)(2,1)}, bf16[2,512,512]{2,1,0:T(8,128)(2,1)}, u32[]{:S(2)}, u32[]{:S(2)}) collective-permute-start(bf16[2,512,512]{2,1,0:T(8,128)(2,1)} %dynamic-slice_bitcast_fusion), channel_id=1, source_target_pairs={{0,12},{4,8},{1,13},{5,9},{2,14},{6,10},{3,15},{7,11}} | collective-permute-start | bytes 3145736 | tf_op jit(solution)/shard_map/ppermute | solution.py:407
  20.5 49.3 %collective-permute-start.8 = (bf16[2,512,512]{2,1,0:T(8,128)(2,1)}, bf16[2,512,512]{2,1,0:T(8,128)(2,1)}, u32[]{:S(2)}, u32[]{:S(2)}) collective-permute-start(bf16[2,512,512]{2,1,0:T(8,128)(2,1)} %dynamic-slice_bitcast_fusion), channel_id=1, source_target_pairs={{0,4},{4,0},{8,12},{12,8},{16,20},{20,16},{24,28},{28,24},{1,5},{5... | collective-permute-start | bytes 3145736 | tf_op jit(solution)/shard_map/ppermute | solution.py:407
  21.1 35.9 %collective-permute-start.4 = (bf16[1,512,512]{2,1,0:T(8,128)(2,1)S(1)}, bf16[1,512,512]{2,1,0:T(8,128)(2,1)S(1)}, u32[]{:S(2)}, u32[]{:S(2)}) collective-permute-start(bf16[1,512,512]{2,1,0:T(8,128)(2,1)S(1)} %bitcast_select_fusion.1), channel_id=1, source_target_pairs={{24,8},{28,12},{8,0},{12,4},{16,24},{20,28},{25,9},{29,13},{9,1},{... | collective-permute-start | bytes 1572872 | tf_op jit(solution)/shard_map/ppermute | solution.py:407
  47.6 12.6 %collective-permute-start.2 = (bf16[1,512,512]{2,1,0:T(8,128)(2,1)}, bf16[1,512,512]{2,1,0:T(8,128)(2,1)S(1)}, u32[]{:S(2)}, u32[]{:S(2)}) collective-permute-start(bf16[1,512,512]{2,1,0:T(8,128)(2,1)} %collective-permute-done.1.q_o), channel_id=1, source_target_pairs={{16,8},{20,12},{24,16},{28,20},{17,9},{21,13},{25,17},{29,21},{18,... | collective-permute-start | bytes 1572872 | tf_op jit(solution)/shard_map/ppermute | solution.py:407
  61.1 41.4 %collective-permute-start.5 = (bf16[1024,512]{1,0:T(8,128)(2,1)S(1)}, bf16[1024,512]{1,0:T(8,128)(2,1)}, u32[]{:S(2)}, u32[]{:S(2)}) collective-permute-start(bf16[1024,512]{1,0:T(8,128)(2,1)S(1)} %copy-done), channel_id=1, source_target_pairs={{0,16},{4,20},{1,17},{5,21},{2,18},{6,22},{3,19},{7,23}} | collective-permute-start | bytes 3145736 | tf_op jit(solution)/shard_map/ppermute | solution.py:407
  62.4 51.5 %collective-permute-start.7 = (bf16[1024,512]{1,0:T(8,128)(2,1)S(1)}, bf16[1024,512]{1,0:T(8,128)(2,1)}, u32[]{:S(2)}, u32[]{:S(2)}) collective-permute-start(bf16[1024,512]{1,0:T(8,128)(2,1)S(1)} %copy-done), channel_id=1, source_target_pairs={{16,0},{20,4},{24,8},{28,12},{17,1},{21,5},{25,9},{29,13},{18,2},{... | collective-permute-start | bytes 3145736 | tf_op jit(solution)/shard_map/ppermute | solution.py:407
  69.9 1.0 copy-start.2
  79.5 30.6 %collective-permute-start.11 = (bf16[1072,256]{1,0:T(8,128)(2,1)}, bf16[1072,256]{1,0:T(8,128)(2,1)}, u32[]{:S(2)}, u32[]{:S(2)}) collective-permute-start(bf16[1072,256]{1,0:T(8,128)(2,1)} %get-tuple-element.39), channel_id=1, source_target_pairs={{8,24},{12,28},{0,8},{4,12},{24,16},{28,20},{9,25},{13,29},{1,9},{... | collective-permute-start | bytes 1646600 | tf_op jit(solution)/shard_map/ppermute | solution.py:407
  80.8 29.3 %collective-permute-start.10 = (bf16[1072,256]{1,0:T(8,128)(2,1)}, bf16[1072,256]{1,0:T(8,128)(2,1)}, u32[]{:S(2)}, u32[]{:S(2)}) collective-permute-start(bf16[1072,256]{1,0:T(8,128)(2,1)} %get-tuple-element.33), channel_id=1, source_target_pairs={{8,16},{12,20},{16,24},{20,28},{9,17},{13,21},{17,25},{21,29},{10,... | collective-permute-start | bytes 1646600 | tf_op jit(solution)/shard_map/ppermute | solution.py:407
  85.4 1.0 copy-start.3
  94.4 31.4 %collective-permute-start.14 = (bf16[1072,256]{1,0:T(8,128)(2,1)S(1)}, bf16[1072,256]{1,0:T(8,128)(2,1)S(1)}, u32[]{:S(2)}, u32[]{:S(2)}) collective-permute-start(bf16[1072,256]{1,0:T(8,128)(2,1)S(1)} %get-tuple-element.35), channel_id=1, source_target_pairs={{8,16},{12,20},{16,24},{20,28},{9,17},{13,21},{17,25},{21,29},{10,... | collective-permute-start | bytes 1646600 | tf_op jit(solution)/shard_map/ppermute | solution.py:407
  102.4 23.3 %collective-permute-start.15 = (bf16[1072,256]{1,0:T(8,128)(2,1)S(1)}, bf16[1072,256]{1,0:T(8,128)(2,1)S(1)}, u32[]{:S(2)}, u32[]{:S(2)}) collective-permute-start(bf16[1072,256]{1,0:T(8,128)(2,1)S(1)} %get-tuple-element.43), channel_id=1, source_target_pairs={{8,24},{12,28},{0,8},{4,12},{24,16},{28,20},{9,25},{13,29},{1,9},{... | collective-permute-start | bytes 1646600 | tf_op jit(solution)/shard_map/ppermute | solution.py:407
  113.3 11.6 %collective-permute-start.13 = (bf16[2,512,256]{2,1,0:T(8,128)(2,1)S(1)}, bf16[2,512,256]{2,1,0:T(8,128)(2,1)S(1)}, u32[]{:S(2)}, u32[]{:S(2)}) collective-permute-start(bf16[2,512,256]{2,1,0:T(8,128)(2,1)S(1)} %merge.2), channel_id=1, source_target_pairs={{0,4},{4,0},{8,12},{12,8},{16,20},{20,16},{24,28},{28,24},{1,5},{5... | collective-permute-start | bytes 1572872 | tf_op jit(solution)/shard_map/ppermute | solution.py:407
  116.2 13.8 %copy-start.4 = (bf16[1,512,512]{2,1,0:T(8,128)(2,1)S(1)}, bf16[1,512,512]{2,1,0:T(8,128)(2,1)}, u32[]{:S(2)}) copy-start(bf16[1,512,512]{2,1,0:T(8,128)(2,1)} %copy-done.1) | copy-start | bytes 1572868
  116.2 33.7 %collective-permute-start.12 = (bf16[1024,512]{1,0:T(8,128)(2,1)}, bf16[1024,512]{1,0:T(8,128)(2,1)}, u32[]{:S(2)}, u32[]{:S(2)}) collective-permute-start(bf16[1024,512]{1,0:T(8,128)(2,1)} %fusion.1.refs_4_), channel_id=1, source_target_pairs={{0,8},{4,12},{8,0},{12,4},{16,24},{20,28},{24,16},{28,20},{1,9},{5... | collective-permute-start | bytes 3145736 | tf_op jit(solution)/shard_map/ppermute | solution.py:407
  125.8 2.4 %copy-start.5 = (bf16[1072,256]{1,0:T(8,128)(2,1)}, bf16[1072,256]{1,0:T(8,128)(2,1)S(1)}, u32[]{:S(2)}) copy-start(bf16[1072,256]{1,0:T(8,128)(2,1)S(1)} %collective-permute-done.15.ob) | copy-start | bytes 1646596
  128.2 21.7 %collective-permute-start.16 = (bf16[2,512,256]{2,1,0:T(8,128)(2,1)S(1)}, bf16[2,512,256]{2,1,0:T(8,128)(2,1)}, u32[]{:S(2)}, u32[]{:S(2)}) collective-permute-start(bf16[2,512,256]{2,1,0:T(8,128)(2,1)S(1)} %merge.3), channel_id=1, source_target_pairs={{0,4},{4,0},{8,12},{12,8},{16,20},{20,16},{24,28},{28,24},{1,5},{5... | collective-permute-start | bytes 1572872 | tf_op jit(solution)/shard_map/ppermute | solution.py:407
  128.8 1.2 slice-start
  128.8 21.1 %copy-start.7 = (bf16[2,512,256]{2,1,0:T(8,128)(2,1)S(1)}, bf16[2,512,256]{2,1,0:T(8,128)(2,1)}, u32[]{:S(2)}) copy-start(bf16[2,512,256]{2,1,0:T(8,128)(2,1)} %copy-done.6) | copy-start | bytes 1572868
  157.3 2.7 %collective-permute-start.21 = (bf16[2,2,2,128,512]{4,3,2,1,0:T(8,128)(2,1)S(1)}, bf16[2,2,2,128,512]{4,3,2,1,0:T(8,128)(2,1)S(1)}, u32[]{:S(2)}, u32[]{:S(2)}) collective-permute-start(bf16[2,2,2,128,512]{4,3,2,1,0:T(8,128)(2,1)S(1)} %get-tuple-element.52), channel_id=1, source_target_pairs={{0,1},{1,0},{2,3},{3,2},{4,5},{5,4},{6,7},{7,6},{8,9},{9,8},{10,11... | collective-permute-start | bytes 3145736 | tf_op jit(solution)/shard_map/ppermute | solution.py:413
  157.4 7.0 %collective-permute-start.17 = (bf16[2,2,2,128,512]{4,3,2,1,0:T(8,128)(2,1)S(1)}, bf16[2,2,2,128,512]{4,3,2,1,0:T(8,128)(2,1)S(1)}, u32[]{:S(2)}, u32[]{:S(2)}) collective-permute-start(bf16[2,2,2,128,512]{4,3,2,1,0:T(8,128)(2,1)S(1)} %get-tuple-element.45), channel_id=1, source_target_pairs={{0,1},{1,0},{2,3},{3,2},{4,5},{5,4},{6,7},{7,6},{8,9},{9,8},{10,11... | collective-permute-start | bytes 3145736 | tf_op jit(solution)/shard_map/ppermute | solution.py:413
  160.9 10.0 %collective-permute-start.22 = (bf16[2,128,512]{2,1,0:T(8,128)(2,1)S(1)}, bf16[2,128,512]{2,1,0:T(8,128)(2,1)S(1)}, u32[]{:S(2)}, u32[]{:S(2)}) collective-permute-start(bf16[2,128,512]{2,1,0:T(8,128)(2,1)S(1)} %get-tuple-element.54), channel_id=1, source_target_pairs={{0,2},{1,3},{2,0},{3,1},{4,6},{5,7},{6,4},{7,5},{8,10},{9,11},{10,... | collective-permute-start | bytes 786440 | tf_op jit(solution)/shard_map/ppermute | solution.py:413
  162.4 9.9 %collective-permute-start.23 = (bf16[2,128,512]{2,1,0:T(8,128)(2,1)S(1)}, bf16[2,128,512]{2,1,0:T(8,128)(2,1)S(1)}, u32[]{:S(2)}, u32[]{:S(2)}) collective-permute-start(bf16[2,128,512]{2,1,0:T(8,128)(2,1)S(1)} %get-tuple-element.55), channel_id=1, source_target_pairs={{0,4},{4,0},{8,12},{12,8},{16,20},{20,16},{24,28},{28,24},{1,5},{5... | collective-permute-start | bytes 786440 | tf_op jit(solution)/shard_map/ppermute | solution.py:407
  163.0 14.3 %collective-permute-start.24 = (bf16[2,128,512]{2,1,0:T(8,128)(2,1)S(1)}, bf16[2,128,512]{2,1,0:T(8,128)(2,1)S(1)}, u32[]{:S(2)}, u32[]{:S(2)}) collective-permute-start(bf16[2,128,512]{2,1,0:T(8,128)(2,1)S(1)} %get-tuple-element.56), channel_id=1, source_target_pairs={{0,6},{1,7},{2,4},{3,5},{4,2},{5,3},{6,0},{7,1},{8,14},{9,15},{10,... | collective-permute-start | bytes 786440 | tf_op jit(solution)/shard_map/ppermute | solution.py:481
  165.2 15.3 %collective-permute-start.18 = (bf16[2,128,512]{2,1,0:T(8,128)(2,1)S(1)}, bf16[2,128,512]{2,1,0:T(8,128)(2,1)S(1)}, u32[]{:S(2)}, u32[]{:S(2)}) collective-permute-start(bf16[2,128,512]{2,1,0:T(8,128)(2,1)S(1)} %get-tuple-element.47), channel_id=1, source_target_pairs={{0,2},{1,3},{2,0},{3,1},{4,6},{5,7},{6,4},{7,5},{8,10},{9,11},{10,... | collective-permute-start | bytes 786440 | tf_op jit(solution)/shard_map/ppermute | solution.py:413
  166.8 16.1 %collective-permute-start.19 = (bf16[2,128,512]{2,1,0:T(8,128)(2,1)S(1)}, bf16[2,128,512]{2,1,0:T(8,128)(2,1)S(1)}, u32[]{:S(2)}, u32[]{:S(2)}) collective-permute-start(bf16[2,128,512]{2,1,0:T(8,128)(2,1)S(1)} %get-tuple-element.48), channel_id=1, source_target_pairs={{0,4},{4,0},{8,12},{12,8},{16,20},{20,16},{24,28},{28,24},{1,5},{5... | collective-permute-start | bytes 786440 | tf_op jit(solution)/shard_map/ppermute | solution.py:407
  170.8 16.5 %collective-permute-start.20 = (bf16[2,128,512]{2,1,0:T(8,128)(2,1)S(1)}, bf16[2,128,512]{2,1,0:T(8,128)(2,1)S(1)}, u32[]{:S(2)}, u32[]{:S(2)}) collective-permute-start(bf16[2,128,512]{2,1,0:T(8,128)(2,1)S(1)} %get-tuple-element.49), channel_id=1, source_target_pairs={{0,6},{1,7},{2,4},{3,5},{4,2},{5,3},{6,0},{7,1},{8,14},{9,15},{10,... | collective-permute-start | bytes 786440 | tf_op jit(solution)/shard_map/ppermute | solution.py:481
  (5 other events, 4.5 us)

commit v15 on v14

--- a/solution.py
+++ b/solution.py
@@ -171,117 +171,116 @@
     return evens, odds
 
 
+LSE_ROWS = 16
+
+
 def put_lse(ref, base, evens, odds):
     rows = jnp.concatenate(evens + odds, axis=0)
-    pad = (-rows.shape[0]) % 16
-    if pad:
-        rows = jnp.concatenate([rows, jnp.zeros((pad, HEAD), F32)], axis=0)
-    count = rows.shape[0]
-    for piece in range(3):
-        part = rows.astype(BF16)
-        ref[pl.ds(base + piece * count, count), :] = part
-        rows = rows - part.astype(F32)
-
-
-def get_lse(ref, base, cols):
-    blocks = cols // HEAD
-    count = -(-2 * blocks // 16) * 16
-    rows = sum(ref[pl.ds(base + piece * count, count), :].astype(F32) for piece in range(3))
+    pieces = []
+    for _ in range(3):
+        pieces.append(rows.astype(BF16).astype(F32))
+        rows = rows - pieces[-1]
+    spare = LSE_ROWS - 3 * rows.shape[0]
+    ref[pl.ds(base, LSE_ROWS), :] = jnp.concatenate(pieces + [jnp.zeros((spare, HEAD), F32)], axis=0).astype(BF16)
+
+
+def get_lse(ref, base, tokens):
+    blocks = tokens // HEAD
+    packed = ref[pl.ds(base, LSE_ROWS), :].astype(F32)
+    rows = sum(packed[i * 2 * blocks : (i + 1) * 2 * blocks] for i in range(3))
     turned = [
         jnp.transpose(jnp.broadcast_to(rows[t : t + 1], (HEAD, HEAD))) for t in range(2 * blocks)
     ]
     return jnp.concatenate(turned[:blocks], axis=0), jnp.concatenate(turned[blocks:], axis=0)
 
 
-def lse_height(cols):
-    return 3 * (-(-2 * (cols // HEAD) // 16) * 16)
+def chunk_rows(array, chunk, chunks, parts):
+    size = array.shape[0] // parts
+    share = size // chunks
+    return jnp.concatenate(
+        [array[p * size + chunk * share : p * size + (chunk + 1) * share] for p in range(parts)], axis=0)
 
 
 def stacked(refs):
     return [ref[i] for ref in refs for i in range(ref.shape[0])]
 
 
-def own_kernel(coef, cols, at, q_m, q_o, kv_m, kv_o, *refs):
-    x, z = at[0], at[1]
-    below = z == 1
-    block = 256
-    tri = lax.broadcasted_iota(jnp.int32, (block, block), 1) <= lax.broadcasted_iota(
-        jnp.int32, (block, block), 0
-    )
-    first = x == 0
-    k_e, k_o = jnp.where(first, kv_m[0], kv_o[0]), jnp.where(first, kv_o[0], kv_m[0])
-    v_e, v_o = jnp.where(first, kv_m[1], kv_o[1]), jnp.where(first, kv_o[1], kv_m[1])
-    v_e, v_o = with_ones(v_e), with_ones(v_o)
-    *low, out = refs
-    m_k, m_v, o_k, o_v = stacked(low)
-    lk_e, lk_o = jnp.where(first, m_k, o_k), jnp.where(first, o_k, m_k)
-    lv_e, lv_o = jnp.where(first, m_v, o_v), jnp.where(first, o_v, m_v)
-    lv_o1 = with_ones(lv_o)
-    q_e, q_o = jnp.where(first, q_m[0], q_o[0]), jnp.where(first, q_o[0], q_m[0])
-    evens, odds = [], []
-    for part in range(cols // block):
-        a, b = part * block, (part + 1) * block
-        mine = slice(a, b)
-        col_e = (lk_e[mine].astype(F32), lv_e[mine].astype(F32), below)
-        col_o = (lk_o[mine].astype(F32), lv_o[mine].astype(F32), below)
-
-        def causal(k, v):
-            blocks = [(k[a:b], v[a:b], tri)]
-            return blocks if part == 0 else [(k[:a], v[:a], None)] + blocks
-
-        o1, l1 = attend(q_e[mine], causal(k_e, v_e) + [(lk_o, lv_o1, below)], [col_e], coef)
-        o2, l2 = attend(q_o[mine], causal(k_o, v_o) + [(k_e, v_e, None)], [col_e, col_o], coef)
-        out[mine] = o1.astype(BF16)
-        out[cols + a : cols + b] = o2.astype(BF16)
-        e, o = lse_rows(l1, l2)
-        evens, odds = evens + e, odds + o
-    put_lse(out, 2 * cols, evens, odds)
-
-
-def upper_kernel(coef, cols, at, qa_m, qa_o, qb_m, qb_o, kv_m, kv_o, *refs):
+def own_kernel(coef, chunk, chunks, parts, at, q_m, q_o, kv_m, kv_o, *refs):
     x, z = at[0], at[1]
     below = z == 1
     first = x == 0
-    block = 256
-    k_e, k_o = jnp.where(first, kv_m[0], kv_o[0]), jnp.where(first, kv_o[0], kv_m[0])
-    v_e, v_o = jnp.where(first, kv_m[1], kv_o[1]), jnp.where(first, kv_o[1], kv_m[1])
-    v_o1 = with_ones(v_o)
+    *low, out = refs
+    cols = q_m.shape[1]
+    tokens = cols // chunks
+
+    def pair(a, b):
+        return jnp.where(first, a, b), jnp.where(first, b, a)
+
+    def mine(array):
+        return chunk_rows(array, chunk, chunks, parts)
+
+    q_e, q_o = pair(mine(q_m[0]), mine(q_o[0]))
+    k_e, k_o = pair(kv_m[0], kv_o[0])
+    v_e, v_o = pair(kv_m[1], kv_o[1])
+    v_e, v_o = with_ones(v_e), with_ones(v_o)
+    m_k, m_v, o_k, o_v = stacked(low)
+    lk_e, lk_o = pair(m_k, o_k)
+    lv_e, lv_o = pair(m_v, o_v)
+    col_e = (mine(lk_e).astype(F32), mine(lv_e).astype(F32), below)
+    col_o = (mine(lk_o).astype(F32), mine(lv_o).astype(F32), below)
+    share = tokens // parts
+    index = lax.broadcasted_iota(jnp.int32, (tokens, cols), 0)
+    index = (index // share) * (cols // parts) + chunk * share + index % share
+    tri = lax.broadcasted_iota(jnp.int32, (tokens, cols), 1) <= index
+    o1, l1 = attend(q_e, [(k_e, v_e, tri), (lk_o, with_ones(lv_o), below)], [col_e], coef)
+    o2, l2 = attend(q_o, [(k_o, v_o, tri), (k_e, v_e, None)], [col_e, col_o], coef)
+    out[:tokens] = o1.astype(BF16)
+    out[tokens : 2 * tokens] = o2.astype(BF16)
+    put_lse(out, 2 * tokens, *lse_rows(l1, l2))
+
+
+def upper_kernel(coef, chunk, chunks, parts, at, qa_m, qa_o, qb_m, qb_o, kv_m, kv_o, *refs):
+    x, z = at[0], at[1]
+    below = z == 1
+    first = x == 0
     *low, weight, out_a, out_b = refs
-    lows = stacked(low)
-    qa = jnp.where(first, qa_m[0], qa_o[0]), jnp.where(first, qa_o[0], qa_m[0])
-    qb = jnp.where(first, qb_m[0], qb_o[0]), jnp.where(first, qb_o[0], qb_m[0])
-    rows_a, rows_b = ([], []), ([], [])
-    for index in range(cols // block):
-        a, b = index * block, (index + 1) * block
-        mine = slice(a, b)
-        m_k, m_v, o_k, o_v = (part[mine].astype(F32) for part in lows)
-        ce = (k_e[mine].astype(F32), v_e[mine].astype(F32), None)
-        co = (k_o[mine].astype(F32), v_o[mine].astype(F32), None)
-        low = [(m_k, m_v, below), (o_k, o_v, below)]
-        for q, out, rows, dense, singles in (
-            (qa, out_a, rows_a, [(k_o, v_o1, None)], [ce]),
-            (qb, out_b, rows_b, [], [ce, co]),
-        ):
-            o1, l1 = attend(q[0][mine], dense, singles + low, coef)
-            o2, l2 = attend(q[1][mine], [], [ce, co] + low, coef)
-            o1, o2 = o1.astype(BF16), o2.astype(BF16)
-            other = slice(cols + a, cols + b)
-            if out is out_b:
-                o1, o2 = jnp.where(below, o1, weight[mine]), jnp.where(below, o2, weight[other])
-            out[mine] = o1
-            out[other] = o2
-            e, o = lse_rows(l1, l2)
-            rows[0].extend(e)
-            rows[1].extend(o)
-    put_lse(out_a, 2 * cols, *rows_a)
-    put_lse(out_b, 2 * cols, *rows_b)
-
-
-def merge_kernel(cols, at, own, oa, ob, out):
+    tokens = qa_m.shape[1] // chunks
+
+    def pair(a, b):
+        return jnp.where(first, a, b), jnp.where(first, b, a)
+
+    def mine(array):
+        return chunk_rows(array, chunk, chunks, parts)
+
+    k_e, k_o = pair(kv_m[0], kv_o[0])
+    v_e, v_o = pair(kv_m[1], kv_o[1])
+    m_k, m_v, o_k, o_v = (mine(part).astype(F32) for part in stacked(low))
+    lower = [(m_k, m_v, below), (o_k, o_v, below)]
+    ce = (mine(k_e).astype(F32), mine(v_e).astype(F32), None)
+    co = (mine(k_o).astype(F32), mine(v_o).astype(F32), None)
+    base = chunk * 2 * tokens
+    for q_m, q_o, out, dense, singles in (
+        (qa_m, qa_o, out_a, [(k_o, with_ones(v_o), None)], [ce]),
+        (qb_m, qb_o, out_b, [], [ce, co]),
+    ):
+        q_e, q_odd = pair(mine(q_m[0]), mine(q_o[0]))
+        o1, l1 = attend(q_e, dense, singles + lower, coef)
+        o2, l2 = attend(q_odd, [], [ce, co] + lower, coef)
+        o1, o2 = o1.astype(BF16), o2.astype(BF16)
+        if out is out_b:
+            o1 = jnp.where(below, o1, weight[base : base + tokens])
+            o2 = jnp.where(below, o2, weight[base + tokens : base + 2 * tokens])
+        out[:tokens] = o1
+        out[tokens : 2 * tokens] = o2
+        put_lse(out, 2 * tokens, *lse_rows(l1, l2))
+
+
+def merge_kernel(at, own, oa, ob, out):
     z = at[1]
-    own_l, a_l, b_l = (get_lse(ref, 2 * cols, cols) for ref in (own, oa, ob))
+    count = out.shape[1]
+    own_l, a_l, b_l = (get_lse(ref, 2 * count, count) for ref in (own, oa, ob))
     for row in range(2):
-        tokens = slice(row * cols, (row + 1) * cols)
+        tokens = slice(row * count, (row + 1) * count)
         l0 = own_l[row]
         l1 = jnp.where(z >= 2, a_l[row], NEG)
         l2 = jnp.where(z >= 3, b_l[row], NEG)
@@ -315,37 +314,38 @@
     )(at, *(a for a, _ in args))
 
 
-def project_kernel(chunks, at, *refs):
+def project_kernel(plan, at, *refs):
     x, core = at[0], at[2]
-    near, far = refs[:chunks], refs[chunks : 2 * chunks]
-    weights, send, keep = refs[2 * chunks : -2], refs[-2], refs[-1]
-    tokens = near[0].shape[3]
-    half = sum(ref.shape[4] for ref in near)
+    *arrays, send, keep = refs
     for who, out in ((1 - core, send), (core, keep)):
-
-        def rows(ref):
-            return jnp.concatenate([ref[r, y, who] for y in range(2) for r in range(2)], axis=0)
-
-        left = jnp.concatenate([rows(ref) for ref in near], axis=1)
-        right = jnp.concatenate([rows(ref) for ref in far], axis=1)
-        base = 0
-        for weight in weights:
+        for s, (near, far, weight) in enumerate(plan):
+            left, right = (
+                jnp.concatenate([arrays[i][r, y, who] for y in range(2) for r in range(2)], axis=0)
+                for i in (near, far)
+            )
+            weight = arrays[weight]
+            half = left.shape[1]
             top = weight[pl.ds(pl.multiple_of(x * half, half), half)]
             bottom = weight[pl.ds(pl.multiple_of((1 - x) * half, half), half)]
             c = jnp.dot(left, top, preferred_element_type=F32) + jnp.dot(right, bottom, preferred_element_type=F32)
-            width = weight.shape[1]
-            s, lane = base // out.shape[4], base % out.shape[4]
-            out[s, :, :, :, lane : lane + width] = c.astype(BF16).reshape(2, 2, tokens, width)
-            base += width
-
-
-def project(at, near, far, weights, out_width):
-    cols = near[0].shape[1]
-    args = [a.reshape(2, 2, 2, cols // 4, a.shape[2]) for a in near + far] + weights
-    layers = sum(w.shape[1] for w in weights) // out_width
-    out = jax.ShapeDtypeStruct((layers, 2, 2, cols // 4, out_width), BF16)
-    return whole_call(
-        functools.partial(project_kernel, len(near)), at, args, [out, out], "project", 2 * layers)
+            out[s] = c.astype(BF16).reshape(out.shape[1:])
+
+
+def project(at, attended, items):
+    arrays, plan = [], []
+
+    def place_of(array):
+        for i, other in enumerate(arrays):
+            if other is array:
+                return i
+        arrays.append(array)
+        return len(arrays) - 1
+
+    for chunk, weight in items:
+        plan.append(tuple(place_of(a) for a in attended[chunk] + (weight,)))
+    _, _, _, tokens, _ = attended[0][0].shape
+    out = jax.ShapeDtypeStruct((len(items), 2, 2, tokens, items[0][1].shape[1]), BF16)
+    return whole_call(functools.partial(project_kernel, plan), at, arrays, [out, out], "project", len(items))
 
 
 def whole_call(kernel, at, args, outs, name, us):
@@ -371,17 +371,20 @@
             out[s] = total(kept[s, yy, xx], got[s, yy, xx])
 
 
-def place_kernel(at, *refs):
+def place_kernel(plan, at, *refs):
     x, z, out = at[0], at[1], refs[-1]
     layers = [z, z + 1 - 2 * (z % 2), (z + 2) % 4, 3 - z]
+    slabs = iter(plan)
     for stay, from_y, from_x, from_xy in zip(*(refs[i:-1:4] for i in range(4))):
-        width = stay.shape[-1]
+        _, tokens, width = stay.shape
         for s in range(stay.shape[0]):
-            base = 2 * layers.pop(0)
+            chunk, layer = next(slabs)
+            rows = pl.ds(chunk * tokens, tokens)
+            base = 2 * layers[layer]
             mine = pl.ds(pl.multiple_of((base + x) * width, width), width)
             theirs = pl.ds(pl.multiple_of((base + 1 - x) * width, width), width)
-            out[:, mine] = total(stay[s], from_y[s])
-            out[:, theirs] = total(from_x[s], from_xy[s])
+            out[rows, mine] = total(stay[s], from_y[s])
+            out[rows, theirs] = total(from_x[s], from_xy[s])
 
 
 def after(value, *earlier):
@@ -392,8 +395,9 @@
     _, _, cols, features = qkv.shape
     half = features // 2
     chunks = 2
-    width = half // chunks
-    heads = width // HEAD
+    heads = half // HEAD
+    parts = lax.axis_size("head")
+    tokens = cols // chunks
     coef = HEAD ** (-0.5) * LOG2E
     me = lax.axis_index("seq")
     who = lax.axis_index("head")
@@ -415,73 +419,75 @@
     def lanes(lo, hi, part, source=local):
         return lax.dynamic_slice(source, (lo, 0, part * half), (hi - lo, cols, half))
 
-    def with_weight(array, part):
-        return jnp.where(z == 3, array, out_weight[part * cols : (part + 1) * cols].reshape(array.shape))
-
-    down, two_down = [(2, 1), (3, 2)], [(3, 1), (1, 0), (2, 3)]
+    down, two_down = [(2, 1), (3, 2)], [(3, 1)]
     q_m = lanes(0, 1, x)
     q_o = swap(lanes(0, 1, 1 - x))
-    qs = [seq_perm(q_m, *down), None, seq_perm(with_weight(q_m, 0), *two_down), None]
+    qs = [seq_perm(q_m, *down), None, seq_perm(q_m, *two_down), None]
     kv_m, kv_give = lanes(1, 3, x), lanes(1, 3, 1 - x)
-    low_m = seq_perm(jnp.where(z == 0, kv_m, out_weight.reshape(kv_m.shape)), (0, 1), (1, 3))
-    low_o = seq_perm(kv_give, (0, 1), cross=True)
+    block = out_weight.reshape(kv_m.shape)
+    low_m = seq_perm(jnp.where(z == 0, kv_m, block), (0, 1), (1, 3))
+    pairs = [(i, 2 + 1 - i) for i in range(2)] + [(2 + i, i) for i in range(2)] + [(4 + i, 6 + i) for i in range(2)]
+    low_o = lax.ppermute(jnp.where(z == 0, kv_give, block), "seq", pairs)
     kv_o = swap(after(kv_give, q_o, qs[0]))
-    qs[1], qs[3] = seq_perm(q_o, *down), seq_perm(with_weight(q_o, 1), *two_down)
-
+    qs[1], qs[3] = seq_perm(q_o, *down), seq_perm(q_o, *two_down)
     w_second = seq_perm(after(out_weight, *qs), (0, 2))
 
     struct = jax.ShapeDtypeStruct
-    partial = struct((2 * cols + lse_height(cols), width), BF16)
+    partial = struct((2 * tokens + LSE_ROWS, half), BF16)
     oa, ob, own = [], [], []
     turn = at
     kvs = [kv_m, kv_o, low_m, low_o]
     for c in range(chunks):
         a, b = head_call(
-            functools.partial(upper_kernel, coef, cols), turn, [(a, c * heads) for a in qs + kvs + [out_weight]],
+            functools.partial(upper_kernel, coef, c, chunks, parts), turn, [(a, 0) for a in qs + kvs + [out_weight]],
             [partial] * 2, heads, "upper_rows", 7)
         turn = after(at, a)
         oa.append(seq_perm(a, (1, 2), (2, 3)))
         ob.append(seq_perm(b, (1, 3), (0, 1), (3, 2)))
     for c in range(chunks):
         (mine,) = head_call(
-            functools.partial(own_kernel, coef, cols), turn, [(a, c * heads) for a in [q_m, q_o] + kvs],
+            functools.partial(own_kernel, coef, c, chunks, parts), turn, [(a, 0) for a in [q_m, q_o] + kvs],
             [partial], heads, "own_rows", 6)
         own.append(mine)
         turn = after(at, mine, w_second)
 
     w_down = seq_perm(after(out_weight, *qs), (2, 0), (3, 1))
-    depth = out_weight.shape[0]
-    ridden = jnp.concatenate([qs[2], qs[3]], axis=1).reshape(out_weight.shape)
-    w_near = jnp.where((z == 0) | (z == 3), ridden, jnp.concatenate([o[:depth] for o in ob], axis=1))
 
     def merged(c, earlier):
         (a,) = head_call(
-            functools.partial(merge_kernel, cols), after(at, earlier), [(a[c], 0) for a in (own, oa, ob)],
-            [struct((2, cols, width), BF16)], heads, "merge", 2)
-        return a, swap(a)
-
-    first_half = merged(0, own[1])
-    w_far = jnp.where(
-        z >= 2, jnp.where(z == 2, w_second, low_m.reshape(out_weight.shape)), after(w_down, first_half[0], own[1]))
-    near, far = map(list, zip(first_half, merged(1, (w_far, first_half[1]))))
+            merge_kernel, after(at, earlier), [(a[c], 0) for a in (own, oa, ob)],
+            [struct((2, tokens, half), BF16)], heads, "merge", 2)
+        shape = (2, 2, 2, tokens // 4, half)
+        return a.reshape(shape), swap(a).reshape(shape)
+
+    attended = [merged(0, own[1])]
+    ridden = jnp.where(z == 2, w_second, low_m.reshape(out_weight.shape))
+    w_far = jnp.where(z >= 2, ridden, after(w_down, attended[0][0], own[1]))
     w_other = seq_perm(w_far, (0, 1), (1, 0), (2, 3), (3, 2))
-
-    parts = []
-    turn = after(at, w_other)
-    for weights in (
-        [out_weight, w_near],
-        [w_far, w_other],
-    ):
-        send, kept = project(turn, near, far, weights, out_weight.shape[1])
+    parts_out, plan = [], []
+
+    def send_out(turn, names):
+        send, kept = project(turn, attended, [(c, weights[layer]) for c, layer in names])
         got = head_perm(send, 1)
         piece = struct(send.shape[:1] + send.shape[3:], BF16)
         stay, to_y, to_x, to_xy = whole_call(split_kernel, at, [kept, got], [piece] * 4, "split", 2)
-        turn = after(at, send)
-        diagonal = [((2 * i + j) * 4 + h, (2 * i + 1 - j) * 4 + (h ^ 2)) for i in range(4) for j in range(2) for h in range(4)]
+        diagonal = [
+            ((2 * i + j) * 4 + h, (2 * i + 1 - j) * 4 + (h ^ 2)) for i in range(4) for j in range(2) for h in range(4)
+        ]
         from_xy = lax.ppermute(to_xy, ("seq", "head"), diagonal)
-        parts += [stay, head_perm(to_y, 2), swap(to_x), from_xy]
+        parts_out.extend([stay, head_perm(to_y, 2), swap(to_x), from_xy])
+        plan.extend(names)
+        return send
+
+    weights = {0: out_weight, 2: w_far, 3: w_other}
+    attended.append(merged(1, (w_far, attended[0][1])))
+    weights[1] = jnp.where(
+        (z == 0) | (z == 3), low_o.reshape(out_weight.shape), jnp.concatenate([o[: 2 * tokens] for o in ob]))
+    send_out(after(at, attended[1][0]), [(0, 0), (0, 2), (0, 1)])
+    send_out(after(at, *parts_out), [(1, 0), (1, 1), (1, 2), (1, 3), (0, 3)])
     (out,) = whole_call(
-        place_kernel, at, parts, [struct((cols // 4, 8 * out_weight.shape[1]), BF16)], "place", 2)
+        functools.partial(place_kernel, plan), at, parts_out,
+        [struct((cols // 4, 8 * out_weight.shape[1]), BF16)], "place", 2)
     return out.reshape(cols // 4, 1, 8 * out_weight.shape[1])
 
 
@@ -491,7 +497,9 @@
     small = mesh.shape["seq"] == 8 and mesh.shape["head"] == 4
 
     def body(qkv, out_weight):
-        if small and qkv.shape[1] == 1:
+        _, rows, cols, features = qkv.shape
+        even = features == 2 * cols and out_weight.shape == (features, cols) and cols % 512 == 0
+        if small and rows == 1 and even:
             return body_eight(qkv, out_weight)
         return body_any(qkv, out_weight)
 

time: 191 us -> 188 us (0.984)
  Pallas kernels: 43.1 us -> 48.6 us
  waiting for transfers between devices: 78.8 us -> 74.5 us
  other arithmetic: 8.29 us -> 5.96 us
    ppermute x19 -> x18, waiting for transfers between devices: 60.5 us -> 38.4 us  [seq_perm(): return lax.ppermute(array, 'seq', pairs)]
    ppermute x2 -> x3, waiting for transfers between devices: 9.37 us -> 21.6 us  [the longest x2 11.6 us: send_out(): from_xy = lax.ppermute(to_xy, ('seq', 'head'), diagonal)]
    pallas_call x6, Pallas kernels: 32.3 us -> 39.5 us  [head_call(): pl.pallas_call(kernel, out_shape=outs, grid_spec=pltpu.PrefetchScalarGrid...]
    ppermute x2 -> x3, starting transfers between devices: 2.92 us -> 9.33 us  [the longest x1 5.46 us: body_eight(): low_o = lax.ppermute(jnp.where(z == 0, kv_give, block), 'seq', pairs)]
    ppermute x19 -> x18, starting transfers between devices: 39.6 us -> 33.4 us  [seq_perm(): return lax.ppermute(array, 'seq', pairs)]
    ppermute x4, waiting for transfers between devices: 8.9 us -> 14.4 us  [head_perm(): return lax.ppermute(array, 'head', [(i, i ^ flip) for i in range(4)])]
    select_n x5 -> x3, other arithmetic: 8.21 us -> 5.89 us  [the longest x1 4.14 us: body_eight(): low_o = lax.ppermute(jnp.where(z == 0, kv_give, block), 'seq', pairs)]
    dynamic_slice x2 -> x1, local copies, waits for them, and re-layouts: 4.63 us -> 2.37 us  [lanes(): lax.dynamic_slice(source, (lo, 0, part * half), (hi - lo, cols, half))]
  transfers between devices with their start and end apart: 25 -> 25, of which waited for: 11 -> 12; matrix products, arithmetic and copies ran while one was open for 6% -> 4% of each run, Pallas kernels for 18% -> 23%
where the time goes in v15:
time: 188 us; the launch traced here: 186 us
  waiting for transfers between devices  74.5 us (40%)
  Pallas kernels  48.6 us (26%)
  starting transfers between devices  45 us (24%)
  local copies, waits for them, and re-layouts  11.5 us (6%)
  other arithmetic  5.96 us (3%)
    pallas_call x6, Pallas kernels, head_call(): pl.pallas_call(kernel, out_shape=outs, grid_spec=pltpu.PrefetchScalarGrid...  39.5 us
    ppermute x18, waiting for transfers between devices, seq_perm(): return lax.ppermute(array, 'seq', pairs)  38.4 us
    ppermute x18, starting transfers between devices, seq_perm(): return lax.ppermute(array, 'seq', pairs)  33.4 us
    ppermute x4, waiting for transfers between devices, head_perm(): return lax.ppermute(array, 'head', [(i, i ^ flip) for i in range(4)])  14.4 us
    ppermute x2, waiting for transfers between devices, send_out(): from_xy = lax.ppermute(to_xy, ('seq', 'head'), diagonal)  11.6 us
    ppermute x1, waiting for transfers between devices, body_eight(): low_o = lax.ppermute(jnp.where(z == 0, kv_give, block), 'seq', pairs)  10 us
    pallas_call x5, Pallas kernels, whole_call(): pl.pallas_call(kernel, out_shape=outs, in_specs=[pl.BlockSpec(memory_spac...  9.07 us
    unnamed x18, local copies, waits for them, and re-layouts  6.95 us
  transfers between devices with their start and end apart: 25, of which 12 were waited for; matrix products, arithmetic and copies ran while one was open for 4% of the time, Pallas kernels for 23%

profile of v15, /device:TPU:16, one launch (start us, length us, event | category | flops | bytes accessed | tf_op | source)
XLA Modules:
  0.0 185.8 jit_solution(9378065369440814137)
XLA Ops:
  0.0 2.4 %dynamic-slice_bitcast_fusion.2 = (bf16[1,512,512]{2,1,0:T(8,128)(2,1)}, bf16[1,512,512]{2,1,0:T(8,128)(2,1)}) fusion(bf16[3,1,512,1024]{3,2,1,0:T(8,128)(2,1)} %param.2, s32[]{:T(128)S(6)} %select_n.65, s32[]{:T(128)S(6)} %select_n.64), kind=kLoop, calls=%fused_computation.7 | loop fusion | bytes 2097160 | tf_op jit(solution)/shard_map/dynamic_slice | solution.py:420
  2.4 2.3 %collective-permute-start = (bf16[1,512,512]{2,1,0:T(8,128)(2,1)}, bf16[1,512,512]{2,1,0:T(8,128)(2,1)}, u32[]{:S(2)}, u32[]{:S(2)}) collective-permute-start(bf16[1,512,512]{2,1,0:T(8,128)(2,1)} %get-tuple-element.64.q_m), channel_id=1, source_target_pairs={{16,8},{20,12},{24,16},{28,20},{17,9},{21,13},{25,17},{29,21},{18,... | collective-permute-start | bytes 1572872 | tf_op jit(solution)/shard_map/ppermute | solution.py:411
  4.7 1.6 collective-permute-start.1
  6.3 1.4 collective-permute-start.3
  7.7 4.1 %broadcast_select_fusion = (bf16[2,512,512]{2,1,0:T(8,128)(2,1)}, bf16[2,512,512]{2,1,0:T(8,128)(2,1)}, bf16[2,512,512]{2,1,0:T(8,128)(2,1)}, bf16[2,512,512]{2,1,0:T(8,128)(2,1)}) fusion(bf16[2,512,512]{2,1,0:T(8,128)(2,1)S(1)} %bitcast.26, pred[]{:T(512)S(6)} %eq.15, bf16[3,1,512,1024]{3,2,1,0:T(8,128)(2,1)} %param.2, s32[]{:T(128)S(6)} %select_n.65, ...), kind=kLoop, calls=%fused_computation.5 | loop fusion | flops 1048576 | bytes 7340041 | tf_op jit(solution)/shard_map/jit(_where)/select_n | solution.py:430
  12.6 5.5 %collective-permute-start.9 = (bf16[2,512,512]{2,1,0:T(8,128)(2,1)}, bf16[2,512,512]{2,1,0:T(8,128)(2,1)S(1)}, u32[]{:S(2)}, u32[]{:S(2)}) collective-permute-start(bf16[2,512,512]{2,1,0:T(8,128)(2,1)} %get-tuple-element.57), channel_id=1, source_target_pairs={{0,12},{4,8},{8,0},{12,4},{16,24},{20,28},{1,13},{5,9},{9,1},{13,5... | collective-permute-start | bytes 3145736 | tf_op jit(solution)/shard_map/ppermute | solution.py:430
  19.4 1.5 collective-permute-start.8
  20.9 1.9 %collective-permute-start.2 = (bf16[1,512,512]{2,1,0:T(8,128)(2,1)}, bf16[1,512,512]{2,1,0:T(8,128)(2,1)S(1)}, u32[]{:S(2)}, u32[]{:S(2)}) collective-permute-start(bf16[1,512,512]{2,1,0:T(8,128)(2,1)} %collective-permute-done.1.q_o), channel_id=1, source_target_pairs={{16,8},{20,12},{24,16},{28,20},{17,9},{21,13},{25,17},{29,21},{18,... | collective-permute-start | bytes 1572872 | tf_op jit(solution)/shard_map/ppermute | solution.py:411
  23.5 18.3 %collective-permute-done.2.qa_o = bf16[1,512,512]{2,1,0:T(8,128)(2,1)S(1)} collective-permute-done((bf16[1,512,512]{2,1,0:T(8,128)(2,1)}, bf16[1,512,512]{2,1,0:T(8,128)(2,1)S(1)}, u32[]{:S(2)}, u32[]{:S(2)}) %collective-permute-start.2) | collective-permute-done | bytes 524320 | tf_op jit(solution)/shard_map/ppermute | solution.py:411
  44.7 7.4 %collective-permute-start.7 = (bf16[1024,512]{1,0:T(8,128)(2,1)S(1)}, bf16[1024,512]{1,0:T(8,128)(2,1)}, u32[]{:S(2)}, u32[]{:S(2)}) collective-permute-start(bf16[1024,512]{1,0:T(8,128)(2,1)S(1)} %copy-done), channel_id=1, source_target_pairs={{16,0},{20,4},{24,8},{28,12},{17,1},{21,5},{25,9},{29,13},{18,2},{... | collective-permute-start | bytes 3145736 | tf_op jit(solution)/shard_map/ppermute | solution.py:411
  52.2 10.0 %collective-permute-done.9.refs_1_ = bf16[2,512,512]{2,1,0:T(8,128)(2,1)S(1)} collective-permute-done((bf16[2,512,512]{2,1,0:T(8,128)(2,1)}, bf16[2,512,512]{2,1,0:T(8,128)(2,1)S(1)}, u32[]{:S(2)}, u32[]{:S(2)}) %collective-permute-start.9) | collective-permute-done | bytes 1048608 | tf_op jit(solution)/shard_map/ppermute | solution.py:430
  65.5 8.1 %upper_rows.2 = (bf16[528,512]{1,0:T(8,128)(2,1)}, bf16[528,512]{1,0:T(8,128)(2,1)}) custom-call(s32[4]{0:T(128)S(1)} %pad_add_fusion.at, bf16[1,512,512]{2,1,0:T(8,128)(2,1)} %collective-permute-done.qa_m, bf16[1,512,512]{2,1,0:T(8,128)(2,1)S(1)} %copy-done.4, bf16[1,512,512]{2,1,0:T(8,128)(2,1)} %collective-permute-done.3.qb_m, ...), custom_call_target="tpu_custom_call" | custom-call | flops 700000000 | bytes 1024 | tf_op jit(solution)/shard_map/upper_rows/pallas_call | solution.py:302
  73.7 4.3 %collective-permute-start.10 = (bf16[528,512]{1,0:T(8,128)(2,1)}, bf16[528,512]{1,0:T(8,128)(2,1)}, u32[]{:S(2)}, u32[]{:S(2)}) collective-permute-start(bf16[528,512]{1,0:T(8,128)(2,1)} %get-tuple-element.33), channel_id=1, source_target_pairs={{8,16},{12,20},{16,24},{20,28},{9,17},{13,21},{17,25},{21,29},{10,... | collective-permute-start | bytes 1622024 | tf_op jit(solution)/shard_map/ppermute | solution.py:411
  79.2 8.3 %upper_rows.3 = (bf16[528,512]{1,0:T(8,128)(2,1)S(1)}, bf16[528,512]{1,0:T(8,128)(2,1)}) custom-call(s32[4]{0:T(128)S(1)} %pad_add_fusion.at, bf16[1,512,512]{2,1,0:T(8,128)(2,1)} %collective-permute-done.qa_m, bf16[1,512,512]{2,1,0:T(8,128)(2,1)S(1)} %copy-done.4, bf16[1,512,512]{2,1,0:T(8,128)(2,1)} %collective-permute-done.3.qb_m, ...), custom_call_target="tpu_custom_call" | custom-call | flops 700000000 | bytes 1024 | tf_op jit(solution)/shard_map/upper_rows/pallas_call | solution.py:302
  90.9 7.7 %own_rows.2.own = bf16[528,512]{1,0:T(8,128)(2,1)S(1)} custom-call(s32[4]{0:T(128)S(1)} %pad_add_fusion.at, bf16[1,512,512]{2,1,0:T(8,128)(2,1)} %get-tuple-element.64.q_m, bf16[1,512,512]{2,1,0:T(8,128)(2,1)} %collective-permute-done.1.q_o, bf16[2,512,512]{2,1,0:T(8,128)(2,1)S(1)} %copy-done.2, bf16[2,512,512]{2,1,0:T(8,128)(2,1)} %collective-permute-done.8.kv_o, ...), custom_call_target="tpu_custom_call" | custom-call | flops 600000000 | bytes 1024 | tf_op jit(solution)/shard_map/own_rows/pallas_call | solution.py:302
  98.6 5.3 %collective-permute-start.13 = (bf16[528,512]{1,0:T(8,128)(2,1)S(1)}, bf16[528,512]{1,0:T(8,128)(2,1)S(1)}, u32[]{:S(2)}, u32[]{:S(2)}) collective-permute-start(bf16[528,512]{1,0:T(8,128)(2,1)S(1)} %copy-done.8), channel_id=1, source_target_pairs={{8,16},{12,20},{16,24},{20,28},{9,17},{13,21},{17,25},{21,29},{10,... | collective-permute-start | bytes 1622024 | tf_op jit(solution)/shard_map/ppermute | solution.py:411
  103.9 7.7 %own_rows.3.own = bf16[528,512]{1,0:T(8,128)(2,1)S(1)} custom-call(s32[4]{0:T(128)S(1)} %pad_add_fusion.at, bf16[1,512,512]{2,1,0:T(8,128)(2,1)} %get-tuple-element.64.q_m, bf16[1,512,512]{2,1,0:T(8,128)(2,1)} %collective-permute-done.1.q_o, bf16[2,512,512]{2,1,0:T(8,128)(2,1)S(1)} %copy-done.2, bf16[2,512,512]{2,1,0:T(8,128)(2,1)} %collective-permute-done.8.kv_o, ...), custom_call_target="tpu_custom_call" | custom-call | flops 600000000 | bytes 1024 | tf_op jit(solution)/shard_map/own_rows/pallas_call | solution.py:302
  111.7 3.9 %merge.2 = bf16[2,256,512]{2,1,0:T(8,128)(2,1)S(1)} custom-call(s32[4]{0:T(128)S(1)} %pad_add_fusion.at, bf16[528,512]{1,0:T(8,128)(2,1)S(1)} %own_rows.2.own, bf16[528,512]{1,0:T(8,128)(2,1)} %collective-permute-done.10.oa, bf16[528,512]{1,0:T(8,128)(2,1)} %collective-permute-done.11.ob), custom_call_target="tpu_custom_call" | custom-call | flops 200000000 | bytes 1024 | tf_op jit(solution)/shard_map/merge/pallas_call | solution.py:302
  120.2 8.5 %collective-permute-done.12 = bf16[2,256,512]{2,1,0:T(8,128)(2,1)S(1)} collective-permute-done((bf16[2,256,512]{2,1,0:T(8,128)(2,1)S(1)}, bf16[2,256,512]{2,1,0:T(8,128)(2,1)S(1)}, u32[]{:S(2)}, u32[]{:S(2)}) %collective-permute-start.12) | collective-permute-done | bytes 524320 | tf_op jit(solution)/shard_map/ppermute | solution.py:411
  128.7 3.8 %merge.3 = bf16[2,256,512]{2,1,0:T(8,128)(2,1)S(1)} custom-call(s32[4]{0:T(128)S(1)} %pad_add_fusion.at, bf16[528,512]{1,0:T(8,128)(2,1)S(1)} %own_rows.3.own, bf16[528,512]{1,0:T(8,128)(2,1)S(1)} %collective-permute-done.13.oa, bf16[528,512]{1,0:T(8,128)(2,1)} %collective-permute-done.14.ob), custom_call_target="tpu_custom_call" | custom-call | flops 200000000 | bytes 1024 | tf_op jit(solution)/shard_map/merge/pallas_call | solution.py:302
  132.5 2.3 %project.2 = (bf16[3,2,2,64,512]{4,3,2,1,0:T(8,128)(2,1)S(1)}, bf16[3,2,2,64,512]{4,3,2,1,0:T(8,128)(2,1)S(1)}) custom-call(s32[4]{0:T(128)S(1)} %pad_add_fusion.at, bf16[2,2,2,64,512]{4,3,2,1,0:T(8,128)(2,1)S(1)} %bitcast.27, bf16[2,2,2,64,512]{4,3,2,1,0:T(8,128)(2,1)S(1)} %bitcast.29, bf16[1024,512]{1,0:T(8,128)(2,1)S(1)} %copy-done, ...), custom_call_target="tpu_custom_call" | custom-call | flops 300000000 | bytes 1024 | tf_op jit(solution)/shard_map/project/pallas_call | solution.py:352
  135.5 1.7 collective-permute-done.15.got
  137.9 1.6 collective-permute-start.16
  141.4 3.5 %collective-permute-done.16.refs_1_ = bf16[3,64,512]{2,1,0:T(8,128)(2,1)S(1)} collective-permute-done((bf16[3,64,512]{2,1,0:T(8,128)(2,1)S(1)}, bf16[3,64,512]{2,1,0:T(8,128)(2,1)S(1)}, u32[]{:S(2)}, u32[]{:S(2)}) %collective-permute-start.16) | collective-permute-done | bytes 196640 | tf_op jit(solution)/shard_map/ppermute | solution.py:417
  144.9 9.0 %collective-permute-done.17.refs_2_ = bf16[3,64,512]{2,1,0:T(8,128)(2,1)S(1)} collective-permute-done((bf16[3,64,512]{2,1,0:T(8,128)(2,1)S(1)}, bf16[3,64,512]{2,1,0:T(8,128)(2,1)S(1)}, u32[]{:S(2)}, u32[]{:S(2)}) %collective-permute-start.17) | collective-permute-done | bytes 196640 | tf_op jit(solution)/shard_map/ppermute | solution.py:411
  153.9 4.7 %collective-permute-done.18.refs_3_ = bf16[3,64,512]{2,1,0:T(8,128)(2,1)S(1)} collective-permute-done((bf16[3,64,512]{2,1,0:T(8,128)(2,1)S(1)}, bf16[3,64,512]{2,1,0:T(8,128)(2,1)S(1)}, u32[]{:S(2)}, u32[]{:S(2)}) %collective-permute-start.18) | collective-permute-done | bytes 196640 | tf_op jit(solution)/shard_map/ppermute | solution.py:477
  158.6 3.4 %project.3 = (bf16[5,2,2,64,512]{4,3,2,1,0:T(8,128)(2,1)S(1)}, bf16[5,2,2,64,512]{4,3,2,1,0:T(8,128)(2,1)S(1)}) custom-call(s32[4]{0:T(128)S(1)} %pad_add_fusion.at, bf16[2,2,2,64,512]{4,3,2,1,0:T(8,128)(2,1)S(1)} %bitcast.31, bf16[2,2,2,64,512]{4,3,2,1,0:T(8,128)(2,1)S(1)} %bitcast.32, bf16[1024,512]{1,0:T(8,128)(2,1)S(1)} %copy-done, ...), custom_call_target="tpu_custom_call" | custom-call | flops 500000000 | bytes 1024 | tf_op jit(solution)/shard_map/project/pallas_call | solution.py:352
  162.1 3.0 %collective-permute-done.21.got = bf16[5,2,2,64,512]{4,3,2,1,0:T(8,128)(2,1)S(1)} collective-permute-done((bf16[5,2,2,64,512]{4,3,2,1,0:T(8,128)(2,1)S(1)}, bf16[5,2,2,64,512]{4,3,2,1,0:T(8,128)(2,1)S(1)}, u32[]{:S(2)}, u32[]{:S(2)}) %collective-permute-start.21) | collective-permute-done | bytes 1310752 | tf_op jit(solution)/shard_map/ppermute | solution.py:417
  167.1 2.4 %collective-permute-start.24 = (bf16[5,64,512]{2,1,0:T(8,128)(2,1)S(1)}, bf16[5,64,512]{2,1,0:T(8,128)(2,1)S(1)}, u32[]{:S(2)}, u32[]{:S(2)}) collective-permute-start(bf16[5,64,512]{2,1,0:T(8,128)(2,1)S(1)} %get-tuple-element.56), channel_id=1, source_target_pairs={{0,6},{1,7},{2,4},{3,5},{4,2},{5,3},{6,0},{7,1},{8,14},{9,15},{10,... | collective-permute-start | bytes 983048 | tf_op jit(solution)/shard_map/ppermute | solution.py:477
  169.5 6.3 %collective-permute-done.22.refs_5_ = bf16[5,64,512]{2,1,0:T(8,128)(2,1)S(1)} collective-permute-done((bf16[5,64,512]{2,1,0:T(8,128)(2,1)S(1)}, bf16[5,64,512]{2,1,0:T(8,128)(2,1)S(1)}, u32[]{:S(2)}, u32[]{:S(2)}) %collective-permute-start.22) | collective-permute-done | bytes 327712 | tf_op jit(solution)/shard_map/ppermute | solution.py:417
  177.2 6.9 %collective-permute-done.24.refs_7_ = bf16[5,64,512]{2,1,0:T(8,128)(2,1)S(1)} collective-permute-done((bf16[5,64,512]{2,1,0:T(8,128)(2,1)S(1)}, bf16[5,64,512]{2,1,0:T(8,128)(2,1)S(1)}, u32[]{:S(2)}, u32[]{:S(2)}) %collective-permute-start.24) | collective-permute-done | bytes 327712 | tf_op jit(solution)/shard_map/ppermute | solution.py:477
  184.0 1.7 place.1
  (54 shorter events, 25.0 us)
Async XLA Ops:
  0.0 7.7 %copy-start = (bf16[1024,512]{1,0:T(8,128)(2,1)S(1)}, bf16[1024,512]{1,0:T(8,128)(2,1)}, u32[]{:S(2)}) copy-start(bf16[1024,512]{1,0:T(8,128)(2,1)} %refs_2_.7) | copy-start | bytes 3145732
  2.4 17.0 %collective-permute-start = (bf16[1,512,512]{2,1,0:T(8,128)(2,1)}, bf16[1,512,512]{2,1,0:T(8,128)(2,1)}, u32[]{:S(2)}, u32[]{:S(2)}) collective-permute-start(bf16[1,512,512]{2,1,0:T(8,128)(2,1)} %get-tuple-element.64.q_m), channel_id=1, source_target_pairs={{16,8},{20,12},{24,16},{28,20},{17,9},{21,13},{25,17},{29,21},{18,... | collective-permute-start | bytes 1572872 | tf_op jit(solution)/shard_map/ppermute | solution.py:411
  4.7 14.7 %collective-permute-start.1 = (bf16[1,512,512]{2,1,0:T(8,128)(2,1)}, bf16[1,512,512]{2,1,0:T(8,128)(2,1)}, u32[]{:S(2)}, u32[]{:S(2)}) collective-permute-start(bf16[1,512,512]{2,1,0:T(8,128)(2,1)} %get-tuple-element.63), channel_id=1, source_target_pairs={{0,4},{4,0},{8,12},{12,8},{16,20},{20,16},{24,28},{28,24},{1,5},{5... | collective-permute-start | bytes 1572872 | tf_op jit(solution)/shard_map/ppermute | solution.py:411
  6.3 16.5 %collective-permute-start.3 = (bf16[1,512,512]{2,1,0:T(8,128)(2,1)}, bf16[1,512,512]{2,1,0:T(8,128)(2,1)}, u32[]{:S(2)}, u32[]{:S(2)}) collective-permute-start(bf16[1,512,512]{2,1,0:T(8,128)(2,1)} %get-tuple-element.64.q_m), channel_id=1, source_target_pairs={{24,8},{28,12},{25,9},{29,13},{26,10},{30,14},{27,11},{31,15}} | collective-permute-start | bytes 1572872 | tf_op jit(solution)/shard_map/ppermute | solution.py:411
  11.9 40.3 %collective-permute-start.6 = (bf16[2,512,512]{2,1,0:T(8,128)(2,1)}, bf16[2,512,512]{2,1,0:T(8,128)(2,1)S(1)}, u32[]{:S(2)}, u32[]{:S(2)}) collective-permute-start(bf16[2,512,512]{2,1,0:T(8,128)(2,1)} %get-tuple-element.61), channel_id=1, source_target_pairs={{0,8},{4,12},{8,24},{12,28},{1,9},{5,13},{9,25},{13,29},{2,10},{6,... | collective-permute-start | bytes 3145736 | tf_op jit(solution)/shard_map/ppermute | solution.py:411
  12.6 49.6 %collective-permute-start.9 = (bf16[2,512,512]{2,1,0:T(8,128)(2,1)}, bf16[2,512,512]{2,1,0:T(8,128)(2,1)S(1)}, u32[]{:S(2)}, u32[]{:S(2)}) collective-permute-start(bf16[2,512,512]{2,1,0:T(8,128)(2,1)} %get-tuple-element.57), channel_id=1, source_target_pairs={{0,12},{4,8},{8,0},{12,4},{16,24},{20,28},{1,13},{5,9},{9,1},{13,5... | collective-permute-start | bytes 3145736 | tf_op jit(solution)/shard_map/ppermute | solution.py:430
  19.4 42.8 %collective-permute-start.8 = (bf16[2,512,512]{2,1,0:T(8,128)(2,1)}, bf16[2,512,512]{2,1,0:T(8,128)(2,1)}, u32[]{:S(2)}, u32[]{:S(2)}) collective-permute-start(bf16[2,512,512]{2,1,0:T(8,128)(2,1)} %get-tuple-element.32), channel_id=1, source_target_pairs={{0,4},{4,0},{8,12},{12,8},{16,20},{20,16},{24,28},{28,24},{1,5},{5... | collective-permute-start | bytes 3145736 | tf_op jit(solution)/shard_map/ppermute | solution.py:411
  20.9 20.9 %collective-permute-start.2 = (bf16[1,512,512]{2,1,0:T(8,128)(2,1)}, bf16[1,512,512]{2,1,0:T(8,128)(2,1)S(1)}, u32[]{:S(2)}, u32[]{:S(2)}) collective-permute-start(bf16[1,512,512]{2,1,0:T(8,128)(2,1)} %collective-permute-done.1.q_o), channel_id=1, source_target_pairs={{16,8},{20,12},{24,16},{28,20},{17,9},{21,13},{25,17},{29,21},{18,... | collective-permute-start | bytes 1572872 | tf_op jit(solution)/shard_map/ppermute | solution.py:411
  22.8 19.8 %collective-permute-start.4 = (bf16[1,512,512]{2,1,0:T(8,128)(2,1)}, bf16[1,512,512]{2,1,0:T(8,128)(2,1)S(1)}, u32[]{:S(2)}, u32[]{:S(2)}) collective-permute-start(bf16[1,512,512]{2,1,0:T(8,128)(2,1)} %collective-permute-done.1.q_o), channel_id=1, source_target_pairs={{24,8},{28,12},{25,9},{29,13},{26,10},{30,14},{27,11},{31,15}} | collective-permute-start | bytes 1572872 | tf_op jit(solution)/shard_map/ppermute | solution.py:411
  41.8 0.8 copy-start.3
  43.4 55.2 %collective-permute-start.5 = (bf16[1024,512]{1,0:T(8,128)(2,1)S(1)}, bf16[1024,512]{1,0:T(8,128)(2,1)}, u32[]{:S(2)}, u32[]{:S(2)}) collective-permute-start(bf16[1024,512]{1,0:T(8,128)(2,1)S(1)} %copy-done), channel_id=1, source_target_pairs={{0,16},{4,20},{1,17},{5,21},{2,18},{6,22},{3,19},{7,23}} | collective-permute-start | bytes 3145736 | tf_op jit(solution)/shard_map/ppermute | solution.py:411
  44.7 71.5 %collective-permute-start.7 = (bf16[1024,512]{1,0:T(8,128)(2,1)S(1)}, bf16[1024,512]{1,0:T(8,128)(2,1)}, u32[]{:S(2)}, u32[]{:S(2)}) collective-permute-start(bf16[1024,512]{1,0:T(8,128)(2,1)S(1)} %copy-done), channel_id=1, source_target_pairs={{16,0},{20,4},{24,8},{28,12},{17,1},{21,5},{25,9},{29,13},{18,2},{... | collective-permute-start | bytes 3145736 | tf_op jit(solution)/shard_map/ppermute | solution.py:411
  62.2 1.2 copy-start.1
  63.5 1.0 copy-start.4
  64.5 1.0 copy-start.6
  73.7 38.0 %collective-permute-start.10 = (bf16[528,512]{1,0:T(8,128)(2,1)}, bf16[528,512]{1,0:T(8,128)(2,1)}, u32[]{:S(2)}, u32[]{:S(2)}) collective-permute-start(bf16[528,512]{1,0:T(8,128)(2,1)} %get-tuple-element.33), channel_id=1, source_target_pairs={{8,16},{12,20},{16,24},{20,28},{9,17},{13,21},{17,25},{21,29},{10,... | collective-permute-start | bytes 1622024 | tf_op jit(solution)/shard_map/ppermute | solution.py:411
  77.9 33.7 %collective-permute-start.11 = (bf16[528,512]{1,0:T(8,128)(2,1)}, bf16[528,512]{1,0:T(8,128)(2,1)}, u32[]{:S(2)}, u32[]{:S(2)}) collective-permute-start(bf16[528,512]{1,0:T(8,128)(2,1)} %get-tuple-element.39), channel_id=1, source_target_pairs={{8,24},{12,28},{0,8},{4,12},{24,16},{28,20},{9,25},{13,29},{1,9},{... | collective-permute-start | bytes 1622024 | tf_op jit(solution)/shard_map/ppermute | solution.py:411
  88.4 30.4 %collective-permute-start.14 = (bf16[528,512]{1,0:T(8,128)(2,1)}, bf16[528,512]{1,0:T(8,128)(2,1)}, u32[]{:S(2)}, u32[]{:S(2)}) collective-permute-start(bf16[528,512]{1,0:T(8,128)(2,1)} %get-tuple-element.42), channel_id=1, source_target_pairs={{8,24},{12,28},{0,8},{4,12},{24,16},{28,20},{9,25},{13,29},{1,9},{... | collective-permute-start | bytes 1622024 | tf_op jit(solution)/shard_map/ppermute | solution.py:411
  89.7 1.2 copy-start.2
  90.9 7.7 %copy-start.8 = (bf16[528,512]{1,0:T(8,128)(2,1)S(1)}, bf16[528,512]{1,0:T(8,128)(2,1)}, u32[]{:S(2)}) copy-start(bf16[528,512]{1,0:T(8,128)(2,1)} %copy-done.7) | copy-start | bytes 1622020
  98.6 30.1 %collective-permute-start.13 = (bf16[528,512]{1,0:T(8,128)(2,1)S(1)}, bf16[528,512]{1,0:T(8,128)(2,1)S(1)}, u32[]{:S(2)}, u32[]{:S(2)}) collective-permute-start(bf16[528,512]{1,0:T(8,128)(2,1)S(1)} %copy-done.8), channel_id=1, source_target_pairs={{8,16},{12,20},{16,24},{20,28},{9,17},{13,21},{17,25},{21,29},{10,... | collective-permute-start | bytes 1622024 | tf_op jit(solution)/shard_map/ppermute | solution.py:411
  115.6 13.1 %collective-permute-start.12 = (bf16[2,256,512]{2,1,0:T(8,128)(2,1)S(1)}, bf16[2,256,512]{2,1,0:T(8,128)(2,1)S(1)}, u32[]{:S(2)}, u32[]{:S(2)}) collective-permute-start(bf16[2,256,512]{2,1,0:T(8,128)(2,1)S(1)} %merge.2), channel_id=1, source_target_pairs={{0,4},{4,0},{8,12},{12,8},{16,20},{20,16},{24,28},{28,24},{1,5},{5... | collective-permute-start | bytes 1572872 | tf_op jit(solution)/shard_map/ppermute | solution.py:411
  117.5 41.1 %collective-permute-start.20 = (bf16[1024,512]{1,0:T(8,128)(2,1)S(1)}, bf16[1024,512]{1,0:T(8,128)(2,1)S(1)}, u32[]{:S(2)}, u32[]{:S(2)}) collective-permute-start(bf16[1024,512]{1,0:T(8,128)(2,1)S(1)} %fusion.refs_3_.refs_4_), channel_id=1, source_target_pairs={{0,8},{4,12},{8,0},{12,4},{16,24},{20,28},{24,16},{28,20},{1,9},{5... | collective-permute-start | bytes 3145736 | tf_op jit(solution)/shard_map/ppermute | solution.py:411
  134.8 2.4 %collective-permute-start.15 = (bf16[3,2,2,64,512]{4,3,2,1,0:T(8,128)(2,1)S(1)}, bf16[3,2,2,64,512]{4,3,2,1,0:T(8,128)(2,1)S(1)}, u32[]{:S(2)}, u32[]{:S(2)}) collective-permute-start(bf16[3,2,2,64,512]{4,3,2,1,0:T(8,128)(2,1)S(1)} %get-tuple-element.45), channel_id=1, source_target_pairs={{0,1},{1,0},{2,3},{3,2},{4,5},{5,4},{6,7},{7,6},{8,9},{9,8},{10,11... | collective-permute-start | bytes 2359304 | tf_op jit(solution)/shard_map/ppermute | solution.py:417
  134.9 23.7 %collective-permute-start.19 = (bf16[2,256,512]{2,1,0:T(8,128)(2,1)S(1)}, bf16[2,256,512]{2,1,0:T(8,128)(2,1)S(1)}, u32[]{:S(2)}, u32[]{:S(2)}) collective-permute-start(bf16[2,256,512]{2,1,0:T(8,128)(2,1)S(1)} %merge.3), channel_id=1, source_target_pairs={{0,4},{4,0},{8,12},{12,8},{16,20},{20,16},{24,28},{28,24},{1,5},{5... | collective-permute-start | bytes 1572872 | tf_op jit(solution)/shard_map/ppermute | solution.py:411
  137.9 7.0 %collective-permute-start.16 = (bf16[3,64,512]{2,1,0:T(8,128)(2,1)S(1)}, bf16[3,64,512]{2,1,0:T(8,128)(2,1)S(1)}, u32[]{:S(2)}, u32[]{:S(2)}) collective-permute-start(bf16[3,64,512]{2,1,0:T(8,128)(2,1)S(1)} %get-tuple-element.47), channel_id=1, source_target_pairs={{0,2},{1,3},{2,0},{3,1},{4,6},{5,7},{6,4},{7,5},{8,10},{9,11},{10,... | collective-permute-start | bytes 589832 | tf_op jit(solution)/shard_map/ppermute | solution.py:417
  139.5 14.4 %collective-permute-start.17 = (bf16[3,64,512]{2,1,0:T(8,128)(2,1)S(1)}, bf16[3,64,512]{2,1,0:T(8,128)(2,1)S(1)}, u32[]{:S(2)}, u32[]{:S(2)}) collective-permute-start(bf16[3,64,512]{2,1,0:T(8,128)(2,1)S(1)} %get-tuple-element.48), channel_id=1, source_target_pairs={{0,4},{4,0},{8,12},{12,8},{16,20},{20,16},{24,28},{28,24},{1,5},{5... | collective-permute-start | bytes 589832 | tf_op jit(solution)/shard_map/ppermute | solution.py:411
  140.0 18.6 %collective-permute-start.18 = (bf16[3,64,512]{2,1,0:T(8,128)(2,1)S(1)}, bf16[3,64,512]{2,1,0:T(8,128)(2,1)S(1)}, u32[]{:S(2)}, u32[]{:S(2)}) collective-permute-start(bf16[3,64,512]{2,1,0:T(8,128)(2,1)S(1)} %get-tuple-element.49), channel_id=1, source_target_pairs={{0,6},{1,7},{2,4},{3,5},{4,2},{5,3},{6,0},{7,1},{8,14},{9,15},{10,... | collective-permute-start | bytes 589832 | tf_op jit(solution)/shard_map/ppermute | solution.py:477
  162.0 3.1 %collective-permute-start.21 = (bf16[5,2,2,64,512]{4,3,2,1,0:T(8,128)(2,1)S(1)}, bf16[5,2,2,64,512]{4,3,2,1,0:T(8,128)(2,1)S(1)}, u32[]{:S(2)}, u32[]{:S(2)}) collective-permute-start(bf16[5,2,2,64,512]{4,3,2,1,0:T(8,128)(2,1)S(1)} %get-tuple-element.52), channel_id=1, source_target_pairs={{0,1},{1,0},{2,3},{3,2},{4,5},{5,4},{6,7},{7,6},{8,9},{9,8},{10,11... | collective-permute-start | bytes 3932168 | tf_op jit(solution)/shard_map/ppermute | solution.py:417
  166.0 9.8 %collective-permute-start.22 = (bf16[5,64,512]{2,1,0:T(8,128)(2,1)S(1)}, bf16[5,64,512]{2,1,0:T(8,128)(2,1)S(1)}, u32[]{:S(2)}, u32[]{:S(2)}) collective-permute-start(bf16[5,64,512]{2,1,0:T(8,128)(2,1)S(1)} %get-tuple-element.54), channel_id=1, source_target_pairs={{0,2},{1,3},{2,0},{3,1},{4,6},{5,7},{6,4},{7,5},{8,10},{9,11},{10,... | collective-permute-start | bytes 983048 | tf_op jit(solution)/shard_map/ppermute | solution.py:417
  166.6 10.6 %collective-permute-start.23 = (bf16[5,64,512]{2,1,0:T(8,128)(2,1)S(1)}, bf16[5,64,512]{2,1,0:T(8,128)(2,1)S(1)}, u32[]{:S(2)}, u32[]{:S(2)}) collective-permute-start(bf16[5,64,512]{2,1,0:T(8,128)(2,1)S(1)} %get-tuple-element.55), channel_id=1, source_target_pairs={{0,4},{4,0},{8,12},{12,8},{16,20},{20,16},{24,28},{28,24},{1,5},{5... | collective-permute-start | bytes 983048 | tf_op jit(solution)/shard_map/ppermute | solution.py:411
  167.1 16.9 %collective-permute-start.24 = (bf16[5,64,512]{2,1,0:T(8,128)(2,1)S(1)}, bf16[5,64,512]{2,1,0:T(8,128)(2,1)S(1)}, u32[]{:S(2)}, u32[]{:S(2)}) collective-permute-start(bf16[5,64,512]{2,1,0:T(8,128)(2,1)S(1)} %get-tuple-element.56), channel_id=1, source_target_pairs={{0,6},{1,7},{2,4},{3,5},{4,2},{5,3},{6,0},{7,1},{8,14},{9,15},{10,... | collective-permute-start | bytes 983048 | tf_op jit(solution)/shard_map/ppermute | solution.py:477
  (2 other events, 1.6 us)

commit v16 on v15

--- a/solution.py
+++ b/solution.py
@@ -345,7 +345,7 @@
         plan.append(tuple(place_of(a) for a in attended[chunk] + (weight,)))
     _, _, _, tokens, _ = attended[0][0].shape
     out = jax.ShapeDtypeStruct((len(items), 2, 2, tokens, items[0][1].shape[1]), BF16)
-    return whole_call(functools.partial(project_kernel, plan), at, arrays, [out, out], "project", len(items))
+    return whole_call(functools.partial(project_kernel, plan), at, arrays, [out, out], "project", 1 * len(items))
 
 
 def whole_call(kernel, at, args, outs, name, us):
@@ -371,20 +371,38 @@
             out[s] = total(kept[s, yy, xx], got[s, yy, xx])
 
 
+def halve_kernel(at, kept, got, stay, to_y):
+    y = at[3]
+    for s in range(kept.shape[0]):
+        for r in range(2):
+            to_y[s, r] = total(kept[s, 1 - y, r], got[s, 1 - y, r])
+            stay[s, r] = total(kept[s, y, r], got[s, y, r])
+
+
+def row_kernel(at, stay, got, mine, to_x):
+    x = at[0]
+    for s in range(stay.shape[0]):
+        to_x[s] = total(stay[s, 1 - x], got[s, 1 - x])
+        mine[s] = total(stay[s, x], got[s, x])
+
+
 def place_kernel(plan, at, *refs):
     x, z, out = at[0], at[1], refs[-1]
     layers = [z, z + 1 - 2 * (z % 2), (z + 2) % 4, 3 - z]
-    slabs = iter(plan)
-    for stay, from_y, from_x, from_xy in zip(*(refs[i:-1:4] for i in range(4))):
-        _, tokens, width = stay.shape
-        for s in range(stay.shape[0]):
-            chunk, layer = next(slabs)
+    refs = iter(refs[:-1])
+    for names, hops in plan:
+        group = [next(refs) for _ in range(2 * hops)]
+        _, tokens, width = group[0].shape
+        for s, (chunk, layer) in enumerate(names):
             rows = pl.ds(chunk * tokens, tokens)
             base = 2 * layers[layer]
             mine = pl.ds(pl.multiple_of((base + x) * width, width), width)
             theirs = pl.ds(pl.multiple_of((base + 1 - x) * width, width), width)
-            out[rows, mine] = total(stay[s], from_y[s])
-            out[rows, theirs] = total(from_x[s], from_xy[s])
+            if hops == 1:
+                out[rows, mine], out[rows, theirs] = group[0][s], group[1][s]
+            else:
+                out[rows, mine] = total(group[0][s], group[1][s])
+                out[rows, theirs] = total(group[2][s], group[3][s])
 
 
 def after(value, *earlier):
@@ -466,25 +484,31 @@
     w_other = seq_perm(w_far, (0, 1), (1, 0), (2, 3), (3, 2))
     parts_out, plan = [], []
 
-    def send_out(turn, names):
+    def summed(turn, names):
         send, kept = project(turn, attended, [(c, weights[layer]) for c, layer in names])
-        got = head_perm(send, 1)
-        piece = struct(send.shape[:1] + send.shape[3:], BF16)
-        stay, to_y, to_x, to_xy = whole_call(split_kernel, at, [kept, got], [piece] * 4, "split", 2)
-        diagonal = [
-            ((2 * i + j) * 4 + h, (2 * i + 1 - j) * 4 + (h ^ 2)) for i in range(4) for j in range(2) for h in range(4)
-        ]
-        from_xy = lax.ppermute(to_xy, ("seq", "head"), diagonal)
-        parts_out.extend([stay, head_perm(to_y, 2), swap(to_x), from_xy])
-        plan.extend(names)
-        return send
-
-    weights = {0: out_weight, 2: w_far, 3: w_other}
+        return send.shape[:1] + send.shape[3:], [kept, head_perm(send, 1)]
+
     attended.append(merged(1, (w_far, attended[0][1])))
-    weights[1] = jnp.where(
+    w_near = jnp.where(
         (z == 0) | (z == 3), low_o.reshape(out_weight.shape), jnp.concatenate([o[: 2 * tokens] for o in ob]))
-    send_out(after(at, attended[1][0]), [(0, 0), (0, 2), (0, 1)])
-    send_out(after(at, *parts_out), [(1, 0), (1, 1), (1, 2), (1, 3), (0, 3)])
+    weights = {0: out_weight, 1: w_near, 2: w_far, 3: w_other}
+    names = [(0, 0), (0, 1)]
+    size, pair = summed(after(at, attended[1][0]), names)
+    both = struct(size[:1] + (2,) + size[1:], BF16)
+    stay, to_y = whole_call(halve_kernel, at, pair, [both] * 2, "halve", 2)
+    from_y = head_perm(to_y, 2)
+    mine, to_x = whole_call(row_kernel, at, [stay, from_y], [struct(size, BF16)] * 2, "rows", 1)
+    parts_out += [mine, swap(to_x)]
+    plan.append((names, 1))
+
+    names = [(1, 0), (1, 1), (1, 2), (1, 3), (0, 2), (0, 3)]
+    size, pair = summed(after(at, mine), names)
+    stay, to_y, to_x, to_xy = whole_call(split_kernel, at, pair, [struct(size, BF16)] * 4, "split", 2)
+    diagonal = [
+        ((2 * i + j) * 4 + h, (2 * i + 1 - j) * 4 + (h ^ 2)) for i in range(4) for j in range(2) for h in range(4)
+    ]
+    parts_out += [stay, head_perm(to_y, 2), swap(to_x), lax.ppermute(to_xy, ("seq", "head"), diagonal)]
+    plan.append((names, 2))
     (out,) = whole_call(
         functools.partial(place_kernel, plan), at, parts_out,
         [struct((cols // 4, 8 * out_weight.shape[1]), BF16)], "place", 2)

time: 188 us -> 186 us (0.989)
    ppermute x18, waiting for transfers between devices: 38.4 us -> 51.8 us  [seq_perm(): return lax.ppermute(array, 'seq', pairs)]
    ppermute x2 -> x1, waiting for transfers between devices: 11.6 us -> 0.01 us  [body_eight(): lax.ppermute(to_xy, ('seq', 'head'), diagonal)]
    ppermute x4, waiting for transfers between devices: 14.4 us -> 11.5 us  [head_perm(): return lax.ppermute(array, 'head', [(i, i ^ flip) for i in range(4)])]
    ppermute x2 -> x1, starting transfers between devices: 3.88 us -> 1.43 us  [body_eight(): lax.ppermute(to_xy, ('seq', 'head'), diagonal)]
    pallas_call x5 -> x6, Pallas kernels: 9.07 us -> 9.63 us  [whole_call(): pl.pallas_call(kernel, out_shape=outs, in_specs=[pl.BlockSpec(memory_spac...]
  transfers between devices with their start and end apart: 25 -> 24, of which waited for: 12 -> 10; matrix products, arithmetic and copies ran while one was open for 4% -> 4% of each run, Pallas kernels for 23% -> 23%
where the time goes in v16:
time: 186 us; the launch traced here: 184 us
  waiting for transfers between devices  73.4 us (39%)
  Pallas kernels  49.1 us (26%)
  starting transfers between devices  43.6 us (23%)
  local copies, waits for them, and re-layouts  11.5 us (6%)
  other arithmetic  5.96 us (3%)
    ppermute x18, waiting for transfers between devices, seq_perm(): return lax.ppermute(array, 'seq', pairs)  51.8 us
    pallas_call x6, Pallas kernels, head_call(): pl.pallas_call(kernel, out_shape=outs, grid_spec=pltpu.PrefetchScalarGrid...  39.5 us
    ppermute x18, starting transfers between devices, seq_perm(): return lax.ppermute(array, 'seq', pairs)  33.4 us
    ppermute x4, waiting for transfers between devices, head_perm(): return lax.ppermute(array, 'head', [(i, i ^ flip) for i in range(4)])  11.5 us
    ppermute x1, waiting for transfers between devices, body_eight(): low_o = lax.ppermute(jnp.where(z == 0, kv_give, block), 'seq', pairs)  10 us
    pallas_call x6, Pallas kernels, whole_call(): pl.pallas_call(kernel, out_shape=outs, in_specs=[pl.BlockSpec(memory_spac...  9.63 us
    unnamed x18, local copies, waits for them, and re-layouts  6.95 us
    ppermute x1, starting transfers between devices, body_eight(): low_o = lax.ppermute(jnp.where(z == 0, kv_give, block), 'seq', pairs)  5.46 us
  transfers between devices with their start and end apart: 24, of which 10 were waited for; matrix products, arithmetic and copies ran while one was open for 4% of the time, Pallas kernels for 23%

profile of v16, /device:TPU:16, one launch (start us, length us, event | category | flops | bytes accessed | tf_op | source)
XLA Modules:
  0.0 183.8 jit_solution(11972938513994531154)
XLA Ops:
  0.0 2.4 %dynamic-slice_bitcast_fusion.2 = (bf16[1,512,512]{2,1,0:T(8,128)(2,1)}, bf16[1,512,512]{2,1,0:T(8,128)(2,1)}) fusion(bf16[3,1,512,1024]{3,2,1,0:T(8,128)(2,1)} %param.2, s32[]{:T(128)S(6)} %select_n.65, s32[]{:T(128)S(6)} %select_n.64), kind=kLoop, calls=%fused_computation.7 | loop fusion | bytes 2097160 | tf_op jit(solution)/shard_map/dynamic_slice | solution.py:438
  2.4 2.3 %collective-permute-start = (bf16[1,512,512]{2,1,0:T(8,128)(2,1)}, bf16[1,512,512]{2,1,0:T(8,128)(2,1)}, u32[]{:S(2)}, u32[]{:S(2)}) collective-permute-start(bf16[1,512,512]{2,1,0:T(8,128)(2,1)} %get-tuple-element.64.q_m), channel_id=1, source_target_pairs={{16,8},{20,12},{24,16},{28,20},{17,9},{21,13},{25,17},{29,21},{18,... | collective-permute-start | bytes 1572872 | tf_op jit(solution)/shard_map/ppermute | solution.py:429
  4.7 1.6 collective-permute-start.1
  6.3 1.4 collective-permute-start.3
  7.7 4.1 %broadcast_select_fusion = (bf16[2,512,512]{2,1,0:T(8,128)(2,1)}, bf16[2,512,512]{2,1,0:T(8,128)(2,1)}, bf16[2,512,512]{2,1,0:T(8,128)(2,1)}, bf16[2,512,512]{2,1,0:T(8,128)(2,1)}) fusion(bf16[2,512,512]{2,1,0:T(8,128)(2,1)S(1)} %bitcast.26, pred[]{:T(512)S(6)} %eq.15, bf16[3,1,512,1024]{3,2,1,0:T(8,128)(2,1)} %param.2, s32[]{:T(128)S(6)} %select_n.65, ...), kind=kLoop, calls=%fused_computation.5 | loop fusion | flops 1048576 | bytes 7340041 | tf_op jit(solution)/shard_map/jit(_where)/select_n | solution.py:448
  12.6 5.5 %collective-permute-start.9 = (bf16[2,512,512]{2,1,0:T(8,128)(2,1)}, bf16[2,512,512]{2,1,0:T(8,128)(2,1)S(1)}, u32[]{:S(2)}, u32[]{:S(2)}) collective-permute-start(bf16[2,512,512]{2,1,0:T(8,128)(2,1)} %get-tuple-element.57), channel_id=1, source_target_pairs={{0,12},{4,8},{8,0},{12,4},{16,24},{20,28},{1,13},{5,9},{9,1},{13,5... | collective-permute-start | bytes 3145736 | tf_op jit(solution)/shard_map/ppermute | solution.py:448
  19.4 1.5 collective-permute-start.8
  20.9 1.9 %collective-permute-start.2 = (bf16[1,512,512]{2,1,0:T(8,128)(2,1)}, bf16[1,512,512]{2,1,0:T(8,128)(2,1)S(1)}, u32[]{:S(2)}, u32[]{:S(2)}) collective-permute-start(bf16[1,512,512]{2,1,0:T(8,128)(2,1)} %collective-permute-done.1.q_o), channel_id=1, source_target_pairs={{16,8},{20,12},{24,16},{28,20},{17,9},{21,13},{25,17},{29,21},{18,... | collective-permute-start | bytes 1572872 | tf_op jit(solution)/shard_map/ppermute | solution.py:429
  23.5 18.3 %collective-permute-done.2.qa_o = bf16[1,512,512]{2,1,0:T(8,128)(2,1)S(1)} collective-permute-done((bf16[1,512,512]{2,1,0:T(8,128)(2,1)}, bf16[1,512,512]{2,1,0:T(8,128)(2,1)S(1)}, u32[]{:S(2)}, u32[]{:S(2)}) %collective-permute-start.2) | collective-permute-done | bytes 524320 | tf_op jit(solution)/shard_map/ppermute | solution.py:429
  44.7 7.4 %collective-permute-start.7 = (bf16[1024,512]{1,0:T(8,128)(2,1)S(1)}, bf16[1024,512]{1,0:T(8,128)(2,1)}, u32[]{:S(2)}, u32[]{:S(2)}) collective-permute-start(bf16[1024,512]{1,0:T(8,128)(2,1)S(1)} %copy-done), channel_id=1, source_target_pairs={{16,0},{20,4},{24,8},{28,12},{17,1},{21,5},{25,9},{29,13},{18,2},{... | collective-permute-start | bytes 3145736 | tf_op jit(solution)/shard_map/ppermute | solution.py:429
  52.2 10.0 %collective-permute-done.9.refs_1_ = bf16[2,512,512]{2,1,0:T(8,128)(2,1)S(1)} collective-permute-done((bf16[2,512,512]{2,1,0:T(8,128)(2,1)}, bf16[2,512,512]{2,1,0:T(8,128)(2,1)S(1)}, u32[]{:S(2)}, u32[]{:S(2)}) %collective-permute-start.9) | collective-permute-done | bytes 1048608 | tf_op jit(solution)/shard_map/ppermute | solution.py:448
  65.5 8.1 %upper_rows.2 = (bf16[528,512]{1,0:T(8,128)(2,1)}, bf16[528,512]{1,0:T(8,128)(2,1)}) custom-call(s32[4]{0:T(128)S(1)} %pad_add_fusion.at, bf16[1,512,512]{2,1,0:T(8,128)(2,1)} %collective-permute-done.qa_m, bf16[1,512,512]{2,1,0:T(8,128)(2,1)S(1)} %copy-done.4, bf16[1,512,512]{2,1,0:T(8,128)(2,1)} %collective-permute-done.3.qb_m, ...), custom_call_target="tpu_custom_call" | custom-call | flops 700000000 | bytes 1024 | tf_op jit(solution)/shard_map/upper_rows/pallas_call | solution.py:302
  73.7 4.3 %collective-permute-start.10 = (bf16[528,512]{1,0:T(8,128)(2,1)}, bf16[528,512]{1,0:T(8,128)(2,1)}, u32[]{:S(2)}, u32[]{:S(2)}) collective-permute-start(bf16[528,512]{1,0:T(8,128)(2,1)} %get-tuple-element.33), channel_id=1, source_target_pairs={{8,16},{12,20},{16,24},{20,28},{9,17},{13,21},{17,25},{21,29},{10,... | collective-permute-start | bytes 1622024 | tf_op jit(solution)/shard_map/ppermute | solution.py:429
  79.2 8.3 %upper_rows.3 = (bf16[528,512]{1,0:T(8,128)(2,1)S(1)}, bf16[528,512]{1,0:T(8,128)(2,1)}) custom-call(s32[4]{0:T(128)S(1)} %pad_add_fusion.at, bf16[1,512,512]{2,1,0:T(8,128)(2,1)} %collective-permute-done.qa_m, bf16[1,512,512]{2,1,0:T(8,128)(2,1)S(1)} %copy-done.4, bf16[1,512,512]{2,1,0:T(8,128)(2,1)} %collective-permute-done.3.qb_m, ...), custom_call_target="tpu_custom_call" | custom-call | flops 700000000 | bytes 1024 | tf_op jit(solution)/shard_map/upper_rows/pallas_call | solution.py:302
  90.9 7.7 %own_rows.2.own = bf16[528,512]{1,0:T(8,128)(2,1)S(1)} custom-call(s32[4]{0:T(128)S(1)} %pad_add_fusion.at, bf16[1,512,512]{2,1,0:T(8,128)(2,1)} %get-tuple-element.64.q_m, bf16[1,512,512]{2,1,0:T(8,128)(2,1)} %collective-permute-done.1.q_o, bf16[2,512,512]{2,1,0:T(8,128)(2,1)S(1)} %copy-done.2, bf16[2,512,512]{2,1,0:T(8,128)(2,1)} %collective-permute-done.8.kv_o, ...), custom_call_target="tpu_custom_call" | custom-call | flops 600000000 | bytes 1024 | tf_op jit(solution)/shard_map/own_rows/pallas_call | solution.py:302
  98.6 5.3 %collective-permute-start.13 = (bf16[528,512]{1,0:T(8,128)(2,1)S(1)}, bf16[528,512]{1,0:T(8,128)(2,1)S(1)}, u32[]{:S(2)}, u32[]{:S(2)}) collective-permute-start(bf16[528,512]{1,0:T(8,128)(2,1)S(1)} %copy-done.8), channel_id=1, source_target_pairs={{8,16},{12,20},{16,24},{20,28},{9,17},{13,21},{17,25},{21,29},{10,... | collective-permute-start | bytes 1622024 | tf_op jit(solution)/shard_map/ppermute | solution.py:429
  103.9 7.7 %own_rows.3.own = bf16[528,512]{1,0:T(8,128)(2,1)S(1)} custom-call(s32[4]{0:T(128)S(1)} %pad_add_fusion.at, bf16[1,512,512]{2,1,0:T(8,128)(2,1)} %get-tuple-element.64.q_m, bf16[1,512,512]{2,1,0:T(8,128)(2,1)} %collective-permute-done.1.q_o, bf16[2,512,512]{2,1,0:T(8,128)(2,1)S(1)} %copy-done.2, bf16[2,512,512]{2,1,0:T(8,128)(2,1)} %collective-permute-done.8.kv_o, ...), custom_call_target="tpu_custom_call" | custom-call | flops 600000000 | bytes 1024 | tf_op jit(solution)/shard_map/own_rows/pallas_call | solution.py:302
  111.7 3.9 %merge.2 = bf16[2,256,512]{2,1,0:T(8,128)(2,1)S(1)} custom-call(s32[4]{0:T(128)S(1)} %pad_add_fusion.at, bf16[528,512]{1,0:T(8,128)(2,1)S(1)} %own_rows.2.own, bf16[528,512]{1,0:T(8,128)(2,1)} %collective-permute-done.10.oa, bf16[528,512]{1,0:T(8,128)(2,1)} %collective-permute-done.11.ob), custom_call_target="tpu_custom_call" | custom-call | flops 200000000 | bytes 1024 | tf_op jit(solution)/shard_map/merge/pallas_call | solution.py:302
  116.2 1.4 fusion.refs_4_
  120.2 8.5 %collective-permute-done.12 = bf16[2,256,512]{2,1,0:T(8,128)(2,1)S(1)} collective-permute-done((bf16[2,256,512]{2,1,0:T(8,128)(2,1)S(1)}, bf16[2,256,512]{2,1,0:T(8,128)(2,1)S(1)}, u32[]{:S(2)}, u32[]{:S(2)}) %collective-permute-start.12) | collective-permute-done | bytes 524320 | tf_op jit(solution)/shard_map/ppermute | solution.py:429
  128.7 3.8 %merge.3 = bf16[2,256,512]{2,1,0:T(8,128)(2,1)S(1)} custom-call(s32[4]{0:T(128)S(1)} %pad_add_fusion.at, bf16[528,512]{1,0:T(8,128)(2,1)S(1)} %own_rows.3.own, bf16[528,512]{1,0:T(8,128)(2,1)S(1)} %collective-permute-done.13.oa, bf16[528,512]{1,0:T(8,128)(2,1)} %collective-permute-done.14.ob), custom_call_target="tpu_custom_call" | custom-call | flops 200000000 | bytes 1024 | tf_op jit(solution)/shard_map/merge/pallas_call | solution.py:302
  132.5 1.8 project.2
  136.9 1.6 collective-permute-start.16
  138.5 6.8 %collective-permute-done.16.got = bf16[2,2,64,512]{3,2,1,0:T(8,128)(2,1)S(1)} collective-permute-done((bf16[2,2,64,512]{3,2,1,0:T(8,128)(2,1)S(1)}, bf16[2,2,64,512]{3,2,1,0:T(8,128)(2,1)S(1)}, u32[]{:S(2)}, u32[]{:S(2)}) %collective-permute-start.16) | collective-permute-done | bytes 262176 | tf_op jit(solution)/shard_map/ppermute | solution.py:435
  145.9 2.7 %collective-permute-done.18 = bf16[2,256,512]{2,1,0:T(8,128)(2,1)S(1)} collective-permute-done((bf16[2,256,512]{2,1,0:T(8,128)(2,1)S(1)}, bf16[2,256,512]{2,1,0:T(8,128)(2,1)S(1)}, u32[]{:S(2)}, u32[]{:S(2)}) %collective-permute-start.18) | collective-permute-done | bytes 524320 | tf_op jit(solution)/shard_map/ppermute | solution.py:429
  148.7 1.4 collective-permute-done.19.refs_5_
  150.1 4.0 %project.3 = (bf16[6,2,2,64,512]{4,3,2,1,0:T(8,128)(2,1)S(1)}, bf16[6,2,2,64,512]{4,3,2,1,0:T(8,128)(2,1)S(1)}) custom-call(s32[4]{0:T(128)S(1)} %pad_add_fusion.at, bf16[2,2,2,64,512]{4,3,2,1,0:T(8,128)(2,1)S(1)} %bitcast.29, bf16[2,2,2,64,512]{4,3,2,1,0:T(8,128)(2,1)S(1)} %bitcast.32, bf16[1024,512]{1,0:T(8,128)(2,1)S(1)} %copy-done, ...), custom_call_target="tpu_custom_call" | custom-call | flops 600000000 | bytes 1024 | tf_op jit(solution)/shard_map/project/pallas_call | solution.py:352
  154.1 3.4 %collective-permute-done.20.got = bf16[6,2,2,64,512]{4,3,2,1,0:T(8,128)(2,1)S(1)} collective-permute-done((bf16[6,2,2,64,512]{4,3,2,1,0:T(8,128)(2,1)S(1)}, bf16[6,2,2,64,512]{4,3,2,1,0:T(8,128)(2,1)S(1)}, u32[]{:S(2)}, u32[]{:S(2)}) %collective-permute-start.20) | collective-permute-done | bytes 1572896 | tf_op jit(solution)/shard_map/ppermute | solution.py:435
  158.4 1.6 collective-permute-start.21
  160.5 1.4 collective-permute-start.23
  162.5 19.6 %collective-permute-done.17.refs_1_ = bf16[2,64,512]{2,1,0:T(8,128)(2,1)S(1)} collective-permute-done((bf16[2,64,512]{2,1,0:T(8,128)(2,1)S(1)}, bf16[2,64,512]{2,1,0:T(8,128)(2,1)S(1)}, u32[]{:S(2)}, u32[]{:S(2)}) %collective-permute-start.17) | collective-permute-done | bytes 131104 | tf_op jit(solution)/shard_map/ppermute | solution.py:429
  182.1 1.7 place.1
  (53 shorter events, 22.2 us)
Async XLA Ops:
  0.0 7.7 %copy-start = (bf16[1024,512]{1,0:T(8,128)(2,1)S(1)}, bf16[1024,512]{1,0:T(8,128)(2,1)}, u32[]{:S(2)}) copy-start(bf16[1024,512]{1,0:T(8,128)(2,1)} %refs_2_.7) | copy-start | bytes 3145732
  2.4 17.0 %collective-permute-start = (bf16[1,512,512]{2,1,0:T(8,128)(2,1)}, bf16[1,512,512]{2,1,0:T(8,128)(2,1)}, u32[]{:S(2)}, u32[]{:S(2)}) collective-permute-start(bf16[1,512,512]{2,1,0:T(8,128)(2,1)} %get-tuple-element.64.q_m), channel_id=1, source_target_pairs={{16,8},{20,12},{24,16},{28,20},{17,9},{21,13},{25,17},{29,21},{18,... | collective-permute-start | bytes 1572872 | tf_op jit(solution)/shard_map/ppermute | solution.py:429
  4.7 14.7 %collective-permute-start.1 = (bf16[1,512,512]{2,1,0:T(8,128)(2,1)}, bf16[1,512,512]{2,1,0:T(8,128)(2,1)}, u32[]{:S(2)}, u32[]{:S(2)}) collective-permute-start(bf16[1,512,512]{2,1,0:T(8,128)(2,1)} %get-tuple-element.63), channel_id=1, source_target_pairs={{0,4},{4,0},{8,12},{12,8},{16,20},{20,16},{24,28},{28,24},{1,5},{5... | collective-permute-start | bytes 1572872 | tf_op jit(solution)/shard_map/ppermute | solution.py:429
  6.3 16.5 %collective-permute-start.3 = (bf16[1,512,512]{2,1,0:T(8,128)(2,1)}, bf16[1,512,512]{2,1,0:T(8,128)(2,1)}, u32[]{:S(2)}, u32[]{:S(2)}) collective-permute-start(bf16[1,512,512]{2,1,0:T(8,128)(2,1)} %get-tuple-element.64.q_m), channel_id=1, source_target_pairs={{24,8},{28,12},{25,9},{29,13},{26,10},{30,14},{27,11},{31,15}} | collective-permute-start | bytes 1572872 | tf_op jit(solution)/shard_map/ppermute | solution.py:429
  11.9 40.3 %collective-permute-start.6 = (bf16[2,512,512]{2,1,0:T(8,128)(2,1)}, bf16[2,512,512]{2,1,0:T(8,128)(2,1)S(1)}, u32[]{:S(2)}, u32[]{:S(2)}) collective-permute-start(bf16[2,512,512]{2,1,0:T(8,128)(2,1)} %get-tuple-element.61), channel_id=1, source_target_pairs={{0,8},{4,12},{8,24},{12,28},{1,9},{5,13},{9,25},{13,29},{2,10},{6,... | collective-permute-start | bytes 3145736 | tf_op jit(solution)/shard_map/ppermute | solution.py:429
  12.6 49.6 %collective-permute-start.9 = (bf16[2,512,512]{2,1,0:T(8,128)(2,1)}, bf16[2,512,512]{2,1,0:T(8,128)(2,1)S(1)}, u32[]{:S(2)}, u32[]{:S(2)}) collective-permute-start(bf16[2,512,512]{2,1,0:T(8,128)(2,1)} %get-tuple-element.57), channel_id=1, source_target_pairs={{0,12},{4,8},{8,0},{12,4},{16,24},{20,28},{1,13},{5,9},{9,1},{13,5... | collective-permute-start | bytes 3145736 | tf_op jit(solution)/shard_map/ppermute | solution.py:448
  19.4 42.8 %collective-permute-start.8 = (bf16[2,512,512]{2,1,0:T(8,128)(2,1)}, bf16[2,512,512]{2,1,0:T(8,128)(2,1)}, u32[]{:S(2)}, u32[]{:S(2)}) collective-permute-start(bf16[2,512,512]{2,1,0:T(8,128)(2,1)} %get-tuple-element.32), channel_id=1, source_target_pairs={{0,4},{4,0},{8,12},{12,8},{16,20},{20,16},{24,28},{28,24},{1,5},{5... | collective-permute-start | bytes 3145736 | tf_op jit(solution)/shard_map/ppermute | solution.py:429
  20.9 20.9 %collective-permute-start.2 = (bf16[1,512,512]{2,1,0:T(8,128)(2,1)}, bf16[1,512,512]{2,1,0:T(8,128)(2,1)S(1)}, u32[]{:S(2)}, u32[]{:S(2)}) collective-permute-start(bf16[1,512,512]{2,1,0:T(8,128)(2,1)} %collective-permute-done.1.q_o), channel_id=1, source_target_pairs={{16,8},{20,12},{24,16},{28,20},{17,9},{21,13},{25,17},{29,21},{18,... | collective-permute-start | bytes 1572872 | tf_op jit(solution)/shard_map/ppermute | solution.py:429
  22.8 19.8 %collective-permute-start.4 = (bf16[1,512,512]{2,1,0:T(8,128)(2,1)}, bf16[1,512,512]{2,1,0:T(8,128)(2,1)S(1)}, u32[]{:S(2)}, u32[]{:S(2)}) collective-permute-start(bf16[1,512,512]{2,1,0:T(8,128)(2,1)} %collective-permute-done.1.q_o), channel_id=1, source_target_pairs={{24,8},{28,12},{25,9},{29,13},{26,10},{30,14},{27,11},{31,15}} | collective-permute-start | bytes 1572872 | tf_op jit(solution)/shard_map/ppermute | solution.py:429
  41.8 0.8 copy-start.3
  42.6 0.8 copy-start.5
  43.4 55.2 %collective-permute-start.5 = (bf16[1024,512]{1,0:T(8,128)(2,1)S(1)}, bf16[1024,512]{1,0:T(8,128)(2,1)}, u32[]{:S(2)}, u32[]{:S(2)}) collective-permute-start(bf16[1024,512]{1,0:T(8,128)(2,1)S(1)} %copy-done), channel_id=1, source_target_pairs={{0,16},{4,20},{1,17},{5,21},{2,18},{6,22},{3,19},{7,23}} | collective-permute-start | bytes 3145736 | tf_op jit(solution)/shard_map/ppermute | solution.py:429
  44.7 71.5 %collective-permute-start.7 = (bf16[1024,512]{1,0:T(8,128)(2,1)S(1)}, bf16[1024,512]{1,0:T(8,128)(2,1)}, u32[]{:S(2)}, u32[]{:S(2)}) collective-permute-start(bf16[1024,512]{1,0:T(8,128)(2,1)S(1)} %copy-done), channel_id=1, source_target_pairs={{16,0},{20,4},{24,8},{28,12},{17,1},{21,5},{25,9},{29,13},{18,2},{... | collective-permute-start | bytes 3145736 | tf_op jit(solution)/shard_map/ppermute | solution.py:429
  62.2 1.2 copy-start.1
  63.5 1.0 copy-start.4
  64.5 1.0 copy-start.6
  73.7 38.0 %collective-permute-start.10 = (bf16[528,512]{1,0:T(8,128)(2,1)}, bf16[528,512]{1,0:T(8,128)(2,1)}, u32[]{:S(2)}, u32[]{:S(2)}) collective-permute-start(bf16[528,512]{1,0:T(8,128)(2,1)} %get-tuple-element.33), channel_id=1, source_target_pairs={{8,16},{12,20},{16,24},{20,28},{9,17},{13,21},{17,25},{21,29},{10,... | collective-permute-start | bytes 1622024 | tf_op jit(solution)/shard_map/ppermute | solution.py:429
  77.9 33.7 %collective-permute-start.11 = (bf16[528,512]{1,0:T(8,128)(2,1)}, bf16[528,512]{1,0:T(8,128)(2,1)}, u32[]{:S(2)}, u32[]{:S(2)}) collective-permute-start(bf16[528,512]{1,0:T(8,128)(2,1)} %get-tuple-element.39), channel_id=1, source_target_pairs={{8,24},{12,28},{0,8},{4,12},{24,16},{28,20},{9,25},{13,29},{1,9},{... | collective-permute-start | bytes 1622024 | tf_op jit(solution)/shard_map/ppermute | solution.py:429
  88.4 30.4 %collective-permute-start.14 = (bf16[528,512]{1,0:T(8,128)(2,1)}, bf16[528,512]{1,0:T(8,128)(2,1)}, u32[]{:S(2)}, u32[]{:S(2)}) collective-permute-start(bf16[528,512]{1,0:T(8,128)(2,1)} %get-tuple-element.42), channel_id=1, source_target_pairs={{8,24},{12,28},{0,8},{4,12},{24,16},{28,20},{9,25},{13,29},{1,9},{... | collective-permute-start | bytes 1622024 | tf_op jit(solution)/shard_map/ppermute | solution.py:429
  89.7 1.2 copy-start.2
  90.9 7.7 %copy-start.8 = (bf16[528,512]{1,0:T(8,128)(2,1)S(1)}, bf16[528,512]{1,0:T(8,128)(2,1)}, u32[]{:S(2)}) copy-start(bf16[528,512]{1,0:T(8,128)(2,1)} %copy-done.7) | copy-start | bytes 1622020
  98.6 30.1 %collective-permute-start.13 = (bf16[528,512]{1,0:T(8,128)(2,1)S(1)}, bf16[528,512]{1,0:T(8,128)(2,1)S(1)}, u32[]{:S(2)}, u32[]{:S(2)}) collective-permute-start(bf16[528,512]{1,0:T(8,128)(2,1)S(1)} %copy-done.8), channel_id=1, source_target_pairs={{8,16},{12,20},{16,24},{20,28},{9,17},{13,21},{17,25},{21,29},{10,... | collective-permute-start | bytes 1622024 | tf_op jit(solution)/shard_map/ppermute | solution.py:429
  115.6 13.1 %collective-permute-start.12 = (bf16[2,256,512]{2,1,0:T(8,128)(2,1)S(1)}, bf16[2,256,512]{2,1,0:T(8,128)(2,1)S(1)}, u32[]{:S(2)}, u32[]{:S(2)}) collective-permute-start(bf16[2,256,512]{2,1,0:T(8,128)(2,1)S(1)} %merge.2), channel_id=1, source_target_pairs={{0,4},{4,0},{8,12},{12,8},{16,20},{20,16},{24,28},{28,24},{1,5},{5... | collective-permute-start | bytes 1572872 | tf_op jit(solution)/shard_map/ppermute | solution.py:429
  117.5 32.5 %collective-permute-start.19 = (bf16[1024,512]{1,0:T(8,128)(2,1)S(1)}, bf16[1024,512]{1,0:T(8,128)(2,1)S(1)}, u32[]{:S(2)}, u32[]{:S(2)}) collective-permute-start(bf16[1024,512]{1,0:T(8,128)(2,1)S(1)} %fusion.refs_4_), channel_id=1, source_target_pairs={{0,8},{4,12},{8,0},{12,4},{16,24},{20,28},{24,16},{28,20},{1,9},{5... | collective-permute-start | bytes 3145736 | tf_op jit(solution)/shard_map/ppermute | solution.py:429
  134.3 2.0 %collective-permute-start.15 = (bf16[2,2,2,64,512]{4,3,2,1,0:T(8,128)(2,1)S(1)}, bf16[2,2,2,64,512]{4,3,2,1,0:T(8,128)(2,1)S(1)}, u32[]{:S(2)}, u32[]{:S(2)}) collective-permute-start(bf16[2,2,2,64,512]{4,3,2,1,0:T(8,128)(2,1)S(1)} %get-tuple-element.45), channel_id=1, source_target_pairs={{0,1},{1,0},{2,3},{3,2},{4,5},{5,4},{6,7},{7,6},{8,9},{9,8},{10,11... | collective-permute-start | bytes 1572872 | tf_op jit(solution)/shard_map/ppermute | solution.py:435
  134.3 14.3 %collective-permute-start.18 = (bf16[2,256,512]{2,1,0:T(8,128)(2,1)S(1)}, bf16[2,256,512]{2,1,0:T(8,128)(2,1)S(1)}, u32[]{:S(2)}, u32[]{:S(2)}) collective-permute-start(bf16[2,256,512]{2,1,0:T(8,128)(2,1)S(1)} %merge.3), channel_id=1, source_target_pairs={{0,4},{4,0},{8,12},{12,8},{16,20},{20,16},{24,28},{28,24},{1,5},{5... | collective-permute-start | bytes 1572872 | tf_op jit(solution)/shard_map/ppermute | solution.py:429
  136.9 8.4 %collective-permute-start.16 = (bf16[2,2,64,512]{3,2,1,0:T(8,128)(2,1)S(1)}, bf16[2,2,64,512]{3,2,1,0:T(8,128)(2,1)S(1)}, u32[]{:S(2)}, u32[]{:S(2)}) collective-permute-start(bf16[2,2,64,512]{3,2,1,0:T(8,128)(2,1)S(1)} %get-tuple-element.47), channel_id=1, source_target_pairs={{0,2},{1,3},{2,0},{3,1},{4,6},{5,7},{6,4},{7,5},{8,10},{9,11},{10,... | collective-permute-start | bytes 786440 | tf_op jit(solution)/shard_map/ppermute | solution.py:435
  154.0 3.5 %collective-permute-start.20 = (bf16[6,2,2,64,512]{4,3,2,1,0:T(8,128)(2,1)S(1)}, bf16[6,2,2,64,512]{4,3,2,1,0:T(8,128)(2,1)S(1)}, u32[]{:S(2)}, u32[]{:S(2)}) collective-permute-start(bf16[6,2,2,64,512]{4,3,2,1,0:T(8,128)(2,1)S(1)} %get-tuple-element.52), channel_id=1, source_target_pairs={{0,1},{1,0},{2,3},{3,2},{4,5},{5,4},{6,7},{7,6},{8,9},{9,8},{10,11... | collective-permute-start | bytes 4718600 | tf_op jit(solution)/shard_map/ppermute | solution.py:435
  158.4 23.7 %collective-permute-start.21 = (bf16[6,64,512]{2,1,0:T(8,128)(2,1)S(1)}, bf16[6,64,512]{2,1,0:T(8,128)(2,1)S(1)}, u32[]{:S(2)}, u32[]{:S(2)}) collective-permute-start(bf16[6,64,512]{2,1,0:T(8,128)(2,1)S(1)} %get-tuple-element.54), channel_id=1, source_target_pairs={{0,2},{1,3},{2,0},{3,1},{4,6},{5,7},{6,4},{7,5},{8,10},{9,11},{10,... | collective-permute-start | bytes 1179656 | tf_op jit(solution)/shard_map/ppermute | solution.py:435
  160.0 22.1 %collective-permute-start.22 = (bf16[6,64,512]{2,1,0:T(8,128)(2,1)S(1)}, bf16[6,64,512]{2,1,0:T(8,128)(2,1)S(1)}, u32[]{:S(2)}, u32[]{:S(2)}) collective-permute-start(bf16[6,64,512]{2,1,0:T(8,128)(2,1)S(1)} %get-tuple-element.55), channel_id=1, source_target_pairs={{0,4},{4,0},{8,12},{12,8},{16,20},{20,16},{24,28},{28,24},{1,5},{5... | collective-permute-start | bytes 1179656 | tf_op jit(solution)/shard_map/ppermute | solution.py:429
  160.5 21.6 %collective-permute-start.23 = (bf16[6,64,512]{2,1,0:T(8,128)(2,1)S(1)}, bf16[6,64,512]{2,1,0:T(8,128)(2,1)S(1)}, u32[]{:S(2)}, u32[]{:S(2)}) collective-permute-start(bf16[6,64,512]{2,1,0:T(8,128)(2,1)S(1)} %get-tuple-element.56), channel_id=1, source_target_pairs={{0,6},{1,7},{2,4},{3,5},{4,2},{5,3},{6,0},{7,1},{8,14},{9,15},{10,... | collective-permute-start | bytes 1179656 | tf_op jit(solution)/shard_map/ppermute | solution.py:510
  162.0 20.1 %collective-permute-start.17 = (bf16[2,64,512]{2,1,0:T(8,128)(2,1)S(1)}, bf16[2,64,512]{2,1,0:T(8,128)(2,1)S(1)}, u32[]{:S(2)}, u32[]{:S(2)}) collective-permute-start(bf16[2,64,512]{2,1,0:T(8,128)(2,1)S(1)} %get-tuple-element.49), channel_id=1, source_target_pairs={{0,4},{4,0},{8,12},{12,8},{16,20},{20,16},{24,28},{28,24},{1,5},{5... | collective-permute-start | bytes 393224 | tf_op jit(solution)/shard_map/ppermute | solution.py:429
  (1 other events, 0.8 us)

commit v17 on v16

--- a/solution.py
+++ b/solution.py
@@ -184,16 +184,6 @@
     ref[pl.ds(base, LSE_ROWS), :] = jnp.concatenate(pieces + [jnp.zeros((spare, HEAD), F32)], axis=0).astype(BF16)
 
 
-def get_lse(ref, base, tokens):
-    blocks = tokens // HEAD
-    packed = ref[pl.ds(base, LSE_ROWS), :].astype(F32)
-    rows = sum(packed[i * 2 * blocks : (i + 1) * 2 * blocks] for i in range(3))
-    turned = [
-        jnp.transpose(jnp.broadcast_to(rows[t : t + 1], (HEAD, HEAD))) for t in range(2 * blocks)
-    ]
-    return jnp.concatenate(turned[:blocks], axis=0), jnp.concatenate(turned[blocks:], axis=0)
-
-
 def chunk_rows(array, chunk, chunks, parts):
     size = array.shape[0] // parts
     share = size // chunks
@@ -275,19 +265,37 @@
         put_lse(out, 2 * tokens, *lse_rows(l1, l2))
 
 
+def lse_packed(ref, base, rows):
+    packed = ref[pl.ds(base, LSE_ROWS), :].astype(F32)
+    return sum(packed[i * rows : (i + 1) * rows] for i in range(3))
+
+
 def merge_kernel(at, own, oa, ob, out):
     z = at[1]
-    count = out.shape[1]
-    own_l, a_l, b_l = (get_lse(ref, 2 * count, count) for ref in (own, oa, ob))
+    tokens = out.shape[1]
+    blocks = tokens // HEAD
+    rows = 2 * blocks
+    l0, l1, l2 = (lse_packed(ref, 2 * tokens, rows) for ref in (own, oa, ob))
+    l1, l2 = jnp.where(z >= 2, l1, NEG), jnp.where(z >= 3, l2, NEG)
+    top = jnp.maximum(l0, jnp.maximum(l1, l2))
+    shares = [jnp.exp2(l - top) for l in (l0, l1, l2)]
+    whole = shares[0] + shares[1] + shares[2]
+    shares = jnp.concatenate([share / whole for share in shares], axis=0)
+    high = shares.astype(BF16).astype(F32)
+    spare = jnp.zeros((32 - 6 * rows, HEAD), F32)
+    pieces = jnp.concatenate([high, shares - high, spare], axis=0).astype(BF16)
+    line = lax.broadcasted_iota(jnp.int32, (32, 3 * HEAD), 0)
+    group = lax.broadcasted_iota(jnp.int32, (32, 3 * HEAD), 1) // HEAD
     for row in range(2):
-        tokens = slice(row * count, (row + 1) * count)
-        l0 = own_l[row]
-        l1 = jnp.where(z >= 2, a_l[row], NEG)
-        l2 = jnp.where(z >= 3, b_l[row], NEG)
-        top = jnp.maximum(l0, jnp.maximum(l1, l2))
-        w0, w1, w2 = jnp.exp2(l0 - top), jnp.exp2(l1 - top), jnp.exp2(l2 - top)
-        mixed = w0 * own[tokens].astype(F32) + w1 * oa[tokens].astype(F32) + w2 * ob[tokens].astype(F32)
-        out[row] = (mixed / (w0 + w1 + w2)).astype(BF16)
+        for block in range(blocks):
+            first = row * blocks + block + group * rows
+            pick = ((line == first) | (line == first + 3 * rows)).astype(BF16)
+            spread = lax.dot_general(pieces, pick, (((0,), (0,)), ((), ())), preferred_element_type=F32)
+            mine = slice(row * tokens + block * HEAD, row * tokens + (block + 1) * HEAD)
+            mixed = spread[:, :HEAD] * own[mine].astype(F32)
+            mixed = mixed + spread[:, HEAD : 2 * HEAD] * oa[mine].astype(F32)
+            mixed = mixed + spread[:, 2 * HEAD :] * ob[mine].astype(F32)
+            out[row, block * HEAD : (block + 1) * HEAD] = mixed.astype(BF16)
 
 
 def cost(us):
@@ -462,13 +470,13 @@
         turn = after(at, a)
         oa.append(seq_perm(a, (1, 2), (2, 3)))
         ob.append(seq_perm(b, (1, 3), (0, 1), (3, 2)))
-    for c in range(chunks):
+    def own_rows(c, turn):
         (mine,) = head_call(
             functools.partial(own_kernel, coef, c, chunks, parts), turn, [(a, 0) for a in [q_m, q_o] + kvs],
             [partial], heads, "own_rows", 6)
-        own.append(mine)
-        turn = after(at, mine, w_second)
-
+        return mine
+
+    own.append(own_rows(0, turn))
     w_down = seq_perm(after(out_weight, *qs), (2, 0), (3, 1))
 
     def merged(c, earlier):
@@ -478,9 +486,10 @@
         shape = (2, 2, 2, tokens // 4, half)
         return a.reshape(shape), swap(a).reshape(shape)
 
-    attended = [merged(0, own[1])]
+    attended = [merged(0, own[0])]
+    own.append(own_rows(1, after(at, attended[0][0], w_second)))
     ridden = jnp.where(z == 2, w_second, low_m.reshape(out_weight.shape))
-    w_far = jnp.where(z >= 2, ridden, after(w_down, attended[0][0], own[1]))
+    w_far = jnp.where(z >= 2, ridden, after(w_down, own[1]))
     w_other = seq_perm(w_far, (0, 1), (1, 0), (2, 3), (3, 2))
     parts_out, plan = [], []
 

time: 186 us -> 186 us (level)
  starting transfers between devices: 43.6 us -> 45.7 us
    ppermute x18, starting transfers between devices: 33.4 us -> 35.5 us  [seq_perm(): return lax.ppermute(array, 'seq', pairs)]
    unnamed x18 -> x20, local copies, waits for them, and re-layouts: 6.95 us -> 7 us
where the time goes in v17:
time: 186 us; the launch traced here: 184 us
  waiting for transfers between devices  71.6 us (38%)
  Pallas kernels  48.7 us (26%)
  starting transfers between devices  45.7 us (25%)
  local copies, waits for them, and re-layouts  11.5 us (6%)
  other arithmetic  6.03 us (3%)
    ppermute x18, waiting for transfers between devices, seq_perm(): return lax.ppermute(array, 'seq', pairs)  50 us
    pallas_call x6, Pallas kernels, head_call(): pl.pallas_call(kernel, out_shape=outs, grid_spec=pltpu.PrefetchScalarGrid...  39.1 us
    ppermute x18, starting transfers between devices, seq_perm(): return lax.ppermute(array, 'seq', pairs)  35.5 us
    ppermute x4, waiting for transfers between devices, head_perm(): return lax.ppermute(array, 'head', [(i, i ^ flip) for i in range(4)])  11.5 us
    ppermute x1, waiting for transfers between devices, body_eight(): low_o = lax.ppermute(jnp.where(z == 0, kv_give, block), 'seq', pairs)  10.1 us
    pallas_call x6, Pallas kernels, whole_call(): pl.pallas_call(kernel, out_shape=outs, in_specs=[pl.BlockSpec(memory_spac...  9.63 us
    unnamed x20, local copies, waits for them, and re-layouts  7 us
    ppermute x1, starting transfers between devices, body_eight(): low_o = lax.ppermute(jnp.where(z == 0, kv_give, block), 'seq', pairs)  5.45 us
  transfers between devices with their start and end apart: 24, of which 10 were waited for; matrix products, arithmetic and copies ran while one was open for 4% of the time, Pallas kernels for 23%

profile of v17, /device:TPU:16, one launch (start us, length us, event | category | flops | bytes accessed | tf_op | source)
XLA Modules:
  0.0 183.8 jit_solution(9957922503439899245)
XLA Ops:
  0.0 2.3 %dynamic-slice_bitcast_fusion.2 = (bf16[1,512,512]{2,1,0:T(8,128)(2,1)}, bf16[1,512,512]{2,1,0:T(8,128)(2,1)}) fusion(bf16[3,1,512,1024]{3,2,1,0:T(8,128)(2,1)} %param.2, s32[]{:T(128)S(6)} %select_n.65, s32[]{:T(128)S(6)} %select_n.64), kind=kLoop, calls=%fused_computation.7 | loop fusion | bytes 2097160 | tf_op jit(solution)/shard_map/dynamic_slice | solution.py:446
  2.3 2.3 %collective-permute-start = (bf16[1,512,512]{2,1,0:T(8,128)(2,1)}, bf16[1,512,512]{2,1,0:T(8,128)(2,1)}, u32[]{:S(2)}, u32[]{:S(2)}) collective-permute-start(bf16[1,512,512]{2,1,0:T(8,128)(2,1)} %get-tuple-element.64.q_m), channel_id=1, source_target_pairs={{16,8},{20,12},{24,16},{28,20},{17,9},{21,13},{25,17},{29,21},{18,... | collective-permute-start | bytes 1572872 | tf_op jit(solution)/shard_map/ppermute | solution.py:437
  4.7 1.6 collective-permute-start.1
  6.2 1.5 collective-permute-start.3
  7.7 4.2 %broadcast_select_fusion = (bf16[2,512,512]{2,1,0:T(8,128)(2,1)}, bf16[2,512,512]{2,1,0:T(8,128)(2,1)}, bf16[2,512,512]{2,1,0:T(8,128)(2,1)}, bf16[2,512,512]{2,1,0:T(8,128)(2,1)}) fusion(bf16[2,512,512]{2,1,0:T(8,128)(2,1)S(1)} %bitcast.26, pred[]{:T(512)S(6)} %eq.15, bf16[3,1,512,1024]{3,2,1,0:T(8,128)(2,1)} %param.2, s32[]{:T(128)S(6)} %select_n.65, ...), kind=kLoop, calls=%fused_computation.5 | loop fusion | flops 1048576 | bytes 7340041 | tf_op jit(solution)/shard_map/jit(_where)/select_n | solution.py:456
  12.6 5.5 %collective-permute-start.9 = (bf16[2,512,512]{2,1,0:T(8,128)(2,1)}, bf16[2,512,512]{2,1,0:T(8,128)(2,1)S(1)}, u32[]{:S(2)}, u32[]{:S(2)}) collective-permute-start(bf16[2,512,512]{2,1,0:T(8,128)(2,1)} %get-tuple-element.57), channel_id=1, source_target_pairs={{0,12},{4,8},{8,0},{12,4},{16,24},{20,28},{1,13},{5,9},{9,1},{13,5... | collective-permute-start | bytes 3145736 | tf_op jit(solution)/shard_map/ppermute | solution.py:456
  19.3 1.5 collective-permute-start.8
  20.8 1.9 %collective-permute-start.2 = (bf16[1,512,512]{2,1,0:T(8,128)(2,1)}, bf16[1,512,512]{2,1,0:T(8,128)(2,1)S(1)}, u32[]{:S(2)}, u32[]{:S(2)}) collective-permute-start(bf16[1,512,512]{2,1,0:T(8,128)(2,1)} %collective-permute-done.1.q_o), channel_id=1, source_target_pairs={{16,8},{20,12},{24,16},{28,20},{17,9},{21,13},{25,17},{29,21},{18,... | collective-permute-start | bytes 1572872 | tf_op jit(solution)/shard_map/ppermute | solution.py:437
  23.5 18.3 %collective-permute-done.2.qa_o = bf16[1,512,512]{2,1,0:T(8,128)(2,1)S(1)} collective-permute-done((bf16[1,512,512]{2,1,0:T(8,128)(2,1)}, bf16[1,512,512]{2,1,0:T(8,128)(2,1)S(1)}, u32[]{:S(2)}, u32[]{:S(2)}) %collective-permute-start.2) | collective-permute-done | bytes 524320 | tf_op jit(solution)/shard_map/ppermute | solution.py:437
  44.7 7.5 %collective-permute-start.7 = (bf16[1024,512]{1,0:T(8,128)(2,1)S(1)}, bf16[1024,512]{1,0:T(8,128)(2,1)}, u32[]{:S(2)}, u32[]{:S(2)}) collective-permute-start(bf16[1024,512]{1,0:T(8,128)(2,1)S(1)} %copy-done), channel_id=1, source_target_pairs={{16,0},{20,4},{24,8},{28,12},{17,1},{21,5},{25,9},{29,13},{18,2},{... | collective-permute-start | bytes 3145736 | tf_op jit(solution)/shard_map/ppermute | solution.py:437
  52.2 10.1 %collective-permute-done.9.refs_1_ = bf16[2,512,512]{2,1,0:T(8,128)(2,1)S(1)} collective-permute-done((bf16[2,512,512]{2,1,0:T(8,128)(2,1)}, bf16[2,512,512]{2,1,0:T(8,128)(2,1)S(1)}, u32[]{:S(2)}, u32[]{:S(2)}) %collective-permute-start.9) | collective-permute-done | bytes 1048608 | tf_op jit(solution)/shard_map/ppermute | solution.py:456
  65.6 8.1 %upper_rows.2 = (bf16[528,512]{1,0:T(8,128)(2,1)}, bf16[528,512]{1,0:T(8,128)(2,1)}) custom-call(s32[4]{0:T(128)S(1)} %pad_add_fusion.at, bf16[1,512,512]{2,1,0:T(8,128)(2,1)} %collective-permute-done.qa_m, bf16[1,512,512]{2,1,0:T(8,128)(2,1)S(1)} %copy-done.5, bf16[1,512,512]{2,1,0:T(8,128)(2,1)} %collective-permute-done.3.qb_m, ...), custom_call_target="tpu_custom_call" | custom-call | flops 700000000 | bytes 1024 | tf_op jit(solution)/shard_map/upper_rows/pallas_call | solution.py:310
  73.7 4.3 %collective-permute-start.10 = (bf16[528,512]{1,0:T(8,128)(2,1)}, bf16[528,512]{1,0:T(8,128)(2,1)}, u32[]{:S(2)}, u32[]{:S(2)}) collective-permute-start(bf16[528,512]{1,0:T(8,128)(2,1)} %get-tuple-element.33), channel_id=1, source_target_pairs={{8,16},{12,20},{16,24},{20,28},{9,17},{13,21},{17,25},{21,29},{10,... | collective-permute-start | bytes 1622024 | tf_op jit(solution)/shard_map/ppermute | solution.py:437
  79.3 8.3 %upper_rows.3 = (bf16[528,512]{1,0:T(8,128)(2,1)S(1)}, bf16[528,512]{1,0:T(8,128)(2,1)}) custom-call(s32[4]{0:T(128)S(1)} %pad_add_fusion.at, bf16[1,512,512]{2,1,0:T(8,128)(2,1)} %collective-permute-done.qa_m, bf16[1,512,512]{2,1,0:T(8,128)(2,1)S(1)} %copy-done.5, bf16[1,512,512]{2,1,0:T(8,128)(2,1)} %collective-permute-done.3.qb_m, ...), custom_call_target="tpu_custom_call" | custom-call | flops 700000000 | bytes 1024 | tf_op jit(solution)/shard_map/upper_rows/pallas_call | solution.py:310
  90.9 7.7 %own_rows.2.own = bf16[528,512]{1,0:T(8,128)(2,1)S(1)} custom-call(s32[4]{0:T(128)S(1)} %pad_add_fusion.at, bf16[1,512,512]{2,1,0:T(8,128)(2,1)} %get-tuple-element.64.q_m, bf16[1,512,512]{2,1,0:T(8,128)(2,1)} %collective-permute-done.1.q_o, bf16[2,512,512]{2,1,0:T(8,128)(2,1)S(1)} %copy-done.2, bf16[2,512,512]{2,1,0:T(8,128)(2,1)} %collective-permute-done.8.kv_o, ...), custom_call_target="tpu_custom_call" | custom-call | flops 600000000 | bytes 1024 | tf_op jit(solution)/shard_map/own_rows/pallas_call | solution.py:310
  98.6 5.5 %collective-permute-start.13 = (bf16[528,512]{1,0:T(8,128)(2,1)S(1)}, bf16[528,512]{1,0:T(8,128)(2,1)S(1)}, u32[]{:S(2)}, u32[]{:S(2)}) collective-permute-start(bf16[528,512]{1,0:T(8,128)(2,1)S(1)} %copy-done.9), channel_id=1, source_target_pairs={{8,16},{12,20},{16,24},{20,28},{9,17},{13,21},{17,25},{21,29},{10,... | collective-permute-start | bytes 1622024 | tf_op jit(solution)/shard_map/ppermute | solution.py:437
  104.1 3.7 %merge.2 = bf16[2,256,512]{2,1,0:T(8,128)(2,1)S(1)} custom-call(s32[4]{0:T(128)S(1)} %pad_add_fusion.at, bf16[528,512]{1,0:T(8,128)(2,1)S(1)} %own_rows.2.own, bf16[528,512]{1,0:T(8,128)(2,1)} %collective-permute-done.10.oa, bf16[528,512]{1,0:T(8,128)(2,1)} %collective-permute-done.11.ob), custom_call_target="tpu_custom_call" | custom-call | flops 200000000 | bytes 1024 | tf_op jit(solution)/shard_map/merge/pallas_call | solution.py:310
  108.4 7.7 %own_rows.3.own = bf16[528,512]{1,0:T(8,128)(2,1)S(1)} custom-call(s32[4]{0:T(128)S(1)} %pad_add_fusion.at, bf16[1,512,512]{2,1,0:T(8,128)(2,1)} %get-tuple-element.64.q_m, bf16[1,512,512]{2,1,0:T(8,128)(2,1)} %collective-permute-done.1.q_o, bf16[2,512,512]{2,1,0:T(8,128)(2,1)S(1)} %copy-done.3, bf16[2,512,512]{2,1,0:T(8,128)(2,1)} %collective-permute-done.8.kv_o, ...), custom_call_target="tpu_custom_call" | custom-call | flops 600000000 | bytes 1024 | tf_op jit(solution)/shard_map/own_rows/pallas_call | solution.py:310
  117.5 2.0 %collective-permute-start.19 = (bf16[1024,512]{1,0:T(8,128)(2,1)S(1)}, bf16[1024,512]{1,0:T(8,128)(2,1)S(1)}, u32[]{:S(2)}, u32[]{:S(2)}) collective-permute-start(bf16[1024,512]{1,0:T(8,128)(2,1)S(1)} %fusion.refs_4_), channel_id=1, source_target_pairs={{0,8},{4,12},{8,0},{12,4},{16,24},{20,28},{24,16},{28,20},{1,9},{5... | collective-permute-start | bytes 3145736 | tf_op jit(solution)/shard_map/ppermute | solution.py:437
  122.1 6.6 %collective-permute-done.13.oa = bf16[528,512]{1,0:T(8,128)(2,1)S(1)} collective-permute-done((bf16[528,512]{1,0:T(8,128)(2,1)S(1)}, bf16[528,512]{1,0:T(8,128)(2,1)S(1)}, u32[]{:S(2)}, u32[]{:S(2)}) %collective-permute-start.13) | collective-permute-done | bytes 540704 | tf_op jit(solution)/shard_map/ppermute | solution.py:437
  128.7 3.6 %merge.3 = bf16[2,256,512]{2,1,0:T(8,128)(2,1)S(1)} custom-call(s32[4]{0:T(128)S(1)} %pad_add_fusion.at, bf16[528,512]{1,0:T(8,128)(2,1)S(1)} %own_rows.3.own, bf16[528,512]{1,0:T(8,128)(2,1)S(1)} %collective-permute-done.13.oa, bf16[528,512]{1,0:T(8,128)(2,1)} %collective-permute-done.14.ob), custom_call_target="tpu_custom_call" | custom-call | flops 200000000 | bytes 1024 | tf_op jit(solution)/shard_map/merge/pallas_call | solution.py:310
  132.3 1.8 project.2
  136.7 1.6 collective-permute-start.16
  138.3 6.8 %collective-permute-done.16.got = bf16[2,2,64,512]{3,2,1,0:T(8,128)(2,1)S(1)} collective-permute-done((bf16[2,2,64,512]{3,2,1,0:T(8,128)(2,1)S(1)}, bf16[2,2,64,512]{3,2,1,0:T(8,128)(2,1)S(1)}, u32[]{:S(2)}, u32[]{:S(2)}) %collective-permute-start.16) | collective-permute-done | bytes 262176 | tf_op jit(solution)/shard_map/ppermute | solution.py:443
  145.8 2.7 %collective-permute-done.18 = bf16[2,256,512]{2,1,0:T(8,128)(2,1)S(1)} collective-permute-done((bf16[2,256,512]{2,1,0:T(8,128)(2,1)S(1)}, bf16[2,256,512]{2,1,0:T(8,128)(2,1)S(1)}, u32[]{:S(2)}, u32[]{:S(2)}) %collective-permute-start.18) | collective-permute-done | bytes 524320 | tf_op jit(solution)/shard_map/ppermute | solution.py:437
  148.5 1.6 collective-permute-done.19.refs_5_
  150.1 4.0 %project.3 = (bf16[6,2,2,64,512]{4,3,2,1,0:T(8,128)(2,1)S(1)}, bf16[6,2,2,64,512]{4,3,2,1,0:T(8,128)(2,1)S(1)}) custom-call(s32[4]{0:T(128)S(1)} %pad_add_fusion.at, bf16[2,2,2,64,512]{4,3,2,1,0:T(8,128)(2,1)S(1)} %bitcast.29, bf16[2,2,2,64,512]{4,3,2,1,0:T(8,128)(2,1)S(1)} %bitcast.32, bf16[1024,512]{1,0:T(8,128)(2,1)S(1)} %copy-done, ...), custom_call_target="tpu_custom_call" | custom-call | flops 600000000 | bytes 1024 | tf_op jit(solution)/shard_map/project/pallas_call | solution.py:360
  154.1 3.4 %collective-permute-done.20.got = bf16[6,2,2,64,512]{4,3,2,1,0:T(8,128)(2,1)S(1)} collective-permute-done((bf16[6,2,2,64,512]{4,3,2,1,0:T(8,128)(2,1)S(1)}, bf16[6,2,2,64,512]{4,3,2,1,0:T(8,128)(2,1)S(1)}, u32[]{:S(2)}, u32[]{:S(2)}) %collective-permute-start.20) | collective-permute-done | bytes 1572896 | tf_op jit(solution)/shard_map/ppermute | solution.py:443
  158.4 1.6 collective-permute-start.21
  160.5 1.4 collective-permute-start.23
  162.5 19.6 %collective-permute-done.17.refs_1_ = bf16[2,64,512]{2,1,0:T(8,128)(2,1)S(1)} collective-permute-done((bf16[2,64,512]{2,1,0:T(8,128)(2,1)S(1)}, bf16[2,64,512]{2,1,0:T(8,128)(2,1)S(1)}, u32[]{:S(2)}, u32[]{:S(2)}) %collective-permute-start.17) | collective-permute-done | bytes 131104 | tf_op jit(solution)/shard_map/ppermute | solution.py:437
  182.1 1.7 place.1
  (55 shorter events, 23.4 us)
Async XLA Ops:
  0.0 7.7 %copy-start = (bf16[1024,512]{1,0:T(8,128)(2,1)S(1)}, bf16[1024,512]{1,0:T(8,128)(2,1)}, u32[]{:S(2)}) copy-start(bf16[1024,512]{1,0:T(8,128)(2,1)} %refs_2_.7) | copy-start | bytes 3145732
  2.3 17.0 %collective-permute-start = (bf16[1,512,512]{2,1,0:T(8,128)(2,1)}, bf16[1,512,512]{2,1,0:T(8,128)(2,1)}, u32[]{:S(2)}, u32[]{:S(2)}) collective-permute-start(bf16[1,512,512]{2,1,0:T(8,128)(2,1)} %get-tuple-element.64.q_m), channel_id=1, source_target_pairs={{16,8},{20,12},{24,16},{28,20},{17,9},{21,13},{25,17},{29,21},{18,... | collective-permute-start | bytes 1572872 | tf_op jit(solution)/shard_map/ppermute | solution.py:437
  4.7 14.7 %collective-permute-start.1 = (bf16[1,512,512]{2,1,0:T(8,128)(2,1)}, bf16[1,512,512]{2,1,0:T(8,128)(2,1)}, u32[]{:S(2)}, u32[]{:S(2)}) collective-permute-start(bf16[1,512,512]{2,1,0:T(8,128)(2,1)} %get-tuple-element.63), channel_id=1, source_target_pairs={{0,4},{4,0},{8,12},{12,8},{16,20},{20,16},{24,28},{28,24},{1,5},{5... | collective-permute-start | bytes 1572872 | tf_op jit(solution)/shard_map/ppermute | solution.py:437
  6.2 16.5 %collective-permute-start.3 = (bf16[1,512,512]{2,1,0:T(8,128)(2,1)}, bf16[1,512,512]{2,1,0:T(8,128)(2,1)}, u32[]{:S(2)}, u32[]{:S(2)}) collective-permute-start(bf16[1,512,512]{2,1,0:T(8,128)(2,1)} %get-tuple-element.64.q_m), channel_id=1, source_target_pairs={{24,8},{28,12},{25,9},{29,13},{26,10},{30,14},{27,11},{31,15}} | collective-permute-start | bytes 1572872 | tf_op jit(solution)/shard_map/ppermute | solution.py:437
  11.9 40.3 %collective-permute-start.6 = (bf16[2,512,512]{2,1,0:T(8,128)(2,1)}, bf16[2,512,512]{2,1,0:T(8,128)(2,1)S(1)}, u32[]{:S(2)}, u32[]{:S(2)}) collective-permute-start(bf16[2,512,512]{2,1,0:T(8,128)(2,1)} %get-tuple-element.61), channel_id=1, source_target_pairs={{0,8},{4,12},{8,24},{12,28},{1,9},{5,13},{9,25},{13,29},{2,10},{6,... | collective-permute-start | bytes 3145736 | tf_op jit(solution)/shard_map/ppermute | solution.py:437
  12.6 49.6 %collective-permute-start.9 = (bf16[2,512,512]{2,1,0:T(8,128)(2,1)}, bf16[2,512,512]{2,1,0:T(8,128)(2,1)S(1)}, u32[]{:S(2)}, u32[]{:S(2)}) collective-permute-start(bf16[2,512,512]{2,1,0:T(8,128)(2,1)} %get-tuple-element.57), channel_id=1, source_target_pairs={{0,12},{4,8},{8,0},{12,4},{16,24},{20,28},{1,13},{5,9},{9,1},{13,5... | collective-permute-start | bytes 3145736 | tf_op jit(solution)/shard_map/ppermute | solution.py:456
  19.3 42.9 %collective-permute-start.8 = (bf16[2,512,512]{2,1,0:T(8,128)(2,1)}, bf16[2,512,512]{2,1,0:T(8,128)(2,1)}, u32[]{:S(2)}, u32[]{:S(2)}) collective-permute-start(bf16[2,512,512]{2,1,0:T(8,128)(2,1)} %get-tuple-element.32), channel_id=1, source_target_pairs={{0,4},{4,0},{8,12},{12,8},{16,20},{20,16},{24,28},{28,24},{1,5},{5... | collective-permute-start | bytes 3145736 | tf_op jit(solution)/shard_map/ppermute | solution.py:437
  20.8 20.9 %collective-permute-start.2 = (bf16[1,512,512]{2,1,0:T(8,128)(2,1)}, bf16[1,512,512]{2,1,0:T(8,128)(2,1)S(1)}, u32[]{:S(2)}, u32[]{:S(2)}) collective-permute-start(bf16[1,512,512]{2,1,0:T(8,128)(2,1)} %collective-permute-done.1.q_o), channel_id=1, source_target_pairs={{16,8},{20,12},{24,16},{28,20},{17,9},{21,13},{25,17},{29,21},{18,... | collective-permute-start | bytes 1572872 | tf_op jit(solution)/shard_map/ppermute | solution.py:437
  22.8 19.8 %collective-permute-start.4 = (bf16[1,512,512]{2,1,0:T(8,128)(2,1)}, bf16[1,512,512]{2,1,0:T(8,128)(2,1)S(1)}, u32[]{:S(2)}, u32[]{:S(2)}) collective-permute-start(bf16[1,512,512]{2,1,0:T(8,128)(2,1)} %collective-permute-done.1.q_o), channel_id=1, source_target_pairs={{24,8},{28,12},{25,9},{29,13},{26,10},{30,14},{27,11},{31,15}} | collective-permute-start | bytes 1572872 | tf_op jit(solution)/shard_map/ppermute | solution.py:437
  41.7 0.8 copy-start.4
  43.4 65.1 %collective-permute-start.5 = (bf16[1024,512]{1,0:T(8,128)(2,1)S(1)}, bf16[1024,512]{1,0:T(8,128)(2,1)}, u32[]{:S(2)}, u32[]{:S(2)}) collective-permute-start(bf16[1024,512]{1,0:T(8,128)(2,1)S(1)} %copy-done), channel_id=1, source_target_pairs={{0,16},{4,20},{1,17},{5,21},{2,18},{6,22},{3,19},{7,23}} | collective-permute-start | bytes 3145736 | tf_op jit(solution)/shard_map/ppermute | solution.py:437
  44.7 71.5 %collective-permute-start.7 = (bf16[1024,512]{1,0:T(8,128)(2,1)S(1)}, bf16[1024,512]{1,0:T(8,128)(2,1)}, u32[]{:S(2)}, u32[]{:S(2)}) collective-permute-start(bf16[1024,512]{1,0:T(8,128)(2,1)S(1)} %copy-done), channel_id=1, source_target_pairs={{16,0},{20,4},{24,8},{28,12},{17,1},{21,5},{25,9},{29,13},{18,2},{... | collective-permute-start | bytes 3145736 | tf_op jit(solution)/shard_map/ppermute | solution.py:437
  62.3 1.2 copy-start.1
  63.5 1.0 copy-start.5
  64.5 1.0 copy-start.7
  73.7 24.9 %collective-permute-start.10 = (bf16[528,512]{1,0:T(8,128)(2,1)}, bf16[528,512]{1,0:T(8,128)(2,1)}, u32[]{:S(2)}, u32[]{:S(2)}) collective-permute-start(bf16[528,512]{1,0:T(8,128)(2,1)} %get-tuple-element.33), channel_id=1, source_target_pairs={{8,16},{12,20},{16,24},{20,28},{9,17},{13,21},{17,25},{21,29},{10,... | collective-permute-start | bytes 1622024 | tf_op jit(solution)/shard_map/ppermute | solution.py:437
  78.0 26.1 %collective-permute-start.11 = (bf16[528,512]{1,0:T(8,128)(2,1)}, bf16[528,512]{1,0:T(8,128)(2,1)}, u32[]{:S(2)}, u32[]{:S(2)}) collective-permute-start(bf16[528,512]{1,0:T(8,128)(2,1)} %get-tuple-element.38), channel_id=1, source_target_pairs={{8,24},{12,28},{0,8},{4,12},{24,16},{28,20},{9,25},{13,29},{1,9},{... | collective-permute-start | bytes 1622024 | tf_op jit(solution)/shard_map/ppermute | solution.py:437
  88.4 32.2 %collective-permute-start.14 = (bf16[528,512]{1,0:T(8,128)(2,1)}, bf16[528,512]{1,0:T(8,128)(2,1)}, u32[]{:S(2)}, u32[]{:S(2)}) collective-permute-start(bf16[528,512]{1,0:T(8,128)(2,1)} %get-tuple-element.42), channel_id=1, source_target_pairs={{8,24},{12,28},{0,8},{4,12},{24,16},{28,20},{9,25},{13,29},{1,9},{... | collective-permute-start | bytes 1622024 | tf_op jit(solution)/shard_map/ppermute | solution.py:437
  89.7 1.2 copy-start.2
  90.9 7.7 %copy-start.9 = (bf16[528,512]{1,0:T(8,128)(2,1)S(1)}, bf16[528,512]{1,0:T(8,128)(2,1)}, u32[]{:S(2)}) copy-start(bf16[528,512]{1,0:T(8,128)(2,1)} %copy-done.8) | copy-start | bytes 1622020
  98.6 9.8 %copy-start.3 = (bf16[2,512,512]{2,1,0:T(8,128)(2,1)S(1)}, bf16[2,512,512]{2,1,0:T(8,128)(2,1)}, u32[]{:S(2)}) copy-start(bf16[2,512,512]{2,1,0:T(8,128)(2,1)} %get-tuple-element.62.kv_m) | copy-start | bytes 3145732
  98.6 30.0 %collective-permute-start.13 = (bf16[528,512]{1,0:T(8,128)(2,1)S(1)}, bf16[528,512]{1,0:T(8,128)(2,1)S(1)}, u32[]{:S(2)}, u32[]{:S(2)}) collective-permute-start(bf16[528,512]{1,0:T(8,128)(2,1)S(1)} %copy-done.9), channel_id=1, source_target_pairs={{8,16},{12,20},{16,24},{20,28},{9,17},{13,21},{17,25},{21,29},{10,... | collective-permute-start | bytes 1622024 | tf_op jit(solution)/shard_map/ppermute | solution.py:437
  107.8 14.2 %collective-permute-start.12 = (bf16[2,256,512]{2,1,0:T(8,128)(2,1)S(1)}, bf16[2,256,512]{2,1,0:T(8,128)(2,1)S(1)}, u32[]{:S(2)}, u32[]{:S(2)}) collective-permute-start(bf16[2,256,512]{2,1,0:T(8,128)(2,1)S(1)} %merge.2), channel_id=1, source_target_pairs={{0,4},{4,0},{8,12},{12,8},{16,20},{20,16},{24,28},{28,24},{1,5},{5... | collective-permute-start | bytes 1572872 | tf_op jit(solution)/shard_map/ppermute | solution.py:437
  117.5 32.5 %collective-permute-start.19 = (bf16[1024,512]{1,0:T(8,128)(2,1)S(1)}, bf16[1024,512]{1,0:T(8,128)(2,1)S(1)}, u32[]{:S(2)}, u32[]{:S(2)}) collective-permute-start(bf16[1024,512]{1,0:T(8,128)(2,1)S(1)} %fusion.refs_4_), channel_id=1, source_target_pairs={{0,8},{4,12},{8,0},{12,4},{16,24},{20,28},{24,16},{28,20},{1,9},{5... | collective-permute-start | bytes 3145736 | tf_op jit(solution)/shard_map/ppermute | solution.py:437
  134.1 2.0 %collective-permute-start.15 = (bf16[2,2,2,64,512]{4,3,2,1,0:T(8,128)(2,1)S(1)}, bf16[2,2,2,64,512]{4,3,2,1,0:T(8,128)(2,1)S(1)}, u32[]{:S(2)}, u32[]{:S(2)}) collective-permute-start(bf16[2,2,2,64,512]{4,3,2,1,0:T(8,128)(2,1)S(1)} %get-tuple-element.45), channel_id=1, source_target_pairs={{0,1},{1,0},{2,3},{3,2},{4,5},{5,4},{6,7},{7,6},{8,9},{9,8},{10,11... | collective-permute-start | bytes 1572872 | tf_op jit(solution)/shard_map/ppermute | solution.py:443
  134.2 14.3 %collective-permute-start.18 = (bf16[2,256,512]{2,1,0:T(8,128)(2,1)S(1)}, bf16[2,256,512]{2,1,0:T(8,128)(2,1)S(1)}, u32[]{:S(2)}, u32[]{:S(2)}) collective-permute-start(bf16[2,256,512]{2,1,0:T(8,128)(2,1)S(1)} %merge.3), channel_id=1, source_target_pairs={{0,4},{4,0},{8,12},{12,8},{16,20},{20,16},{24,28},{28,24},{1,5},{5... | collective-permute-start | bytes 1572872 | tf_op jit(solution)/shard_map/ppermute | solution.py:437
  136.7 8.4 %collective-permute-start.16 = (bf16[2,2,64,512]{3,2,1,0:T(8,128)(2,1)S(1)}, bf16[2,2,64,512]{3,2,1,0:T(8,128)(2,1)S(1)}, u32[]{:S(2)}, u32[]{:S(2)}) collective-permute-start(bf16[2,2,64,512]{3,2,1,0:T(8,128)(2,1)S(1)} %get-tuple-element.47), channel_id=1, source_target_pairs={{0,2},{1,3},{2,0},{3,1},{4,6},{5,7},{6,4},{7,5},{8,10},{9,11},{10,... | collective-permute-start | bytes 786440 | tf_op jit(solution)/shard_map/ppermute | solution.py:443
  154.0 3.5 %collective-permute-start.20 = (bf16[6,2,2,64,512]{4,3,2,1,0:T(8,128)(2,1)S(1)}, bf16[6,2,2,64,512]{4,3,2,1,0:T(8,128)(2,1)S(1)}, u32[]{:S(2)}, u32[]{:S(2)}) collective-permute-start(bf16[6,2,2,64,512]{4,3,2,1,0:T(8,128)(2,1)S(1)} %get-tuple-element.52), channel_id=1, source_target_pairs={{0,1},{1,0},{2,3},{3,2},{4,5},{5,4},{6,7},{7,6},{8,9},{9,8},{10,11... | collective-permute-start | bytes 4718600 | tf_op jit(solution)/shard_map/ppermute | solution.py:443
  158.4 23.7 %collective-permute-start.21 = (bf16[6,64,512]{2,1,0:T(8,128)(2,1)S(1)}, bf16[6,64,512]{2,1,0:T(8,128)(2,1)S(1)}, u32[]{:S(2)}, u32[]{:S(2)}) collective-permute-start(bf16[6,64,512]{2,1,0:T(8,128)(2,1)S(1)} %get-tuple-element.54), channel_id=1, source_target_pairs={{0,2},{1,3},{2,0},{3,1},{4,6},{5,7},{6,4},{7,5},{8,10},{9,11},{10,... | collective-permute-start | bytes 1179656 | tf_op jit(solution)/shard_map/ppermute | solution.py:443
  160.0 22.1 %collective-permute-start.22 = (bf16[6,64,512]{2,1,0:T(8,128)(2,1)S(1)}, bf16[6,64,512]{2,1,0:T(8,128)(2,1)S(1)}, u32[]{:S(2)}, u32[]{:S(2)}) collective-permute-start(bf16[6,64,512]{2,1,0:T(8,128)(2,1)S(1)} %get-tuple-element.55), channel_id=1, source_target_pairs={{0,4},{4,0},{8,12},{12,8},{16,20},{20,16},{24,28},{28,24},{1,5},{5... | collective-permute-start | bytes 1179656 | tf_op jit(solution)/shard_map/ppermute | solution.py:437
  160.5 21.6 %collective-permute-start.23 = (bf16[6,64,512]{2,1,0:T(8,128)(2,1)S(1)}, bf16[6,64,512]{2,1,0:T(8,128)(2,1)S(1)}, u32[]{:S(2)}, u32[]{:S(2)}) collective-permute-start(bf16[6,64,512]{2,1,0:T(8,128)(2,1)S(1)} %get-tuple-element.56), channel_id=1, source_target_pairs={{0,6},{1,7},{2,4},{3,5},{4,2},{5,3},{6,0},{7,1},{8,14},{9,15},{10,... | collective-permute-start | bytes 1179656 | tf_op jit(solution)/shard_map/ppermute | solution.py:519
  162.0 20.1 %collective-permute-start.17 = (bf16[2,64,512]{2,1,0:T(8,128)(2,1)S(1)}, bf16[2,64,512]{2,1,0:T(8,128)(2,1)S(1)}, u32[]{:S(2)}, u32[]{:S(2)}) collective-permute-start(bf16[2,64,512]{2,1,0:T(8,128)(2,1)S(1)} %get-tuple-element.49), channel_id=1, source_target_pairs={{0,4},{4,0},{8,12},{12,8},{16,20},{20,16},{24,28},{28,24},{1,5},{5... | collective-permute-start | bytes 393224 | tf_op jit(solution)/shard_map/ppermute | solution.py:437
  (2 other events, 1.6 us)

commit v18 on v17

--- a/solution.py
+++ b/solution.py
@@ -10,7 +10,7 @@
 LOG2E = 1.4426950408889634
 NEG = -1e30
 QB = 128
-VMEM = 24 * 1024 * 1024
+VMEM = 14 * 1024 * 1024
 F32, BF16 = jnp.float32, jnp.bfloat16
 
 
@@ -467,7 +467,7 @@
         a, b = head_call(
             functools.partial(upper_kernel, coef, c, chunks, parts), turn, [(a, 0) for a in qs + kvs + [out_weight]],
             [partial] * 2, heads, "upper_rows", 7)
-        turn = after(at, a)
+        turn = after(at, a, w_second)
         oa.append(seq_perm(a, (1, 2), (2, 3)))
         ob.append(seq_perm(b, (1, 3), (0, 1), (3, 2)))
     def own_rows(c, turn):
@@ -489,7 +489,7 @@
     attended = [merged(0, own[0])]
     own.append(own_rows(1, after(at, attended[0][0], w_second)))
     ridden = jnp.where(z == 2, w_second, low_m.reshape(out_weight.shape))
-    w_far = jnp.where(z >= 2, ridden, after(w_down, own[1]))
+    w_far = jnp.where(z >= 2, ridden, after(w_down, attended[0][0]))
     w_other = seq_perm(w_far, (0, 1), (1, 0), (2, 3), (3, 2))
     parts_out, plan = [], []
 
@@ -497,12 +497,12 @@
         send, kept = project(turn, attended, [(c, weights[layer]) for c, layer in names])
         return send.shape[:1] + send.shape[3:], [kept, head_perm(send, 1)]
 
-    attended.append(merged(1, (w_far, attended[0][1])))
     w_near = jnp.where(
-        (z == 0) | (z == 3), low_o.reshape(out_weight.shape), jnp.concatenate([o[: 2 * tokens] for o in ob]))
+        (z == 0) | (z == 3), low_o.reshape(out_weight.shape), jnp.concatenate([o[: 2 * tokens] for o in after(ob, own[1])]))
+    attended.append(merged(1, (w_far, attended[0][1], w_near)))
     weights = {0: out_weight, 1: w_near, 2: w_far, 3: w_other}
     names = [(0, 0), (0, 1)]
-    size, pair = summed(after(at, attended[1][0]), names)
+    size, pair = summed(at, names)
     both = struct(size[:1] + (2,) + size[1:], BF16)
     stay, to_y = whole_call(halve_kernel, at, pair, [both] * 2, "halve", 2)
     from_y = head_perm(to_y, 2)

time: 186 us -> 195 us (1.048)
  waiting for transfers between devices: 71.6 us -> 78.9 us
    ppermute x1, waiting for transfers between devices: 10.1 us -> 18.7 us  [body_eight(): low_o = lax.ppermute(jnp.where(z == 0, kv_give, block), 'seq', pairs)]
    ppermute x4, waiting for transfers between devices: 11.5 us -> 8.66 us  [head_perm(): return lax.ppermute(array, 'head', [(i, i ^ flip) for i in range(4)])]
    ppermute x18, starting transfers between devices: 35.5 us -> 37.7 us  [seq_perm(): return lax.ppermute(array, 'seq', pairs)]
    unnamed x20 -> x22, local copies, waits for them, and re-layouts: 7 us -> 8.89 us
  transfers between devices with their start and end apart: 24 -> 24, of which waited for: 10 -> 10; matrix products, arithmetic and copies ran while one was open for 4% -> 4% of each run, Pallas kernels for 23% -> 22%
where the time goes in v18:
time: 195 us; the launch traced here: 193 us
  waiting for transfers between devices  78.9 us (40%)
  Pallas kernels  48.8 us (25%)
  starting transfers between devices  46.2 us (24%)
  local copies, waits for them, and re-layouts  13.2 us (7%)
  other arithmetic  6.06 us (3%)
    ppermute x18, waiting for transfers between devices, seq_perm(): return lax.ppermute(array, 'seq', pairs)  51.6 us
    pallas_call x6, Pallas kernels, head_call(): pl.pallas_call(kernel, out_shape=outs, grid_spec=pltpu.PrefetchScalarGrid...  39.1 us
    ppermute x18, starting transfers between devices, seq_perm(): return lax.ppermute(array, 'seq', pairs)  37.7 us
    ppermute x1, waiting for transfers between devices, body_eight(): low_o = lax.ppermute(jnp.where(z == 0, kv_give, block), 'seq', pairs)  18.7 us
    pallas_call x6, Pallas kernels, whole_call(): pl.pallas_call(kernel, out_shape=outs, in_specs=[pl.BlockSpec(memory_spac...  9.64 us
    unnamed x22, local copies, waits for them, and re-layouts  8.89 us
    ppermute x4, waiting for transfers between devices, head_perm(): return lax.ppermute(array, 'head', [(i, i ^ flip) for i in range(4)])  8.66 us
    ppermute x1, starting transfers between devices, body_eight(): low_o = lax.ppermute(jnp.where(z == 0, kv_give, block), 'seq', pairs)  4.75 us
  transfers between devices with their start and end apart: 24, of which 10 were waited for; matrix products, arithmetic and copies ran while one was open for 4% of the time, Pallas kernels for 22%

profile of v18, /device:TPU:16, one launch (start us, length us, event | category | flops | bytes accessed | tf_op | source)
XLA Modules:
  0.0 193.5 jit_solution(16648257059470106970)
XLA Ops:
  0.0 2.1 %dynamic-slice_bitcast_fusion.2 = (bf16[1,512,512]{2,1,0:T(8,128)(2,1)S(1)}, bf16[1,512,512]{2,1,0:T(8,128)(2,1)}) fusion(bf16[3,1,512,1024]{3,2,1,0:T(8,128)(2,1)} %param.2, s32[]{:T(128)S(6)} %select_n.63, s32[]{:T(128)S(6)} %select_n.62), kind=kLoop, calls=%fused_computation.7 | loop fusion | bytes 2097160 | tf_op jit(solution)/shard_map/dynamic_slice | solution.py:446
  3.6 2.3 %collective-permute-start = (bf16[1,512,512]{2,1,0:T(8,128)(2,1)}, bf16[1,512,512]{2,1,0:T(8,128)(2,1)S(1)}, u32[]{:S(2)}, u32[]{:S(2)}) collective-permute-start(bf16[1,512,512]{2,1,0:T(8,128)(2,1)} %get-tuple-element.66.q_m), channel_id=1, source_target_pairs={{16,8},{20,12},{24,16},{28,20},{17,9},{21,13},{25,17},{29,21},{18,... | collective-permute-start | bytes 1572872 | tf_op jit(solution)/shard_map/ppermute | solution.py:437
  7.4 8.5 %collective-permute-done.1.q_o = bf16[1,512,512]{2,1,0:T(8,128)(2,1)} collective-permute-done((bf16[1,512,512]{2,1,0:T(8,128)(2,1)S(1)}, bf16[1,512,512]{2,1,0:T(8,128)(2,1)}, u32[]{:S(2)}, u32[]{:S(2)}) %collective-permute-start.1) | collective-permute-done | bytes 524320 | tf_op jit(solution)/shard_map/ppermute | solution.py:437
  15.9 2.3 %collective-permute-start.2 = (bf16[1,512,512]{2,1,0:T(8,128)(2,1)}, bf16[1,512,512]{2,1,0:T(8,128)(2,1)S(1)}, u32[]{:S(2)}, u32[]{:S(2)}) collective-permute-start(bf16[1,512,512]{2,1,0:T(8,128)(2,1)} %collective-permute-done.1.q_o), channel_id=1, source_target_pairs={{16,8},{20,12},{24,16},{28,20},{17,9},{21,13},{25,17},{29,21},{18,... | collective-permute-start | bytes 1572872 | tf_op jit(solution)/shard_map/ppermute | solution.py:437
  19.0 4.2 %broadcast_select_fusion = (bf16[2,512,512]{2,1,0:T(8,128)(2,1)}, bf16[2,512,512]{2,1,0:T(8,128)(2,1)}, bf16[2,512,512]{2,1,0:T(8,128)(2,1)}, bf16[2,512,512]{2,1,0:T(8,128)(2,1)}) fusion(bf16[2,512,512]{2,1,0:T(8,128)(2,1)S(1)} %bitcast.26, pred[]{:T(512)S(6)} %eq.14, bf16[3,1,512,1024]{3,2,1,0:T(8,128)(2,1)} %param.2, s32[]{:T(128)S(6)} %select_n.63, ...), kind=kLoop, calls=%fused_computation.5 | loop fusion | flops 1048576 | bytes 7340041 | tf_op jit(solution)/shard_map/jit(_where)/select_n | solution.py:456
  24.7 4.8 %collective-permute-start.7 = (bf16[2,512,512]{2,1,0:T(8,128)(2,1)}, bf16[2,512,512]{2,1,0:T(8,128)(2,1)S(1)}, u32[]{:S(2)}, u32[]{:S(2)}) collective-permute-start(bf16[2,512,512]{2,1,0:T(8,128)(2,1)} %get-tuple-element.59), channel_id=1, source_target_pairs={{0,12},{4,8},{8,0},{12,4},{16,24},{20,28},{1,13},{5,9},{9,1},{13,5... | collective-permute-start | bytes 3145736 | tf_op jit(solution)/shard_map/ppermute | solution.py:456
  29.5 1.6 collective-permute-start.5
  31.0 12.1 %collective-permute-done.2.qa_o = bf16[1,512,512]{2,1,0:T(8,128)(2,1)S(1)} collective-permute-done((bf16[1,512,512]{2,1,0:T(8,128)(2,1)}, bf16[1,512,512]{2,1,0:T(8,128)(2,1)S(1)}, u32[]{:S(2)}, u32[]{:S(2)}) %collective-permute-start.2) | collective-permute-done | bytes 524320 | tf_op jit(solution)/shard_map/ppermute | solution.py:437
  46.0 7.4 %collective-permute-start.16 = (bf16[1024,512]{1,0:T(8,128)(2,1)S(1)}, bf16[1024,512]{1,0:T(8,128)(2,1)}, u32[]{:S(2)}, u32[]{:S(2)}) collective-permute-start(bf16[1024,512]{1,0:T(8,128)(2,1)S(1)} %copy-done), channel_id=1, source_target_pairs={{16,0},{20,4},{24,8},{28,12},{17,1},{21,5},{25,9},{29,13},{18,2},{... | collective-permute-start | bytes 3145736 | tf_op jit(solution)/shard_map/ppermute | solution.py:437
  53.5 18.7 %collective-permute-done.7.refs_1_ = bf16[2,512,512]{2,1,0:T(8,128)(2,1)S(1)} collective-permute-done((bf16[2,512,512]{2,1,0:T(8,128)(2,1)}, bf16[2,512,512]{2,1,0:T(8,128)(2,1)S(1)}, u32[]{:S(2)}, u32[]{:S(2)}) %collective-permute-start.7) | collective-permute-done | bytes 1048608 | tf_op jit(solution)/shard_map/ppermute | solution.py:456
  76.6 8.1 %upper_rows.2 = (bf16[528,512]{1,0:T(8,128)(2,1)}, bf16[528,512]{1,0:T(8,128)(2,1)}) custom-call(s32[4]{0:T(128)S(1)} %pad_add_fusion.at, bf16[1,512,512]{2,1,0:T(8,128)(2,1)S(1)} %copy-done.5, bf16[1,512,512]{2,1,0:T(8,128)(2,1)S(1)} %copy-done.7, bf16[1,512,512]{2,1,0:T(8,128)(2,1)} %collective-permute-done.3.qb_m, bf16[1,512,512]{2,1,0:T(8,128)(2,1)S(1)} %copy-done.9, ...), custom_call_target="tpu_custom_call" | custom-call | flops 700000000 | bytes 1024 | tf_op jit(solution)/shard_map/upper_rows/pallas_call | solution.py:310
  86.0 4.9 %collective-permute-start.9 = (bf16[528,512]{1,0:T(8,128)(2,1)}, bf16[528,512]{1,0:T(8,128)(2,1)}, u32[]{:S(2)}, u32[]{:S(2)}) collective-permute-start(bf16[528,512]{1,0:T(8,128)(2,1)} %get-tuple-element.33), channel_id=1, source_target_pairs={{8,16},{12,20},{16,24},{20,28},{9,17},{13,21},{17,25},{21,29},{10,... | collective-permute-start | bytes 1622024 | tf_op jit(solution)/shard_map/ppermute | solution.py:437
  90.9 4.9 %collective-permute-done.8 = bf16[1024,512]{1,0:T(8,128)(2,1)} collective-permute-done((bf16[1024,512]{1,0:T(8,128)(2,1)S(1)}, bf16[1024,512]{1,0:T(8,128)(2,1)}, u32[]{:S(2)}, u32[]{:S(2)}) %collective-permute-start.8) | collective-permute-done | bytes 1048608 | tf_op jit(solution)/shard_map/ppermute | solution.py:437
  95.8 8.3 %upper_rows.3 = (bf16[528,512]{1,0:T(8,128)(2,1)S(1)}, bf16[528,512]{1,0:T(8,128)(2,1)}) custom-call(s32[4]{0:T(128)S(1)} %pad_add_fusion.at, bf16[1,512,512]{2,1,0:T(8,128)(2,1)S(1)} %copy-done.5, bf16[1,512,512]{2,1,0:T(8,128)(2,1)S(1)} %copy-done.7, bf16[1,512,512]{2,1,0:T(8,128)(2,1)} %collective-permute-done.3.qb_m, bf16[1,512,512]{2,1,0:T(8,128)(2,1)S(1)} %copy-done.9, ...), custom_call_target="tpu_custom_call" | custom-call | flops 700000000 | bytes 1024 | tf_op jit(solution)/shard_map/upper_rows/pallas_call | solution.py:310
  106.3 4.7 %collective-permute-start.17 = (bf16[528,512]{1,0:T(8,128)(2,1)}, bf16[528,512]{1,0:T(8,128)(2,1)S(1)}, u32[]{:S(2)}, u32[]{:S(2)}) collective-permute-start(bf16[528,512]{1,0:T(8,128)(2,1)} %copy-done.10), channel_id=1, source_target_pairs={{8,16},{12,20},{16,24},{20,28},{9,17},{13,21},{17,25},{21,29},{10,... | collective-permute-start | bytes 1622024 | tf_op jit(solution)/shard_map/ppermute | solution.py:437
  112.3 7.7 %own_rows.2.own = bf16[528,512]{1,0:T(8,128)(2,1)S(1)} custom-call(s32[4]{0:T(128)S(1)} %pad_add_fusion.at, bf16[1,512,512]{2,1,0:T(8,128)(2,1)} %get-tuple-element.66.q_m, bf16[1,512,512]{2,1,0:T(8,128)(2,1)} %collective-permute-done.1.q_o, bf16[2,512,512]{2,1,0:T(8,128)(2,1)S(1)} %copy-done.2, bf16[2,512,512]{2,1,0:T(8,128)(2,1)} %collective-permute-done.5.kv_o, ...), custom_call_target="tpu_custom_call" | custom-call | flops 600000000 | bytes 1024 | tf_op jit(solution)/shard_map/own_rows/pallas_call | solution.py:310
  120.0 3.7 %merge.2 = bf16[2,256,512]{2,1,0:T(8,128)(2,1)S(1)} custom-call(s32[4]{0:T(128)S(1)} %pad_add_fusion.at, bf16[528,512]{1,0:T(8,128)(2,1)S(1)} %own_rows.2.own, bf16[528,512]{1,0:T(8,128)(2,1)} %collective-permute-done.9.oa, bf16[528,512]{1,0:T(8,128)(2,1)} %collective-permute-done.10.ob), custom_call_target="tpu_custom_call" | custom-call | flops 200000000 | bytes 1024 | tf_op jit(solution)/shard_map/merge/pallas_call | solution.py:310
  123.7 1.6 collective-permute-start.11
  126.8 7.7 %own_rows.3.own = bf16[528,512]{1,0:T(8,128)(2,1)S(1)} custom-call(s32[4]{0:T(128)S(1)} %pad_add_fusion.at, bf16[1,512,512]{2,1,0:T(8,128)(2,1)} %get-tuple-element.66.q_m, bf16[1,512,512]{2,1,0:T(8,128)(2,1)} %collective-permute-done.1.q_o, bf16[2,512,512]{2,1,0:T(8,128)(2,1)S(1)} %copy-done.3, bf16[2,512,512]{2,1,0:T(8,128)(2,1)} %collective-permute-done.5.kv_o, ...), custom_call_target="tpu_custom_call" | custom-call | flops 600000000 | bytes 1024 | tf_op jit(solution)/shard_map/own_rows/pallas_call | solution.py:310
  137.1 1.8 project.2
  140.1 3.6 %merge.3 = bf16[2,256,512]{2,1,0:T(8,128)(2,1)S(1)} custom-call(s32[4]{0:T(128)S(1)} %pad_add_fusion.at, bf16[528,512]{1,0:T(8,128)(2,1)S(1)} %own_rows.3.own, bf16[528,512]{1,0:T(8,128)(2,1)S(1)} %collective-permute-done.17.oa, bf16[528,512]{1,0:T(8,128)(2,1)} %collective-permute-done.12.ob), custom_call_target="tpu_custom_call" | custom-call | flops 200000000 | bytes 1024 | tf_op jit(solution)/shard_map/merge/pallas_call | solution.py:310
  143.7 1.6 collective-permute-start.18
  146.0 1.6 collective-permute-start.14
  147.6 5.3 %collective-permute-done.14.got = bf16[2,2,64,512]{3,2,1,0:T(8,128)(2,1)S(1)} collective-permute-done((bf16[2,2,64,512]{3,2,1,0:T(8,128)(2,1)S(1)}, bf16[2,2,64,512]{3,2,1,0:T(8,128)(2,1)S(1)}, u32[]{:S(2)}, u32[]{:S(2)}) %collective-permute-start.14) | collective-permute-done | bytes 262176 | tf_op jit(solution)/shard_map/ppermute | solution.py:443
  153.4 3.5 %collective-permute-done.18 = bf16[2,256,512]{2,1,0:T(8,128)(2,1)S(1)} collective-permute-done((bf16[2,256,512]{2,1,0:T(8,128)(2,1)S(1)}, bf16[2,256,512]{2,1,0:T(8,128)(2,1)S(1)}, u32[]{:S(2)}, u32[]{:S(2)}) %collective-permute-start.18) | collective-permute-done | bytes 524320 | tf_op jit(solution)/shard_map/ppermute | solution.py:437
  157.0 2.8 %collective-permute-done.19.refs_5_ = bf16[1024,512]{1,0:T(8,128)(2,1)S(1)} collective-permute-done((bf16[1024,512]{1,0:T(8,128)(2,1)S(1)}, bf16[1024,512]{1,0:T(8,128)(2,1)S(1)}, u32[]{:S(2)}, u32[]{:S(2)}) %collective-permute-start.19) | collective-permute-done | bytes 1048608 | tf_op jit(solution)/shard_map/ppermute | solution.py:437
  159.7 4.0 %project.3 = (bf16[6,2,2,64,512]{4,3,2,1,0:T(8,128)(2,1)S(1)}, bf16[6,2,2,64,512]{4,3,2,1,0:T(8,128)(2,1)S(1)}) custom-call(s32[4]{0:T(128)S(1)} %pad_add_fusion.at, bf16[2,2,2,64,512]{4,3,2,1,0:T(8,128)(2,1)S(1)} %bitcast.29, bf16[2,2,2,64,512]{4,3,2,1,0:T(8,128)(2,1)S(1)} %bitcast.32, bf16[1024,512]{1,0:T(8,128)(2,1)S(1)} %copy-done, ...), custom_call_target="tpu_custom_call" | custom-call | flops 600000000 | bytes 1024 | tf_op jit(solution)/shard_map/project/pallas_call | solution.py:360
  163.8 3.4 %collective-permute-done.20.got = bf16[6,2,2,64,512]{4,3,2,1,0:T(8,128)(2,1)S(1)} collective-permute-done((bf16[6,2,2,64,512]{4,3,2,1,0:T(8,128)(2,1)S(1)}, bf16[6,2,2,64,512]{4,3,2,1,0:T(8,128)(2,1)S(1)}, u32[]{:S(2)}, u32[]{:S(2)}) %collective-permute-start.20) | collective-permute-done | bytes 1572896 | tf_op jit(solution)/shard_map/ppermute | solution.py:443
  168.1 1.6 collective-permute-start.21
  171.6 1.5 collective-permute-start.15
  173.1 18.6 %collective-permute-done.15.refs_1_ = bf16[2,64,512]{2,1,0:T(8,128)(2,1)S(1)} collective-permute-done((bf16[2,64,512]{2,1,0:T(8,128)(2,1)S(1)}, bf16[2,64,512]{2,1,0:T(8,128)(2,1)S(1)}, u32[]{:S(2)}, u32[]{:S(2)}) %collective-permute-start.15) | collective-permute-done | bytes 131104 | tf_op jit(solution)/shard_map/ppermute | solution.py:437
  191.8 1.7 place.1
  (57 shorter events, 26.7 us)
Async XLA Ops:
  0.0 19.0 %copy-start = (bf16[1024,512]{1,0:T(8,128)(2,1)S(1)}, bf16[1024,512]{1,0:T(8,128)(2,1)}, u32[]{:S(2)}) copy-start(bf16[1024,512]{1,0:T(8,128)(2,1)} %refs_2_.7) | copy-start | bytes 3145732
  2.1 13.8 %collective-permute-start.1 = (bf16[1,512,512]{2,1,0:T(8,128)(2,1)S(1)}, bf16[1,512,512]{2,1,0:T(8,128)(2,1)}, u32[]{:S(2)}, u32[]{:S(2)}) collective-permute-start(bf16[1,512,512]{2,1,0:T(8,128)(2,1)S(1)} %get-tuple-element.65), channel_id=1, source_target_pairs={{0,4},{4,0},{8,12},{12,8},{16,20},{20,16},{24,28},{28,24},{1,5},{5... | collective-permute-start | bytes 1572872 | tf_op jit(solution)/shard_map/ppermute | solution.py:437
  3.6 20.2 %collective-permute-start = (bf16[1,512,512]{2,1,0:T(8,128)(2,1)}, bf16[1,512,512]{2,1,0:T(8,128)(2,1)S(1)}, u32[]{:S(2)}, u32[]{:S(2)}) collective-permute-start(bf16[1,512,512]{2,1,0:T(8,128)(2,1)} %get-tuple-element.66.q_m), channel_id=1, source_target_pairs={{16,8},{20,12},{24,16},{28,20},{17,9},{21,13},{25,17},{29,21},{18,... | collective-permute-start | bytes 1572872 | tf_op jit(solution)/shard_map/ppermute | solution.py:437
  6.0 23.5 %collective-permute-start.3 = (bf16[1,512,512]{2,1,0:T(8,128)(2,1)}, bf16[1,512,512]{2,1,0:T(8,128)(2,1)}, u32[]{:S(2)}, u32[]{:S(2)}) collective-permute-start(bf16[1,512,512]{2,1,0:T(8,128)(2,1)} %get-tuple-element.66.q_m), channel_id=1, source_target_pairs={{24,8},{28,12},{25,9},{29,13},{26,10},{30,14},{27,11},{31,15}} | collective-permute-start | bytes 1572872 | tf_op jit(solution)/shard_map/ppermute | solution.py:437
  15.9 27.2 %collective-permute-start.2 = (bf16[1,512,512]{2,1,0:T(8,128)(2,1)}, bf16[1,512,512]{2,1,0:T(8,128)(2,1)S(1)}, u32[]{:S(2)}, u32[]{:S(2)}) collective-permute-start(bf16[1,512,512]{2,1,0:T(8,128)(2,1)} %collective-permute-done.1.q_o), channel_id=1, source_target_pairs={{16,8},{20,12},{24,16},{28,20},{17,9},{21,13},{25,17},{29,21},{18,... | collective-permute-start | bytes 1572872 | tf_op jit(solution)/shard_map/ppermute | solution.py:437
  18.3 25.7 %collective-permute-start.4 = (bf16[1,512,512]{2,1,0:T(8,128)(2,1)}, bf16[1,512,512]{2,1,0:T(8,128)(2,1)S(1)}, u32[]{:S(2)}, u32[]{:S(2)}) collective-permute-start(bf16[1,512,512]{2,1,0:T(8,128)(2,1)} %collective-permute-done.1.q_o), channel_id=1, source_target_pairs={{24,8},{28,12},{25,9},{29,13},{26,10},{30,14},{27,11},{31,15}} | collective-permute-start | bytes 1572872 | tf_op jit(solution)/shard_map/ppermute | solution.py:437
  23.1 30.4 %collective-permute-start.6 = (bf16[2,512,512]{2,1,0:T(8,128)(2,1)}, bf16[2,512,512]{2,1,0:T(8,128)(2,1)S(1)}, u32[]{:S(2)}, u32[]{:S(2)}) collective-permute-start(bf16[2,512,512]{2,1,0:T(8,128)(2,1)} %get-tuple-element.63), channel_id=1, source_target_pairs={{0,8},{4,12},{8,24},{12,28},{1,9},{5,13},{9,25},{13,29},{2,10},{6,... | collective-permute-start | bytes 3145736 | tf_op jit(solution)/shard_map/ppermute | solution.py:437
  24.7 47.5 %collective-permute-start.7 = (bf16[2,512,512]{2,1,0:T(8,128)(2,1)}, bf16[2,512,512]{2,1,0:T(8,128)(2,1)S(1)}, u32[]{:S(2)}, u32[]{:S(2)}) collective-permute-start(bf16[2,512,512]{2,1,0:T(8,128)(2,1)} %get-tuple-element.59), channel_id=1, source_target_pairs={{0,12},{4,8},{8,0},{12,4},{16,24},{20,28},{1,13},{5,9},{9,1},{13,5... | collective-permute-start | bytes 3145736 | tf_op jit(solution)/shard_map/ppermute | solution.py:456
  29.5 42.7 %collective-permute-start.5 = (bf16[2,512,512]{2,1,0:T(8,128)(2,1)}, bf16[2,512,512]{2,1,0:T(8,128)(2,1)}, u32[]{:S(2)}, u32[]{:S(2)}) collective-permute-start(bf16[2,512,512]{2,1,0:T(8,128)(2,1)} %get-tuple-element.32), channel_id=1, source_target_pairs={{0,4},{4,0},{8,12},{12,8},{16,20},{20,16},{24,28},{28,24},{1,5},{5... | collective-permute-start | bytes 3145736 | tf_op jit(solution)/shard_map/ppermute | solution.py:437
  44.7 51.1 %collective-permute-start.8 = (bf16[1024,512]{1,0:T(8,128)(2,1)S(1)}, bf16[1024,512]{1,0:T(8,128)(2,1)}, u32[]{:S(2)}, u32[]{:S(2)}) collective-permute-start(bf16[1024,512]{1,0:T(8,128)(2,1)S(1)} %copy-done), channel_id=1, source_target_pairs={{0,16},{4,20},{1,17},{5,21},{2,18},{6,22},{3,19},{7,23}} | collective-permute-start | bytes 3145736 | tf_op jit(solution)/shard_map/ppermute | solution.py:437
  46.0 79.2 %collective-permute-start.16 = (bf16[1024,512]{1,0:T(8,128)(2,1)S(1)}, bf16[1024,512]{1,0:T(8,128)(2,1)}, u32[]{:S(2)}, u32[]{:S(2)}) collective-permute-start(bf16[1024,512]{1,0:T(8,128)(2,1)S(1)} %copy-done), channel_id=1, source_target_pairs={{16,0},{20,4},{24,8},{28,12},{17,1},{21,5},{25,9},{29,13},{18,2},{... | collective-permute-start | bytes 3145736 | tf_op jit(solution)/shard_map/ppermute | solution.py:437
  72.2 1.2 copy-start.1
  73.4 1.0 copy-start.5
  74.5 1.0 copy-start.7
  75.5 1.0 copy-start.9
  84.7 35.3 %collective-permute-start.10 = (bf16[528,512]{1,0:T(8,128)(2,1)}, bf16[528,512]{1,0:T(8,128)(2,1)}, u32[]{:S(2)}, u32[]{:S(2)}) collective-permute-start(bf16[528,512]{1,0:T(8,128)(2,1)} %get-tuple-element.39), channel_id=1, source_target_pairs={{8,24},{12,28},{0,8},{4,12},{24,16},{28,20},{9,25},{13,29},{1,9},{... | collective-permute-start | bytes 1622024 | tf_op jit(solution)/shard_map/ppermute | solution.py:437
  86.0 34.0 %collective-permute-start.9 = (bf16[528,512]{1,0:T(8,128)(2,1)}, bf16[528,512]{1,0:T(8,128)(2,1)}, u32[]{:S(2)}, u32[]{:S(2)}) collective-permute-start(bf16[528,512]{1,0:T(8,128)(2,1)} %get-tuple-element.33), channel_id=1, source_target_pairs={{8,16},{12,20},{16,24},{20,28},{9,17},{13,21},{17,25},{21,29},{10,... | collective-permute-start | bytes 1622024 | tf_op jit(solution)/shard_map/ppermute | solution.py:437
  104.2 0.9 copy-start.10
  105.0 29.5 %collective-permute-start.12 = (bf16[528,512]{1,0:T(8,128)(2,1)}, bf16[528,512]{1,0:T(8,128)(2,1)}, u32[]{:S(2)}, u32[]{:S(2)}) collective-permute-start(bf16[528,512]{1,0:T(8,128)(2,1)} %get-tuple-element.40), channel_id=1, source_target_pairs={{8,24},{12,28},{0,8},{4,12},{24,16},{28,20},{9,25},{13,29},{1,9},{... | collective-permute-start | bytes 1622024 | tf_op jit(solution)/shard_map/ppermute | solution.py:437
  106.3 33.8 %collective-permute-start.17 = (bf16[528,512]{1,0:T(8,128)(2,1)}, bf16[528,512]{1,0:T(8,128)(2,1)S(1)}, u32[]{:S(2)}, u32[]{:S(2)}) collective-permute-start(bf16[528,512]{1,0:T(8,128)(2,1)} %copy-done.10), channel_id=1, source_target_pairs={{8,16},{12,20},{16,24},{20,28},{9,17},{13,21},{17,25},{21,29},{10,... | collective-permute-start | bytes 1622024 | tf_op jit(solution)/shard_map/ppermute | solution.py:437
  111.1 1.2 copy-start.2
  123.7 13.3 %collective-permute-start.11 = (bf16[2,256,512]{2,1,0:T(8,128)(2,1)S(1)}, bf16[2,256,512]{2,1,0:T(8,128)(2,1)S(1)}, u32[]{:S(2)}, u32[]{:S(2)}) collective-permute-start(bf16[2,256,512]{2,1,0:T(8,128)(2,1)S(1)} %merge.2), channel_id=1, source_target_pairs={{0,4},{4,0},{8,12},{12,8},{16,20},{20,16},{24,28},{28,24},{1,5},{5... | collective-permute-start | bytes 1572872 | tf_op jit(solution)/shard_map/ppermute | solution.py:437
  125.3 1.5 copy-start.3
  126.7 33.0 %collective-permute-start.19 = (bf16[1024,512]{1,0:T(8,128)(2,1)S(1)}, bf16[1024,512]{1,0:T(8,128)(2,1)S(1)}, u32[]{:S(2)}, u32[]{:S(2)}) collective-permute-start(bf16[1024,512]{1,0:T(8,128)(2,1)S(1)} %fusion.refs_4_), channel_id=1, source_target_pairs={{0,8},{4,12},{8,0},{12,4},{16,24},{20,28},{24,16},{28,20},{1,9},{5... | collective-permute-start | bytes 3145736 | tf_op jit(solution)/shard_map/ppermute | solution.py:437
  138.9 6.4 %collective-permute-start.13 = (bf16[2,2,2,64,512]{4,3,2,1,0:T(8,128)(2,1)S(1)}, bf16[2,2,2,64,512]{4,3,2,1,0:T(8,128)(2,1)S(1)}, u32[]{:S(2)}, u32[]{:S(2)}) collective-permute-start(bf16[2,2,2,64,512]{4,3,2,1,0:T(8,128)(2,1)S(1)} %get-tuple-element.45), channel_id=1, source_target_pairs={{0,1},{1,0},{2,3},{3,2},{4,5},{5,4},{6,7},{7,6},{8,9},{9,8},{10,11... | collective-permute-start | bytes 1572872 | tf_op jit(solution)/shard_map/ppermute | solution.py:443
  143.7 13.2 %collective-permute-start.18 = (bf16[2,256,512]{2,1,0:T(8,128)(2,1)S(1)}, bf16[2,256,512]{2,1,0:T(8,128)(2,1)S(1)}, u32[]{:S(2)}, u32[]{:S(2)}) collective-permute-start(bf16[2,256,512]{2,1,0:T(8,128)(2,1)S(1)} %merge.3), channel_id=1, source_target_pairs={{0,4},{4,0},{8,12},{12,8},{16,20},{20,16},{24,28},{28,24},{1,5},{5... | collective-permute-start | bytes 1572872 | tf_op jit(solution)/shard_map/ppermute | solution.py:437
  146.0 6.8 %collective-permute-start.14 = (bf16[2,2,64,512]{3,2,1,0:T(8,128)(2,1)S(1)}, bf16[2,2,64,512]{3,2,1,0:T(8,128)(2,1)S(1)}, u32[]{:S(2)}, u32[]{:S(2)}) collective-permute-start(bf16[2,2,64,512]{3,2,1,0:T(8,128)(2,1)S(1)} %get-tuple-element.47), channel_id=1, source_target_pairs={{0,2},{1,3},{2,0},{3,1},{4,6},{5,7},{6,4},{7,5},{8,10},{9,11},{10,... | collective-permute-start | bytes 786440 | tf_op jit(solution)/shard_map/ppermute | solution.py:443
  163.7 3.5 %collective-permute-start.20 = (bf16[6,2,2,64,512]{4,3,2,1,0:T(8,128)(2,1)S(1)}, bf16[6,2,2,64,512]{4,3,2,1,0:T(8,128)(2,1)S(1)}, u32[]{:S(2)}, u32[]{:S(2)}) collective-permute-start(bf16[6,2,2,64,512]{4,3,2,1,0:T(8,128)(2,1)S(1)} %get-tuple-element.54), channel_id=1, source_target_pairs={{0,1},{1,0},{2,3},{3,2},{4,5},{5,4},{6,7},{7,6},{8,9},{9,8},{10,11... | collective-permute-start | bytes 4718600 | tf_op jit(solution)/shard_map/ppermute | solution.py:443
  168.1 23.7 %collective-permute-start.21 = (bf16[6,64,512]{2,1,0:T(8,128)(2,1)S(1)}, bf16[6,64,512]{2,1,0:T(8,128)(2,1)S(1)}, u32[]{:S(2)}, u32[]{:S(2)}) collective-permute-start(bf16[6,64,512]{2,1,0:T(8,128)(2,1)S(1)} %get-tuple-element.56), channel_id=1, source_target_pairs={{0,2},{1,3},{2,0},{3,1},{4,6},{5,7},{6,4},{7,5},{8,10},{9,11},{10,... | collective-permute-start | bytes 1179656 | tf_op jit(solution)/shard_map/ppermute | solution.py:443
  169.7 22.1 %collective-permute-start.22 = (bf16[6,64,512]{2,1,0:T(8,128)(2,1)S(1)}, bf16[6,64,512]{2,1,0:T(8,128)(2,1)S(1)}, u32[]{:S(2)}, u32[]{:S(2)}) collective-permute-start(bf16[6,64,512]{2,1,0:T(8,128)(2,1)S(1)} %get-tuple-element.57), channel_id=1, source_target_pairs={{0,4},{4,0},{8,12},{12,8},{16,20},{20,16},{24,28},{28,24},{1,5},{5... | collective-permute-start | bytes 1179656 | tf_op jit(solution)/shard_map/ppermute | solution.py:437
  171.1 20.6 %collective-permute-start.23 = (bf16[6,64,512]{2,1,0:T(8,128)(2,1)S(1)}, bf16[6,64,512]{2,1,0:T(8,128)(2,1)S(1)}, u32[]{:S(2)}, u32[]{:S(2)}) collective-permute-start(bf16[6,64,512]{2,1,0:T(8,128)(2,1)S(1)} %get-tuple-element.58), channel_id=1, source_target_pairs={{0,6},{1,7},{2,4},{3,5},{4,2},{5,3},{6,0},{7,1},{8,14},{9,15},{10,... | collective-permute-start | bytes 1179656 | tf_op jit(solution)/shard_map/ppermute | solution.py:519
  171.6 20.1 %collective-permute-start.15 = (bf16[2,64,512]{2,1,0:T(8,128)(2,1)S(1)}, bf16[2,64,512]{2,1,0:T(8,128)(2,1)S(1)}, u32[]{:S(2)}, u32[]{:S(2)}) collective-permute-start(bf16[2,64,512]{2,1,0:T(8,128)(2,1)S(1)} %get-tuple-element.49), channel_id=1, source_target_pairs={{0,4},{4,0},{8,12},{12,8},{16,20},{20,16},{24,28},{28,24},{1,5},{5... | collective-permute-start | bytes 393224 | tf_op jit(solution)/shard_map/ppermute | solution.py:437
  (3 other events, 2.5 us)

commit v19 on v18

--- a/solution.py
+++ b/solution.py
@@ -10,7 +10,7 @@
 LOG2E = 1.4426950408889634
 NEG = -1e30
 QB = 128
-VMEM = 14 * 1024 * 1024
+VMEM = 24 * 1024 * 1024
 F32, BF16 = jnp.float32, jnp.bfloat16
 
 
@@ -213,20 +213,30 @@
     k_e, k_o = pair(kv_m[0], kv_o[0])
     v_e, v_o = pair(kv_m[1], kv_o[1])
     v_e, v_o = with_ones(v_e), with_ones(v_o)
-    m_k, m_v, o_k, o_v = stacked(low)
-    lk_e, lk_o = pair(m_k, o_k)
-    lv_e, lv_o = pair(m_v, o_v)
-    col_e = (mine(lk_e).astype(F32), mine(lv_e).astype(F32), below)
-    col_o = (mine(lk_o).astype(F32), mine(lv_o).astype(F32), below)
     share = tokens // parts
     index = lax.broadcasted_iota(jnp.int32, (tokens, cols), 0)
     index = (index // share) * (cols // parts) + chunk * share + index % share
     tri = lax.broadcasted_iota(jnp.int32, (tokens, cols), 1) <= index
-    o1, l1 = attend(q_e, [(k_e, v_e, tri), (lk_o, with_ones(lv_o), below)], [col_e], coef)
-    o2, l2 = attend(q_o, [(k_o, v_o, tri), (k_e, v_e, None)], [col_e, col_o], coef)
-    out[:tokens] = o1.astype(BF16)
-    out[tokens : 2 * tokens] = o2.astype(BF16)
-    put_lse(out, 2 * tokens, *lse_rows(l1, l2))
+
+    def run(even, odd):
+        o1, l1 = attend(q_e, [(k_e, v_e, tri)] + even[0], even[1], coef)
+        o2, l2 = attend(q_o, [(k_o, v_o, tri), (k_e, v_e, None)], odd, coef)
+        out[:tokens] = o1.astype(BF16)
+        out[tokens : 2 * tokens] = o2.astype(BF16)
+        put_lse(out, 2 * tokens, *lse_rows(l1, l2))
+
+    @pl.when(below)
+    def _():
+        m_k, m_v, o_k, o_v = stacked(low)
+        lk_e, lk_o = pair(m_k, o_k)
+        lv_e, lv_o = pair(m_v, o_v)
+        col_e = (mine(lk_e).astype(F32), mine(lv_e).astype(F32), None)
+        col_o = (mine(lk_o).astype(F32), mine(lv_o).astype(F32), None)
+        run(([(lk_o, with_ones(lv_o), None)], [col_e]), [col_e, col_o])
+
+    @pl.when(jnp.logical_not(below))
+    def _():
+        run(([], []), [])
 
 
 def upper_kernel(coef, chunk, chunks, parts, at, qa_m, qa_o, qb_m, qb_o, kv_m, kv_o, *refs):
@@ -244,25 +254,40 @@
 
     k_e, k_o = pair(kv_m[0], kv_o[0])
     v_e, v_o = pair(kv_m[1], kv_o[1])
-    m_k, m_v, o_k, o_v = (mine(part).astype(F32) for part in stacked(low))
-    lower = [(m_k, m_v, below), (o_k, o_v, below)]
     ce = (mine(k_e).astype(F32), mine(v_e).astype(F32), None)
     co = (mine(k_o).astype(F32), mine(v_o).astype(F32), None)
     base = chunk * 2 * tokens
-    for q_m, q_o, out, dense, singles in (
-        (qa_m, qa_o, out_a, [(k_o, with_ones(v_o), None)], [ce]),
-        (qb_m, qb_o, out_b, [], [ce, co]),
-    ):
+
+    def run(q_m, q_o, out, dense, singles, lower):
         q_e, q_odd = pair(mine(q_m[0]), mine(q_o[0]))
         o1, l1 = attend(q_e, dense, singles + lower, coef)
         o2, l2 = attend(q_odd, [], [ce, co] + lower, coef)
-        o1, o2 = o1.astype(BF16), o2.astype(BF16)
-        if out is out_b:
-            o1 = jnp.where(below, o1, weight[base : base + tokens])
-            o2 = jnp.where(below, o2, weight[base + tokens : base + 2 * tokens])
-        out[:tokens] = o1
-        out[tokens : 2 * tokens] = o2
+        out[:tokens] = o1.astype(BF16)
+        out[tokens : 2 * tokens] = o2.astype(BF16)
         put_lse(out, 2 * tokens, *lse_rows(l1, l2))
+
+    def first_rows(lower):
+        run(qa_m, qa_o, out_a, [(k_o, with_ones(v_o), None)], [ce], lower)
+
+    @pl.when(below)
+    def _():
+        m_k, m_v, o_k, o_v = (mine(part).astype(F32) for part in stacked(low))
+        lower = [(m_k, m_v, None), (o_k, o_v, None)]
+        first_rows(lower)
+        run(qb_m, qb_o, out_b, [], [ce, co], lower)
+
+    @pl.when(jnp.logical_not(below))
+    def _():
+        out_b[: 2 * tokens] = weight[base : base + 2 * tokens]
+        out_b[pl.ds(2 * tokens, LSE_ROWS), :] = jnp.zeros((LSE_ROWS, HEAD), BF16)
+
+    @pl.when(z == 2)
+    def _():
+        first_rows([])
+
+    @pl.when(z % 3 == 0)
+    def _():
+        out_a[...] = jnp.zeros(out_a.shape, BF16)
 
 
 def lse_packed(ref, base, rows):
@@ -467,7 +492,7 @@
         a, b = head_call(
             functools.partial(upper_kernel, coef, c, chunks, parts), turn, [(a, 0) for a in qs + kvs + [out_weight]],
             [partial] * 2, heads, "upper_rows", 7)
-        turn = after(at, a, w_second)
+        turn = after(at, a)
         oa.append(seq_perm(a, (1, 2), (2, 3)))
         ob.append(seq_perm(b, (1, 3), (0, 1), (3, 2)))
     def own_rows(c, turn):
@@ -489,7 +514,7 @@
     attended = [merged(0, own[0])]
     own.append(own_rows(1, after(at, attended[0][0], w_second)))
     ridden = jnp.where(z == 2, w_second, low_m.reshape(out_weight.shape))
-    w_far = jnp.where(z >= 2, ridden, after(w_down, attended[0][0]))
+    w_far = jnp.where(z >= 2, ridden, after(w_down, own[1]))
     w_other = seq_perm(w_far, (0, 1), (1, 0), (2, 3), (3, 2))
     parts_out, plan = [], []
 

time: 195 us -> 186 us (0.954)
  waiting for transfers between devices: 78.9 us -> 73.1 us
  Pallas kernels: 48.8 us -> 44.2 us
  starting transfers between devices: 46.2 us -> 48.8 us
    ppermute x1, waiting for transfers between devices: 18.7 us -> 10.1 us  [body_eight(): low_o = lax.ppermute(jnp.where(z == 0, kv_give, block), 'seq', pairs)]
    pallas_call x6, Pallas kernels: 39.1 us -> 34.5 us  [head_call(): pl.pallas_call(kernel, out_shape=outs, grid_spec=pltpu.PrefetchScalarGrid...]
    unnamed x22 -> x20, local copies, waits for them, and re-layouts: 8.89 us -> 7 us
  transfers between devices with their start and end apart: 24 -> 24, of which waited for: 10 -> 10; matrix products, arithmetic and copies ran while one was open for 4% -> 4% of each run, Pallas kernels for 22% -> 20%
where the time goes in v19:
time: 186 us; the launch traced here: 184 us
  waiting for transfers between devices  73.1 us (39%)
  starting transfers between devices  48.8 us (26%)
  Pallas kernels  44.2 us (24%)
  local copies, waits for them, and re-layouts  11.5 us (6%)
  other arithmetic  6.01 us (3%)
    ppermute x18, waiting for transfers between devices, seq_perm(): return lax.ppermute(array, 'seq', pairs)  53.2 us
    ppermute x18, starting transfers between devices, seq_perm(): return lax.ppermute(array, 'seq', pairs)  38.6 us
    pallas_call x6, Pallas kernels, head_call(): pl.pallas_call(kernel, out_shape=outs, grid_spec=pltpu.PrefetchScalarGrid...  34.5 us
    ppermute x1, waiting for transfers between devices, body_eight(): low_o = lax.ppermute(jnp.where(z == 0, kv_give, block), 'seq', pairs)  10.1 us
    ppermute x4, waiting for transfers between devices, head_perm(): return lax.ppermute(array, 'head', [(i, i ^ flip) for i in range(4)])  9.83 us
    pallas_call x6, Pallas kernels, whole_call(): pl.pallas_call(kernel, out_shape=outs, in_specs=[pl.BlockSpec(memory_spac...  9.63 us
    unnamed x20, local copies, waits for them, and re-layouts  7 us
    ppermute x1, starting transfers between devices, body_eight(): low_o = lax.ppermute(jnp.where(z == 0, kv_give, block), 'seq', pairs)  5.45 us
  transfers between devices with their start and end apart: 24, of which 10 were waited for; matrix products, arithmetic and copies ran while one was open for 4% of the time, Pallas kernels for 20%

profile of v19, /device:TPU:16, one launch (start us, length us, event | category | flops | bytes accessed | tf_op | source)
XLA Modules:
  0.0 183.8 jit_solution(2010769781287319243)
XLA Ops:
  0.0 2.3 %dynamic-slice_bitcast_fusion.2 = (bf16[1,512,512]{2,1,0:T(8,128)(2,1)}, bf16[1,512,512]{2,1,0:T(8,128)(2,1)}) fusion(bf16[3,1,512,1024]{3,2,1,0:T(8,128)(2,1)} %param.2, s32[]{:T(128)S(6)} %select_n.63, s32[]{:T(128)S(6)} %select_n.62), kind=kLoop, calls=%fused_computation.7 | loop fusion | bytes 2097160 | tf_op jit(solution)/shard_map/dynamic_slice | solution.py:471
  2.3 2.3 %collective-permute-start = (bf16[1,512,512]{2,1,0:T(8,128)(2,1)}, bf16[1,512,512]{2,1,0:T(8,128)(2,1)}, u32[]{:S(2)}, u32[]{:S(2)}) collective-permute-start(bf16[1,512,512]{2,1,0:T(8,128)(2,1)} %get-tuple-element.66.q_m), channel_id=1, source_target_pairs={{16,8},{20,12},{24,16},{28,20},{17,9},{21,13},{25,17},{29,21},{18,... | collective-permute-start | bytes 1572872 | tf_op jit(solution)/shard_map/ppermute | solution.py:462
  4.7 1.6 collective-permute-start.1
  6.2 1.5 collective-permute-start.3
  7.7 4.2 %broadcast_select_fusion = (bf16[2,512,512]{2,1,0:T(8,128)(2,1)}, bf16[2,512,512]{2,1,0:T(8,128)(2,1)}, bf16[2,512,512]{2,1,0:T(8,128)(2,1)}, bf16[2,512,512]{2,1,0:T(8,128)(2,1)}) fusion(bf16[2,512,512]{2,1,0:T(8,128)(2,1)S(1)} %bitcast.26, pred[]{:T(512)S(6)} %eq.14, bf16[3,1,512,1024]{3,2,1,0:T(8,128)(2,1)} %param.2, s32[]{:T(128)S(6)} %select_n.63, ...), kind=kLoop, calls=%fused_computation.5 | loop fusion | flops 1048576 | bytes 7340041 | tf_op jit(solution)/shard_map/jit(_where)/select_n | solution.py:481
  12.6 5.5 %collective-permute-start.7 = (bf16[2,512,512]{2,1,0:T(8,128)(2,1)}, bf16[2,512,512]{2,1,0:T(8,128)(2,1)S(1)}, u32[]{:S(2)}, u32[]{:S(2)}) collective-permute-start(bf16[2,512,512]{2,1,0:T(8,128)(2,1)} %get-tuple-element.59), channel_id=1, source_target_pairs={{0,12},{4,8},{8,0},{12,4},{16,24},{20,28},{1,13},{5,9},{9,1},{13,5... | collective-permute-start | bytes 3145736 | tf_op jit(solution)/shard_map/ppermute | solution.py:481
  19.3 1.5 collective-permute-start.5
  20.8 1.9 %collective-permute-start.2 = (bf16[1,512,512]{2,1,0:T(8,128)(2,1)}, bf16[1,512,512]{2,1,0:T(8,128)(2,1)S(1)}, u32[]{:S(2)}, u32[]{:S(2)}) collective-permute-start(bf16[1,512,512]{2,1,0:T(8,128)(2,1)} %collective-permute-done.1.q_o), channel_id=1, source_target_pairs={{16,8},{20,12},{24,16},{28,20},{17,9},{21,13},{25,17},{29,21},{18,... | collective-permute-start | bytes 1572872 | tf_op jit(solution)/shard_map/ppermute | solution.py:462
  23.5 18.3 %collective-permute-done.2.qa_o = bf16[1,512,512]{2,1,0:T(8,128)(2,1)S(1)} collective-permute-done((bf16[1,512,512]{2,1,0:T(8,128)(2,1)}, bf16[1,512,512]{2,1,0:T(8,128)(2,1)S(1)}, u32[]{:S(2)}, u32[]{:S(2)}) %collective-permute-start.2) | collective-permute-done | bytes 524320 | tf_op jit(solution)/shard_map/ppermute | solution.py:462
  44.7 7.4 %collective-permute-start.16 = (bf16[1024,512]{1,0:T(8,128)(2,1)S(1)}, bf16[1024,512]{1,0:T(8,128)(2,1)}, u32[]{:S(2)}, u32[]{:S(2)}) collective-permute-start(bf16[1024,512]{1,0:T(8,128)(2,1)S(1)} %copy-done), channel_id=1, source_target_pairs={{16,0},{20,4},{24,8},{28,12},{17,1},{21,5},{25,9},{29,13},{18,2},{... | collective-permute-start | bytes 3145736 | tf_op jit(solution)/shard_map/ppermute | solution.py:462
  52.2 10.1 %collective-permute-done.7.refs_1_ = bf16[2,512,512]{2,1,0:T(8,128)(2,1)S(1)} collective-permute-done((bf16[2,512,512]{2,1,0:T(8,128)(2,1)}, bf16[2,512,512]{2,1,0:T(8,128)(2,1)S(1)}, u32[]{:S(2)}, u32[]{:S(2)}) %collective-permute-start.7) | collective-permute-done | bytes 1048608 | tf_op jit(solution)/shard_map/ppermute | solution.py:481
  65.6 6.0 %upper_rows.2 = (bf16[528,512]{1,0:T(8,128)(2,1)}, bf16[528,512]{1,0:T(8,128)(2,1)}) custom-call(s32[4]{0:T(128)S(1)} %pad_add_fusion.at, bf16[1,512,512]{2,1,0:T(8,128)(2,1)} %collective-permute-done.qa_m, bf16[1,512,512]{2,1,0:T(8,128)(2,1)S(1)} %copy-done.5, bf16[1,512,512]{2,1,0:T(8,128)(2,1)} %collective-permute-done.3.qb_m, ...), custom_call_target="tpu_custom_call" | custom-call | flops 700000000 | bytes 1024 | tf_op jit(solution)/shard_map/upper_rows/pallas_call | solution.py:335
  71.6 2.8 %collective-permute-start.8 = (bf16[528,512]{1,0:T(8,128)(2,1)}, bf16[528,512]{1,0:T(8,128)(2,1)}, u32[]{:S(2)}, u32[]{:S(2)}) collective-permute-start(bf16[528,512]{1,0:T(8,128)(2,1)} %get-tuple-element.33), channel_id=1, source_target_pairs={{8,16},{12,20},{16,24},{20,28},{9,17},{13,21},{17,25},{21,29},{10,... | collective-permute-start | bytes 1622024 | tf_op jit(solution)/shard_map/ppermute | solution.py:462
  75.7 6.0 %upper_rows.3 = (bf16[528,512]{1,0:T(8,128)(2,1)S(1)}, bf16[528,512]{1,0:T(8,128)(2,1)}) custom-call(s32[4]{0:T(128)S(1)} %pad_add_fusion.at, bf16[1,512,512]{2,1,0:T(8,128)(2,1)} %collective-permute-done.qa_m, bf16[1,512,512]{2,1,0:T(8,128)(2,1)S(1)} %copy-done.5, bf16[1,512,512]{2,1,0:T(8,128)(2,1)} %collective-permute-done.3.qb_m, ...), custom_call_target="tpu_custom_call" | custom-call | flops 700000000 | bytes 1024 | tf_op jit(solution)/shard_map/upper_rows/pallas_call | solution.py:335
  85.1 7.6 %own_rows.2.own = bf16[528,512]{1,0:T(8,128)(2,1)S(1)} custom-call(s32[4]{0:T(128)S(1)} %pad_add_fusion.at, bf16[1,512,512]{2,1,0:T(8,128)(2,1)} %get-tuple-element.66.q_m, bf16[1,512,512]{2,1,0:T(8,128)(2,1)} %collective-permute-done.1.q_o, bf16[2,512,512]{2,1,0:T(8,128)(2,1)S(1)} %copy-done.2, bf16[2,512,512]{2,1,0:T(8,128)(2,1)} %collective-permute-done.5.kv_o, ...), custom_call_target="tpu_custom_call" | custom-call | flops 600000000 | bytes 1024 | tf_op jit(solution)/shard_map/own_rows/pallas_call | solution.py:335
  94.1 3.5 %collective-permute-start.17 = (bf16[528,512]{1,0:T(8,128)(2,1)S(1)}, bf16[528,512]{1,0:T(8,128)(2,1)S(1)}, u32[]{:S(2)}, u32[]{:S(2)}) collective-permute-start(bf16[528,512]{1,0:T(8,128)(2,1)S(1)} %copy-done.9), channel_id=1, source_target_pairs={{8,16},{12,20},{16,24},{20,28},{9,17},{13,21},{17,25},{21,29},{10,... | collective-permute-start | bytes 1622024 | tf_op jit(solution)/shard_map/ppermute | solution.py:462
  97.6 3.7 %merge.2 = bf16[2,256,512]{2,1,0:T(8,128)(2,1)S(1)} custom-call(s32[4]{0:T(128)S(1)} %pad_add_fusion.at, bf16[528,512]{1,0:T(8,128)(2,1)S(1)} %own_rows.2.own, bf16[528,512]{1,0:T(8,128)(2,1)} %collective-permute-done.8.oa, bf16[528,512]{1,0:T(8,128)(2,1)} %collective-permute-done.9.ob), custom_call_target="tpu_custom_call" | custom-call | flops 200000000 | bytes 1024 | tf_op jit(solution)/shard_map/merge/pallas_call | solution.py:335
  101.9 7.6 %own_rows.3.own = bf16[528,512]{1,0:T(8,128)(2,1)S(1)} custom-call(s32[4]{0:T(128)S(1)} %pad_add_fusion.at, bf16[1,512,512]{2,1,0:T(8,128)(2,1)} %get-tuple-element.66.q_m, bf16[1,512,512]{2,1,0:T(8,128)(2,1)} %collective-permute-done.1.q_o, bf16[2,512,512]{2,1,0:T(8,128)(2,1)S(1)} %copy-done.3, bf16[2,512,512]{2,1,0:T(8,128)(2,1)} %collective-permute-done.5.kv_o, ...), custom_call_target="tpu_custom_call" | custom-call | flops 600000000 | bytes 1024 | tf_op jit(solution)/shard_map/own_rows/pallas_call | solution.py:335
  113.0 8.6 %collective-permute-start.19 = (bf16[1024,512]{1,0:T(8,128)(2,1)S(1)}, bf16[1024,512]{1,0:T(8,128)(2,1)S(1)}, u32[]{:S(2)}, u32[]{:S(2)}) collective-permute-start(bf16[1024,512]{1,0:T(8,128)(2,1)S(1)} %fusion.refs_4_), channel_id=1, source_target_pairs={{0,8},{4,12},{8,0},{12,4},{16,24},{20,28},{24,16},{28,20},{1,9},{5... | collective-permute-start | bytes 3145736 | tf_op jit(solution)/shard_map/ppermute | solution.py:462
  122.0 1.8 project.2
  123.8 4.8 %collective-permute-done.17.oa = bf16[528,512]{1,0:T(8,128)(2,1)S(1)} collective-permute-done((bf16[528,512]{1,0:T(8,128)(2,1)S(1)}, bf16[528,512]{1,0:T(8,128)(2,1)S(1)}, u32[]{:S(2)}, u32[]{:S(2)}) %collective-permute-start.17) | collective-permute-done | bytes 540704 | tf_op jit(solution)/shard_map/ppermute | solution.py:462
  128.7 3.6 %merge.3 = bf16[2,256,512]{2,1,0:T(8,128)(2,1)S(1)} custom-call(s32[4]{0:T(128)S(1)} %pad_add_fusion.at, bf16[528,512]{1,0:T(8,128)(2,1)S(1)} %own_rows.3.own, bf16[528,512]{1,0:T(8,128)(2,1)S(1)} %collective-permute-done.17.oa, bf16[528,512]{1,0:T(8,128)(2,1)} %collective-permute-done.11.ob), custom_call_target="tpu_custom_call" | custom-call | flops 200000000 | bytes 1024 | tf_op jit(solution)/shard_map/merge/pallas_call | solution.py:335
  133.6 1.6 collective-permute-start.14
  135.1 6.4 %collective-permute-done.14.got = bf16[2,2,64,512]{3,2,1,0:T(8,128)(2,1)S(1)} collective-permute-done((bf16[2,2,64,512]{3,2,1,0:T(8,128)(2,1)S(1)}, bf16[2,2,64,512]{3,2,1,0:T(8,128)(2,1)S(1)}, u32[]{:S(2)}, u32[]{:S(2)}) %collective-permute-start.14) | collective-permute-done | bytes 262176 | tf_op jit(solution)/shard_map/ppermute | solution.py:468
  142.2 4.0 %collective-permute-done.18 = bf16[2,256,512]{2,1,0:T(8,128)(2,1)S(1)} collective-permute-done((bf16[2,256,512]{2,1,0:T(8,128)(2,1)S(1)}, bf16[2,256,512]{2,1,0:T(8,128)(2,1)S(1)}, u32[]{:S(2)}, u32[]{:S(2)}) %collective-permute-start.18) | collective-permute-done | bytes 524320 | tf_op jit(solution)/shard_map/ppermute | solution.py:462
  146.2 3.9 %collective-permute-done.19.refs_5_ = bf16[1024,512]{1,0:T(8,128)(2,1)S(1)} collective-permute-done((bf16[1024,512]{1,0:T(8,128)(2,1)S(1)}, bf16[1024,512]{1,0:T(8,128)(2,1)S(1)}, u32[]{:S(2)}, u32[]{:S(2)}) %collective-permute-start.19) | collective-permute-done | bytes 1048608 | tf_op jit(solution)/shard_map/ppermute | solution.py:462
  150.1 4.0 %project.3 = (bf16[6,2,2,64,512]{4,3,2,1,0:T(8,128)(2,1)S(1)}, bf16[6,2,2,64,512]{4,3,2,1,0:T(8,128)(2,1)S(1)}) custom-call(s32[4]{0:T(128)S(1)} %pad_add_fusion.at, bf16[2,2,2,64,512]{4,3,2,1,0:T(8,128)(2,1)S(1)} %bitcast.29, bf16[2,2,2,64,512]{4,3,2,1,0:T(8,128)(2,1)S(1)} %bitcast.32, bf16[1024,512]{1,0:T(8,128)(2,1)S(1)} %copy-done, ...), custom_call_target="tpu_custom_call" | custom-call | flops 600000000 | bytes 1024 | tf_op jit(solution)/shard_map/project/pallas_call | solution.py:385
  154.1 3.4 %collective-permute-done.20.got = bf16[6,2,2,64,512]{4,3,2,1,0:T(8,128)(2,1)S(1)} collective-permute-done((bf16[6,2,2,64,512]{4,3,2,1,0:T(8,128)(2,1)S(1)}, bf16[6,2,2,64,512]{4,3,2,1,0:T(8,128)(2,1)S(1)}, u32[]{:S(2)}, u32[]{:S(2)}) %collective-permute-start.20) | collective-permute-done | bytes 1572896 | tf_op jit(solution)/shard_map/ppermute | solution.py:468
  158.4 1.6 collective-permute-start.21
  160.5 1.4 collective-permute-start.23
  162.5 19.6 %collective-permute-done.15.refs_1_ = bf16[2,64,512]{2,1,0:T(8,128)(2,1)S(1)} collective-permute-done((bf16[2,64,512]{2,1,0:T(8,128)(2,1)S(1)}, bf16[2,64,512]{2,1,0:T(8,128)(2,1)S(1)}, u32[]{:S(2)}, u32[]{:S(2)}) %collective-permute-start.15) | collective-permute-done | bytes 131104 | tf_op jit(solution)/shard_map/ppermute | solution.py:462
  182.1 1.7 place.1
  (55 shorter events, 23.5 us)
Async XLA Ops:
  0.0 7.7 %copy-start = (bf16[1024,512]{1,0:T(8,128)(2,1)S(1)}, bf16[1024,512]{1,0:T(8,128)(2,1)}, u32[]{:S(2)}) copy-start(bf16[1024,512]{1,0:T(8,128)(2,1)} %refs_2_.7) | copy-start | bytes 3145732
  2.3 17.0 %collective-permute-start = (bf16[1,512,512]{2,1,0:T(8,128)(2,1)}, bf16[1,512,512]{2,1,0:T(8,128)(2,1)}, u32[]{:S(2)}, u32[]{:S(2)}) collective-permute-start(bf16[1,512,512]{2,1,0:T(8,128)(2,1)} %get-tuple-element.66.q_m), channel_id=1, source_target_pairs={{16,8},{20,12},{24,16},{28,20},{17,9},{21,13},{25,17},{29,21},{18,... | collective-permute-start | bytes 1572872 | tf_op jit(solution)/shard_map/ppermute | solution.py:462
  4.7 14.7 %collective-permute-start.1 = (bf16[1,512,512]{2,1,0:T(8,128)(2,1)}, bf16[1,512,512]{2,1,0:T(8,128)(2,1)}, u32[]{:S(2)}, u32[]{:S(2)}) collective-permute-start(bf16[1,512,512]{2,1,0:T(8,128)(2,1)} %get-tuple-element.65), channel_id=1, source_target_pairs={{0,4},{4,0},{8,12},{12,8},{16,20},{20,16},{24,28},{28,24},{1,5},{5... | collective-permute-start | bytes 1572872 | tf_op jit(solution)/shard_map/ppermute | solution.py:462
  6.2 16.5 %collective-permute-start.3 = (bf16[1,512,512]{2,1,0:T(8,128)(2,1)}, bf16[1,512,512]{2,1,0:T(8,128)(2,1)}, u32[]{:S(2)}, u32[]{:S(2)}) collective-permute-start(bf16[1,512,512]{2,1,0:T(8,128)(2,1)} %get-tuple-element.66.q_m), channel_id=1, source_target_pairs={{24,8},{28,12},{25,9},{29,13},{26,10},{30,14},{27,11},{31,15}} | collective-permute-start | bytes 1572872 | tf_op jit(solution)/shard_map/ppermute | solution.py:462
  11.9 40.3 %collective-permute-start.6 = (bf16[2,512,512]{2,1,0:T(8,128)(2,1)}, bf16[2,512,512]{2,1,0:T(8,128)(2,1)S(1)}, u32[]{:S(2)}, u32[]{:S(2)}) collective-permute-start(bf16[2,512,512]{2,1,0:T(8,128)(2,1)} %get-tuple-element.63), channel_id=1, source_target_pairs={{0,8},{4,12},{8,24},{12,28},{1,9},{5,13},{9,25},{13,29},{2,10},{6,... | collective-permute-start | bytes 3145736 | tf_op jit(solution)/shard_map/ppermute | solution.py:462
  12.6 49.6 %collective-permute-start.7 = (bf16[2,512,512]{2,1,0:T(8,128)(2,1)}, bf16[2,512,512]{2,1,0:T(8,128)(2,1)S(1)}, u32[]{:S(2)}, u32[]{:S(2)}) collective-permute-start(bf16[2,512,512]{2,1,0:T(8,128)(2,1)} %get-tuple-element.59), channel_id=1, source_target_pairs={{0,12},{4,8},{8,0},{12,4},{16,24},{20,28},{1,13},{5,9},{9,1},{13,5... | collective-permute-start | bytes 3145736 | tf_op jit(solution)/shard_map/ppermute | solution.py:481
  19.3 42.9 %collective-permute-start.5 = (bf16[2,512,512]{2,1,0:T(8,128)(2,1)}, bf16[2,512,512]{2,1,0:T(8,128)(2,1)}, u32[]{:S(2)}, u32[]{:S(2)}) collective-permute-start(bf16[2,512,512]{2,1,0:T(8,128)(2,1)} %get-tuple-element.32), channel_id=1, source_target_pairs={{0,4},{4,0},{8,12},{12,8},{16,20},{20,16},{24,28},{28,24},{1,5},{5... | collective-permute-start | bytes 3145736 | tf_op jit(solution)/shard_map/ppermute | solution.py:462
  20.8 20.9 %collective-permute-start.2 = (bf16[1,512,512]{2,1,0:T(8,128)(2,1)}, bf16[1,512,512]{2,1,0:T(8,128)(2,1)S(1)}, u32[]{:S(2)}, u32[]{:S(2)}) collective-permute-start(bf16[1,512,512]{2,1,0:T(8,128)(2,1)} %collective-permute-done.1.q_o), channel_id=1, source_target_pairs={{16,8},{20,12},{24,16},{28,20},{17,9},{21,13},{25,17},{29,21},{18,... | collective-permute-start | bytes 1572872 | tf_op jit(solution)/shard_map/ppermute | solution.py:462
  22.8 19.8 %collective-permute-start.4 = (bf16[1,512,512]{2,1,0:T(8,128)(2,1)}, bf16[1,512,512]{2,1,0:T(8,128)(2,1)S(1)}, u32[]{:S(2)}, u32[]{:S(2)}) collective-permute-start(bf16[1,512,512]{2,1,0:T(8,128)(2,1)} %collective-permute-done.1.q_o), channel_id=1, source_target_pairs={{24,8},{28,12},{25,9},{29,13},{26,10},{30,14},{27,11},{31,15}} | collective-permute-start | bytes 1572872 | tf_op jit(solution)/shard_map/ppermute | solution.py:462
  41.7 0.8 copy-start.4
  43.4 58.5 %collective-permute-start.12 = (bf16[1024,512]{1,0:T(8,128)(2,1)S(1)}, bf16[1024,512]{1,0:T(8,128)(2,1)}, u32[]{:S(2)}, u32[]{:S(2)}) collective-permute-start(bf16[1024,512]{1,0:T(8,128)(2,1)S(1)} %copy-done), channel_id=1, source_target_pairs={{0,16},{4,20},{1,17},{5,21},{2,18},{6,22},{3,19},{7,23}} | collective-permute-start | bytes 3145736 | tf_op jit(solution)/shard_map/ppermute | solution.py:462
  44.7 64.8 %collective-permute-start.16 = (bf16[1024,512]{1,0:T(8,128)(2,1)S(1)}, bf16[1024,512]{1,0:T(8,128)(2,1)}, u32[]{:S(2)}, u32[]{:S(2)}) collective-permute-start(bf16[1024,512]{1,0:T(8,128)(2,1)S(1)} %copy-done), channel_id=1, source_target_pairs={{16,0},{20,4},{24,8},{28,12},{17,1},{21,5},{25,9},{29,13},{18,2},{... | collective-permute-start | bytes 3145736 | tf_op jit(solution)/shard_map/ppermute | solution.py:462
  62.3 1.2 copy-start.1
  63.5 1.0 copy-start.5
  64.5 1.0 copy-start.7
  71.6 22.5 %collective-permute-start.8 = (bf16[528,512]{1,0:T(8,128)(2,1)}, bf16[528,512]{1,0:T(8,128)(2,1)}, u32[]{:S(2)}, u32[]{:S(2)}) collective-permute-start(bf16[528,512]{1,0:T(8,128)(2,1)} %get-tuple-element.33), channel_id=1, source_target_pairs={{8,16},{12,20},{16,24},{20,28},{9,17},{13,21},{17,25},{21,29},{10,... | collective-permute-start | bytes 1622024 | tf_op jit(solution)/shard_map/ppermute | solution.py:462
  74.4 23.2 %collective-permute-start.9 = (bf16[528,512]{1,0:T(8,128)(2,1)}, bf16[528,512]{1,0:T(8,128)(2,1)}, u32[]{:S(2)}, u32[]{:S(2)}) collective-permute-start(bf16[528,512]{1,0:T(8,128)(2,1)} %get-tuple-element.38), channel_id=1, source_target_pairs={{8,24},{12,28},{0,8},{4,12},{24,16},{28,20},{9,25},{13,29},{1,9},{... | collective-permute-start | bytes 1622024 | tf_op jit(solution)/shard_map/ppermute | solution.py:462
  82.5 27.0 %collective-permute-start.11 = (bf16[528,512]{1,0:T(8,128)(2,1)}, bf16[528,512]{1,0:T(8,128)(2,1)}, u32[]{:S(2)}, u32[]{:S(2)}) collective-permute-start(bf16[528,512]{1,0:T(8,128)(2,1)} %get-tuple-element.39), channel_id=1, source_target_pairs={{8,24},{12,28},{0,8},{4,12},{24,16},{28,20},{9,25},{13,29},{1,9},{... | collective-permute-start | bytes 1622024 | tf_op jit(solution)/shard_map/ppermute | solution.py:462
  83.8 1.2 copy-start.2
  85.1 9.0 %copy-start.9 = (bf16[528,512]{1,0:T(8,128)(2,1)S(1)}, bf16[528,512]{1,0:T(8,128)(2,1)}, u32[]{:S(2)}) copy-start(bf16[528,512]{1,0:T(8,128)(2,1)} %copy-done.8) | copy-start | bytes 1622020
  92.7 9.2 %copy-start.3 = (bf16[2,512,512]{2,1,0:T(8,128)(2,1)S(1)}, bf16[2,512,512]{2,1,0:T(8,128)(2,1)}, u32[]{:S(2)}) copy-start(bf16[2,512,512]{2,1,0:T(8,128)(2,1)} %get-tuple-element.64.kv_m) | copy-start | bytes 3145732
  94.1 34.6 %collective-permute-start.17 = (bf16[528,512]{1,0:T(8,128)(2,1)S(1)}, bf16[528,512]{1,0:T(8,128)(2,1)S(1)}, u32[]{:S(2)}, u32[]{:S(2)}) collective-permute-start(bf16[528,512]{1,0:T(8,128)(2,1)S(1)} %copy-done.9), channel_id=1, source_target_pairs={{8,16},{12,20},{16,24},{20,28},{9,17},{13,21},{17,25},{21,29},{10,... | collective-permute-start | bytes 1622024 | tf_op jit(solution)/shard_map/ppermute | solution.py:462
  101.3 20.7 %collective-permute-start.10 = (bf16[2,256,512]{2,1,0:T(8,128)(2,1)S(1)}, bf16[2,256,512]{2,1,0:T(8,128)(2,1)S(1)}, u32[]{:S(2)}, u32[]{:S(2)}) collective-permute-start(bf16[2,256,512]{2,1,0:T(8,128)(2,1)S(1)} %merge.2), channel_id=1, source_target_pairs={{0,4},{4,0},{8,12},{12,8},{16,20},{20,16},{24,28},{28,24},{1,5},{5... | collective-permute-start | bytes 1572872 | tf_op jit(solution)/shard_map/ppermute | solution.py:462
  113.0 37.0 %collective-permute-start.19 = (bf16[1024,512]{1,0:T(8,128)(2,1)S(1)}, bf16[1024,512]{1,0:T(8,128)(2,1)S(1)}, u32[]{:S(2)}, u32[]{:S(2)}) collective-permute-start(bf16[1024,512]{1,0:T(8,128)(2,1)S(1)} %fusion.refs_4_), channel_id=1, source_target_pairs={{0,8},{4,12},{8,0},{12,4},{16,24},{20,28},{24,16},{28,20},{1,9},{5... | collective-permute-start | bytes 3145736 | tf_op jit(solution)/shard_map/ppermute | solution.py:462
  123.8 9.1 %collective-permute-start.13 = (bf16[2,2,2,64,512]{4,3,2,1,0:T(8,128)(2,1)S(1)}, bf16[2,2,2,64,512]{4,3,2,1,0:T(8,128)(2,1)S(1)}, u32[]{:S(2)}, u32[]{:S(2)}) collective-permute-start(bf16[2,2,2,64,512]{4,3,2,1,0:T(8,128)(2,1)S(1)} %get-tuple-element.45), channel_id=1, source_target_pairs={{0,1},{1,0},{2,3},{3,2},{4,5},{5,4},{6,7},{7,6},{8,9},{9,8},{10,11... | collective-permute-start | bytes 1572872 | tf_op jit(solution)/shard_map/ppermute | solution.py:468
  132.3 13.9 %collective-permute-start.18 = (bf16[2,256,512]{2,1,0:T(8,128)(2,1)S(1)}, bf16[2,256,512]{2,1,0:T(8,128)(2,1)S(1)}, u32[]{:S(2)}, u32[]{:S(2)}) collective-permute-start(bf16[2,256,512]{2,1,0:T(8,128)(2,1)S(1)} %merge.3), channel_id=1, source_target_pairs={{0,4},{4,0},{8,12},{12,8},{16,20},{20,16},{24,28},{28,24},{1,5},{5... | collective-permute-start | bytes 1572872 | tf_op jit(solution)/shard_map/ppermute | solution.py:462
  133.6 8.0 %collective-permute-start.14 = (bf16[2,2,64,512]{3,2,1,0:T(8,128)(2,1)S(1)}, bf16[2,2,64,512]{3,2,1,0:T(8,128)(2,1)S(1)}, u32[]{:S(2)}, u32[]{:S(2)}) collective-permute-start(bf16[2,2,64,512]{3,2,1,0:T(8,128)(2,1)S(1)} %get-tuple-element.47), channel_id=1, source_target_pairs={{0,2},{1,3},{2,0},{3,1},{4,6},{5,7},{6,4},{7,5},{8,10},{9,11},{10,... | collective-permute-start | bytes 786440 | tf_op jit(solution)/shard_map/ppermute | solution.py:468
  154.0 3.5 %collective-permute-start.20 = (bf16[6,2,2,64,512]{4,3,2,1,0:T(8,128)(2,1)S(1)}, bf16[6,2,2,64,512]{4,3,2,1,0:T(8,128)(2,1)S(1)}, u32[]{:S(2)}, u32[]{:S(2)}) collective-permute-start(bf16[6,2,2,64,512]{4,3,2,1,0:T(8,128)(2,1)S(1)} %get-tuple-element.54), channel_id=1, source_target_pairs={{0,1},{1,0},{2,3},{3,2},{4,5},{5,4},{6,7},{7,6},{8,9},{9,8},{10,11... | collective-permute-start | bytes 4718600 | tf_op jit(solution)/shard_map/ppermute | solution.py:468
  158.4 23.7 %collective-permute-start.21 = (bf16[6,64,512]{2,1,0:T(8,128)(2,1)S(1)}, bf16[6,64,512]{2,1,0:T(8,128)(2,1)S(1)}, u32[]{:S(2)}, u32[]{:S(2)}) collective-permute-start(bf16[6,64,512]{2,1,0:T(8,128)(2,1)S(1)} %get-tuple-element.56), channel_id=1, source_target_pairs={{0,2},{1,3},{2,0},{3,1},{4,6},{5,7},{6,4},{7,5},{8,10},{9,11},{10,... | collective-permute-start | bytes 1179656 | tf_op jit(solution)/shard_map/ppermute | solution.py:468
  160.0 22.1 %collective-permute-start.22 = (bf16[6,64,512]{2,1,0:T(8,128)(2,1)S(1)}, bf16[6,64,512]{2,1,0:T(8,128)(2,1)S(1)}, u32[]{:S(2)}, u32[]{:S(2)}) collective-permute-start(bf16[6,64,512]{2,1,0:T(8,128)(2,1)S(1)} %get-tuple-element.57), channel_id=1, source_target_pairs={{0,4},{4,0},{8,12},{12,8},{16,20},{20,16},{24,28},{28,24},{1,5},{5... | collective-permute-start | bytes 1179656 | tf_op jit(solution)/shard_map/ppermute | solution.py:462
  160.5 21.6 %collective-permute-start.23 = (bf16[6,64,512]{2,1,0:T(8,128)(2,1)S(1)}, bf16[6,64,512]{2,1,0:T(8,128)(2,1)S(1)}, u32[]{:S(2)}, u32[]{:S(2)}) collective-permute-start(bf16[6,64,512]{2,1,0:T(8,128)(2,1)S(1)} %get-tuple-element.58), channel_id=1, source_target_pairs={{0,6},{1,7},{2,4},{3,5},{4,2},{5,3},{6,0},{7,1},{8,14},{9,15},{10,... | collective-permute-start | bytes 1179656 | tf_op jit(solution)/shard_map/ppermute | solution.py:544
  162.0 20.1 %collective-permute-start.15 = (bf16[2,64,512]{2,1,0:T(8,128)(2,1)S(1)}, bf16[2,64,512]{2,1,0:T(8,128)(2,1)S(1)}, u32[]{:S(2)}, u32[]{:S(2)}) collective-permute-start(bf16[2,64,512]{2,1,0:T(8,128)(2,1)S(1)} %get-tuple-element.49), channel_id=1, source_target_pairs={{0,4},{4,0},{8,12},{12,8},{16,20},{20,16},{24,28},{28,24},{1,5},{5... | collective-permute-start | bytes 393224 | tf_op jit(solution)/shard_map/ppermute | solution.py:462
  (2 other events, 1.6 us)

commit v20 on v19

--- a/solution.py
+++ b/solution.py
@@ -481,7 +481,6 @@
     low_o = lax.ppermute(jnp.where(z == 0, kv_give, block), "seq", pairs)
     kv_o = swap(after(kv_give, q_o, qs[0]))
     qs[1], qs[3] = seq_perm(q_o, *down), seq_perm(q_o, *two_down)
-    w_second = seq_perm(after(out_weight, *qs), (0, 2))
 
     struct = jax.ShapeDtypeStruct
     partial = struct((2 * tokens + LSE_ROWS, half), BF16)
@@ -502,7 +501,7 @@
         return mine
 
     own.append(own_rows(0, turn))
-    w_down = seq_perm(after(out_weight, *qs), (2, 0), (3, 1))
+    w_down = seq_perm(after(out_weight, *qs), (0, 2), (2, 0), (3, 1))
 
     def merged(c, earlier):
         (a,) = head_call(
@@ -512,9 +511,8 @@
         return a.reshape(shape), swap(a).reshape(shape)
 
     attended = [merged(0, own[0])]
-    own.append(own_rows(1, after(at, attended[0][0], w_second)))
-    ridden = jnp.where(z == 2, w_second, low_m.reshape(out_weight.shape))
-    w_far = jnp.where(z >= 2, ridden, after(w_down, own[1]))
+    w_far = jnp.where(z == 3, low_m.reshape(out_weight.shape), after(w_down, attended[0][0]))
+    own.append(own_rows(1, after(at, w_far)))
     w_other = seq_perm(w_far, (0, 1), (1, 0), (2, 3), (3, 2))
     parts_out, plan = [], []
 

time: 186 us -> 191 us (1.027)
  starting transfers between devices: 48.8 us -> 54.5 us
    ppermute x18 -> x17, waiting for transfers between devices: 53.2 us -> 64.2 us  [seq_perm(): return lax.ppermute(array, 'seq', pairs)]
    ppermute x1, waiting for transfers between devices: 10.1 us -> 0.01 us  [body_eight(): low_o = lax.ppermute(jnp.where(z == 0, kv_give, block), 'seq', pairs)]
    ppermute x18 -> x17, starting transfers between devices: 38.6 us -> 44.5 us  [seq_perm(): return lax.ppermute(array, 'seq', pairs)]
    unnamed x20 -> x18, local copies, waits for them, and re-layouts: 7 us -> 7.01 us
  transfers between devices with their start and end apart: 24 -> 23, of which waited for: 10 -> 10; matrix products, arithmetic and copies ran while one was open for 4% -> 4% of each run, Pallas kernels for 20% -> 20%
where the time goes in v20:
time: 191 us; the launch traced here: 190 us
  waiting for transfers between devices  74 us (39%)
  starting transfers between devices  54.5 us (29%)
  Pallas kernels  44.1 us (23%)
  local copies, waits for them, and re-layouts  11.5 us (6%)
  other arithmetic  5.92 us (3%)
    ppermute x17, waiting for transfers between devices, seq_perm(): return lax.ppermute(array, 'seq', pairs)  64.2 us
    ppermute x17, starting transfers between devices, seq_perm(): return lax.ppermute(array, 'seq', pairs)  44.5 us
    pallas_call x6, Pallas kernels, head_call(): pl.pallas_call(kernel, out_shape=outs, grid_spec=pltpu.PrefetchScalarGrid...  34.5 us
    ppermute x4, waiting for transfers between devices, head_perm(): return lax.ppermute(array, 'head', [(i, i ^ flip) for i in range(4)])  9.84 us
    pallas_call x6, Pallas kernels, whole_call(): pl.pallas_call(kernel, out_shape=outs, in_specs=[pl.BlockSpec(memory_spac...  9.63 us
    unnamed x18, local copies, waits for them, and re-layouts  7.01 us
    ppermute x1, starting transfers between devices, body_eight(): low_o = lax.ppermute(jnp.where(z == 0, kv_give, block), 'seq', pairs)  4.94 us
    select_n x1, other arithmetic, body_eight(): low_o = lax.ppermute(jnp.where(z == 0, kv_give, block), 'seq', pairs)  4.13 us
  transfers between devices with their start and end apart: 23, of which 10 were waited for; matrix products, arithmetic and copies ran while one was open for 4% of the time, Pallas kernels for 20%

profile of v20, /device:TPU:16, one launch (start us, length us, event | category | flops | bytes accessed | tf_op | source)
XLA Modules:
  0.0 190.4 jit_solution(12538053565092510878)
XLA Ops:
  0.0 2.3 %dynamic-slice_bitcast_fusion.2 = (bf16[1,512,512]{2,1,0:T(8,128)(2,1)}, bf16[1,512,512]{2,1,0:T(8,128)(2,1)}) fusion(bf16[3,1,512,1024]{3,2,1,0:T(8,128)(2,1)} %param.2, s32[]{:T(128)S(6)} %select_n.57, s32[]{:T(128)S(6)} %select_n.56), kind=kLoop, calls=%fused_computation.6 | loop fusion | bytes 2097160 | tf_op jit(solution)/shard_map/dynamic_slice | solution.py:471
  2.3 1.5 collective-permute-start.1
  3.8 2.3 %collective-permute-start = (bf16[1,512,512]{2,1,0:T(8,128)(2,1)}, bf16[1,512,512]{2,1,0:T(8,128)(2,1)}, u32[]{:S(2)}, u32[]{:S(2)}) collective-permute-start(bf16[1,512,512]{2,1,0:T(8,128)(2,1)} %get-tuple-element.66.q_m), channel_id=1, source_target_pairs={{16,8},{20,12},{24,16},{28,20},{17,9},{21,13},{25,17},{29,21},{18,... | collective-permute-start | bytes 1572872 | tf_op jit(solution)/shard_map/ppermute | solution.py:462
  6.2 1.5 collective-permute-start.3
  7.7 4.1 %broadcast_select_fusion = (bf16[2,512,512]{2,1,0:T(8,128)(2,1)}, bf16[2,512,512]{2,1,0:T(8,128)(2,1)}, bf16[2,512,512]{2,1,0:T(8,128)(2,1)}, bf16[2,512,512]{2,1,0:T(8,128)(2,1)}) fusion(bf16[2,512,512]{2,1,0:T(8,128)(2,1)S(1)} %bitcast.24, pred[]{:T(512)S(6)} %eq.12, bf16[3,1,512,1024]{3,2,1,0:T(8,128)(2,1)} %param.2, s32[]{:T(128)S(6)} %select_n.57, ...), kind=kLoop, calls=%fused_computation.4 | loop fusion | flops 1048576 | bytes 7340041 | tf_op jit(solution)/shard_map/jit(_where)/select_n | solution.py:481
  11.8 4.9 %collective-permute-start.7 = (bf16[2,512,512]{2,1,0:T(8,128)(2,1)}, bf16[2,512,512]{2,1,0:T(8,128)(2,1)S(1)}, u32[]{:S(2)}, u32[]{:S(2)}) collective-permute-start(bf16[2,512,512]{2,1,0:T(8,128)(2,1)} %get-tuple-element.59), channel_id=1, source_target_pairs={{0,12},{4,8},{8,0},{12,4},{16,24},{20,28},{1,13},{5,9},{9,1},{13,5... | collective-permute-start | bytes 3145736 | tf_op jit(solution)/shard_map/ppermute | solution.py:481
  17.5 3.4 %collective-permute-done.qa_m = bf16[1,512,512]{2,1,0:T(8,128)(2,1)} collective-permute-done((bf16[1,512,512]{2,1,0:T(8,128)(2,1)}, bf16[1,512,512]{2,1,0:T(8,128)(2,1)}, u32[]{:S(2)}, u32[]{:S(2)}) %collective-permute-start) | collective-permute-done | bytes 524320 | tf_op jit(solution)/shard_map/ppermute | solution.py:462
  22.1 21.8 %collective-permute-start.2 = (bf16[1,512,512]{2,1,0:T(8,128)(2,1)}, bf16[1,512,512]{2,1,0:T(8,128)(2,1)S(1)}, u32[]{:S(2)}, u32[]{:S(2)}) collective-permute-start(bf16[1,512,512]{2,1,0:T(8,128)(2,1)} %collective-permute-done.1.q_o), channel_id=1, source_target_pairs={{16,8},{20,12},{24,16},{28,20},{17,9},{21,13},{25,17},{29,21},{18,... | collective-permute-start | bytes 1572872 | tf_op jit(solution)/shard_map/ppermute | solution.py:462
  44.8 20.1 %collective-permute-done.2.qa_o = bf16[1,512,512]{2,1,0:T(8,128)(2,1)S(1)} collective-permute-done((bf16[1,512,512]{2,1,0:T(8,128)(2,1)}, bf16[1,512,512]{2,1,0:T(8,128)(2,1)S(1)}, u32[]{:S(2)}, u32[]{:S(2)}) %collective-permute-start.2) | collective-permute-done | bytes 524320 | tf_op jit(solution)/shard_map/ppermute | solution.py:462
  65.7 1.9 %collective-permute-start.12 = (bf16[1024,512]{1,0:T(8,128)(2,1)S(1)}, bf16[1024,512]{1,0:T(8,128)(2,1)}, u32[]{:S(2)}, u32[]{:S(2)}) collective-permute-start(bf16[1024,512]{1,0:T(8,128)(2,1)S(1)} %copy-done), channel_id=1, source_target_pairs={{0,16},{4,20},{16,0},{20,4},{24,8},{28,12},{1,17},{5,21},{17,1},{2... | collective-permute-start | bytes 3145736 | tf_op jit(solution)/shard_map/ppermute | solution.py:462
  71.1 6.0 %upper_rows.2 = (bf16[528,512]{1,0:T(8,128)(2,1)}, bf16[528,512]{1,0:T(8,128)(2,1)}) custom-call(s32[4]{0:T(128)S(1)} %pad_add_fusion.at, bf16[1,512,512]{2,1,0:T(8,128)(2,1)} %collective-permute-done.qa_m, bf16[1,512,512]{2,1,0:T(8,128)(2,1)S(1)} %copy-done.7, bf16[1,512,512]{2,1,0:T(8,128)(2,1)} %collective-permute-done.3.qb_m, ...), custom_call_target="tpu_custom_call" | custom-call | flops 700000000 | bytes 1024 | tf_op jit(solution)/shard_map/upper_rows/pallas_call | solution.py:335
  78.3 4.9 %collective-permute-start.8 = (bf16[528,512]{1,0:T(8,128)(2,1)}, bf16[528,512]{1,0:T(8,128)(2,1)}, u32[]{:S(2)}, u32[]{:S(2)}) collective-permute-start(bf16[528,512]{1,0:T(8,128)(2,1)} %get-tuple-element.33), channel_id=1, source_target_pairs={{8,16},{12,20},{16,24},{20,28},{9,17},{13,21},{17,25},{21,29},{10,... | collective-permute-start | bytes 1622024 | tf_op jit(solution)/shard_map/ppermute | solution.py:462
  83.3 6.0 %upper_rows.3 = (bf16[528,512]{1,0:T(8,128)(2,1)S(1)}, bf16[528,512]{1,0:T(8,128)(2,1)}) custom-call(s32[4]{0:T(128)S(1)} %pad_add_fusion.at, bf16[1,512,512]{2,1,0:T(8,128)(2,1)} %collective-permute-done.qa_m, bf16[1,512,512]{2,1,0:T(8,128)(2,1)S(1)} %copy-done.7, bf16[1,512,512]{2,1,0:T(8,128)(2,1)} %collective-permute-done.3.qb_m, ...), custom_call_target="tpu_custom_call" | custom-call | flops 700000000 | bytes 1024 | tf_op jit(solution)/shard_map/upper_rows/pallas_call | solution.py:335
  91.4 4.7 %collective-permute-start.16 = (bf16[528,512]{1,0:T(8,128)(2,1)}, bf16[528,512]{1,0:T(8,128)(2,1)S(1)}, u32[]{:S(2)}, u32[]{:S(2)}) collective-permute-start(bf16[528,512]{1,0:T(8,128)(2,1)} %copy-done.8), channel_id=1, source_target_pairs={{8,16},{12,20},{16,24},{20,28},{9,17},{13,21},{17,25},{21,29},{10,... | collective-permute-start | bytes 1622024 | tf_op jit(solution)/shard_map/ppermute | solution.py:462
  97.4 7.6 %own_rows.2.own = bf16[528,512]{1,0:T(8,128)(2,1)S(1)} custom-call(s32[4]{0:T(128)S(1)} %pad_add_fusion.at, bf16[1,512,512]{2,1,0:T(8,128)(2,1)} %get-tuple-element.66.q_m, bf16[1,512,512]{2,1,0:T(8,128)(2,1)} %collective-permute-done.1.q_o, bf16[2,512,512]{2,1,0:T(8,128)(2,1)S(1)} %copy-done.2, bf16[2,512,512]{2,1,0:T(8,128)(2,1)} %collective-permute-done.5.kv_o, ...), custom_call_target="tpu_custom_call" | custom-call | flops 600000000 | bytes 1024 | tf_op jit(solution)/shard_map/own_rows/pallas_call | solution.py:335
  106.2 9.8 %collective-permute-done.8.oa = bf16[528,512]{1,0:T(8,128)(2,1)} collective-permute-done((bf16[528,512]{1,0:T(8,128)(2,1)}, bf16[528,512]{1,0:T(8,128)(2,1)}, u32[]{:S(2)}, u32[]{:S(2)}) %collective-permute-start.8) | collective-permute-done | bytes 540704 | tf_op jit(solution)/shard_map/ppermute | solution.py:462
  116.1 3.7 %merge.2 = bf16[2,256,512]{2,1,0:T(8,128)(2,1)S(1)} custom-call(s32[4]{0:T(128)S(1)} %pad_add_fusion.at, bf16[528,512]{1,0:T(8,128)(2,1)S(1)} %own_rows.2.own, bf16[528,512]{1,0:T(8,128)(2,1)} %collective-permute-done.8.oa, bf16[528,512]{1,0:T(8,128)(2,1)} %collective-permute-done.9.ob), custom_call_target="tpu_custom_call" | custom-call | flops 200000000 | bytes 1024 | tf_op jit(solution)/shard_map/merge/pallas_call | solution.py:335
  120.1 1.3 bitcast_select_fusion.refs_4_
  121.6 7.6 %own_rows.3.own = bf16[528,512]{1,0:T(8,128)(2,1)S(1)} custom-call(s32[4]{0:T(128)S(1)} %pad_add_fusion.at, bf16[1,512,512]{2,1,0:T(8,128)(2,1)} %get-tuple-element.66.q_m, bf16[1,512,512]{2,1,0:T(8,128)(2,1)} %collective-permute-done.1.q_o, bf16[2,512,512]{2,1,0:T(8,128)(2,1)S(1)} %copy-done.3, bf16[2,512,512]{2,1,0:T(8,128)(2,1)} %collective-permute-done.5.kv_o, ...), custom_call_target="tpu_custom_call" | custom-call | flops 600000000 | bytes 1024 | tf_op jit(solution)/shard_map/own_rows/pallas_call | solution.py:335
  131.7 1.9 collective-permute-done.10
  133.6 1.8 project.2
  135.5 3.6 %collective-permute-done.16.oa = bf16[528,512]{1,0:T(8,128)(2,1)S(1)} collective-permute-done((bf16[528,512]{1,0:T(8,128)(2,1)}, bf16[528,512]{1,0:T(8,128)(2,1)S(1)}, u32[]{:S(2)}, u32[]{:S(2)}) %collective-permute-start.16) | collective-permute-done | bytes 540704 | tf_op jit(solution)/shard_map/ppermute | solution.py:462
  139.1 3.6 %merge.3 = bf16[2,256,512]{2,1,0:T(8,128)(2,1)S(1)} custom-call(s32[4]{0:T(128)S(1)} %pad_add_fusion.at, bf16[528,512]{1,0:T(8,128)(2,1)S(1)} %own_rows.3.own, bf16[528,512]{1,0:T(8,128)(2,1)S(1)} %collective-permute-done.16.oa, bf16[528,512]{1,0:T(8,128)(2,1)} %collective-permute-done.11.ob), custom_call_target="tpu_custom_call" | custom-call | flops 200000000 | bytes 1024 | tf_op jit(solution)/shard_map/merge/pallas_call | solution.py:335
  143.7 1.6 collective-permute-start.14
  145.3 6.4 %collective-permute-done.14.got = bf16[2,2,64,512]{3,2,1,0:T(8,128)(2,1)S(1)} collective-permute-done((bf16[2,2,64,512]{3,2,1,0:T(8,128)(2,1)S(1)}, bf16[2,2,64,512]{3,2,1,0:T(8,128)(2,1)S(1)}, u32[]{:S(2)}, u32[]{:S(2)}) %collective-permute-start.14) | collective-permute-done | bytes 262176 | tf_op jit(solution)/shard_map/ppermute | solution.py:468
  152.4 4.2 %collective-permute-done.17 = bf16[2,256,512]{2,1,0:T(8,128)(2,1)S(1)} collective-permute-done((bf16[2,256,512]{2,1,0:T(8,128)(2,1)S(1)}, bf16[2,256,512]{2,1,0:T(8,128)(2,1)S(1)}, u32[]{:S(2)}, u32[]{:S(2)}) %collective-permute-start.17) | collective-permute-done | bytes 524320 | tf_op jit(solution)/shard_map/ppermute | solution.py:462
  156.6 4.0 %project.3 = (bf16[6,2,2,64,512]{4,3,2,1,0:T(8,128)(2,1)S(1)}, bf16[6,2,2,64,512]{4,3,2,1,0:T(8,128)(2,1)S(1)}) custom-call(s32[4]{0:T(128)S(1)} %pad_add_fusion.at, bf16[2,2,2,64,512]{4,3,2,1,0:T(8,128)(2,1)S(1)} %bitcast.27, bf16[2,2,2,64,512]{4,3,2,1,0:T(8,128)(2,1)S(1)} %bitcast.30, bf16[1024,512]{1,0:T(8,128)(2,1)S(1)} %copy-done, ...), custom_call_target="tpu_custom_call" | custom-call | flops 600000000 | bytes 1024 | tf_op jit(solution)/shard_map/project/pallas_call | solution.py:385
  160.7 3.4 %collective-permute-done.19.got = bf16[6,2,2,64,512]{4,3,2,1,0:T(8,128)(2,1)S(1)} collective-permute-done((bf16[6,2,2,64,512]{4,3,2,1,0:T(8,128)(2,1)S(1)}, bf16[6,2,2,64,512]{4,3,2,1,0:T(8,128)(2,1)S(1)}, u32[]{:S(2)}, u32[]{:S(2)}) %collective-permute-start.19) | collective-permute-done | bytes 1572896 | tf_op jit(solution)/shard_map/ppermute | solution.py:468
  165.0 1.6 collective-permute-start.20
  166.8 1.7 collective-permute-start.22
  168.8 19.9 %collective-permute-done.15.refs_1_ = bf16[2,64,512]{2,1,0:T(8,128)(2,1)S(1)} collective-permute-done((bf16[2,64,512]{2,1,0:T(8,128)(2,1)S(1)}, bf16[2,64,512]{2,1,0:T(8,128)(2,1)S(1)}, u32[]{:S(2)}, u32[]{:S(2)}) %collective-permute-start.15) | collective-permute-done | bytes 131104 | tf_op jit(solution)/shard_map/ppermute | solution.py:462
  188.7 1.7 place.1
  (51 shorter events, 19.1 us)
Async XLA Ops:
  0.0 7.7 %copy-start = (bf16[1024,512]{1,0:T(8,128)(2,1)S(1)}, bf16[1024,512]{1,0:T(8,128)(2,1)}, u32[]{:S(2)}) copy-start(bf16[1024,512]{1,0:T(8,128)(2,1)} %refs_2_.7) | copy-start | bytes 3145732
  2.3 15.1 %collective-permute-start.1 = (bf16[1,512,512]{2,1,0:T(8,128)(2,1)}, bf16[1,512,512]{2,1,0:T(8,128)(2,1)}, u32[]{:S(2)}, u32[]{:S(2)}) collective-permute-start(bf16[1,512,512]{2,1,0:T(8,128)(2,1)} %get-tuple-element.65), channel_id=1, source_target_pairs={{0,4},{4,0},{8,12},{12,8},{16,20},{20,16},{24,28},{28,24},{1,5},{5... | collective-permute-start | bytes 1572872 | tf_op jit(solution)/shard_map/ppermute | solution.py:462
  3.8 17.0 %collective-permute-start = (bf16[1,512,512]{2,1,0:T(8,128)(2,1)}, bf16[1,512,512]{2,1,0:T(8,128)(2,1)}, u32[]{:S(2)}, u32[]{:S(2)}) collective-permute-start(bf16[1,512,512]{2,1,0:T(8,128)(2,1)} %get-tuple-element.66.q_m), channel_id=1, source_target_pairs={{16,8},{20,12},{24,16},{28,20},{17,9},{21,13},{25,17},{29,21},{18,... | collective-permute-start | bytes 1572872 | tf_op jit(solution)/shard_map/ppermute | solution.py:462
  6.2 15.9 %collective-permute-start.3 = (bf16[1,512,512]{2,1,0:T(8,128)(2,1)}, bf16[1,512,512]{2,1,0:T(8,128)(2,1)}, u32[]{:S(2)}, u32[]{:S(2)}) collective-permute-start(bf16[1,512,512]{2,1,0:T(8,128)(2,1)} %get-tuple-element.66.q_m), channel_id=1, source_target_pairs={{24,8},{28,12},{25,9},{29,13},{26,10},{30,14},{27,11},{31,15}} | collective-permute-start | bytes 1572872 | tf_op jit(solution)/shard_map/ppermute | solution.py:462
  11.8 56.0 %collective-permute-start.7 = (bf16[2,512,512]{2,1,0:T(8,128)(2,1)}, bf16[2,512,512]{2,1,0:T(8,128)(2,1)S(1)}, u32[]{:S(2)}, u32[]{:S(2)}) collective-permute-start(bf16[2,512,512]{2,1,0:T(8,128)(2,1)} %get-tuple-element.59), channel_id=1, source_target_pairs={{0,12},{4,8},{8,0},{12,4},{16,24},{20,28},{1,13},{5,9},{9,1},{13,5... | collective-permute-start | bytes 3145736 | tf_op jit(solution)/shard_map/ppermute | solution.py:481
  16.7 51.0 %collective-permute-start.6 = (bf16[2,512,512]{2,1,0:T(8,128)(2,1)}, bf16[2,512,512]{2,1,0:T(8,128)(2,1)S(1)}, u32[]{:S(2)}, u32[]{:S(2)}) collective-permute-start(bf16[2,512,512]{2,1,0:T(8,128)(2,1)} %get-tuple-element.63), channel_id=1, source_target_pairs={{0,8},{4,12},{8,24},{12,28},{1,9},{5,13},{9,25},{13,29},{2,10},{6,... | collective-permute-start | bytes 3145736 | tf_op jit(solution)/shard_map/ppermute | solution.py:462
  20.9 46.9 %collective-permute-start.5 = (bf16[2,512,512]{2,1,0:T(8,128)(2,1)}, bf16[2,512,512]{2,1,0:T(8,128)(2,1)}, u32[]{:S(2)}, u32[]{:S(2)}) collective-permute-start(bf16[2,512,512]{2,1,0:T(8,128)(2,1)} %get-tuple-element.32), channel_id=1, source_target_pairs={{0,4},{4,0},{8,12},{12,8},{16,20},{20,16},{24,28},{28,24},{1,5},{5... | collective-permute-start | bytes 3145736 | tf_op jit(solution)/shard_map/ppermute | solution.py:462
  21.4 22.5 %collective-permute-start.4 = (bf16[1,512,512]{2,1,0:T(8,128)(2,1)}, bf16[1,512,512]{2,1,0:T(8,128)(2,1)S(1)}, u32[]{:S(2)}, u32[]{:S(2)}) collective-permute-start(bf16[1,512,512]{2,1,0:T(8,128)(2,1)} %collective-permute-done.1.q_o), channel_id=1, source_target_pairs={{24,8},{28,12},{25,9},{29,13},{26,10},{30,14},{27,11},{31,15}} | collective-permute-start | bytes 1572872 | tf_op jit(solution)/shard_map/ppermute | solution.py:462
  22.1 42.8 %collective-permute-start.2 = (bf16[1,512,512]{2,1,0:T(8,128)(2,1)}, bf16[1,512,512]{2,1,0:T(8,128)(2,1)S(1)}, u32[]{:S(2)}, u32[]{:S(2)}) collective-permute-start(bf16[1,512,512]{2,1,0:T(8,128)(2,1)} %collective-permute-done.1.q_o), channel_id=1, source_target_pairs={{16,8},{20,12},{24,16},{28,20},{17,9},{21,13},{25,17},{29,21},{18,... | collective-permute-start | bytes 1572872 | tf_op jit(solution)/shard_map/ppermute | solution.py:462
  43.9 0.8 copy-start.4
  64.9 0.9 copy-start.6
  65.7 54.4 %collective-permute-start.12 = (bf16[1024,512]{1,0:T(8,128)(2,1)S(1)}, bf16[1024,512]{1,0:T(8,128)(2,1)}, u32[]{:S(2)}, u32[]{:S(2)}) collective-permute-start(bf16[1024,512]{1,0:T(8,128)(2,1)S(1)} %copy-done), channel_id=1, source_target_pairs={{0,16},{4,20},{16,0},{20,4},{24,8},{28,12},{1,17},{5,21},{17,1},{2... | collective-permute-start | bytes 3145736 | tf_op jit(solution)/shard_map/ppermute | solution.py:462
  67.8 1.2 copy-start.1
  69.0 1.0 copy-start.5
  70.0 1.0 copy-start.7
  77.0 29.2 %collective-permute-start.9 = (bf16[528,512]{1,0:T(8,128)(2,1)}, bf16[528,512]{1,0:T(8,128)(2,1)}, u32[]{:S(2)}, u32[]{:S(2)}) collective-permute-start(bf16[528,512]{1,0:T(8,128)(2,1)} %get-tuple-element.38), channel_id=1, source_target_pairs={{8,24},{12,28},{0,8},{4,12},{24,16},{28,20},{9,25},{13,29},{1,9},{... | collective-permute-start | bytes 1622024 | tf_op jit(solution)/shard_map/ppermute | solution.py:462
  78.3 37.7 %collective-permute-start.8 = (bf16[528,512]{1,0:T(8,128)(2,1)}, bf16[528,512]{1,0:T(8,128)(2,1)}, u32[]{:S(2)}, u32[]{:S(2)}) collective-permute-start(bf16[528,512]{1,0:T(8,128)(2,1)} %get-tuple-element.33), channel_id=1, source_target_pairs={{8,16},{12,20},{16,24},{20,28},{9,17},{13,21},{17,25},{21,29},{10,... | collective-permute-start | bytes 1622024 | tf_op jit(solution)/shard_map/ppermute | solution.py:462
  89.3 0.8 copy-start.8
  90.1 39.1 %collective-permute-start.11 = (bf16[528,512]{1,0:T(8,128)(2,1)}, bf16[528,512]{1,0:T(8,128)(2,1)}, u32[]{:S(2)}, u32[]{:S(2)}) collective-permute-start(bf16[528,512]{1,0:T(8,128)(2,1)} %get-tuple-element.39), channel_id=1, source_target_pairs={{8,24},{12,28},{0,8},{4,12},{24,16},{28,20},{9,25},{13,29},{1,9},{... | collective-permute-start | bytes 1622024 | tf_op jit(solution)/shard_map/ppermute | solution.py:462
  91.4 47.7 %collective-permute-start.16 = (bf16[528,512]{1,0:T(8,128)(2,1)}, bf16[528,512]{1,0:T(8,128)(2,1)S(1)}, u32[]{:S(2)}, u32[]{:S(2)}) collective-permute-start(bf16[528,512]{1,0:T(8,128)(2,1)} %copy-done.8), channel_id=1, source_target_pairs={{8,16},{12,20},{16,24},{20,28},{9,17},{13,21},{17,25},{21,29},{10,... | collective-permute-start | bytes 1622024 | tf_op jit(solution)/shard_map/ppermute | solution.py:462
  96.1 1.2 copy-start.2
  119.8 1.8 copy-start.3
  119.8 13.8 %collective-permute-start.10 = (bf16[2,256,512]{2,1,0:T(8,128)(2,1)S(1)}, bf16[2,256,512]{2,1,0:T(8,128)(2,1)S(1)}, u32[]{:S(2)}, u32[]{:S(2)}) collective-permute-start(bf16[2,256,512]{2,1,0:T(8,128)(2,1)S(1)} %merge.2), channel_id=1, source_target_pairs={{0,4},{4,0},{8,12},{12,8},{16,20},{20,16},{24,28},{28,24},{1,5},{5... | collective-permute-start | bytes 1572872 | tf_op jit(solution)/shard_map/ppermute | solution.py:462
  121.5 35.1 %collective-permute-start.18 = (bf16[1024,512]{1,0:T(8,128)(2,1)S(1)}, bf16[1024,512]{1,0:T(8,128)(2,1)S(1)}, u32[]{:S(2)}, u32[]{:S(2)}) collective-permute-start(bf16[1024,512]{1,0:T(8,128)(2,1)S(1)} %bitcast_select_fusion.refs_4_), channel_id=1, source_target_pairs={{0,8},{4,12},{8,0},{12,4},{16,24},{20,28},{24,16},{28,20},{1,9},{5... | collective-permute-start | bytes 3145736 | tf_op jit(solution)/shard_map/ppermute | solution.py:462
  135.4 7.7 %collective-permute-start.13 = (bf16[2,2,2,64,512]{4,3,2,1,0:T(8,128)(2,1)S(1)}, bf16[2,2,2,64,512]{4,3,2,1,0:T(8,128)(2,1)S(1)}, u32[]{:S(2)}, u32[]{:S(2)}) collective-permute-start(bf16[2,2,2,64,512]{4,3,2,1,0:T(8,128)(2,1)S(1)} %get-tuple-element.46), channel_id=1, source_target_pairs={{0,1},{1,0},{2,3},{3,2},{4,5},{5,4},{6,7},{7,6},{8,9},{9,8},{10,11... | collective-permute-start | bytes 1572872 | tf_op jit(solution)/shard_map/ppermute | solution.py:468
  142.7 13.9 %collective-permute-start.17 = (bf16[2,256,512]{2,1,0:T(8,128)(2,1)S(1)}, bf16[2,256,512]{2,1,0:T(8,128)(2,1)S(1)}, u32[]{:S(2)}, u32[]{:S(2)}) collective-permute-start(bf16[2,256,512]{2,1,0:T(8,128)(2,1)S(1)} %merge.3), channel_id=1, source_target_pairs={{0,4},{4,0},{8,12},{12,8},{16,20},{20,16},{24,28},{28,24},{1,5},{5... | collective-permute-start | bytes 1572872 | tf_op jit(solution)/shard_map/ppermute | solution.py:462
  143.7 8.0 %collective-permute-start.14 = (bf16[2,2,64,512]{3,2,1,0:T(8,128)(2,1)S(1)}, bf16[2,2,64,512]{3,2,1,0:T(8,128)(2,1)S(1)}, u32[]{:S(2)}, u32[]{:S(2)}) collective-permute-start(bf16[2,2,64,512]{3,2,1,0:T(8,128)(2,1)S(1)} %get-tuple-element.48), channel_id=1, source_target_pairs={{0,2},{1,3},{2,0},{3,1},{4,6},{5,7},{6,4},{7,5},{8,10},{9,11},{10,... | collective-permute-start | bytes 786440 | tf_op jit(solution)/shard_map/ppermute | solution.py:468
  160.6 3.5 %collective-permute-start.19 = (bf16[6,2,2,64,512]{4,3,2,1,0:T(8,128)(2,1)S(1)}, bf16[6,2,2,64,512]{4,3,2,1,0:T(8,128)(2,1)S(1)}, u32[]{:S(2)}, u32[]{:S(2)}) collective-permute-start(bf16[6,2,2,64,512]{4,3,2,1,0:T(8,128)(2,1)S(1)} %get-tuple-element.54), channel_id=1, source_target_pairs={{0,1},{1,0},{2,3},{3,2},{4,5},{5,4},{6,7},{7,6},{8,9},{9,8},{10,11... | collective-permute-start | bytes 4718600 | tf_op jit(solution)/shard_map/ppermute | solution.py:468
  165.0 23.7 %collective-permute-start.20 = (bf16[6,64,512]{2,1,0:T(8,128)(2,1)S(1)}, bf16[6,64,512]{2,1,0:T(8,128)(2,1)S(1)}, u32[]{:S(2)}, u32[]{:S(2)}) collective-permute-start(bf16[6,64,512]{2,1,0:T(8,128)(2,1)S(1)} %get-tuple-element.56), channel_id=1, source_target_pairs={{0,2},{1,3},{2,0},{3,1},{4,6},{5,7},{6,4},{7,5},{8,10},{9,11},{10,... | collective-permute-start | bytes 1179656 | tf_op jit(solution)/shard_map/ppermute | solution.py:468
  166.6 22.1 %collective-permute-start.21 = (bf16[6,64,512]{2,1,0:T(8,128)(2,1)S(1)}, bf16[6,64,512]{2,1,0:T(8,128)(2,1)S(1)}, u32[]{:S(2)}, u32[]{:S(2)}) collective-permute-start(bf16[6,64,512]{2,1,0:T(8,128)(2,1)S(1)} %get-tuple-element.57), channel_id=1, source_target_pairs={{0,4},{4,0},{8,12},{12,8},{16,20},{20,16},{24,28},{28,24},{1,5},{5... | collective-permute-start | bytes 1179656 | tf_op jit(solution)/shard_map/ppermute | solution.py:462
  166.8 21.8 %collective-permute-start.22 = (bf16[6,64,512]{2,1,0:T(8,128)(2,1)S(1)}, bf16[6,64,512]{2,1,0:T(8,128)(2,1)S(1)}, u32[]{:S(2)}, u32[]{:S(2)}) collective-permute-start(bf16[6,64,512]{2,1,0:T(8,128)(2,1)S(1)} %get-tuple-element.58), channel_id=1, source_target_pairs={{0,6},{1,7},{2,4},{3,5},{4,2},{5,3},{6,0},{7,1},{8,14},{9,15},{10,... | collective-permute-start | bytes 1179656 | tf_op jit(solution)/shard_map/ppermute | solution.py:542
  168.5 20.1 %collective-permute-start.15 = (bf16[2,64,512]{2,1,0:T(8,128)(2,1)S(1)}, bf16[2,64,512]{2,1,0:T(8,128)(2,1)S(1)}, u32[]{:S(2)}, u32[]{:S(2)}) collective-permute-start(bf16[2,64,512]{2,1,0:T(8,128)(2,1)S(1)} %get-tuple-element.50), channel_id=1, source_target_pairs={{0,4},{4,0},{8,12},{12,8},{16,20},{20,16},{24,28},{28,24},{1,5},{5... | collective-permute-start | bytes 393224 | tf_op jit(solution)/shard_map/ppermute | solution.py:462

commit v21 on v20

--- a/solution.py
+++ b/solution.py
@@ -478,7 +478,7 @@
     block = out_weight.reshape(kv_m.shape)
     low_m = seq_perm(jnp.where(z == 0, kv_m, block), (0, 1), (1, 3))
     pairs = [(i, 2 + 1 - i) for i in range(2)] + [(2 + i, i) for i in range(2)] + [(4 + i, 6 + i) for i in range(2)]
-    low_o = lax.ppermute(jnp.where(z == 0, kv_give, block), "seq", pairs)
+    low_o = lax.ppermute(after(jnp.where(z == 0, kv_give, block), q_o), "seq", pairs)
     kv_o = swap(after(kv_give, q_o, qs[0]))
     qs[1], qs[3] = seq_perm(q_o, *down), seq_perm(q_o, *two_down)
 

time: 191 us -> 182 us (0.953)
  starting transfers between devices: 54.5 us -> 40.7 us
  local copies, waits for them, and re-layouts: 11.5 us -> 14.3 us
    ppermute x17, starting transfers between devices: 44.5 us -> 34.4 us  [seq_perm(): return lax.ppermute(array, 'seq', pairs)]
    ppermute x1, waiting for transfers between devices: 0.01 us -> 5.54 us  [body_eight(): lax.ppermute(after(jnp.where(z == 0, kv_give, block), q_o), 'seq', pairs)]
    ppermute x17, waiting for transfers between devices: 64.2 us -> 60.7 us  [seq_perm(): return lax.ppermute(array, 'seq', pairs)]
    ppermute x1, starting transfers between devices: 4.94 us -> 1.61 us  [body_eight(): lax.ppermute(after(jnp.where(z == 0, kv_give, block), q_o), 'seq', pairs)]
    unnamed x18 -> x28, local copies, waits for them, and re-layouts: 7.01 us -> 9.87 us
  transfers between devices with their start and end apart: 23 -> 23, of which waited for: 10 -> 11; matrix products, arithmetic and copies ran while one was open for 4% -> 4% of each run, Pallas kernels for 20% -> 21%
where the time goes in v21:
time: 182 us; the launch traced here: 180 us
  waiting for transfers between devices  74.8 us (41%)
  Pallas kernels  44.1 us (24%)
  starting transfers between devices  40.7 us (22%)
  local copies, waits for them, and re-layouts  14.3 us (8%)
  other arithmetic  5.94 us (3%)
    ppermute x17, waiting for transfers between devices, seq_perm(): return lax.ppermute(array, 'seq', pairs)  60.7 us
    pallas_call x6, Pallas kernels, head_call(): pl.pallas_call(kernel, out_shape=outs, grid_spec=pltpu.PrefetchScalarGrid...  34.4 us
    ppermute x17, starting transfers between devices, seq_perm(): return lax.ppermute(array, 'seq', pairs)  34.4 us
    unnamed x28, local copies, waits for them, and re-layouts  9.87 us
    pallas_call x6, Pallas kernels, whole_call(): pl.pallas_call(kernel, out_shape=outs, in_specs=[pl.BlockSpec(memory_spac...  9.63 us
    ppermute x4, waiting for transfers between devices, head_perm(): return lax.ppermute(array, 'head', [(i, i ^ flip) for i in range(4)])  8.64 us
    ppermute x1, waiting for transfers between devices, body_eight(): lax.ppermute(after(jnp.where(z == 0, kv_give, block), q_o), 'seq', pairs)  5.54 us
    select_n x1, other arithmetic, body_eight(): jnp.where(z == 0, kv_give, block)  4.15 us
  transfers between devices with their start and end apart: 23, of which 11 were waited for; matrix products, arithmetic and copies ran while one was open for 4% of the time, Pallas kernels for 21%

profile of v21, /device:TPU:16, one launch (start us, length us, event | category | flops | bytes accessed | tf_op | source)
XLA Modules:
  0.0 180.2 jit_solution(1806364922599772217)
XLA Ops:
  0.0 2.3 %dynamic-slice_bitcast_fusion.2 = (bf16[1,512,512]{2,1,0:T(8,128)(2,1)}, bf16[1,512,512]{2,1,0:T(8,128)(2,1)}) fusion(bf16[3,1,512,1024]{3,2,1,0:T(8,128)(2,1)} %param.2, s32[]{:T(128)S(6)} %select_n.57, s32[]{:T(128)S(6)} %select_n.56), kind=kLoop, calls=%fused_computation.6 | loop fusion | bytes 2097160 | tf_op jit(solution)/shard_map/dynamic_slice | solution.py:471
  2.3 1.5 collective-permute-start.1
  3.8 2.3 %collective-permute-start = (bf16[1,512,512]{2,1,0:T(8,128)(2,1)}, bf16[1,512,512]{2,1,0:T(8,128)(2,1)S(1)}, u32[]{:S(2)}, u32[]{:S(2)}) collective-permute-start(bf16[1,512,512]{2,1,0:T(8,128)(2,1)} %get-tuple-element.68.q_m), channel_id=1, source_target_pairs={{16,8},{20,12},{24,16},{28,20},{17,9},{21,13},{25,17},{29,21},{18,... | collective-permute-start | bytes 1572872 | tf_op jit(solution)/shard_map/ppermute | solution.py:462
  6.2 1.5 collective-permute-start.3
  7.6 4.1 %broadcast_select_fusion = (bf16[2,512,512]{2,1,0:T(8,128)(2,1)}, bf16[2,512,512]{2,1,0:T(8,128)(2,1)}, bf16[2,512,512]{2,1,0:T(8,128)(2,1)}, bf16[2,512,512]{2,1,0:T(8,128)(2,1)}) fusion(bf16[2,512,512]{2,1,0:T(8,128)(2,1)S(1)} %bitcast.24, pred[]{:T(512)S(6)} %eq.12, bf16[3,1,512,1024]{3,2,1,0:T(8,128)(2,1)} %param.2, s32[]{:T(128)S(6)} %select_n.57, ...), kind=kLoop, calls=%fused_computation.4 | loop fusion | flops 1048576 | bytes 7340041 | tf_op jit(solution)/shard_map/jit(_where)/select_n | solution.py:481
  12.5 3.7 %collective-permute-done.1.q_o = bf16[1,512,512]{2,1,0:T(8,128)(2,1)S(1)} collective-permute-done((bf16[1,512,512]{2,1,0:T(8,128)(2,1)}, bf16[1,512,512]{2,1,0:T(8,128)(2,1)S(1)}, u32[]{:S(2)}, u32[]{:S(2)}) %collective-permute-start.1) | collective-permute-done | bytes 524320 | tf_op jit(solution)/shard_map/ppermute | solution.py:462
  16.2 4.6 %collective-permute-done.qa_m = bf16[1,512,512]{2,1,0:T(8,128)(2,1)S(1)} collective-permute-done((bf16[1,512,512]{2,1,0:T(8,128)(2,1)}, bf16[1,512,512]{2,1,0:T(8,128)(2,1)S(1)}, u32[]{:S(2)}, u32[]{:S(2)}) %collective-permute-start) | collective-permute-done | bytes 524320 | tf_op jit(solution)/shard_map/ppermute | solution.py:462
  22.1 1.6 collective-permute-start.7
  24.4 11.0 %collective-permute-start.2 = (bf16[1,512,512]{2,1,0:T(8,128)(2,1)}, bf16[1,512,512]{2,1,0:T(8,128)(2,1)S(1)}, u32[]{:S(2)}, u32[]{:S(2)}) collective-permute-start(bf16[1,512,512]{2,1,0:T(8,128)(2,1)} %copy-done.4), channel_id=1, source_target_pairs={{16,8},{20,12},{24,16},{28,20},{17,9},{21,13},{25,17},{29,21},{18,... | collective-permute-start | bytes 1572872 | tf_op jit(solution)/shard_map/ppermute | solution.py:462
  36.3 16.7 %collective-permute-done.2.qa_o = bf16[1,512,512]{2,1,0:T(8,128)(2,1)S(1)} collective-permute-done((bf16[1,512,512]{2,1,0:T(8,128)(2,1)}, bf16[1,512,512]{2,1,0:T(8,128)(2,1)S(1)}, u32[]{:S(2)}, u32[]{:S(2)}) %collective-permute-start.2) | collective-permute-done | bytes 524320 | tf_op jit(solution)/shard_map/ppermute | solution.py:462
  53.9 1.9 %collective-permute-start.12 = (bf16[1024,512]{1,0:T(8,128)(2,1)S(1)}, bf16[1024,512]{1,0:T(8,128)(2,1)}, u32[]{:S(2)}, u32[]{:S(2)}) collective-permute-start(bf16[1024,512]{1,0:T(8,128)(2,1)S(1)} %copy-done), channel_id=1, source_target_pairs={{0,16},{4,20},{16,0},{20,4},{24,8},{28,12},{1,17},{5,21},{17,1},{2... | collective-permute-start | bytes 3145736 | tf_op jit(solution)/shard_map/ppermute | solution.py:462
  55.9 5.5 %collective-permute-done.7.refs_1_ = bf16[2,512,512]{2,1,0:T(8,128)(2,1)S(1)} collective-permute-done((bf16[2,512,512]{2,1,0:T(8,128)(2,1)}, bf16[2,512,512]{2,1,0:T(8,128)(2,1)S(1)}, u32[]{:S(2)}, u32[]{:S(2)}) %collective-permute-start.7) | collective-permute-done | bytes 1048608 | tf_op jit(solution)/shard_map/ppermute | solution.py:481
  65.8 6.0 %upper_rows.2 = (bf16[528,512]{1,0:T(8,128)(2,1)}, bf16[528,512]{1,0:T(8,128)(2,1)}) custom-call(s32[4]{0:T(128)S(1)} %pad_add_fusion.at, bf16[1,512,512]{2,1,0:T(8,128)(2,1)S(1)} %copy-done.8, bf16[1,512,512]{2,1,0:T(8,128)(2,1)S(1)} %copy-done.12, bf16[1,512,512]{2,1,0:T(8,128)(2,1)} %collective-permute-done.3.qb_m, bf16[1,512,512]{2,1,0:T(8,128)(2,1)S(1)} %copy-done.10, ...), custom_call_target="tpu_custom_call" | custom-call | flops 700000000 | bytes 1024 | tf_op jit(solution)/shard_map/upper_rows/pallas_call | solution.py:335
  73.0 4.6 %collective-permute-start.8 = (bf16[528,512]{1,0:T(8,128)(2,1)}, bf16[528,512]{1,0:T(8,128)(2,1)}, u32[]{:S(2)}, u32[]{:S(2)}) collective-permute-start(bf16[528,512]{1,0:T(8,128)(2,1)} %get-tuple-element.35), channel_id=1, source_target_pairs={{8,16},{12,20},{16,24},{20,28},{9,17},{13,21},{17,25},{21,29},{10,... | collective-permute-start | bytes 1622024 | tf_op jit(solution)/shard_map/ppermute | solution.py:462
  77.6 6.0 %upper_rows.3 = (bf16[528,512]{1,0:T(8,128)(2,1)S(1)}, bf16[528,512]{1,0:T(8,128)(2,1)}) custom-call(s32[4]{0:T(128)S(1)} %pad_add_fusion.at, bf16[1,512,512]{2,1,0:T(8,128)(2,1)S(1)} %copy-done.8, bf16[1,512,512]{2,1,0:T(8,128)(2,1)S(1)} %copy-done.12, bf16[1,512,512]{2,1,0:T(8,128)(2,1)} %collective-permute-done.3.qb_m, ...), custom_call_target="tpu_custom_call" | custom-call | flops 700000000 | bytes 1024 | tf_op jit(solution)/shard_map/upper_rows/pallas_call | solution.py:335
  85.7 4.7 %collective-permute-start.16 = (bf16[528,512]{1,0:T(8,128)(2,1)}, bf16[528,512]{1,0:T(8,128)(2,1)S(1)}, u32[]{:S(2)}, u32[]{:S(2)}) collective-permute-start(bf16[528,512]{1,0:T(8,128)(2,1)} %copy-done.13), channel_id=1, source_target_pairs={{8,16},{12,20},{16,24},{20,28},{9,17},{13,21},{17,25},{21,29},{10,... | collective-permute-start | bytes 1622024 | tf_op jit(solution)/shard_map/ppermute | solution.py:462
  92.7 7.6 %own_rows.2.own = bf16[528,512]{1,0:T(8,128)(2,1)S(1)} custom-call(s32[4]{0:T(128)S(1)} %pad_add_fusion.at, bf16[1,512,512]{2,1,0:T(8,128)(2,1)} %get-tuple-element.68.q_m, bf16[1,512,512]{2,1,0:T(8,128)(2,1)S(1)} %copy-done.5, bf16[2,512,512]{2,1,0:T(8,128)(2,1)S(1)} %copy-done.2, bf16[2,512,512]{2,1,0:T(8,128)(2,1)} %collective-permute-done.5.kv_o, ...), custom_call_target="tpu_custom_call" | custom-call | flops 600000000 | bytes 1024 | tf_op jit(solution)/shard_map/own_rows/pallas_call | solution.py:335
  100.3 6.5 %collective-permute-done.8.oa = bf16[528,512]{1,0:T(8,128)(2,1)} collective-permute-done((bf16[528,512]{1,0:T(8,128)(2,1)}, bf16[528,512]{1,0:T(8,128)(2,1)}, u32[]{:S(2)}, u32[]{:S(2)}) %collective-permute-start.8) | collective-permute-done | bytes 540704 | tf_op jit(solution)/shard_map/ppermute | solution.py:462
  106.8 3.7 %merge.2 = bf16[2,256,512]{2,1,0:T(8,128)(2,1)S(1)} custom-call(s32[4]{0:T(128)S(1)} %pad_add_fusion.at, bf16[528,512]{1,0:T(8,128)(2,1)S(1)} %own_rows.2.own, bf16[528,512]{1,0:T(8,128)(2,1)} %collective-permute-done.8.oa, bf16[528,512]{1,0:T(8,128)(2,1)} %collective-permute-done.9.ob), custom_call_target="tpu_custom_call" | custom-call | flops 200000000 | bytes 1024 | tf_op jit(solution)/shard_map/merge/pallas_call | solution.py:335
  112.5 7.6 %own_rows.3.own = bf16[528,512]{1,0:T(8,128)(2,1)S(1)} custom-call(s32[4]{0:T(128)S(1)} %pad_add_fusion.at, bf16[1,512,512]{2,1,0:T(8,128)(2,1)} %get-tuple-element.68.q_m, bf16[1,512,512]{2,1,0:T(8,128)(2,1)S(1)} %copy-done.6, bf16[2,512,512]{2,1,0:T(8,128)(2,1)S(1)} %copy-done.3, bf16[2,512,512]{2,1,0:T(8,128)(2,1)} %collective-permute-done.5.kv_o, ...), custom_call_target="tpu_custom_call" | custom-call | flops 600000000 | bytes 1024 | tf_op jit(solution)/shard_map/own_rows/pallas_call | solution.py:335
  122.7 1.8 project.2
  124.6 4.0 %collective-permute-done.16.oa = bf16[528,512]{1,0:T(8,128)(2,1)S(1)} collective-permute-done((bf16[528,512]{1,0:T(8,128)(2,1)}, bf16[528,512]{1,0:T(8,128)(2,1)S(1)}, u32[]{:S(2)}, u32[]{:S(2)}) %collective-permute-start.16) | collective-permute-done | bytes 540704 | tf_op jit(solution)/shard_map/ppermute | solution.py:462
  128.6 3.6 %merge.3 = bf16[2,256,512]{2,1,0:T(8,128)(2,1)S(1)} custom-call(s32[4]{0:T(128)S(1)} %pad_add_fusion.at, bf16[528,512]{1,0:T(8,128)(2,1)S(1)} %own_rows.3.own, bf16[528,512]{1,0:T(8,128)(2,1)S(1)} %collective-permute-done.16.oa, bf16[528,512]{1,0:T(8,128)(2,1)} %collective-permute-done.11.ob), custom_call_target="tpu_custom_call" | custom-call | flops 200000000 | bytes 1024 | tf_op jit(solution)/shard_map/merge/pallas_call | solution.py:335
  133.5 1.6 collective-permute-start.14
  135.1 5.2 %collective-permute-done.14.got = bf16[2,2,64,512]{3,2,1,0:T(8,128)(2,1)S(1)} collective-permute-done((bf16[2,2,64,512]{3,2,1,0:T(8,128)(2,1)S(1)}, bf16[2,2,64,512]{3,2,1,0:T(8,128)(2,1)S(1)}, u32[]{:S(2)}, u32[]{:S(2)}) %collective-permute-start.14) | collective-permute-done | bytes 262176 | tf_op jit(solution)/shard_map/ppermute | solution.py:468
  140.9 4.0 %collective-permute-done.17 = bf16[2,256,512]{2,1,0:T(8,128)(2,1)S(1)} collective-permute-done((bf16[2,256,512]{2,1,0:T(8,128)(2,1)S(1)}, bf16[2,256,512]{2,1,0:T(8,128)(2,1)S(1)}, u32[]{:S(2)}, u32[]{:S(2)}) %collective-permute-start.17) | collective-permute-done | bytes 524320 | tf_op jit(solution)/shard_map/ppermute | solution.py:462
  144.9 1.5 collective-permute-done.18.refs_5_
  146.4 4.0 %project.3 = (bf16[6,2,2,64,512]{4,3,2,1,0:T(8,128)(2,1)S(1)}, bf16[6,2,2,64,512]{4,3,2,1,0:T(8,128)(2,1)S(1)}) custom-call(s32[4]{0:T(128)S(1)} %pad_add_fusion.at, bf16[2,2,2,64,512]{4,3,2,1,0:T(8,128)(2,1)S(1)} %bitcast.27, bf16[2,2,2,64,512]{4,3,2,1,0:T(8,128)(2,1)S(1)} %bitcast.30, bf16[1024,512]{1,0:T(8,128)(2,1)S(1)} %copy-done, ...), custom_call_target="tpu_custom_call" | custom-call | flops 600000000 | bytes 1024 | tf_op jit(solution)/shard_map/project/pallas_call | solution.py:385
  150.5 3.4 %collective-permute-done.19.got = bf16[6,2,2,64,512]{4,3,2,1,0:T(8,128)(2,1)S(1)} collective-permute-done((bf16[6,2,2,64,512]{4,3,2,1,0:T(8,128)(2,1)S(1)}, bf16[6,2,2,64,512]{4,3,2,1,0:T(8,128)(2,1)S(1)}, u32[]{:S(2)}, u32[]{:S(2)}) %collective-permute-start.19) | collective-permute-done | bytes 1572896 | tf_op jit(solution)/shard_map/ppermute | solution.py:468
  154.8 1.6 collective-permute-start.20
  158.9 19.6 %collective-permute-done.15.refs_1_ = bf16[2,64,512]{2,1,0:T(8,128)(2,1)S(1)} collective-permute-done((bf16[2,64,512]{2,1,0:T(8,128)(2,1)S(1)}, bf16[2,64,512]{2,1,0:T(8,128)(2,1)S(1)}, u32[]{:S(2)}, u32[]{:S(2)}) %collective-permute-start.15) | collective-permute-done | bytes 131104 | tf_op jit(solution)/shard_map/ppermute | solution.py:462
  178.5 1.7 place.1
  (61 shorter events, 24.4 us)
Async XLA Ops:
  0.0 7.6 %copy-start = (bf16[1024,512]{1,0:T(8,128)(2,1)S(1)}, bf16[1024,512]{1,0:T(8,128)(2,1)}, u32[]{:S(2)}) copy-start(bf16[1024,512]{1,0:T(8,128)(2,1)} %refs_2_.7) | copy-start | bytes 3145732
  2.3 13.9 %collective-permute-start.1 = (bf16[1,512,512]{2,1,0:T(8,128)(2,1)}, bf16[1,512,512]{2,1,0:T(8,128)(2,1)S(1)}, u32[]{:S(2)}, u32[]{:S(2)}) collective-permute-start(bf16[1,512,512]{2,1,0:T(8,128)(2,1)} %get-tuple-element.67), channel_id=1, source_target_pairs={{0,4},{4,0},{8,12},{12,8},{16,20},{20,16},{24,28},{28,24},{1,5},{5... | collective-permute-start | bytes 1572872 | tf_op jit(solution)/shard_map/ppermute | solution.py:462
  3.8 16.9 %collective-permute-start = (bf16[1,512,512]{2,1,0:T(8,128)(2,1)}, bf16[1,512,512]{2,1,0:T(8,128)(2,1)S(1)}, u32[]{:S(2)}, u32[]{:S(2)}) collective-permute-start(bf16[1,512,512]{2,1,0:T(8,128)(2,1)} %get-tuple-element.68.q_m), channel_id=1, source_target_pairs={{16,8},{20,12},{24,16},{28,20},{17,9},{21,13},{25,17},{29,21},{18,... | collective-permute-start | bytes 1572872 | tf_op jit(solution)/shard_map/ppermute | solution.py:462
  6.2 18.2 %collective-permute-start.3 = (bf16[1,512,512]{2,1,0:T(8,128)(2,1)}, bf16[1,512,512]{2,1,0:T(8,128)(2,1)}, u32[]{:S(2)}, u32[]{:S(2)}) collective-permute-start(bf16[1,512,512]{2,1,0:T(8,128)(2,1)} %get-tuple-element.68.q_m), channel_id=1, source_target_pairs={{24,8},{28,12},{25,9},{29,13},{26,10},{30,14},{27,11},{31,15}} | collective-permute-start | bytes 1572872 | tf_op jit(solution)/shard_map/ppermute | solution.py:462
  11.8 44.1 %collective-permute-start.6 = (bf16[2,512,512]{2,1,0:T(8,128)(2,1)}, bf16[2,512,512]{2,1,0:T(8,128)(2,1)S(1)}, u32[]{:S(2)}, u32[]{:S(2)}) collective-permute-start(bf16[2,512,512]{2,1,0:T(8,128)(2,1)} %get-tuple-element.65), channel_id=1, source_target_pairs={{0,8},{4,12},{8,24},{12,28},{1,9},{5,13},{9,25},{13,29},{2,10},{6,... | collective-permute-start | bytes 3145736 | tf_op jit(solution)/shard_map/ppermute | solution.py:462
  16.2 5.4 %copy-start.4 = (bf16[1,512,512]{2,1,0:T(8,128)(2,1)}, bf16[1,512,512]{2,1,0:T(8,128)(2,1)S(1)}, u32[]{:S(2)}) copy-start(bf16[1,512,512]{2,1,0:T(8,128)(2,1)S(1)} %collective-permute-done.1.q_o) | copy-start | bytes 1572868
  21.5 34.3 %collective-permute-start.5 = (bf16[2,512,512]{2,1,0:T(8,128)(2,1)}, bf16[2,512,512]{2,1,0:T(8,128)(2,1)}, u32[]{:S(2)}, u32[]{:S(2)}) collective-permute-start(bf16[2,512,512]{2,1,0:T(8,128)(2,1)} %get-tuple-element.33), channel_id=1, source_target_pairs={{0,4},{4,0},{8,12},{12,8},{16,20},{20,16},{24,28},{28,24},{1,5},{5... | collective-permute-start | bytes 3145736 | tf_op jit(solution)/shard_map/ppermute | solution.py:462
  22.1 39.3 %collective-permute-start.7 = (bf16[2,512,512]{2,1,0:T(8,128)(2,1)}, bf16[2,512,512]{2,1,0:T(8,128)(2,1)S(1)}, u32[]{:S(2)}, u32[]{:S(2)}) collective-permute-start(bf16[2,512,512]{2,1,0:T(8,128)(2,1)} %get-tuple-element.34), channel_id=1, source_target_pairs={{0,12},{4,8},{8,0},{12,4},{16,24},{20,28},{1,13},{5,9},{9,1},{13,5... | collective-permute-start | bytes 3145736 | tf_op jit(solution)/shard_map/ppermute | solution.py:481
  23.7 11.8 %collective-permute-start.4 = (bf16[1,512,512]{2,1,0:T(8,128)(2,1)}, bf16[1,512,512]{2,1,0:T(8,128)(2,1)S(1)}, u32[]{:S(2)}, u32[]{:S(2)}) collective-permute-start(bf16[1,512,512]{2,1,0:T(8,128)(2,1)} %copy-done.4), channel_id=1, source_target_pairs={{24,8},{28,12},{25,9},{29,13},{26,10},{30,14},{27,11},{31,15}} | collective-permute-start | bytes 1572872 | tf_op jit(solution)/shard_map/ppermute | solution.py:462
  24.4 28.6 %collective-permute-start.2 = (bf16[1,512,512]{2,1,0:T(8,128)(2,1)}, bf16[1,512,512]{2,1,0:T(8,128)(2,1)S(1)}, u32[]{:S(2)}, u32[]{:S(2)}) collective-permute-start(bf16[1,512,512]{2,1,0:T(8,128)(2,1)} %copy-done.4), channel_id=1, source_target_pairs={{16,8},{20,12},{24,16},{28,20},{17,9},{21,13},{25,17},{29,21},{18,... | collective-permute-start | bytes 1572872 | tf_op jit(solution)/shard_map/ppermute | solution.py:462
  53.9 57.2 %collective-permute-start.12 = (bf16[1024,512]{1,0:T(8,128)(2,1)S(1)}, bf16[1024,512]{1,0:T(8,128)(2,1)}, u32[]{:S(2)}, u32[]{:S(2)}) collective-permute-start(bf16[1024,512]{1,0:T(8,128)(2,1)S(1)} %copy-done), channel_id=1, source_target_pairs={{0,16},{4,20},{16,0},{20,4},{24,8},{28,12},{1,17},{5,21},{17,1},{2... | collective-permute-start | bytes 3145736 | tf_op jit(solution)/shard_map/ppermute | solution.py:462
  61.4 1.2 copy-start.1
  62.7 1.0 copy-start.8
  63.7 1.0 copy-start.10
  64.7 1.0 copy-start.12
  71.7 28.5 %collective-permute-start.9 = (bf16[528,512]{1,0:T(8,128)(2,1)}, bf16[528,512]{1,0:T(8,128)(2,1)}, u32[]{:S(2)}, u32[]{:S(2)}) collective-permute-start(bf16[528,512]{1,0:T(8,128)(2,1)} %get-tuple-element.40), channel_id=1, source_target_pairs={{8,24},{12,28},{0,8},{4,12},{24,16},{28,20},{9,25},{13,29},{1,9},{... | collective-permute-start | bytes 1622024 | tf_op jit(solution)/shard_map/ppermute | solution.py:462
  73.0 33.8 %collective-permute-start.8 = (bf16[528,512]{1,0:T(8,128)(2,1)}, bf16[528,512]{1,0:T(8,128)(2,1)}, u32[]{:S(2)}, u32[]{:S(2)}) collective-permute-start(bf16[528,512]{1,0:T(8,128)(2,1)} %get-tuple-element.35), channel_id=1, source_target_pairs={{8,16},{12,20},{16,24},{20,28},{9,17},{13,21},{17,25},{21,29},{10,... | collective-permute-start | bytes 1622024 | tf_op jit(solution)/shard_map/ppermute | solution.py:462
  84.4 35.8 %collective-permute-start.11 = (bf16[528,512]{1,0:T(8,128)(2,1)}, bf16[528,512]{1,0:T(8,128)(2,1)}, u32[]{:S(2)}, u32[]{:S(2)}) collective-permute-start(bf16[528,512]{1,0:T(8,128)(2,1)} %get-tuple-element.41), channel_id=1, source_target_pairs={{8,24},{12,28},{0,8},{4,12},{24,16},{28,20},{9,25},{13,29},{1,9},{... | collective-permute-start | bytes 1622024 | tf_op jit(solution)/shard_map/ppermute | solution.py:462
  85.7 42.9 %collective-permute-start.16 = (bf16[528,512]{1,0:T(8,128)(2,1)}, bf16[528,512]{1,0:T(8,128)(2,1)S(1)}, u32[]{:S(2)}, u32[]{:S(2)}) collective-permute-start(bf16[528,512]{1,0:T(8,128)(2,1)} %copy-done.13), channel_id=1, source_target_pairs={{8,16},{12,20},{16,24},{20,28},{9,17},{13,21},{17,25},{21,29},{10,... | collective-permute-start | bytes 1622024 | tf_op jit(solution)/shard_map/ppermute | solution.py:462
  90.4 1.2 copy-start.2
  110.5 2.0 %copy-start.3 = (bf16[2,512,512]{2,1,0:T(8,128)(2,1)S(1)}, bf16[2,512,512]{2,1,0:T(8,128)(2,1)}, u32[]{:S(2)}) copy-start(bf16[2,512,512]{2,1,0:T(8,128)(2,1)} %get-tuple-element.66.kv_m) | copy-start | bytes 3145732
  110.5 2.0 %copy-start.6 = (bf16[1,512,512]{2,1,0:T(8,128)(2,1)S(1)}, bf16[1,512,512]{2,1,0:T(8,128)(2,1)}, u32[]{:S(2)}) copy-start(bf16[1,512,512]{2,1,0:T(8,128)(2,1)} %copy-done.4) | copy-start | bytes 1572868
  110.5 12.2 %collective-permute-start.10 = (bf16[2,256,512]{2,1,0:T(8,128)(2,1)S(1)}, bf16[2,256,512]{2,1,0:T(8,128)(2,1)S(1)}, u32[]{:S(2)}, u32[]{:S(2)}) collective-permute-start(bf16[2,256,512]{2,1,0:T(8,128)(2,1)S(1)} %merge.2), channel_id=1, source_target_pairs={{0,4},{4,0},{8,12},{12,8},{16,20},{20,16},{24,28},{28,24},{1,5},{5... | collective-permute-start | bytes 1572872 | tf_op jit(solution)/shard_map/ppermute | solution.py:462
  112.4 34.0 %collective-permute-start.18 = (bf16[1024,512]{1,0:T(8,128)(2,1)S(1)}, bf16[1024,512]{1,0:T(8,128)(2,1)S(1)}, u32[]{:S(2)}, u32[]{:S(2)}) collective-permute-start(bf16[1024,512]{1,0:T(8,128)(2,1)S(1)} %bitcast_select_fusion.refs_4_), channel_id=1, source_target_pairs={{0,8},{4,12},{8,0},{12,4},{16,24},{20,28},{24,16},{28,20},{1,9},{5... | collective-permute-start | bytes 3145736 | tf_op jit(solution)/shard_map/ppermute | solution.py:462
  124.5 8.3 %collective-permute-start.13 = (bf16[2,2,2,64,512]{4,3,2,1,0:T(8,128)(2,1)S(1)}, bf16[2,2,2,64,512]{4,3,2,1,0:T(8,128)(2,1)S(1)}, u32[]{:S(2)}, u32[]{:S(2)}) collective-permute-start(bf16[2,2,2,64,512]{4,3,2,1,0:T(8,128)(2,1)S(1)} %get-tuple-element.48), channel_id=1, source_target_pairs={{0,1},{1,0},{2,3},{3,2},{4,5},{5,4},{6,7},{7,6},{8,9},{9,8},{10,11... | collective-permute-start | bytes 1572872 | tf_op jit(solution)/shard_map/ppermute | solution.py:468
  132.2 12.7 %collective-permute-start.17 = (bf16[2,256,512]{2,1,0:T(8,128)(2,1)S(1)}, bf16[2,256,512]{2,1,0:T(8,128)(2,1)S(1)}, u32[]{:S(2)}, u32[]{:S(2)}) collective-permute-start(bf16[2,256,512]{2,1,0:T(8,128)(2,1)S(1)} %merge.3), channel_id=1, source_target_pairs={{0,4},{4,0},{8,12},{12,8},{16,20},{20,16},{24,28},{28,24},{1,5},{5... | collective-permute-start | bytes 1572872 | tf_op jit(solution)/shard_map/ppermute | solution.py:462
  133.5 6.8 %collective-permute-start.14 = (bf16[2,2,64,512]{3,2,1,0:T(8,128)(2,1)S(1)}, bf16[2,2,64,512]{3,2,1,0:T(8,128)(2,1)S(1)}, u32[]{:S(2)}, u32[]{:S(2)}) collective-permute-start(bf16[2,2,64,512]{3,2,1,0:T(8,128)(2,1)S(1)} %get-tuple-element.50), channel_id=1, source_target_pairs={{0,2},{1,3},{2,0},{3,1},{4,6},{5,7},{6,4},{7,5},{8,10},{9,11},{10,... | collective-permute-start | bytes 786440 | tf_op jit(solution)/shard_map/ppermute | solution.py:468
  150.4 3.5 %collective-permute-start.19 = (bf16[6,2,2,64,512]{4,3,2,1,0:T(8,128)(2,1)S(1)}, bf16[6,2,2,64,512]{4,3,2,1,0:T(8,128)(2,1)S(1)}, u32[]{:S(2)}, u32[]{:S(2)}) collective-permute-start(bf16[6,2,2,64,512]{4,3,2,1,0:T(8,128)(2,1)S(1)} %get-tuple-element.56), channel_id=1, source_target_pairs={{0,1},{1,0},{2,3},{3,2},{4,5},{5,4},{6,7},{7,6},{8,9},{9,8},{10,11... | collective-permute-start | bytes 4718600 | tf_op jit(solution)/shard_map/ppermute | solution.py:468
  154.8 23.7 %collective-permute-start.20 = (bf16[6,64,512]{2,1,0:T(8,128)(2,1)S(1)}, bf16[6,64,512]{2,1,0:T(8,128)(2,1)S(1)}, u32[]{:S(2)}, u32[]{:S(2)}) collective-permute-start(bf16[6,64,512]{2,1,0:T(8,128)(2,1)S(1)} %get-tuple-element.58), channel_id=1, source_target_pairs={{0,2},{1,3},{2,0},{3,1},{4,6},{5,7},{6,4},{7,5},{8,10},{9,11},{10,... | collective-permute-start | bytes 1179656 | tf_op jit(solution)/shard_map/ppermute | solution.py:468
  156.4 22.1 %collective-permute-start.21 = (bf16[6,64,512]{2,1,0:T(8,128)(2,1)S(1)}, bf16[6,64,512]{2,1,0:T(8,128)(2,1)S(1)}, u32[]{:S(2)}, u32[]{:S(2)}) collective-permute-start(bf16[6,64,512]{2,1,0:T(8,128)(2,1)S(1)} %get-tuple-element.59), channel_id=1, source_target_pairs={{0,4},{4,0},{8,12},{12,8},{16,20},{20,16},{24,28},{28,24},{1,5},{5... | collective-permute-start | bytes 1179656 | tf_op jit(solution)/shard_map/ppermute | solution.py:462
  156.9 21.6 %collective-permute-start.22 = (bf16[6,64,512]{2,1,0:T(8,128)(2,1)S(1)}, bf16[6,64,512]{2,1,0:T(8,128)(2,1)S(1)}, u32[]{:S(2)}, u32[]{:S(2)}) collective-permute-start(bf16[6,64,512]{2,1,0:T(8,128)(2,1)S(1)} %get-tuple-element.60), channel_id=1, source_target_pairs={{0,6},{1,7},{2,4},{3,5},{4,2},{5,3},{6,0},{7,1},{8,14},{9,15},{10,... | collective-permute-start | bytes 1179656 | tf_op jit(solution)/shard_map/ppermute | solution.py:542
  158.4 20.1 %collective-permute-start.15 = (bf16[2,64,512]{2,1,0:T(8,128)(2,1)S(1)}, bf16[2,64,512]{2,1,0:T(8,128)(2,1)S(1)}, u32[]{:S(2)}, u32[]{:S(2)}) collective-permute-start(bf16[2,64,512]{2,1,0:T(8,128)(2,1)S(1)} %get-tuple-element.52), channel_id=1, source_target_pairs={{0,4},{4,0},{8,12},{12,8},{16,20},{20,16},{24,28},{28,24},{1,5},{5... | collective-permute-start | bytes 393224 | tf_op jit(solution)/shard_map/ppermute | solution.py:462
  (5 other events, 4.3 us)

commit v22 on v21

--- a/solution.py
+++ b/solution.py
@@ -533,14 +533,16 @@
     parts_out += [mine, swap(to_x)]
     plan.append((names, 1))
 
-    names = [(1, 0), (1, 1), (1, 2), (1, 3), (0, 2), (0, 3)]
-    size, pair = summed(after(at, mine), names)
-    stay, to_y, to_x, to_xy = whole_call(split_kernel, at, pair, [struct(size, BF16)] * 4, "split", 2)
     diagonal = [
         ((2 * i + j) * 4 + h, (2 * i + 1 - j) * 4 + (h ^ 2)) for i in range(4) for j in range(2) for h in range(4)
     ]
-    parts_out += [stay, head_perm(to_y, 2), swap(to_x), lax.ppermute(to_xy, ("seq", "head"), diagonal)]
-    plan.append((names, 2))
+    turn = after(at, mine)
+    for names in ([(1, 0), (1, 1), (0, 2)], [(1, 2), (1, 3), (0, 3)]):
+        size, pair = summed(turn, names)
+        turn = after(at, pair[0])
+        stay, to_y, to_x, to_xy = whole_call(split_kernel, at, pair, [struct(size, BF16)] * 4, "split", 2)
+        parts_out += [stay, head_perm(to_y, 2), swap(to_x), lax.ppermute(to_xy, ("seq", "head"), diagonal)]
+        plan.append((names, 2))
     (out,) = whole_call(
         functools.partial(place_kernel, plan), at, parts_out,
         [struct((cols // 4, 8 * out_weight.shape[1]), BF16)], "place", 2)

time: 182 us -> 178 us (0.978)
  waiting for transfers between devices: 74.8 us -> 65.6 us
  starting transfers between devices: 40.7 us -> 44.8 us
    ppermute x17 -> x18, waiting for transfers between devices: 60.7 us -> 47.2 us  [seq_perm(): return lax.ppermute(array, 'seq', pairs)]
    ppermute x1 -> x2, waiting for transfers between devices: 0.01 us -> 7.12 us  [body_eight(): lax.ppermute(to_xy, ('seq', 'head'), diagonal)]
    ppermute x4 -> x6, waiting for transfers between devices: 8.64 us -> 5.38 us  [head_perm(): return lax.ppermute(array, 'head', [(i, i ^ flip) for i in range(4)])]
    ppermute x4 -> x6, starting transfers between devices: 3.32 us -> 5.44 us  [head_perm(): return lax.ppermute(array, 'head', [(i, i ^ flip) for i in range(4)])]
    ppermute x17 -> x18, starting transfers between devices: 34.4 us -> 35.9 us  [seq_perm(): return lax.ppermute(array, 'seq', pairs)]
    pallas_call x6 -> x8, Pallas kernels: 9.63 us -> 10.9 us  [whole_call(): pl.pallas_call(kernel, out_shape=outs, in_specs=[pl.BlockSpec(memory_spac...]
  transfers between devices with their start and end apart: 23 -> 27, of which waited for: 11 -> 13; matrix products, arithmetic and copies ran while one was open for 4% -> 5% of each run, Pallas kernels for 21% -> 25%
where the time goes in v22:
time: 178 us; the launch traced here: 177 us
  waiting for transfers between devices  65.6 us (37%)
  Pallas kernels  45.3 us (25%)
  starting transfers between devices  44.8 us (25%)
  local copies, waits for them, and re-layouts  14.3 us (8%)
  other arithmetic  6.32 us (4%)
    ppermute x18, waiting for transfers between devices, seq_perm(): return lax.ppermute(array, 'seq', pairs)  47.2 us
    ppermute x18, starting transfers between devices, seq_perm(): return lax.ppermute(array, 'seq', pairs)  35.9 us
    pallas_call x6, Pallas kernels, head_call(): pl.pallas_call(kernel, out_shape=outs, grid_spec=pltpu.PrefetchScalarGrid...  34.5 us
    pallas_call x8, Pallas kernels, whole_call(): pl.pallas_call(kernel, out_shape=outs, in_specs=[pl.BlockSpec(memory_spac...  10.9 us
    unnamed x28, local copies, waits for them, and re-layouts  9.9 us
    ppermute x2, waiting for transfers between devices, body_eight(): lax.ppermute(to_xy, ('seq', 'head'), diagonal)  7.12 us
    ppermute x1, waiting for transfers between devices, body_eight(): lax.ppermute(after(jnp.where(z == 0, kv_give, block), q_o), 'seq', pairs)  5.91 us
    ppermute x6, starting transfers between devices, head_perm(): return lax.ppermute(array, 'head', [(i, i ^ flip) for i in range(4)])  5.44 us
  transfers between devices with their start and end apart: 27, of which 13 were waited for; matrix products, arithmetic and copies ran while one was open for 5% of the time, Pallas kernels for 25%

profile of v22, /device:TPU:16, one launch (start us, length us, event | category | flops | bytes accessed | tf_op | source)
XLA Modules:
  0.0 176.7 jit_solution(17417768109410405819)
XLA Ops:
  0.0 2.2 %dynamic-slice_bitcast_fusion.2 = (bf16[1,512,512]{2,1,0:T(8,128)(2,1)}, bf16[1,512,512]{2,1,0:T(8,128)(2,1)}) fusion(bf16[3,1,512,1024]{3,2,1,0:T(8,128)(2,1)} %param.2, s32[]{:T(128)S(6)} %select_n.57, s32[]{:T(128)S(6)} %select_n.56), kind=kLoop, calls=%fused_computation.6 | loop fusion | bytes 2097160 | tf_op jit(solution)/shard_map/dynamic_slice | solution.py:471
  3.7 2.3 %collective-permute-start = (bf16[1,512,512]{2,1,0:T(8,128)(2,1)}, bf16[1,512,512]{2,1,0:T(8,128)(2,1)S(1)}, u32[]{:S(2)}, u32[]{:S(2)}) collective-permute-start(bf16[1,512,512]{2,1,0:T(8,128)(2,1)} %get-tuple-element.82.q_m), channel_id=1, source_target_pairs={{16,8},{20,12},{24,16},{28,20},{17,9},{21,13},{25,17},{29,21},{18,... | collective-permute-start | bytes 1572872 | tf_op jit(solution)/shard_map/ppermute | solution.py:462
  7.5 4.5 %broadcast_select_fusion = (bf16[2,512,512]{2,1,0:T(8,128)(2,1)}, bf16[2,512,512]{2,1,0:T(8,128)(2,1)}, bf16[2,512,512]{2,1,0:T(8,128)(2,1)}, bf16[2,512,512]{2,1,0:T(8,128)(2,1)}) fusion(bf16[2,512,512]{2,1,0:T(8,128)(2,1)} %bitcast.24, pred[]{:T(512)S(6)} %eq.12, bf16[3,1,512,1024]{3,2,1,0:T(8,128)(2,1)} %param.2, s32[]{:T(128)S(6)} %select_n.57, ...), kind=kLoop, calls=%fused_computation.4 | loop fusion | flops 1048576 | bytes 7340041 | tf_op jit(solution)/shard_map/jit(_where)/select_n | solution.py:481
  12.8 3.3 %collective-permute-done.1.q_o = bf16[1,512,512]{2,1,0:T(8,128)(2,1)S(1)} collective-permute-done((bf16[1,512,512]{2,1,0:T(8,128)(2,1)}, bf16[1,512,512]{2,1,0:T(8,128)(2,1)S(1)}, u32[]{:S(2)}, u32[]{:S(2)}) %collective-permute-start.1) | collective-permute-done | bytes 524320 | tf_op jit(solution)/shard_map/ppermute | solution.py:462
  16.1 4.6 %collective-permute-done.qa_m = bf16[1,512,512]{2,1,0:T(8,128)(2,1)S(1)} collective-permute-done((bf16[1,512,512]{2,1,0:T(8,128)(2,1)}, bf16[1,512,512]{2,1,0:T(8,128)(2,1)S(1)}, u32[]{:S(2)}, u32[]{:S(2)}) %collective-permute-start) | collective-permute-done | bytes 524320 | tf_op jit(solution)/shard_map/ppermute | solution.py:462
  22.0 1.6 collective-permute-start.7
  24.3 11.0 %collective-permute-start.2 = (bf16[1,512,512]{2,1,0:T(8,128)(2,1)}, bf16[1,512,512]{2,1,0:T(8,128)(2,1)S(1)}, u32[]{:S(2)}, u32[]{:S(2)}) collective-permute-start(bf16[1,512,512]{2,1,0:T(8,128)(2,1)} %copy-done.4), channel_id=1, source_target_pairs={{16,8},{20,12},{24,16},{28,20},{17,9},{21,13},{25,17},{29,21},{18,... | collective-permute-start | bytes 1572872 | tf_op jit(solution)/shard_map/ppermute | solution.py:462
  36.2 16.7 %collective-permute-done.2.qa_o = bf16[1,512,512]{2,1,0:T(8,128)(2,1)S(1)} collective-permute-done((bf16[1,512,512]{2,1,0:T(8,128)(2,1)}, bf16[1,512,512]{2,1,0:T(8,128)(2,1)S(1)}, u32[]{:S(2)}, u32[]{:S(2)}) %collective-permute-start.2) | collective-permute-done | bytes 524320 | tf_op jit(solution)/shard_map/ppermute | solution.py:462
  53.8 1.9 %collective-permute-start.12 = (bf16[1024,512]{1,0:T(8,128)(2,1)S(1)}, bf16[1024,512]{1,0:T(8,128)(2,1)}, u32[]{:S(2)}, u32[]{:S(2)}) collective-permute-start(bf16[1024,512]{1,0:T(8,128)(2,1)S(1)} %copy-done), channel_id=1, source_target_pairs={{0,16},{4,20},{16,0},{20,4},{24,8},{28,12},{1,17},{5,21},{17,1},{2... | collective-permute-start | bytes 3145736 | tf_op jit(solution)/shard_map/ppermute | solution.py:462
  55.8 5.9 %collective-permute-done.7.refs_1_ = bf16[2,512,512]{2,1,0:T(8,128)(2,1)S(1)} collective-permute-done((bf16[2,512,512]{2,1,0:T(8,128)(2,1)}, bf16[2,512,512]{2,1,0:T(8,128)(2,1)S(1)}, u32[]{:S(2)}, u32[]{:S(2)}) %collective-permute-start.7) | collective-permute-done | bytes 1048608 | tf_op jit(solution)/shard_map/ppermute | solution.py:481
  66.1 6.0 %upper_rows.2 = (bf16[528,512]{1,0:T(8,128)(2,1)}, bf16[528,512]{1,0:T(8,128)(2,1)}) custom-call(s32[4]{0:T(128)S(1)} %pad_add_fusion.at, bf16[1,512,512]{2,1,0:T(8,128)(2,1)S(1)} %copy-done.8, bf16[1,512,512]{2,1,0:T(8,128)(2,1)S(1)} %copy-done.12, bf16[1,512,512]{2,1,0:T(8,128)(2,1)} %collective-permute-done.3.qb_m, bf16[1,512,512]{2,1,0:T(8,128)(2,1)S(1)} %copy-done.10, ...), custom_call_target="tpu_custom_call" | custom-call | flops 700000000 | bytes 1024 | tf_op jit(solution)/shard_map/upper_rows/pallas_call | solution.py:335
  73.3 4.6 %collective-permute-start.8 = (bf16[528,512]{1,0:T(8,128)(2,1)}, bf16[528,512]{1,0:T(8,128)(2,1)}, u32[]{:S(2)}, u32[]{:S(2)}) collective-permute-start(bf16[528,512]{1,0:T(8,128)(2,1)} %get-tuple-element.42), channel_id=1, source_target_pairs={{8,16},{12,20},{16,24},{20,28},{9,17},{13,21},{17,25},{21,29},{10,... | collective-permute-start | bytes 1622024 | tf_op jit(solution)/shard_map/ppermute | solution.py:462
  77.9 6.0 %upper_rows.3 = (bf16[528,512]{1,0:T(8,128)(2,1)S(1)}, bf16[528,512]{1,0:T(8,128)(2,1)}) custom-call(s32[4]{0:T(128)S(1)} %pad_add_fusion.at, bf16[1,512,512]{2,1,0:T(8,128)(2,1)S(1)} %copy-done.8, bf16[1,512,512]{2,1,0:T(8,128)(2,1)S(1)} %copy-done.12, bf16[1,512,512]{2,1,0:T(8,128)(2,1)} %collective-permute-done.3.qb_m, ...), custom_call_target="tpu_custom_call" | custom-call | flops 700000000 | bytes 1024 | tf_op jit(solution)/shard_map/upper_rows/pallas_call | solution.py:335
  86.0 4.7 %collective-permute-start.16 = (bf16[528,512]{1,0:T(8,128)(2,1)}, bf16[528,512]{1,0:T(8,128)(2,1)S(1)}, u32[]{:S(2)}, u32[]{:S(2)}) collective-permute-start(bf16[528,512]{1,0:T(8,128)(2,1)} %copy-done.13), channel_id=1, source_target_pairs={{8,16},{12,20},{16,24},{20,28},{9,17},{13,21},{17,25},{21,29},{10,... | collective-permute-start | bytes 1622024 | tf_op jit(solution)/shard_map/ppermute | solution.py:462
  93.0 7.6 %own_rows.2.own = bf16[528,512]{1,0:T(8,128)(2,1)S(1)} custom-call(s32[4]{0:T(128)S(1)} %pad_add_fusion.at, bf16[1,512,512]{2,1,0:T(8,128)(2,1)} %get-tuple-element.82.q_m, bf16[1,512,512]{2,1,0:T(8,128)(2,1)S(1)} %copy-done.5, bf16[2,512,512]{2,1,0:T(8,128)(2,1)S(1)} %copy-done.2, bf16[2,512,512]{2,1,0:T(8,128)(2,1)} %collective-permute-done.5.kv_o, ...), custom_call_target="tpu_custom_call" | custom-call | flops 600000000 | bytes 1024 | tf_op jit(solution)/shard_map/own_rows/pallas_call | solution.py:335
  100.6 6.3 %collective-permute-done.8.oa = bf16[528,512]{1,0:T(8,128)(2,1)} collective-permute-done((bf16[528,512]{1,0:T(8,128)(2,1)}, bf16[528,512]{1,0:T(8,128)(2,1)}, u32[]{:S(2)}, u32[]{:S(2)}) %collective-permute-start.8) | collective-permute-done | bytes 540704 | tf_op jit(solution)/shard_map/ppermute | solution.py:462
  106.9 3.7 %merge.2 = bf16[2,256,512]{2,1,0:T(8,128)(2,1)S(1)} custom-call(s32[4]{0:T(128)S(1)} %pad_add_fusion.at, bf16[528,512]{1,0:T(8,128)(2,1)S(1)} %own_rows.2.own, bf16[528,512]{1,0:T(8,128)(2,1)} %collective-permute-done.8.oa, bf16[528,512]{1,0:T(8,128)(2,1)} %collective-permute-done.9.ob), custom_call_target="tpu_custom_call" | custom-call | flops 200000000 | bytes 1024 | tf_op jit(solution)/shard_map/merge/pallas_call | solution.py:335
  112.7 7.6 %own_rows.3.own = bf16[528,512]{1,0:T(8,128)(2,1)S(1)} custom-call(s32[4]{0:T(128)S(1)} %pad_add_fusion.at, bf16[1,512,512]{2,1,0:T(8,128)(2,1)} %get-tuple-element.82.q_m, bf16[1,512,512]{2,1,0:T(8,128)(2,1)S(1)} %copy-done.6, bf16[2,512,512]{2,1,0:T(8,128)(2,1)S(1)} %copy-done.3, bf16[2,512,512]{2,1,0:T(8,128)(2,1)} %collective-permute-done.5.kv_o, ...), custom_call_target="tpu_custom_call" | custom-call | flops 600000000 | bytes 1024 | tf_op jit(solution)/shard_map/own_rows/pallas_call | solution.py:335
  122.8 1.8 %project.3 = (bf16[2,2,2,64,512]{4,3,2,1,0:T(8,128)(2,1)S(1)}, bf16[2,2,2,64,512]{4,3,2,1,0:T(8,128)(2,1)S(1)}) custom-call(s32[4]{0:T(128)S(1)} %pad_add_fusion.at, bf16[2,2,2,64,512]{4,3,2,1,0:T(8,128)(2,1)S(1)} %bitcast.25, bf16[2,2,2,64,512]{4,3,2,1,0:T(8,128)(2,1)S(1)} %bitcast.30, bf16[1024,512]{1,0:T(8,128)(2,1)S(1)} %copy-done, ...), custom_call_target="tpu_custom_call" | custom-call | flops 200000000 | bytes 1024 | tf_op jit(solution)/shard_map/project/pallas_call | solution.py:385
  124.7 4.2 %collective-permute-done.16.oa = bf16[528,512]{1,0:T(8,128)(2,1)S(1)} collective-permute-done((bf16[528,512]{1,0:T(8,128)(2,1)}, bf16[528,512]{1,0:T(8,128)(2,1)S(1)}, u32[]{:S(2)}, u32[]{:S(2)}) %collective-permute-start.16) | collective-permute-done | bytes 540704 | tf_op jit(solution)/shard_map/ppermute | solution.py:462
  128.9 3.6 %merge.3 = bf16[2,256,512]{2,1,0:T(8,128)(2,1)S(1)} custom-call(s32[4]{0:T(128)S(1)} %pad_add_fusion.at, bf16[528,512]{1,0:T(8,128)(2,1)S(1)} %own_rows.3.own, bf16[528,512]{1,0:T(8,128)(2,1)S(1)} %collective-permute-done.16.oa, bf16[528,512]{1,0:T(8,128)(2,1)} %collective-permute-done.11.ob), custom_call_target="tpu_custom_call" | custom-call | flops 200000000 | bytes 1024 | tf_op jit(solution)/shard_map/merge/pallas_call | solution.py:335
  133.8 1.6 collective-permute-start.14
  135.4 5.4 %collective-permute-done.14.got = bf16[2,2,64,512]{3,2,1,0:T(8,128)(2,1)S(1)} collective-permute-done((bf16[2,2,64,512]{3,2,1,0:T(8,128)(2,1)S(1)}, bf16[2,2,64,512]{3,2,1,0:T(8,128)(2,1)S(1)}, u32[]{:S(2)}, u32[]{:S(2)}) %collective-permute-start.14) | collective-permute-done | bytes 262176 | tf_op jit(solution)/shard_map/ppermute | solution.py:468
  141.4 4.0 %collective-permute-done.17 = bf16[2,256,512]{2,1,0:T(8,128)(2,1)S(1)} collective-permute-done((bf16[2,256,512]{2,1,0:T(8,128)(2,1)S(1)}, bf16[2,256,512]{2,1,0:T(8,128)(2,1)S(1)}, u32[]{:S(2)}, u32[]{:S(2)}) %collective-permute-start.17) | collective-permute-done | bytes 524320 | tf_op jit(solution)/shard_map/ppermute | solution.py:462
  145.4 2.3 %project.4 = (bf16[3,2,2,64,512]{4,3,2,1,0:T(8,128)(2,1)S(1)}, bf16[3,2,2,64,512]{4,3,2,1,0:T(8,128)(2,1)S(1)}) custom-call(s32[4]{0:T(128)S(1)} %pad_add_fusion.at, bf16[2,2,2,64,512]{4,3,2,1,0:T(8,128)(2,1)S(1)} %bitcast.28, bf16[2,2,2,64,512]{4,3,2,1,0:T(8,128)(2,1)S(1)} %bitcast.33, bf16[1024,512]{1,0:T(8,128)(2,1)S(1)} %copy-done, ...), custom_call_target="tpu_custom_call" | custom-call | flops 300000000 | bytes 1024 | tf_op jit(solution)/shard_map/project/pallas_call | solution.py:385
  147.8 2.3 %project.5 = (bf16[3,2,2,64,512]{4,3,2,1,0:T(8,128)(2,1)S(1)}, bf16[3,2,2,64,512]{4,3,2,1,0:T(8,128)(2,1)S(1)}) custom-call(s32[4]{0:T(128)S(1)} %pad_add_fusion.at, bf16[2,2,2,64,512]{4,3,2,1,0:T(8,128)(2,1)S(1)} %bitcast.29, bf16[2,2,2,64,512]{4,3,2,1,0:T(8,128)(2,1)S(1)} %bitcast.34, bf16[1024,512]{1,0:T(8,128)(2,1)S(1)} %bitcast_select_fusion.refs_6_.refs_2_, ...), custom_call_target="tpu_custom_call" | custom-call | flops 300000000 | bytes 1024 | tf_op jit(solution)/shard_map/project/pallas_call | solution.py:385
  156.3 1.6 collective-permute-start.24
  161.4 2.2 %collective-permute-done.20.refs_4_ = bf16[3,64,512]{2,1,0:T(8,128)(2,1)S(1)} collective-permute-done((bf16[3,64,512]{2,1,0:T(8,128)(2,1)S(1)}, bf16[3,64,512]{2,1,0:T(8,128)(2,1)S(1)}, u32[]{:S(2)}, u32[]{:S(2)}) %collective-permute-start.20) | collective-permute-done | bytes 196640 | tf_op jit(solution)/shard_map/ppermute | solution.py:462
  163.6 4.2 %collective-permute-done.21.refs_5_ = bf16[3,64,512]{2,1,0:T(8,128)(2,1)S(1)} collective-permute-done((bf16[3,64,512]{2,1,0:T(8,128)(2,1)S(1)}, bf16[3,64,512]{2,1,0:T(8,128)(2,1)S(1)}, u32[]{:S(2)}, u32[]{:S(2)}) %collective-permute-start.21) | collective-permute-done | bytes 196640 | tf_op jit(solution)/shard_map/ppermute | solution.py:544
  167.8 4.3 %collective-permute-done.25.refs_8_ = bf16[3,64,512]{2,1,0:T(8,128)(2,1)S(1)} collective-permute-done((bf16[3,64,512]{2,1,0:T(8,128)(2,1)S(1)}, bf16[3,64,512]{2,1,0:T(8,128)(2,1)S(1)}, u32[]{:S(2)}, u32[]{:S(2)}) %collective-permute-start.25) | collective-permute-done | bytes 196640 | tf_op jit(solution)/shard_map/ppermute | solution.py:462
  172.1 2.9 %collective-permute-done.26.refs_9_ = bf16[3,64,512]{2,1,0:T(8,128)(2,1)S(1)} collective-permute-done((bf16[3,64,512]{2,1,0:T(8,128)(2,1)S(1)}, bf16[3,64,512]{2,1,0:T(8,128)(2,1)S(1)}, u32[]{:S(2)}, u32[]{:S(2)}) %collective-permute-start.26) | collective-permute-done | bytes 196640 | tf_op jit(solution)/shard_map/ppermute | solution.py:544
  175.0 1.7 place.1
  (71 shorter events, 33.7 us)
Async XLA Ops:
  2.2 13.9 %collective-permute-start.1 = (bf16[1,512,512]{2,1,0:T(8,128)(2,1)}, bf16[1,512,512]{2,1,0:T(8,128)(2,1)S(1)}, u32[]{:S(2)}, u32[]{:S(2)}) collective-permute-start(bf16[1,512,512]{2,1,0:T(8,128)(2,1)} %get-tuple-element.81), channel_id=1, source_target_pairs={{0,4},{4,0},{8,12},{12,8},{16,20},{20,16},{24,28},{28,24},{1,5},{5... | collective-permute-start | bytes 1572872 | tf_op jit(solution)/shard_map/ppermute | solution.py:462
  3.7 16.9 %collective-permute-start = (bf16[1,512,512]{2,1,0:T(8,128)(2,1)}, bf16[1,512,512]{2,1,0:T(8,128)(2,1)S(1)}, u32[]{:S(2)}, u32[]{:S(2)}) collective-permute-start(bf16[1,512,512]{2,1,0:T(8,128)(2,1)} %get-tuple-element.82.q_m), channel_id=1, source_target_pairs={{16,8},{20,12},{24,16},{28,20},{17,9},{21,13},{25,17},{29,21},{18,... | collective-permute-start | bytes 1572872 | tf_op jit(solution)/shard_map/ppermute | solution.py:462
  6.1 18.3 %collective-permute-start.3 = (bf16[1,512,512]{2,1,0:T(8,128)(2,1)}, bf16[1,512,512]{2,1,0:T(8,128)(2,1)}, u32[]{:S(2)}, u32[]{:S(2)}) collective-permute-start(bf16[1,512,512]{2,1,0:T(8,128)(2,1)} %get-tuple-element.82.q_m), channel_id=1, source_target_pairs={{24,8},{28,12},{25,9},{29,13},{26,10},{30,14},{27,11},{31,15}} | collective-permute-start | bytes 1572872 | tf_op jit(solution)/shard_map/ppermute | solution.py:462
  7.5 46.3 %copy-start = (bf16[1024,512]{1,0:T(8,128)(2,1)S(1)}, bf16[1024,512]{1,0:T(8,128)(2,1)}, u32[]{:S(2)}) copy-start(bf16[1024,512]{1,0:T(8,128)(2,1)} %refs_2_.7) | copy-start | bytes 3145732
  12.1 43.7 %collective-permute-start.6 = (bf16[2,512,512]{2,1,0:T(8,128)(2,1)}, bf16[2,512,512]{2,1,0:T(8,128)(2,1)S(1)}, u32[]{:S(2)}, u32[]{:S(2)}) collective-permute-start(bf16[2,512,512]{2,1,0:T(8,128)(2,1)} %get-tuple-element.79), channel_id=1, source_target_pairs={{0,8},{4,12},{8,24},{12,28},{1,9},{5,13},{9,25},{13,29},{2,10},{6,... | collective-permute-start | bytes 3145736 | tf_op jit(solution)/shard_map/ppermute | solution.py:462
  16.1 5.4 %copy-start.4 = (bf16[1,512,512]{2,1,0:T(8,128)(2,1)}, bf16[1,512,512]{2,1,0:T(8,128)(2,1)S(1)}, u32[]{:S(2)}) copy-start(bf16[1,512,512]{2,1,0:T(8,128)(2,1)S(1)} %collective-permute-done.1.q_o) | copy-start | bytes 1572868
  21.5 34.3 %collective-permute-start.5 = (bf16[2,512,512]{2,1,0:T(8,128)(2,1)}, bf16[2,512,512]{2,1,0:T(8,128)(2,1)}, u32[]{:S(2)}, u32[]{:S(2)}) collective-permute-start(bf16[2,512,512]{2,1,0:T(8,128)(2,1)} %get-tuple-element.40), channel_id=1, source_target_pairs={{0,4},{4,0},{8,12},{12,8},{16,20},{20,16},{24,28},{28,24},{1,5},{5... | collective-permute-start | bytes 3145736 | tf_op jit(solution)/shard_map/ppermute | solution.py:462
  22.0 39.7 %collective-permute-start.7 = (bf16[2,512,512]{2,1,0:T(8,128)(2,1)}, bf16[2,512,512]{2,1,0:T(8,128)(2,1)S(1)}, u32[]{:S(2)}, u32[]{:S(2)}) collective-permute-start(bf16[2,512,512]{2,1,0:T(8,128)(2,1)} %get-tuple-element.41), channel_id=1, source_target_pairs={{0,12},{4,8},{8,0},{12,4},{16,24},{20,28},{1,13},{5,9},{9,1},{13,5... | collective-permute-start | bytes 3145736 | tf_op jit(solution)/shard_map/ppermute | solution.py:481
  23.6 11.8 %collective-permute-start.4 = (bf16[1,512,512]{2,1,0:T(8,128)(2,1)}, bf16[1,512,512]{2,1,0:T(8,128)(2,1)S(1)}, u32[]{:S(2)}, u32[]{:S(2)}) collective-permute-start(bf16[1,512,512]{2,1,0:T(8,128)(2,1)} %copy-done.4), channel_id=1, source_target_pairs={{24,8},{28,12},{25,9},{29,13},{26,10},{30,14},{27,11},{31,15}} | collective-permute-start | bytes 1572872 | tf_op jit(solution)/shard_map/ppermute | solution.py:462
  24.3 28.6 %collective-permute-start.2 = (bf16[1,512,512]{2,1,0:T(8,128)(2,1)}, bf16[1,512,512]{2,1,0:T(8,128)(2,1)S(1)}, u32[]{:S(2)}, u32[]{:S(2)}) collective-permute-start(bf16[1,512,512]{2,1,0:T(8,128)(2,1)} %copy-done.4), channel_id=1, source_target_pairs={{16,8},{20,12},{24,16},{28,20},{17,9},{21,13},{25,17},{29,21},{18,... | collective-permute-start | bytes 1572872 | tf_op jit(solution)/shard_map/ppermute | solution.py:462
  53.8 57.5 %collective-permute-start.12 = (bf16[1024,512]{1,0:T(8,128)(2,1)S(1)}, bf16[1024,512]{1,0:T(8,128)(2,1)}, u32[]{:S(2)}, u32[]{:S(2)}) collective-permute-start(bf16[1024,512]{1,0:T(8,128)(2,1)S(1)} %copy-done), channel_id=1, source_target_pairs={{0,16},{4,20},{16,0},{20,4},{24,8},{28,12},{1,17},{5,21},{17,1},{2... | collective-permute-start | bytes 3145736 | tf_op jit(solution)/shard_map/ppermute | solution.py:462
  72.0 28.6 %collective-permute-start.9 = (bf16[528,512]{1,0:T(8,128)(2,1)}, bf16[528,512]{1,0:T(8,128)(2,1)}, u32[]{:S(2)}, u32[]{:S(2)}) collective-permute-start(bf16[528,512]{1,0:T(8,128)(2,1)} %get-tuple-element.47), channel_id=1, source_target_pairs={{8,24},{12,28},{0,8},{4,12},{24,16},{28,20},{9,25},{13,29},{1,9},{... | collective-permute-start | bytes 1622024 | tf_op jit(solution)/shard_map/ppermute | solution.py:462
  73.3 33.6 %collective-permute-start.8 = (bf16[528,512]{1,0:T(8,128)(2,1)}, bf16[528,512]{1,0:T(8,128)(2,1)}, u32[]{:S(2)}, u32[]{:S(2)}) collective-permute-start(bf16[528,512]{1,0:T(8,128)(2,1)} %get-tuple-element.42), channel_id=1, source_target_pairs={{8,16},{12,20},{16,24},{20,28},{9,17},{13,21},{17,25},{21,29},{10,... | collective-permute-start | bytes 1622024 | tf_op jit(solution)/shard_map/ppermute | solution.py:462
  84.7 35.6 %collective-permute-start.11 = (bf16[528,512]{1,0:T(8,128)(2,1)}, bf16[528,512]{1,0:T(8,128)(2,1)}, u32[]{:S(2)}, u32[]{:S(2)}) collective-permute-start(bf16[528,512]{1,0:T(8,128)(2,1)} %get-tuple-element.48), channel_id=1, source_target_pairs={{8,24},{12,28},{0,8},{4,12},{24,16},{28,20},{9,25},{13,29},{1,9},{... | collective-permute-start | bytes 1622024 | tf_op jit(solution)/shard_map/ppermute | solution.py:462
  86.0 42.9 %collective-permute-start.16 = (bf16[528,512]{1,0:T(8,128)(2,1)}, bf16[528,512]{1,0:T(8,128)(2,1)S(1)}, u32[]{:S(2)}, u32[]{:S(2)}) collective-permute-start(bf16[528,512]{1,0:T(8,128)(2,1)} %copy-done.13), channel_id=1, source_target_pairs={{8,16},{12,20},{16,24},{20,28},{9,17},{13,21},{17,25},{21,29},{10,... | collective-permute-start | bytes 1622024 | tf_op jit(solution)/shard_map/ppermute | solution.py:462
  90.7 1.2 copy-start.2
  100.6 12.1 %copy-start.3 = (bf16[2,512,512]{2,1,0:T(8,128)(2,1)S(1)}, bf16[2,512,512]{2,1,0:T(8,128)(2,1)}, u32[]{:S(2)}) copy-start(bf16[2,512,512]{2,1,0:T(8,128)(2,1)} %get-tuple-element.80.kv_m) | copy-start | bytes 3145732
  100.6 12.1 %copy-start.6 = (bf16[1,512,512]{2,1,0:T(8,128)(2,1)S(1)}, bf16[1,512,512]{2,1,0:T(8,128)(2,1)}, u32[]{:S(2)}) copy-start(bf16[1,512,512]{2,1,0:T(8,128)(2,1)} %copy-done.4) | copy-start | bytes 1572868
  110.6 12.2 %collective-permute-start.10 = (bf16[2,256,512]{2,1,0:T(8,128)(2,1)S(1)}, bf16[2,256,512]{2,1,0:T(8,128)(2,1)S(1)}, u32[]{:S(2)}, u32[]{:S(2)}) collective-permute-start(bf16[2,256,512]{2,1,0:T(8,128)(2,1)S(1)} %merge.2), channel_id=1, source_target_pairs={{0,4},{4,0},{8,12},{12,8},{16,20},{20,16},{24,28},{28,24},{1,5},{5... | collective-permute-start | bytes 1572872 | tf_op jit(solution)/shard_map/ppermute | solution.py:462
  112.6 35.2 %collective-permute-start.22 = (bf16[1024,512]{1,0:T(8,128)(2,1)S(1)}, bf16[1024,512]{1,0:T(8,128)(2,1)S(1)}, u32[]{:S(2)}, u32[]{:S(2)}) collective-permute-start(bf16[1024,512]{1,0:T(8,128)(2,1)S(1)} %bitcast_select_fusion.refs_6_.refs_2_), channel_id=1, source_target_pairs={{0,8},{4,12},{8,0},{12,4},{16,24},{20,28},{24,16},{28,20},{1,9},{5... | collective-permute-start | bytes 3145736 | tf_op jit(solution)/shard_map/ppermute | solution.py:462
  124.6 8.5 %collective-permute-start.13 = (bf16[2,2,2,64,512]{4,3,2,1,0:T(8,128)(2,1)S(1)}, bf16[2,2,2,64,512]{4,3,2,1,0:T(8,128)(2,1)S(1)}, u32[]{:S(2)}, u32[]{:S(2)}) collective-permute-start(bf16[2,2,2,64,512]{4,3,2,1,0:T(8,128)(2,1)S(1)} %get-tuple-element.55), channel_id=1, source_target_pairs={{0,1},{1,0},{2,3},{3,2},{4,5},{5,4},{6,7},{7,6},{8,9},{9,8},{10,11... | collective-permute-start | bytes 1572872 | tf_op jit(solution)/shard_map/ppermute | solution.py:468
  132.5 12.9 %collective-permute-start.17 = (bf16[2,256,512]{2,1,0:T(8,128)(2,1)S(1)}, bf16[2,256,512]{2,1,0:T(8,128)(2,1)S(1)}, u32[]{:S(2)}, u32[]{:S(2)}) collective-permute-start(bf16[2,256,512]{2,1,0:T(8,128)(2,1)S(1)} %merge.3), channel_id=1, source_target_pairs={{0,4},{4,0},{8,12},{12,8},{16,20},{20,16},{24,28},{28,24},{1,5},{5... | collective-permute-start | bytes 1572872 | tf_op jit(solution)/shard_map/ppermute | solution.py:462
  133.8 7.0 %collective-permute-start.14 = (bf16[2,2,64,512]{3,2,1,0:T(8,128)(2,1)S(1)}, bf16[2,2,64,512]{3,2,1,0:T(8,128)(2,1)S(1)}, u32[]{:S(2)}, u32[]{:S(2)}) collective-permute-start(bf16[2,2,64,512]{3,2,1,0:T(8,128)(2,1)S(1)} %get-tuple-element.57), channel_id=1, source_target_pairs={{0,2},{1,3},{2,0},{3,1},{4,6},{5,7},{6,4},{7,5},{8,10},{9,11},{10,... | collective-permute-start | bytes 786440 | tf_op jit(solution)/shard_map/ppermute | solution.py:468
  147.7 3.0 %collective-permute-start.18 = (bf16[3,2,2,64,512]{4,3,2,1,0:T(8,128)(2,1)S(1)}, bf16[3,2,2,64,512]{4,3,2,1,0:T(8,128)(2,1)S(1)}, u32[]{:S(2)}, u32[]{:S(2)}) collective-permute-start(bf16[3,2,2,64,512]{4,3,2,1,0:T(8,128)(2,1)S(1)} %get-tuple-element.63), channel_id=1, source_target_pairs={{0,1},{1,0},{2,3},{3,2},{4,5},{5,4},{6,7},{7,6},{8,9},{9,8},{10,11... | collective-permute-start | bytes 2359304 | tf_op jit(solution)/shard_map/ppermute | solution.py:468
  150.1 5.4 %collective-permute-start.23 = (bf16[3,2,2,64,512]{4,3,2,1,0:T(8,128)(2,1)S(1)}, bf16[3,2,2,64,512]{4,3,2,1,0:T(8,128)(2,1)S(1)}, u32[]{:S(2)}, u32[]{:S(2)}) collective-permute-start(bf16[3,2,2,64,512]{4,3,2,1,0:T(8,128)(2,1)S(1)} %get-tuple-element.70), channel_id=1, source_target_pairs={{0,1},{1,0},{2,3},{3,2},{4,5},{5,4},{6,7},{7,6},{8,9},{9,8},{10,11... | collective-permute-start | bytes 2359304 | tf_op jit(solution)/shard_map/ppermute | solution.py:468
  151.4 8.5 %collective-permute-start.19 = (bf16[3,64,512]{2,1,0:T(8,128)(2,1)S(1)}, bf16[3,64,512]{2,1,0:T(8,128)(2,1)S(1)}, u32[]{:S(2)}, u32[]{:S(2)}) collective-permute-start(bf16[3,64,512]{2,1,0:T(8,128)(2,1)S(1)} %get-tuple-element.65), channel_id=1, source_target_pairs={{0,2},{1,3},{2,0},{3,1},{4,6},{5,7},{6,4},{7,5},{8,10},{9,11},{10,... | collective-permute-start | bytes 589832 | tf_op jit(solution)/shard_map/ppermute | solution.py:468
  153.0 6.4 %collective-permute-start.15 = (bf16[2,64,512]{2,1,0:T(8,128)(2,1)S(1)}, bf16[2,64,512]{2,1,0:T(8,128)(2,1)S(1)}, u32[]{:S(2)}, u32[]{:S(2)}) collective-permute-start(bf16[2,64,512]{2,1,0:T(8,128)(2,1)S(1)} %get-tuple-element.59), channel_id=1, source_target_pairs={{0,4},{4,0},{8,12},{12,8},{16,20},{20,16},{24,28},{28,24},{1,5},{5... | collective-permute-start | bytes 393224 | tf_op jit(solution)/shard_map/ppermute | solution.py:462
  153.6 10.1 %collective-permute-start.20 = (bf16[3,64,512]{2,1,0:T(8,128)(2,1)S(1)}, bf16[3,64,512]{2,1,0:T(8,128)(2,1)S(1)}, u32[]{:S(2)}, u32[]{:S(2)}) collective-permute-start(bf16[3,64,512]{2,1,0:T(8,128)(2,1)S(1)} %get-tuple-element.66), channel_id=1, source_target_pairs={{0,4},{4,0},{8,12},{12,8},{16,20},{20,16},{24,28},{28,24},{1,5},{5... | collective-permute-start | bytes 589832 | tf_op jit(solution)/shard_map/ppermute | solution.py:462
  155.0 12.8 %collective-permute-start.21 = (bf16[3,64,512]{2,1,0:T(8,128)(2,1)S(1)}, bf16[3,64,512]{2,1,0:T(8,128)(2,1)S(1)}, u32[]{:S(2)}, u32[]{:S(2)}) collective-permute-start(bf16[3,64,512]{2,1,0:T(8,128)(2,1)S(1)} %get-tuple-element.67), channel_id=1, source_target_pairs={{0,6},{1,7},{2,4},{3,5},{4,2},{5,3},{6,0},{7,1},{8,14},{9,15},{10,... | collective-permute-start | bytes 589832 | tf_op jit(solution)/shard_map/ppermute | solution.py:544
  156.3 11.6 %collective-permute-start.24 = (bf16[3,64,512]{2,1,0:T(8,128)(2,1)S(1)}, bf16[3,64,512]{2,1,0:T(8,128)(2,1)S(1)}, u32[]{:S(2)}, u32[]{:S(2)}) collective-permute-start(bf16[3,64,512]{2,1,0:T(8,128)(2,1)S(1)} %get-tuple-element.72), channel_id=1, source_target_pairs={{0,2},{1,3},{2,0},{3,1},{4,6},{5,7},{6,4},{7,5},{8,10},{9,11},{10,... | collective-permute-start | bytes 589832 | tf_op jit(solution)/shard_map/ppermute | solution.py:468
  159.4 12.7 %collective-permute-start.25 = (bf16[3,64,512]{2,1,0:T(8,128)(2,1)S(1)}, bf16[3,64,512]{2,1,0:T(8,128)(2,1)S(1)}, u32[]{:S(2)}, u32[]{:S(2)}) collective-permute-start(bf16[3,64,512]{2,1,0:T(8,128)(2,1)S(1)} %get-tuple-element.73), channel_id=1, source_target_pairs={{0,4},{4,0},{8,12},{12,8},{16,20},{20,16},{24,28},{28,24},{1,5},{5... | collective-permute-start | bytes 589832 | tf_op jit(solution)/shard_map/ppermute | solution.py:462
  160.0 15.0 %collective-permute-start.26 = (bf16[3,64,512]{2,1,0:T(8,128)(2,1)S(1)}, bf16[3,64,512]{2,1,0:T(8,128)(2,1)S(1)}, u32[]{:S(2)}, u32[]{:S(2)}) collective-permute-start(bf16[3,64,512]{2,1,0:T(8,128)(2,1)S(1)} %get-tuple-element.74), channel_id=1, source_target_pairs={{0,6},{1,7},{2,4},{3,5},{4,2},{5,3},{6,0},{7,1},{8,14},{9,15},{10,... | collective-permute-start | bytes 589832 | tf_op jit(solution)/shard_map/ppermute | solution.py:544
  (9 other events, 8.7 us)

commit v23 on v22

--- a/solution.py
+++ b/solution.py
@@ -290,37 +290,42 @@
         out_a[...] = jnp.zeros(out_a.shape, BF16)
 
 
-def lse_packed(ref, base, rows):
-    packed = ref[pl.ds(base, LSE_ROWS), :].astype(F32)
-    return sum(packed[i * rows : (i + 1) * rows] for i in range(3))
-
-
-def merge_kernel(at, own, oa, ob, out):
+def merge_kernel(heads, at, own, oa, ob, out):
     z = at[1]
     tokens = out.shape[1]
     blocks = tokens // HEAD
     rows = 2 * blocks
-    l0, l1, l2 = (lse_packed(ref, 2 * tokens, rows) for ref in (own, oa, ob))
-    l1, l2 = jnp.where(z >= 2, l1, NEG), jnp.where(z >= 3, l2, NEG)
-    top = jnp.maximum(l0, jnp.maximum(l1, l2))
-    shares = [jnp.exp2(l - top) for l in (l0, l1, l2)]
-    whole = shares[0] + shares[1] + shares[2]
-    shares = jnp.concatenate([share / whole for share in shares], axis=0)
-    high = shares.astype(BF16).astype(F32)
-    spare = jnp.zeros((32 - 6 * rows, HEAD), F32)
-    pieces = jnp.concatenate([high, shares - high, spare], axis=0).astype(BF16)
     line = lax.broadcasted_iota(jnp.int32, (32, 3 * HEAD), 0)
     group = lax.broadcasted_iota(jnp.int32, (32, 3 * HEAD), 1) // HEAD
-    for row in range(2):
-        for block in range(blocks):
-            first = row * blocks + block + group * rows
-            pick = ((line == first) | (line == first + 3 * rows)).astype(BF16)
-            spread = lax.dot_general(pieces, pick, (((0,), (0,)), ((), ())), preferred_element_type=F32)
-            mine = slice(row * tokens + block * HEAD, row * tokens + (block + 1) * HEAD)
-            mixed = spread[:, :HEAD] * own[mine].astype(F32)
-            mixed = mixed + spread[:, HEAD : 2 * HEAD] * oa[mine].astype(F32)
-            mixed = mixed + spread[:, 2 * HEAD :] * ob[mine].astype(F32)
-            out[row, block * HEAD : (block + 1) * HEAD] = mixed.astype(BF16)
+    picks = []
+    for first in range(rows):
+        at_line = first + group * rows
+        picks.append(((line == at_line) | (line == at_line + 3 * rows)).astype(BF16))
+    for head in range(heads):
+        lanes = slice(head * HEAD, (head + 1) * HEAD)
+
+        def totals(ref):
+            packed = ref[pl.ds(2 * tokens, LSE_ROWS), lanes].astype(F32)
+            return sum(packed[i * rows : (i + 1) * rows] for i in range(3))
+
+        l0, l1, l2 = (totals(ref) for ref in (own, oa, ob))
+        l1, l2 = jnp.where(z >= 2, l1, NEG), jnp.where(z >= 3, l2, NEG)
+        top = jnp.maximum(l0, jnp.maximum(l1, l2))
+        shares = [jnp.exp2(l - top) for l in (l0, l1, l2)]
+        whole = shares[0] + shares[1] + shares[2]
+        shares = jnp.concatenate([share / whole for share in shares], axis=0)
+        high = shares.astype(BF16).astype(F32)
+        spare = jnp.zeros((32 - 6 * rows, HEAD), F32)
+        pieces = jnp.concatenate([high, shares - high, spare], axis=0).astype(BF16)
+        for row in range(2):
+            for block in range(blocks):
+                pick = picks[row * blocks + block]
+                spread = lax.dot_general(pieces, pick, (((0,), (0,)), ((), ())), preferred_element_type=F32)
+                mine = slice(row * tokens + block * HEAD, row * tokens + (block + 1) * HEAD)
+                mixed = spread[:, :HEAD] * own[mine, lanes].astype(F32)
+                mixed = mixed + spread[:, HEAD : 2 * HEAD] * oa[mine, lanes].astype(F32)
+                mixed = mixed + spread[:, 2 * HEAD :] * ob[mine, lanes].astype(F32)
+                out[row, block * HEAD : (block + 1) * HEAD, lanes] = mixed.astype(BF16)
 
 
 def cost(us):
@@ -504,9 +509,9 @@
     w_down = seq_perm(after(out_weight, *qs), (0, 2), (2, 0), (3, 1))
 
     def merged(c, earlier):
-        (a,) = head_call(
-            merge_kernel, after(at, earlier), [(a[c], 0) for a in (own, oa, ob)],
-            [struct((2, tokens, half), BF16)], heads, "merge", 2)
+        (a,) = whole_call(
+            functools.partial(merge_kernel, heads), after(at, earlier), [own[c], oa[c], ob[c]],
+            [struct((2, tokens, half), BF16)], "merge", 2)
         shape = (2, 2, 2, tokens // 4, half)
         return a.reshape(shape), swap(a).reshape(shape)
 

time: 178 us -> 178 us (level)
  Pallas kernels: 45.3 us -> 41.5 us
  waiting for transfers between devices: 65.6 us -> 68.8 us
    pallas_call x6 -> x4, Pallas kernels: 34.5 us -> 27.1 us  [head_call(): pl.pallas_call(kernel, out_shape=outs, grid_spec=pltpu.PrefetchScalarGrid...]
    pallas_call x8 -> x10, Pallas kernels: 10.9 us -> 14.4 us  [whole_call(): pl.pallas_call(kernel, out_shape=outs, in_specs=[pl.BlockSpec(memory_spac...]
    ppermute x18, waiting for transfers between devices: 47.2 us -> 49.9 us  [seq_perm(): return lax.ppermute(array, 'seq', pairs)]
  transfers between devices with their start and end apart: 27 -> 27, of which waited for: 13 -> 14; matrix products, arithmetic and copies ran while one was open for 5% -> 5% of each run, Pallas kernels for 25% -> 23%
where the time goes in v23:
time: 178 us; the launch traced here: 176 us
  waiting for transfers between devices  68.8 us (39%)
  starting transfers between devices  44.3 us (25%)
  Pallas kernels  41.5 us (23%)
  local copies, waits for them, and re-layouts  14.3 us (8%)
  other arithmetic  6.32 us (4%)
    ppermute x18, waiting for transfers between devices, seq_perm(): return lax.ppermute(array, 'seq', pairs)  49.9 us
    ppermute x18, starting transfers between devices, seq_perm(): return lax.ppermute(array, 'seq', pairs)  35.9 us
    pallas_call x4, Pallas kernels, head_call(): pl.pallas_call(kernel, out_shape=outs, grid_spec=pltpu.PrefetchScalarGrid...  27.1 us
    pallas_call x10, Pallas kernels, whole_call(): pl.pallas_call(kernel, out_shape=outs, in_specs=[pl.BlockSpec(memory_spac...  14.4 us
    unnamed x28, local copies, waits for them, and re-layouts  9.9 us
    ppermute x2, waiting for transfers between devices, body_eight(): lax.ppermute(to_xy, ('seq', 'head'), diagonal)  7.63 us
    ppermute x1, waiting for transfers between devices, body_eight(): lax.ppermute(after(jnp.where(z == 0, kv_give, block), q_o), 'seq', pairs)  5.91 us
    ppermute x6, waiting for transfers between devices, head_perm(): return lax.ppermute(array, 'head', [(i, i ^ flip) for i in range(4)])  5.39 us
  transfers between devices with their start and end apart: 27, of which 14 were waited for; matrix products, arithmetic and copies ran while one was open for 5% of the time, Pallas kernels for 23%

profile of v23, /device:TPU:16, one launch (start us, length us, event | category | flops | bytes accessed | tf_op | source)
XLA Modules:
  0.0 175.7 jit_solution(13444436851038958803)
XLA Ops:
  0.0 2.2 %dynamic-slice_bitcast_fusion.2 = (bf16[1,512,512]{2,1,0:T(8,128)(2,1)}, bf16[1,512,512]{2,1,0:T(8,128)(2,1)}) fusion(bf16[3,1,512,1024]{3,2,1,0:T(8,128)(2,1)} %param.2, s32[]{:T(128)S(6)} %select_n.57, s32[]{:T(128)S(6)} %select_n.56), kind=kLoop, calls=%fused_computation.6 | loop fusion | bytes 2097160 | tf_op jit(solution)/shard_map/dynamic_slice | solution.py:476
  3.7 2.3 %collective-permute-start = (bf16[1,512,512]{2,1,0:T(8,128)(2,1)}, bf16[1,512,512]{2,1,0:T(8,128)(2,1)S(1)}, u32[]{:S(2)}, u32[]{:S(2)}) collective-permute-start(bf16[1,512,512]{2,1,0:T(8,128)(2,1)} %get-tuple-element.82.q_m), channel_id=1, source_target_pairs={{16,8},{20,12},{24,16},{28,20},{17,9},{21,13},{25,17},{29,21},{18,... | collective-permute-start | bytes 1572872 | tf_op jit(solution)/shard_map/ppermute | solution.py:467
  7.5 4.5 %broadcast_select_fusion = (bf16[2,512,512]{2,1,0:T(8,128)(2,1)}, bf16[2,512,512]{2,1,0:T(8,128)(2,1)}, bf16[2,512,512]{2,1,0:T(8,128)(2,1)}, bf16[2,512,512]{2,1,0:T(8,128)(2,1)}) fusion(bf16[2,512,512]{2,1,0:T(8,128)(2,1)} %bitcast.24, pred[]{:T(512)S(6)} %eq.12, bf16[3,1,512,1024]{3,2,1,0:T(8,128)(2,1)} %param.2, s32[]{:T(128)S(6)} %select_n.57, ...), kind=kLoop, calls=%fused_computation.4 | loop fusion | flops 1048576 | bytes 7340041 | tf_op jit(solution)/shard_map/jit(_where)/select_n | solution.py:486
  12.8 3.3 %collective-permute-done.1.q_o = bf16[1,512,512]{2,1,0:T(8,128)(2,1)S(1)} collective-permute-done((bf16[1,512,512]{2,1,0:T(8,128)(2,1)}, bf16[1,512,512]{2,1,0:T(8,128)(2,1)S(1)}, u32[]{:S(2)}, u32[]{:S(2)}) %collective-permute-start.1) | collective-permute-done | bytes 524320 | tf_op jit(solution)/shard_map/ppermute | solution.py:467
  16.1 4.6 %collective-permute-done.qa_m = bf16[1,512,512]{2,1,0:T(8,128)(2,1)S(1)} collective-permute-done((bf16[1,512,512]{2,1,0:T(8,128)(2,1)}, bf16[1,512,512]{2,1,0:T(8,128)(2,1)S(1)}, u32[]{:S(2)}, u32[]{:S(2)}) %collective-permute-start) | collective-permute-done | bytes 524320 | tf_op jit(solution)/shard_map/ppermute | solution.py:467
  22.0 1.6 collective-permute-start.7
  24.3 11.0 %collective-permute-start.2 = (bf16[1,512,512]{2,1,0:T(8,128)(2,1)}, bf16[1,512,512]{2,1,0:T(8,128)(2,1)S(1)}, u32[]{:S(2)}, u32[]{:S(2)}) collective-permute-start(bf16[1,512,512]{2,1,0:T(8,128)(2,1)} %copy-done.4), channel_id=1, source_target_pairs={{16,8},{20,12},{24,16},{28,20},{17,9},{21,13},{25,17},{29,21},{18,... | collective-permute-start | bytes 1572872 | tf_op jit(solution)/shard_map/ppermute | solution.py:467
  36.2 16.7 %collective-permute-done.2.qa_o = bf16[1,512,512]{2,1,0:T(8,128)(2,1)S(1)} collective-permute-done((bf16[1,512,512]{2,1,0:T(8,128)(2,1)}, bf16[1,512,512]{2,1,0:T(8,128)(2,1)S(1)}, u32[]{:S(2)}, u32[]{:S(2)}) %collective-permute-start.2) | collective-permute-done | bytes 524320 | tf_op jit(solution)/shard_map/ppermute | solution.py:467
  53.8 1.9 %collective-permute-start.12 = (bf16[1024,512]{1,0:T(8,128)(2,1)S(1)}, bf16[1024,512]{1,0:T(8,128)(2,1)}, u32[]{:S(2)}, u32[]{:S(2)}) collective-permute-start(bf16[1024,512]{1,0:T(8,128)(2,1)S(1)} %copy-done), channel_id=1, source_target_pairs={{0,16},{4,20},{16,0},{20,4},{24,8},{28,12},{1,17},{5,21},{17,1},{2... | collective-permute-start | bytes 3145736 | tf_op jit(solution)/shard_map/ppermute | solution.py:467
  55.8 5.9 %collective-permute-done.7.refs_1_ = bf16[2,512,512]{2,1,0:T(8,128)(2,1)S(1)} collective-permute-done((bf16[2,512,512]{2,1,0:T(8,128)(2,1)}, bf16[2,512,512]{2,1,0:T(8,128)(2,1)S(1)}, u32[]{:S(2)}, u32[]{:S(2)}) %collective-permute-start.7) | collective-permute-done | bytes 1048608 | tf_op jit(solution)/shard_map/ppermute | solution.py:486
  66.1 6.0 %upper_rows.2 = (bf16[528,512]{1,0:T(8,128)(2,1)}, bf16[528,512]{1,0:T(8,128)(2,1)}) custom-call(s32[4]{0:T(128)S(1)} %pad_add_fusion.at, bf16[1,512,512]{2,1,0:T(8,128)(2,1)S(1)} %copy-done.8, bf16[1,512,512]{2,1,0:T(8,128)(2,1)S(1)} %copy-done.12, bf16[1,512,512]{2,1,0:T(8,128)(2,1)} %collective-permute-done.3.qb_m, bf16[1,512,512]{2,1,0:T(8,128)(2,1)S(1)} %copy-done.10, ...), custom_call_target="tpu_custom_call" | custom-call | flops 700000000 | bytes 1024 | tf_op jit(solution)/shard_map/upper_rows/pallas_call | solution.py:340
  73.3 4.6 %collective-permute-start.8 = (bf16[528,512]{1,0:T(8,128)(2,1)}, bf16[528,512]{1,0:T(8,128)(2,1)}, u32[]{:S(2)}, u32[]{:S(2)}) collective-permute-start(bf16[528,512]{1,0:T(8,128)(2,1)} %get-tuple-element.42), channel_id=1, source_target_pairs={{8,16},{12,20},{16,24},{20,28},{9,17},{13,21},{17,25},{21,29},{10,... | collective-permute-start | bytes 1622024 | tf_op jit(solution)/shard_map/ppermute | solution.py:467
  77.9 6.0 %upper_rows.3 = (bf16[528,512]{1,0:T(8,128)(2,1)S(1)}, bf16[528,512]{1,0:T(8,128)(2,1)}) custom-call(s32[4]{0:T(128)S(1)} %pad_add_fusion.at, bf16[1,512,512]{2,1,0:T(8,128)(2,1)S(1)} %copy-done.8, bf16[1,512,512]{2,1,0:T(8,128)(2,1)S(1)} %copy-done.12, bf16[1,512,512]{2,1,0:T(8,128)(2,1)} %collective-permute-done.3.qb_m, ...), custom_call_target="tpu_custom_call" | custom-call | flops 700000000 | bytes 1024 | tf_op jit(solution)/shard_map/upper_rows/pallas_call | solution.py:340
  86.0 4.7 %collective-permute-start.16 = (bf16[528,512]{1,0:T(8,128)(2,1)}, bf16[528,512]{1,0:T(8,128)(2,1)S(1)}, u32[]{:S(2)}, u32[]{:S(2)}) collective-permute-start(bf16[528,512]{1,0:T(8,128)(2,1)} %copy-done.13), channel_id=1, source_target_pairs={{8,16},{12,20},{16,24},{20,28},{9,17},{13,21},{17,25},{21,29},{10,... | collective-permute-start | bytes 1622024 | tf_op jit(solution)/shard_map/ppermute | solution.py:467
  93.0 7.6 %own_rows.2.own = bf16[528,512]{1,0:T(8,128)(2,1)S(1)} custom-call(s32[4]{0:T(128)S(1)} %pad_add_fusion.at, bf16[1,512,512]{2,1,0:T(8,128)(2,1)} %get-tuple-element.82.q_m, bf16[1,512,512]{2,1,0:T(8,128)(2,1)S(1)} %copy-done.5, bf16[2,512,512]{2,1,0:T(8,128)(2,1)S(1)} %copy-done.2, bf16[2,512,512]{2,1,0:T(8,128)(2,1)} %collective-permute-done.5.kv_o, ...), custom_call_target="tpu_custom_call" | custom-call | flops 600000000 | bytes 1024 | tf_op jit(solution)/shard_map/own_rows/pallas_call | solution.py:340
  100.6 6.3 %collective-permute-done.8.oa = bf16[528,512]{1,0:T(8,128)(2,1)} collective-permute-done((bf16[528,512]{1,0:T(8,128)(2,1)}, bf16[528,512]{1,0:T(8,128)(2,1)}, u32[]{:S(2)}, u32[]{:S(2)}) %collective-permute-start.8) | collective-permute-done | bytes 540704 | tf_op jit(solution)/shard_map/ppermute | solution.py:467
  106.9 1.8 %merge.2 = bf16[2,256,512]{2,1,0:T(8,128)(2,1)S(1)} custom-call(s32[4]{0:T(128)S(1)} %pad_add_fusion.at, bf16[528,512]{1,0:T(8,128)(2,1)S(1)} %own_rows.2.own, bf16[528,512]{1,0:T(8,128)(2,1)} %collective-permute-done.8.oa, bf16[528,512]{1,0:T(8,128)(2,1)} %collective-permute-done.9.ob), custom_call_target="tpu_custom_call" | custom-call | flops 200000000 | bytes 1024 | tf_op jit(solution)/shard_map/merge/pallas_call | solution.py:390
  110.8 7.6 %own_rows.3.own = bf16[528,512]{1,0:T(8,128)(2,1)S(1)} custom-call(s32[4]{0:T(128)S(1)} %pad_add_fusion.at, bf16[1,512,512]{2,1,0:T(8,128)(2,1)} %get-tuple-element.82.q_m, bf16[1,512,512]{2,1,0:T(8,128)(2,1)S(1)} %copy-done.6, bf16[2,512,512]{2,1,0:T(8,128)(2,1)S(1)} %copy-done.3, bf16[2,512,512]{2,1,0:T(8,128)(2,1)} %collective-permute-done.5.kv_o, ...), custom_call_target="tpu_custom_call" | custom-call | flops 600000000 | bytes 1024 | tf_op jit(solution)/shard_map/own_rows/pallas_call | solution.py:340
  121.0 1.8 %project.3 = (bf16[2,2,2,64,512]{4,3,2,1,0:T(8,128)(2,1)S(1)}, bf16[2,2,2,64,512]{4,3,2,1,0:T(8,128)(2,1)S(1)}) custom-call(s32[4]{0:T(128)S(1)} %pad_add_fusion.at, bf16[2,2,2,64,512]{4,3,2,1,0:T(8,128)(2,1)S(1)} %bitcast.25, bf16[2,2,2,64,512]{4,3,2,1,0:T(8,128)(2,1)S(1)} %bitcast.30, bf16[1024,512]{1,0:T(8,128)(2,1)S(1)} %copy-done, ...), custom_call_target="tpu_custom_call" | custom-call | flops 200000000 | bytes 1024 | tf_op jit(solution)/shard_map/project/pallas_call | solution.py:390
  122.8 6.0 %collective-permute-done.16.oa = bf16[528,512]{1,0:T(8,128)(2,1)S(1)} collective-permute-done((bf16[528,512]{1,0:T(8,128)(2,1)}, bf16[528,512]{1,0:T(8,128)(2,1)S(1)}, u32[]{:S(2)}, u32[]{:S(2)}) %collective-permute-start.16) | collective-permute-done | bytes 540704 | tf_op jit(solution)/shard_map/ppermute | solution.py:467
  128.9 1.7 merge.3
  133.4 5.4 %collective-permute-done.14.got = bf16[2,2,64,512]{3,2,1,0:T(8,128)(2,1)S(1)} collective-permute-done((bf16[2,2,64,512]{3,2,1,0:T(8,128)(2,1)S(1)}, bf16[2,2,64,512]{3,2,1,0:T(8,128)(2,1)S(1)}, u32[]{:S(2)}, u32[]{:S(2)}) %collective-permute-start.14) | collective-permute-done | bytes 262176 | tf_op jit(solution)/shard_map/ppermute | solution.py:473
  139.4 4.0 %collective-permute-done.17 = bf16[2,256,512]{2,1,0:T(8,128)(2,1)S(1)} collective-permute-done((bf16[2,256,512]{2,1,0:T(8,128)(2,1)S(1)}, bf16[2,256,512]{2,1,0:T(8,128)(2,1)S(1)}, u32[]{:S(2)}, u32[]{:S(2)}) %collective-permute-start.17) | collective-permute-done | bytes 524320 | tf_op jit(solution)/shard_map/ppermute | solution.py:467
  143.4 2.3 %project.4 = (bf16[3,2,2,64,512]{4,3,2,1,0:T(8,128)(2,1)S(1)}, bf16[3,2,2,64,512]{4,3,2,1,0:T(8,128)(2,1)S(1)}) custom-call(s32[4]{0:T(128)S(1)} %pad_add_fusion.at, bf16[2,2,2,64,512]{4,3,2,1,0:T(8,128)(2,1)S(1)} %bitcast.28, bf16[2,2,2,64,512]{4,3,2,1,0:T(8,128)(2,1)S(1)} %bitcast.33, bf16[1024,512]{1,0:T(8,128)(2,1)S(1)} %copy-done, ...), custom_call_target="tpu_custom_call" | custom-call | flops 300000000 | bytes 1024 | tf_op jit(solution)/shard_map/project/pallas_call | solution.py:390
  146.8 2.3 %project.5 = (bf16[3,2,2,64,512]{4,3,2,1,0:T(8,128)(2,1)S(1)}, bf16[3,2,2,64,512]{4,3,2,1,0:T(8,128)(2,1)S(1)}) custom-call(s32[4]{0:T(128)S(1)} %pad_add_fusion.at, bf16[2,2,2,64,512]{4,3,2,1,0:T(8,128)(2,1)S(1)} %bitcast.29, bf16[2,2,2,64,512]{4,3,2,1,0:T(8,128)(2,1)S(1)} %bitcast.34, bf16[1024,512]{1,0:T(8,128)(2,1)S(1)} %bitcast_select_fusion.refs_6_.refs_2_, ...), custom_call_target="tpu_custom_call" | custom-call | flops 300000000 | bytes 1024 | tf_op jit(solution)/shard_map/project/pallas_call | solution.py:390
  149.9 1.6 collective-permute-start.19
  154.7 1.6 collective-permute-start.24
  159.8 2.2 %collective-permute-done.20.refs_4_ = bf16[3,64,512]{2,1,0:T(8,128)(2,1)S(1)} collective-permute-done((bf16[3,64,512]{2,1,0:T(8,128)(2,1)S(1)}, bf16[3,64,512]{2,1,0:T(8,128)(2,1)S(1)}, u32[]{:S(2)}, u32[]{:S(2)}) %collective-permute-start.20) | collective-permute-done | bytes 196640 | tf_op jit(solution)/shard_map/ppermute | solution.py:467
  162.1 4.2 %collective-permute-done.21.refs_5_ = bf16[3,64,512]{2,1,0:T(8,128)(2,1)S(1)} collective-permute-done((bf16[3,64,512]{2,1,0:T(8,128)(2,1)S(1)}, bf16[3,64,512]{2,1,0:T(8,128)(2,1)S(1)}, u32[]{:S(2)}, u32[]{:S(2)}) %collective-permute-start.21) | collective-permute-done | bytes 196640 | tf_op jit(solution)/shard_map/ppermute | solution.py:549
  166.3 4.3 %collective-permute-done.25.refs_8_ = bf16[3,64,512]{2,1,0:T(8,128)(2,1)S(1)} collective-permute-done((bf16[3,64,512]{2,1,0:T(8,128)(2,1)S(1)}, bf16[3,64,512]{2,1,0:T(8,128)(2,1)S(1)}, u32[]{:S(2)}, u32[]{:S(2)}) %collective-permute-start.25) | collective-permute-done | bytes 196640 | tf_op jit(solution)/shard_map/ppermute | solution.py:467
  170.5 3.4 %collective-permute-done.26.refs_9_ = bf16[3,64,512]{2,1,0:T(8,128)(2,1)S(1)} collective-permute-done((bf16[3,64,512]{2,1,0:T(8,128)(2,1)S(1)}, bf16[3,64,512]{2,1,0:T(8,128)(2,1)S(1)}, u32[]{:S(2)}, u32[]{:S(2)}) %collective-permute-start.26) | collective-permute-done | bytes 196640 | tf_op jit(solution)/shard_map/ppermute | solution.py:549
  174.0 1.7 place.1
  (71 shorter events, 34.0 us)
Async XLA Ops:
  2.2 13.9 %collective-permute-start.1 = (bf16[1,512,512]{2,1,0:T(8,128)(2,1)}, bf16[1,512,512]{2,1,0:T(8,128)(2,1)S(1)}, u32[]{:S(2)}, u32[]{:S(2)}) collective-permute-start(bf16[1,512,512]{2,1,0:T(8,128)(2,1)} %get-tuple-element.81), channel_id=1, source_target_pairs={{0,4},{4,0},{8,12},{12,8},{16,20},{20,16},{24,28},{28,24},{1,5},{5... | collective-permute-start | bytes 1572872 | tf_op jit(solution)/shard_map/ppermute | solution.py:467
  3.7 16.9 %collective-permute-start = (bf16[1,512,512]{2,1,0:T(8,128)(2,1)}, bf16[1,512,512]{2,1,0:T(8,128)(2,1)S(1)}, u32[]{:S(2)}, u32[]{:S(2)}) collective-permute-start(bf16[1,512,512]{2,1,0:T(8,128)(2,1)} %get-tuple-element.82.q_m), channel_id=1, source_target_pairs={{16,8},{20,12},{24,16},{28,20},{17,9},{21,13},{25,17},{29,21},{18,... | collective-permute-start | bytes 1572872 | tf_op jit(solution)/shard_map/ppermute | solution.py:467
  6.1 18.3 %collective-permute-start.3 = (bf16[1,512,512]{2,1,0:T(8,128)(2,1)}, bf16[1,512,512]{2,1,0:T(8,128)(2,1)}, u32[]{:S(2)}, u32[]{:S(2)}) collective-permute-start(bf16[1,512,512]{2,1,0:T(8,128)(2,1)} %get-tuple-element.82.q_m), channel_id=1, source_target_pairs={{24,8},{28,12},{25,9},{29,13},{26,10},{30,14},{27,11},{31,15}} | collective-permute-start | bytes 1572872 | tf_op jit(solution)/shard_map/ppermute | solution.py:467
  7.5 46.3 %copy-start = (bf16[1024,512]{1,0:T(8,128)(2,1)S(1)}, bf16[1024,512]{1,0:T(8,128)(2,1)}, u32[]{:S(2)}) copy-start(bf16[1024,512]{1,0:T(8,128)(2,1)} %refs_2_.7) | copy-start | bytes 3145732
  12.1 43.7 %collective-permute-start.6 = (bf16[2,512,512]{2,1,0:T(8,128)(2,1)}, bf16[2,512,512]{2,1,0:T(8,128)(2,1)S(1)}, u32[]{:S(2)}, u32[]{:S(2)}) collective-permute-start(bf16[2,512,512]{2,1,0:T(8,128)(2,1)} %get-tuple-element.79), channel_id=1, source_target_pairs={{0,8},{4,12},{8,24},{12,28},{1,9},{5,13},{9,25},{13,29},{2,10},{6,... | collective-permute-start | bytes 3145736 | tf_op jit(solution)/shard_map/ppermute | solution.py:467
  16.1 5.4 %copy-start.4 = (bf16[1,512,512]{2,1,0:T(8,128)(2,1)}, bf16[1,512,512]{2,1,0:T(8,128)(2,1)S(1)}, u32[]{:S(2)}) copy-start(bf16[1,512,512]{2,1,0:T(8,128)(2,1)S(1)} %collective-permute-done.1.q_o) | copy-start | bytes 1572868
  21.5 34.3 %collective-permute-start.5 = (bf16[2,512,512]{2,1,0:T(8,128)(2,1)}, bf16[2,512,512]{2,1,0:T(8,128)(2,1)}, u32[]{:S(2)}, u32[]{:S(2)}) collective-permute-start(bf16[2,512,512]{2,1,0:T(8,128)(2,1)} %get-tuple-element.40), channel_id=1, source_target_pairs={{0,4},{4,0},{8,12},{12,8},{16,20},{20,16},{24,28},{28,24},{1,5},{5... | collective-permute-start | bytes 3145736 | tf_op jit(solution)/shard_map/ppermute | solution.py:467
  22.0 39.7 %collective-permute-start.7 = (bf16[2,512,512]{2,1,0:T(8,128)(2,1)}, bf16[2,512,512]{2,1,0:T(8,128)(2,1)S(1)}, u32[]{:S(2)}, u32[]{:S(2)}) collective-permute-start(bf16[2,512,512]{2,1,0:T(8,128)(2,1)} %get-tuple-element.41), channel_id=1, source_target_pairs={{0,12},{4,8},{8,0},{12,4},{16,24},{20,28},{1,13},{5,9},{9,1},{13,5... | collective-permute-start | bytes 3145736 | tf_op jit(solution)/shard_map/ppermute | solution.py:486
  23.6 11.8 %collective-permute-start.4 = (bf16[1,512,512]{2,1,0:T(8,128)(2,1)}, bf16[1,512,512]{2,1,0:T(8,128)(2,1)S(1)}, u32[]{:S(2)}, u32[]{:S(2)}) collective-permute-start(bf16[1,512,512]{2,1,0:T(8,128)(2,1)} %copy-done.4), channel_id=1, source_target_pairs={{24,8},{28,12},{25,9},{29,13},{26,10},{30,14},{27,11},{31,15}} | collective-permute-start | bytes 1572872 | tf_op jit(solution)/shard_map/ppermute | solution.py:467
  24.3 28.6 %collective-permute-start.2 = (bf16[1,512,512]{2,1,0:T(8,128)(2,1)}, bf16[1,512,512]{2,1,0:T(8,128)(2,1)S(1)}, u32[]{:S(2)}, u32[]{:S(2)}) collective-permute-start(bf16[1,512,512]{2,1,0:T(8,128)(2,1)} %copy-done.4), channel_id=1, source_target_pairs={{16,8},{20,12},{24,16},{28,20},{17,9},{21,13},{25,17},{29,21},{18,... | collective-permute-start | bytes 1572872 | tf_op jit(solution)/shard_map/ppermute | solution.py:467
  53.8 55.6 %collective-permute-start.12 = (bf16[1024,512]{1,0:T(8,128)(2,1)S(1)}, bf16[1024,512]{1,0:T(8,128)(2,1)}, u32[]{:S(2)}, u32[]{:S(2)}) collective-permute-start(bf16[1024,512]{1,0:T(8,128)(2,1)S(1)} %copy-done), channel_id=1, source_target_pairs={{0,16},{4,20},{16,0},{20,4},{24,8},{28,12},{1,17},{5,21},{17,1},{2... | collective-permute-start | bytes 3145736 | tf_op jit(solution)/shard_map/ppermute | solution.py:467
  72.0 28.6 %collective-permute-start.9 = (bf16[528,512]{1,0:T(8,128)(2,1)}, bf16[528,512]{1,0:T(8,128)(2,1)}, u32[]{:S(2)}, u32[]{:S(2)}) collective-permute-start(bf16[528,512]{1,0:T(8,128)(2,1)} %get-tuple-element.47), channel_id=1, source_target_pairs={{8,24},{12,28},{0,8},{4,12},{24,16},{28,20},{9,25},{13,29},{1,9},{... | collective-permute-start | bytes 1622024 | tf_op jit(solution)/shard_map/ppermute | solution.py:467
  73.3 33.6 %collective-permute-start.8 = (bf16[528,512]{1,0:T(8,128)(2,1)}, bf16[528,512]{1,0:T(8,128)(2,1)}, u32[]{:S(2)}, u32[]{:S(2)}) collective-permute-start(bf16[528,512]{1,0:T(8,128)(2,1)} %get-tuple-element.42), channel_id=1, source_target_pairs={{8,16},{12,20},{16,24},{20,28},{9,17},{13,21},{17,25},{21,29},{10,... | collective-permute-start | bytes 1622024 | tf_op jit(solution)/shard_map/ppermute | solution.py:467
  84.7 33.7 %collective-permute-start.11 = (bf16[528,512]{1,0:T(8,128)(2,1)}, bf16[528,512]{1,0:T(8,128)(2,1)}, u32[]{:S(2)}, u32[]{:S(2)}) collective-permute-start(bf16[528,512]{1,0:T(8,128)(2,1)} %get-tuple-element.48), channel_id=1, source_target_pairs={{8,24},{12,28},{0,8},{4,12},{24,16},{28,20},{9,25},{13,29},{1,9},{... | collective-permute-start | bytes 1622024 | tf_op jit(solution)/shard_map/ppermute | solution.py:467
  86.0 42.9 %collective-permute-start.16 = (bf16[528,512]{1,0:T(8,128)(2,1)}, bf16[528,512]{1,0:T(8,128)(2,1)S(1)}, u32[]{:S(2)}, u32[]{:S(2)}) collective-permute-start(bf16[528,512]{1,0:T(8,128)(2,1)} %copy-done.13), channel_id=1, source_target_pairs={{8,16},{12,20},{16,24},{20,28},{9,17},{13,21},{17,25},{21,29},{10,... | collective-permute-start | bytes 1622024 | tf_op jit(solution)/shard_map/ppermute | solution.py:467
  90.7 1.2 copy-start.2
  100.6 10.2 %copy-start.3 = (bf16[2,512,512]{2,1,0:T(8,128)(2,1)S(1)}, bf16[2,512,512]{2,1,0:T(8,128)(2,1)}, u32[]{:S(2)}) copy-start(bf16[2,512,512]{2,1,0:T(8,128)(2,1)} %get-tuple-element.80.kv_m) | copy-start | bytes 3145732
  100.6 10.2 %copy-start.6 = (bf16[1,512,512]{2,1,0:T(8,128)(2,1)S(1)}, bf16[1,512,512]{2,1,0:T(8,128)(2,1)}, u32[]{:S(2)}) copy-start(bf16[1,512,512]{2,1,0:T(8,128)(2,1)} %copy-done.4) | copy-start | bytes 1572868
  108.8 12.2 %collective-permute-start.10 = (bf16[2,256,512]{2,1,0:T(8,128)(2,1)S(1)}, bf16[2,256,512]{2,1,0:T(8,128)(2,1)S(1)}, u32[]{:S(2)}, u32[]{:S(2)}) collective-permute-start(bf16[2,256,512]{2,1,0:T(8,128)(2,1)S(1)} %merge.2), channel_id=1, source_target_pairs={{0,4},{4,0},{8,12},{12,8},{16,20},{20,16},{24,28},{28,24},{1,5},{5... | collective-permute-start | bytes 1572872 | tf_op jit(solution)/shard_map/ppermute | solution.py:467
  110.7 36.0 %collective-permute-start.22 = (bf16[1024,512]{1,0:T(8,128)(2,1)S(1)}, bf16[1024,512]{1,0:T(8,128)(2,1)S(1)}, u32[]{:S(2)}, u32[]{:S(2)}) collective-permute-start(bf16[1024,512]{1,0:T(8,128)(2,1)S(1)} %bitcast_select_fusion.refs_6_.refs_2_), channel_id=1, source_target_pairs={{0,8},{4,12},{8,0},{12,4},{16,24},{20,28},{24,16},{28,20},{1,9},{5... | collective-permute-start | bytes 3145736 | tf_op jit(solution)/shard_map/ppermute | solution.py:467
  122.8 8.4 %collective-permute-start.13 = (bf16[2,2,2,64,512]{4,3,2,1,0:T(8,128)(2,1)S(1)}, bf16[2,2,2,64,512]{4,3,2,1,0:T(8,128)(2,1)S(1)}, u32[]{:S(2)}, u32[]{:S(2)}) collective-permute-start(bf16[2,2,2,64,512]{4,3,2,1,0:T(8,128)(2,1)S(1)} %get-tuple-element.55), channel_id=1, source_target_pairs={{0,1},{1,0},{2,3},{3,2},{4,5},{5,4},{6,7},{7,6},{8,9},{9,8},{10,11... | collective-permute-start | bytes 1572872 | tf_op jit(solution)/shard_map/ppermute | solution.py:473
  130.6 12.9 %collective-permute-start.17 = (bf16[2,256,512]{2,1,0:T(8,128)(2,1)S(1)}, bf16[2,256,512]{2,1,0:T(8,128)(2,1)S(1)}, u32[]{:S(2)}, u32[]{:S(2)}) collective-permute-start(bf16[2,256,512]{2,1,0:T(8,128)(2,1)S(1)} %merge.3), channel_id=1, source_target_pairs={{0,4},{4,0},{8,12},{12,8},{16,20},{20,16},{24,28},{28,24},{1,5},{5... | collective-permute-start | bytes 1572872 | tf_op jit(solution)/shard_map/ppermute | solution.py:467
  131.9 7.0 %collective-permute-start.14 = (bf16[2,2,64,512]{3,2,1,0:T(8,128)(2,1)S(1)}, bf16[2,2,64,512]{3,2,1,0:T(8,128)(2,1)S(1)}, u32[]{:S(2)}, u32[]{:S(2)}) collective-permute-start(bf16[2,2,64,512]{3,2,1,0:T(8,128)(2,1)S(1)} %get-tuple-element.57), channel_id=1, source_target_pairs={{0,2},{1,3},{2,0},{3,1},{4,6},{5,7},{6,4},{7,5},{8,10},{9,11},{10,... | collective-permute-start | bytes 786440 | tf_op jit(solution)/shard_map/ppermute | solution.py:473
  145.8 3.4 %collective-permute-start.18 = (bf16[3,2,2,64,512]{4,3,2,1,0:T(8,128)(2,1)S(1)}, bf16[3,2,2,64,512]{4,3,2,1,0:T(8,128)(2,1)S(1)}, u32[]{:S(2)}, u32[]{:S(2)}) collective-permute-start(bf16[3,2,2,64,512]{4,3,2,1,0:T(8,128)(2,1)S(1)} %get-tuple-element.63), channel_id=1, source_target_pairs={{0,1},{1,0},{2,3},{3,2},{4,5},{5,4},{6,7},{7,6},{8,9},{9,8},{10,11... | collective-permute-start | bytes 2359304 | tf_op jit(solution)/shard_map/ppermute | solution.py:473
  149.1 4.9 %collective-permute-start.23 = (bf16[3,2,2,64,512]{4,3,2,1,0:T(8,128)(2,1)S(1)}, bf16[3,2,2,64,512]{4,3,2,1,0:T(8,128)(2,1)S(1)}, u32[]{:S(2)}, u32[]{:S(2)}) collective-permute-start(bf16[3,2,2,64,512]{4,3,2,1,0:T(8,128)(2,1)S(1)} %get-tuple-element.70), channel_id=1, source_target_pairs={{0,1},{1,0},{2,3},{3,2},{4,5},{5,4},{6,7},{7,6},{8,9},{9,8},{10,11... | collective-permute-start | bytes 2359304 | tf_op jit(solution)/shard_map/ppermute | solution.py:473
  149.9 8.5 %collective-permute-start.19 = (bf16[3,64,512]{2,1,0:T(8,128)(2,1)S(1)}, bf16[3,64,512]{2,1,0:T(8,128)(2,1)S(1)}, u32[]{:S(2)}, u32[]{:S(2)}) collective-permute-start(bf16[3,64,512]{2,1,0:T(8,128)(2,1)S(1)} %get-tuple-element.65), channel_id=1, source_target_pairs={{0,2},{1,3},{2,0},{3,1},{4,6},{5,7},{6,4},{7,5},{8,10},{9,11},{10,... | collective-permute-start | bytes 589832 | tf_op jit(solution)/shard_map/ppermute | solution.py:473
  151.5 6.3 %collective-permute-start.15 = (bf16[2,64,512]{2,1,0:T(8,128)(2,1)S(1)}, bf16[2,64,512]{2,1,0:T(8,128)(2,1)S(1)}, u32[]{:S(2)}, u32[]{:S(2)}) collective-permute-start(bf16[2,64,512]{2,1,0:T(8,128)(2,1)S(1)} %get-tuple-element.59), channel_id=1, source_target_pairs={{0,4},{4,0},{8,12},{12,8},{16,20},{20,16},{24,28},{28,24},{1,5},{5... | collective-permute-start | bytes 393224 | tf_op jit(solution)/shard_map/ppermute | solution.py:467
  152.0 10.0 %collective-permute-start.20 = (bf16[3,64,512]{2,1,0:T(8,128)(2,1)S(1)}, bf16[3,64,512]{2,1,0:T(8,128)(2,1)S(1)}, u32[]{:S(2)}, u32[]{:S(2)}) collective-permute-start(bf16[3,64,512]{2,1,0:T(8,128)(2,1)S(1)} %get-tuple-element.66), channel_id=1, source_target_pairs={{0,4},{4,0},{8,12},{12,8},{16,20},{20,16},{24,28},{28,24},{1,5},{5... | collective-permute-start | bytes 589832 | tf_op jit(solution)/shard_map/ppermute | solution.py:467
  153.5 12.7 %collective-permute-start.21 = (bf16[3,64,512]{2,1,0:T(8,128)(2,1)S(1)}, bf16[3,64,512]{2,1,0:T(8,128)(2,1)S(1)}, u32[]{:S(2)}, u32[]{:S(2)}) collective-permute-start(bf16[3,64,512]{2,1,0:T(8,128)(2,1)S(1)} %get-tuple-element.67), channel_id=1, source_target_pairs={{0,6},{1,7},{2,4},{3,5},{4,2},{5,3},{6,0},{7,1},{8,14},{9,15},{10,... | collective-permute-start | bytes 589832 | tf_op jit(solution)/shard_map/ppermute | solution.py:549
  154.7 11.5 %collective-permute-start.24 = (bf16[3,64,512]{2,1,0:T(8,128)(2,1)S(1)}, bf16[3,64,512]{2,1,0:T(8,128)(2,1)S(1)}, u32[]{:S(2)}, u32[]{:S(2)}) collective-permute-start(bf16[3,64,512]{2,1,0:T(8,128)(2,1)S(1)} %get-tuple-element.72), channel_id=1, source_target_pairs={{0,2},{1,3},{2,0},{3,1},{4,6},{5,7},{6,4},{7,5},{8,10},{9,11},{10,... | collective-permute-start | bytes 589832 | tf_op jit(solution)/shard_map/ppermute | solution.py:473
  157.8 12.7 %collective-permute-start.25 = (bf16[3,64,512]{2,1,0:T(8,128)(2,1)S(1)}, bf16[3,64,512]{2,1,0:T(8,128)(2,1)S(1)}, u32[]{:S(2)}, u32[]{:S(2)}) collective-permute-start(bf16[3,64,512]{2,1,0:T(8,128)(2,1)S(1)} %get-tuple-element.73), channel_id=1, source_target_pairs={{0,4},{4,0},{8,12},{12,8},{16,20},{20,16},{24,28},{28,24},{1,5},{5... | collective-permute-start | bytes 589832 | tf_op jit(solution)/shard_map/ppermute | solution.py:467
  158.4 15.6 %collective-permute-start.26 = (bf16[3,64,512]{2,1,0:T(8,128)(2,1)S(1)}, bf16[3,64,512]{2,1,0:T(8,128)(2,1)S(1)}, u32[]{:S(2)}, u32[]{:S(2)}) collective-permute-start(bf16[3,64,512]{2,1,0:T(8,128)(2,1)S(1)} %get-tuple-element.74), channel_id=1, source_target_pairs={{0,6},{1,7},{2,4},{3,5},{4,2},{5,3},{6,0},{7,1},{8,14},{9,15},{10,... | collective-permute-start | bytes 589832 | tf_op jit(solution)/shard_map/ppermute | solution.py:549
  (9 other events, 8.7 us)

commit v24 on v23

--- a/solution.py
+++ b/solution.py
@@ -529,25 +529,28 @@
         (z == 0) | (z == 3), low_o.reshape(out_weight.shape), jnp.concatenate([o[: 2 * tokens] for o in after(ob, own[1])]))
     attended.append(merged(1, (w_far, attended[0][1], w_near)))
     weights = {0: out_weight, 1: w_near, 2: w_far, 3: w_other}
-    names = [(0, 0), (0, 1)]
-    size, pair = summed(at, names)
-    both = struct(size[:1] + (2,) + size[1:], BF16)
-    stay, to_y = whole_call(halve_kernel, at, pair, [both] * 2, "halve", 2)
-    from_y = head_perm(to_y, 2)
-    mine, to_x = whole_call(row_kernel, at, [stay, from_y], [struct(size, BF16)] * 2, "rows", 1)
-    parts_out += [mine, swap(to_x)]
-    plan.append((names, 1))
-
     diagonal = [
         ((2 * i + j) * 4 + h, (2 * i + 1 - j) * 4 + (h ^ 2)) for i in range(4) for j in range(2) for h in range(4)
     ]
-    turn = after(at, mine)
-    for names in ([(1, 0), (1, 1), (0, 2)], [(1, 2), (1, 3), (0, 3)]):
+    turn = at
+    groups = [
+        ([(0, 0), (0, 1)], 1),
+        ([(1, 0), (1, 1), (0, 2)], 1),
+        ([(1, 2), (1, 3), (0, 3)], 2),
+    ]
+    for index, (names, hops) in enumerate(groups):
         size, pair = summed(turn, names)
-        turn = after(at, pair[0])
-        stay, to_y, to_x, to_xy = whole_call(split_kernel, at, pair, [struct(size, BF16)] * 4, "split", 2)
-        parts_out += [stay, head_perm(to_y, 2), swap(to_x), lax.ppermute(to_xy, ("seq", "head"), diagonal)]
-        plan.append((names, 2))
+        plan.append((names, hops))
+        if hops == 1:
+            both = struct(size[:1] + (2,) + size[1:], BF16)
+            stay, to_y = whole_call(halve_kernel, at, pair, [both] * 2, "halve", 2)
+            from_y = head_perm(to_y, 2)
+            mine, to_x = whole_call(row_kernel, at, [stay, from_y], [struct(size, BF16)] * 2, "rows", 1)
+            parts_out += [mine, swap(to_x)]
+        else:
+            stay, to_y, to_x, to_xy = whole_call(split_kernel, at, pair, [struct(size, BF16)] * 4, "split", 2)
+            parts_out += [stay, head_perm(to_y, 2), swap(to_x), lax.ppermute(to_xy, ("seq", "head"), diagonal)]
+        turn = after(at, mine if index == 0 else pair[0])
     (out,) = whole_call(
         functools.partial(place_kernel, plan), at, parts_out,
         [struct((cols // 4, 8 * out_weight.shape[1]), BF16)], "place", 2)

time: 178 us -> 182 us (1.022)
    ppermute x6, waiting for transfers between devices: 5.39 us -> 15.7 us  [head_perm(): return lax.ppermute(array, 'head', [(i, i ^ flip) for i in range(4)])]
    ppermute x2 -> x1, waiting for transfers between devices: 7.63 us -> 0.01 us  [body_eight(): lax.ppermute(to_xy, ('seq', 'head'), diagonal)]
    ppermute x18, starting transfers between devices: 35.9 us -> 38.6 us  [seq_perm(): return lax.ppermute(array, 'seq', pairs)]
    pallas_call x10 -> x11, Pallas kernels: 14.4 us -> 15 us  [whole_call(): pl.pallas_call(kernel, out_shape=outs, in_specs=[pl.BlockSpec(memory_spac...]
  transfers between devices with their start and end apart: 27 -> 26, of which waited for: 14 -> 11; matrix products, arithmetic and copies ran while one was open for 5% -> 5% of each run, Pallas kernels for 23% -> 23%
where the time goes in v24:
time: 182 us; the launch traced here: 179 us
  waiting for transfers between devices  70.3 us (39%)
  starting transfers between devices  45.6 us (25%)
  Pallas kernels  42.1 us (23%)
  local copies, waits for them, and re-layouts  14.3 us (8%)
  other arithmetic  6.3 us (3%)
    ppermute x18, waiting for transfers between devices, seq_perm(): return lax.ppermute(array, 'seq', pairs)  48.7 us
    ppermute x18, starting transfers between devices, seq_perm(): return lax.ppermute(array, 'seq', pairs)  38.6 us
    pallas_call x4, Pallas kernels, head_call(): pl.pallas_call(kernel, out_shape=outs, grid_spec=pltpu.PrefetchScalarGrid...  27.1 us
    ppermute x6, waiting for transfers between devices, head_perm(): return lax.ppermute(array, 'head', [(i, i ^ flip) for i in range(4)])  15.7 us
    pallas_call x11, Pallas kernels, whole_call(): pl.pallas_call(kernel, out_shape=outs, in_specs=[pl.BlockSpec(memory_spac...  15 us
    unnamed x28, local copies, waits for them, and re-layouts  9.9 us
    ppermute x1, waiting for transfers between devices, body_eight(): lax.ppermute(after(jnp.where(z == 0, kv_give, block), q_o), 'seq', pairs)  5.91 us
    ppermute x6, starting transfers between devices, head_perm(): return lax.ppermute(array, 'head', [(i, i ^ flip) for i in range(4)])  4.89 us
  transfers between devices with their start and end apart: 26, of which 11 were waited for; matrix products, arithmetic and copies ran while one was open for 5% of the time, Pallas kernels for 23%

profile of v24, /device:TPU:16, one launch (start us, length us, event | category | flops | bytes accessed | tf_op | source)
XLA Modules:
  0.0 179.0 jit_solution(9031410031128831644)
XLA Ops:
  0.0 2.2 %dynamic-slice_bitcast_fusion.2 = (bf16[1,512,512]{2,1,0:T(8,128)(2,1)}, bf16[1,512,512]{2,1,0:T(8,128)(2,1)}) fusion(bf16[3,1,512,1024]{3,2,1,0:T(8,128)(2,1)} %param.2, s32[]{:T(128)S(6)} %select_n.57, s32[]{:T(128)S(6)} %select_n.56), kind=kLoop, calls=%fused_computation.6 | loop fusion | bytes 2097160 | tf_op jit(solution)/shard_map/dynamic_slice | solution.py:476
  3.7 2.3 %collective-permute-start = (bf16[1,512,512]{2,1,0:T(8,128)(2,1)}, bf16[1,512,512]{2,1,0:T(8,128)(2,1)S(1)}, u32[]{:S(2)}, u32[]{:S(2)}) collective-permute-start(bf16[1,512,512]{2,1,0:T(8,128)(2,1)} %get-tuple-element.82.q_m), channel_id=1, source_target_pairs={{16,8},{20,12},{24,16},{28,20},{17,9},{21,13},{25,17},{29,21},{18,... | collective-permute-start | bytes 1572872 | tf_op jit(solution)/shard_map/ppermute | solution.py:467
  7.5 4.5 %broadcast_select_fusion = (bf16[2,512,512]{2,1,0:T(8,128)(2,1)}, bf16[2,512,512]{2,1,0:T(8,128)(2,1)}, bf16[2,512,512]{2,1,0:T(8,128)(2,1)}, bf16[2,512,512]{2,1,0:T(8,128)(2,1)}) fusion(bf16[2,512,512]{2,1,0:T(8,128)(2,1)} %bitcast.24, pred[]{:T(512)S(6)} %eq.12, bf16[3,1,512,1024]{3,2,1,0:T(8,128)(2,1)} %param.2, s32[]{:T(128)S(6)} %select_n.57, ...), kind=kLoop, calls=%fused_computation.4 | loop fusion | flops 1048576 | bytes 7340041 | tf_op jit(solution)/shard_map/jit(_where)/select_n | solution.py:486
  12.8 3.3 %collective-permute-done.1.q_o = bf16[1,512,512]{2,1,0:T(8,128)(2,1)S(1)} collective-permute-done((bf16[1,512,512]{2,1,0:T(8,128)(2,1)}, bf16[1,512,512]{2,1,0:T(8,128)(2,1)S(1)}, u32[]{:S(2)}, u32[]{:S(2)}) %collective-permute-start.1) | collective-permute-done | bytes 524320 | tf_op jit(solution)/shard_map/ppermute | solution.py:467
  16.1 4.6 %collective-permute-done.qa_m = bf16[1,512,512]{2,1,0:T(8,128)(2,1)S(1)} collective-permute-done((bf16[1,512,512]{2,1,0:T(8,128)(2,1)}, bf16[1,512,512]{2,1,0:T(8,128)(2,1)S(1)}, u32[]{:S(2)}, u32[]{:S(2)}) %collective-permute-start) | collective-permute-done | bytes 524320 | tf_op jit(solution)/shard_map/ppermute | solution.py:467
  22.0 1.6 collective-permute-start.7
  24.3 11.0 %collective-permute-start.2 = (bf16[1,512,512]{2,1,0:T(8,128)(2,1)}, bf16[1,512,512]{2,1,0:T(8,128)(2,1)S(1)}, u32[]{:S(2)}, u32[]{:S(2)}) collective-permute-start(bf16[1,512,512]{2,1,0:T(8,128)(2,1)} %copy-done.4), channel_id=1, source_target_pairs={{16,8},{20,12},{24,16},{28,20},{17,9},{21,13},{25,17},{29,21},{18,... | collective-permute-start | bytes 1572872 | tf_op jit(solution)/shard_map/ppermute | solution.py:467
  36.2 16.7 %collective-permute-done.2.qa_o = bf16[1,512,512]{2,1,0:T(8,128)(2,1)S(1)} collective-permute-done((bf16[1,512,512]{2,1,0:T(8,128)(2,1)}, bf16[1,512,512]{2,1,0:T(8,128)(2,1)S(1)}, u32[]{:S(2)}, u32[]{:S(2)}) %collective-permute-start.2) | collective-permute-done | bytes 524320 | tf_op jit(solution)/shard_map/ppermute | solution.py:467
  53.8 1.9 %collective-permute-start.12 = (bf16[1024,512]{1,0:T(8,128)(2,1)S(1)}, bf16[1024,512]{1,0:T(8,128)(2,1)}, u32[]{:S(2)}, u32[]{:S(2)}) collective-permute-start(bf16[1024,512]{1,0:T(8,128)(2,1)S(1)} %copy-done), channel_id=1, source_target_pairs={{0,16},{4,20},{16,0},{20,4},{24,8},{28,12},{1,17},{5,21},{17,1},{2... | collective-permute-start | bytes 3145736 | tf_op jit(solution)/shard_map/ppermute | solution.py:467
  55.8 5.9 %collective-permute-done.7.refs_1_ = bf16[2,512,512]{2,1,0:T(8,128)(2,1)S(1)} collective-permute-done((bf16[2,512,512]{2,1,0:T(8,128)(2,1)}, bf16[2,512,512]{2,1,0:T(8,128)(2,1)S(1)}, u32[]{:S(2)}, u32[]{:S(2)}) %collective-permute-start.7) | collective-permute-done | bytes 1048608 | tf_op jit(solution)/shard_map/ppermute | solution.py:486
  66.1 6.0 %upper_rows.2 = (bf16[528,512]{1,0:T(8,128)(2,1)}, bf16[528,512]{1,0:T(8,128)(2,1)}) custom-call(s32[4]{0:T(128)S(1)} %pad_add_fusion.at, bf16[1,512,512]{2,1,0:T(8,128)(2,1)S(1)} %copy-done.8, bf16[1,512,512]{2,1,0:T(8,128)(2,1)S(1)} %copy-done.12, bf16[1,512,512]{2,1,0:T(8,128)(2,1)} %collective-permute-done.3.qb_m, bf16[1,512,512]{2,1,0:T(8,128)(2,1)S(1)} %copy-done.10, ...), custom_call_target="tpu_custom_call" | custom-call | flops 700000000 | bytes 1024 | tf_op jit(solution)/shard_map/upper_rows/pallas_call | solution.py:340
  73.3 4.6 %collective-permute-start.8 = (bf16[528,512]{1,0:T(8,128)(2,1)}, bf16[528,512]{1,0:T(8,128)(2,1)}, u32[]{:S(2)}, u32[]{:S(2)}) collective-permute-start(bf16[528,512]{1,0:T(8,128)(2,1)} %get-tuple-element.42), channel_id=1, source_target_pairs={{8,16},{12,20},{16,24},{20,28},{9,17},{13,21},{17,25},{21,29},{10,... | collective-permute-start | bytes 1622024 | tf_op jit(solution)/shard_map/ppermute | solution.py:467
  77.9 6.0 %upper_rows.3 = (bf16[528,512]{1,0:T(8,128)(2,1)S(1)}, bf16[528,512]{1,0:T(8,128)(2,1)}) custom-call(s32[4]{0:T(128)S(1)} %pad_add_fusion.at, bf16[1,512,512]{2,1,0:T(8,128)(2,1)S(1)} %copy-done.8, bf16[1,512,512]{2,1,0:T(8,128)(2,1)S(1)} %copy-done.12, bf16[1,512,512]{2,1,0:T(8,128)(2,1)} %collective-permute-done.3.qb_m, ...), custom_call_target="tpu_custom_call" | custom-call | flops 700000000 | bytes 1024 | tf_op jit(solution)/shard_map/upper_rows/pallas_call | solution.py:340
  86.0 4.7 %collective-permute-start.16 = (bf16[528,512]{1,0:T(8,128)(2,1)}, bf16[528,512]{1,0:T(8,128)(2,1)S(1)}, u32[]{:S(2)}, u32[]{:S(2)}) collective-permute-start(bf16[528,512]{1,0:T(8,128)(2,1)} %copy-done.13), channel_id=1, source_target_pairs={{8,16},{12,20},{16,24},{20,28},{9,17},{13,21},{17,25},{21,29},{10,... | collective-permute-start | bytes 1622024 | tf_op jit(solution)/shard_map/ppermute | solution.py:467
  93.0 7.6 %own_rows.2.own = bf16[528,512]{1,0:T(8,128)(2,1)S(1)} custom-call(s32[4]{0:T(128)S(1)} %pad_add_fusion.at, bf16[1,512,512]{2,1,0:T(8,128)(2,1)} %get-tuple-element.82.q_m, bf16[1,512,512]{2,1,0:T(8,128)(2,1)S(1)} %copy-done.5, bf16[2,512,512]{2,1,0:T(8,128)(2,1)S(1)} %copy-done.2, bf16[2,512,512]{2,1,0:T(8,128)(2,1)} %collective-permute-done.5.kv_o, ...), custom_call_target="tpu_custom_call" | custom-call | flops 600000000 | bytes 1024 | tf_op jit(solution)/shard_map/own_rows/pallas_call | solution.py:340
  100.6 6.3 %collective-permute-done.8.oa = bf16[528,512]{1,0:T(8,128)(2,1)} collective-permute-done((bf16[528,512]{1,0:T(8,128)(2,1)}, bf16[528,512]{1,0:T(8,128)(2,1)}, u32[]{:S(2)}, u32[]{:S(2)}) %collective-permute-start.8) | collective-permute-done | bytes 540704 | tf_op jit(solution)/shard_map/ppermute | solution.py:467
  106.9 1.8 %merge.2 = bf16[2,256,512]{2,1,0:T(8,128)(2,1)S(1)} custom-call(s32[4]{0:T(128)S(1)} %pad_add_fusion.at, bf16[528,512]{1,0:T(8,128)(2,1)S(1)} %own_rows.2.own, bf16[528,512]{1,0:T(8,128)(2,1)} %collective-permute-done.8.oa, bf16[528,512]{1,0:T(8,128)(2,1)} %collective-permute-done.9.ob), custom_call_target="tpu_custom_call" | custom-call | flops 200000000 | bytes 1024 | tf_op jit(solution)/shard_map/merge/pallas_call | solution.py:390
  110.7 7.6 %own_rows.3.own = bf16[528,512]{1,0:T(8,128)(2,1)S(1)} custom-call(s32[4]{0:T(128)S(1)} %pad_add_fusion.at, bf16[1,512,512]{2,1,0:T(8,128)(2,1)} %get-tuple-element.82.q_m, bf16[1,512,512]{2,1,0:T(8,128)(2,1)S(1)} %copy-done.6, bf16[2,512,512]{2,1,0:T(8,128)(2,1)S(1)} %copy-done.3, bf16[2,512,512]{2,1,0:T(8,128)(2,1)} %collective-permute-done.5.kv_o, ...), custom_call_target="tpu_custom_call" | custom-call | flops 600000000 | bytes 1024 | tf_op jit(solution)/shard_map/own_rows/pallas_call | solution.py:340
  120.9 1.8 %project.3 = (bf16[2,2,2,64,512]{4,3,2,1,0:T(8,128)(2,1)S(1)}, bf16[2,2,2,64,512]{4,3,2,1,0:T(8,128)(2,1)S(1)}) custom-call(s32[4]{0:T(128)S(1)} %pad_add_fusion.at, bf16[2,2,2,64,512]{4,3,2,1,0:T(8,128)(2,1)S(1)} %bitcast.25, bf16[2,2,2,64,512]{4,3,2,1,0:T(8,128)(2,1)S(1)} %bitcast.30, bf16[1024,512]{1,0:T(8,128)(2,1)S(1)} %copy-done, ...), custom_call_target="tpu_custom_call" | custom-call | flops 200000000 | bytes 1024 | tf_op jit(solution)/shard_map/project/pallas_call | solution.py:390
  122.8 1.7 collective-permute-start.21
  124.5 4.4 %collective-permute-done.16.oa = bf16[528,512]{1,0:T(8,128)(2,1)S(1)} collective-permute-done((bf16[528,512]{1,0:T(8,128)(2,1)}, bf16[528,512]{1,0:T(8,128)(2,1)S(1)}, u32[]{:S(2)}, u32[]{:S(2)}) %collective-permute-start.16) | collective-permute-done | bytes 540704 | tf_op jit(solution)/shard_map/ppermute | solution.py:467
  128.9 1.7 merge.3
  131.9 1.6 collective-permute-start.14
  133.4 5.4 %collective-permute-done.14.got = bf16[2,2,64,512]{3,2,1,0:T(8,128)(2,1)S(1)} collective-permute-done((bf16[2,2,64,512]{3,2,1,0:T(8,128)(2,1)S(1)}, bf16[2,2,64,512]{3,2,1,0:T(8,128)(2,1)S(1)}, u32[]{:S(2)}, u32[]{:S(2)}) %collective-permute-start.14) | collective-permute-done | bytes 262176 | tf_op jit(solution)/shard_map/ppermute | solution.py:473
  139.4 4.0 %collective-permute-done.17 = bf16[2,256,512]{2,1,0:T(8,128)(2,1)S(1)} collective-permute-done((bf16[2,256,512]{2,1,0:T(8,128)(2,1)S(1)}, bf16[2,256,512]{2,1,0:T(8,128)(2,1)S(1)}, u32[]{:S(2)}, u32[]{:S(2)}) %collective-permute-start.17) | collective-permute-done | bytes 524320 | tf_op jit(solution)/shard_map/ppermute | solution.py:467
  143.4 2.3 %project.4 = (bf16[3,2,2,64,512]{4,3,2,1,0:T(8,128)(2,1)S(1)}, bf16[3,2,2,64,512]{4,3,2,1,0:T(8,128)(2,1)S(1)}) custom-call(s32[4]{0:T(128)S(1)} %pad_add_fusion.at, bf16[2,2,2,64,512]{4,3,2,1,0:T(8,128)(2,1)S(1)} %bitcast.28, bf16[2,2,2,64,512]{4,3,2,1,0:T(8,128)(2,1)S(1)} %bitcast.33, bf16[1024,512]{1,0:T(8,128)(2,1)S(1)} %copy-done, ...), custom_call_target="tpu_custom_call" | custom-call | flops 300000000 | bytes 1024 | tf_op jit(solution)/shard_map/project/pallas_call | solution.py:390
  145.9 2.5 %collective-permute-done.21.refs_3_ = bf16[1024,512]{1,0:T(8,128)(2,1)S(1)} collective-permute-done((bf16[1024,512]{1,0:T(8,128)(2,1)S(1)}, bf16[1024,512]{1,0:T(8,128)(2,1)S(1)}, u32[]{:S(2)}, u32[]{:S(2)}) %collective-permute-start.21) | collective-permute-done | bytes 1048608 | tf_op jit(solution)/shard_map/ppermute | solution.py:467
  148.3 2.3 %project.5 = (bf16[3,2,2,64,512]{4,3,2,1,0:T(8,128)(2,1)S(1)}, bf16[3,2,2,64,512]{4,3,2,1,0:T(8,128)(2,1)S(1)}) custom-call(s32[4]{0:T(128)S(1)} %pad_add_fusion.at, bf16[2,2,2,64,512]{4,3,2,1,0:T(8,128)(2,1)S(1)} %bitcast.29, bf16[2,2,2,64,512]{4,3,2,1,0:T(8,128)(2,1)S(1)} %bitcast.34, bf16[1024,512]{1,0:T(8,128)(2,1)S(1)} %bitcast_select_fusion.refs_6_.refs_2_, ...), custom_call_target="tpu_custom_call" | custom-call | flops 300000000 | bytes 1024 | tf_op jit(solution)/shard_map/project/pallas_call | solution.py:390
  151.5 1.6 collective-permute-start.19
  157.4 10.3 %collective-permute-done.19.got = bf16[3,2,64,512]{3,2,1,0:T(8,128)(2,1)S(1)} collective-permute-done((bf16[3,2,64,512]{3,2,1,0:T(8,128)(2,1)S(1)}, bf16[3,2,64,512]{3,2,1,0:T(8,128)(2,1)S(1)}, u32[]{:S(2)}, u32[]{:S(2)}) %collective-permute-start.19) | collective-permute-done | bytes 393248 | tf_op jit(solution)/shard_map/ppermute | solution.py:473
  170.4 6.9 %collective-permute-done.15.refs_1_ = bf16[2,64,512]{2,1,0:T(8,128)(2,1)S(1)} collective-permute-done((bf16[2,64,512]{2,1,0:T(8,128)(2,1)S(1)}, bf16[2,64,512]{2,1,0:T(8,128)(2,1)S(1)}, u32[]{:S(2)}, u32[]{:S(2)}) %collective-permute-start.15) | collective-permute-done | bytes 131104 | tf_op jit(solution)/shard_map/ppermute | solution.py:467
  177.3 1.7 place.1
  (70 shorter events, 31.8 us)
Async XLA Ops:
  2.2 13.9 %collective-permute-start.1 = (bf16[1,512,512]{2,1,0:T(8,128)(2,1)}, bf16[1,512,512]{2,1,0:T(8,128)(2,1)S(1)}, u32[]{:S(2)}, u32[]{:S(2)}) collective-permute-start(bf16[1,512,512]{2,1,0:T(8,128)(2,1)} %get-tuple-element.81), channel_id=1, source_target_pairs={{0,4},{4,0},{8,12},{12,8},{16,20},{20,16},{24,28},{28,24},{1,5},{5... | collective-permute-start | bytes 1572872 | tf_op jit(solution)/shard_map/ppermute | solution.py:467
  3.7 16.9 %collective-permute-start = (bf16[1,512,512]{2,1,0:T(8,128)(2,1)}, bf16[1,512,512]{2,1,0:T(8,128)(2,1)S(1)}, u32[]{:S(2)}, u32[]{:S(2)}) collective-permute-start(bf16[1,512,512]{2,1,0:T(8,128)(2,1)} %get-tuple-element.82.q_m), channel_id=1, source_target_pairs={{16,8},{20,12},{24,16},{28,20},{17,9},{21,13},{25,17},{29,21},{18,... | collective-permute-start | bytes 1572872 | tf_op jit(solution)/shard_map/ppermute | solution.py:467
  6.1 18.3 %collective-permute-start.3 = (bf16[1,512,512]{2,1,0:T(8,128)(2,1)}, bf16[1,512,512]{2,1,0:T(8,128)(2,1)}, u32[]{:S(2)}, u32[]{:S(2)}) collective-permute-start(bf16[1,512,512]{2,1,0:T(8,128)(2,1)} %get-tuple-element.82.q_m), channel_id=1, source_target_pairs={{24,8},{28,12},{25,9},{29,13},{26,10},{30,14},{27,11},{31,15}} | collective-permute-start | bytes 1572872 | tf_op jit(solution)/shard_map/ppermute | solution.py:467
  7.5 46.3 %copy-start = (bf16[1024,512]{1,0:T(8,128)(2,1)S(1)}, bf16[1024,512]{1,0:T(8,128)(2,1)}, u32[]{:S(2)}) copy-start(bf16[1024,512]{1,0:T(8,128)(2,1)} %refs_2_.7) | copy-start | bytes 3145732
  12.1 43.7 %collective-permute-start.6 = (bf16[2,512,512]{2,1,0:T(8,128)(2,1)}, bf16[2,512,512]{2,1,0:T(8,128)(2,1)S(1)}, u32[]{:S(2)}, u32[]{:S(2)}) collective-permute-start(bf16[2,512,512]{2,1,0:T(8,128)(2,1)} %get-tuple-element.79), channel_id=1, source_target_pairs={{0,8},{4,12},{8,24},{12,28},{1,9},{5,13},{9,25},{13,29},{2,10},{6,... | collective-permute-start | bytes 3145736 | tf_op jit(solution)/shard_map/ppermute | solution.py:467
  16.1 5.4 %copy-start.4 = (bf16[1,512,512]{2,1,0:T(8,128)(2,1)}, bf16[1,512,512]{2,1,0:T(8,128)(2,1)S(1)}, u32[]{:S(2)}) copy-start(bf16[1,512,512]{2,1,0:T(8,128)(2,1)S(1)} %collective-permute-done.1.q_o) | copy-start | bytes 1572868
  21.5 34.3 %collective-permute-start.5 = (bf16[2,512,512]{2,1,0:T(8,128)(2,1)}, bf16[2,512,512]{2,1,0:T(8,128)(2,1)}, u32[]{:S(2)}, u32[]{:S(2)}) collective-permute-start(bf16[2,512,512]{2,1,0:T(8,128)(2,1)} %get-tuple-element.40), channel_id=1, source_target_pairs={{0,4},{4,0},{8,12},{12,8},{16,20},{20,16},{24,28},{28,24},{1,5},{5... | collective-permute-start | bytes 3145736 | tf_op jit(solution)/shard_map/ppermute | solution.py:467
  22.0 39.7 %collective-permute-start.7 = (bf16[2,512,512]{2,1,0:T(8,128)(2,1)}, bf16[2,512,512]{2,1,0:T(8,128)(2,1)S(1)}, u32[]{:S(2)}, u32[]{:S(2)}) collective-permute-start(bf16[2,512,512]{2,1,0:T(8,128)(2,1)} %get-tuple-element.41), channel_id=1, source_target_pairs={{0,12},{4,8},{8,0},{12,4},{16,24},{20,28},{1,13},{5,9},{9,1},{13,5... | collective-permute-start | bytes 3145736 | tf_op jit(solution)/shard_map/ppermute | solution.py:486
  23.6 11.8 %collective-permute-start.4 = (bf16[1,512,512]{2,1,0:T(8,128)(2,1)}, bf16[1,512,512]{2,1,0:T(8,128)(2,1)S(1)}, u32[]{:S(2)}, u32[]{:S(2)}) collective-permute-start(bf16[1,512,512]{2,1,0:T(8,128)(2,1)} %copy-done.4), channel_id=1, source_target_pairs={{24,8},{28,12},{25,9},{29,13},{26,10},{30,14},{27,11},{31,15}} | collective-permute-start | bytes 1572872 | tf_op jit(solution)/shard_map/ppermute | solution.py:467
  24.3 28.6 %collective-permute-start.2 = (bf16[1,512,512]{2,1,0:T(8,128)(2,1)}, bf16[1,512,512]{2,1,0:T(8,128)(2,1)S(1)}, u32[]{:S(2)}, u32[]{:S(2)}) collective-permute-start(bf16[1,512,512]{2,1,0:T(8,128)(2,1)} %copy-done.4), channel_id=1, source_target_pairs={{16,8},{20,12},{24,16},{28,20},{17,9},{21,13},{25,17},{29,21},{18,... | collective-permute-start | bytes 1572872 | tf_op jit(solution)/shard_map/ppermute | solution.py:467
  53.8 55.6 %collective-permute-start.12 = (bf16[1024,512]{1,0:T(8,128)(2,1)S(1)}, bf16[1024,512]{1,0:T(8,128)(2,1)}, u32[]{:S(2)}, u32[]{:S(2)}) collective-permute-start(bf16[1024,512]{1,0:T(8,128)(2,1)S(1)} %copy-done), channel_id=1, source_target_pairs={{0,16},{4,20},{16,0},{20,4},{24,8},{28,12},{1,17},{5,21},{17,1},{2... | collective-permute-start | bytes 3145736 | tf_op jit(solution)/shard_map/ppermute | solution.py:467
  61.7 1.2 copy-start.1
  72.0 28.6 %collective-permute-start.9 = (bf16[528,512]{1,0:T(8,128)(2,1)}, bf16[528,512]{1,0:T(8,128)(2,1)}, u32[]{:S(2)}, u32[]{:S(2)}) collective-permute-start(bf16[528,512]{1,0:T(8,128)(2,1)} %get-tuple-element.47), channel_id=1, source_target_pairs={{8,24},{12,28},{0,8},{4,12},{24,16},{28,20},{9,25},{13,29},{1,9},{... | collective-permute-start | bytes 1622024 | tf_op jit(solution)/shard_map/ppermute | solution.py:467
  73.3 33.6 %collective-permute-start.8 = (bf16[528,512]{1,0:T(8,128)(2,1)}, bf16[528,512]{1,0:T(8,128)(2,1)}, u32[]{:S(2)}, u32[]{:S(2)}) collective-permute-start(bf16[528,512]{1,0:T(8,128)(2,1)} %get-tuple-element.42), channel_id=1, source_target_pairs={{8,16},{12,20},{16,24},{20,28},{9,17},{13,21},{17,25},{21,29},{10,... | collective-permute-start | bytes 1622024 | tf_op jit(solution)/shard_map/ppermute | solution.py:467
  84.7 33.6 %collective-permute-start.11 = (bf16[528,512]{1,0:T(8,128)(2,1)}, bf16[528,512]{1,0:T(8,128)(2,1)}, u32[]{:S(2)}, u32[]{:S(2)}) collective-permute-start(bf16[528,512]{1,0:T(8,128)(2,1)} %get-tuple-element.48), channel_id=1, source_target_pairs={{8,24},{12,28},{0,8},{4,12},{24,16},{28,20},{9,25},{13,29},{1,9},{... | collective-permute-start | bytes 1622024 | tf_op jit(solution)/shard_map/ppermute | solution.py:467
  86.0 42.9 %collective-permute-start.16 = (bf16[528,512]{1,0:T(8,128)(2,1)}, bf16[528,512]{1,0:T(8,128)(2,1)S(1)}, u32[]{:S(2)}, u32[]{:S(2)}) collective-permute-start(bf16[528,512]{1,0:T(8,128)(2,1)} %copy-done.13), channel_id=1, source_target_pairs={{8,16},{12,20},{16,24},{20,28},{9,17},{13,21},{17,25},{21,29},{10,... | collective-permute-start | bytes 1622024 | tf_op jit(solution)/shard_map/ppermute | solution.py:467
  90.7 1.2 copy-start.2
  100.6 10.1 %copy-start.3 = (bf16[2,512,512]{2,1,0:T(8,128)(2,1)S(1)}, bf16[2,512,512]{2,1,0:T(8,128)(2,1)}, u32[]{:S(2)}) copy-start(bf16[2,512,512]{2,1,0:T(8,128)(2,1)} %get-tuple-element.80.kv_m) | copy-start | bytes 3145732
  100.6 10.1 %copy-start.6 = (bf16[1,512,512]{2,1,0:T(8,128)(2,1)S(1)}, bf16[1,512,512]{2,1,0:T(8,128)(2,1)}, u32[]{:S(2)}) copy-start(bf16[1,512,512]{2,1,0:T(8,128)(2,1)} %copy-done.4) | copy-start | bytes 1572868
  108.8 12.1 %collective-permute-start.10 = (bf16[2,256,512]{2,1,0:T(8,128)(2,1)S(1)}, bf16[2,256,512]{2,1,0:T(8,128)(2,1)S(1)}, u32[]{:S(2)}, u32[]{:S(2)}) collective-permute-start(bf16[2,256,512]{2,1,0:T(8,128)(2,1)S(1)} %merge.2), channel_id=1, source_target_pairs={{0,4},{4,0},{8,12},{12,8},{16,20},{20,16},{24,28},{28,24},{1,5},{5... | collective-permute-start | bytes 1572872 | tf_op jit(solution)/shard_map/ppermute | solution.py:467
  122.7 8.5 %collective-permute-start.13 = (bf16[2,2,2,64,512]{4,3,2,1,0:T(8,128)(2,1)S(1)}, bf16[2,2,2,64,512]{4,3,2,1,0:T(8,128)(2,1)S(1)}, u32[]{:S(2)}, u32[]{:S(2)}) collective-permute-start(bf16[2,2,2,64,512]{4,3,2,1,0:T(8,128)(2,1)S(1)} %get-tuple-element.55), channel_id=1, source_target_pairs={{0,1},{1,0},{2,3},{3,2},{4,5},{5,4},{6,7},{7,6},{8,9},{9,8},{10,11... | collective-permute-start | bytes 1572872 | tf_op jit(solution)/shard_map/ppermute | solution.py:473
  122.8 25.6 %collective-permute-start.21 = (bf16[1024,512]{1,0:T(8,128)(2,1)S(1)}, bf16[1024,512]{1,0:T(8,128)(2,1)S(1)}, u32[]{:S(2)}, u32[]{:S(2)}) collective-permute-start(bf16[1024,512]{1,0:T(8,128)(2,1)S(1)} %bitcast_select_fusion.refs_6_.refs_2_), channel_id=1, source_target_pairs={{0,8},{4,12},{8,0},{12,4},{16,24},{20,28},{24,16},{28,20},{1,9},{5... | collective-permute-start | bytes 3145736 | tf_op jit(solution)/shard_map/ppermute | solution.py:467
  130.6 12.9 %collective-permute-start.17 = (bf16[2,256,512]{2,1,0:T(8,128)(2,1)S(1)}, bf16[2,256,512]{2,1,0:T(8,128)(2,1)S(1)}, u32[]{:S(2)}, u32[]{:S(2)}) collective-permute-start(bf16[2,256,512]{2,1,0:T(8,128)(2,1)S(1)} %merge.3), channel_id=1, source_target_pairs={{0,4},{4,0},{8,12},{12,8},{16,20},{20,16},{24,28},{28,24},{1,5},{5... | collective-permute-start | bytes 1572872 | tf_op jit(solution)/shard_map/ppermute | solution.py:467
  131.9 7.0 %collective-permute-start.14 = (bf16[2,2,64,512]{3,2,1,0:T(8,128)(2,1)S(1)}, bf16[2,2,64,512]{3,2,1,0:T(8,128)(2,1)S(1)}, u32[]{:S(2)}, u32[]{:S(2)}) collective-permute-start(bf16[2,2,64,512]{3,2,1,0:T(8,128)(2,1)S(1)} %get-tuple-element.57), channel_id=1, source_target_pairs={{0,2},{1,3},{2,0},{3,1},{4,6},{5,7},{6,4},{7,5},{8,10},{9,11},{10,... | collective-permute-start | bytes 786440 | tf_op jit(solution)/shard_map/ppermute | solution.py:473
  145.8 5.0 %collective-permute-start.18 = (bf16[3,2,2,64,512]{4,3,2,1,0:T(8,128)(2,1)S(1)}, bf16[3,2,2,64,512]{4,3,2,1,0:T(8,128)(2,1)S(1)}, u32[]{:S(2)}, u32[]{:S(2)}) collective-permute-start(bf16[3,2,2,64,512]{4,3,2,1,0:T(8,128)(2,1)S(1)} %get-tuple-element.63), channel_id=1, source_target_pairs={{0,1},{1,0},{2,3},{3,2},{4,5},{5,4},{6,7},{7,6},{8,9},{9,8},{10,11... | collective-permute-start | bytes 2359304 | tf_op jit(solution)/shard_map/ppermute | solution.py:473
  150.7 2.4 %collective-permute-start.22 = (bf16[3,2,2,64,512]{4,3,2,1,0:T(8,128)(2,1)S(1)}, bf16[3,2,2,64,512]{4,3,2,1,0:T(8,128)(2,1)S(1)}, u32[]{:S(2)}, u32[]{:S(2)}) collective-permute-start(bf16[3,2,2,64,512]{4,3,2,1,0:T(8,128)(2,1)S(1)} %get-tuple-element.70), channel_id=1, source_target_pairs={{0,1},{1,0},{2,3},{3,2},{4,5},{5,4},{6,7},{7,6},{8,9},{9,8},{10,11... | collective-permute-start | bytes 2359304 | tf_op jit(solution)/shard_map/ppermute | solution.py:473
  151.5 16.2 %collective-permute-start.19 = (bf16[3,2,64,512]{3,2,1,0:T(8,128)(2,1)S(1)}, bf16[3,2,64,512]{3,2,1,0:T(8,128)(2,1)S(1)}, u32[]{:S(2)}, u32[]{:S(2)}) collective-permute-start(bf16[3,2,64,512]{3,2,1,0:T(8,128)(2,1)S(1)} %get-tuple-element.65), channel_id=1, source_target_pairs={{0,2},{1,3},{2,0},{3,1},{4,6},{5,7},{6,4},{7,5},{8,10},{9,11},{10,... | collective-permute-start | bytes 1179656 | tf_op jit(solution)/shard_map/ppermute | solution.py:473
  153.8 23.5 %collective-permute-start.23 = (bf16[3,64,512]{2,1,0:T(8,128)(2,1)S(1)}, bf16[3,64,512]{2,1,0:T(8,128)(2,1)S(1)}, u32[]{:S(2)}, u32[]{:S(2)}) collective-permute-start(bf16[3,64,512]{2,1,0:T(8,128)(2,1)S(1)} %get-tuple-element.72), channel_id=1, source_target_pairs={{0,2},{1,3},{2,0},{3,1},{4,6},{5,7},{6,4},{7,5},{8,10},{9,11},{10,... | collective-permute-start | bytes 589832 | tf_op jit(solution)/shard_map/ppermute | solution.py:473
  155.3 22.0 %collective-permute-start.24 = (bf16[3,64,512]{2,1,0:T(8,128)(2,1)S(1)}, bf16[3,64,512]{2,1,0:T(8,128)(2,1)S(1)}, u32[]{:S(2)}, u32[]{:S(2)}) collective-permute-start(bf16[3,64,512]{2,1,0:T(8,128)(2,1)S(1)} %get-tuple-element.73), channel_id=1, source_target_pairs={{0,4},{4,0},{8,12},{12,8},{16,20},{20,16},{24,28},{28,24},{1,5},{5... | collective-permute-start | bytes 589832 | tf_op jit(solution)/shard_map/ppermute | solution.py:467
  156.8 20.5 %collective-permute-start.25 = (bf16[3,64,512]{2,1,0:T(8,128)(2,1)S(1)}, bf16[3,64,512]{2,1,0:T(8,128)(2,1)S(1)}, u32[]{:S(2)}, u32[]{:S(2)}) collective-permute-start(bf16[3,64,512]{2,1,0:T(8,128)(2,1)S(1)} %get-tuple-element.74), channel_id=1, source_target_pairs={{0,6},{1,7},{2,4},{3,5},{4,2},{5,3},{6,0},{7,1},{8,14},{9,15},{10,... | collective-permute-start | bytes 589832 | tf_op jit(solution)/shard_map/ppermute | solution.py:552
  168.3 9.0 %collective-permute-start.20 = (bf16[3,64,512]{2,1,0:T(8,128)(2,1)S(1)}, bf16[3,64,512]{2,1,0:T(8,128)(2,1)S(1)}, u32[]{:S(2)}, u32[]{:S(2)}) collective-permute-start(bf16[3,64,512]{2,1,0:T(8,128)(2,1)S(1)} %get-tuple-element.67), channel_id=1, source_target_pairs={{0,4},{4,0},{8,12},{12,8},{16,20},{20,16},{24,28},{28,24},{1,5},{5... | collective-permute-start | bytes 589832 | tf_op jit(solution)/shard_map/ppermute | solution.py:467
  169.9 7.4 %collective-permute-start.15 = (bf16[2,64,512]{2,1,0:T(8,128)(2,1)S(1)}, bf16[2,64,512]{2,1,0:T(8,128)(2,1)S(1)}, u32[]{:S(2)}, u32[]{:S(2)}) collective-permute-start(bf16[2,64,512]{2,1,0:T(8,128)(2,1)S(1)} %get-tuple-element.59), channel_id=1, source_target_pairs={{0,4},{4,0},{8,12},{12,8},{16,20},{20,16},{24,28},{28,24},{1,5},{5... | collective-permute-start | bytes 393224 | tf_op jit(solution)/shard_map/ppermute | solution.py:467
  (8 other events, 7.5 us)

commit v25 on v23

--- a/solution.py
+++ b/solution.py
@@ -544,7 +544,7 @@
     turn = after(at, mine)
     for names in ([(1, 0), (1, 1), (0, 2)], [(1, 2), (1, 3), (0, 3)]):
         size, pair = summed(turn, names)
-        turn = after(at, pair[0])
+        turn = after(at, pair[0], parts_out[1])
         stay, to_y, to_x, to_xy = whole_call(split_kernel, at, pair, [struct(size, BF16)] * 4, "split", 2)
         parts_out += [stay, head_perm(to_y, 2), swap(to_x), lax.ppermute(to_xy, ("seq", "head"), diagonal)]
         plan.append((names, 2))

time: 178 us -> 179 us (level)
  waiting for transfers between devices: 68.8 us -> 70.9 us
    ppermute x6, waiting for transfers between devices: 5.39 us -> 8.99 us  [head_perm(): return lax.ppermute(array, 'head', [(i, i ^ flip) for i in range(4)])]
  transfers between devices with their start and end apart: 27 -> 27, of which waited for: 14 -> 15; matrix products, arithmetic and copies ran while one was open for 5% -> 5% of each run, Pallas kernels for 23% -> 22%
where the time goes in v25:
time: 179 us; the launch traced here: 178 us
  waiting for transfers between devices  70.9 us (40%)
  starting transfers between devices  44.5 us (25%)
  Pallas kernels  41.5 us (23%)
  local copies, waits for them, and re-layouts  14.3 us (8%)
  other arithmetic  6.32 us (4%)
    ppermute x18, waiting for transfers between devices, seq_perm(): return lax.ppermute(array, 'seq', pairs)  48.4 us
    ppermute x18, starting transfers between devices, seq_perm(): return lax.ppermute(array, 'seq', pairs)  35 us
    pallas_call x4, Pallas kernels, head_call(): pl.pallas_call(kernel, out_shape=outs, grid_spec=pltpu.PrefetchScalarGrid...  27.1 us
    pallas_call x10, Pallas kernels, whole_call(): pl.pallas_call(kernel, out_shape=outs, in_specs=[pl.BlockSpec(memory_spac...  14.4 us
    unnamed x28, local copies, waits for them, and re-layouts  9.9 us
    ppermute x6, waiting for transfers between devices, head_perm(): return lax.ppermute(array, 'head', [(i, i ^ flip) for i in range(4)])  8.99 us
    ppermute x2, waiting for transfers between devices, body_eight(): lax.ppermute(to_xy, ('seq', 'head'), diagonal)  7.65 us
    ppermute x1, waiting for transfers between devices, body_eight(): lax.ppermute(after(jnp.where(z == 0, kv_give, block), q_o), 'seq', pairs)  5.91 us
  transfers between devices with their start and end apart: 27, of which 15 were waited for; matrix products, arithmetic and copies ran while one was open for 5% of the time, Pallas kernels for 22%

profile of v25, /device:TPU:16, one launch (start us, length us, event | category | flops | bytes accessed | tf_op | source)
XLA Modules:
  0.0 177.9 jit_solution(5565049933200983657)
XLA Ops:
  0.0 2.2 %dynamic-slice_bitcast_fusion.2 = (bf16[1,512,512]{2,1,0:T(8,128)(2,1)}, bf16[1,512,512]{2,1,0:T(8,128)(2,1)}) fusion(bf16[3,1,512,1024]{3,2,1,0:T(8,128)(2,1)} %param.2, s32[]{:T(128)S(6)} %select_n.57, s32[]{:T(128)S(6)} %select_n.56), kind=kLoop, calls=%fused_computation.6 | loop fusion | bytes 2097160 | tf_op jit(solution)/shard_map/dynamic_slice | solution.py:476
  3.7 2.3 %collective-permute-start = (bf16[1,512,512]{2,1,0:T(8,128)(2,1)}, bf16[1,512,512]{2,1,0:T(8,128)(2,1)S(1)}, u32[]{:S(2)}, u32[]{:S(2)}) collective-permute-start(bf16[1,512,512]{2,1,0:T(8,128)(2,1)} %get-tuple-element.82.q_m), channel_id=1, source_target_pairs={{16,8},{20,12},{24,16},{28,20},{17,9},{21,13},{25,17},{29,21},{18,... | collective-permute-start | bytes 1572872 | tf_op jit(solution)/shard_map/ppermute | solution.py:467
  7.5 4.5 %broadcast_select_fusion = (bf16[2,512,512]{2,1,0:T(8,128)(2,1)}, bf16[2,512,512]{2,1,0:T(8,128)(2,1)}, bf16[2,512,512]{2,1,0:T(8,128)(2,1)}, bf16[2,512,512]{2,1,0:T(8,128)(2,1)}) fusion(bf16[2,512,512]{2,1,0:T(8,128)(2,1)} %bitcast.24, pred[]{:T(512)S(6)} %eq.12, bf16[3,1,512,1024]{3,2,1,0:T(8,128)(2,1)} %param.2, s32[]{:T(128)S(6)} %select_n.57, ...), kind=kLoop, calls=%fused_computation.4 | loop fusion | flops 1048576 | bytes 7340041 | tf_op jit(solution)/shard_map/jit(_where)/select_n | solution.py:486
  12.8 3.3 %collective-permute-done.1.q_o = bf16[1,512,512]{2,1,0:T(8,128)(2,1)S(1)} collective-permute-done((bf16[1,512,512]{2,1,0:T(8,128)(2,1)}, bf16[1,512,512]{2,1,0:T(8,128)(2,1)S(1)}, u32[]{:S(2)}, u32[]{:S(2)}) %collective-permute-start.1) | collective-permute-done | bytes 524320 | tf_op jit(solution)/shard_map/ppermute | solution.py:467
  16.1 4.6 %collective-permute-done.qa_m = bf16[1,512,512]{2,1,0:T(8,128)(2,1)S(1)} collective-permute-done((bf16[1,512,512]{2,1,0:T(8,128)(2,1)}, bf16[1,512,512]{2,1,0:T(8,128)(2,1)S(1)}, u32[]{:S(2)}, u32[]{:S(2)}) %collective-permute-start) | collective-permute-done | bytes 524320 | tf_op jit(solution)/shard_map/ppermute | solution.py:467
  22.0 1.6 collective-permute-start.7
  24.3 11.0 %collective-permute-start.2 = (bf16[1,512,512]{2,1,0:T(8,128)(2,1)}, bf16[1,512,512]{2,1,0:T(8,128)(2,1)S(1)}, u32[]{:S(2)}, u32[]{:S(2)}) collective-permute-start(bf16[1,512,512]{2,1,0:T(8,128)(2,1)} %copy-done.4), channel_id=1, source_target_pairs={{16,8},{20,12},{24,16},{28,20},{17,9},{21,13},{25,17},{29,21},{18,... | collective-permute-start | bytes 1572872 | tf_op jit(solution)/shard_map/ppermute | solution.py:467
  36.2 16.7 %collective-permute-done.2.qa_o = bf16[1,512,512]{2,1,0:T(8,128)(2,1)S(1)} collective-permute-done((bf16[1,512,512]{2,1,0:T(8,128)(2,1)}, bf16[1,512,512]{2,1,0:T(8,128)(2,1)S(1)}, u32[]{:S(2)}, u32[]{:S(2)}) %collective-permute-start.2) | collective-permute-done | bytes 524320 | tf_op jit(solution)/shard_map/ppermute | solution.py:467
  53.8 1.9 %collective-permute-start.12 = (bf16[1024,512]{1,0:T(8,128)(2,1)S(1)}, bf16[1024,512]{1,0:T(8,128)(2,1)}, u32[]{:S(2)}, u32[]{:S(2)}) collective-permute-start(bf16[1024,512]{1,0:T(8,128)(2,1)S(1)} %copy-done), channel_id=1, source_target_pairs={{0,16},{4,20},{16,0},{20,4},{24,8},{28,12},{1,17},{5,21},{17,1},{2... | collective-permute-start | bytes 3145736 | tf_op jit(solution)/shard_map/ppermute | solution.py:467
  55.8 5.9 %collective-permute-done.7.refs_1_ = bf16[2,512,512]{2,1,0:T(8,128)(2,1)S(1)} collective-permute-done((bf16[2,512,512]{2,1,0:T(8,128)(2,1)}, bf16[2,512,512]{2,1,0:T(8,128)(2,1)S(1)}, u32[]{:S(2)}, u32[]{:S(2)}) %collective-permute-start.7) | collective-permute-done | bytes 1048608 | tf_op jit(solution)/shard_map/ppermute | solution.py:486
  66.1 6.0 %upper_rows.2 = (bf16[528,512]{1,0:T(8,128)(2,1)}, bf16[528,512]{1,0:T(8,128)(2,1)}) custom-call(s32[4]{0:T(128)S(1)} %pad_add_fusion.at, bf16[1,512,512]{2,1,0:T(8,128)(2,1)S(1)} %copy-done.8, bf16[1,512,512]{2,1,0:T(8,128)(2,1)S(1)} %copy-done.12, bf16[1,512,512]{2,1,0:T(8,128)(2,1)} %collective-permute-done.3.qb_m, bf16[1,512,512]{2,1,0:T(8,128)(2,1)S(1)} %copy-done.10, ...), custom_call_target="tpu_custom_call" | custom-call | flops 700000000 | bytes 1024 | tf_op jit(solution)/shard_map/upper_rows/pallas_call | solution.py:340
  73.3 4.6 %collective-permute-start.8 = (bf16[528,512]{1,0:T(8,128)(2,1)}, bf16[528,512]{1,0:T(8,128)(2,1)}, u32[]{:S(2)}, u32[]{:S(2)}) collective-permute-start(bf16[528,512]{1,0:T(8,128)(2,1)} %get-tuple-element.42), channel_id=1, source_target_pairs={{8,16},{12,20},{16,24},{20,28},{9,17},{13,21},{17,25},{21,29},{10,... | collective-permute-start | bytes 1622024 | tf_op jit(solution)/shard_map/ppermute | solution.py:467
  77.9 6.0 %upper_rows.3 = (bf16[528,512]{1,0:T(8,128)(2,1)S(1)}, bf16[528,512]{1,0:T(8,128)(2,1)}) custom-call(s32[4]{0:T(128)S(1)} %pad_add_fusion.at, bf16[1,512,512]{2,1,0:T(8,128)(2,1)S(1)} %copy-done.8, bf16[1,512,512]{2,1,0:T(8,128)(2,1)S(1)} %copy-done.12, bf16[1,512,512]{2,1,0:T(8,128)(2,1)} %collective-permute-done.3.qb_m, ...), custom_call_target="tpu_custom_call" | custom-call | flops 700000000 | bytes 1024 | tf_op jit(solution)/shard_map/upper_rows/pallas_call | solution.py:340
  86.0 4.7 %collective-permute-start.16 = (bf16[528,512]{1,0:T(8,128)(2,1)}, bf16[528,512]{1,0:T(8,128)(2,1)S(1)}, u32[]{:S(2)}, u32[]{:S(2)}) collective-permute-start(bf16[528,512]{1,0:T(8,128)(2,1)} %copy-done.13), channel_id=1, source_target_pairs={{8,16},{12,20},{16,24},{20,28},{9,17},{13,21},{17,25},{21,29},{10,... | collective-permute-start | bytes 1622024 | tf_op jit(solution)/shard_map/ppermute | solution.py:467
  93.0 7.6 %own_rows.2.own = bf16[528,512]{1,0:T(8,128)(2,1)S(1)} custom-call(s32[4]{0:T(128)S(1)} %pad_add_fusion.at, bf16[1,512,512]{2,1,0:T(8,128)(2,1)} %get-tuple-element.82.q_m, bf16[1,512,512]{2,1,0:T(8,128)(2,1)S(1)} %copy-done.5, bf16[2,512,512]{2,1,0:T(8,128)(2,1)S(1)} %copy-done.2, bf16[2,512,512]{2,1,0:T(8,128)(2,1)} %collective-permute-done.5.kv_o, ...), custom_call_target="tpu_custom_call" | custom-call | flops 600000000 | bytes 1024 | tf_op jit(solution)/shard_map/own_rows/pallas_call | solution.py:340
  100.6 6.3 %collective-permute-done.8.oa = bf16[528,512]{1,0:T(8,128)(2,1)} collective-permute-done((bf16[528,512]{1,0:T(8,128)(2,1)}, bf16[528,512]{1,0:T(8,128)(2,1)}, u32[]{:S(2)}, u32[]{:S(2)}) %collective-permute-start.8) | collective-permute-done | bytes 540704 | tf_op jit(solution)/shard_map/ppermute | solution.py:467
  106.9 1.8 %merge.2 = bf16[2,256,512]{2,1,0:T(8,128)(2,1)S(1)} custom-call(s32[4]{0:T(128)S(1)} %pad_add_fusion.at, bf16[528,512]{1,0:T(8,128)(2,1)S(1)} %own_rows.2.own, bf16[528,512]{1,0:T(8,128)(2,1)} %collective-permute-done.8.oa, bf16[528,512]{1,0:T(8,128)(2,1)} %collective-permute-done.9.ob), custom_call_target="tpu_custom_call" | custom-call | flops 200000000 | bytes 1024 | tf_op jit(solution)/shard_map/merge/pallas_call | solution.py:390
  110.8 7.6 %own_rows.3.own = bf16[528,512]{1,0:T(8,128)(2,1)S(1)} custom-call(s32[4]{0:T(128)S(1)} %pad_add_fusion.at, bf16[1,512,512]{2,1,0:T(8,128)(2,1)} %get-tuple-element.82.q_m, bf16[1,512,512]{2,1,0:T(8,128)(2,1)S(1)} %copy-done.6, bf16[2,512,512]{2,1,0:T(8,128)(2,1)S(1)} %copy-done.3, bf16[2,512,512]{2,1,0:T(8,128)(2,1)} %collective-permute-done.5.kv_o, ...), custom_call_target="tpu_custom_call" | custom-call | flops 600000000 | bytes 1024 | tf_op jit(solution)/shard_map/own_rows/pallas_call | solution.py:340
  121.0 1.8 %project.3 = (bf16[2,2,2,64,512]{4,3,2,1,0:T(8,128)(2,1)S(1)}, bf16[2,2,2,64,512]{4,3,2,1,0:T(8,128)(2,1)S(1)}) custom-call(s32[4]{0:T(128)S(1)} %pad_add_fusion.at, bf16[2,2,2,64,512]{4,3,2,1,0:T(8,128)(2,1)S(1)} %bitcast.25, bf16[2,2,2,64,512]{4,3,2,1,0:T(8,128)(2,1)S(1)} %bitcast.30, bf16[1024,512]{1,0:T(8,128)(2,1)S(1)} %copy-done, ...), custom_call_target="tpu_custom_call" | custom-call | flops 200000000 | bytes 1024 | tf_op jit(solution)/shard_map/project/pallas_call | solution.py:390
  122.8 6.0 %collective-permute-done.16.oa = bf16[528,512]{1,0:T(8,128)(2,1)S(1)} collective-permute-done((bf16[528,512]{1,0:T(8,128)(2,1)}, bf16[528,512]{1,0:T(8,128)(2,1)S(1)}, u32[]{:S(2)}, u32[]{:S(2)}) %collective-permute-start.16) | collective-permute-done | bytes 540704 | tf_op jit(solution)/shard_map/ppermute | solution.py:467
  128.9 1.7 merge.3
  131.9 1.6 collective-permute-start.14
  133.4 5.4 %collective-permute-done.14.got = bf16[2,2,64,512]{3,2,1,0:T(8,128)(2,1)S(1)} collective-permute-done((bf16[2,2,64,512]{3,2,1,0:T(8,128)(2,1)S(1)}, bf16[2,2,64,512]{3,2,1,0:T(8,128)(2,1)S(1)}, u32[]{:S(2)}, u32[]{:S(2)}) %collective-permute-start.14) | collective-permute-done | bytes 262176 | tf_op jit(solution)/shard_map/ppermute | solution.py:473
  139.4 4.0 %collective-permute-done.17 = bf16[2,256,512]{2,1,0:T(8,128)(2,1)S(1)} collective-permute-done((bf16[2,256,512]{2,1,0:T(8,128)(2,1)S(1)}, bf16[2,256,512]{2,1,0:T(8,128)(2,1)S(1)}, u32[]{:S(2)}, u32[]{:S(2)}) %collective-permute-start.17) | collective-permute-done | bytes 524320 | tf_op jit(solution)/shard_map/ppermute | solution.py:467
  143.4 2.3 %project.4 = (bf16[3,2,2,64,512]{4,3,2,1,0:T(8,128)(2,1)S(1)}, bf16[3,2,2,64,512]{4,3,2,1,0:T(8,128)(2,1)S(1)}) custom-call(s32[4]{0:T(128)S(1)} %pad_add_fusion.at, bf16[2,2,2,64,512]{4,3,2,1,0:T(8,128)(2,1)S(1)} %bitcast.28, bf16[2,2,2,64,512]{4,3,2,1,0:T(8,128)(2,1)S(1)} %bitcast.33, bf16[1024,512]{1,0:T(8,128)(2,1)S(1)} %copy-done, ...), custom_call_target="tpu_custom_call" | custom-call | flops 300000000 | bytes 1024 | tf_op jit(solution)/shard_map/project/pallas_call | solution.py:390
  146.4 5.3 %collective-permute-done.15.refs_1_ = bf16[2,64,512]{2,1,0:T(8,128)(2,1)S(1)} collective-permute-done((bf16[2,64,512]{2,1,0:T(8,128)(2,1)S(1)}, bf16[2,64,512]{2,1,0:T(8,128)(2,1)S(1)}, u32[]{:S(2)}, u32[]{:S(2)}) %collective-permute-start.15) | collective-permute-done | bytes 131104 | tf_op jit(solution)/shard_map/ppermute | solution.py:467
  151.8 2.3 %project.5 = (bf16[3,2,2,64,512]{4,3,2,1,0:T(8,128)(2,1)S(1)}, bf16[3,2,2,64,512]{4,3,2,1,0:T(8,128)(2,1)S(1)}) custom-call(s32[4]{0:T(128)S(1)} %pad_add_fusion.at, bf16[2,2,2,64,512]{4,3,2,1,0:T(8,128)(2,1)S(1)} %bitcast.29, bf16[2,2,2,64,512]{4,3,2,1,0:T(8,128)(2,1)S(1)} %bitcast.34, bf16[1024,512]{1,0:T(8,128)(2,1)S(1)} %bitcast_select_fusion.refs_6_.refs_2_, ...), custom_call_target="tpu_custom_call" | custom-call | flops 300000000 | bytes 1024 | tf_op jit(solution)/shard_map/project/pallas_call | solution.py:390
  164.3 4.2 %collective-permute-done.21.refs_5_ = bf16[3,64,512]{2,1,0:T(8,128)(2,1)S(1)} collective-permute-done((bf16[3,64,512]{2,1,0:T(8,128)(2,1)S(1)}, bf16[3,64,512]{2,1,0:T(8,128)(2,1)S(1)}, u32[]{:S(2)}, u32[]{:S(2)}) %collective-permute-start.21) | collective-permute-done | bytes 196640 | tf_op jit(solution)/shard_map/ppermute | solution.py:549
  168.5 2.3 %collective-permute-done.24.refs_7_ = bf16[3,64,512]{2,1,0:T(8,128)(2,1)S(1)} collective-permute-done((bf16[3,64,512]{2,1,0:T(8,128)(2,1)S(1)}, bf16[3,64,512]{2,1,0:T(8,128)(2,1)S(1)}, u32[]{:S(2)}, u32[]{:S(2)}) %collective-permute-start.24) | collective-permute-done | bytes 196640 | tf_op jit(solution)/shard_map/ppermute | solution.py:473
  170.7 2.0 %collective-permute-done.25.refs_8_ = bf16[3,64,512]{2,1,0:T(8,128)(2,1)S(1)} collective-permute-done((bf16[3,64,512]{2,1,0:T(8,128)(2,1)S(1)}, bf16[3,64,512]{2,1,0:T(8,128)(2,1)S(1)}, u32[]{:S(2)}, u32[]{:S(2)}) %collective-permute-start.25) | collective-permute-done | bytes 196640 | tf_op jit(solution)/shard_map/ppermute | solution.py:467
  172.7 3.4 %collective-permute-done.26.refs_9_ = bf16[3,64,512]{2,1,0:T(8,128)(2,1)S(1)} collective-permute-done((bf16[3,64,512]{2,1,0:T(8,128)(2,1)S(1)}, bf16[3,64,512]{2,1,0:T(8,128)(2,1)S(1)}, u32[]{:S(2)}, u32[]{:S(2)}) %collective-permute-start.26) | collective-permute-done | bytes 196640 | tf_op jit(solution)/shard_map/ppermute | solution.py:549
  176.2 1.7 place.1
  (71 shorter events, 34.7 us)
Async XLA Ops:
  2.2 13.9 %collective-permute-start.1 = (bf16[1,512,512]{2,1,0:T(8,128)(2,1)}, bf16[1,512,512]{2,1,0:T(8,128)(2,1)S(1)}, u32[]{:S(2)}, u32[]{:S(2)}) collective-permute-start(bf16[1,512,512]{2,1,0:T(8,128)(2,1)} %get-tuple-element.81), channel_id=1, source_target_pairs={{0,4},{4,0},{8,12},{12,8},{16,20},{20,16},{24,28},{28,24},{1,5},{5... | collective-permute-start | bytes 1572872 | tf_op jit(solution)/shard_map/ppermute | solution.py:467
  3.7 16.9 %collective-permute-start = (bf16[1,512,512]{2,1,0:T(8,128)(2,1)}, bf16[1,512,512]{2,1,0:T(8,128)(2,1)S(1)}, u32[]{:S(2)}, u32[]{:S(2)}) collective-permute-start(bf16[1,512,512]{2,1,0:T(8,128)(2,1)} %get-tuple-element.82.q_m), channel_id=1, source_target_pairs={{16,8},{20,12},{24,16},{28,20},{17,9},{21,13},{25,17},{29,21},{18,... | collective-permute-start | bytes 1572872 | tf_op jit(solution)/shard_map/ppermute | solution.py:467
  6.1 18.3 %collective-permute-start.3 = (bf16[1,512,512]{2,1,0:T(8,128)(2,1)}, bf16[1,512,512]{2,1,0:T(8,128)(2,1)}, u32[]{:S(2)}, u32[]{:S(2)}) collective-permute-start(bf16[1,512,512]{2,1,0:T(8,128)(2,1)} %get-tuple-element.82.q_m), channel_id=1, source_target_pairs={{24,8},{28,12},{25,9},{29,13},{26,10},{30,14},{27,11},{31,15}} | collective-permute-start | bytes 1572872 | tf_op jit(solution)/shard_map/ppermute | solution.py:467
  7.5 46.3 %copy-start = (bf16[1024,512]{1,0:T(8,128)(2,1)S(1)}, bf16[1024,512]{1,0:T(8,128)(2,1)}, u32[]{:S(2)}) copy-start(bf16[1024,512]{1,0:T(8,128)(2,1)} %refs_2_.7) | copy-start | bytes 3145732
  12.1 43.7 %collective-permute-start.6 = (bf16[2,512,512]{2,1,0:T(8,128)(2,1)}, bf16[2,512,512]{2,1,0:T(8,128)(2,1)S(1)}, u32[]{:S(2)}, u32[]{:S(2)}) collective-permute-start(bf16[2,512,512]{2,1,0:T(8,128)(2,1)} %get-tuple-element.79), channel_id=1, source_target_pairs={{0,8},{4,12},{8,24},{12,28},{1,9},{5,13},{9,25},{13,29},{2,10},{6,... | collective-permute-start | bytes 3145736 | tf_op jit(solution)/shard_map/ppermute | solution.py:467
  16.1 5.4 %copy-start.4 = (bf16[1,512,512]{2,1,0:T(8,128)(2,1)}, bf16[1,512,512]{2,1,0:T(8,128)(2,1)S(1)}, u32[]{:S(2)}) copy-start(bf16[1,512,512]{2,1,0:T(8,128)(2,1)S(1)} %collective-permute-done.1.q_o) | copy-start | bytes 1572868
  21.5 34.3 %collective-permute-start.5 = (bf16[2,512,512]{2,1,0:T(8,128)(2,1)}, bf16[2,512,512]{2,1,0:T(8,128)(2,1)}, u32[]{:S(2)}, u32[]{:S(2)}) collective-permute-start(bf16[2,512,512]{2,1,0:T(8,128)(2,1)} %get-tuple-element.40), channel_id=1, source_target_pairs={{0,4},{4,0},{8,12},{12,8},{16,20},{20,16},{24,28},{28,24},{1,5},{5... | collective-permute-start | bytes 3145736 | tf_op jit(solution)/shard_map/ppermute | solution.py:467
  22.0 39.7 %collective-permute-start.7 = (bf16[2,512,512]{2,1,0:T(8,128)(2,1)}, bf16[2,512,512]{2,1,0:T(8,128)(2,1)S(1)}, u32[]{:S(2)}, u32[]{:S(2)}) collective-permute-start(bf16[2,512,512]{2,1,0:T(8,128)(2,1)} %get-tuple-element.41), channel_id=1, source_target_pairs={{0,12},{4,8},{8,0},{12,4},{16,24},{20,28},{1,13},{5,9},{9,1},{13,5... | collective-permute-start | bytes 3145736 | tf_op jit(solution)/shard_map/ppermute | solution.py:486
  23.6 11.8 %collective-permute-start.4 = (bf16[1,512,512]{2,1,0:T(8,128)(2,1)}, bf16[1,512,512]{2,1,0:T(8,128)(2,1)S(1)}, u32[]{:S(2)}, u32[]{:S(2)}) collective-permute-start(bf16[1,512,512]{2,1,0:T(8,128)(2,1)} %copy-done.4), channel_id=1, source_target_pairs={{24,8},{28,12},{25,9},{29,13},{26,10},{30,14},{27,11},{31,15}} | collective-permute-start | bytes 1572872 | tf_op jit(solution)/shard_map/ppermute | solution.py:467
  24.3 28.6 %collective-permute-start.2 = (bf16[1,512,512]{2,1,0:T(8,128)(2,1)}, bf16[1,512,512]{2,1,0:T(8,128)(2,1)S(1)}, u32[]{:S(2)}, u32[]{:S(2)}) collective-permute-start(bf16[1,512,512]{2,1,0:T(8,128)(2,1)} %copy-done.4), channel_id=1, source_target_pairs={{16,8},{20,12},{24,16},{28,20},{17,9},{21,13},{25,17},{29,21},{18,... | collective-permute-start | bytes 1572872 | tf_op jit(solution)/shard_map/ppermute | solution.py:467
  53.8 55.6 %collective-permute-start.12 = (bf16[1024,512]{1,0:T(8,128)(2,1)S(1)}, bf16[1024,512]{1,0:T(8,128)(2,1)}, u32[]{:S(2)}, u32[]{:S(2)}) collective-permute-start(bf16[1024,512]{1,0:T(8,128)(2,1)S(1)} %copy-done), channel_id=1, source_target_pairs={{0,16},{4,20},{16,0},{20,4},{24,8},{28,12},{1,17},{5,21},{17,1},{2... | collective-permute-start | bytes 3145736 | tf_op jit(solution)/shard_map/ppermute | solution.py:467
  72.0 28.6 %collective-permute-start.9 = (bf16[528,512]{1,0:T(8,128)(2,1)}, bf16[528,512]{1,0:T(8,128)(2,1)}, u32[]{:S(2)}, u32[]{:S(2)}) collective-permute-start(bf16[528,512]{1,0:T(8,128)(2,1)} %get-tuple-element.47), channel_id=1, source_target_pairs={{8,24},{12,28},{0,8},{4,12},{24,16},{28,20},{9,25},{13,29},{1,9},{... | collective-permute-start | bytes 1622024 | tf_op jit(solution)/shard_map/ppermute | solution.py:467
  73.3 33.6 %collective-permute-start.8 = (bf16[528,512]{1,0:T(8,128)(2,1)}, bf16[528,512]{1,0:T(8,128)(2,1)}, u32[]{:S(2)}, u32[]{:S(2)}) collective-permute-start(bf16[528,512]{1,0:T(8,128)(2,1)} %get-tuple-element.42), channel_id=1, source_target_pairs={{8,16},{12,20},{16,24},{20,28},{9,17},{13,21},{17,25},{21,29},{10,... | collective-permute-start | bytes 1622024 | tf_op jit(solution)/shard_map/ppermute | solution.py:467
  84.7 33.7 %collective-permute-start.11 = (bf16[528,512]{1,0:T(8,128)(2,1)}, bf16[528,512]{1,0:T(8,128)(2,1)}, u32[]{:S(2)}, u32[]{:S(2)}) collective-permute-start(bf16[528,512]{1,0:T(8,128)(2,1)} %get-tuple-element.48), channel_id=1, source_target_pairs={{8,24},{12,28},{0,8},{4,12},{24,16},{28,20},{9,25},{13,29},{1,9},{... | collective-permute-start | bytes 1622024 | tf_op jit(solution)/shard_map/ppermute | solution.py:467
  86.0 42.9 %collective-permute-start.16 = (bf16[528,512]{1,0:T(8,128)(2,1)}, bf16[528,512]{1,0:T(8,128)(2,1)S(1)}, u32[]{:S(2)}, u32[]{:S(2)}) collective-permute-start(bf16[528,512]{1,0:T(8,128)(2,1)} %copy-done.13), channel_id=1, source_target_pairs={{8,16},{12,20},{16,24},{20,28},{9,17},{13,21},{17,25},{21,29},{10,... | collective-permute-start | bytes 1622024 | tf_op jit(solution)/shard_map/ppermute | solution.py:467
  90.7 1.2 copy-start.2
  100.6 10.2 %copy-start.3 = (bf16[2,512,512]{2,1,0:T(8,128)(2,1)S(1)}, bf16[2,512,512]{2,1,0:T(8,128)(2,1)}, u32[]{:S(2)}) copy-start(bf16[2,512,512]{2,1,0:T(8,128)(2,1)} %get-tuple-element.80.kv_m) | copy-start | bytes 3145732
  100.6 10.2 %copy-start.6 = (bf16[1,512,512]{2,1,0:T(8,128)(2,1)S(1)}, bf16[1,512,512]{2,1,0:T(8,128)(2,1)}, u32[]{:S(2)}) copy-start(bf16[1,512,512]{2,1,0:T(8,128)(2,1)} %copy-done.4) | copy-start | bytes 1572868
  108.8 12.2 %collective-permute-start.10 = (bf16[2,256,512]{2,1,0:T(8,128)(2,1)S(1)}, bf16[2,256,512]{2,1,0:T(8,128)(2,1)S(1)}, u32[]{:S(2)}, u32[]{:S(2)}) collective-permute-start(bf16[2,256,512]{2,1,0:T(8,128)(2,1)S(1)} %merge.2), channel_id=1, source_target_pairs={{0,4},{4,0},{8,12},{12,8},{16,20},{20,16},{24,28},{28,24},{1,5},{5... | collective-permute-start | bytes 1572872 | tf_op jit(solution)/shard_map/ppermute | solution.py:467
  110.7 41.0 %collective-permute-start.22 = (bf16[1024,512]{1,0:T(8,128)(2,1)S(1)}, bf16[1024,512]{1,0:T(8,128)(2,1)S(1)}, u32[]{:S(2)}, u32[]{:S(2)}) collective-permute-start(bf16[1024,512]{1,0:T(8,128)(2,1)S(1)} %bitcast_select_fusion.refs_6_.refs_2_), channel_id=1, source_target_pairs={{0,8},{4,12},{8,0},{12,4},{16,24},{20,28},{24,16},{28,20},{1,9},{5... | collective-permute-start | bytes 3145736 | tf_op jit(solution)/shard_map/ppermute | solution.py:467
  122.8 8.4 %collective-permute-start.13 = (bf16[2,2,2,64,512]{4,3,2,1,0:T(8,128)(2,1)S(1)}, bf16[2,2,2,64,512]{4,3,2,1,0:T(8,128)(2,1)S(1)}, u32[]{:S(2)}, u32[]{:S(2)}) collective-permute-start(bf16[2,2,2,64,512]{4,3,2,1,0:T(8,128)(2,1)S(1)} %get-tuple-element.55), channel_id=1, source_target_pairs={{0,1},{1,0},{2,3},{3,2},{4,5},{5,4},{6,7},{7,6},{8,9},{9,8},{10,11... | collective-permute-start | bytes 1572872 | tf_op jit(solution)/shard_map/ppermute | solution.py:473
  130.6 12.9 %collective-permute-start.17 = (bf16[2,256,512]{2,1,0:T(8,128)(2,1)S(1)}, bf16[2,256,512]{2,1,0:T(8,128)(2,1)S(1)}, u32[]{:S(2)}, u32[]{:S(2)}) collective-permute-start(bf16[2,256,512]{2,1,0:T(8,128)(2,1)S(1)} %merge.3), channel_id=1, source_target_pairs={{0,4},{4,0},{8,12},{12,8},{16,20},{20,16},{24,28},{28,24},{1,5},{5... | collective-permute-start | bytes 1572872 | tf_op jit(solution)/shard_map/ppermute | solution.py:467
  131.9 7.0 %collective-permute-start.14 = (bf16[2,2,64,512]{3,2,1,0:T(8,128)(2,1)S(1)}, bf16[2,2,64,512]{3,2,1,0:T(8,128)(2,1)S(1)}, u32[]{:S(2)}, u32[]{:S(2)}) collective-permute-start(bf16[2,2,64,512]{3,2,1,0:T(8,128)(2,1)S(1)} %get-tuple-element.57), channel_id=1, source_target_pairs={{0,2},{1,3},{2,0},{3,1},{4,6},{5,7},{6,4},{7,5},{8,10},{9,11},{10,... | collective-permute-start | bytes 786440 | tf_op jit(solution)/shard_map/ppermute | solution.py:473
  145.8 8.4 %collective-permute-start.18 = (bf16[3,2,2,64,512]{4,3,2,1,0:T(8,128)(2,1)S(1)}, bf16[3,2,2,64,512]{4,3,2,1,0:T(8,128)(2,1)S(1)}, u32[]{:S(2)}, u32[]{:S(2)}) collective-permute-start(bf16[3,2,2,64,512]{4,3,2,1,0:T(8,128)(2,1)S(1)} %get-tuple-element.63), channel_id=1, source_target_pairs={{0,1},{1,0},{2,3},{3,2},{4,5},{5,4},{6,7},{7,6},{8,9},{9,8},{10,11... | collective-permute-start | bytes 2359304 | tf_op jit(solution)/shard_map/ppermute | solution.py:473
  145.9 5.9 %collective-permute-start.15 = (bf16[2,64,512]{2,1,0:T(8,128)(2,1)S(1)}, bf16[2,64,512]{2,1,0:T(8,128)(2,1)S(1)}, u32[]{:S(2)}, u32[]{:S(2)}) collective-permute-start(bf16[2,64,512]{2,1,0:T(8,128)(2,1)S(1)} %get-tuple-element.59), channel_id=1, source_target_pairs={{0,4},{4,0},{8,12},{12,8},{16,20},{20,16},{24,28},{28,24},{1,5},{5... | collective-permute-start | bytes 393224 | tf_op jit(solution)/shard_map/ppermute | solution.py:467
  154.1 4.4 %collective-permute-start.23 = (bf16[3,2,2,64,512]{4,3,2,1,0:T(8,128)(2,1)S(1)}, bf16[3,2,2,64,512]{4,3,2,1,0:T(8,128)(2,1)S(1)}, u32[]{:S(2)}, u32[]{:S(2)}) collective-permute-start(bf16[3,2,2,64,512]{4,3,2,1,0:T(8,128)(2,1)S(1)} %get-tuple-element.70), channel_id=1, source_target_pairs={{0,1},{1,0},{2,3},{3,2},{4,5},{5,4},{6,7},{7,6},{8,9},{9,8},{10,11... | collective-permute-start | bytes 2359304 | tf_op jit(solution)/shard_map/ppermute | solution.py:473
  154.9 7.8 %collective-permute-start.19 = (bf16[3,64,512]{2,1,0:T(8,128)(2,1)S(1)}, bf16[3,64,512]{2,1,0:T(8,128)(2,1)S(1)}, u32[]{:S(2)}, u32[]{:S(2)}) collective-permute-start(bf16[3,64,512]{2,1,0:T(8,128)(2,1)S(1)} %get-tuple-element.65), channel_id=1, source_target_pairs={{0,2},{1,3},{2,0},{3,1},{4,6},{5,7},{6,4},{7,5},{8,10},{9,11},{10,... | collective-permute-start | bytes 589832 | tf_op jit(solution)/shard_map/ppermute | solution.py:473
  156.5 7.7 %collective-permute-start.20 = (bf16[3,64,512]{2,1,0:T(8,128)(2,1)S(1)}, bf16[3,64,512]{2,1,0:T(8,128)(2,1)S(1)}, u32[]{:S(2)}, u32[]{:S(2)}) collective-permute-start(bf16[3,64,512]{2,1,0:T(8,128)(2,1)S(1)} %get-tuple-element.66), channel_id=1, source_target_pairs={{0,4},{4,0},{8,12},{12,8},{16,20},{20,16},{24,28},{28,24},{1,5},{5... | collective-permute-start | bytes 589832 | tf_op jit(solution)/shard_map/ppermute | solution.py:467
  157.1 11.4 %collective-permute-start.21 = (bf16[3,64,512]{2,1,0:T(8,128)(2,1)S(1)}, bf16[3,64,512]{2,1,0:T(8,128)(2,1)S(1)}, u32[]{:S(2)}, u32[]{:S(2)}) collective-permute-start(bf16[3,64,512]{2,1,0:T(8,128)(2,1)S(1)} %get-tuple-element.67), channel_id=1, source_target_pairs={{0,6},{1,7},{2,4},{3,5},{4,2},{5,3},{6,0},{7,1},{8,14},{9,15},{10,... | collective-permute-start | bytes 589832 | tf_op jit(solution)/shard_map/ppermute | solution.py:549
  159.2 11.5 %collective-permute-start.24 = (bf16[3,64,512]{2,1,0:T(8,128)(2,1)S(1)}, bf16[3,64,512]{2,1,0:T(8,128)(2,1)S(1)}, u32[]{:S(2)}, u32[]{:S(2)}) collective-permute-start(bf16[3,64,512]{2,1,0:T(8,128)(2,1)S(1)} %get-tuple-element.72), channel_id=1, source_target_pairs={{0,2},{1,3},{2,0},{3,1},{4,6},{5,7},{6,4},{7,5},{8,10},{9,11},{10,... | collective-permute-start | bytes 589832 | tf_op jit(solution)/shard_map/ppermute | solution.py:473
  160.8 11.9 %collective-permute-start.25 = (bf16[3,64,512]{2,1,0:T(8,128)(2,1)S(1)}, bf16[3,64,512]{2,1,0:T(8,128)(2,1)S(1)}, u32[]{:S(2)}, u32[]{:S(2)}) collective-permute-start(bf16[3,64,512]{2,1,0:T(8,128)(2,1)S(1)} %get-tuple-element.73), channel_id=1, source_target_pairs={{0,4},{4,0},{8,12},{12,8},{16,20},{20,16},{24,28},{28,24},{1,5},{5... | collective-permute-start | bytes 589832 | tf_op jit(solution)/shard_map/ppermute | solution.py:467
  162.7 13.5 %collective-permute-start.26 = (bf16[3,64,512]{2,1,0:T(8,128)(2,1)S(1)}, bf16[3,64,512]{2,1,0:T(8,128)(2,1)S(1)}, u32[]{:S(2)}, u32[]{:S(2)}) collective-permute-start(bf16[3,64,512]{2,1,0:T(8,128)(2,1)S(1)} %get-tuple-element.74), channel_id=1, source_target_pairs={{0,6},{1,7},{2,4},{3,5},{4,2},{5,3},{6,0},{7,1},{8,14},{9,15},{10,... | collective-permute-start | bytes 589832 | tf_op jit(solution)/shard_map/ppermute | solution.py:549
  (9 other events, 8.7 us)

commit v26 on v23

--- a/solution.py
+++ b/solution.py
@@ -484,7 +484,7 @@
     low_m = seq_perm(jnp.where(z == 0, kv_m, block), (0, 1), (1, 3))
     pairs = [(i, 2 + 1 - i) for i in range(2)] + [(2 + i, i) for i in range(2)] + [(4 + i, 6 + i) for i in range(2)]
     low_o = lax.ppermute(after(jnp.where(z == 0, kv_give, block), q_o), "seq", pairs)
-    kv_o = swap(after(kv_give, q_o, qs[0]))
+    kv_o = swap(after(kv_give, q_o))
     qs[1], qs[3] = seq_perm(q_o, *down), seq_perm(q_o, *two_down)
 
     struct = jax.ShapeDtypeStruct

time: 178 us -> 177 us (level)
  waiting for transfers between devices: 68.8 us -> 74.5 us
  starting transfers between devices: 44.3 us -> 39.8 us
    ppermute x18, starting transfers between devices: 35.9 us -> 28.9 us  [seq_perm(): return lax.ppermute(array, 'seq', pairs)]
    ppermute x18, waiting for transfers between devices: 49.9 us -> 54.3 us  [seq_perm(): return lax.ppermute(array, 'seq', pairs)]
    ppermute x1, starting transfers between devices: 1.61 us -> 3.53 us  [body_eight(): lax.ppermute(after(jnp.where(z == 0, kv_give, block), q_o), 'seq', pairs)]
    unnamed x28 -> x24, local copies, waits for them, and re-layouts: 9.9 us -> 8.85 us
where the time goes in v26:
time: 177 us; the launch traced here: 176 us
  waiting for transfers between devices  74.5 us (42%)
  Pallas kernels  41.6 us (24%)
  starting transfers between devices  39.8 us (22%)
  local copies, waits for them, and re-layouts  13.1 us (7%)
  other arithmetic  6.32 us (4%)
    ppermute x18, waiting for transfers between devices, seq_perm(): return lax.ppermute(array, 'seq', pairs)  54.3 us
    ppermute x18, starting transfers between devices, seq_perm(): return lax.ppermute(array, 'seq', pairs)  28.9 us
    pallas_call x4, Pallas kernels, head_call(): pl.pallas_call(kernel, out_shape=outs, grid_spec=pltpu.PrefetchScalarGrid...  27.2 us
    pallas_call x10, Pallas kernels, whole_call(): pl.pallas_call(kernel, out_shape=outs, in_specs=[pl.BlockSpec(memory_spac...  14.4 us
    unnamed x24, local copies, waits for them, and re-layouts  8.85 us
    ppermute x2, waiting for transfers between devices, body_eight(): lax.ppermute(to_xy, ('seq', 'head'), diagonal)  7.1 us
    ppermute x1, waiting for transfers between devices, body_eight(): lax.ppermute(after(jnp.where(z == 0, kv_give, block), q_o), 'seq', pairs)  6.64 us
    ppermute x6, waiting for transfers between devices, head_perm(): return lax.ppermute(array, 'head', [(i, i ^ flip) for i in range(4)])  6.39 us
  transfers between devices with their start and end apart: 27, of which 14 were waited for; matrix products, arithmetic and copies ran while one was open for 5% of the time, Pallas kernels for 23%

profile of v26, /device:TPU:16, one launch (start us, length us, event | category | flops | bytes accessed | tf_op | source)
XLA Modules:
  0.0 175.6 jit_solution(13192133187627839826)
XLA Ops:
  0.0 2.1 %dynamic-slice_bitcast_fusion.2 = (bf16[1,512,512]{2,1,0:T(8,128)(2,1)S(1)}, bf16[1,512,512]{2,1,0:T(8,128)(2,1)}) fusion(bf16[3,1,512,1024]{3,2,1,0:T(8,128)(2,1)} %param.2, s32[]{:T(128)S(6)} %select_n.57, s32[]{:T(128)S(6)} %select_n.56), kind=kLoop, calls=%fused_computation.6 | loop fusion | bytes 2097160 | tf_op jit(solution)/shard_map/dynamic_slice | solution.py:476
  5.0 2.2 %collective-permute-start = (bf16[1,512,512]{2,1,0:T(8,128)(2,1)}, bf16[1,512,512]{2,1,0:T(8,128)(2,1)}, u32[]{:S(2)}, u32[]{:S(2)}) collective-permute-start(bf16[1,512,512]{2,1,0:T(8,128)(2,1)} %get-tuple-element.82.q_m), channel_id=1, source_target_pairs={{16,8},{20,12},{24,16},{28,20},{17,9},{21,13},{25,17},{29,21},{18,... | collective-permute-start | bytes 1572872 | tf_op jit(solution)/shard_map/ppermute | solution.py:467
  7.3 4.5 %broadcast_select_fusion = (bf16[2,512,512]{2,1,0:T(8,128)(2,1)}, bf16[2,512,512]{2,1,0:T(8,128)(2,1)}, bf16[2,512,512]{2,1,0:T(8,128)(2,1)}, bf16[2,512,512]{2,1,0:T(8,128)(2,1)}) fusion(bf16[2,512,512]{2,1,0:T(8,128)(2,1)} %bitcast.24, pred[]{:T(512)S(6)} %eq.12, bf16[3,1,512,1024]{3,2,1,0:T(8,128)(2,1)} %param.2, s32[]{:T(128)S(6)} %select_n.57, ...), kind=kLoop, calls=%fused_computation.4 | loop fusion | flops 1048576 | bytes 7340041 | tf_op jit(solution)/shard_map/jit(_where)/select_n | solution.py:486
  12.5 3.2 %collective-permute-done.1.q_o = bf16[1,512,512]{2,1,0:T(8,128)(2,1)S(1)} collective-permute-done((bf16[1,512,512]{2,1,0:T(8,128)(2,1)S(1)}, bf16[1,512,512]{2,1,0:T(8,128)(2,1)S(1)}, u32[]{:S(2)}, u32[]{:S(2)}) %collective-permute-start.1) | collective-permute-done | bytes 524320 | tf_op jit(solution)/shard_map/ppermute | solution.py:467
  18.0 3.5 %collective-permute-start.7 = (bf16[2,512,512]{2,1,0:T(8,128)(2,1)}, bf16[2,512,512]{2,1,0:T(8,128)(2,1)S(1)}, u32[]{:S(2)}, u32[]{:S(2)}) collective-permute-start(bf16[2,512,512]{2,1,0:T(8,128)(2,1)} %get-tuple-element.41), channel_id=1, source_target_pairs={{0,12},{4,8},{8,0},{12,4},{16,24},{20,28},{1,13},{5,9},{9,1},{13,5... | collective-permute-start | bytes 3145736 | tf_op jit(solution)/shard_map/ppermute | solution.py:486
  22.3 9.5 %collective-permute-done.qa_m = bf16[1,512,512]{2,1,0:T(8,128)(2,1)} collective-permute-done((bf16[1,512,512]{2,1,0:T(8,128)(2,1)}, bf16[1,512,512]{2,1,0:T(8,128)(2,1)}, u32[]{:S(2)}, u32[]{:S(2)}) %collective-permute-start) | collective-permute-done | bytes 524320 | tf_op jit(solution)/shard_map/ppermute | solution.py:467
  31.8 3.3 %collective-permute-start.2 = (bf16[1,512,512]{2,1,0:T(8,128)(2,1)}, bf16[1,512,512]{2,1,0:T(8,128)(2,1)S(1)}, u32[]{:S(2)}, u32[]{:S(2)}) collective-permute-start(bf16[1,512,512]{2,1,0:T(8,128)(2,1)} %copy-done.4), channel_id=1, source_target_pairs={{16,8},{20,12},{24,16},{28,20},{17,9},{21,13},{25,17},{29,21},{18,... | collective-permute-start | bytes 1572872 | tf_op jit(solution)/shard_map/ppermute | solution.py:467
  35.9 16.8 %collective-permute-done.2.qa_o = bf16[1,512,512]{2,1,0:T(8,128)(2,1)S(1)} collective-permute-done((bf16[1,512,512]{2,1,0:T(8,128)(2,1)}, bf16[1,512,512]{2,1,0:T(8,128)(2,1)S(1)}, u32[]{:S(2)}, u32[]{:S(2)}) %collective-permute-start.2) | collective-permute-done | bytes 524320 | tf_op jit(solution)/shard_map/ppermute | solution.py:467
  53.6 1.9 %collective-permute-start.12 = (bf16[1024,512]{1,0:T(8,128)(2,1)S(1)}, bf16[1024,512]{1,0:T(8,128)(2,1)}, u32[]{:S(2)}, u32[]{:S(2)}) collective-permute-start(bf16[1024,512]{1,0:T(8,128)(2,1)S(1)} %copy-done), channel_id=1, source_target_pairs={{0,16},{4,20},{16,0},{20,4},{24,8},{28,12},{1,17},{5,21},{17,1},{2... | collective-permute-start | bytes 3145736 | tf_op jit(solution)/shard_map/ppermute | solution.py:467
  55.6 6.6 %collective-permute-done.7.refs_1_ = bf16[2,512,512]{2,1,0:T(8,128)(2,1)S(1)} collective-permute-done((bf16[2,512,512]{2,1,0:T(8,128)(2,1)}, bf16[2,512,512]{2,1,0:T(8,128)(2,1)S(1)}, u32[]{:S(2)}, u32[]{:S(2)}) %collective-permute-start.7) | collective-permute-done | bytes 1048608 | tf_op jit(solution)/shard_map/ppermute | solution.py:486
  65.5 6.0 %upper_rows.2 = (bf16[528,512]{1,0:T(8,128)(2,1)}, bf16[528,512]{1,0:T(8,128)(2,1)}) custom-call(s32[4]{0:T(128)S(1)} %pad_add_fusion.at, bf16[1,512,512]{2,1,0:T(8,128)(2,1)} %collective-permute-done.qa_m, bf16[1,512,512]{2,1,0:T(8,128)(2,1)S(1)} %copy-done.10, bf16[1,512,512]{2,1,0:T(8,128)(2,1)} %collective-permute-done.3.qb_m, ...), custom_call_target="tpu_custom_call" | custom-call | flops 700000000 | bytes 1024 | tf_op jit(solution)/shard_map/upper_rows/pallas_call | solution.py:340
  72.8 4.6 %collective-permute-start.8 = (bf16[528,512]{1,0:T(8,128)(2,1)}, bf16[528,512]{1,0:T(8,128)(2,1)}, u32[]{:S(2)}, u32[]{:S(2)}) collective-permute-start(bf16[528,512]{1,0:T(8,128)(2,1)} %get-tuple-element.42), channel_id=1, source_target_pairs={{8,16},{12,20},{16,24},{20,28},{9,17},{13,21},{17,25},{21,29},{10,... | collective-permute-start | bytes 1622024 | tf_op jit(solution)/shard_map/ppermute | solution.py:467
  77.4 6.1 %upper_rows.3 = (bf16[528,512]{1,0:T(8,128)(2,1)S(1)}, bf16[528,512]{1,0:T(8,128)(2,1)}) custom-call(s32[4]{0:T(128)S(1)} %pad_add_fusion.at, bf16[1,512,512]{2,1,0:T(8,128)(2,1)} %collective-permute-done.qa_m, bf16[1,512,512]{2,1,0:T(8,128)(2,1)S(1)} %copy-done.10, bf16[1,512,512]{2,1,0:T(8,128)(2,1)} %collective-permute-done.3.qb_m, ...), custom_call_target="tpu_custom_call" | custom-call | flops 700000000 | bytes 1024 | tf_op jit(solution)/shard_map/upper_rows/pallas_call | solution.py:340
  85.5 4.7 %collective-permute-start.16 = (bf16[528,512]{1,0:T(8,128)(2,1)}, bf16[528,512]{1,0:T(8,128)(2,1)S(1)}, u32[]{:S(2)}, u32[]{:S(2)}) collective-permute-start(bf16[528,512]{1,0:T(8,128)(2,1)} %copy-done.11), channel_id=1, source_target_pairs={{8,16},{12,20},{16,24},{20,28},{9,17},{13,21},{17,25},{21,29},{10,... | collective-permute-start | bytes 1622024 | tf_op jit(solution)/shard_map/ppermute | solution.py:467
  92.5 7.6 %own_rows.2.own = bf16[528,512]{1,0:T(8,128)(2,1)S(1)} custom-call(s32[4]{0:T(128)S(1)} %pad_add_fusion.at, bf16[1,512,512]{2,1,0:T(8,128)(2,1)} %get-tuple-element.82.q_m, bf16[1,512,512]{2,1,0:T(8,128)(2,1)S(1)} %copy-done.5, bf16[2,512,512]{2,1,0:T(8,128)(2,1)S(1)} %copy-done.2, bf16[2,512,512]{2,1,0:T(8,128)(2,1)} %collective-permute-done.5.kv_o, ...), custom_call_target="tpu_custom_call" | custom-call | flops 600000000 | bytes 1024 | tf_op jit(solution)/shard_map/own_rows/pallas_call | solution.py:340
  100.1 5.6 %collective-permute-done.8.oa = bf16[528,512]{1,0:T(8,128)(2,1)} collective-permute-done((bf16[528,512]{1,0:T(8,128)(2,1)}, bf16[528,512]{1,0:T(8,128)(2,1)}, u32[]{:S(2)}, u32[]{:S(2)}) %collective-permute-start.8) | collective-permute-done | bytes 540704 | tf_op jit(solution)/shard_map/ppermute | solution.py:467
  105.8 1.8 %merge.2 = bf16[2,256,512]{2,1,0:T(8,128)(2,1)S(1)} custom-call(s32[4]{0:T(128)S(1)} %pad_add_fusion.at, bf16[528,512]{1,0:T(8,128)(2,1)S(1)} %own_rows.2.own, bf16[528,512]{1,0:T(8,128)(2,1)} %collective-permute-done.8.oa, bf16[528,512]{1,0:T(8,128)(2,1)} %collective-permute-done.9.ob), custom_call_target="tpu_custom_call" | custom-call | flops 200000000 | bytes 1024 | tf_op jit(solution)/shard_map/merge/pallas_call | solution.py:390
  109.7 7.6 %own_rows.3.own = bf16[528,512]{1,0:T(8,128)(2,1)S(1)} custom-call(s32[4]{0:T(128)S(1)} %pad_add_fusion.at, bf16[1,512,512]{2,1,0:T(8,128)(2,1)} %get-tuple-element.82.q_m, bf16[1,512,512]{2,1,0:T(8,128)(2,1)S(1)} %copy-done.6, bf16[2,512,512]{2,1,0:T(8,128)(2,1)S(1)} %copy-done.3, bf16[2,512,512]{2,1,0:T(8,128)(2,1)} %collective-permute-done.5.kv_o, ...), custom_call_target="tpu_custom_call" | custom-call | flops 600000000 | bytes 1024 | tf_op jit(solution)/shard_map/own_rows/pallas_call | solution.py:340
  121.3 1.8 %project.3 = (bf16[2,2,2,64,512]{4,3,2,1,0:T(8,128)(2,1)S(1)}, bf16[2,2,2,64,512]{4,3,2,1,0:T(8,128)(2,1)S(1)}) custom-call(s32[4]{0:T(128)S(1)} %pad_add_fusion.at, bf16[2,2,2,64,512]{4,3,2,1,0:T(8,128)(2,1)S(1)} %bitcast.25, bf16[2,2,2,64,512]{4,3,2,1,0:T(8,128)(2,1)S(1)} %bitcast.30, bf16[1024,512]{1,0:T(8,128)(2,1)S(1)} %copy-done, ...), custom_call_target="tpu_custom_call" | custom-call | flops 200000000 | bytes 1024 | tf_op jit(solution)/shard_map/project/pallas_call | solution.py:390
  123.2 5.5 %collective-permute-done.16.oa = bf16[528,512]{1,0:T(8,128)(2,1)S(1)} collective-permute-done((bf16[528,512]{1,0:T(8,128)(2,1)}, bf16[528,512]{1,0:T(8,128)(2,1)S(1)}, u32[]{:S(2)}, u32[]{:S(2)}) %collective-permute-start.16) | collective-permute-done | bytes 540704 | tf_op jit(solution)/shard_map/ppermute | solution.py:467
  128.7 1.7 merge.3
  133.3 6.4 %collective-permute-done.14.got = bf16[2,2,64,512]{3,2,1,0:T(8,128)(2,1)S(1)} collective-permute-done((bf16[2,2,64,512]{3,2,1,0:T(8,128)(2,1)S(1)}, bf16[2,2,64,512]{3,2,1,0:T(8,128)(2,1)S(1)}, u32[]{:S(2)}, u32[]{:S(2)}) %collective-permute-start.14) | collective-permute-done | bytes 262176 | tf_op jit(solution)/shard_map/ppermute | solution.py:473
  140.3 4.0 %collective-permute-done.17 = bf16[2,256,512]{2,1,0:T(8,128)(2,1)S(1)} collective-permute-done((bf16[2,256,512]{2,1,0:T(8,128)(2,1)S(1)}, bf16[2,256,512]{2,1,0:T(8,128)(2,1)S(1)}, u32[]{:S(2)}, u32[]{:S(2)}) %collective-permute-start.17) | collective-permute-done | bytes 524320 | tf_op jit(solution)/shard_map/ppermute | solution.py:467
  144.3 2.3 %project.4 = (bf16[3,2,2,64,512]{4,3,2,1,0:T(8,128)(2,1)S(1)}, bf16[3,2,2,64,512]{4,3,2,1,0:T(8,128)(2,1)S(1)}) custom-call(s32[4]{0:T(128)S(1)} %pad_add_fusion.at, bf16[2,2,2,64,512]{4,3,2,1,0:T(8,128)(2,1)S(1)} %bitcast.28, bf16[2,2,2,64,512]{4,3,2,1,0:T(8,128)(2,1)S(1)} %bitcast.33, bf16[1024,512]{1,0:T(8,128)(2,1)S(1)} %copy-done, ...), custom_call_target="tpu_custom_call" | custom-call | flops 300000000 | bytes 1024 | tf_op jit(solution)/shard_map/project/pallas_call | solution.py:390
  146.7 2.3 %project.5 = (bf16[3,2,2,64,512]{4,3,2,1,0:T(8,128)(2,1)S(1)}, bf16[3,2,2,64,512]{4,3,2,1,0:T(8,128)(2,1)S(1)}) custom-call(s32[4]{0:T(128)S(1)} %pad_add_fusion.at, bf16[2,2,2,64,512]{4,3,2,1,0:T(8,128)(2,1)S(1)} %bitcast.29, bf16[2,2,2,64,512]{4,3,2,1,0:T(8,128)(2,1)S(1)} %bitcast.34, bf16[1024,512]{1,0:T(8,128)(2,1)S(1)} %bitcast_select_fusion.refs_6_.refs_2_, ...), custom_call_target="tpu_custom_call" | custom-call | flops 300000000 | bytes 1024 | tf_op jit(solution)/shard_map/project/pallas_call | solution.py:390
  150.3 1.6 collective-permute-start.19
  155.2 1.6 collective-permute-start.24
  160.3 2.2 %collective-permute-done.20.refs_4_ = bf16[3,64,512]{2,1,0:T(8,128)(2,1)S(1)} collective-permute-done((bf16[3,64,512]{2,1,0:T(8,128)(2,1)S(1)}, bf16[3,64,512]{2,1,0:T(8,128)(2,1)S(1)}, u32[]{:S(2)}, u32[]{:S(2)}) %collective-permute-start.20) | collective-permute-done | bytes 196640 | tf_op jit(solution)/shard_map/ppermute | solution.py:467
  162.5 4.2 %collective-permute-done.21.refs_5_ = bf16[3,64,512]{2,1,0:T(8,128)(2,1)S(1)} collective-permute-done((bf16[3,64,512]{2,1,0:T(8,128)(2,1)S(1)}, bf16[3,64,512]{2,1,0:T(8,128)(2,1)S(1)}, u32[]{:S(2)}, u32[]{:S(2)}) %collective-permute-start.21) | collective-permute-done | bytes 196640 | tf_op jit(solution)/shard_map/ppermute | solution.py:549
  166.7 4.3 %collective-permute-done.25.refs_8_ = bf16[3,64,512]{2,1,0:T(8,128)(2,1)S(1)} collective-permute-done((bf16[3,64,512]{2,1,0:T(8,128)(2,1)S(1)}, bf16[3,64,512]{2,1,0:T(8,128)(2,1)S(1)}, u32[]{:S(2)}, u32[]{:S(2)}) %collective-permute-start.25) | collective-permute-done | bytes 196640 | tf_op jit(solution)/shard_map/ppermute | solution.py:467
  171.0 2.9 %collective-permute-done.26.refs_9_ = bf16[3,64,512]{2,1,0:T(8,128)(2,1)S(1)} collective-permute-done((bf16[3,64,512]{2,1,0:T(8,128)(2,1)S(1)}, bf16[3,64,512]{2,1,0:T(8,128)(2,1)S(1)}, u32[]{:S(2)}, u32[]{:S(2)}) %collective-permute-start.26) | collective-permute-done | bytes 196640 | tf_op jit(solution)/shard_map/ppermute | solution.py:549
  173.9 1.7 place.1
  (67 shorter events, 35.1 us)
Async XLA Ops:
  2.1 13.7 %collective-permute-start.1 = (bf16[1,512,512]{2,1,0:T(8,128)(2,1)S(1)}, bf16[1,512,512]{2,1,0:T(8,128)(2,1)S(1)}, u32[]{:S(2)}, u32[]{:S(2)}) collective-permute-start(bf16[1,512,512]{2,1,0:T(8,128)(2,1)S(1)} %get-tuple-element.81), channel_id=1, source_target_pairs={{0,4},{4,0},{8,12},{12,8},{16,20},{20,16},{24,28},{28,24},{1,5},{5... | collective-permute-start | bytes 1572872 | tf_op jit(solution)/shard_map/ppermute | solution.py:467
  3.6 18.0 %collective-permute-start.3 = (bf16[1,512,512]{2,1,0:T(8,128)(2,1)}, bf16[1,512,512]{2,1,0:T(8,128)(2,1)}, u32[]{:S(2)}, u32[]{:S(2)}) collective-permute-start(bf16[1,512,512]{2,1,0:T(8,128)(2,1)} %get-tuple-element.82.q_m), channel_id=1, source_target_pairs={{24,8},{28,12},{25,9},{29,13},{26,10},{30,14},{27,11},{31,15}} | collective-permute-start | bytes 1572872 | tf_op jit(solution)/shard_map/ppermute | solution.py:467
  5.0 26.8 %collective-permute-start = (bf16[1,512,512]{2,1,0:T(8,128)(2,1)}, bf16[1,512,512]{2,1,0:T(8,128)(2,1)}, u32[]{:S(2)}, u32[]{:S(2)}) collective-permute-start(bf16[1,512,512]{2,1,0:T(8,128)(2,1)} %get-tuple-element.82.q_m), channel_id=1, source_target_pairs={{16,8},{20,12},{24,16},{28,20},{17,9},{21,13},{25,17},{29,21},{18,... | collective-permute-start | bytes 1572872 | tf_op jit(solution)/shard_map/ppermute | solution.py:467
  7.2 46.3 %copy-start = (bf16[1024,512]{1,0:T(8,128)(2,1)S(1)}, bf16[1024,512]{1,0:T(8,128)(2,1)}, u32[]{:S(2)}) copy-start(bf16[1024,512]{1,0:T(8,128)(2,1)} %refs_2_.7) | copy-start | bytes 3145732
  11.8 43.8 %collective-permute-start.6 = (bf16[2,512,512]{2,1,0:T(8,128)(2,1)}, bf16[2,512,512]{2,1,0:T(8,128)(2,1)S(1)}, u32[]{:S(2)}, u32[]{:S(2)}) collective-permute-start(bf16[2,512,512]{2,1,0:T(8,128)(2,1)} %get-tuple-element.79), channel_id=1, source_target_pairs={{0,8},{4,12},{8,24},{12,28},{1,9},{5,13},{9,25},{13,29},{2,10},{6,... | collective-permute-start | bytes 3145736 | tf_op jit(solution)/shard_map/ppermute | solution.py:467
  16.5 39.1 %collective-permute-start.5 = (bf16[2,512,512]{2,1,0:T(8,128)(2,1)}, bf16[2,512,512]{2,1,0:T(8,128)(2,1)}, u32[]{:S(2)}, u32[]{:S(2)}) collective-permute-start(bf16[2,512,512]{2,1,0:T(8,128)(2,1)} %get-tuple-element.40), channel_id=1, source_target_pairs={{0,4},{4,0},{8,12},{12,8},{16,20},{20,16},{24,28},{28,24},{1,5},{5... | collective-permute-start | bytes 3145736 | tf_op jit(solution)/shard_map/ppermute | solution.py:467
  18.0 44.2 %collective-permute-start.7 = (bf16[2,512,512]{2,1,0:T(8,128)(2,1)}, bf16[2,512,512]{2,1,0:T(8,128)(2,1)S(1)}, u32[]{:S(2)}, u32[]{:S(2)}) collective-permute-start(bf16[2,512,512]{2,1,0:T(8,128)(2,1)} %get-tuple-element.41), channel_id=1, source_target_pairs={{0,12},{4,8},{8,0},{12,4},{16,24},{20,28},{1,13},{5,9},{9,1},{13,5... | collective-permute-start | bytes 3145736 | tf_op jit(solution)/shard_map/ppermute | solution.py:486
  21.6 13.5 %collective-permute-start.4 = (bf16[1,512,512]{2,1,0:T(8,128)(2,1)}, bf16[1,512,512]{2,1,0:T(8,128)(2,1)S(1)}, u32[]{:S(2)}, u32[]{:S(2)}) collective-permute-start(bf16[1,512,512]{2,1,0:T(8,128)(2,1)} %copy-done.4), channel_id=1, source_target_pairs={{24,8},{28,12},{25,9},{29,13},{26,10},{30,14},{27,11},{31,15}} | collective-permute-start | bytes 1572872 | tf_op jit(solution)/shard_map/ppermute | solution.py:467
  31.8 20.9 %collective-permute-start.2 = (bf16[1,512,512]{2,1,0:T(8,128)(2,1)}, bf16[1,512,512]{2,1,0:T(8,128)(2,1)S(1)}, u32[]{:S(2)}, u32[]{:S(2)}) collective-permute-start(bf16[1,512,512]{2,1,0:T(8,128)(2,1)} %copy-done.4), channel_id=1, source_target_pairs={{16,8},{20,12},{24,16},{28,20},{17,9},{21,13},{25,17},{29,21},{18,... | collective-permute-start | bytes 1572872 | tf_op jit(solution)/shard_map/ppermute | solution.py:467
  53.6 54.7 %collective-permute-start.12 = (bf16[1024,512]{1,0:T(8,128)(2,1)S(1)}, bf16[1024,512]{1,0:T(8,128)(2,1)}, u32[]{:S(2)}, u32[]{:S(2)}) collective-permute-start(bf16[1024,512]{1,0:T(8,128)(2,1)S(1)} %copy-done), channel_id=1, source_target_pairs={{0,16},{4,20},{16,0},{20,4},{24,8},{28,12},{1,17},{5,21},{17,1},{2... | collective-permute-start | bytes 3145736 | tf_op jit(solution)/shard_map/ppermute | solution.py:467
  62.2 1.2 copy-start.1
  71.5 28.6 %collective-permute-start.9 = (bf16[528,512]{1,0:T(8,128)(2,1)}, bf16[528,512]{1,0:T(8,128)(2,1)}, u32[]{:S(2)}, u32[]{:S(2)}) collective-permute-start(bf16[528,512]{1,0:T(8,128)(2,1)} %get-tuple-element.47), channel_id=1, source_target_pairs={{8,24},{12,28},{0,8},{4,12},{24,16},{28,20},{9,25},{13,29},{1,9},{... | collective-permute-start | bytes 1622024 | tf_op jit(solution)/shard_map/ppermute | solution.py:467
  72.8 33.0 %collective-permute-start.8 = (bf16[528,512]{1,0:T(8,128)(2,1)}, bf16[528,512]{1,0:T(8,128)(2,1)}, u32[]{:S(2)}, u32[]{:S(2)}) collective-permute-start(bf16[528,512]{1,0:T(8,128)(2,1)} %get-tuple-element.42), channel_id=1, source_target_pairs={{8,16},{12,20},{16,24},{20,28},{9,17},{13,21},{17,25},{21,29},{10,... | collective-permute-start | bytes 1622024 | tf_op jit(solution)/shard_map/ppermute | solution.py:467
  84.2 33.0 %collective-permute-start.11 = (bf16[528,512]{1,0:T(8,128)(2,1)}, bf16[528,512]{1,0:T(8,128)(2,1)}, u32[]{:S(2)}, u32[]{:S(2)}) collective-permute-start(bf16[528,512]{1,0:T(8,128)(2,1)} %get-tuple-element.48), channel_id=1, source_target_pairs={{8,24},{12,28},{0,8},{4,12},{24,16},{28,20},{9,25},{13,29},{1,9},{... | collective-permute-start | bytes 1622024 | tf_op jit(solution)/shard_map/ppermute | solution.py:467
  85.5 43.2 %collective-permute-start.16 = (bf16[528,512]{1,0:T(8,128)(2,1)}, bf16[528,512]{1,0:T(8,128)(2,1)S(1)}, u32[]{:S(2)}, u32[]{:S(2)}) collective-permute-start(bf16[528,512]{1,0:T(8,128)(2,1)} %copy-done.11), channel_id=1, source_target_pairs={{8,16},{12,20},{16,24},{20,28},{9,17},{13,21},{17,25},{21,29},{10,... | collective-permute-start | bytes 1622024 | tf_op jit(solution)/shard_map/ppermute | solution.py:467
  90.3 1.2 copy-start.2
  100.1 9.5 %copy-start.3 = (bf16[2,512,512]{2,1,0:T(8,128)(2,1)S(1)}, bf16[2,512,512]{2,1,0:T(8,128)(2,1)}, u32[]{:S(2)}) copy-start(bf16[2,512,512]{2,1,0:T(8,128)(2,1)} %get-tuple-element.80.kv_m) | copy-start | bytes 3145732
  100.1 9.5 %copy-start.6 = (bf16[1,512,512]{2,1,0:T(8,128)(2,1)S(1)}, bf16[1,512,512]{2,1,0:T(8,128)(2,1)}, u32[]{:S(2)}) copy-start(bf16[1,512,512]{2,1,0:T(8,128)(2,1)} %copy-done.4) | copy-start | bytes 1572868
  107.6 13.7 %collective-permute-start.10 = (bf16[2,256,512]{2,1,0:T(8,128)(2,1)S(1)}, bf16[2,256,512]{2,1,0:T(8,128)(2,1)S(1)}, u32[]{:S(2)}, u32[]{:S(2)}) collective-permute-start(bf16[2,256,512]{2,1,0:T(8,128)(2,1)S(1)} %merge.2), channel_id=1, source_target_pairs={{0,4},{4,0},{8,12},{12,8},{16,20},{20,16},{24,28},{28,24},{1,5},{5... | collective-permute-start | bytes 1572872 | tf_op jit(solution)/shard_map/ppermute | solution.py:467
  109.6 37.1 %collective-permute-start.22 = (bf16[1024,512]{1,0:T(8,128)(2,1)S(1)}, bf16[1024,512]{1,0:T(8,128)(2,1)S(1)}, u32[]{:S(2)}, u32[]{:S(2)}) collective-permute-start(bf16[1024,512]{1,0:T(8,128)(2,1)S(1)} %bitcast_select_fusion.refs_6_.refs_2_), channel_id=1, source_target_pairs={{0,8},{4,12},{8,0},{12,4},{16,24},{20,28},{24,16},{28,20},{1,9},{5... | collective-permute-start | bytes 3145736 | tf_op jit(solution)/shard_map/ppermute | solution.py:467
  123.1 7.9 %collective-permute-start.13 = (bf16[2,2,2,64,512]{4,3,2,1,0:T(8,128)(2,1)S(1)}, bf16[2,2,2,64,512]{4,3,2,1,0:T(8,128)(2,1)S(1)}, u32[]{:S(2)}, u32[]{:S(2)}) collective-permute-start(bf16[2,2,2,64,512]{4,3,2,1,0:T(8,128)(2,1)S(1)} %get-tuple-element.55), channel_id=1, source_target_pairs={{0,1},{1,0},{2,3},{3,2},{4,5},{5,4},{6,7},{7,6},{8,9},{9,8},{10,11... | collective-permute-start | bytes 1572872 | tf_op jit(solution)/shard_map/ppermute | solution.py:473
  130.4 13.9 %collective-permute-start.17 = (bf16[2,256,512]{2,1,0:T(8,128)(2,1)S(1)}, bf16[2,256,512]{2,1,0:T(8,128)(2,1)S(1)}, u32[]{:S(2)}, u32[]{:S(2)}) collective-permute-start(bf16[2,256,512]{2,1,0:T(8,128)(2,1)S(1)} %merge.3), channel_id=1, source_target_pairs={{0,4},{4,0},{8,12},{12,8},{16,20},{20,16},{24,28},{28,24},{1,5},{5... | collective-permute-start | bytes 1572872 | tf_op jit(solution)/shard_map/ppermute | solution.py:467
  131.7 8.0 %collective-permute-start.14 = (bf16[2,2,64,512]{3,2,1,0:T(8,128)(2,1)S(1)}, bf16[2,2,64,512]{3,2,1,0:T(8,128)(2,1)S(1)}, u32[]{:S(2)}, u32[]{:S(2)}) collective-permute-start(bf16[2,2,64,512]{3,2,1,0:T(8,128)(2,1)S(1)} %get-tuple-element.57), channel_id=1, source_target_pairs={{0,2},{1,3},{2,0},{3,1},{4,6},{5,7},{6,4},{7,5},{8,10},{9,11},{10,... | collective-permute-start | bytes 786440 | tf_op jit(solution)/shard_map/ppermute | solution.py:473
  146.6 3.0 %collective-permute-start.18 = (bf16[3,2,2,64,512]{4,3,2,1,0:T(8,128)(2,1)S(1)}, bf16[3,2,2,64,512]{4,3,2,1,0:T(8,128)(2,1)S(1)}, u32[]{:S(2)}, u32[]{:S(2)}) collective-permute-start(bf16[3,2,2,64,512]{4,3,2,1,0:T(8,128)(2,1)S(1)} %get-tuple-element.63), channel_id=1, source_target_pairs={{0,1},{1,0},{2,3},{3,2},{4,5},{5,4},{6,7},{7,6},{8,9},{9,8},{10,11... | collective-permute-start | bytes 2359304 | tf_op jit(solution)/shard_map/ppermute | solution.py:473
  149.1 5.4 %collective-permute-start.23 = (bf16[3,2,2,64,512]{4,3,2,1,0:T(8,128)(2,1)S(1)}, bf16[3,2,2,64,512]{4,3,2,1,0:T(8,128)(2,1)S(1)}, u32[]{:S(2)}, u32[]{:S(2)}) collective-permute-start(bf16[3,2,2,64,512]{4,3,2,1,0:T(8,128)(2,1)S(1)} %get-tuple-element.70), channel_id=1, source_target_pairs={{0,1},{1,0},{2,3},{3,2},{4,5},{5,4},{6,7},{7,6},{8,9},{9,8},{10,11... | collective-permute-start | bytes 2359304 | tf_op jit(solution)/shard_map/ppermute | solution.py:473
  150.3 8.5 %collective-permute-start.19 = (bf16[3,64,512]{2,1,0:T(8,128)(2,1)S(1)}, bf16[3,64,512]{2,1,0:T(8,128)(2,1)S(1)}, u32[]{:S(2)}, u32[]{:S(2)}) collective-permute-start(bf16[3,64,512]{2,1,0:T(8,128)(2,1)S(1)} %get-tuple-element.65), channel_id=1, source_target_pairs={{0,2},{1,3},{2,0},{3,1},{4,6},{5,7},{6,4},{7,5},{8,10},{9,11},{10,... | collective-permute-start | bytes 589832 | tf_op jit(solution)/shard_map/ppermute | solution.py:473
  151.9 6.4 %collective-permute-start.15 = (bf16[2,64,512]{2,1,0:T(8,128)(2,1)S(1)}, bf16[2,64,512]{2,1,0:T(8,128)(2,1)S(1)}, u32[]{:S(2)}, u32[]{:S(2)}) collective-permute-start(bf16[2,64,512]{2,1,0:T(8,128)(2,1)S(1)} %get-tuple-element.59), channel_id=1, source_target_pairs={{0,4},{4,0},{8,12},{12,8},{16,20},{20,16},{24,28},{28,24},{1,5},{5... | collective-permute-start | bytes 393224 | tf_op jit(solution)/shard_map/ppermute | solution.py:467
  152.5 10.1 %collective-permute-start.20 = (bf16[3,64,512]{2,1,0:T(8,128)(2,1)S(1)}, bf16[3,64,512]{2,1,0:T(8,128)(2,1)S(1)}, u32[]{:S(2)}, u32[]{:S(2)}) collective-permute-start(bf16[3,64,512]{2,1,0:T(8,128)(2,1)S(1)} %get-tuple-element.66), channel_id=1, source_target_pairs={{0,4},{4,0},{8,12},{12,8},{16,20},{20,16},{24,28},{28,24},{1,5},{5... | collective-permute-start | bytes 589832 | tf_op jit(solution)/shard_map/ppermute | solution.py:467
  154.0 12.8 %collective-permute-start.21 = (bf16[3,64,512]{2,1,0:T(8,128)(2,1)S(1)}, bf16[3,64,512]{2,1,0:T(8,128)(2,1)S(1)}, u32[]{:S(2)}, u32[]{:S(2)}) collective-permute-start(bf16[3,64,512]{2,1,0:T(8,128)(2,1)S(1)} %get-tuple-element.67), channel_id=1, source_target_pairs={{0,6},{1,7},{2,4},{3,5},{4,2},{5,3},{6,0},{7,1},{8,14},{9,15},{10,... | collective-permute-start | bytes 589832 | tf_op jit(solution)/shard_map/ppermute | solution.py:549
  155.2 11.6 %collective-permute-start.24 = (bf16[3,64,512]{2,1,0:T(8,128)(2,1)S(1)}, bf16[3,64,512]{2,1,0:T(8,128)(2,1)S(1)}, u32[]{:S(2)}, u32[]{:S(2)}) collective-permute-start(bf16[3,64,512]{2,1,0:T(8,128)(2,1)S(1)} %get-tuple-element.72), channel_id=1, source_target_pairs={{0,2},{1,3},{2,0},{3,1},{4,6},{5,7},{6,4},{7,5},{8,10},{9,11},{10,... | collective-permute-start | bytes 589832 | tf_op jit(solution)/shard_map/ppermute | solution.py:473
  158.3 12.7 %collective-permute-start.25 = (bf16[3,64,512]{2,1,0:T(8,128)(2,1)S(1)}, bf16[3,64,512]{2,1,0:T(8,128)(2,1)S(1)}, u32[]{:S(2)}, u32[]{:S(2)}) collective-permute-start(bf16[3,64,512]{2,1,0:T(8,128)(2,1)S(1)} %get-tuple-element.73), channel_id=1, source_target_pairs={{0,4},{4,0},{8,12},{12,8},{16,20},{20,16},{24,28},{28,24},{1,5},{5... | collective-permute-start | bytes 589832 | tf_op jit(solution)/shard_map/ppermute | solution.py:467
  158.9 15.1 %collective-permute-start.26 = (bf16[3,64,512]{2,1,0:T(8,128)(2,1)S(1)}, bf16[3,64,512]{2,1,0:T(8,128)(2,1)S(1)}, u32[]{:S(2)}, u32[]{:S(2)}) collective-permute-start(bf16[3,64,512]{2,1,0:T(8,128)(2,1)S(1)} %get-tuple-element.74), channel_id=1, source_target_pairs={{0,6},{1,7},{2,4},{3,5},{4,2},{5,3},{6,0},{7,1},{8,14},{9,15},{10,... | collective-permute-start | bytes 589832 | tf_op jit(solution)/shard_map/ppermute | solution.py:549
  (7 other events, 6.4 us)

commit v27 on v26

--- a/solution.py
+++ b/solution.py
@@ -131,7 +131,7 @@
         scores.append(s if allowed is None else jnp.where(allowed, s, NEG))
     singles = []
     if cols:
-        wide = q.astype(F32)
+        wide = q.astype(F32) * coef
     for k, _, allowed in cols:
         c = col_scores(wide, k)
         singles.append(c if allowed is None else jnp.where(allowed, c, NEG))
@@ -142,9 +142,9 @@
             peak = part if peak is None else jnp.maximum(peak, part)
     if peak is not None:
         peak = jnp.broadcast_to(jnp.max(peak, axis=1, keepdims=True), (rows, HEAD))
+        peak = peak * coef
     for c in singles:
         peak = c if peak is None else jnp.maximum(peak, c)
-    peak = peak * coef
     both = None
     for s, (_, v, _) in zip(scores, dense):
         tiled = jnp.concatenate([peak] * (s.shape[1] // HEAD), axis=1)
@@ -154,7 +154,7 @@
     out = None if both is None else both[:, :HEAD]
     total = None if both is None else both[:, HEAD:]
     for c, (_, v, _) in zip(singles, cols):
-        w = jnp.exp2(c * coef - peak)
+        w = jnp.exp2(c - peak)
         total = w if total is None else total + w
         out = w * v if out is None else out + w * v
     return out / total, peak + jnp.log2(total)

time: 177 us -> 177 us (level)
  no operation moved by 1% of the time
where the time goes in v27:
time: 177 us; the launch traced here: 176 us
  waiting for transfers between devices  74.6 us (42%)
  Pallas kernels  41.6 us (24%)
  starting transfers between devices  39.8 us (22%)
  local copies, waits for them, and re-layouts  13.1 us (7%)
  other arithmetic  6.32 us (4%)
    ppermute x18, waiting for transfers between devices, seq_perm(): return lax.ppermute(array, 'seq', pairs)  54.4 us
    ppermute x18, starting transfers between devices, seq_perm(): return lax.ppermute(array, 'seq', pairs)  28.9 us
    pallas_call x4, Pallas kernels, head_call(): pl.pallas_call(kernel, out_shape=outs, grid_spec=pltpu.PrefetchScalarGrid...  27.1 us
    pallas_call x10, Pallas kernels, whole_call(): pl.pallas_call(kernel, out_shape=outs, in_specs=[pl.BlockSpec(memory_spac...  14.4 us
    unnamed x24, local copies, waits for them, and re-layouts  8.85 us
    ppermute x2, waiting for transfers between devices, body_eight(): lax.ppermute(to_xy, ('seq', 'head'), diagonal)  7.09 us
    ppermute x1, waiting for transfers between devices, body_eight(): lax.ppermute(after(jnp.where(z == 0, kv_give, block), q_o), 'seq', pairs)  6.64 us
    ppermute x6, waiting for transfers between devices, head_perm(): return lax.ppermute(array, 'head', [(i, i ^ flip) for i in range(4)])  6.45 us
  transfers between devices with their start and end apart: 27, of which 14 were waited for; matrix products, arithmetic and copies ran while one was open for 5% of the time, Pallas kernels for 23%

profile of v27, /device:TPU:16, one launch (start us, length us, event | category | flops | bytes accessed | tf_op | source)
XLA Modules:
  0.0 175.7 jit_solution(13334570528565829894)
XLA Ops:
  0.0 2.1 %dynamic-slice_bitcast_fusion.2 = (bf16[1,512,512]{2,1,0:T(8,128)(2,1)S(1)}, bf16[1,512,512]{2,1,0:T(8,128)(2,1)}) fusion(bf16[3,1,512,1024]{3,2,1,0:T(8,128)(2,1)} %param.2, s32[]{:T(128)S(6)} %select_n.57, s32[]{:T(128)S(6)} %select_n.56), kind=kLoop, calls=%fused_computation.6 | loop fusion | bytes 2097160 | tf_op jit(solution)/shard_map/dynamic_slice | solution.py:476
  5.0 2.2 %collective-permute-start = (bf16[1,512,512]{2,1,0:T(8,128)(2,1)}, bf16[1,512,512]{2,1,0:T(8,128)(2,1)}, u32[]{:S(2)}, u32[]{:S(2)}) collective-permute-start(bf16[1,512,512]{2,1,0:T(8,128)(2,1)} %get-tuple-element.82.q_m), channel_id=1, source_target_pairs={{16,8},{20,12},{24,16},{28,20},{17,9},{21,13},{25,17},{29,21},{18,... | collective-permute-start | bytes 1572872 | tf_op jit(solution)/shard_map/ppermute | solution.py:467
  7.3 4.5 %broadcast_select_fusion = (bf16[2,512,512]{2,1,0:T(8,128)(2,1)}, bf16[2,512,512]{2,1,0:T(8,128)(2,1)}, bf16[2,512,512]{2,1,0:T(8,128)(2,1)}, bf16[2,512,512]{2,1,0:T(8,128)(2,1)}) fusion(bf16[2,512,512]{2,1,0:T(8,128)(2,1)} %bitcast.24, pred[]{:T(512)S(6)} %eq.12, bf16[3,1,512,1024]{3,2,1,0:T(8,128)(2,1)} %param.2, s32[]{:T(128)S(6)} %select_n.57, ...), kind=kLoop, calls=%fused_computation.4 | loop fusion | flops 1048576 | bytes 7340041 | tf_op jit(solution)/shard_map/jit(_where)/select_n | solution.py:486
  12.5 3.2 %collective-permute-done.1.q_o = bf16[1,512,512]{2,1,0:T(8,128)(2,1)S(1)} collective-permute-done((bf16[1,512,512]{2,1,0:T(8,128)(2,1)S(1)}, bf16[1,512,512]{2,1,0:T(8,128)(2,1)S(1)}, u32[]{:S(2)}, u32[]{:S(2)}) %collective-permute-start.1) | collective-permute-done | bytes 524320 | tf_op jit(solution)/shard_map/ppermute | solution.py:467
  18.0 3.5 %collective-permute-start.7 = (bf16[2,512,512]{2,1,0:T(8,128)(2,1)}, bf16[2,512,512]{2,1,0:T(8,128)(2,1)S(1)}, u32[]{:S(2)}, u32[]{:S(2)}) collective-permute-start(bf16[2,512,512]{2,1,0:T(8,128)(2,1)} %get-tuple-element.41), channel_id=1, source_target_pairs={{0,12},{4,8},{8,0},{12,4},{16,24},{20,28},{1,13},{5,9},{9,1},{13,5... | collective-permute-start | bytes 3145736 | tf_op jit(solution)/shard_map/ppermute | solution.py:486
  22.3 9.5 %collective-permute-done.qa_m = bf16[1,512,512]{2,1,0:T(8,128)(2,1)} collective-permute-done((bf16[1,512,512]{2,1,0:T(8,128)(2,1)}, bf16[1,512,512]{2,1,0:T(8,128)(2,1)}, u32[]{:S(2)}, u32[]{:S(2)}) %collective-permute-start) | collective-permute-done | bytes 524320 | tf_op jit(solution)/shard_map/ppermute | solution.py:467
  31.8 3.3 %collective-permute-start.2 = (bf16[1,512,512]{2,1,0:T(8,128)(2,1)}, bf16[1,512,512]{2,1,0:T(8,128)(2,1)S(1)}, u32[]{:S(2)}, u32[]{:S(2)}) collective-permute-start(bf16[1,512,512]{2,1,0:T(8,128)(2,1)} %copy-done.4), channel_id=1, source_target_pairs={{16,8},{20,12},{24,16},{28,20},{17,9},{21,13},{25,17},{29,21},{18,... | collective-permute-start | bytes 1572872 | tf_op jit(solution)/shard_map/ppermute | solution.py:467
  35.9 16.8 %collective-permute-done.2.qa_o = bf16[1,512,512]{2,1,0:T(8,128)(2,1)S(1)} collective-permute-done((bf16[1,512,512]{2,1,0:T(8,128)(2,1)}, bf16[1,512,512]{2,1,0:T(8,128)(2,1)S(1)}, u32[]{:S(2)}, u32[]{:S(2)}) %collective-permute-start.2) | collective-permute-done | bytes 524320 | tf_op jit(solution)/shard_map/ppermute | solution.py:467
  53.6 1.9 %collective-permute-start.12 = (bf16[1024,512]{1,0:T(8,128)(2,1)S(1)}, bf16[1024,512]{1,0:T(8,128)(2,1)}, u32[]{:S(2)}, u32[]{:S(2)}) collective-permute-start(bf16[1024,512]{1,0:T(8,128)(2,1)S(1)} %copy-done), channel_id=1, source_target_pairs={{0,16},{4,20},{16,0},{20,4},{24,8},{28,12},{1,17},{5,21},{17,1},{2... | collective-permute-start | bytes 3145736 | tf_op jit(solution)/shard_map/ppermute | solution.py:467
  55.6 6.6 %collective-permute-done.7.refs_1_ = bf16[2,512,512]{2,1,0:T(8,128)(2,1)S(1)} collective-permute-done((bf16[2,512,512]{2,1,0:T(8,128)(2,1)}, bf16[2,512,512]{2,1,0:T(8,128)(2,1)S(1)}, u32[]{:S(2)}, u32[]{:S(2)}) %collective-permute-start.7) | collective-permute-done | bytes 1048608 | tf_op jit(solution)/shard_map/ppermute | solution.py:486
  65.5 5.9 %upper_rows.2 = (bf16[528,512]{1,0:T(8,128)(2,1)}, bf16[528,512]{1,0:T(8,128)(2,1)}) custom-call(s32[4]{0:T(128)S(1)} %pad_add_fusion.at, bf16[1,512,512]{2,1,0:T(8,128)(2,1)} %collective-permute-done.qa_m, bf16[1,512,512]{2,1,0:T(8,128)(2,1)S(1)} %copy-done.10, bf16[1,512,512]{2,1,0:T(8,128)(2,1)} %collective-permute-done.3.qb_m, ...), custom_call_target="tpu_custom_call" | custom-call | flops 700000000 | bytes 1024 | tf_op jit(solution)/shard_map/upper_rows/pallas_call | solution.py:340
  72.8 4.6 %collective-permute-start.8 = (bf16[528,512]{1,0:T(8,128)(2,1)}, bf16[528,512]{1,0:T(8,128)(2,1)}, u32[]{:S(2)}, u32[]{:S(2)}) collective-permute-start(bf16[528,512]{1,0:T(8,128)(2,1)} %get-tuple-element.42), channel_id=1, source_target_pairs={{8,16},{12,20},{16,24},{20,28},{9,17},{13,21},{17,25},{21,29},{10,... | collective-permute-start | bytes 1622024 | tf_op jit(solution)/shard_map/ppermute | solution.py:467
  77.3 6.1 %upper_rows.3 = (bf16[528,512]{1,0:T(8,128)(2,1)S(1)}, bf16[528,512]{1,0:T(8,128)(2,1)}) custom-call(s32[4]{0:T(128)S(1)} %pad_add_fusion.at, bf16[1,512,512]{2,1,0:T(8,128)(2,1)} %collective-permute-done.qa_m, bf16[1,512,512]{2,1,0:T(8,128)(2,1)S(1)} %copy-done.10, bf16[1,512,512]{2,1,0:T(8,128)(2,1)} %collective-permute-done.3.qb_m, ...), custom_call_target="tpu_custom_call" | custom-call | flops 700000000 | bytes 1024 | tf_op jit(solution)/shard_map/upper_rows/pallas_call | solution.py:340
  85.5 4.7 %collective-permute-start.16 = (bf16[528,512]{1,0:T(8,128)(2,1)}, bf16[528,512]{1,0:T(8,128)(2,1)S(1)}, u32[]{:S(2)}, u32[]{:S(2)}) collective-permute-start(bf16[528,512]{1,0:T(8,128)(2,1)} %copy-done.11), channel_id=1, source_target_pairs={{8,16},{12,20},{16,24},{20,28},{9,17},{13,21},{17,25},{21,29},{10,... | collective-permute-start | bytes 1622024 | tf_op jit(solution)/shard_map/ppermute | solution.py:467
  92.5 7.6 %own_rows.2.own = bf16[528,512]{1,0:T(8,128)(2,1)S(1)} custom-call(s32[4]{0:T(128)S(1)} %pad_add_fusion.at, bf16[1,512,512]{2,1,0:T(8,128)(2,1)} %get-tuple-element.82.q_m, bf16[1,512,512]{2,1,0:T(8,128)(2,1)S(1)} %copy-done.5, bf16[2,512,512]{2,1,0:T(8,128)(2,1)S(1)} %copy-done.2, bf16[2,512,512]{2,1,0:T(8,128)(2,1)} %collective-permute-done.5.kv_o, ...), custom_call_target="tpu_custom_call" | custom-call | flops 600000000 | bytes 1024 | tf_op jit(solution)/shard_map/own_rows/pallas_call | solution.py:340
  100.1 5.6 %collective-permute-done.8.oa = bf16[528,512]{1,0:T(8,128)(2,1)} collective-permute-done((bf16[528,512]{1,0:T(8,128)(2,1)}, bf16[528,512]{1,0:T(8,128)(2,1)}, u32[]{:S(2)}, u32[]{:S(2)}) %collective-permute-start.8) | collective-permute-done | bytes 540704 | tf_op jit(solution)/shard_map/ppermute | solution.py:467
  105.7 1.9 %merge.2 = bf16[2,256,512]{2,1,0:T(8,128)(2,1)S(1)} custom-call(s32[4]{0:T(128)S(1)} %pad_add_fusion.at, bf16[528,512]{1,0:T(8,128)(2,1)S(1)} %own_rows.2.own, bf16[528,512]{1,0:T(8,128)(2,1)} %collective-permute-done.8.oa, bf16[528,512]{1,0:T(8,128)(2,1)} %collective-permute-done.9.ob), custom_call_target="tpu_custom_call" | custom-call | flops 200000000 | bytes 1024 | tf_op jit(solution)/shard_map/merge/pallas_call | solution.py:390
  109.6 7.6 %own_rows.3.own = bf16[528,512]{1,0:T(8,128)(2,1)S(1)} custom-call(s32[4]{0:T(128)S(1)} %pad_add_fusion.at, bf16[1,512,512]{2,1,0:T(8,128)(2,1)} %get-tuple-element.82.q_m, bf16[1,512,512]{2,1,0:T(8,128)(2,1)S(1)} %copy-done.6, bf16[2,512,512]{2,1,0:T(8,128)(2,1)S(1)} %copy-done.3, bf16[2,512,512]{2,1,0:T(8,128)(2,1)} %collective-permute-done.5.kv_o, ...), custom_call_target="tpu_custom_call" | custom-call | flops 600000000 | bytes 1024 | tf_op jit(solution)/shard_map/own_rows/pallas_call | solution.py:340
  119.7 1.6 collective-permute-done.10
  121.4 1.8 %project.3 = (bf16[2,2,2,64,512]{4,3,2,1,0:T(8,128)(2,1)S(1)}, bf16[2,2,2,64,512]{4,3,2,1,0:T(8,128)(2,1)S(1)}) custom-call(s32[4]{0:T(128)S(1)} %pad_add_fusion.at, bf16[2,2,2,64,512]{4,3,2,1,0:T(8,128)(2,1)S(1)} %bitcast.25, bf16[2,2,2,64,512]{4,3,2,1,0:T(8,128)(2,1)S(1)} %bitcast.30, bf16[1024,512]{1,0:T(8,128)(2,1)S(1)} %copy-done, ...), custom_call_target="tpu_custom_call" | custom-call | flops 200000000 | bytes 1024 | tf_op jit(solution)/shard_map/project/pallas_call | solution.py:390
  123.3 5.5 %collective-permute-done.16.oa = bf16[528,512]{1,0:T(8,128)(2,1)S(1)} collective-permute-done((bf16[528,512]{1,0:T(8,128)(2,1)}, bf16[528,512]{1,0:T(8,128)(2,1)S(1)}, u32[]{:S(2)}, u32[]{:S(2)}) %collective-permute-start.16) | collective-permute-done | bytes 540704 | tf_op jit(solution)/shard_map/ppermute | solution.py:467
  128.7 1.7 merge.3
  133.3 6.4 %collective-permute-done.14.got = bf16[2,2,64,512]{3,2,1,0:T(8,128)(2,1)S(1)} collective-permute-done((bf16[2,2,64,512]{3,2,1,0:T(8,128)(2,1)S(1)}, bf16[2,2,64,512]{3,2,1,0:T(8,128)(2,1)S(1)}, u32[]{:S(2)}, u32[]{:S(2)}) %collective-permute-start.14) | collective-permute-done | bytes 262176 | tf_op jit(solution)/shard_map/ppermute | solution.py:473
  140.3 4.0 %collective-permute-done.17 = bf16[2,256,512]{2,1,0:T(8,128)(2,1)S(1)} collective-permute-done((bf16[2,256,512]{2,1,0:T(8,128)(2,1)S(1)}, bf16[2,256,512]{2,1,0:T(8,128)(2,1)S(1)}, u32[]{:S(2)}, u32[]{:S(2)}) %collective-permute-start.17) | collective-permute-done | bytes 524320 | tf_op jit(solution)/shard_map/ppermute | solution.py:467
  144.3 2.3 %project.4 = (bf16[3,2,2,64,512]{4,3,2,1,0:T(8,128)(2,1)S(1)}, bf16[3,2,2,64,512]{4,3,2,1,0:T(8,128)(2,1)S(1)}) custom-call(s32[4]{0:T(128)S(1)} %pad_add_fusion.at, bf16[2,2,2,64,512]{4,3,2,1,0:T(8,128)(2,1)S(1)} %bitcast.28, bf16[2,2,2,64,512]{4,3,2,1,0:T(8,128)(2,1)S(1)} %bitcast.33, bf16[1024,512]{1,0:T(8,128)(2,1)S(1)} %copy-done, ...), custom_call_target="tpu_custom_call" | custom-call | flops 300000000 | bytes 1024 | tf_op jit(solution)/shard_map/project/pallas_call | solution.py:390
  146.8 2.3 %project.5 = (bf16[3,2,2,64,512]{4,3,2,1,0:T(8,128)(2,1)S(1)}, bf16[3,2,2,64,512]{4,3,2,1,0:T(8,128)(2,1)S(1)}) custom-call(s32[4]{0:T(128)S(1)} %pad_add_fusion.at, bf16[2,2,2,64,512]{4,3,2,1,0:T(8,128)(2,1)S(1)} %bitcast.29, bf16[2,2,2,64,512]{4,3,2,1,0:T(8,128)(2,1)S(1)} %bitcast.34, bf16[1024,512]{1,0:T(8,128)(2,1)S(1)} %bitcast_select_fusion.refs_6_.refs_2_, ...), custom_call_target="tpu_custom_call" | custom-call | flops 300000000 | bytes 1024 | tf_op jit(solution)/shard_map/project/pallas_call | solution.py:390
  150.4 1.6 collective-permute-start.19
  160.4 2.2 %collective-permute-done.20.refs_4_ = bf16[3,64,512]{2,1,0:T(8,128)(2,1)S(1)} collective-permute-done((bf16[3,64,512]{2,1,0:T(8,128)(2,1)S(1)}, bf16[3,64,512]{2,1,0:T(8,128)(2,1)S(1)}, u32[]{:S(2)}, u32[]{:S(2)}) %collective-permute-start.20) | collective-permute-done | bytes 196640 | tf_op jit(solution)/shard_map/ppermute | solution.py:467
  162.6 4.2 %collective-permute-done.21.refs_5_ = bf16[3,64,512]{2,1,0:T(8,128)(2,1)S(1)} collective-permute-done((bf16[3,64,512]{2,1,0:T(8,128)(2,1)S(1)}, bf16[3,64,512]{2,1,0:T(8,128)(2,1)S(1)}, u32[]{:S(2)}, u32[]{:S(2)}) %collective-permute-start.21) | collective-permute-done | bytes 196640 | tf_op jit(solution)/shard_map/ppermute | solution.py:549
  166.8 4.3 %collective-permute-done.25.refs_8_ = bf16[3,64,512]{2,1,0:T(8,128)(2,1)S(1)} collective-permute-done((bf16[3,64,512]{2,1,0:T(8,128)(2,1)S(1)}, bf16[3,64,512]{2,1,0:T(8,128)(2,1)S(1)}, u32[]{:S(2)}, u32[]{:S(2)}) %collective-permute-start.25) | collective-permute-done | bytes 196640 | tf_op jit(solution)/shard_map/ppermute | solution.py:467
  171.1 2.9 %collective-permute-done.26.refs_9_ = bf16[3,64,512]{2,1,0:T(8,128)(2,1)S(1)} collective-permute-done((bf16[3,64,512]{2,1,0:T(8,128)(2,1)S(1)}, bf16[3,64,512]{2,1,0:T(8,128)(2,1)S(1)}, u32[]{:S(2)}, u32[]{:S(2)}) %collective-permute-start.26) | collective-permute-done | bytes 196640 | tf_op jit(solution)/shard_map/ppermute | solution.py:549
  174.0 1.7 place.1
  (67 shorter events, 35.1 us)
Async XLA Ops:
  2.1 13.7 %collective-permute-start.1 = (bf16[1,512,512]{2,1,0:T(8,128)(2,1)S(1)}, bf16[1,512,512]{2,1,0:T(8,128)(2,1)S(1)}, u32[]{:S(2)}, u32[]{:S(2)}) collective-permute-start(bf16[1,512,512]{2,1,0:T(8,128)(2,1)S(1)} %get-tuple-element.81), channel_id=1, source_target_pairs={{0,4},{4,0},{8,12},{12,8},{16,20},{20,16},{24,28},{28,24},{1,5},{5... | collective-permute-start | bytes 1572872 | tf_op jit(solution)/shard_map/ppermute | solution.py:467
  3.6 18.0 %collective-permute-start.3 = (bf16[1,512,512]{2,1,0:T(8,128)(2,1)}, bf16[1,512,512]{2,1,0:T(8,128)(2,1)}, u32[]{:S(2)}, u32[]{:S(2)}) collective-permute-start(bf16[1,512,512]{2,1,0:T(8,128)(2,1)} %get-tuple-element.82.q_m), channel_id=1, source_target_pairs={{24,8},{28,12},{25,9},{29,13},{26,10},{30,14},{27,11},{31,15}} | collective-permute-start | bytes 1572872 | tf_op jit(solution)/shard_map/ppermute | solution.py:467
  5.0 26.8 %collective-permute-start = (bf16[1,512,512]{2,1,0:T(8,128)(2,1)}, bf16[1,512,512]{2,1,0:T(8,128)(2,1)}, u32[]{:S(2)}, u32[]{:S(2)}) collective-permute-start(bf16[1,512,512]{2,1,0:T(8,128)(2,1)} %get-tuple-element.82.q_m), channel_id=1, source_target_pairs={{16,8},{20,12},{24,16},{28,20},{17,9},{21,13},{25,17},{29,21},{18,... | collective-permute-start | bytes 1572872 | tf_op jit(solution)/shard_map/ppermute | solution.py:467
  7.2 46.3 %copy-start = (bf16[1024,512]{1,0:T(8,128)(2,1)S(1)}, bf16[1024,512]{1,0:T(8,128)(2,1)}, u32[]{:S(2)}) copy-start(bf16[1024,512]{1,0:T(8,128)(2,1)} %refs_2_.7) | copy-start | bytes 3145732
  11.8 43.8 %collective-permute-start.6 = (bf16[2,512,512]{2,1,0:T(8,128)(2,1)}, bf16[2,512,512]{2,1,0:T(8,128)(2,1)S(1)}, u32[]{:S(2)}, u32[]{:S(2)}) collective-permute-start(bf16[2,512,512]{2,1,0:T(8,128)(2,1)} %get-tuple-element.79), channel_id=1, source_target_pairs={{0,8},{4,12},{8,24},{12,28},{1,9},{5,13},{9,25},{13,29},{2,10},{6,... | collective-permute-start | bytes 3145736 | tf_op jit(solution)/shard_map/ppermute | solution.py:467
  16.5 39.1 %collective-permute-start.5 = (bf16[2,512,512]{2,1,0:T(8,128)(2,1)}, bf16[2,512,512]{2,1,0:T(8,128)(2,1)}, u32[]{:S(2)}, u32[]{:S(2)}) collective-permute-start(bf16[2,512,512]{2,1,0:T(8,128)(2,1)} %get-tuple-element.40), channel_id=1, source_target_pairs={{0,4},{4,0},{8,12},{12,8},{16,20},{20,16},{24,28},{28,24},{1,5},{5... | collective-permute-start | bytes 3145736 | tf_op jit(solution)/shard_map/ppermute | solution.py:467
  18.0 44.2 %collective-permute-start.7 = (bf16[2,512,512]{2,1,0:T(8,128)(2,1)}, bf16[2,512,512]{2,1,0:T(8,128)(2,1)S(1)}, u32[]{:S(2)}, u32[]{:S(2)}) collective-permute-start(bf16[2,512,512]{2,1,0:T(8,128)(2,1)} %get-tuple-element.41), channel_id=1, source_target_pairs={{0,12},{4,8},{8,0},{12,4},{16,24},{20,28},{1,13},{5,9},{9,1},{13,5... | collective-permute-start | bytes 3145736 | tf_op jit(solution)/shard_map/ppermute | solution.py:486
  21.6 13.5 %collective-permute-start.4 = (bf16[1,512,512]{2,1,0:T(8,128)(2,1)}, bf16[1,512,512]{2,1,0:T(8,128)(2,1)S(1)}, u32[]{:S(2)}, u32[]{:S(2)}) collective-permute-start(bf16[1,512,512]{2,1,0:T(8,128)(2,1)} %copy-done.4), channel_id=1, source_target_pairs={{24,8},{28,12},{25,9},{29,13},{26,10},{30,14},{27,11},{31,15}} | collective-permute-start | bytes 1572872 | tf_op jit(solution)/shard_map/ppermute | solution.py:467
  31.8 20.9 %collective-permute-start.2 = (bf16[1,512,512]{2,1,0:T(8,128)(2,1)}, bf16[1,512,512]{2,1,0:T(8,128)(2,1)S(1)}, u32[]{:S(2)}, u32[]{:S(2)}) collective-permute-start(bf16[1,512,512]{2,1,0:T(8,128)(2,1)} %copy-done.4), channel_id=1, source_target_pairs={{16,8},{20,12},{24,16},{28,20},{17,9},{21,13},{25,17},{29,21},{18,... | collective-permute-start | bytes 1572872 | tf_op jit(solution)/shard_map/ppermute | solution.py:467
  53.6 54.6 %collective-permute-start.12 = (bf16[1024,512]{1,0:T(8,128)(2,1)S(1)}, bf16[1024,512]{1,0:T(8,128)(2,1)}, u32[]{:S(2)}, u32[]{:S(2)}) collective-permute-start(bf16[1024,512]{1,0:T(8,128)(2,1)S(1)} %copy-done), channel_id=1, source_target_pairs={{0,16},{4,20},{16,0},{20,4},{24,8},{28,12},{1,17},{5,21},{17,1},{2... | collective-permute-start | bytes 3145736 | tf_op jit(solution)/shard_map/ppermute | solution.py:467
  62.2 1.2 copy-start.1
  71.5 28.6 %collective-permute-start.9 = (bf16[528,512]{1,0:T(8,128)(2,1)}, bf16[528,512]{1,0:T(8,128)(2,1)}, u32[]{:S(2)}, u32[]{:S(2)}) collective-permute-start(bf16[528,512]{1,0:T(8,128)(2,1)} %get-tuple-element.47), channel_id=1, source_target_pairs={{8,24},{12,28},{0,8},{4,12},{24,16},{28,20},{9,25},{13,29},{1,9},{... | collective-permute-start | bytes 1622024 | tf_op jit(solution)/shard_map/ppermute | solution.py:467
  72.8 33.0 %collective-permute-start.8 = (bf16[528,512]{1,0:T(8,128)(2,1)}, bf16[528,512]{1,0:T(8,128)(2,1)}, u32[]{:S(2)}, u32[]{:S(2)}) collective-permute-start(bf16[528,512]{1,0:T(8,128)(2,1)} %get-tuple-element.42), channel_id=1, source_target_pairs={{8,16},{12,20},{16,24},{20,28},{9,17},{13,21},{17,25},{21,29},{10,... | collective-permute-start | bytes 1622024 | tf_op jit(solution)/shard_map/ppermute | solution.py:467
  84.2 33.0 %collective-permute-start.11 = (bf16[528,512]{1,0:T(8,128)(2,1)}, bf16[528,512]{1,0:T(8,128)(2,1)}, u32[]{:S(2)}, u32[]{:S(2)}) collective-permute-start(bf16[528,512]{1,0:T(8,128)(2,1)} %get-tuple-element.48), channel_id=1, source_target_pairs={{8,24},{12,28},{0,8},{4,12},{24,16},{28,20},{9,25},{13,29},{1,9},{... | collective-permute-start | bytes 1622024 | tf_op jit(solution)/shard_map/ppermute | solution.py:467
  85.5 43.3 %collective-permute-start.16 = (bf16[528,512]{1,0:T(8,128)(2,1)}, bf16[528,512]{1,0:T(8,128)(2,1)S(1)}, u32[]{:S(2)}, u32[]{:S(2)}) collective-permute-start(bf16[528,512]{1,0:T(8,128)(2,1)} %copy-done.11), channel_id=1, source_target_pairs={{8,16},{12,20},{16,24},{20,28},{9,17},{13,21},{17,25},{21,29},{10,... | collective-permute-start | bytes 1622024 | tf_op jit(solution)/shard_map/ppermute | solution.py:467
  90.2 1.2 copy-start.2
  100.1 9.5 %copy-start.3 = (bf16[2,512,512]{2,1,0:T(8,128)(2,1)S(1)}, bf16[2,512,512]{2,1,0:T(8,128)(2,1)}, u32[]{:S(2)}) copy-start(bf16[2,512,512]{2,1,0:T(8,128)(2,1)} %get-tuple-element.80.kv_m) | copy-start | bytes 3145732
  100.1 9.5 %copy-start.6 = (bf16[1,512,512]{2,1,0:T(8,128)(2,1)S(1)}, bf16[1,512,512]{2,1,0:T(8,128)(2,1)}, u32[]{:S(2)}) copy-start(bf16[1,512,512]{2,1,0:T(8,128)(2,1)} %copy-done.4) | copy-start | bytes 1572868
  107.6 13.8 %collective-permute-start.10 = (bf16[2,256,512]{2,1,0:T(8,128)(2,1)S(1)}, bf16[2,256,512]{2,1,0:T(8,128)(2,1)S(1)}, u32[]{:S(2)}, u32[]{:S(2)}) collective-permute-start(bf16[2,256,512]{2,1,0:T(8,128)(2,1)S(1)} %merge.2), channel_id=1, source_target_pairs={{0,4},{4,0},{8,12},{12,8},{16,20},{20,16},{24,28},{28,24},{1,5},{5... | collective-permute-start | bytes 1572872 | tf_op jit(solution)/shard_map/ppermute | solution.py:467
  109.5 37.2 %collective-permute-start.22 = (bf16[1024,512]{1,0:T(8,128)(2,1)S(1)}, bf16[1024,512]{1,0:T(8,128)(2,1)S(1)}, u32[]{:S(2)}, u32[]{:S(2)}) collective-permute-start(bf16[1024,512]{1,0:T(8,128)(2,1)S(1)} %bitcast_select_fusion.refs_6_.refs_2_), channel_id=1, source_target_pairs={{0,8},{4,12},{8,0},{12,4},{16,24},{20,28},{24,16},{28,20},{1,9},{5... | collective-permute-start | bytes 3145736 | tf_op jit(solution)/shard_map/ppermute | solution.py:467
  123.2 7.8 %collective-permute-start.13 = (bf16[2,2,2,64,512]{4,3,2,1,0:T(8,128)(2,1)S(1)}, bf16[2,2,2,64,512]{4,3,2,1,0:T(8,128)(2,1)S(1)}, u32[]{:S(2)}, u32[]{:S(2)}) collective-permute-start(bf16[2,2,2,64,512]{4,3,2,1,0:T(8,128)(2,1)S(1)} %get-tuple-element.55), channel_id=1, source_target_pairs={{0,1},{1,0},{2,3},{3,2},{4,5},{5,4},{6,7},{7,6},{8,9},{9,8},{10,11... | collective-permute-start | bytes 1572872 | tf_op jit(solution)/shard_map/ppermute | solution.py:473
  130.4 13.9 %collective-permute-start.17 = (bf16[2,256,512]{2,1,0:T(8,128)(2,1)S(1)}, bf16[2,256,512]{2,1,0:T(8,128)(2,1)S(1)}, u32[]{:S(2)}, u32[]{:S(2)}) collective-permute-start(bf16[2,256,512]{2,1,0:T(8,128)(2,1)S(1)} %merge.3), channel_id=1, source_target_pairs={{0,4},{4,0},{8,12},{12,8},{16,20},{20,16},{24,28},{28,24},{1,5},{5... | collective-permute-start | bytes 1572872 | tf_op jit(solution)/shard_map/ppermute | solution.py:467
  131.7 8.0 %collective-permute-start.14 = (bf16[2,2,64,512]{3,2,1,0:T(8,128)(2,1)S(1)}, bf16[2,2,64,512]{3,2,1,0:T(8,128)(2,1)S(1)}, u32[]{:S(2)}, u32[]{:S(2)}) collective-permute-start(bf16[2,2,64,512]{3,2,1,0:T(8,128)(2,1)S(1)} %get-tuple-element.57), channel_id=1, source_target_pairs={{0,2},{1,3},{2,0},{3,1},{4,6},{5,7},{6,4},{7,5},{8,10},{9,11},{10,... | collective-permute-start | bytes 786440 | tf_op jit(solution)/shard_map/ppermute | solution.py:473
  146.7 3.0 %collective-permute-start.18 = (bf16[3,2,2,64,512]{4,3,2,1,0:T(8,128)(2,1)S(1)}, bf16[3,2,2,64,512]{4,3,2,1,0:T(8,128)(2,1)S(1)}, u32[]{:S(2)}, u32[]{:S(2)}) collective-permute-start(bf16[3,2,2,64,512]{4,3,2,1,0:T(8,128)(2,1)S(1)} %get-tuple-element.63), channel_id=1, source_target_pairs={{0,1},{1,0},{2,3},{3,2},{4,5},{5,4},{6,7},{7,6},{8,9},{9,8},{10,11... | collective-permute-start | bytes 2359304 | tf_op jit(solution)/shard_map/ppermute | solution.py:473
  149.1 5.4 %collective-permute-start.23 = (bf16[3,2,2,64,512]{4,3,2,1,0:T(8,128)(2,1)S(1)}, bf16[3,2,2,64,512]{4,3,2,1,0:T(8,128)(2,1)S(1)}, u32[]{:S(2)}, u32[]{:S(2)}) collective-permute-start(bf16[3,2,2,64,512]{4,3,2,1,0:T(8,128)(2,1)S(1)} %get-tuple-element.70), channel_id=1, source_target_pairs={{0,1},{1,0},{2,3},{3,2},{4,5},{5,4},{6,7},{7,6},{8,9},{9,8},{10,11... | collective-permute-start | bytes 2359304 | tf_op jit(solution)/shard_map/ppermute | solution.py:473
  150.4 8.5 %collective-permute-start.19 = (bf16[3,64,512]{2,1,0:T(8,128)(2,1)S(1)}, bf16[3,64,512]{2,1,0:T(8,128)(2,1)S(1)}, u32[]{:S(2)}, u32[]{:S(2)}) collective-permute-start(bf16[3,64,512]{2,1,0:T(8,128)(2,1)S(1)} %get-tuple-element.65), channel_id=1, source_target_pairs={{0,2},{1,3},{2,0},{3,1},{4,6},{5,7},{6,4},{7,5},{8,10},{9,11},{10,... | collective-permute-start | bytes 589832 | tf_op jit(solution)/shard_map/ppermute | solution.py:473
  152.0 6.4 %collective-permute-start.15 = (bf16[2,64,512]{2,1,0:T(8,128)(2,1)S(1)}, bf16[2,64,512]{2,1,0:T(8,128)(2,1)S(1)}, u32[]{:S(2)}, u32[]{:S(2)}) collective-permute-start(bf16[2,64,512]{2,1,0:T(8,128)(2,1)S(1)} %get-tuple-element.59), channel_id=1, source_target_pairs={{0,4},{4,0},{8,12},{12,8},{16,20},{20,16},{24,28},{28,24},{1,5},{5... | collective-permute-start | bytes 393224 | tf_op jit(solution)/shard_map/ppermute | solution.py:467
  152.5 10.1 %collective-permute-start.20 = (bf16[3,64,512]{2,1,0:T(8,128)(2,1)S(1)}, bf16[3,64,512]{2,1,0:T(8,128)(2,1)S(1)}, u32[]{:S(2)}, u32[]{:S(2)}) collective-permute-start(bf16[3,64,512]{2,1,0:T(8,128)(2,1)S(1)} %get-tuple-element.66), channel_id=1, source_target_pairs={{0,4},{4,0},{8,12},{12,8},{16,20},{20,16},{24,28},{28,24},{1,5},{5... | collective-permute-start | bytes 589832 | tf_op jit(solution)/shard_map/ppermute | solution.py:467
  154.0 12.8 %collective-permute-start.21 = (bf16[3,64,512]{2,1,0:T(8,128)(2,1)S(1)}, bf16[3,64,512]{2,1,0:T(8,128)(2,1)S(1)}, u32[]{:S(2)}, u32[]{:S(2)}) collective-permute-start(bf16[3,64,512]{2,1,0:T(8,128)(2,1)S(1)} %get-tuple-element.67), channel_id=1, source_target_pairs={{0,6},{1,7},{2,4},{3,5},{4,2},{5,3},{6,0},{7,1},{8,14},{9,15},{10,... | collective-permute-start | bytes 589832 | tf_op jit(solution)/shard_map/ppermute | solution.py:549
  155.2 11.6 %collective-permute-start.24 = (bf16[3,64,512]{2,1,0:T(8,128)(2,1)S(1)}, bf16[3,64,512]{2,1,0:T(8,128)(2,1)S(1)}, u32[]{:S(2)}, u32[]{:S(2)}) collective-permute-start(bf16[3,64,512]{2,1,0:T(8,128)(2,1)S(1)} %get-tuple-element.72), channel_id=1, source_target_pairs={{0,2},{1,3},{2,0},{3,1},{4,6},{5,7},{6,4},{7,5},{8,10},{9,11},{10,... | collective-permute-start | bytes 589832 | tf_op jit(solution)/shard_map/ppermute | solution.py:473
  158.4 12.7 %collective-permute-start.25 = (bf16[3,64,512]{2,1,0:T(8,128)(2,1)S(1)}, bf16[3,64,512]{2,1,0:T(8,128)(2,1)S(1)}, u32[]{:S(2)}, u32[]{:S(2)}) collective-permute-start(bf16[3,64,512]{2,1,0:T(8,128)(2,1)S(1)} %get-tuple-element.73), channel_id=1, source_target_pairs={{0,4},{4,0},{8,12},{12,8},{16,20},{20,16},{24,28},{28,24},{1,5},{5... | collective-permute-start | bytes 589832 | tf_op jit(solution)/shard_map/ppermute | solution.py:467
  158.9 15.1 %collective-permute-start.26 = (bf16[3,64,512]{2,1,0:T(8,128)(2,1)S(1)}, bf16[3,64,512]{2,1,0:T(8,128)(2,1)S(1)}, u32[]{:S(2)}, u32[]{:S(2)}) collective-permute-start(bf16[3,64,512]{2,1,0:T(8,128)(2,1)S(1)} %get-tuple-element.74), channel_id=1, source_target_pairs={{0,6},{1,7},{2,4},{3,5},{4,2},{5,3},{6,0},{7,1},{8,14},{9,15},{10,... | collective-permute-start | bytes 589832 | tf_op jit(solution)/shard_map/ppermute | solution.py:549
  (7 other events, 6.4 us)
